TPU v7x, 32 devices: a whole 2x2x4 slice. The times are simulated.
32 devices in a mesh: mod: 2 (over core), dp: 8 (over z, y), tensor: 2 (over x).
Axes of the slice: x: 2, y: 2, z: 4, core: 2. Of those that a mesh axis runs over, the one named last changes fastest.
Arguments:
- tokens: bfloat16 [5120, 4096], P('dp', 'tensor'), may hold values from -400 to 400
- modality: int32 [5120], P('dp'), may hold values from 0 to 1, as said below
- norm_gains: float32 [2, 4096], P('mod'), may hold values from 0.5 to 2
- qkv_weight: bfloat16 [2, 4096, 3, 2048], P('mod', 'dp', None, 'tensor'), may hold values from -3 to 3
- out_weight: bfloat16 [2, 2048, 4096], P('mod', 'dp', 'tensor'), may hold values from -0.125 to 0.125
Outputs:
- mixed: bfloat16 [5120, 4096], P('dp', 'tensor')
Inputs may be any that keep to these rules, and one draw needn't show every extreme that they name: Each sequence's positions fall into aligned spans of 32 positions of one modality each. Each sequence holds at most 480 tokens of either modality; in every draw some sequence holds exactly 480 image tokens and another exactly 480 text tokens.
All inputs are finite; a program needn't handle non-finite values.
Results may differ from a plain program's by a relative error of at most 0.015.
Values may be sent and summed in bfloat16 or wider, within the bound.
No kernel may reach another device: no remote copies, remote signals or barrier semaphores. Data moves between devices by JAX's collectives and lax.ppermute only.
A program may use at most 128 MiB of HBM per device.

v0:
```python
import jax
import jax.numpy as jnp
from jax import lax
from jax.sharding import PartitionSpec as P

HDIM = 128


def from_partner(x, axis, bit):
    return lax.ppermute(x, axis, [(i, i ^ 1 << bit) for i in range(lax.axis_size(axis))])


def on_device(tokens, modality, norm_gains, qkv_weight, out_weight):
    tower_id = lax.axis_index("mod")
    own_rows = modality == tower_id
    gathered = lax.all_gather(tokens, "tensor", axis=1, tiled=True)
    length = gathered.shape[0]
    local_width = qkv_weight.shape[3]
    local_heads = local_width // HDIM
    gain_row = norm_gains[0]
    scale = HDIM ** (-0.5)
    wide_rows = gathered.astype(jnp.float32)
    inverse = lax.rsqrt(jnp.mean(wide_rows * wide_rows, axis=-1, keepdims=True) + 1e-05)
    row_block = (wide_rows * inverse * gain_row).astype(jnp.bfloat16)
    weight_piece = lax.all_gather(qkv_weight, "dp", axis=1, tiled=True)
    count = weight_piece.shape[1]
    columns = row_block
    projected = (
        jnp.dot(
            columns,
            weight_piece[0].reshape(count, 3 * local_width),
            preferred_element_type=jnp.float32,
        )
        .astype(jnp.bfloat16)
        .reshape(length, 3, local_heads, HDIM)
    )
    queries = projected[:, 0]
    own_pair = projected[:, 1:]
    other_pair = from_partner(own_pair, "mod", 0)
    key_pairs = jnp.where(own_rows[:, None, None, None], own_pair, other_pair)
    key_pos = jnp.arange(length, dtype=jnp.int32)
    scores = (
        jnp.einsum("qhd,khd->hqk", queries, key_pairs[:, 0], preferred_element_type=jnp.float32)
        * scale
    )
    allowed = key_pos[None, :] <= key_pos[:, None]
    scores = jnp.where(allowed[None], scores, -jnp.inf)
    soft_weights = jax.nn.softmax(scores, axis=-1).astype(jnp.bfloat16)
    attended = jnp.einsum(
        "hqk,khd->qhd", soft_weights, key_pairs[:, 1], preferred_element_type=jnp.float32
    )
    attended = attended.astype(jnp.bfloat16).reshape(queries.shape[0], local_width)
    all_heads = lax.all_gather(attended, "tensor", axis=1, tiled=True)
    weight_piece = lax.all_gather(out_weight, "dp", axis=1, tiled=True)
    columns = all_heads
    projected_out = jnp.dot(columns, weight_piece[0], preferred_element_type=jnp.float32).astype(
        jnp.bfloat16
    )
    placed = jnp.where(own_rows[:, None], projected_out, jnp.zeros_like(projected_out))
    combined = lax.psum(placed.astype(jnp.float32).astype(jnp.bfloat16), "mod")
    return combined


def solution(mesh):
    return jax.shard_map(
        on_device,
        mesh=mesh,
        in_specs=(
            P("dp", "tensor"),
            P("dp"),
            P("mod", None),
            P("mod", "dp", None, "tensor"),
            P("mod", "dp", "tensor"),
        ),
        out_specs=P("dp", "tensor"),
        check_vma=False,
    )
```

profile of v0, /device:TPU:0, one launch (start us, length us, event | category | flops | bytes accessed | tf_op | source)
XLA Modules:
  0.0 770.3 jit_solution(14420945542751699245)
XLA Ops:
  6.5 0.0 all-gather.5.cloned.1.call-start
  6.5 0.7 all-gather.5.cloned.1.call-update
  7.3 0.0 all-gather.7.cloned.1.call-start
  7.3 4.6 copy.10
  11.9 0.0 all-gather.7.cloned.1.call-update
  12.0 0.0 copy-start.3
  12.0 0.0 all-gather.11.cloned.1.call-start
  12.0 0.7 all-gather.11.cloned.1.call-update
  12.7 0.0 all-gather.9.cloned.1.call-start
  12.8 67.4 %all-gather.5.cloned.1.call-done = bf16[640,4096]{1,0:T(8,128)(2,1)} async-done(((bf16[640,2048]{1,0:T(8,128)(2,1)}), bf16[640,4096]{1,0:T(8,128)(2,1)}) %all-gather.5.cloned.1.call-update) | async-done | bytes 5242896 | tf_op jit(solution)/shard_map/all_gather | solution.py:16
  80.2 3.6 fusion.2
  83.8 478.4 %all-gather.7.cloned.1.call-done = bf16[1,4096,3,1024]{1,3,2,0:T(8,128)(2,1)} async-done(((bf16[1,512,3,1024]{1,3,2,0:T(8,128)(2,1)}), bf16[1,4096,3,1024]{1,3,2,0:T(8,128)(2,1)}) %all-gather.7.cloned.1.call-update) | async-done | bytes 25165840 | tf_op jit(solution)/shard_map/all_gather | solution.py:25
  562.2 0.0 copy-done.3
  562.2 21.7 %fusion.24 = bf16[80,8,24,128]{3,1,2,0:T(8,128)(2,1)S(1)} fusion(bf16[4096,3072]{0,1:T(8,128)(2,1)} %bitcast.48, bf16[640,4096]{1,0:T(8,128)(2,1)} %all-gather.5.cloned.1.call-done, f32[4096]{0:T(1024)S(1)} %bitcast.49, f32[640]{0:T(1024)S(1)} %add_rsqrt_fusion), kind=kOutput, calls=%fused_computation.23 | convolution fusion | flops 16118579200 | bytes 34359808 | tf_op jit(solution)/shard_map/dot_general | solution.py:29
  583.9 1.1 copy.19
  585.0 0.0 copy-start
  585.0 0.5 slice.16
  585.5 0.0 copy-start.2
  585.5 2.3 copy.17
  587.8 0.0 copy-done
  587.8 0.0 collective-permute-start
  587.8 0.1 iota_compare_fusion
  588.0 0.0 copy-done.2
  588.0 2.5 slice.18
  590.4 2.6 collective-permute-done
  593.1 3.9 broadcast_select_fusion
  597.0 0.0 copy-start.1
  597.0 6.3 fusion.37
  603.3 0.0 copy-done.1
  603.3 8.4 %fusion.29 = bf16[8,128,640]{2,1,0:T(8,128)(2,1)} fusion(f32[8,640]{1,0:T(8,128)S(1)} %fusion.37, bf16[640,2,8,128]{3,0,2,1:T(8,128)(2,1)S(1)} %copy-done.1, pred[640,640]{0,1:T(8,128)(4,1)S(1)} %iota_compare_fusion, bf16[640,1,8,128]{3,2,1,0:T(8,128)(2,1)} %slice.18), kind=kOutput, calls=%fused_computation.26 | convolution fusion | flops 1694766720 | bytes 5672960 | tf_op jit(solution)/shard_map/hqk,khd->qhd/dot_general | solution.py:49
  611.7 0.0 all-gather.9.cloned.1.call-update
  611.7 0.0 all-reduce.2.cloned.1.call-start
  611.8 77.5 %all-gather.11.cloned.1.call-done = bf16[1,2048,2048]{2,1,0:T(8,128)(2,1)} async-done(((bf16[1,256,2048]{2,1,0:T(8,128)(2,1)}), bf16[1,2048,2048]{2,1,0:T(8,128)(2,1)}) %all-gather.11.cloned.1.call-update) | async-done | bytes 8388624 | tf_op jit(solution)/shard_map/all_gather | solution.py:54
  689.3 38.6 %all-gather.9.cloned.1.call-done = bf16[640,2048]{0,1:T(8,128)(2,1)} async-done(((bf16[640,1024]{0,1:T(8,128)(2,1)}), bf16[640,2048]{0,1:T(8,128)(2,1)}) %all-gather.9.cloned.1.call-update) | async-done | bytes 2621456 | tf_op jit(solution)/shard_map/all_gather | solution.py:53
  727.9 9.9 %fusion.21 = bf16[640,2048]{1,0:T(8,128)(2,1)} fusion(bf16[640,2048]{0,1:T(8,128)(2,1)} %all-gather.9.cloned.1.call-done, bf16[1,2048,2048]{2,1,0:T(8,128)(2,1)} %all-gather.11.cloned.1.call-done, pred[640]{0:T(1024)(128)(4,1)S(1)} %broadcast_compare_fusion), kind=kOutput, calls=%fused_computation.21 | convolution fusion | flops 5371330560 | bytes 13632128 | tf_op jit(solution)/shard_map/dot_general | solution.py:56
  737.8 0.0 all-reduce.2.cloned.1.call-update
  737.9 22.3 %all-reduce.2.cloned.1.call-done = bf16[640,2048]{1,0:T(8,128)(2,1)} async-done(((bf16[640,2048]{1,0:T(8,128)(2,1)}), bf16[640,2048]{1,0:T(8,128)(2,1)}) %all-reduce.2.cloned.1.call-update) | async-done | bytes 2621456 | tf_op jit(solution)/shard_map/psum | solution.py:60
  760.2 3.6 copy.34
  (2 shorter events, 0.0 us)
Async XLA Ops:
  6.5 73.7 %all-gather.5.cloned.1.call-start = ((), (), s32[]{:S(2)}) async-start(), calls=%async_computation | async-start | bytes 7864320 | tf_op jit(solution)/shard_map/all_gather | solution.py:16
  7.3 555.0 %all-gather.7.cloned.1.call-start = ((), (), s32[]{:S(2)}) async-start(), calls=%async_computation.1 | async-start | bytes 28311552 | tf_op jit(solution)/shard_map/all_gather | solution.py:25
  12.0 550.3 %copy-start.3 = (f32[1,4096]{1,0:T(1,128)S(1)}, f32[1,4096]{1,0:T(1,128)}, u32[]{:S(2)}) copy-start(f32[1,4096]{1,0:T(1,128)} %param.7) | copy-start | bytes 49156
  12.0 677.3 %all-gather.11.cloned.1.call-start = ((), (), s32[]{:S(2)}) async-start(), calls=%async_computation.3 | async-start | bytes 9437184 | tf_op jit(solution)/shard_map/all_gather | solution.py:54
  12.7 715.2 %all-gather.9.cloned.1.call-start = ((), (), s32[]{:S(2)}) async-start(), calls=%async_computation.2 | async-start | bytes 3932160 | tf_op jit(solution)/shard_map/all_gather | solution.py:53
  585.0 2.8 copy-start
  585.5 2.5 copy-start.2
  587.8 5.3 collective-permute-start
  597.0 6.3 copy-start.1
  611.7 148.5 %all-reduce.2.cloned.1.call-start = ((), (), s32[]{:S(2)}) async-start(), calls=%async_computation.4 | async-start | bytes 5242880 | tf_op jit(solution)/shard_map/psum | solution.py:60
Sparse Core Ops, SparseCore 0:
  8.9 71.2 all-gather.4
  81.7 480.4 all-gather.6
  564.3 124.8 all-gather.10
  690.7 37.1 all-gather.8
  738.0 22.1 all-reduce.1
where the time goes:
time: 771 us; the launch traced here: 770 us
  waiting for transfers between devices  688 us (89%)
  matrix products  46.3 us (6%)
  local copies, waits for them, and re-layouts  14.6 us (2%)
  between operations  13.2 us (2%)
    all_gather x1, waiting for transfers between devices, on_device(): weight_piece = lax.all_gather(qkv_weight, 'dp', axis=1, tiled=True)  478 us
    all_gather x1, waiting for transfers between devices, on_device(): weight_piece = lax.all_gather(out_weight, 'dp', axis=1, tiled=True)  77.5 us
    all_gather x1, waiting for transfers between devices, on_device(): gathered = lax.all_gather(tokens, 'tensor', axis=1, tiled=True)  67.4 us
    all_gather x1, waiting for transfers between devices, on_device(): all_heads = lax.all_gather(attended, 'tensor', axis=1, tiled=True)  38.6 us
    psum x1, waiting for transfers between devices, on_device(): combined = lax.psum(placed.astype(jnp.float32).astype(jnp.bfloat16), 'mod')  22.3 us
    dot_general x1, matrix products, on_device(): jnp.dot(columns, weight_piece[0].reshape(count, 3 * local_width), preferr...  21.7 us
  transfers between devices with their start and end apart: 6, of which 6 were waited for; matrix products, arithmetic and copies ran while one was open for 7% of the time, Pallas kernels for 0%

commit v1 on v0

v1 whole, which is shorter than its diff:
```python
import jax
import jax.numpy as jnp
from jax import lax
from jax.sharding import PartitionSpec as P

HDIM = 128
AXES = ("mod", "dp", "tensor")


def make_move(mesh):
    mods, rings, shards = mesh.shape["mod"], mesh.shape["dp"] // 2, mesh.shape["tensor"]

    def flat(m, z, y, x):
        return (m * rings * 2 + z * 2 + y) * shards + x

    def move(array, where):
        pairs = [
            (flat(m, z, y, x), flat(*where(m, z, y, x)))
            for m in range(mods)
            for z in range(rings)
            for y in range(2)
            for x in range(shards)
        ]
        return lax.ppermute(array, AXES, pairs)

    return move


def solution(mesh):
    rings, shards = mesh.shape["dp"] // 2, mesh.shape["tensor"]
    move = make_move(mesh)

    def to_core(array):
        return move(array, lambda m, z, y, x: (1 - m, z, y, x))

    def to_pair(array):
        return move(array, lambda m, z, y, x: (m, z, 1 - y, x))

    def around(array, step):
        return move(array, lambda m, z, y, x: (m, (z + step) % rings, y, x))

    def over_tensor(array):
        own = lax.axis_index("tensor")
        held = jnp.zeros((shards,) + array.shape, array.dtype)
        held = lax.dynamic_update_index_in_dim(held, array, own, 0)
        for step in range(1, shards):
            got = move(array, lambda m, z, y, x: (m, z, y, (x + step) % shards))
            held = lax.dynamic_update_index_in_dim(held, got, (own - step) % shards, 0)
        return held

    def ring(block, ahead, back):
        found = []
        for count, step in ((ahead, 1), (back, -1)):
            held = block
            for hop in range(1, count + 1):
                held = around(held, step)
                found.append((-step * hop, held))
        return found

    def on_device(tokens, modality, norm_gains, qkv_weight, out_weight):
        core = lax.axis_index("mod")
        place = lax.axis_index("dp")
        z, y = place // 2, place % 2
        length, features = tokens.shape
        kept = qkv_weight.shape[1]
        width = qkv_weight.shape[3] // 2
        heads = width // HDIM
        scale = HDIM ** (-0.5)

        def half(which):
            parts = [
                lax.dynamic_slice_in_dim(qkv_weight[0, :, j, :], which * width, width, 1)
                for j in range(3)
            ]
            return jnp.concatenate(parts, axis=1)

        own_block = half(y)
        pair_block = to_pair(half(1 - y))
        mid, rest = rings // 2, rings - 1 - rings // 2
        blocks = [(2 * z + y, own_block), (2 * z + 1 - y, pair_block)]
        blocks += [(2 * ((z + k) % rings) + y, b) for k, b in ring(own_block, mid, rest)]
        blocks += [(2 * ((z + k) % rings) + 1 - y, b) for k, b in ring(pair_block, rest, mid)]

        some = length // 2
        rows = lax.dynamic_slice_in_dim(tokens, core * some, some, 0)
        other_rows = to_pair(rows)
        fetched = jnp.stack([over_tensor(rows), over_tensor(other_rows)])
        swapped = to_core(fetched)
        first = jnp.where(core == 0, fetched, swapped)
        second = jnp.where(core == 0, swapped, fetched)
        full = jnp.stack([first, second], axis=2)
        full = full.reshape(2, shards, length, features)
        wide = full.astype(jnp.float32)
        inverse = lax.rsqrt(
            jnp.sum(wide * wide, axis=(1, 3), keepdims=True) / (shards * features) + 1e-05
        )
        gains = norm_gains[0].reshape(1, shards, 1, features)
        normed = (wide * inverse * gains).astype(jnp.bfloat16)
        normed = normed.reshape(2, shards, length, features // kept, kept)
        normed = normed.transpose(1, 3, 0, 2, 4).reshape(2 * rings, 2 * length, kept)

        total = jnp.zeros((2 * length, 3 * width), jnp.float32)
        for index, block in blocks:
            columns = lax.dynamic_index_in_dim(normed, index, 0, keepdims=False)
            total = total + jnp.dot(columns, block, preferred_element_type=jnp.float32)
        projected = total.astype(jnp.bfloat16).reshape(2, length, 3 * width)

        which = core ^ y
        own = lax.dynamic_index_in_dim(projected, which, 0, keepdims=False)
        got = to_core(lax.dynamic_index_in_dim(projected, 1 - which, 0, keepdims=False))
        kinds = jnp.stack([modality, to_pair(modality)])
        kind = lax.dynamic_index_in_dim(kinds, which, 0, keepdims=False)
        qkv = jnp.where((kind == core)[:, None], own, got).reshape(length, 3, heads, HDIM)
        position = jnp.arange(length, dtype=jnp.int32)
        allowed = position[None, :] <= position[:, None]
        scores = (
            jnp.einsum("qhd,khd->hqk", qkv[:, 0], qkv[:, 1], preferred_element_type=jnp.float32)
            * scale
        )
        scores = jnp.where(allowed[None], scores, -jnp.inf)
        probs = jax.nn.softmax(scores, axis=-1).astype(jnp.bfloat16)
        attended = jnp.einsum(
            "hqk,khd->qhd", probs, qkv[:, 2], preferred_element_type=jnp.float32
        )
        attended = attended.astype(jnp.bfloat16).reshape(length, width)

        attended = move(
            attended, lambda m, z, y, x: (m, z, y, x) if m == y else (1 - m, z, 1 - y, x)
        )
        attended = over_tensor(attended)
        swapped = to_core(attended)
        first = jnp.where(core == 0, attended, swapped)
        second = jnp.where(core == 0, swapped, attended)
        all_heads = jnp.stack([first, second], axis=1)
        all_heads = all_heads.transpose(2, 0, 1, 3).reshape(length, shards * 2 * width)

        held = out_weight.shape[1]
        own_out = out_weight[0]
        pair_out = to_pair(own_out)
        outs = [(2 * z + y, own_out), (2 * z + 1 - y, pair_out)]
        outs += [(2 * ((z + k) % rings) + y, b) for k, b in ring(own_out, mid, rest)]
        outs += [(2 * ((z + k) % rings) + 1 - y, b) for k, b in ring(pair_out, rest, mid)]
        result = jnp.zeros((length, out_weight.shape[2]), jnp.float32)
        for index, block in outs:
            columns = lax.dynamic_slice_in_dim(all_heads, index * held, held, 1)
            result = result + jnp.dot(columns, block, preferred_element_type=jnp.float32)
        result = result.astype(jnp.bfloat16)
        return jnp.where((modality == core)[:, None], result, to_core(result))

    return jax.shard_map(
        on_device,
        mesh=mesh,
        in_specs=(
            P("dp", "tensor"),
            P("dp"),
            P("mod", None),
            P("mod", "dp", None, "tensor"),
            P("mod", "dp", "tensor"),
        ),
        out_specs=P("dp", "tensor"),
        check_vma=False,
    )
```

time: 771 us -> 505 us (0.65)
  the two profiles are of different devices: /device:TPU:0 before, /device:TPU:31 now
where the time goes in v1:
time: 505 us; the launch traced here: 497 us
  waiting for transfers between devices  267 us (53%)
  matrix products  83.6 us (17%)
  local copies, waits for them, and re-layouts  58.4 us (12%)
  other arithmetic  48.6 us (10%)
  starting transfers between devices  39.5 us (8%)
    ppermute x24, waiting for transfers between devices, move(): return lax.ppermute(array, AXES, pairs)  267 us
    dot_general x8, matrix products, on_device(): total = total + jnp.dot(columns, block, preferred_element_type=jnp.float32)  41.2 us
    dot_general x8, matrix products, on_device(): jnp.dot(columns, block, preferred_element_type=jnp.float32)  40.5 us
    ppermute x24, starting transfers between devices, move(): return lax.ppermute(array, AXES, pairs)  39.5 us
    convert_element_type x1, local copies, waits for them, and re-layouts, on_device(): wide = full.astype(jnp.float32)  25.3 us
    transpose x1, other arithmetic, on_device(): normed.transpose(1, 3, 0, 2, 4).reshape(2 * rings, 2 * length, kept)  15.6 us
    convert_element_type x1, other arithmetic, on_device(): wide = full.astype(jnp.float32)  12.4 us
    transpose x1, local copies, waits for them, and re-layouts, on_device(): normed.transpose(1, 3, 0, 2, 4).reshape(2 * rings, 2 * length, kept)  10.4 us
  transfers between devices with their start and end apart: 24, of which 11 were waited for; matrix products, arithmetic and copies ran while one was open for 29% of the time, Pallas kernels for 0%

profile of v1, /device:TPU:31, one launch (start us, length us, event | category | flops | bytes accessed | tf_op | source)
XLA Modules:
  0.0 497.4 jit_solution(15030700574941239031)
XLA Ops:
  3.6 29.5 %collective-permute-done.2 = bf16[320,2048]{1,0:T(8,128)(2,1)} collective-permute-done((bf16[320,2048]{1,0:T(8,128)(2,1)}, bf16[320,2048]{1,0:T(8,128)(2,1)}, u32[]{:S(2)}, u32[]{:S(2)}) %collective-permute-start.2) | collective-permute-done | bytes 1310752 | tf_op jit(solution)/shard_map/ppermute | solution.py:24
  36.6 25.5 %collective-permute-done.3 = bf16[320,2048]{1,0:T(8,128)(2,1)} collective-permute-done((bf16[320,2048]{1,0:T(8,128)(2,1)}, bf16[320,2048]{1,0:T(8,128)(2,1)}, u32[]{:S(2)}, u32[]{:S(2)}) %collective-permute-start.3) | collective-permute-done | bytes 1310752 | tf_op jit(solution)/shard_map/ppermute | solution.py:24
  63.6 3.1 pad_maximum_fusion
  66.8 2.5 collective-permute-start.4
  69.2 2.2 fusion.66
  73.6 34.5 %collective-permute-done.5 = bf16[512,1536]{1,0:T(8,128)(2,1)} collective-permute-done((bf16[512,1536]{1,0:T(8,128)(2,1)S(1)}, bf16[512,1536]{1,0:T(8,128)(2,1)}, u32[]{:S(2)}, u32[]{:S(2)}) %collective-permute-start.5) | collective-permute-done | bytes 1572896 | tf_op jit(solution)/shard_map/ppermute | solution.py:24
  109.7 3.1 collective-permute-start.9
  114.2 31.3 %collective-permute-done.10 = bf16[512,1536]{1,0:T(8,128)(2,1)} collective-permute-done((bf16[512,1536]{1,0:T(8,128)(2,1)}, bf16[512,1536]{1,0:T(8,128)(2,1)}, u32[]{:S(2)}, u32[]{:S(2)}) %collective-permute-start.10) | collective-permute-done | bytes 1572896 | tf_op jit(solution)/shard_map/ppermute | solution.py:24
  145.5 4.1 select_bitcast_fusion.1
  149.6 2.4 copy-done
  153.5 2.1 multiply_reduce_fusion
  155.6 12.4 %maximum_convert_fusion = f32[2,2,2,320,2048]{4,3,2,1,0:T(8,128)} fusion(bf16[2,2,1,320,2048]{4,3,2,1,0:T(8,128)(2,1)} %copy-done.1, bf16[2,2,1,320,2048]{4,3,2,1,0:T(8,128)(2,1)} %copy-done), kind=kLoop, calls=%fused_computation.4 | loop fusion | flops 10485760 | bytes 31457280 | tf_op jit(solution)/shard_map/convert_element_type | solution.py:93
  168.1 25.3 %reshape.85 = f32[2,2,640,4,512]{4,3,2,1,0:T(4,128)} reshape(f32[2,2,2,320,2048]{4,3,2,1,0:T(8,128)} %maximum_convert_fusion) | data formatting | bytes 41943040 | tf_op jit(solution)/shard_map/convert_element_type | solution.py:93
  193.4 15.6 %fusion.1 = bf16[2,4,2,640,512]{4,1,3,0,2:T(4,128)(2,1)} fusion(f32[2,2,640,4,512]{4,3,2,1,0:T(4,128)} %reshape.85, f32[2,4,512]{2,1,0:T(4,128)S(1)} %mul.97, f32[2,640]{1,0:T(2,128)S(1)} %rsqrt.12), kind=kLoop, calls=%fused_computation.3 | loop fusion | flops 15728640 | bytes 31478784 | tf_op jit(solution)/shard_map/transpose | solution.py:100
  209.0 10.4 %copy.9 = bf16[2,4,2,640,512]{4,3,2,1,0:T(8,128)(2,1)} copy(bf16[2,4,2,640,512]{4,1,3,0,2:T(4,128)(2,1)} %fusion.1) | data formatting | bytes 20971520 | tf_op jit(solution)/shard_map/transpose | solution.py:100
  219.4 3.7 fusion.20
  223.8 3.6 convolution_add_fusion.4
  227.5 3.7 convolution_add_fusion.3
  231.2 6.7 %fusion.15 = f32[1280,1536]{1,0:T(8,128)} fusion(bf16[512,1536]{1,0:T(8,128)(2,1)} %collective-permute-done.8, bf16[8,1280,512]{2,1,0:T(8,128)(2,1)S(1)} %bitcast.107, s32[]{:T(128)S(6)} %select_n.190), kind=kOutput, calls=%fused_computation.36 | convolution fusion | flops 2013265920 | bytes 10747908 | tf_op jit(solution)/shard_map/dot_general | solution.py:105
  237.9 10.3 %collective-permute-done.7 = bf16[512,1536]{1,0:T(8,128)(2,1)} collective-permute-done((bf16[512,1536]{1,0:T(8,128)(2,1)}, bf16[512,1536]{1,0:T(8,128)(2,1)}, u32[]{:S(2)}, u32[]{:S(2)}) %collective-permute-start.7) | collective-permute-done | bytes 1572896 | tf_op jit(solution)/shard_map/ppermute | solution.py:24
  248.3 6.4 %fusion.2 = f32[1280,1536]{1,0:T(8,128)S(1)} fusion(f32[1280,1536]{1,0:T(8,128)} %fusion.15, f32[1280,1536]{1,0:T(8,128)S(1)} %convolution_add_fusion.3, bf16[512,1536]{1,0:T(8,128)(2,1)} %collective-permute-done.7, bf16[8,1280,512]{2,1,0:T(8,128)(2,1)S(1)} %bitcast.108, s32[]{:T(128)S(6)} %select_n.188), kind=kOutput, calls=%fused_computation.10 | convolution fusion | flops 2017198080 | bytes 26476548 | tf_op jit(solution)/shard_map/dot_general | solution.py:105
  254.7 7.0 %fusion.12 = f32[1280,1536]{1,0:T(8,128)} fusion(bf16[512,1536]{1,0:T(8,128)(2,1)} %collective-permute-done.10, bf16[8,1280,512]{2,1,0:T(8,128)(2,1)S(1)} %bitcast.109, s32[]{:T(128)S(6)} %select_n.192), kind=kOutput, calls=%fused_computation.33 | convolution fusion | flops 2013265920 | bytes 10747908 | tf_op jit(solution)/shard_map/dot_general | solution.py:105
  261.6 6.4 %fusion.3 = f32[1280,1536]{1,0:T(8,128)S(1)} fusion(f32[1280,1536]{1,0:T(8,128)} %fusion.12, f32[1280,1536]{1,0:T(8,128)S(1)} %fusion.2, bf16[512,1536]{1,0:T(8,128)(2,1)} %collective-permute-done.9, bf16[8,1280,512]{2,1,0:T(8,128)(2,1)S(1)} %bitcast.110, s32[]{:T(128)S(6)} %select_n.191), kind=kOutput, calls=%fused_computation.11 | convolution fusion | flops 2017198080 | bytes 26476548 | tf_op jit(solution)/shard_map/dot_general | solution.py:105
  268.0 12.2 %collective-permute-done.11 = bf16[512,1536]{1,0:T(8,128)(2,1)} collective-permute-done((bf16[512,1536]{1,0:T(8,128)(2,1)}, bf16[512,1536]{1,0:T(8,128)(2,1)}, u32[]{:S(2)}, u32[]{:S(2)}) %collective-permute-start.11) | collective-permute-done | bytes 1572896 | tf_op jit(solution)/shard_map/ppermute | solution.py:24
  280.3 3.7 fusion.4
  285.5 2.3 copy.11
  287.8 1.7 collective-permute-start.12
  289.8 2.1 collective-permute-done
  292.0 2.8 copy.10
  294.8 1.8 bitcast_select_fusion
  297.6 3.3 fusion.67
  302.7 11.9 %collective-permute-start.16 = (bf16[256,2048]{1,0:T(8,128)(2,1)}, bf16[256,2048]{1,0:T(8,128)(2,1)}, u32[]{:S(2)}, u32[]{:S(2)}) collective-permute-start(bf16[256,2048]{1,0:T(8,128)(2,1)} %bitcast.39), channel_id=1, source_target_pairs={{0,2},{1,3},{2,0},{3,1},{4,6},{5,7},{6,4},{7,5},{8,10},{9,11},{10,... | collective-permute-start | bytes 3145736 | tf_op jit(solution)/shard_map/ppermute | solution.py:24
  314.9 10.5 %collective-permute-start.15 = (bf16[2,640,512]{1,2,0:T(8,128)(2,1)S(1)}, bf16[2,640,512]{1,2,0:T(8,128)(2,1)S(1)}, u32[]{:S(2)}, u32[]{:S(2)}) collective-permute-start(bf16[2,640,512]{1,2,0:T(8,128)(2,1)S(1)} %bitcast_dynamic-update-slice_fusion.4), channel_id=1, source_target_pairs={{0,16},{1,17},{2,18},{3,19},{4,20},{5,21},{6,22},{7,23},{8,24},{9,... | collective-permute-start | bytes 3932168 | tf_op jit(solution)/shard_map/ppermute | solution.py:24
  325.5 11.6 %collective-permute-done.16 = bf16[256,2048]{1,0:T(8,128)(2,1)} collective-permute-done((bf16[256,2048]{1,0:T(8,128)(2,1)}, bf16[256,2048]{1,0:T(8,128)(2,1)}, u32[]{:S(2)}, u32[]{:S(2)}) %collective-permute-start.16) | collective-permute-done | bytes 1048608 | tf_op jit(solution)/shard_map/ppermute | solution.py:24
  337.1 3.3 collective-permute-start.20
  340.4 55.1 %collective-permute-done.17 = bf16[256,2048]{1,0:T(8,128)(2,1)} collective-permute-done((bf16[256,2048]{1,0:T(8,128)(2,1)}, bf16[256,2048]{1,0:T(8,128)(2,1)}, u32[]{:S(2)}, u32[]{:S(2)}) %collective-permute-start.17) | collective-permute-done | bytes 1048608 | tf_op jit(solution)/shard_map/ppermute | solution.py:24
  395.5 1.7 collective-permute-start.22
  397.7 2.1 fusion.44
  399.8 4.5 fusion.40
  404.3 4.4 fusion.42
  408.7 4.4 fusion.32
  413.2 49.6 %collective-permute-done.18 = bf16[256,2048]{1,0:T(8,128)(2,1)S(1)} collective-permute-done((bf16[256,2048]{1,0:T(8,128)(2,1)}, bf16[256,2048]{1,0:T(8,128)(2,1)S(1)}, u32[]{:S(2)}, u32[]{:S(2)}) %collective-permute-start.18) | collective-permute-done | bytes 1048608 | tf_op jit(solution)/shard_map/ppermute | solution.py:24
  462.8 3.2 fusion.38
  466.0 4.4 fusion.36
  470.4 3.3 fusion.34
  473.6 14.2 %add_convert_fusion = bf16[640,2048]{1,0:T(8,128)(2,1)} fusion(f32[640,2048]{1,0:T(8,128)} %fusion.32, f32[640,2048]{1,0:T(8,128)} %fusion.34, f32[640,2048]{1,0:T(8,128)} %fusion.36, f32[640,2048]{1,0:T(8,128)} %fusion.38, f32[640,2048]{1,0:T(8,128)} %fusion.40, f32[640,2048]{1,0:T(8,128)S(1)} %fusion.44, f32[640,2048]{1,0:T(8,128)} %fusion.42, ...), kind=kOutput, calls=%fused_computation.17 | convolution fusion | flops 681574400 | bytes 40697860 | tf_op jit(solution)/shard_map/dot_general | solution.py:146
  488.7 4.7 collective-permute-done.23
  493.4 3.6 broadcast_select_fusion
  (79 shorter events, 22.5 us)
Async XLA Ops:
  0.0 1.7 copy-start.8
  3.1 30.0 %collective-permute-start.2 = (bf16[320,2048]{1,0:T(8,128)(2,1)}, bf16[320,2048]{1,0:T(8,128)(2,1)}, u32[]{:S(2)}, u32[]{:S(2)}) collective-permute-start(bf16[320,2048]{1,0:T(8,128)(2,1)} %get-tuple-element.6), channel_id=1, source_target_pairs={{0,2},{1,3},{2,0},{3,1},{4,6},{5,7},{6,4},{7,5},{8,10},{9,11},{10,... | collective-permute-start | bytes 3932168 | tf_op jit(solution)/shard_map/ppermute | solution.py:24
  3.3 31.8 %collective-permute-start.1 = (bf16[320,2048]{1,0:T(8,128)(2,1)}, bf16[320,2048]{1,0:T(8,128)(2,1)}, u32[]{:S(2)}, u32[]{:S(2)}) collective-permute-start(bf16[320,2048]{1,0:T(8,128)(2,1)} %get-tuple-element.6), channel_id=1, source_target_pairs={{0,1},{1,0},{2,3},{3,2},{4,5},{5,4},{6,7},{7,6},{8,9},{9,8},{10,11... | collective-permute-start | bytes 3932168 | tf_op jit(solution)/shard_map/ppermute | solution.py:24
  33.0 29.0 %collective-permute-start.3 = (bf16[320,2048]{1,0:T(8,128)(2,1)}, bf16[320,2048]{1,0:T(8,128)(2,1)}, u32[]{:S(2)}, u32[]{:S(2)}) collective-permute-start(bf16[320,2048]{1,0:T(8,128)(2,1)} %collective-permute-done.2), channel_id=1, source_target_pairs={{0,1},{1,0},{2,3},{3,2},{4,5},{5,4},{6,7},{7,6},{8,9},{9,8},{10,11... | collective-permute-start | bytes 3932168 | tf_op jit(solution)/shard_map/ppermute | solution.py:24
  63.5 3.2 copy-start.3
  66.8 78.7 %collective-permute-start.4 = (bf16[2,2,320,2048]{3,2,1,0:T(8,128)(2,1)}, bf16[2,2,320,2048]{3,2,1,0:T(8,128)(2,1)}, u32[]{:S(2)}, u32[]{:S(2)}) collective-permute-start(bf16[2,2,320,2048]{3,2,1,0:T(8,128)(2,1)} %pad_maximum_fusion), channel_id=1, source_target_pairs={{0,16},{1,17},{2,18},{3,19},{4,20},{5,21},{6,22},{7,23},{8,24},{9,... | collective-permute-start | bytes 15728648 | tf_op jit(solution)/shard_map/ppermute | solution.py:24
  71.5 0.8 copy-start.6
  71.8 1.8 copy-start.4
  71.8 37.2 %copy-start.9 = (f32[1,4096]{1,0:T(1,128)S(1)}, f32[1,4096]{1,0:T(1,128)}, u32[]{:S(2)}) copy-start(f32[1,4096]{1,0:T(1,128)} %param.7) | copy-start | bytes 49156
  71.9 36.2 %collective-permute-start.5 = (bf16[512,1536]{1,0:T(8,128)(2,1)S(1)}, bf16[512,1536]{1,0:T(8,128)(2,1)}, u32[]{:S(2)}, u32[]{:S(2)}) collective-permute-start(bf16[512,1536]{1,0:T(8,128)(2,1)S(1)} %pad_maximum_fusion.3), channel_id=1, source_target_pairs={{0,2},{1,3},{2,0},{3,1},{4,6},{5,7},{6,4},{7,5},{8,10},{9,11},{10,... | collective-permute-start | bytes 4718600 | tf_op jit(solution)/shard_map/ppermute | solution.py:24
  73.6 39.3 %collective-permute-start.6 = (bf16[512,1536]{1,0:T(8,128)(2,1)}, bf16[512,1536]{1,0:T(8,128)(2,1)}, u32[]{:S(2)}, u32[]{:S(2)}) collective-permute-start(bf16[512,1536]{1,0:T(8,128)(2,1)} %pad_maximum_fusion.2), channel_id=1, source_target_pairs={{0,4},{1,5},{2,6},{3,7},{4,8},{5,9},{6,10},{7,11},{8,12},{9,13},{1... | collective-permute-start | bytes 4718600 | tf_op jit(solution)/shard_map/ppermute | solution.py:24
  108.1 37.3 %collective-permute-start.10 = (bf16[512,1536]{1,0:T(8,128)(2,1)}, bf16[512,1536]{1,0:T(8,128)(2,1)}, u32[]{:S(2)}, u32[]{:S(2)}) collective-permute-start(bf16[512,1536]{1,0:T(8,128)(2,1)} %collective-permute-done.5), channel_id=1, source_target_pairs={{0,12},{1,13},{2,14},{3,15},{4,0},{5,1},{6,2},{7,3},{8,4},{9,5},{1... | collective-permute-start | bytes 4718600 | tf_op jit(solution)/shard_map/ppermute | solution.py:24
  108.3 122.9 %collective-permute-start.8 = (bf16[512,1536]{1,0:T(8,128)(2,1)}, bf16[512,1536]{1,0:T(8,128)(2,1)}, u32[]{:S(2)}, u32[]{:S(2)}) collective-permute-start(bf16[512,1536]{1,0:T(8,128)(2,1)} %pad_maximum_fusion.2), channel_id=1, source_target_pairs={{0,12},{1,13},{2,14},{3,15},{4,0},{5,1},{6,2},{7,3},{8,4},{9,5},{1... | collective-permute-start | bytes 4718600 | tf_op jit(solution)/shard_map/ppermute | solution.py:24
  109.7 151.9 %collective-permute-start.9 = (bf16[512,1536]{1,0:T(8,128)(2,1)}, bf16[512,1536]{1,0:T(8,128)(2,1)}, u32[]{:S(2)}, u32[]{:S(2)}) collective-permute-start(bf16[512,1536]{1,0:T(8,128)(2,1)} %collective-permute-done.5), channel_id=1, source_target_pairs={{0,4},{1,5},{2,6},{3,7},{4,8},{5,9},{6,10},{7,11},{8,12},{9,13},{1... | collective-permute-start | bytes 4718600 | tf_op jit(solution)/shard_map/ppermute | solution.py:24
  112.9 135.4 %collective-permute-start.7 = (bf16[512,1536]{1,0:T(8,128)(2,1)}, bf16[512,1536]{1,0:T(8,128)(2,1)}, u32[]{:S(2)}, u32[]{:S(2)}) collective-permute-start(bf16[512,1536]{1,0:T(8,128)(2,1)} %collective-permute-done.6), channel_id=1, source_target_pairs={{0,4},{1,5},{2,6},{3,7},{4,8},{5,9},{6,10},{7,11},{8,12},{9,13},{1... | collective-permute-start | bytes 4718600 | tf_op jit(solution)/shard_map/ppermute | solution.py:24
  145.5 134.8 %collective-permute-start.11 = (bf16[512,1536]{1,0:T(8,128)(2,1)}, bf16[512,1536]{1,0:T(8,128)(2,1)}, u32[]{:S(2)}, u32[]{:S(2)}) collective-permute-start(bf16[512,1536]{1,0:T(8,128)(2,1)} %collective-permute-done.10), channel_id=1, source_target_pairs={{0,12},{1,13},{2,14},{3,15},{4,0},{5,1},{6,2},{7,3},{8,4},{9,5},{1... | collective-permute-start | bytes 4718600 | tf_op jit(solution)/shard_map/ppermute | solution.py:24
  149.5 2.4 copy-start
  149.6 3.9 copy-start.1
  209.0 10.4 %copy-start.5 = (bf16[512,512]{1,0:T(8,128)(2,1)S(1)}, bf16[512,512]{1,0:T(8,128)(2,1)}, u32[]{:S(2)}) copy-start(bf16[512,512]{1,0:T(8,128)(2,1)} %copy-done.4) | copy-start | bytes 1572868
  209.0 10.4 %copy-start.7 = (bf16[512,512]{1,0:T(8,128)(2,1)S(1)}, bf16[512,512]{1,0:T(8,128)(2,1)}, u32[]{:S(2)}) copy-start(bf16[512,512]{1,0:T(8,128)(2,1)} %copy-done.6) | copy-start | bytes 1572868
  219.4 4.4 copy-start.2
  285.5 4.0 copy-start.10
  287.8 7.0 %collective-permute-start.12 = (bf16[640,1536]{0,1:T(8,128)(2,1)}, bf16[640,1536]{0,1:T(8,128)(2,1)}, u32[]{:S(2)}, u32[]{:S(2)}) collective-permute-start(bf16[640,1536]{0,1:T(8,128)(2,1)} %bitcast.123), channel_id=1, source_target_pairs={{0,16},{1,17},{2,18},{3,19},{4,20},{5,21},{6,22},{7,23},{8,24},{9,... | collective-permute-start | bytes 5898248 | tf_op jit(solution)/shard_map/ppermute | solution.py:24
  289.5 2.5 collective-permute-start
  301.7 0.7 collective-permute-start.13
  302.4 12.4 %collective-permute-start.14 = (bf16[640,512]{0,1:T(8,128)(2,1)S(1)}, bf16[640,512]{0,1:T(8,128)(2,1)S(1)}, u32[]{:S(2)}, u32[]{:S(2)}) collective-permute-start(bf16[640,512]{0,1:T(8,128)(2,1)S(1)} %collective-permute-done.13), channel_id=1, source_target_pairs={{0,1},{1,0},{2,3},{3,2},{4,5},{5,4},{6,7},{7,6},{8,9},{9,8},{10,11... | collective-permute-start | bytes 1966088 | tf_op jit(solution)/shard_map/ppermute | solution.py:24
  302.7 34.4 %collective-permute-start.16 = (bf16[256,2048]{1,0:T(8,128)(2,1)}, bf16[256,2048]{1,0:T(8,128)(2,1)}, u32[]{:S(2)}, u32[]{:S(2)}) collective-permute-start(bf16[256,2048]{1,0:T(8,128)(2,1)} %bitcast.39), channel_id=1, source_target_pairs={{0,2},{1,3},{2,0},{3,1},{4,6},{5,7},{6,4},{7,5},{8,10},{9,11},{10,... | collective-permute-start | bytes 3145736 | tf_op jit(solution)/shard_map/ppermute | solution.py:24
  314.9 82.2 %collective-permute-start.15 = (bf16[2,640,512]{1,2,0:T(8,128)(2,1)S(1)}, bf16[2,640,512]{1,2,0:T(8,128)(2,1)S(1)}, u32[]{:S(2)}, u32[]{:S(2)}) collective-permute-start(bf16[2,640,512]{1,2,0:T(8,128)(2,1)S(1)} %bitcast_dynamic-update-slice_fusion.4), channel_id=1, source_target_pairs={{0,16},{1,17},{2,18},{3,19},{4,20},{5,21},{6,22},{7,23},{8,24},{9,... | collective-permute-start | bytes 3932168 | tf_op jit(solution)/shard_map/ppermute | solution.py:24
  325.5 70.0 %collective-permute-start.17 = (bf16[256,2048]{1,0:T(8,128)(2,1)}, bf16[256,2048]{1,0:T(8,128)(2,1)}, u32[]{:S(2)}, u32[]{:S(2)}) collective-permute-start(bf16[256,2048]{1,0:T(8,128)(2,1)} %bitcast.39), channel_id=1, source_target_pairs={{0,4},{1,5},{2,6},{3,7},{4,8},{5,9},{6,10},{7,11},{8,12},{9,13},{1... | collective-permute-start | bytes 3145736 | tf_op jit(solution)/shard_map/ppermute | solution.py:24
  337.1 58.4 %collective-permute-start.21 = (bf16[256,2048]{1,0:T(8,128)(2,1)}, bf16[256,2048]{1,0:T(8,128)(2,1)}, u32[]{:S(2)}, u32[]{:S(2)}) collective-permute-start(bf16[256,2048]{1,0:T(8,128)(2,1)} %collective-permute-done.16), channel_id=1, source_target_pairs={{0,12},{1,13},{2,14},{3,15},{4,0},{5,1},{6,2},{7,3},{8,4},{9,5},{1... | collective-permute-start | bytes 3145736 | tf_op jit(solution)/shard_map/ppermute | solution.py:24
  337.1 128.9 %collective-permute-start.19 = (bf16[256,2048]{1,0:T(8,128)(2,1)}, bf16[256,2048]{1,0:T(8,128)(2,1)}, u32[]{:S(2)}, u32[]{:S(2)}) collective-permute-start(bf16[256,2048]{1,0:T(8,128)(2,1)} %bitcast.39), channel_id=1, source_target_pairs={{0,12},{1,13},{2,14},{3,15},{4,0},{5,1},{6,2},{7,3},{8,4},{9,5},{1... | collective-permute-start | bytes 3145736 | tf_op jit(solution)/shard_map/ppermute | solution.py:24
  337.1 133.3 %collective-permute-start.20 = (bf16[256,2048]{1,0:T(8,128)(2,1)}, bf16[256,2048]{1,0:T(8,128)(2,1)S(1)}, u32[]{:S(2)}, u32[]{:S(2)}) collective-permute-start(bf16[256,2048]{1,0:T(8,128)(2,1)} %collective-permute-done.16), channel_id=1, source_target_pairs={{0,4},{1,5},{2,6},{3,7},{4,8},{5,9},{6,10},{7,11},{8,12},{9,13},{1... | collective-permute-start | bytes 3145736 | tf_op jit(solution)/shard_map/ppermute | solution.py:24
  395.5 67.3 %collective-permute-start.18 = (bf16[256,2048]{1,0:T(8,128)(2,1)}, bf16[256,2048]{1,0:T(8,128)(2,1)S(1)}, u32[]{:S(2)}, u32[]{:S(2)}) collective-permute-start(bf16[256,2048]{1,0:T(8,128)(2,1)} %collective-permute-done.17), channel_id=1, source_target_pairs={{0,4},{1,5},{2,6},{3,7},{4,8},{5,9},{6,10},{7,11},{8,12},{9,13},{1... | collective-permute-start | bytes 3145736 | tf_op jit(solution)/shard_map/ppermute | solution.py:24
  395.5 78.2 %collective-permute-start.22 = (bf16[256,2048]{1,0:T(8,128)(2,1)}, bf16[256,2048]{1,0:T(8,128)(2,1)}, u32[]{:S(2)}, u32[]{:S(2)}) collective-permute-start(bf16[256,2048]{1,0:T(8,128)(2,1)} %collective-permute-done.21), channel_id=1, source_target_pairs={{0,12},{1,13},{2,14},{3,15},{4,0},{5,1},{6,2},{7,3},{8,4},{9,5},{1... | collective-permute-start | bytes 3145736 | tf_op jit(solution)/shard_map/ppermute | solution.py:24
  487.8 5.6 %collective-permute-start.23 = (bf16[640,2048]{1,0:T(8,128)(2,1)}, bf16[640,2048]{1,0:T(8,128)(2,1)S(1)}, u32[]{:S(2)}, u32[]{:S(2)}) collective-permute-start(bf16[640,2048]{1,0:T(8,128)(2,1)} %add_convert_fusion), channel_id=1, source_target_pairs={{0,16},{1,17},{2,18},{3,19},{4,20},{5,21},{6,22},{7,23},{8,24},{9,... | collective-permute-start | bytes 7864328 | tf_op jit(solution)/shard_map/ppermute | solution.py:24

commit v2 on v0

v2 whole, which is shorter than its diff:
```python
import jax
import jax.numpy as jnp
from jax import lax
from jax.experimental import pallas as pl
from jax.experimental.pallas import tpu as pltpu
from jax.sharding import PartitionSpec as P

HDIM = 128
AXES = ("mod", "dp", "tensor")
VMEM = 50 * 1024 * 1024
F32, BF16, I32 = jnp.float32, jnp.bfloat16, jnp.int32


def make_move(mesh):
    mods, rings, shards = mesh.shape["mod"], mesh.shape["dp"] // 2, mesh.shape["tensor"]

    def flat(m, z, y, x):
        return (m * rings * 2 + z * 2 + y) * shards + x

    def move(array, where):
        pairs = [
            (flat(m, z, y, x), flat(*where(m, z, y, x)))
            for m in range(mods)
            for z in range(rings)
            for y in range(2)
            for x in range(shards)
        ]
        return lax.ppermute(array, AXES, pairs)

    return move


def after(array, *earlier):
    return lax.optimization_barrier((array,) + earlier)[0]


def call(kernel, grid, in_specs, out_specs, out_shape, prefetch, args, flops, aliases=None, moved=0):
    outs = jax.tree.leaves(out_shape)
    moved = moved or sum(a.size * a.dtype.itemsize for a in list(args) + outs)
    return pl.pallas_call(
        kernel,
        grid_spec=pltpu.PrefetchScalarGridSpec(
            num_scalar_prefetch=1, grid=grid, in_specs=in_specs, out_specs=out_specs
        ),
        out_shape=out_shape,
        input_output_aliases=aliases or {},
        cost_estimate=pl.CostEstimate(flops=flops, bytes_accessed=moved, transcendentals=0),
        compiler_params=pltpu.CompilerParams(vmem_limit_bytes=VMEM),
    )(prefetch, *args)


def halves(weight, y):
    kinds, depth, width = weight.shape
    half, tile = width // 2, min(depth, 128)

    def kernel(y_ref, in_ref, own_ref, other_ref):
        low, high = in_ref[:, :, :half], in_ref[:, :, half:]
        first = y_ref[0] == 0
        own_ref[...] = jnp.where(first, low, high)
        other_ref[...] = jnp.where(first, high, low)

    out = jax.ShapeDtypeStruct((kinds, depth, half), weight.dtype)
    spec = pl.BlockSpec((kinds, tile, half), lambda i, y: (0, i, 0))
    return call(
        kernel,
        (depth // tile,),
        [pl.BlockSpec((kinds, tile, width), lambda i, y: (0, i, 0))],
        [spec, spec],
        [out, out],
        y.reshape(1),
        [weight],
        0,
    )


def normalize(places, held, gains, mine, theirs, shape, start, kept):
    slots, blocks, length, _ = shape
    shards = len(mine)
    count, features = mine[0].shape
    tile = 80 if count % 80 == 0 else count
    steps, half = count // tile, length // 2
    per = features // kept

    def kernel(p_ref, *refs):
        refs = refs[1:] if held is not None else refs
        gain_ref, out_ref = refs[0], refs[-1]
        core, own = p_ref[0], p_ref[1]

        def write(group):
            wide = [ref[...].astype(F32) for ref in group]
            total = sum(jnp.sum(w * w, axis=-1, keepdims=True) for w in wide)
            inverse = lax.rsqrt(total / (shards * features) + 1e-05)
            for step, w in enumerate(wide):
                shard = lax.rem(own - step + shards, shards)
                for i in range(per):
                    block = shard * per + i
                    part = w[:, i * kept : (i + 1) * kept] * inverse * gain_ref[block]
                    out_ref[0, block] = part.astype(BF16)

        @pl.when(pl.program_id(0) == core)
        def _():
            write(refs[1 : 1 + shards])

        @pl.when(pl.program_id(0) != core)
        def _():
            write(refs[1 + shards : 1 + 2 * shards])

    own_spec = pl.BlockSpec(
        (tile, features), lambda h, i, p: (jnp.where(h == p[0], i, jnp.where(h == 0, 0, steps - 1)), 0)
    )
    other_spec = pl.BlockSpec(
        (tile, features), lambda h, i, p: (jnp.where(h != p[0], i, jnp.where(h == 0, 0, steps - 1)), 0)
    )
    in_specs = [pl.BlockSpec((blocks, 1, kept), lambda h, i, p: (0, 0, 0))]
    in_specs += [own_spec] * shards + [other_spec] * shards
    args = [gains] + list(mine) + list(theirs)
    if held is not None:
        in_specs = [pl.BlockSpec(memory_space=pl.ANY)] + in_specs
        args = [held] + args
    out_spec = pl.BlockSpec(
        (1, blocks, tile, kept), lambda h, i, p: (p[2], 0, (h * half + start) // tile + i, 0)
    )
    return call(
        kernel,
        (2, steps),
        in_specs,
        out_spec,
        jax.ShapeDtypeStruct(shape, BF16),
        places,
        args,
        0,
        {1: 0} if held is not None else None,
        moved=8 * count * features * shards,
    )


def project(places, normed, blocks, total, final, fresh):
    slots, _, length, kept = normed.shape
    kinds, _, width = blocks[0].shape
    tile = min(width, 256)
    per = width // tile
    count = len(blocks)

    def kernel(p_ref, *refs):
        out_ref = refs[-1]
        summed = None if fresh else refs[2 * count][0]
        for i in range(count):
            part = jnp.dot(refs[i][0, 0], refs[count + i][0], preferred_element_type=F32)
            summed = part if summed is None else summed + part
        if final:
            out_ref[...] = summed.astype(BF16)
        else:
            out_ref[0] = summed

    def columns(i):
        return pl.BlockSpec((1, 1, length, kept), lambda n, p: (p[0], p[1 + i], 0, 0))

    total_spec = pl.BlockSpec((1, length, tile), lambda n, p: (p[0], 0, n))
    in_specs = [columns(i) for i in range(count)]
    in_specs += [pl.BlockSpec((1, kept, tile), lambda n, p: (n // per, 0, n % per))] * count
    args = [normed] * count + list(blocks)
    if total is not None:
        in_specs.append(pl.BlockSpec(memory_space=pl.ANY) if fresh else total_spec)
        args.append(total)
    aliases = None
    if final:
        out_spec = pl.BlockSpec((length, tile), lambda n, p: (0, n))
        out_shape = jax.ShapeDtypeStruct((length, kinds * width), BF16)
    else:
        out_spec, out_shape = total_spec, jax.ShapeDtypeStruct((slots, length, kinds * width), F32)
        if total is not None:
            aliases = {1 + 2 * count: 0}
    return call(
        kernel,
        (kinds * per,),
        in_specs,
        out_spec,
        out_shape,
        places,
        args,
        2 * count * length * kept * kinds * width,
        aliases,
        moved=2 * count * kept * (length + kinds * width) + 4 * length * kinds * width,
    )


def attend(own, got, mine):
    length, width = own.shape[0], own.shape[1] // 3
    heads = width // HDIM
    scale = HDIM ** (-0.5)
    tile = 128 if length % 128 == 0 else length

    def kernel(_, mine_ref, qo, ko, vo, qg, kg, vg, out_ref):
        keep = mine_ref[...] != 0

        def pick(a, b):
            return jnp.where(keep, a[...].astype(F32), b[...].astype(F32)).astype(BF16)

        query, key, value = pick(qo, qg), pick(ko, kg), pick(vo, vg)
        for i in range(length // tile):
            low, high = i * tile, (i + 1) * tile
            scores = lax.dot_general(
                query[low:high], key[:high], (((1,), (1,)), ((), ())), preferred_element_type=F32
            )
            rows = low + lax.broadcasted_iota(I32, (tile, high), 0)
            cols = lax.broadcasted_iota(I32, (tile, high), 1)
            scores = jnp.where(cols <= rows, scores * scale, -jnp.inf)
            top = jnp.max(scores, axis=-1, keepdims=True)
            raised = jnp.exp(scores - top)
            probs = (raised / jnp.sum(raised, axis=-1, keepdims=True)).astype(BF16)
            out = jnp.dot(probs, value[:high], preferred_element_type=F32)
            out_ref[low:high, :] = out.astype(BF16)

    def part(j):
        return pl.BlockSpec((length, HDIM), lambda h, p: (0, j * heads + h))

    return call(
        kernel,
        (heads,),
        [pl.BlockSpec((length, 1), lambda h, p: (0, 0))] + [part(0), part(1), part(2)] * 2,
        pl.BlockSpec((length, HDIM), lambda h, p: (0, h)),
        jax.ShapeDtypeStruct((length, width), BF16),
        jnp.zeros((1,), I32),
        [mine, own, own, own, got, got, got],
        4 * length * length * width,
    )


def combine(places, pieces, blocks, total, final):
    _, length, width = pieces.shape
    held, features = blocks[0][0].shape
    tile = min(features, 512)
    count = len(blocks)

    def kernel(p_ref, *refs):
        out_ref = refs[-1]
        summed = None if total is None else refs[3 * count][...]
        first = p_ref[0] == 0
        for i in range(count):
            low, high = refs[i][0, :, :held], refs[i][0, :, held:]
            near, far = jnp.where(first, low, high), jnp.where(first, high, low)
            part = jnp.dot(near, refs[count + 2 * i][...], preferred_element_type=F32)
            part += jnp.dot(far, refs[count + 2 * i + 1][...], preferred_element_type=F32)
            summed = part if summed is None else summed + part
        out_ref[...] = summed.astype(out_ref.dtype)

    def piece(i):
        return pl.BlockSpec((1, length, width), lambda n, p: (p[1 + i], 0, 0))

    total_spec = pl.BlockSpec((length, tile), lambda n, p: (0, n))
    in_specs = [piece(i) for i in range(count)]
    in_specs += [pl.BlockSpec((held, tile), lambda n, p: (0, n))] * (2 * count)
    args = [pieces] * count + [b for pair in blocks for b in pair]
    if total is not None:
        in_specs.append(total_spec)
        args.append(total)
    return call(
        kernel,
        (features // tile,),
        in_specs,
        total_spec,
        jax.ShapeDtypeStruct((length, features), BF16 if final else F32),
        places,
        args,
        2 * count * length * width * features,
        moved=2 * count * width * (length + features) + 4 * length * features,
    )


def solution(mesh):
    rings, shards = mesh.shape["dp"] // 2, mesh.shape["tensor"]
    move = make_move(mesh)

    def to_core(array):
        return move(array, lambda m, z, y, x: (1 - m, z, y, x))

    def to_pair(array):
        return move(array, lambda m, z, y, x: (m, z, 1 - y, x))

    def around(array, step):
        return move(array, lambda m, z, y, x: (m, (z + step) % rings, y, x))

    def over_tensor(array):
        return [array] + [
            move(array, lambda m, z, y, x: (m, z, y, (x + step) % shards))
            for step in range(1, shards)
        ]

    def ring(own, pair, begin):
        mid, rest = rings // 2, rings - 1 - rings // 2
        found, last = {}, []
        for step, counts in ((1, (mid, rest)), (-1, (rest, mid))):
            held, before = [own, pair], begin
            for hop in range(1, mid + 1):
                for kind in range(2):
                    if hop <= counts[kind]:
                        held[kind] = around(after(held[kind], *before), step)
                        before = (held[kind],)
                        found[kind, (-step * hop) % rings] = held[kind]
            last += list(before)
        return found, tuple(last)

    def on_device(tokens, modality, norm_gains, qkv_weight, out_weight):
        core = lax.axis_index("mod").astype(I32)
        place = lax.axis_index("dp").astype(I32)
        own = lax.axis_index("tensor").astype(I32)
        z, y = place // 2, place % 2
        length, features = tokens.shape
        kept = qkv_weight.shape[1]
        width = qkv_weight.shape[3] // 2
        half, quarter = length // 2, length // 4
        which = core ^ y

        own_block, away_block = halves(qkv_weight[0].transpose(1, 0, 2), y)
        pair_block = to_pair(away_block)
        found, ring_end = ring(own_block, pair_block, ())

        rows = lax.dynamic_slice_in_dim(tokens, core * half, half, 0)
        rest_rows = lax.dynamic_slice_in_dim(tokens, (1 - core) * half, half, 0)
        fetched = over_tensor(rows)
        swapped = [rest_rows] + [to_core(a) for a in fetched[1:]]
        gains = norm_gains[0].reshape(2 * rings, 1, kept)
        shape = (2, 2 * rings, length, kept)
        normed = normalize(
            jnp.stack([core, own, which]), None, gains, fetched, swapped, shape, 0, kept
        )
        before = pair_block
        behind = fetched[-1]
        for start in (0, quarter):
            part = to_pair(after(lax.slice_in_dim(rows, start, start + quarter, axis=0), before))
            before = part
            part = over_tensor(after(part, behind))
            behind = part[-1]
            normed = normalize(
                jnp.stack([core, own, 1 - which]),
                normed,
                gains,
                part,
                [to_core(a) for a in part],
                shape,
                start,
                kept,
            )
        y_end = before

        def index(kind, distance):
            return 2 * ((z + distance) % rings) + (y if kind == 0 else 1 - y)

        tags = {(0, 0): own_block, (1, 0): pair_block, **found}
        far = [t for t in ((0, rings // 2), (1, rings // 2)) if t in found]
        early = [t for t in tags if t not in far and (t[1] == 0 or (t[0] == 0 and t[1] in (1, rings - 1)))]
        middle = [t for t in tags if t not in early and t not in far]

        def add(slot, group, total, final=False, fresh=False):
            places = jnp.stack([slot] + [index(*t) for t in group]).astype(I32)
            return project(places, normed, [tags[t] for t in group], total, final, fresh)

        total = add(which, early, None, fresh=True)
        if middle:
            total = add(which, middle, total)
        total = add(1 - which, early + middle, total, fresh=True)
        zero = jnp.zeros((), I32)
        theirs = add(zero + 1, far, total, final=True)
        got = to_core(theirs)
        ours = add(zero, far, total, final=True)

        kinds = jnp.stack([modality, to_pair(modality)])
        kind = lax.dynamic_index_in_dim(kinds, which, 0, keepdims=False)
        attended = attend(ours, got, (kind == core).astype(I32)[:, None])

        attended = move(
            attended, lambda m, z, y, x: (m, z, y, x) if m == y else (1 - m, z, 1 - y, x)
        )
        held = over_tensor(attended)
        pieces = jnp.concatenate([jnp.stack(held), jnp.stack([to_core(a) for a in held])])

        own_out = after(out_weight[0], y_end)
        pair_out = to_pair(own_out)
        found, _ = ring(own_out, pair_out, ring_end)
        tags_out = {(0, 0): own_out, (1, 0): pair_out, **found}
        far_out = [rings // 2]
        near_out = [k for k in range(rings) if k not in far_out]

        def gather(group, total, final):
            found_at = []
            for distance in group:
                piece = (z + distance) % rings
                shard, part = piece // 2, piece % 2
                found_at.append(
                    jnp.where(part == core, 0, shards) + (own - shard + shards) % shards
                )
            places = jnp.stack([y] + found_at).astype(I32)
            blocks = [(tags_out[0, k], tags_out[1, k]) for k in group]
            return combine(places, pieces, blocks, total, final)

        result = gather(far_out, gather(near_out, None, False), True)
        return jnp.where((modality == core)[:, None], result, to_core(result))

    return jax.shard_map(
        on_device,
        mesh=mesh,
        in_specs=(
            P("dp", "tensor"),
            P("dp"),
            P("mod", None),
            P("mod", "dp", None, "tensor"),
            P("mod", "dp", "tensor"),
        ),
        out_specs=P("dp", "tensor"),
        check_vma=False,
    )
```

time: 771 us -> 385 us (0.50)
  waiting for transfers between devices: 688 us -> 226 us
  Pallas kernels: 0 us -> 93 us
  matrix products: 46.3 us -> 0 us
  starting transfers between devices: 0.16 us -> 44.6 us
  between operations: 13.2 us -> 0.13 us
    all_gather x4 -> x0, waiting for transfers between devices: 662 us -> none  [the longest x1 478 us: on_device(): weight_piece = lax.all_gather(qkv_weight, 'dp', axis=1, tiled=True)]
    ppermute x1 -> x31, waiting for transfers between devices: 2.64 us -> 226 us  [move(): return lax.ppermute(array, AXES, pairs)]
    pallas_call x0 -> x12, Pallas kernels: none -> 93 us  [call(): pl.pallas_call(kernel, grid_spec=pltpu.PrefetchScalarGridSpec(num_scalar_...]
    ppermute x1 -> x31, starting transfers between devices: 0.01 us -> 44.6 us  [move(): return lax.ppermute(array, AXES, pairs)]
    dot_general x3 -> x0, matrix products: 40 us -> none  [the longest x1 21.7 us: on_device(): jnp.dot(columns, weight_piece[0].reshape(count, 3 * local_width), preferr...]
    psum x1 -> x0, waiting for transfers between devices: 22.3 us -> none  [on_device(): combined = lax.psum(placed.astype(jnp.float32).astype(jnp.bfloat16), 'mod')]
  transfers between devices with their start and end apart: 6 -> 31, of which waited for: 6 -> 16; matrix products, arithmetic and copies ran while one was open for 7% -> 2% of each run, Pallas kernels for 0% -> 20%
where the time goes in v2:
time: 385 us; the launch traced here: 384 us
  waiting for transfers between devices  226 us (59%)
  Pallas kernels  93 us (24%)
  starting transfers between devices  44.6 us (12%)
  local copies, waits for them, and re-layouts  12.5 us (3%)
  other arithmetic  7.62 us (2%)
    ppermute x31, waiting for transfers between devices, move(): return lax.ppermute(array, AXES, pairs)  226 us
    pallas_call x12, Pallas kernels, call(): pl.pallas_call(kernel, grid_spec=pltpu.PrefetchScalarGridSpec(num_scalar_...  93 us
    ppermute x31, starting transfers between devices, move(): return lax.ppermute(array, AXES, pairs)  44.6 us
  transfers between devices with their start and end apart: 31, of which 16 were waited for; matrix products, arithmetic and copies ran while one was open for 2% of the time, Pallas kernels for 20%

profile of v2, /device:TPU:0, one launch (start us, length us, event | category | flops | bytes accessed | tf_op | source)
XLA Modules:
  0.0 383.7 jit_solution(4168717101386560511)
XLA Ops:
  0.0 4.0 %shard_map.56 = (bf16[3,512,512]{2,1,0:T(8,128)(2,1)S(1)}, bf16[3,512,512]{2,1,0:T(8,128)(2,1)}) custom-call(s32[1]{0:T(128)} %bitcast.y_ref, bf16[3,512,1024]{2,1,0:T(8,128)(2,1)} %bitcast.31), custom_call_target="tpu_custom_call" | custom-call | bytes 6291456 | tf_op jit(solution)/shard_map/pallas_call | solution.py:40
  4.0 3.0 collective-permute-start.3
  7.0 1.6 collective-permute-start.12
  8.5 2.2 collective-permute-start.15
  10.8 3.5 constant_dynamic-slice_fusion.2
  14.3 1.5 collective-permute-start.1
  17.2 24.3 %collective-permute-done.3.refs_5_.refs_7_ = bf16[3,512,512]{2,1,0:T(8,128)(2,1)S(1)} collective-permute-done((bf16[3,512,512]{2,1,0:T(8,128)(2,1)}, bf16[3,512,512]{2,1,0:T(8,128)(2,1)S(1)}, u32[]{:S(2)}, u32[]{:S(2)}) %collective-permute-start.3) | collective-permute-done | bytes 1572896 | tf_op jit(solution)/shard_map/ppermute | solution.py:28
  41.6 1.7 collective-permute-start.4
  43.3 2.9 collective-permute-done.12.refs_6_.refs_8_
  46.2 32.5 %collective-permute-done.15.refs_7_.refs_9_ = bf16[3,512,512]{2,1,0:T(8,128)(2,1)} collective-permute-done((bf16[3,512,512]{2,1,0:T(8,128)(2,1)S(1)}, bf16[3,512,512]{2,1,0:T(8,128)(2,1)}, u32[]{:S(2)}, u32[]{:S(2)}) %collective-permute-start.15) | collective-permute-done | bytes 1572896 | tf_op jit(solution)/shard_map/ppermute | solution.py:28
  78.7 2.8 collective-permute-start.16
  82.7 1.5 collective-permute-start.5
  84.7 12.2 %collective-permute-done.5.refs_3_ = bf16[160,2048]{1,0:T(8,128)(2,1)} collective-permute-done((bf16[160,2048]{1,0:T(8,128)(2,1)}, bf16[160,2048]{1,0:T(8,128)(2,1)}, u32[]{:S(2)}, u32[]{:S(2)}) %collective-permute-start.5) | collective-permute-done | bytes 655392 | tf_op jit(solution)/shard_map/ppermute | solution.py:28
  97.6 1.5 collective-permute-start.9
  99.1 15.2 %collective-permute-done.13.refs_2_.refs_10_ = bf16[3,512,512]{2,1,0:T(8,128)(2,1)S(1)} collective-permute-done((bf16[3,512,512]{2,1,0:T(8,128)(2,1)S(1)}, bf16[3,512,512]{2,1,0:T(8,128)(2,1)S(1)}, u32[]{:S(2)}, u32[]{:S(2)}) %collective-permute-start.13) | collective-permute-done | bytes 1572896 | tf_op jit(solution)/shard_map/ppermute | solution.py:28
  115.5 30.4 %collective-permute-done.16.refs_3_.refs_11_ = bf16[3,512,512]{2,1,0:T(8,128)(2,1)S(1)} collective-permute-done((bf16[3,512,512]{2,1,0:T(8,128)(2,1)S(1)}, bf16[3,512,512]{2,1,0:T(8,128)(2,1)S(1)}, u32[]{:S(2)}, u32[]{:S(2)}) %collective-permute-start.16) | collective-permute-done | bytes 1572896 | tf_op jit(solution)/shard_map/ppermute | solution.py:28
  149.1 3.3 collective-permute-start.17
  154.0 8.3 %shard_map.55.refs_0_ = bf16[2,8,640,512]{3,2,1,0:T(8,128)(2,1)} custom-call(s32[3]{0:T(128)S(1)} %pad_add_fusion.3.p_ref, f32[8,1,512]{2,1,0:T(1,128)S(1)} %bitcast.28, bf16[320,2048]{1,0:T(8,128)(2,1)} %get-tuple-element.40.refs_1_, bf16[320,2048]{1,0:T(8,128)(2,1)} %collective-permute-done.1.refs_2_, bf16[320,2048]{1,0:T(8,128)(2,1)S(1)} %copy-done.9, ...), custom_call_target="tpu_custom_call" | custom-call | bytes 10485760 | tf_op jit(solution)/shard_map/pallas_call | solution.py:40
  162.3 5.1 %shard_map.57.refs_0_ = bf16[2,8,640,512]{3,2,1,0:T(8,128)(2,1)} custom-call(s32[3]{0:T(128)S(1)} %pad_add_fusion.1.p_ref, bf16[2,8,640,512]{3,2,1,0:T(8,128)(2,1)} %shard_map.55.refs_0_, f32[8,1,512]{2,1,0:T(1,128)S(1)} %bitcast.29, bf16[160,2048]{1,0:T(8,128)(2,1)} %collective-permute-done.4.refs_2_, ...), custom_call_target="tpu_custom_call", output_to_operand_aliasing={{}: (1, {})} | custom-call | bytes 5242880 | tf_op jit(solution)/shard_map/pallas_call | solution.py:40
  167.4 5.5 %shard_map.58.refs_0_.refs_1_.refs_2_.refs_3_.refs_4_.refs_5_ = bf16[2,8,640,512]{3,2,1,0:T(8,128)(2,1)} custom-call(s32[3]{0:T(128)S(1)} %pad_add_fusion.1.p_ref, bf16[2,8,640,512]{3,2,1,0:T(8,128)(2,1)} %shard_map.57.refs_0_, f32[8,1,512]{2,1,0:T(1,128)S(1)} %bitcast.30, ...), custom_call_target="tpu_custom_call", output_to_operand_aliasing={{}: (1, {})} | custom-call | bytes 5242880 | tf_op jit(solution)/shard_map/pallas_call | solution.py:40
  173.0 9.8 %shard_map.59.refs_4_ = f32[2,640,1536]{2,1,0:T(8,128)} custom-call(s32[5]{0:T(128)S(1)} %stack.140.p_ref, bf16[2,8,640,512]{3,2,1,0:T(8,128)(2,1)} %shard_map.58.refs_0_.refs_1_.refs_2_.refs_3_.refs_4_.refs_5_, bf16[2,8,640,512]{3,2,1,0:T(8,128)(2,1)} %shard_map.58.refs_0_.refs_1_.refs_2_.refs_3_.refs_4_.refs_5_, ...), custom_call_target="tpu_custom_call" | custom-call | flops 4026531840 | bytes 12845056 | tf_op jit(solution)/shard_map/pallas_call | solution.py:40
  182.8 8.0 %shard_map.60.refs_12_ = f32[2,640,1536]{2,1,0:T(8,128)} custom-call(s32[3]{0:T(128)S(1)} %pad_add_fusion.4.p_ref, bf16[2,8,640,512]{3,2,1,0:T(8,128)(2,1)} %shard_map.58.refs_0_.refs_1_.refs_2_.refs_3_.refs_4_.refs_5_, bf16[2,8,640,512]{3,2,1,0:T(8,128)(2,1)} %shard_map.58.refs_0_.refs_1_.refs_2_.refs_3_.refs_4_.refs_5_, ...), custom_call_target="tpu_custom_call", output_to_operand_aliasing={{}: (5, {})} | custom-call | flops 2013265920 | bytes 8388608 | tf_op jit(solution)/shard_map/pallas_call | solution.py:40
  190.7 11.7 %shard_map.61.refs_4_ = f32[2,640,1536]{2,1,0:T(8,128)} custom-call(s32[7]{0:T(128)S(1)} %stack.138.p_ref, bf16[2,8,640,512]{3,2,1,0:T(8,128)(2,1)} %shard_map.58.refs_0_.refs_1_.refs_2_.refs_3_.refs_4_.refs_5_, bf16[2,8,640,512]{3,2,1,0:T(8,128)(2,1)} %shard_map.58.refs_0_.refs_1_.refs_2_.refs_3_.refs_4_.refs_5_, ...), custom_call_target="tpu_custom_call", output_to_operand_aliasing={{}: (13, {})} | custom-call | flops 6039797760 | bytes 17301504 | tf_op jit(solution)/shard_map/pallas_call | solution.py:40
  202.4 16.6 %collective-permute-done.17.refs_3_ = bf16[3,512,512]{2,1,0:T(8,128)(2,1)S(1)} collective-permute-done((bf16[3,512,512]{2,1,0:T(8,128)(2,1)}, bf16[3,512,512]{2,1,0:T(8,128)(2,1)S(1)}, u32[]{:S(2)}, u32[]{:S(2)}) %collective-permute-start.17) | collective-permute-done | bytes 1572896 | tf_op jit(solution)/shard_map/ppermute | solution.py:28
  219.1 7.6 %shard_map.63 = bf16[640,1536]{1,0:T(8,128)(2,1)} custom-call(s32[3]{0:T(128)S(1)} %add_add_fusion.1.p_ref, bf16[2,8,640,512]{3,2,1,0:T(8,128)(2,1)} %shard_map.58.refs_0_.refs_1_.refs_2_.refs_3_.refs_4_.refs_5_, bf16[2,8,640,512]{3,2,1,0:T(8,128)(2,1)} %shard_map.58.refs_0_.refs_1_.refs_2_.refs_3_.refs_4_.refs_5_, ...), custom_call_target="tpu_custom_call" | custom-call | flops 2013265920 | bytes 8388608 | tf_op jit(solution)/shard_map/pallas_call | solution.py:40
  228.4 2.6 collective-permute-start.27
  231.0 1.5 collective-permute-start
  232.6 20.0 %collective-permute-done = s32[640]{0:T(1024)S(1)} collective-permute-done((s32[640]{0:T(1024)S(1)}, s32[640]{0:T(1024)S(1)}, u32[]{:S(2)}, u32[]{:S(2)}) %collective-permute-start) | collective-permute-done | bytes 2592 | tf_op jit(solution)/shard_map/ppermute | solution.py:28
  252.8 7.5 %shard_map.62.qo.ko.vo = bf16[640,1536]{1,0:T(8,128)(2,1)} custom-call(s32[3]{0:T(128)S(1)} %add_add_fusion.p_ref, bf16[2,8,640,512]{3,2,1,0:T(8,128)(2,1)} %shard_map.58.refs_0_.refs_1_.refs_2_.refs_3_.refs_4_.refs_5_, bf16[2,8,640,512]{3,2,1,0:T(8,128)(2,1)} %shard_map.58.refs_0_.refs_1_.refs_2_.refs_3_.refs_4_.refs_5_, ...), custom_call_target="tpu_custom_call" | custom-call | flops 2013265920 | bytes 8388608 | tf_op jit(solution)/shard_map/pallas_call | solution.py:40
  260.4 1.5 copy-done
  261.9 9.8 %shard_map.64 = bf16[640,512]{1,0:T(8,128)(2,1)S(1)} custom-call(s32[1]{0:T(128)} %constant.161.clone.1._, s32[640,1]{1,0:T(8,128)S(1)} %copy.10.mine_ref, bf16[640,1536]{1,0:T(8,128)(2,1)S(1)} %copy-done, bf16[640,1536]{1,0:T(8,128)(2,1)S(1)} %copy-done, bf16[640,1536]{1,0:T(8,128)(2,1)S(1)} %copy-done, bf16[640,1536]{1,0:T(8,128)(2,1)} %collective-permute-done.18.qg.kg.vg, ...), custom_call_target="tpu_custom_call" | custom-call | flops 838860800 | bytes 12454400 | tf_op jit(solution)/shard_map/pallas_call | solution.py:40
  271.7 1.5 collective-permute-start.19
  274.4 1.8 collective-permute-done.27.refs_5_
  276.2 2.1 collective-permute-start.28
  278.3 1.5 collective-permute-start.20
  279.8 5.2 %collective-permute-start.21 = (bf16[640,512]{1,0:T(8,128)(2,1)}, bf16[640,512]{1,0:T(8,128)(2,1)}, u32[]{:S(2)}, u32[]{:S(2)}) collective-permute-start(bf16[640,512]{1,0:T(8,128)(2,1)} %collective-permute-done.19), channel_id=1, source_target_pairs={{0,16},{1,17},{2,18},{3,19},{4,20},{5,21},{6,22},{7,23},{8,24},{9,... | collective-permute-start | bytes 1966088 | tf_op jit(solution)/shard_map/ppermute | solution.py:28
  285.0 6.6 %collective-permute-done.20 = bf16[640,512]{1,0:T(8,128)(2,1)} collective-permute-done((bf16[640,512]{1,0:T(8,128)(2,1)}, bf16[640,512]{1,0:T(8,128)(2,1)}, u32[]{:S(2)}, u32[]{:S(2)}) %collective-permute-start.20) | collective-permute-done | bytes 655392 | tf_op jit(solution)/shard_map/ppermute | solution.py:28
  291.6 4.6 %collective-permute-start.22 = (bf16[640,512]{1,0:T(8,128)(2,1)}, bf16[640,512]{1,0:T(8,128)(2,1)}, u32[]{:S(2)}, u32[]{:S(2)}) collective-permute-start(bf16[640,512]{1,0:T(8,128)(2,1)} %collective-permute-done.20), channel_id=1, source_target_pairs={{0,16},{1,17},{2,18},{3,19},{4,20},{5,21},{6,22},{7,23},{8,24},{9,... | collective-permute-start | bytes 1966088 | tf_op jit(solution)/shard_map/ppermute | solution.py:28
  296.2 5.0 %collective-permute-done.25.refs_8_ = bf16[256,2048]{1,0:T(8,128)(2,1)S(1)} collective-permute-done((bf16[256,2048]{1,0:T(8,128)(2,1)}, bf16[256,2048]{1,0:T(8,128)(2,1)S(1)}, u32[]{:S(2)}, u32[]{:S(2)}) %collective-permute-start.25) | collective-permute-done | bytes 1048608 | tf_op jit(solution)/shard_map/ppermute | solution.py:28
  301.3 21.9 %collective-permute-done.28.refs_6_ = bf16[256,2048]{1,0:T(8,128)(2,1)} collective-permute-done((bf16[256,2048]{1,0:T(8,128)(2,1)}, bf16[256,2048]{1,0:T(8,128)(2,1)}, u32[]{:S(2)}, u32[]{:S(2)}) %collective-permute-start.28) | collective-permute-done | bytes 1048608 | tf_op jit(solution)/shard_map/ppermute | solution.py:28
  323.2 1.9 collective-permute-start.29
  325.2 3.5 pad_maximum_fusion.refs_0_.refs_1_.refs_2_
  328.7 9.4 %shard_map.65.refs_3_ = f32[640,2048]{1,0:T(8,128)} custom-call(s32[4]{0:T(128)S(1)} %pad_add_fusion.5.p_ref, bf16[4,640,512]{2,1,0:T(8,128)(2,1)} %pad_maximum_fusion.refs_0_.refs_1_.refs_2_, bf16[4,640,512]{2,1,0:T(8,128)(2,1)} %pad_maximum_fusion.refs_0_.refs_1_.refs_2_, bf16[4,640,512]{2,1,0:T(8,128)(2,1)} %pad_maximum_fusion.refs_0_.refs_1_.refs_2_, ...), custom_call_target="tpu_custom_call" | custom-call | flops 4026531840 | bytes 13500416 | tf_op jit(solution)/shard_map/pallas_call | solution.py:40
  338.1 8.2 %collective-permute-done.26.refs_1_ = bf16[256,2048]{1,0:T(8,128)(2,1)S(1)} collective-permute-done((bf16[256,2048]{1,0:T(8,128)(2,1)}, bf16[256,2048]{1,0:T(8,128)(2,1)S(1)}, u32[]{:S(2)}, u32[]{:S(2)}) %collective-permute-start.26) | collective-permute-done | bytes 1048608 | tf_op jit(solution)/shard_map/ppermute | solution.py:28
  346.3 22.5 %collective-permute-done.29.refs_2_ = bf16[256,2048]{1,0:T(8,128)(2,1)S(1)} collective-permute-done((bf16[256,2048]{1,0:T(8,128)(2,1)}, bf16[256,2048]{1,0:T(8,128)(2,1)S(1)}, u32[]{:S(2)}, u32[]{:S(2)}) %collective-permute-start.29) | collective-permute-done | bytes 1048608 | tf_op jit(solution)/shard_map/ppermute | solution.py:28
  368.7 6.3 %shard_map.66 = bf16[640,2048]{1,0:T(8,128)(2,1)} custom-call(s32[2]{0:T(128)S(1)} %pad_add_fusion.p_ref, bf16[4,640,512]{2,1,0:T(8,128)(2,1)} %pad_maximum_fusion.refs_0_.refs_1_.refs_2_, bf16[256,2048]{1,0:T(8,128)(2,1)S(1)} %collective-permute-done.26.refs_1_, bf16[256,2048]{1,0:T(8,128)(2,1)S(1)} %collective-permute-done.29.refs_2_, ...), custom_call_target="tpu_custom_call" | custom-call | flops 1342177280 | bytes 7995392 | tf_op jit(solution)/shard_map/pallas_call | solution.py:40
  375.1 5.1 %collective-permute-done.30 = bf16[640,2048]{1,0:T(8,128)(2,1)S(1)} collective-permute-done((bf16[640,2048]{1,0:T(8,128)(2,1)}, bf16[640,2048]{1,0:T(8,128)(2,1)S(1)}, u32[]{:S(2)}, u32[]{:S(2)}) %collective-permute-start.30) | collective-permute-done | bytes 2621472 | tf_op jit(solution)/shard_map/ppermute | solution.py:28
  380.2 3.6 broadcast_select_fusion
  (74 shorter events, 13.3 us)
Async XLA Ops:
  4.0 10.3 %copy-start.1 = (bf16[3,512,512]{2,1,0:T(8,128)(2,1)}, bf16[3,512,512]{2,1,0:T(8,128)(2,1)S(1)}, u32[]{:S(2)}) copy-start(bf16[3,512,512]{2,1,0:T(8,128)(2,1)S(1)} %get-tuple-element.26.refs_4_.refs_6_) | copy-start | bytes 4718596
  4.0 37.6 %collective-permute-start.3 = (bf16[3,512,512]{2,1,0:T(8,128)(2,1)}, bf16[3,512,512]{2,1,0:T(8,128)(2,1)S(1)}, u32[]{:S(2)}, u32[]{:S(2)}) collective-permute-start(bf16[3,512,512]{2,1,0:T(8,128)(2,1)} %get-tuple-element.21), channel_id=1, source_target_pairs={{0,2},{1,3},{2,0},{3,1},{4,6},{5,7},{6,4},{7,5},{8,10},{9,11},{10,... | collective-permute-start | bytes 4718600 | tf_op jit(solution)/shard_map/ppermute | solution.py:28
  7.0 39.3 %collective-permute-start.12 = (bf16[3,512,512]{2,1,0:T(8,128)(2,1)S(1)}, bf16[3,512,512]{2,1,0:T(8,128)(2,1)}, u32[]{:S(2)}, u32[]{:S(2)}) collective-permute-start(bf16[3,512,512]{2,1,0:T(8,128)(2,1)S(1)} %get-tuple-element.26.refs_4_.refs_6_), channel_id=1, source_target_pairs={{0,4},{1,5},{2,6},{3,7},{4,8},{5,9},{6,10},{7,11},{8,12},{9,13},{1... | collective-permute-start | bytes 4718600 | tf_op jit(solution)/shard_map/ppermute | solution.py:28
  8.5 70.2 %collective-permute-start.15 = (bf16[3,512,512]{2,1,0:T(8,128)(2,1)S(1)}, bf16[3,512,512]{2,1,0:T(8,128)(2,1)}, u32[]{:S(2)}, u32[]{:S(2)}) collective-permute-start(bf16[3,512,512]{2,1,0:T(8,128)(2,1)S(1)} %get-tuple-element.26.refs_4_.refs_6_), channel_id=1, source_target_pairs={{0,12},{1,13},{2,14},{3,15},{4,0},{5,1},{6,2},{7,3},{8,4},{9,5},{1... | collective-permute-start | bytes 4718600 | tf_op jit(solution)/shard_map/ppermute | solution.py:28
  14.3 138.4 %copy-start.12 = (f32[1,4096]{1,0:T(1,128)S(1)}, f32[1,4096]{1,0:T(1,128)}, u32[]{:S(2)}) copy-start(f32[1,4096]{1,0:T(1,128)} %param.7) | copy-start | bytes 49156
  14.3 68.4 %collective-permute-start.1 = (bf16[320,2048]{1,0:T(8,128)(2,1)}, bf16[320,2048]{1,0:T(8,128)(2,1)}, u32[]{:S(2)}, u32[]{:S(2)}) collective-permute-start(bf16[320,2048]{1,0:T(8,128)(2,1)} %get-tuple-element.40.refs_1_), channel_id=1, source_target_pairs={{0,1},{1,0},{2,3},{3,2},{4,5},{5,4},{6,7},{7,6},{8,9},{9,8},{10,11... | collective-permute-start | bytes 3932168 | tf_op jit(solution)/shard_map/ppermute | solution.py:28
  41.6 41.1 %collective-permute-start.4 = (bf16[160,2048]{1,0:T(8,128)(2,1)S(1)}, bf16[160,2048]{1,0:T(8,128)(2,1)}, u32[]{:S(2)}, u32[]{:S(2)}) collective-permute-start(bf16[160,2048]{1,0:T(8,128)(2,1)S(1)} %get-tuple-element.22), channel_id=1, source_target_pairs={{0,2},{1,3},{2,0},{3,1},{4,6},{5,7},{6,4},{7,5},{8,10},{9,11},{10,... | collective-permute-start | bytes 1966088 | tf_op jit(solution)/shard_map/ppermute | solution.py:28
  46.2 68.1 %collective-permute-start.13 = (bf16[3,512,512]{2,1,0:T(8,128)(2,1)S(1)}, bf16[3,512,512]{2,1,0:T(8,128)(2,1)S(1)}, u32[]{:S(2)}, u32[]{:S(2)}) collective-permute-start(bf16[3,512,512]{2,1,0:T(8,128)(2,1)S(1)} %collective-permute-done.3.refs_5_.refs_7_), channel_id=1, source_target_pairs={{0,4},{1,5},{2,6},{3,7},{4,8},{5,9},{6,10},{7,11},{8,12},{9,13},{1... | collective-permute-start | bytes 4718600 | tf_op jit(solution)/shard_map/ppermute | solution.py:28
  78.7 67.1 %collective-permute-start.16 = (bf16[3,512,512]{2,1,0:T(8,128)(2,1)S(1)}, bf16[3,512,512]{2,1,0:T(8,128)(2,1)S(1)}, u32[]{:S(2)}, u32[]{:S(2)}) collective-permute-start(bf16[3,512,512]{2,1,0:T(8,128)(2,1)S(1)} %collective-permute-done.3.refs_5_.refs_7_), channel_id=1, source_target_pairs={{0,12},{1,13},{2,14},{3,15},{4,0},{5,1},{6,2},{7,3},{8,4},{9,5},{1... | collective-permute-start | bytes 4718600 | tf_op jit(solution)/shard_map/ppermute | solution.py:28
  81.5 1.2 copy-start.3
  82.7 14.2 %collective-permute-start.5 = (bf16[160,2048]{1,0:T(8,128)(2,1)}, bf16[160,2048]{1,0:T(8,128)(2,1)}, u32[]{:S(2)}, u32[]{:S(2)}) collective-permute-start(bf16[160,2048]{1,0:T(8,128)(2,1)} %collective-permute-done.4.refs_2_), channel_id=1, source_target_pairs={{0,1},{1,0},{2,3},{3,2},{4,5},{5,4},{6,7},{7,6},{8,9},{9,8},{10,11... | collective-permute-start | bytes 1966088 | tf_op jit(solution)/shard_map/ppermute | solution.py:28
  84.2 13.4 %collective-permute-start.8 = (bf16[160,2048]{1,0:T(8,128)(2,1)S(1)}, bf16[160,2048]{1,0:T(8,128)(2,1)}, u32[]{:S(2)}, u32[]{:S(2)}) collective-permute-start(bf16[160,2048]{1,0:T(8,128)(2,1)S(1)} %get-tuple-element.24), channel_id=1, source_target_pairs={{0,2},{1,3},{2,0},{3,1},{4,6},{5,7},{6,4},{7,5},{8,10},{9,11},{10,... | collective-permute-start | bytes 1966088 | tf_op jit(solution)/shard_map/ppermute | solution.py:28
  84.7 63.0 %collective-permute-start.2 = (bf16[320,2048]{1,0:T(8,128)(2,1)}, bf16[320,2048]{1,0:T(8,128)(2,1)}, u32[]{:S(2)}, u32[]{:S(2)}) collective-permute-start(bf16[320,2048]{1,0:T(8,128)(2,1)} %collective-permute-done.1.refs_2_), channel_id=1, source_target_pairs={{0,16},{1,17},{2,18},{3,19},{4,20},{5,21},{6,22},{7,23},{8,24},{9,... | collective-permute-start | bytes 3932168 | tf_op jit(solution)/shard_map/ppermute | solution.py:28
  97.6 49.4 %collective-permute-start.9 = (bf16[160,2048]{1,0:T(8,128)(2,1)}, bf16[160,2048]{1,0:T(8,128)(2,1)}, u32[]{:S(2)}, u32[]{:S(2)}) collective-permute-start(bf16[160,2048]{1,0:T(8,128)(2,1)} %collective-permute-done.8.refs_2_), channel_id=1, source_target_pairs={{0,1},{1,0},{2,3},{3,2},{4,5},{5,4},{6,7},{7,6},{8,9},{9,8},{10,11... | collective-permute-start | bytes 1966088 | tf_op jit(solution)/shard_map/ppermute | solution.py:28
  99.1 49.2 %collective-permute-start.6 = (bf16[160,2048]{1,0:T(8,128)(2,1)}, bf16[160,2048]{1,0:T(8,128)(2,1)S(1)}, u32[]{:S(2)}, u32[]{:S(2)}) collective-permute-start(bf16[160,2048]{1,0:T(8,128)(2,1)} %collective-permute-done.4.refs_2_), channel_id=1, source_target_pairs={{0,16},{1,17},{2,18},{3,19},{4,20},{5,21},{6,22},{7,23},{8,24},{9,... | collective-permute-start | bytes 1966088 | tf_op jit(solution)/shard_map/ppermute | solution.py:28
  114.3 1.2 copy-start.5
  115.5 46.9 %collective-permute-start.7 = (bf16[160,2048]{1,0:T(8,128)(2,1)}, bf16[160,2048]{1,0:T(8,128)(2,1)}, u32[]{:S(2)}, u32[]{:S(2)}) collective-permute-start(bf16[160,2048]{1,0:T(8,128)(2,1)} %collective-permute-done.5.refs_3_), channel_id=1, source_target_pairs={{0,16},{1,17},{2,18},{3,19},{4,20},{5,21},{6,22},{7,23},{8,24},{9,... | collective-permute-start | bytes 1966088 | tf_op jit(solution)/shard_map/ppermute | solution.py:28
  145.8 1.1 copy-start.7
  147.0 20.4 %collective-permute-start.10 = (bf16[160,2048]{1,0:T(8,128)(2,1)}, bf16[160,2048]{1,0:T(8,128)(2,1)}, u32[]{:S(2)}, u32[]{:S(2)}) collective-permute-start(bf16[160,2048]{1,0:T(8,128)(2,1)} %collective-permute-done.8.refs_2_), channel_id=1, source_target_pairs={{0,16},{1,17},{2,18},{3,19},{4,20},{5,21},{6,22},{7,23},{8,24},{9,... | collective-permute-start | bytes 1966088 | tf_op jit(solution)/shard_map/ppermute | solution.py:28
  147.0 20.4 %collective-permute-start.11 = (bf16[160,2048]{1,0:T(8,128)(2,1)}, bf16[160,2048]{1,0:T(8,128)(2,1)}, u32[]{:S(2)}, u32[]{:S(2)}) collective-permute-start(bf16[160,2048]{1,0:T(8,128)(2,1)} %collective-permute-done.9.refs_3_), channel_id=1, source_target_pairs={{0,16},{1,17},{2,18},{3,19},{4,20},{5,21},{6,22},{7,23},{8,24},{9,... | collective-permute-start | bytes 1966088 | tf_op jit(solution)/shard_map/ppermute | solution.py:28
  147.7 54.8 %collective-permute-start.14 = (bf16[3,512,512]{2,1,0:T(8,128)(2,1)}, bf16[3,512,512]{2,1,0:T(8,128)(2,1)S(1)}, u32[]{:S(2)}, u32[]{:S(2)}) collective-permute-start(bf16[3,512,512]{2,1,0:T(8,128)(2,1)} %collective-permute-done.12.refs_6_.refs_8_), channel_id=1, source_target_pairs={{0,4},{1,5},{2,6},{3,7},{4,8},{5,9},{6,10},{7,11},{8,12},{9,13},{1... | collective-permute-start | bytes 4718600 | tf_op jit(solution)/shard_map/ppermute | solution.py:28
  148.3 0.9 copy-start.10
  149.1 70.0 %collective-permute-start.17 = (bf16[3,512,512]{2,1,0:T(8,128)(2,1)}, bf16[3,512,512]{2,1,0:T(8,128)(2,1)S(1)}, u32[]{:S(2)}, u32[]{:S(2)}) collective-permute-start(bf16[3,512,512]{2,1,0:T(8,128)(2,1)} %copy-done.7), channel_id=1, source_target_pairs={{0,12},{1,13},{2,14},{3,15},{4,0},{5,1},{6,2},{7,3},{8,4},{9,5},{1... | collective-permute-start | bytes 4718600 | tf_op jit(solution)/shard_map/ppermute | solution.py:28
  152.7 1.3 copy-start.9
  154.0 8.3 %copy-start.11 = (bf16[160,2048]{1,0:T(8,128)(2,1)S(1)}, bf16[160,2048]{1,0:T(8,128)(2,1)}, u32[]{:S(2)}) copy-start(bf16[160,2048]{1,0:T(8,128)(2,1)} %copy-done.10) | copy-start | bytes 1966084
  167.4 5.5 %copy-start.2 = (bf16[3,512,512]{2,1,0:T(8,128)(2,1)S(1)}, bf16[3,512,512]{2,1,0:T(8,128)(2,1)}, u32[]{:S(2)}) copy-start(bf16[3,512,512]{2,1,0:T(8,128)(2,1)} %copy-done.1) | copy-start | bytes 4718596
  167.4 5.5 %copy-start.4 = (bf16[3,512,512]{2,1,0:T(8,128)(2,1)S(1)}, bf16[3,512,512]{2,1,0:T(8,128)(2,1)}, u32[]{:S(2)}) copy-start(bf16[3,512,512]{2,1,0:T(8,128)(2,1)} %copy-done.3) | copy-start | bytes 4718596
  172.9 9.8 %copy-start.6 = (bf16[3,512,512]{2,1,0:T(8,128)(2,1)S(1)}, bf16[3,512,512]{2,1,0:T(8,128)(2,1)}, u32[]{:S(2)}) copy-start(bf16[3,512,512]{2,1,0:T(8,128)(2,1)} %copy-done.5) | copy-start | bytes 4718596
  173.0 9.8 %copy-start.8 = (bf16[3,512,512]{2,1,0:T(8,128)(2,1)S(1)}, bf16[3,512,512]{2,1,0:T(8,128)(2,1)}, u32[]{:S(2)}) copy-start(bf16[3,512,512]{2,1,0:T(8,128)(2,1)} %copy-done.7) | copy-start | bytes 4718596
  202.4 28.6 %copy-start.14 = (s32[640]{0:T(1024)S(1)}, s32[640]{0:T(1024)}, u32[]{:S(2)}) copy-start(s32[640]{0:T(1024)} %param.6) | copy-start | bytes 7684
  226.7 33.7 %collective-permute-start.18 = (bf16[640,1536]{1,0:T(8,128)(2,1)}, bf16[640,1536]{1,0:T(8,128)(2,1)}, u32[]{:S(2)}, u32[]{:S(2)}) collective-permute-start(bf16[640,1536]{1,0:T(8,128)(2,1)} %shard_map.63), channel_id=1, source_target_pairs={{0,16},{1,17},{2,18},{3,19},{4,20},{5,21},{6,22},{7,23},{8,24},{9,... | collective-permute-start | bytes 5898248 | tf_op jit(solution)/shard_map/ppermute | solution.py:28
  226.7 46.5 %collective-permute-start.24 = (bf16[256,2048]{1,0:T(8,128)(2,1)}, bf16[256,2048]{1,0:T(8,128)(2,1)}, u32[]{:S(2)}, u32[]{:S(2)}) collective-permute-start(bf16[256,2048]{1,0:T(8,128)(2,1)} %bitcast.22.refs_3_), channel_id=1, source_target_pairs={{0,2},{1,3},{2,0},{3,1},{4,6},{5,7},{6,4},{7,5},{8,10},{9,11},{10,... | collective-permute-start | bytes 3145736 | tf_op jit(solution)/shard_map/ppermute | solution.py:28
  227.2 46.0 %collective-permute-start.23 = (bf16[256,2048]{1,0:T(8,128)(2,1)}, bf16[256,2048]{1,0:T(8,128)(2,1)}, u32[]{:S(2)}, u32[]{:S(2)}) collective-permute-start(bf16[256,2048]{1,0:T(8,128)(2,1)} %bitcast.22.refs_3_), channel_id=1, source_target_pairs={{0,4},{1,5},{2,6},{3,7},{4,8},{5,9},{6,10},{7,11},{8,12},{9,13},{1... | collective-permute-start | bytes 3145736 | tf_op jit(solution)/shard_map/ppermute | solution.py:28
  228.4 47.8 %collective-permute-start.27 = (bf16[256,2048]{1,0:T(8,128)(2,1)}, bf16[256,2048]{1,0:T(8,128)(2,1)}, u32[]{:S(2)}, u32[]{:S(2)}) collective-permute-start(bf16[256,2048]{1,0:T(8,128)(2,1)} %bitcast.22.refs_3_), channel_id=1, source_target_pairs={{0,12},{1,13},{2,14},{3,15},{4,0},{5,1},{6,2},{7,3},{8,4},{9,5},{1... | collective-permute-start | bytes 3145736 | tf_op jit(solution)/shard_map/ppermute | solution.py:28
  231.0 21.6 %collective-permute-start = (s32[640]{0:T(1024)S(1)}, s32[640]{0:T(1024)S(1)}, u32[]{:S(2)}, u32[]{:S(2)}) collective-permute-start(s32[640]{0:T(1024)S(1)} %copy-done.14), channel_id=1, source_target_pairs={{0,2},{1,3},{2,0},{3,1},{4,6},{5,7},{6,4},{7,5},{8,10},{9,11},{10,... | collective-permute-start | bytes 7688 | tf_op jit(solution)/shard_map/ppermute | solution.py:28
  260.4 1.5 copy-start
  271.7 6.6 %collective-permute-start.19 = (bf16[640,512]{1,0:T(8,128)(2,1)S(1)}, bf16[640,512]{1,0:T(8,128)(2,1)}, u32[]{:S(2)}, u32[]{:S(2)}) collective-permute-start(bf16[640,512]{1,0:T(8,128)(2,1)S(1)} %shard_map.64), channel_id=1, source_target_pairs={{0,0},{1,1},{2,16},{3,17},{4,4},{5,5},{6,20},{7,21},{8,8},{9,9},{1... | collective-permute-start | bytes 1966088 | tf_op jit(solution)/shard_map/ppermute | solution.py:28
  273.2 28.1 %collective-permute-start.25 = (bf16[256,2048]{1,0:T(8,128)(2,1)}, bf16[256,2048]{1,0:T(8,128)(2,1)S(1)}, u32[]{:S(2)}, u32[]{:S(2)}) collective-permute-start(bf16[256,2048]{1,0:T(8,128)(2,1)} %collective-permute-done.24.refs_4_), channel_id=1, source_target_pairs={{0,4},{1,5},{2,6},{3,7},{4,8},{5,9},{6,10},{7,11},{8,12},{9,13},{1... | collective-permute-start | bytes 3145736 | tf_op jit(solution)/shard_map/ppermute | solution.py:28
  276.2 47.0 %collective-permute-start.28 = (bf16[256,2048]{1,0:T(8,128)(2,1)}, bf16[256,2048]{1,0:T(8,128)(2,1)}, u32[]{:S(2)}, u32[]{:S(2)}) collective-permute-start(bf16[256,2048]{1,0:T(8,128)(2,1)} %collective-permute-done.24.refs_4_), channel_id=1, source_target_pairs={{0,12},{1,13},{2,14},{3,15},{4,0},{5,1},{6,2},{7,3},{8,4},{9,5},{1... | collective-permute-start | bytes 3145736 | tf_op jit(solution)/shard_map/ppermute | solution.py:28
  278.3 13.3 %collective-permute-start.20 = (bf16[640,512]{1,0:T(8,128)(2,1)}, bf16[640,512]{1,0:T(8,128)(2,1)}, u32[]{:S(2)}, u32[]{:S(2)}) collective-permute-start(bf16[640,512]{1,0:T(8,128)(2,1)} %collective-permute-done.19), channel_id=1, source_target_pairs={{0,1},{1,0},{2,3},{3,2},{4,5},{5,4},{6,7},{7,6},{8,9},{9,8},{10,11... | collective-permute-start | bytes 1966088 | tf_op jit(solution)/shard_map/ppermute | solution.py:28
  279.8 45.4 %collective-permute-start.21 = (bf16[640,512]{1,0:T(8,128)(2,1)}, bf16[640,512]{1,0:T(8,128)(2,1)}, u32[]{:S(2)}, u32[]{:S(2)}) collective-permute-start(bf16[640,512]{1,0:T(8,128)(2,1)} %collective-permute-done.19), channel_id=1, source_target_pairs={{0,16},{1,17},{2,18},{3,19},{4,20},{5,21},{6,22},{7,23},{8,24},{9,... | collective-permute-start | bytes 1966088 | tf_op jit(solution)/shard_map/ppermute | solution.py:28
  291.6 33.6 %collective-permute-start.22 = (bf16[640,512]{1,0:T(8,128)(2,1)}, bf16[640,512]{1,0:T(8,128)(2,1)}, u32[]{:S(2)}, u32[]{:S(2)}) collective-permute-start(bf16[640,512]{1,0:T(8,128)(2,1)} %collective-permute-done.20), channel_id=1, source_target_pairs={{0,16},{1,17},{2,18},{3,19},{4,20},{5,21},{6,22},{7,23},{8,24},{9,... | collective-permute-start | bytes 1966088 | tf_op jit(solution)/shard_map/ppermute | solution.py:28
  301.3 27.5 %copy-start.13 = (bf16[256,2048]{1,0:T(8,128)(2,1)}, bf16[256,2048]{1,0:T(8,128)(2,1)S(1)}, u32[]{:S(2)}) copy-start(bf16[256,2048]{1,0:T(8,128)(2,1)S(1)} %collective-permute-done.25.refs_8_) | copy-start | bytes 3145732
  301.3 45.0 %collective-permute-start.26 = (bf16[256,2048]{1,0:T(8,128)(2,1)}, bf16[256,2048]{1,0:T(8,128)(2,1)S(1)}, u32[]{:S(2)}, u32[]{:S(2)}) collective-permute-start(bf16[256,2048]{1,0:T(8,128)(2,1)} %collective-permute-done.23.refs_7_), channel_id=1, source_target_pairs={{0,4},{1,5},{2,6},{3,7},{4,8},{5,9},{6,10},{7,11},{8,12},{9,13},{1... | collective-permute-start | bytes 3145736 | tf_op jit(solution)/shard_map/ppermute | solution.py:28
  323.2 45.5 %collective-permute-start.29 = (bf16[256,2048]{1,0:T(8,128)(2,1)}, bf16[256,2048]{1,0:T(8,128)(2,1)S(1)}, u32[]{:S(2)}, u32[]{:S(2)}) collective-permute-start(bf16[256,2048]{1,0:T(8,128)(2,1)} %collective-permute-done.28.refs_6_), channel_id=1, source_target_pairs={{0,12},{1,13},{2,14},{3,15},{4,0},{5,1},{6,2},{7,3},{8,4},{9,5},{1... | collective-permute-start | bytes 3145736 | tf_op jit(solution)/shard_map/ppermute | solution.py:28
  375.1 5.1 %collective-permute-start.30 = (bf16[640,2048]{1,0:T(8,128)(2,1)}, bf16[640,2048]{1,0:T(8,128)(2,1)S(1)}, u32[]{:S(2)}, u32[]{:S(2)}) collective-permute-start(bf16[640,2048]{1,0:T(8,128)(2,1)} %shard_map.66), channel_id=1, source_target_pairs={{0,16},{1,17},{2,18},{3,19},{4,20},{5,21},{6,22},{7,23},{8,24},{9,... | collective-permute-start | bytes 7864328 | tf_op jit(solution)/shard_map/ppermute | solution.py:28

commit v3 on v2

v3 whole, which is shorter than its diff:
```python
import jax
import jax.numpy as jnp
from jax import lax
from jax.experimental import pallas as pl
from jax.experimental.pallas import tpu as pltpu
from jax.sharding import PartitionSpec as P

HDIM = 128
AXES = ("mod", "dp", "tensor")
VMEM = 50 * 1024 * 1024
F32, BF16, I32 = jnp.float32, jnp.bfloat16, jnp.int32


def after(array, *earlier):
    return lax.optimization_barrier((array,) + earlier)[0]


def call(kernel, grid, in_specs, out_specs, out_shape, prefetch, args, flops, aliases=None, moved=0):
    outs = jax.tree.leaves(out_shape)
    moved = moved or sum(a.size * a.dtype.itemsize for a in list(args) + outs)
    return pl.pallas_call(
        kernel,
        grid_spec=pltpu.PrefetchScalarGridSpec(
            num_scalar_prefetch=1, grid=grid, in_specs=in_specs, out_specs=out_specs
        ),
        out_shape=out_shape,
        input_output_aliases=aliases or {},
        cost_estimate=pl.CostEstimate(flops=flops, bytes_accessed=moved, transcendentals=0),
        compiler_params=pltpu.CompilerParams(vmem_limit_bytes=VMEM),
    )(prefetch, *args)


def halves(weight, outer, chunks):
    kinds, depth, width = weight.shape
    half, rows = width // 2, depth // chunks

    def kernel(o_ref, in_ref, low_ref, high_ref, mine_ref, away_ref):
        low, high = in_ref[:, :, :half], in_ref[:, :, half:]
        first = o_ref[0] == 1
        low_ref[...] = low
        high_ref[...] = high
        mine_ref[...] = jnp.where(first, low, high)
        away_ref[...] = jnp.where(first, high, low)

    tile = min(rows, 64)
    out = jax.ShapeDtypeStruct((kinds, rows, half), weight.dtype)
    spec = pl.BlockSpec((kinds, tile, half), lambda i, o: (0, i, 0))
    found = []
    for chunk in range(chunks):
        first = chunk * (rows // tile)
        found.append(
            call(
                kernel,
                (rows // tile,),
                [pl.BlockSpec((kinds, tile, width), lambda i, o, first=first: (0, first + i, 0))],
                [spec] * 4,
                [out] * 4,
                outer.reshape(1).astype(I32),
                [weight],
                0,
                moved=6 * kinds * rows * width,
            )
        )
    return found


def normalize(places, held, gains, mine, theirs, shape, start, kept):
    slots, blocks, length, _ = shape
    shards = len(mine)
    count, features = mine[0].shape
    tile = 80 if count % 80 == 0 else count
    steps, half = count // tile, length // 2
    per = features // kept

    def kernel(p_ref, *refs):
        refs = refs[1:] if held is not None else refs
        gain_ref, out_ref = refs[0], refs[-1]
        core, own = p_ref[0], p_ref[1]

        def write(group):
            wide = [ref[...].astype(F32) for ref in group]
            total = sum(jnp.sum(w * w, axis=-1, keepdims=True) for w in wide)
            inverse = lax.rsqrt(total / (shards * features) + 1e-05)
            for step, w in enumerate(wide):
                shard = lax.rem(own - step + shards, shards)
                for i in range(per):
                    block = shard * per + i
                    part = w[:, i * kept : (i + 1) * kept] * inverse * gain_ref[block]
                    out_ref[0, block] = part.astype(BF16)

        @pl.when(pl.program_id(0) == core)
        def _():
            write(refs[1 : 1 + shards])

        @pl.when(pl.program_id(0) != core)
        def _():
            write(refs[1 + shards : 1 + 2 * shards])

    own_spec = pl.BlockSpec(
        (tile, features), lambda h, i, p: (jnp.where(h == p[0], i, jnp.where(h == 0, 0, steps - 1)), 0)
    )
    other_spec = pl.BlockSpec(
        (tile, features), lambda h, i, p: (jnp.where(h != p[0], i, jnp.where(h == 0, 0, steps - 1)), 0)
    )
    in_specs = [pl.BlockSpec((blocks, 1, kept), lambda h, i, p: (0, 0, 0))]
    in_specs += [own_spec] * shards + [other_spec] * shards
    args = [gains] + list(mine) + list(theirs)
    if held is not None:
        in_specs = [pl.BlockSpec(memory_space=pl.ANY)] + in_specs
        args = [held] + args
    out_spec = pl.BlockSpec(
        (1, blocks, tile, kept), lambda h, i, p: (p[2], 0, (h * half + start) // tile + i, 0)
    )
    return call(
        kernel,
        (2, steps),
        in_specs,
        out_spec,
        jax.ShapeDtypeStruct(shape, BF16),
        places,
        args,
        0,
        {1: 0} if held is not None else None,
        moved=8 * count * features * shards,
    )


def project(places, normed, blocks, total, final, fresh):
    slots, _, length, kept = normed.shape
    kinds, _, width = blocks[0].shape
    tile = min(width, 256)
    per = width // tile
    count = len(blocks)

    def kernel(p_ref, *refs):
        out_ref = refs[-1]
        summed = None if fresh else refs[2 * count][0]
        for i in range(count):
            part = jnp.dot(refs[i][0, 0], refs[count + i][0], preferred_element_type=F32)
            summed = part if summed is None else summed + part
        if final:
            out_ref[...] = summed.astype(BF16)
        else:
            out_ref[0] = summed

    def columns(i):
        return pl.BlockSpec((1, 1, length, kept), lambda n, p: (p[0], p[1 + i], 0, 0))

    total_spec = pl.BlockSpec((1, length, tile), lambda n, p: (p[0], 0, n))
    in_specs = [columns(i) for i in range(count)]
    in_specs += [pl.BlockSpec((1, kept, tile), lambda n, p: (n // per, 0, n % per))] * count
    args = [normed] * count + list(blocks)
    if total is not None:
        in_specs.append(pl.BlockSpec(memory_space=pl.ANY) if fresh else total_spec)
        args.append(total)
    aliases = None
    if final:
        out_spec = pl.BlockSpec((length, tile), lambda n, p: (0, n))
        out_shape = jax.ShapeDtypeStruct((length, kinds * width), BF16)
    else:
        out_spec, out_shape = total_spec, jax.ShapeDtypeStruct((slots, length, kinds * width), F32)
        if total is not None:
            aliases = {1 + 2 * count: 0}
    return call(
        kernel,
        (kinds * per,),
        in_specs,
        out_spec,
        out_shape,
        places,
        args,
        2 * count * length * kept * kinds * width,
        aliases,
        moved=2 * count * kept * (length + kinds * width) + 4 * length * kinds * width,
    )


def attend(own, got, mine):
    length, width = own.shape[0], own.shape[1] // 3
    heads = width // HDIM
    scale = HDIM ** (-0.5)
    tile = 128 if length % 128 == 0 else length

    def kernel(_, mine_ref, qo, ko, vo, qg, kg, vg, out_ref):
        keep = mine_ref[...] != 0

        def pick(a, b):
            return jnp.where(keep, a[...].astype(F32), b[...].astype(F32)).astype(BF16)

        query, key, value = pick(qo, qg), pick(ko, kg), pick(vo, vg)
        for i in range(length // tile):
            low, high = i * tile, (i + 1) * tile
            scores = lax.dot_general(
                query[low:high], key[:high], (((1,), (1,)), ((), ())), preferred_element_type=F32
            )
            rows = low + lax.broadcasted_iota(I32, (tile, high), 0)
            cols = lax.broadcasted_iota(I32, (tile, high), 1)
            scores = jnp.where(cols <= rows, scores * scale, -jnp.inf)
            top = jnp.max(scores, axis=-1, keepdims=True)
            raised = jnp.exp(scores - top)
            probs = (raised / jnp.sum(raised, axis=-1, keepdims=True)).astype(BF16)
            out = jnp.dot(probs, value[:high], preferred_element_type=F32)
            out_ref[low:high, :] = out.astype(BF16)

    def part(j):
        return pl.BlockSpec((length, HDIM), lambda h, p: (0, j * heads + h))

    return call(
        kernel,
        (heads,),
        [pl.BlockSpec((length, 1), lambda h, p: (0, 0))] + [part(0), part(1), part(2)] * 2,
        pl.BlockSpec((length, HDIM), lambda h, p: (0, h)),
        jax.ShapeDtypeStruct((length, width), BF16),
        jnp.zeros((1,), I32),
        [mine, own, own, own, got, got, got],
        4 * length * length * width,
    )


def combine(places, pieces, blocks, total, final):
    _, _, length, width = pieces.shape
    _, held, features = blocks[0].shape
    tile = min(features, 256)
    count = len(blocks)
    cut = held % 128 == 0

    def kernel(p_ref, *refs):
        out_ref = refs[-1]
        summed = None if total is None else refs[2 * count][...]
        for i in range(count):
            if cut:
                columns = refs[i][0, 0]
            else:
                whole = refs[i][0, 0]
                columns = jnp.where(p_ref[2 + 2 * i] == 0, whole[:, :held], whole[:, held:])
            part = jnp.dot(columns, refs[count + i][0], preferred_element_type=F32)
            summed = part if summed is None else summed + part
        out_ref[...] = summed.astype(out_ref.dtype)

    def piece(i):
        if cut:
            return pl.BlockSpec(
                (1, 1, length, held), lambda n, p: (p[0], p[1 + 2 * i], 0, p[2 + 2 * i])
            )
        return pl.BlockSpec((1, 1, length, width), lambda n, p: (p[0], p[1 + 2 * i], 0, 0))

    total_spec = pl.BlockSpec((length, tile), lambda n, p: (0, n))
    in_specs = [piece(i) for i in range(count)]
    in_specs += [pl.BlockSpec((1, held, tile), lambda n, p: (0, 0, n))] * count
    args = [pieces] * count + list(blocks)
    if total is not None:
        in_specs.append(total_spec)
        args.append(total)
    return call(
        kernel,
        (features // tile,),
        in_specs,
        total_spec,
        jax.ShapeDtypeStruct((length, features), BF16 if final else F32),
        places,
        args,
        2 * count * length * held * features,
        moved=2 * count * held * (length + features) + 4 * length * features,
    )


def assemble(places, mine, near, near_other, far, far_other):
    length, width = near.shape
    tile = 80 if length % 160 == 0 else length // 2
    steps = length // 2 // tile

    def kernel(p_ref, mine_ref, a_ref, b_ref, c_ref, d_ref, out_ref):
        keep = mine_ref[...] != 0
        own = jnp.where(keep, a_ref[...].astype(F32), b_ref[...].astype(F32)).astype(BF16)
        held = (pl.program_id(0) // steps) == p_ref[0]
        other = jnp.where(held, c_ref[...], d_ref[...])
        first = p_ref[1] == 0
        out_ref[:, :width] = jnp.where(first, own, other)
        out_ref[:, width:] = jnp.where(first, other, own)

    rows = pl.BlockSpec((tile, width), lambda i, p: (i, 0))
    part = pl.BlockSpec((tile, width), lambda i, p: (i % steps, 0))
    return call(
        kernel,
        (2 * steps,),
        [pl.BlockSpec((tile, 1), lambda i, p: (i, 0)), rows, rows, part, part],
        pl.BlockSpec((tile, 2 * width), lambda i, p: (i, 0)),
        jax.ShapeDtypeStruct((length, 2 * width), BF16),
        places,
        [mine, near, near_other, far, far_other],
        0,
    )


def solution(mesh):
    places, shards = mesh.shape["dp"], mesh.shape["tensor"]
    mods = mesh.shape["mod"]
    lined = places == 8

    def move(array, where):
        pairs = []
        for m in range(mods):
            for d in range(places):
                for x in range(shards):
                    to = where(m, d, x)
                    if to is not None:
                        target = (to[0] * places + to[1]) * shards + to[2]
                        pairs.append(((m * places + d) * shards + x, target))
        return lax.ppermute(array, AXES, pairs)

    def to_core(array):
        return move(array, lambda m, d, x: (1 - m, d, x))

    def over_tensor(array):
        return [array] + [
            move(array, lambda m, d, x: (m, d, (x + step) % shards)) for step in range(1, shards)
        ]

    def edge(m, d, x):
        return m, d ^ 2, x

    def outward(m, d, x):
        return (m, d ^ 2, x) if d // 2 in (1, 2) else None

    def across(m, d, x):
        return (m, (3 - d // 2) * 2 + d % 2, x) if d // 2 in (1, 2) else None

    def across_or_stay(m, d, x):
        return across(m, d, x) or (m, d, x)

    def pair(m, d, x):
        return m, d ^ 1, x

    class Links:
        def __init__(self, depth):
            self.depth, self.sent = depth, {}

        def send(self, link, array, where):
            sent = self.sent.setdefault(link, [])
            if len(sent) >= self.depth:
                array = after(array, sent[-self.depth])
            sent.append(move(array, where))
            return sent[-1]

    def gather(links, chunks, place, outer, between):
        steps = range(len(chunks))
        z, y = place // 2, place % 2
        if not lined:
            column = (z ^ (z // 2)) & 1
            group = [(place, c, chunks[c][2]) for c in steps]
            for step in range(1, places):
                to = ((place + step) % places) // 2
                same = ((to ^ (to // 2)) & 1) == column
                for c in steps:
                    sent = jnp.where(same, chunks[c][2], chunks[c][3])
                    got = move(sent, lambda m, d, x: (m, (d + step) % places, x))
                    group.append(((place - step) % places, c, got))
            between()
            return [[], group[:-2], group[-2:]]
        send = links.send
        far_inner = jnp.where(z < 2, 2, 1)
        far_outer = 3 - 3 * (z // 2)
        first, second, third, fourth = [], [], [], []
        e1, e2, m1, m2 = [], [], [], []
        for c in steps:
            low, high, mine, away = chunks[c]
            e1.append(send("edge", away, edge))
            m1.append(send("middle", low, across_or_stay))
            first += [(place, c, mine), (place ^ 1, c, send("pair", mine, pair))]
        for c in steps:
            e2.append(send("edge", m1[c], edge))
            m2.append(send("middle", chunks[c][1], across))
            second += [(place ^ 2, c, e1[c]), (place ^ 3, c, send("pair", e1[c], pair))]
        between()
        for c in steps:
            block = jnp.where(outer, e2[c], m2[c])
            index = far_inner * 2
            third += [(index + y, c, block), (index + 1 - y, c, send("pair", block, pair))]
        for c in steps:
            m3 = send("middle", e2[c], across)
            m4 = send("middle", e1[c], across)
            block = jnp.where(outer, send("edge", m3, outward), m4)
            index = far_outer * 2
            fourth += [(index + y, c, block), (index + 1 - y, c, send("pair", block, pair))]
        return [first + second, third, fourth]

    def on_device(tokens, modality, norm_gains, qkv_weight, out_weight):
        core = lax.axis_index("mod").astype(I32)
        place = lax.axis_index("dp").astype(I32)
        own = lax.axis_index("tensor").astype(I32)
        z = place // 2
        column = (z ^ (z // 2)) & 1
        outer = column == 0
        length, features = tokens.shape
        chunks = 2 if lined else 1
        kept = qkv_weight.shape[1] // chunks
        half = length // 2
        which = core ^ (z & 1)
        links = Links(1)

        rows = lax.dynamic_slice_in_dim(tokens, core * half, half, 0)
        rest_rows = lax.dynamic_slice_in_dim(tokens, (1 - core) * half, half, 0)
        fetched = over_tensor(rows)
        other_modality = move(modality, edge)
        passed = []

        def pass_rows():
            passed.append(links.send("edge", after(rows, other_modality, fetched[-1]), edge))

        weights = halves(qkv_weight[0].transpose(1, 0, 2), outer, chunks)
        early, middle, last = gather(links, weights, place, outer, pass_rows)

        gains = norm_gains[0].reshape(places * chunks, 1, kept)
        shape = (2, places * chunks, length, kept)
        swapped = [rest_rows] + [to_core(a) for a in fetched[1:]]
        normed = normalize(
            jnp.stack([core, own, which]), None, gains, fetched, swapped, shape, 0, kept
        )
        part = over_tensor(passed[0])
        normed = normalize(
            jnp.stack([core, own, 1 - which]),
            normed,
            gains,
            part,
            [to_core(a) for a in part],
            shape,
            0,
            kept,
        )

        def add(slot, group, total, final=False, fresh=False):
            found = jnp.stack([slot] + [i * chunks + c for i, c, _ in group]).astype(I32)
            return project(found, normed, [b for _, _, b in group], total, final, fresh)

        total = None
        if early:
            total = add(which, early, None, fresh=True)
            total = add(which, middle, total)
        else:
            total = add(which, middle, None, fresh=True)
        total = add(1 - which, early + middle, total, fresh=True)
        zero = jnp.zeros((), I32)
        theirs = add(zero + 1, last, total, final=True)
        got = to_core(theirs)
        ours = add(zero, last, total, final=True)

        own_rows = (modality == core).astype(I32)[:, None]
        other_rows = (other_modality == core).astype(I32)[:, None]
        attended = attend(ours, got, jnp.where(which == 0, own_rows, other_rows))

        held = over_tensor(attended)
        held += over_tensor(move(attended, edge))
        pieces = jnp.stack([jnp.stack(held), jnp.stack([to_core(a) for a in held])])

        blocks = halves(out_weight, outer, 1)
        early, middle, last = gather(links, blocks, place, outer, lambda: None)

        def gathered(slot, group, total, final):
            found = [slot]
            for index, _, _ in group:
                piece = index // 2
                shard, part = piece // 2, piece % 2
                found.append(jnp.where(part == column, 0, shards) + (own - shard + shards) % shards)
                found.append(index % 2)
            found = jnp.stack(found).astype(I32)
            return combine(found, pieces, [b for _, _, b in group], total, final)

        sums = [gathered(slot, early + middle, None, False) for slot in (1 - which, which)]
        away = gathered(1 - which, last, sums[0], True)
        near = gathered(which, last, sums[1], True)

        kept_away = lax.dynamic_slice_in_dim(away, core * half, half, 0)
        sent_away = to_core(lax.dynamic_slice_in_dim(away, (1 - core) * half, half, 0))
        keep = lax.dynamic_slice_in_dim(other_rows, core * half, half, 0)
        far = move(jnp.where(keep != 0, kept_away, sent_away), edge)
        return assemble(
            jnp.stack([core, column]), own_rows, near, to_core(near), far, to_core(far)
        )

    return jax.shard_map(
        on_device,
        mesh=mesh,
        in_specs=(
            P("dp", "tensor"),
            P("dp"),
            P("mod", None),
            P("mod", "dp", None, "tensor"),
            P("mod", "dp", "tensor"),
        ),
        out_specs=P("dp", "tensor"),
        check_vma=False,
    )
```

time: 385 us -> 358 us (0.930)
  waiting for transfers between devices: 226 us -> 143 us
  starting transfers between devices: 44.6 us -> 74.6 us
  Pallas kernels: 93 us -> 107 us
  local copies, waits for them, and re-layouts: 12.5 us -> 18.9 us
    ppermute x31 -> x52, waiting for transfers between devices: 226 us -> 143 us  [move(): return lax.ppermute(array, AXES, pairs)]
    ppermute x31 -> x52, starting transfers between devices: 44.6 us -> 74.6 us  [move(): return lax.ppermute(array, AXES, pairs)]
    pallas_call x12 -> x16, Pallas kernels: 93 us -> 107 us  [call(): pl.pallas_call(kernel, grid_spec=pltpu.PrefetchScalarGridSpec(num_scalar_...]
    unnamed x30 -> x98, local copies, waits for them, and re-layouts: 7.25 us -> 13.9 us
    another operation x5 -> x4, other arithmetic: 0.38 us -> 6.67 us  [the longest x3 6.59 us: on_device(): pieces = jnp.stack([jnp.stack(held), jnp.stack([to_core(a) for a in held])])]
  transfers between devices with their start and end apart: 31 -> 52, of which waited for: 16 -> 21; matrix products, arithmetic and copies ran while one was open for 2% -> 4% of each run, Pallas kernels for 20% -> 24%
where the time goes in v3:
time: 358 us; the launch traced here: 355 us
  waiting for transfers between devices  143 us (40%)
  Pallas kernels  107 us (30%)
  starting transfers between devices  74.6 us (21%)
  local copies, waits for them, and re-layouts  18.9 us (5%)
  other arithmetic  10.9 us (3%)
    ppermute x52, waiting for transfers between devices, move(): return lax.ppermute(array, AXES, pairs)  143 us
    pallas_call x16, Pallas kernels, call(): pl.pallas_call(kernel, grid_spec=pltpu.PrefetchScalarGridSpec(num_scalar_...  107 us
    ppermute x52, starting transfers between devices, move(): return lax.ppermute(array, AXES, pairs)  74.6 us
    unnamed x98, local copies, waits for them, and re-layouts  13.9 us
  transfers between devices with their start and end apart: 52, of which 21 were waited for; matrix products, arithmetic and copies ran while one was open for 4% of the time, Pallas kernels for 24%

profile of v3, /device:TPU:0, one launch (start us, length us, event | category | flops | bytes accessed | tf_op | source)
XLA Modules:
  0.0 354.7 jit_solution(16780321538308013424)
XLA Ops:
  0.0 2.4 shard_map.57
  2.4 3.1 collective-permute-start.5
  6.2 3.6 %shard_map.56 = (bf16[3,256,512]{2,1,0:T(8,128)(2,1)}, bf16[3,256,512]{2,1,0:T(8,128)(2,1)S(1)}, bf16[3,256,512]{2,1,0:T(8,128)(2,1)S(1)}, bf16[3,256,512]{2,1,0:T(8,128)(2,1)}) custom-call(s32[1]{0:T(128)} %bitcast.14.o_ref, bf16[3,512,1024]{2,1,0:T(8,128)(2,1)} %bitcast.58), custom_call_target="tpu_custom_call" | custom-call | bytes 4718592 | tf_op jit(solution)/shard_map/pallas_call | solution.py:21
  10.8 12.3 %collective-permute-done.5.refs_12_.refs_16_ = bf16[3,256,512]{2,1,0:T(8,128)(2,1)S(1)} collective-permute-done((bf16[3,256,512]{2,1,0:T(8,128)(2,1)S(1)}, bf16[3,256,512]{2,1,0:T(8,128)(2,1)S(1)}, u32[]{:S(2)}, u32[]{:S(2)}) %collective-permute-start.5) | collective-permute-done | bytes 786464 | tf_op jit(solution)/shard_map/ppermute | solution.py:309
  23.1 1.7 collective-permute-start.6
  24.8 7.4 %collective-permute-start.4 = (bf16[3,256,512]{2,1,0:T(8,128)(2,1)}, bf16[3,256,512]{2,1,0:T(8,128)(2,1)}, u32[]{:S(2)}, u32[]{:S(2)}) collective-permute-start(bf16[3,256,512]{2,1,0:T(8,128)(2,1)} %get-tuple-element.52), channel_id=1, source_target_pairs={{0,0},{1,1},{2,2},{3,3},{4,8},{5,9},{6,10},{7,11},{8,4},{9,5},{10,... | collective-permute-start | bytes 2359304 | tf_op jit(solution)/shard_map/ppermute | solution.py:309
  33.7 8.4 %collective-permute-done.6.refs_14_.refs_18_ = bf16[3,256,512]{2,1,0:T(8,128)(2,1)} collective-permute-done((bf16[3,256,512]{2,1,0:T(8,128)(2,1)}, bf16[3,256,512]{2,1,0:T(8,128)(2,1)}, u32[]{:S(2)}, u32[]{:S(2)}) %collective-permute-start.6) | collective-permute-done | bytes 786464 | tf_op jit(solution)/shard_map/ppermute | solution.py:309
  44.4 3.0 constant_dynamic-slice_fusion.1
  51.9 8.2 %collective-permute-done.7 = bf16[3,256,512]{2,1,0:T(8,128)(2,1)S(1)} collective-permute-done((bf16[3,256,512]{2,1,0:T(8,128)(2,1)}, bf16[3,256,512]{2,1,0:T(8,128)(2,1)S(1)}, u32[]{:S(2)}, u32[]{:S(2)}) %collective-permute-start.7) | collective-permute-done | bytes 786464 | tf_op jit(solution)/shard_map/ppermute | solution.py:309
  61.9 5.6 %collective-permute-done.19.refs_11_.refs_15_ = bf16[3,256,512]{2,1,0:T(8,128)(2,1)S(1)} collective-permute-done((bf16[3,256,512]{2,1,0:T(8,128)(2,1)S(1)}, bf16[3,256,512]{2,1,0:T(8,128)(2,1)S(1)}, u32[]{:S(2)}, u32[]{:S(2)}) %collective-permute-start.19) | collective-permute-done | bytes 786464 | tf_op jit(solution)/shard_map/ppermute | solution.py:309
  70.0 5.7 %collective-permute-start = (s32[640]{0:T(1024)S(1)}, s32[640]{0:T(1024)S(1)}, u32[]{:S(2)}, u32[]{:S(2)}) collective-permute-start(s32[640]{0:T(1024)S(1)} %copy-done.47), channel_id=1, source_target_pairs={{0,4},{1,5},{2,6},{3,7},{4,0},{5,1},{6,2},{7,3},{8,12},{9,13},{10,... | collective-permute-start | bytes 7688 | tf_op jit(solution)/shard_map/ppermute | solution.py:309
  77.3 5.7 %collective-permute-start.9 = (bf16[320,2048]{1,0:T(8,128)(2,1)S(1)}, bf16[320,2048]{1,0:T(8,128)(2,1)}, u32[]{:S(2)}, u32[]{:S(2)}) collective-permute-start(bf16[320,2048]{1,0:T(8,128)(2,1)S(1)} %get-tuple-element.58.refs_1_), channel_id=1, source_target_pairs={{0,4},{1,5},{2,6},{3,7},{4,0},{5,1},{6,2},{7,3},{8,12},{9,13},{10,... | collective-permute-start | bytes 3932168 | tf_op jit(solution)/shard_map/ppermute | solution.py:309
  83.8 2.2 collective-permute-done.20.refs_13_.refs_17_
  88.3 15.5 %collective-permute-done.21.refs_15_.refs_19_ = bf16[3,256,512]{2,1,0:T(8,128)(2,1)S(1)} collective-permute-done((bf16[3,256,512]{2,1,0:T(8,128)(2,1)}, bf16[3,256,512]{2,1,0:T(8,128)(2,1)S(1)}, u32[]{:S(2)}, u32[]{:S(2)}) %collective-permute-start.21) | collective-permute-done | bytes 786464 | tf_op jit(solution)/shard_map/ppermute | solution.py:309
  105.3 3.3 collective-permute-done.9.refs_2_
  111.4 1.6 collective-permute-start.25
  113.1 6.5 %collective-permute-done.22.refs_5_.refs_21_ = bf16[3,256,512]{2,1,0:T(8,128)(2,1)S(1)} collective-permute-done((bf16[3,256,512]{2,1,0:T(8,128)(2,1)S(1)}, bf16[3,256,512]{2,1,0:T(8,128)(2,1)S(1)}, u32[]{:S(2)}, u32[]{:S(2)}) %collective-permute-start.22) | collective-permute-done | bytes 786464 | tf_op jit(solution)/shard_map/ppermute | solution.py:309
  122.1 9.9 %collective-permute-done.16 = bf16[3,256,512]{2,1,0:T(8,128)(2,1)S(1)} collective-permute-done((bf16[3,256,512]{2,1,0:T(8,128)(2,1)S(1)}, bf16[3,256,512]{2,1,0:T(8,128)(2,1)S(1)}, u32[]{:S(2)}, u32[]{:S(2)}) %collective-permute-start.16) | collective-permute-done | bytes 786464 | tf_op jit(solution)/shard_map/ppermute | solution.py:309
  132.0 3.5 collective-permute-done.10.refs_3_
  146.5 7.6 %shard_map.55.refs_0_ = bf16[2,16,640,256]{3,2,1,0:T(8,128)(2,1)} custom-call(s32[3]{0:T(128)S(1)} %pad_add_fusion.3.p_ref, f32[16,1,256]{2,1,0:T(1,128)S(1)} %bitcast.55, bf16[320,2048]{1,0:T(8,128)(2,1)S(1)} %copy-done.5, bf16[320,2048]{1,0:T(8,128)(2,1)S(1)} %copy-done.34, bf16[320,2048]{1,0:T(8,128)(2,1)S(1)} %copy-done.3, bf16[320,2048]{1,0:T(8,128)(2,1)} %copy-done.44), custom_call_target="tpu_custom_call" | custom-call | bytes 10485760 | tf_op jit(solution)/shard_map/pallas_call | solution.py:21
  154.1 3.6 %collective-permute-done.26 = bf16[3,256,512]{2,1,0:T(8,128)(2,1)} collective-permute-done((bf16[3,256,512]{2,1,0:T(8,128)(2,1)}, bf16[3,256,512]{2,1,0:T(8,128)(2,1)}, u32[]{:S(2)}, u32[]{:S(2)}) %collective-permute-start.26) | collective-permute-done | bytes 786464 | tf_op jit(solution)/shard_map/ppermute | solution.py:309
  158.9 1.6 collective-permute-done.24.refs_5_
  162.1 8.6 %shard_map.58.refs_0_.refs_1_.refs_2_.refs_3_.refs_4_.refs_5_.refs_6_.refs_7_.refs_8_.refs_9_.refs_10_.refs_11_ = bf16[2,16,640,256]{3,2,1,0:T(8,128)(2,1)} custom-call(s32[3]{0:T(128)S(1)} %pad_add_fusion.1.p_ref, bf16[2,16,640,256]{3,2,1,0:T(8,128)(2,1)} %shard_map.55.refs_0_, f32[16,1,256]{2,1,0:T(1,128)S(1)} %bitcast.56, ...), custom_call_target="tpu_custom_call", output_to_operand_aliasing={{}: (1, {})} | custom-call | bytes 10485760 | tf_op jit(solution)/shard_map/pallas_call | solution.py:21
  170.8 9.6 %shard_map.59.refs_8_ = f32[2,640,1536]{2,1,0:T(8,128)} custom-call(s32[9]{0:T(128)S(1)} %stack.260.p_ref, bf16[2,16,640,256]{3,2,1,0:T(8,128)(2,1)} %shard_map.58.refs_0_.refs_1_.refs_2_.refs_3_.refs_4_.refs_5_.refs_6_.refs_7_.refs_8_.refs_9_.refs_10_.refs_11_, ...), custom_call_target="tpu_custom_call" | custom-call | flops 4026531840 | bytes 12845056 | tf_op jit(solution)/shard_map/pallas_call | solution.py:21
  180.4 8.0 %shard_map.60.refs_24_ = f32[2,640,1536]{2,1,0:T(8,128)} custom-call(s32[5]{0:T(128)S(1)} %stack.259.p_ref, bf16[2,16,640,256]{3,2,1,0:T(8,128)(2,1)} %shard_map.58.refs_0_.refs_1_.refs_2_.refs_3_.refs_4_.refs_5_.refs_6_.refs_7_.refs_8_.refs_9_.refs_10_.refs_11_, ...), custom_call_target="tpu_custom_call", output_to_operand_aliasing={{}: (9, {})} | custom-call | flops 2013265920 | bytes 8388608 | tf_op jit(solution)/shard_map/pallas_call | solution.py:21
  188.4 12.2 %shard_map.61.refs_8_ = f32[2,640,1536]{2,1,0:T(8,128)} custom-call(s32[13]{0:T(128)S(1)} %stack.258.p_ref, bf16[2,16,640,256]{3,2,1,0:T(8,128)(2,1)} %shard_map.58.refs_0_.refs_1_.refs_2_.refs_3_.refs_4_.refs_5_.refs_6_.refs_7_.refs_8_.refs_9_.refs_10_.refs_11_, ...), custom_call_target="tpu_custom_call", output_to_operand_aliasing={{}: (25, {})} | custom-call | flops 6039797760 | bytes 17301504 | tf_op jit(solution)/shard_map/pallas_call | solution.py:21
  200.6 7.8 %shard_map.63 = bf16[640,1536]{1,0:T(8,128)(2,1)} custom-call(s32[5]{0:T(128)S(1)} %stack.261.p_ref, bf16[2,16,640,256]{3,2,1,0:T(8,128)(2,1)} %shard_map.58.refs_0_.refs_1_.refs_2_.refs_3_.refs_4_.refs_5_.refs_6_.refs_7_.refs_8_.refs_9_.refs_10_.refs_11_, ...), custom_call_target="tpu_custom_call" | custom-call | flops 2013265920 | bytes 8388608 | tf_op jit(solution)/shard_map/pallas_call | solution.py:21
  210.0 5.4 %collective-permute-start.37 = (bf16[1,256,1024]{2,1,0:T(8,128)(2,1)}, bf16[1,256,1024]{2,1,0:T(8,128)(2,1)}, u32[]{:S(2)}, u32[]{:S(2)}) collective-permute-start(bf16[1,256,1024]{2,1,0:T(8,128)(2,1)} %get-tuple-element.79), channel_id=1, source_target_pairs={{0,0},{1,1},{2,2},{3,3},{4,8},{5,9},{6,10},{7,11},{8,4},{9,5},{10,... | collective-permute-start | bytes 1572872 | tf_op jit(solution)/shard_map/ppermute | solution.py:309
  215.4 2.1 collective-permute-start.38
  217.7 12.2 %collective-permute-done.38.refs_8_ = bf16[1,256,1024]{2,1,0:T(8,128)(2,1)S(1)} collective-permute-done((bf16[1,256,1024]{2,1,0:T(8,128)(2,1)}, bf16[1,256,1024]{2,1,0:T(8,128)(2,1)S(1)}, u32[]{:S(2)}, u32[]{:S(2)}) %collective-permute-start.38) | collective-permute-done | bytes 524320 | tf_op jit(solution)/shard_map/ppermute | solution.py:309
  229.9 1.7 collective-permute-start.39
  233.5 7.7 %shard_map.62.qo.ko.vo = bf16[640,1536]{1,0:T(8,128)(2,1)} custom-call(s32[5]{0:T(128)S(1)} %stack.241.p_ref, bf16[2,16,640,256]{3,2,1,0:T(8,128)(2,1)} %shard_map.58.refs_0_.refs_1_.refs_2_.refs_3_.refs_4_.refs_5_.refs_6_.refs_7_.refs_8_.refs_9_.refs_10_.refs_11_, ...), custom_call_target="tpu_custom_call" | custom-call | flops 2013265920 | bytes 8388608 | tf_op jit(solution)/shard_map/pallas_call | solution.py:21
  242.7 9.8 %shard_map.64 = bf16[640,512]{1,0:T(8,128)(2,1)S(1)} custom-call(s32[1]{0:T(128)} %constant.338.clone.1._, s32[640,1]{1,0:T(8,128)S(1)} %select_n.377.mine_ref, bf16[640,1536]{1,0:T(8,128)(2,1)S(1)} %copy-done, bf16[640,1536]{1,0:T(8,128)(2,1)S(1)} %copy-done, bf16[640,1536]{1,0:T(8,128)(2,1)S(1)} %copy-done, ...), custom_call_target="tpu_custom_call" | custom-call | flops 838860800 | bytes 12454400 | tf_op jit(solution)/shard_map/pallas_call | solution.py:21
  252.6 3.3 collective-permute-start.31
  258.6 11.4 %collective-permute-done.31 = bf16[640,512]{1,0:T(8,128)(2,1)} collective-permute-done((bf16[640,512]{1,0:T(8,128)(2,1)S(1)}, bf16[640,512]{1,0:T(8,128)(2,1)}, u32[]{:S(2)}, u32[]{:S(2)}) %collective-permute-start.31) | collective-permute-done | bytes 655392 | tf_op jit(solution)/shard_map/ppermute | solution.py:309
  274.2 9.3 %collective-permute-done.45.refs_9_ = bf16[1,256,1024]{2,1,0:T(8,128)(2,1)S(1)} collective-permute-done((bf16[1,256,1024]{2,1,0:T(8,128)(2,1)S(1)}, bf16[1,256,1024]{2,1,0:T(8,128)(2,1)S(1)}, u32[]{:S(2)}, u32[]{:S(2)}) %collective-permute-start.45) | collective-permute-done | bytes 524320 | tf_op jit(solution)/shard_map/ppermute | solution.py:309
  284.0 1.6 collective-permute-done.42
  288.4 7.2 %collective-permute-done.46.refs_11_ = bf16[1,256,1024]{2,1,0:T(8,128)(2,1)} collective-permute-done((bf16[1,256,1024]{2,1,0:T(8,128)(2,1)S(1)}, bf16[1,256,1024]{2,1,0:T(8,128)(2,1)}, u32[]{:S(2)}, u32[]{:S(2)}) %collective-permute-start.46) | collective-permute-done | bytes 524320 | tf_op jit(solution)/shard_map/ppermute | solution.py:309
  296.1 1.8 maximum_bitcast_fusion
  298.0 2.0 maximum_bitcast_fusion.1
  300.0 2.8 pad_maximum_fusion.refs_0_.refs_1_.refs_2_.refs_3_.refs_4_.refs_5_
  302.8 6.5 %shard_map.68.refs_4_ = f32[640,1024]{1,0:T(8,128)} custom-call(s32[13]{0:T(128)S(1)} %stack.289.p_ref, bf16[2,4,640,512]{3,2,1,0:T(8,128)(2,1)} %pad_maximum_fusion.refs_0_.refs_1_.refs_2_.refs_3_.refs_4_.refs_5_, bf16[2,4,640,512]{3,2,1,0:T(8,128)(2,1)} %pad_maximum_fusion.refs_0_.refs_1_.refs_2_.refs_3_.refs_4_.refs_5_, ...), custom_call_target="tpu_custom_call" | custom-call | flops 2013265920 | bytes 7733248 | tf_op jit(solution)/shard_map/pallas_call | solution.py:21
  309.2 4.3 %shard_map.69 = bf16[640,1024]{1,0:T(8,128)(2,1)S(1)} custom-call(s32[5]{0:T(128)S(1)} %stack.288.p_ref, bf16[2,4,640,512]{3,2,1,0:T(8,128)(2,1)} %pad_maximum_fusion.refs_0_.refs_1_.refs_2_.refs_3_.refs_4_.refs_5_, bf16[2,4,640,512]{3,2,1,0:T(8,128)(2,1)} %pad_maximum_fusion.refs_0_.refs_1_.refs_2_.refs_3_.refs_4_.refs_5_, ...), custom_call_target="tpu_custom_call" | custom-call | flops 671088640 | bytes 4325376 | tf_op jit(solution)/shard_map/pallas_call | solution.py:21
  316.7 6.4 %shard_map.66.refs_4_ = f32[640,1024]{1,0:T(8,128)} custom-call(s32[13]{0:T(128)S(1)} %stack.287.p_ref, bf16[2,4,640,512]{3,2,1,0:T(8,128)(2,1)} %pad_maximum_fusion.refs_0_.refs_1_.refs_2_.refs_3_.refs_4_.refs_5_, bf16[2,4,640,512]{3,2,1,0:T(8,128)(2,1)} %pad_maximum_fusion.refs_0_.refs_1_.refs_2_.refs_3_.refs_4_.refs_5_, ...), custom_call_target="tpu_custom_call" | custom-call | flops 2013265920 | bytes 7733248 | tf_op jit(solution)/shard_map/pallas_call | solution.py:21
  323.2 4.2 %shard_map.67.a_ref = bf16[640,1024]{1,0:T(8,128)(2,1)S(1)} custom-call(s32[5]{0:T(128)S(1)} %stack.236.p_ref, bf16[2,4,640,512]{3,2,1,0:T(8,128)(2,1)} %pad_maximum_fusion.refs_0_.refs_1_.refs_2_.refs_3_.refs_4_.refs_5_, bf16[2,4,640,512]{3,2,1,0:T(8,128)(2,1)} %pad_maximum_fusion.refs_0_.refs_1_.refs_2_.refs_3_.refs_4_.refs_5_, ...), custom_call_target="tpu_custom_call" | custom-call | flops 671088640 | bytes 4325376 | tf_op jit(solution)/shard_map/pallas_call | solution.py:21
  330.7 15.4 %collective-permute-done.50.c_ref = bf16[320,1024]{1,0:T(8,128)(2,1)S(1)} collective-permute-done((bf16[320,1024]{1,0:T(8,128)(2,1)S(1)}, bf16[320,1024]{1,0:T(8,128)(2,1)S(1)}, u32[]{:S(2)}, u32[]{:S(2)}) %collective-permute-start.50) | collective-permute-done | bytes 655392 | tf_op jit(solution)/shard_map/ppermute | solution.py:309
  346.3 1.9 collective-permute-done.51.d_ref
  348.2 6.6 %shard_map.70 = bf16[640,2048]{1,0:T(8,128)(2,1)} custom-call(s32[2]{0:T(128)S(1)} %pad_add_fusion.p_ref, s32[640,1]{1,0:T(8,128)S(1)} %broadcast_in_dim.14.mine_ref, bf16[640,1024]{1,0:T(8,128)(2,1)S(1)} %shard_map.67.a_ref, bf16[640,1024]{1,0:T(8,128)(2,1)} %copy-done.43, bf16[320,1024]{1,0:T(8,128)(2,1)S(1)} %collective-permute-done.50.c_ref, ...), custom_call_target="tpu_custom_call" | custom-call | bytes 6556160 | tf_op jit(solution)/shard_map/pallas_call | solution.py:21
  (198 shorter events, 61.7 us)
Async XLA Ops:
  2.4 20.6 %collective-permute-start.5 = (bf16[3,256,512]{2,1,0:T(8,128)(2,1)S(1)}, bf16[3,256,512]{2,1,0:T(8,128)(2,1)S(1)}, u32[]{:S(2)}, u32[]{:S(2)}) collective-permute-start(bf16[3,256,512]{2,1,0:T(8,128)(2,1)S(1)} %get-tuple-element.54), channel_id=1, source_target_pairs={{0,4},{1,5},{2,6},{3,7},{4,0},{5,1},{6,2},{7,3},{8,12},{9,13},{10,... | collective-permute-start | bytes 2359304 | tf_op jit(solution)/shard_map/ppermute | solution.py:309
  5.5 19.3 %collective-permute-start.3 = (bf16[3,256,512]{2,1,0:T(8,128)(2,1)S(1)}, bf16[3,256,512]{2,1,0:T(8,128)(2,1)S(1)}, u32[]{:S(2)}, u32[]{:S(2)}) collective-permute-start(bf16[3,256,512]{2,1,0:T(8,128)(2,1)S(1)} %get-tuple-element.51), channel_id=1, source_target_pairs={{0,0},{1,1},{2,2},{3,3},{4,8},{5,9},{6,10},{7,11},{8,4},{9,5},{10,... | collective-permute-start | bytes 2359304 | tf_op jit(solution)/shard_map/ppermute | solution.py:309
  23.1 19.0 %collective-permute-start.6 = (bf16[3,256,512]{2,1,0:T(8,128)(2,1)}, bf16[3,256,512]{2,1,0:T(8,128)(2,1)}, u32[]{:S(2)}, u32[]{:S(2)}) collective-permute-start(bf16[3,256,512]{2,1,0:T(8,128)(2,1)} %get-tuple-element.55), channel_id=1, source_target_pairs={{0,4},{1,5},{2,6},{3,7},{4,0},{5,1},{6,2},{7,3},{8,12},{9,13},{10,... | collective-permute-start | bytes 2359304 | tf_op jit(solution)/shard_map/ppermute | solution.py:309
  24.8 18.7 %collective-permute-start.4 = (bf16[3,256,512]{2,1,0:T(8,128)(2,1)}, bf16[3,256,512]{2,1,0:T(8,128)(2,1)}, u32[]{:S(2)}, u32[]{:S(2)}) collective-permute-start(bf16[3,256,512]{2,1,0:T(8,128)(2,1)} %get-tuple-element.52), channel_id=1, source_target_pairs={{0,0},{1,1},{2,2},{3,3},{4,8},{5,9},{6,10},{7,11},{8,4},{9,5},{10,... | collective-permute-start | bytes 2359304 | tf_op jit(solution)/shard_map/ppermute | solution.py:309
  32.2 18.1 %collective-permute-start.18 = (bf16[3,256,512]{2,1,0:T(8,128)(2,1)S(1)}, bf16[3,256,512]{2,1,0:T(8,128)(2,1)S(1)}, u32[]{:S(2)}, u32[]{:S(2)}) collective-permute-start(bf16[3,256,512]{2,1,0:T(8,128)(2,1)S(1)} %get-tuple-element.67.refs_8_.refs_12_), channel_id=1, source_target_pairs={{0,2},{1,3},{2,0},{3,1},{4,6},{5,7},{6,4},{7,5},{8,10},{9,11},{10,... | collective-permute-start | bytes 2359304 | tf_op jit(solution)/shard_map/ppermute | solution.py:309
  42.1 18.0 %collective-permute-start.7 = (bf16[3,256,512]{2,1,0:T(8,128)(2,1)}, bf16[3,256,512]{2,1,0:T(8,128)(2,1)S(1)}, u32[]{:S(2)}, u32[]{:S(2)}) collective-permute-start(bf16[3,256,512]{2,1,0:T(8,128)(2,1)} %copy-done.48), channel_id=1, source_target_pairs={{0,4},{1,5},{2,6},{3,7},{4,0},{5,1},{6,2},{7,3},{8,12},{9,13},{10,... | collective-permute-start | bytes 2359304 | tf_op jit(solution)/shard_map/ppermute | solution.py:309
  43.5 17.7 %collective-permute-start.13 = (bf16[3,256,512]{2,1,0:T(8,128)(2,1)}, bf16[3,256,512]{2,1,0:T(8,128)(2,1)S(1)}, u32[]{:S(2)}, u32[]{:S(2)}) collective-permute-start(bf16[3,256,512]{2,1,0:T(8,128)(2,1)} %copy-done.39), channel_id=1, source_target_pairs={{4,8},{5,9},{6,10},{7,11},{8,4},{9,5},{10,6},{11,7},{20,24},{21,25... | collective-permute-start | bytes 2359304 | tf_op jit(solution)/shard_map/ppermute | solution.py:309
  47.4 29.9 %collective-permute-start.1 = (bf16[320,2048]{1,0:T(8,128)(2,1)S(1)}, bf16[320,2048]{1,0:T(8,128)(2,1)S(1)}, u32[]{:S(2)}, u32[]{:S(2)}) collective-permute-start(bf16[320,2048]{1,0:T(8,128)(2,1)S(1)} %get-tuple-element.58.refs_1_), channel_id=1, source_target_pairs={{0,1},{1,0},{2,3},{3,2},{4,5},{5,4},{6,7},{7,6},{8,9},{9,8},{10,11... | collective-permute-start | bytes 3932168 | tf_op jit(solution)/shard_map/ppermute | solution.py:309
  50.4 17.2 %collective-permute-start.19 = (bf16[3,256,512]{2,1,0:T(8,128)(2,1)S(1)}, bf16[3,256,512]{2,1,0:T(8,128)(2,1)S(1)}, u32[]{:S(2)}, u32[]{:S(2)}) collective-permute-start(bf16[3,256,512]{2,1,0:T(8,128)(2,1)S(1)} %get-tuple-element.68.refs_10_.refs_14_), channel_id=1, source_target_pairs={{0,2},{1,3},{2,0},{3,1},{4,6},{5,7},{6,4},{7,5},{8,10},{9,11},{10,... | collective-permute-start | bytes 2359304 | tf_op jit(solution)/shard_map/ppermute | solution.py:309
  60.1 17.2 %collective-permute-start.8 = (bf16[3,256,512]{2,1,0:T(8,128)(2,1)}, bf16[3,256,512]{2,1,0:T(8,128)(2,1)S(1)}, u32[]{:S(2)}, u32[]{:S(2)}) collective-permute-start(bf16[3,256,512]{2,1,0:T(8,128)(2,1)} %collective-permute-done.4), channel_id=1, source_target_pairs={{0,4},{1,5},{2,6},{3,7},{4,0},{5,1},{6,2},{7,3},{8,12},{9,13},{10,... | collective-permute-start | bytes 2359304 | tf_op jit(solution)/shard_map/ppermute | solution.py:309
  61.2 21.8 %collective-permute-start.14 = (bf16[3,256,512]{2,1,0:T(8,128)(2,1)S(1)}, bf16[3,256,512]{2,1,0:T(8,128)(2,1)S(1)}, u32[]{:S(2)}, u32[]{:S(2)}) collective-permute-start(bf16[3,256,512]{2,1,0:T(8,128)(2,1)S(1)} %copy-done.38), channel_id=1, source_target_pairs={{4,8},{5,9},{6,10},{7,11},{8,4},{9,5},{10,6},{11,7},{20,24},{21,25... | collective-permute-start | bytes 2359304 | tf_op jit(solution)/shard_map/ppermute | solution.py:309
  68.4 17.5 %collective-permute-start.20 = (bf16[3,256,512]{2,1,0:T(8,128)(2,1)S(1)}, bf16[3,256,512]{2,1,0:T(8,128)(2,1)S(1)}, u32[]{:S(2)}, u32[]{:S(2)}) collective-permute-start(bf16[3,256,512]{2,1,0:T(8,128)(2,1)S(1)} %collective-permute-done.5.refs_12_.refs_16_), channel_id=1, source_target_pairs={{0,2},{1,3},{2,0},{3,1},{4,6},{5,7},{6,4},{7,5},{8,10},{9,11},{10,... | collective-permute-start | bytes 2359304 | tf_op jit(solution)/shard_map/ppermute | solution.py:309
  77.3 31.3 %collective-permute-start.9 = (bf16[320,2048]{1,0:T(8,128)(2,1)S(1)}, bf16[320,2048]{1,0:T(8,128)(2,1)}, u32[]{:S(2)}, u32[]{:S(2)}) collective-permute-start(bf16[320,2048]{1,0:T(8,128)(2,1)S(1)} %get-tuple-element.58.refs_1_), channel_id=1, source_target_pairs={{0,4},{1,5},{2,6},{3,7},{4,0},{5,1},{6,2},{7,3},{8,12},{9,13},{10,... | collective-permute-start | bytes 3932168 | tf_op jit(solution)/shard_map/ppermute | solution.py:309
  85.9 17.8 %collective-permute-start.21 = (bf16[3,256,512]{2,1,0:T(8,128)(2,1)}, bf16[3,256,512]{2,1,0:T(8,128)(2,1)S(1)}, u32[]{:S(2)}, u32[]{:S(2)}) collective-permute-start(bf16[3,256,512]{2,1,0:T(8,128)(2,1)} %collective-permute-done.6.refs_14_.refs_18_), channel_id=1, source_target_pairs={{0,2},{1,3},{2,0},{3,1},{4,6},{5,7},{6,4},{7,5},{8,10},{9,11},{10,... | collective-permute-start | bytes 2359304 | tf_op jit(solution)/shard_map/ppermute | solution.py:309
  87.5 23.9 %collective-permute-start.17 = (bf16[3,256,512]{2,1,0:T(8,128)(2,1)S(1)}, bf16[3,256,512]{2,1,0:T(8,128)(2,1)S(1)}, u32[]{:S(2)}, u32[]{:S(2)}) collective-permute-start(bf16[3,256,512]{2,1,0:T(8,128)(2,1)S(1)} %collective-permute-done.5.refs_12_.refs_16_), channel_id=1, source_target_pairs={{4,8},{5,9},{6,10},{7,11},{8,4},{9,5},{10,6},{11,7},{20,24},{21,25... | collective-permute-start | bytes 2359304 | tf_op jit(solution)/shard_map/ppermute | solution.py:309
  103.8 15.9 %collective-permute-start.22 = (bf16[3,256,512]{2,1,0:T(8,128)(2,1)S(1)}, bf16[3,256,512]{2,1,0:T(8,128)(2,1)S(1)}, u32[]{:S(2)}, u32[]{:S(2)}) collective-permute-start(bf16[3,256,512]{2,1,0:T(8,128)(2,1)S(1)} %broadcast_select_fusion.1.refs_4_.refs_20_), channel_id=1, source_target_pairs={{0,2},{1,3},{2,0},{3,1},{4,6},{5,7},{6,4},{7,5},{8,10},{9,11},{10,... | collective-permute-start | bytes 2359304 | tf_op jit(solution)/shard_map/ppermute | solution.py:309
  108.6 26.9 %collective-permute-start.10 = (bf16[320,2048]{1,0:T(8,128)(2,1)}, bf16[320,2048]{1,0:T(8,128)(2,1)}, u32[]{:S(2)}, u32[]{:S(2)}) collective-permute-start(bf16[320,2048]{1,0:T(8,128)(2,1)} %collective-permute-done.9.refs_2_), channel_id=1, source_target_pairs={{0,1},{1,0},{2,3},{3,2},{4,5},{5,4},{6,7},{7,6},{8,9},{9,8},{10,11... | collective-permute-start | bytes 3932168 | tf_op jit(solution)/shard_map/ppermute | solution.py:309
  110.1 29.3 %collective-permute-start.2 = (bf16[320,2048]{1,0:T(8,128)(2,1)S(1)}, bf16[320,2048]{1,0:T(8,128)(2,1)S(1)}, u32[]{:S(2)}, u32[]{:S(2)}) collective-permute-start(bf16[320,2048]{1,0:T(8,128)(2,1)S(1)} %collective-permute-done.1.refs_2_), channel_id=1, source_target_pairs={{0,16},{1,17},{2,18},{3,19},{4,20},{5,21},{6,22},{7,23},{8,24},{9,... | collective-permute-start | bytes 3932168 | tf_op jit(solution)/shard_map/ppermute | solution.py:309
  110.1 21.8 %collective-permute-start.16 = (bf16[3,256,512]{2,1,0:T(8,128)(2,1)S(1)}, bf16[3,256,512]{2,1,0:T(8,128)(2,1)S(1)}, u32[]{:S(2)}, u32[]{:S(2)}) collective-permute-start(bf16[3,256,512]{2,1,0:T(8,128)(2,1)S(1)} %collective-permute-done.15), channel_id=1, source_target_pairs={{4,0},{5,1},{6,2},{7,3},{8,12},{9,13},{10,14},{11,15},{20,16},{21,... | collective-permute-start | bytes 2359304 | tf_op jit(solution)/shard_map/ppermute | solution.py:309
  111.4 24.1 %collective-permute-start.25 = (bf16[3,256,512]{2,1,0:T(8,128)(2,1)S(1)}, bf16[3,256,512]{2,1,0:T(8,128)(2,1)}, u32[]{:S(2)}, u32[]{:S(2)}) collective-permute-start(bf16[3,256,512]{2,1,0:T(8,128)(2,1)S(1)} %collective-permute-done.8), channel_id=1, source_target_pairs={{4,8},{5,9},{6,10},{7,11},{8,4},{9,5},{10,6},{11,7},{20,24},{21,25... | collective-permute-start | bytes 2359304 | tf_op jit(solution)/shard_map/ppermute | solution.py:309
  120.5 16.3 %collective-permute-start.23 = (bf16[3,256,512]{2,1,0:T(8,128)(2,1)S(1)}, bf16[3,256,512]{2,1,0:T(8,128)(2,1)S(1)}, u32[]{:S(2)}, u32[]{:S(2)}) collective-permute-start(bf16[3,256,512]{2,1,0:T(8,128)(2,1)S(1)} %broadcast_select_fusion.2.refs_6_.refs_22_), channel_id=1, source_target_pairs={{0,2},{1,3},{2,0},{3,1},{4,6},{5,7},{6,4},{7,5},{8,10},{9,11},{10,... | collective-permute-start | bytes 2359304 | tf_op jit(solution)/shard_map/ppermute | solution.py:309
  132.0 30.2 %collective-permute-start.11 = (bf16[320,2048]{1,0:T(8,128)(2,1)}, bf16[320,2048]{1,0:T(8,128)(2,1)}, u32[]{:S(2)}, u32[]{:S(2)}) collective-permute-start(bf16[320,2048]{1,0:T(8,128)(2,1)} %collective-permute-done.9.refs_2_), channel_id=1, source_target_pairs={{0,16},{1,17},{2,18},{3,19},{4,20},{5,21},{6,22},{7,23},{8,24},{9,... | collective-permute-start | bytes 3932168 | tf_op jit(solution)/shard_map/ppermute | solution.py:309
  135.5 26.6 %collective-permute-start.12 = (bf16[320,2048]{1,0:T(8,128)(2,1)}, bf16[320,2048]{1,0:T(8,128)(2,1)}, u32[]{:S(2)}, u32[]{:S(2)}) collective-permute-start(bf16[320,2048]{1,0:T(8,128)(2,1)} %collective-permute-done.10.refs_3_), channel_id=1, source_target_pairs={{0,16},{1,17},{2,18},{3,19},{4,20},{5,21},{6,22},{7,23},{8,24},{9,... | collective-permute-start | bytes 3932168 | tf_op jit(solution)/shard_map/ppermute | solution.py:309
  135.5 22.2 %collective-permute-start.26 = (bf16[3,256,512]{2,1,0:T(8,128)(2,1)}, bf16[3,256,512]{2,1,0:T(8,128)(2,1)}, u32[]{:S(2)}, u32[]{:S(2)}) collective-permute-start(bf16[3,256,512]{2,1,0:T(8,128)(2,1)} %collective-permute-done.25), channel_id=1, source_target_pairs={{4,0},{5,1},{6,2},{7,3},{8,12},{9,13},{10,14},{11,15},{20,16},{21,... | collective-permute-start | bytes 2359304 | tf_op jit(solution)/shard_map/ppermute | solution.py:309
  137.7 20.0 %collective-permute-start.27 = (bf16[3,256,512]{2,1,0:T(8,128)(2,1)}, bf16[3,256,512]{2,1,0:T(8,128)(2,1)}, u32[]{:S(2)}, u32[]{:S(2)}) collective-permute-start(bf16[3,256,512]{2,1,0:T(8,128)(2,1)} %collective-permute-done.6.refs_14_.refs_18_), channel_id=1, source_target_pairs={{4,8},{5,9},{6,10},{7,11},{8,4},{9,5},{10,6},{11,7},{20,24},{21,25... | collective-permute-start | bytes 2359304 | tf_op jit(solution)/shard_map/ppermute | solution.py:309
  140.5 20.1 %collective-permute-start.24 = (bf16[3,256,512]{2,1,0:T(8,128)(2,1)S(1)}, bf16[3,256,512]{2,1,0:T(8,128)(2,1)}, u32[]{:S(2)}, u32[]{:S(2)}) collective-permute-start(bf16[3,256,512]{2,1,0:T(8,128)(2,1)S(1)} %broadcast_select_fusion.3.refs_4_), channel_id=1, source_target_pairs={{0,2},{1,3},{2,0},{3,1},{4,6},{5,7},{6,4},{7,5},{8,10},{9,11},{10,... | collective-permute-start | bytes 2359304 | tf_op jit(solution)/shard_map/ppermute | solution.py:309
  160.6 40.0 %collective-permute-start.28 = (bf16[3,256,512]{2,1,0:T(8,128)(2,1)S(1)}, bf16[3,256,512]{2,1,0:T(8,128)(2,1)S(1)}, u32[]{:S(2)}, u32[]{:S(2)}) collective-permute-start(bf16[3,256,512]{2,1,0:T(8,128)(2,1)S(1)} %broadcast_select_fusion.refs_6_), channel_id=1, source_target_pairs={{0,2},{1,3},{2,0},{3,1},{4,6},{5,7},{6,4},{7,5},{8,10},{9,11},{10,... | collective-permute-start | bytes 2359304 | tf_op jit(solution)/shard_map/ppermute | solution.py:309
  208.4 32.7 %collective-permute-start.29 = (bf16[640,1536]{1,0:T(8,128)(2,1)}, bf16[640,1536]{1,0:T(8,128)(2,1)}, u32[]{:S(2)}, u32[]{:S(2)}) collective-permute-start(bf16[640,1536]{1,0:T(8,128)(2,1)} %shard_map.63), channel_id=1, source_target_pairs={{0,16},{1,17},{2,18},{3,19},{4,20},{5,21},{6,22},{7,23},{8,24},{9,... | collective-permute-start | bytes 5898248 | tf_op jit(solution)/shard_map/ppermute | solution.py:309
  215.4 14.5 %collective-permute-start.38 = (bf16[1,256,1024]{2,1,0:T(8,128)(2,1)}, bf16[1,256,1024]{2,1,0:T(8,128)(2,1)S(1)}, u32[]{:S(2)}, u32[]{:S(2)}) collective-permute-start(bf16[1,256,1024]{2,1,0:T(8,128)(2,1)} %get-tuple-element.81), channel_id=1, source_target_pairs={{0,4},{1,5},{2,6},{3,7},{4,0},{5,1},{6,2},{7,3},{8,12},{9,13},{10,... | collective-permute-start | bytes 1572872 | tf_op jit(solution)/shard_map/ppermute | solution.py:309
  229.9 26.4 %collective-permute-start.39 = (bf16[1,256,1024]{2,1,0:T(8,128)(2,1)}, bf16[1,256,1024]{2,1,0:T(8,128)(2,1)S(1)}, u32[]{:S(2)}, u32[]{:S(2)}) collective-permute-start(bf16[1,256,1024]{2,1,0:T(8,128)(2,1)} %collective-permute-done.37), channel_id=1, source_target_pairs={{0,4},{1,5},{2,6},{3,7},{4,0},{5,1},{6,2},{7,3},{8,12},{9,13},{10,... | collective-permute-start | bytes 1572872 | tf_op jit(solution)/shard_map/ppermute | solution.py:309
  231.6 24.7 %collective-permute-start.40 = (bf16[1,256,1024]{2,1,0:T(8,128)(2,1)}, bf16[1,256,1024]{2,1,0:T(8,128)(2,1)S(1)}, u32[]{:S(2)}, u32[]{:S(2)}) collective-permute-start(bf16[1,256,1024]{2,1,0:T(8,128)(2,1)} %copy-done.40), channel_id=1, source_target_pairs={{4,8},{5,9},{6,10},{7,11},{8,4},{9,5},{10,6},{11,7},{20,24},{21,25... | collective-permute-start | bytes 1572872 | tf_op jit(solution)/shard_map/ppermute | solution.py:309
  252.6 17.4 %collective-permute-start.31 = (bf16[640,512]{1,0:T(8,128)(2,1)S(1)}, bf16[640,512]{1,0:T(8,128)(2,1)}, u32[]{:S(2)}, u32[]{:S(2)}) collective-permute-start(bf16[640,512]{1,0:T(8,128)(2,1)S(1)} %shard_map.64), channel_id=1, source_target_pairs={{0,4},{1,5},{2,6},{3,7},{4,0},{5,1},{6,2},{7,3},{8,12},{9,13},{10,... | collective-permute-start | bytes 1966088 | tf_op jit(solution)/shard_map/ppermute | solution.py:309
  255.8 15.6 %collective-permute-start.44 = (bf16[1,256,1024]{2,1,0:T(8,128)(2,1)S(1)}, bf16[1,256,1024]{2,1,0:T(8,128)(2,1)S(1)}, u32[]{:S(2)}, u32[]{:S(2)}) collective-permute-start(bf16[1,256,1024]{2,1,0:T(8,128)(2,1)S(1)} %get-tuple-element.89.refs_6_), channel_id=1, source_target_pairs={{0,2},{1,3},{2,0},{3,1},{4,6},{5,7},{6,4},{7,5},{8,10},{9,11},{10,... | collective-permute-start | bytes 1572872 | tf_op jit(solution)/shard_map/ppermute | solution.py:309
  256.3 15.7 %collective-permute-start.41 = (bf16[1,256,1024]{2,1,0:T(8,128)(2,1)S(1)}, bf16[1,256,1024]{2,1,0:T(8,128)(2,1)S(1)}, u32[]{:S(2)}, u32[]{:S(2)}) collective-permute-start(bf16[1,256,1024]{2,1,0:T(8,128)(2,1)S(1)} %collective-permute-done.39), channel_id=1, source_target_pairs={{4,8},{5,9},{6,10},{7,11},{8,4},{9,5},{10,6},{11,7},{20,24},{21,25... | collective-permute-start | bytes 1572872 | tf_op jit(solution)/shard_map/ppermute | solution.py:309
  257.0 29.1 %collective-permute-start.30 = (bf16[640,512]{1,0:T(8,128)(2,1)S(1)}, bf16[640,512]{1,0:T(8,128)(2,1)}, u32[]{:S(2)}, u32[]{:S(2)}) collective-permute-start(bf16[640,512]{1,0:T(8,128)(2,1)S(1)} %shard_map.64), channel_id=1, source_target_pairs={{0,1},{1,0},{2,3},{3,2},{4,5},{5,4},{6,7},{7,6},{8,9},{9,8},{10,11... | collective-permute-start | bytes 1966088 | tf_op jit(solution)/shard_map/ppermute | solution.py:309
  269.9 16.7 %collective-permute-start.32 = (bf16[640,512]{1,0:T(8,128)(2,1)}, bf16[640,512]{1,0:T(8,128)(2,1)}, u32[]{:S(2)}, u32[]{:S(2)}) collective-permute-start(bf16[640,512]{1,0:T(8,128)(2,1)} %collective-permute-done.31), channel_id=1, source_target_pairs={{0,1},{1,0},{2,3},{3,2},{4,5},{5,4},{6,7},{7,6},{8,9},{9,8},{10,11... | collective-permute-start | bytes 1966088 | tf_op jit(solution)/shard_map/ppermute | solution.py:309
  271.4 12.1 %collective-permute-start.45 = (bf16[1,256,1024]{2,1,0:T(8,128)(2,1)S(1)}, bf16[1,256,1024]{2,1,0:T(8,128)(2,1)S(1)}, u32[]{:S(2)}, u32[]{:S(2)}) collective-permute-start(bf16[1,256,1024]{2,1,0:T(8,128)(2,1)S(1)} %copy-done.25), channel_id=1, source_target_pairs={{0,2},{1,3},{2,0},{3,1},{4,6},{5,7},{6,4},{7,5},{8,10},{9,11},{10,... | collective-permute-start | bytes 1572872 | tf_op jit(solution)/shard_map/ppermute | solution.py:309
  272.0 13.6 %collective-permute-start.42 = (bf16[1,256,1024]{2,1,0:T(8,128)(2,1)S(1)}, bf16[1,256,1024]{2,1,0:T(8,128)(2,1)S(1)}, u32[]{:S(2)}, u32[]{:S(2)}) collective-permute-start(bf16[1,256,1024]{2,1,0:T(8,128)(2,1)S(1)} %collective-permute-done.41), channel_id=1, source_target_pairs={{4,0},{5,1},{6,2},{7,3},{8,12},{9,13},{10,14},{11,15},{20,16},{21,... | collective-permute-start | bytes 1572872 | tf_op jit(solution)/shard_map/ppermute | solution.py:309
  273.3 12.3 %collective-permute-start.43 = (bf16[1,256,1024]{2,1,0:T(8,128)(2,1)S(1)}, bf16[1,256,1024]{2,1,0:T(8,128)(2,1)S(1)}, u32[]{:S(2)}, u32[]{:S(2)}) collective-permute-start(bf16[1,256,1024]{2,1,0:T(8,128)(2,1)S(1)} %copy-done.25), channel_id=1, source_target_pairs={{4,8},{5,9},{6,10},{7,11},{8,4},{9,5},{10,6},{11,7},{20,24},{21,25... | collective-permute-start | bytes 1572872 | tf_op jit(solution)/shard_map/ppermute | solution.py:309
  283.5 12.1 %collective-permute-start.46 = (bf16[1,256,1024]{2,1,0:T(8,128)(2,1)S(1)}, bf16[1,256,1024]{2,1,0:T(8,128)(2,1)}, u32[]{:S(2)}, u32[]{:S(2)}) collective-permute-start(bf16[1,256,1024]{2,1,0:T(8,128)(2,1)S(1)} %broadcast_select_fusion.4.refs_10_), channel_id=1, source_target_pairs={{0,2},{1,3},{2,0},{3,1},{4,6},{5,7},{6,4},{7,5},{8,10},{9,11},{10,... | collective-permute-start | bytes 1572872 | tf_op jit(solution)/shard_map/ppermute | solution.py:309
  285.6 12.3 %collective-permute-start.33 = (bf16[640,512]{1,0:T(8,128)(2,1)S(1)}, bf16[640,512]{1,0:T(8,128)(2,1)}, u32[]{:S(2)}, u32[]{:S(2)}) collective-permute-start(bf16[640,512]{1,0:T(8,128)(2,1)S(1)} %shard_map.64), channel_id=1, source_target_pairs={{0,16},{1,17},{2,18},{3,19},{4,20},{5,21},{6,22},{7,23},{8,24},{9,... | collective-permute-start | bytes 1966088 | tf_op jit(solution)/shard_map/ppermute | solution.py:309
  285.6 12.3 %collective-permute-start.35 = (bf16[640,512]{1,0:T(8,128)(2,1)}, bf16[640,512]{1,0:T(8,128)(2,1)}, u32[]{:S(2)}, u32[]{:S(2)}) collective-permute-start(bf16[640,512]{1,0:T(8,128)(2,1)} %collective-permute-done.31), channel_id=1, source_target_pairs={{0,16},{1,17},{2,18},{3,19},{4,20},{5,21},{6,22},{7,23},{8,24},{9,... | collective-permute-start | bytes 1966088 | tf_op jit(solution)/shard_map/ppermute | solution.py:309
  286.4 11.5 %collective-permute-start.34 = (bf16[640,512]{1,0:T(8,128)(2,1)}, bf16[640,512]{1,0:T(8,128)(2,1)}, u32[]{:S(2)}, u32[]{:S(2)}) collective-permute-start(bf16[640,512]{1,0:T(8,128)(2,1)} %collective-permute-done.30), channel_id=1, source_target_pairs={{0,16},{1,17},{2,18},{3,19},{4,20},{5,21},{6,22},{7,23},{8,24},{9,... | collective-permute-start | bytes 1966088 | tf_op jit(solution)/shard_map/ppermute | solution.py:309
  286.6 11.4 %collective-permute-start.36 = (bf16[640,512]{1,0:T(8,128)(2,1)}, bf16[640,512]{1,0:T(8,128)(2,1)}, u32[]{:S(2)}, u32[]{:S(2)}) collective-permute-start(bf16[640,512]{1,0:T(8,128)(2,1)} %collective-permute-done.32), channel_id=1, source_target_pairs={{0,16},{1,17},{2,18},{3,19},{4,20},{5,21},{6,22},{7,23},{8,24},{9,... | collective-permute-start | bytes 1966088 | tf_op jit(solution)/shard_map/ppermute | solution.py:309
  295.6 13.6 %collective-permute-start.47 = (bf16[1,256,1024]{2,1,0:T(8,128)(2,1)S(1)}, bf16[1,256,1024]{2,1,0:T(8,128)(2,1)S(1)}, u32[]{:S(2)}, u32[]{:S(2)}) collective-permute-start(bf16[1,256,1024]{2,1,0:T(8,128)(2,1)S(1)} %broadcast_select_fusion.5.refs_2_), channel_id=1, source_target_pairs={{0,2},{1,3},{2,0},{3,1},{4,6},{5,7},{6,4},{7,5},{8,10},{9,11},{10,... | collective-permute-start | bytes 1572872 | tf_op jit(solution)/shard_map/ppermute | solution.py:309
  314.4 13.6 %collective-permute-start.49 = (bf16[320,1024]{1,0:T(8,128)(2,1)}, bf16[320,1024]{1,0:T(8,128)(2,1)}, u32[]{:S(2)}, u32[]{:S(2)}) collective-permute-start(bf16[320,1024]{1,0:T(8,128)(2,1)} %constant_dynamic-slice_fusion), channel_id=1, source_target_pairs={{0,16},{1,17},{2,18},{3,19},{4,20},{5,21},{6,22},{7,23},{8,24},{9,... | collective-permute-start | bytes 1966088 | tf_op jit(solution)/shard_map/ppermute | solution.py:309
  327.4 18.8 %collective-permute-start.48 = (bf16[640,1024]{1,0:T(8,128)(2,1)S(1)}, bf16[640,1024]{1,0:T(8,128)(2,1)S(1)}, u32[]{:S(2)}, u32[]{:S(2)}) collective-permute-start(bf16[640,1024]{1,0:T(8,128)(2,1)S(1)} %shard_map.67.a_ref), channel_id=1, source_target_pairs={{0,16},{1,17},{2,18},{3,19},{4,20},{5,21},{6,22},{7,23},{8,24},{9,... | collective-permute-start | bytes 3932168 | tf_op jit(solution)/shard_map/ppermute | solution.py:309
  329.3 16.7 %collective-permute-start.50 = (bf16[320,1024]{1,0:T(8,128)(2,1)S(1)}, bf16[320,1024]{1,0:T(8,128)(2,1)S(1)}, u32[]{:S(2)}, u32[]{:S(2)}) collective-permute-start(bf16[320,1024]{1,0:T(8,128)(2,1)S(1)} %dynamic-slice_select_fusion), channel_id=1, source_target_pairs={{0,4},{1,5},{2,6},{3,7},{4,0},{5,1},{6,2},{7,3},{8,12},{9,13},{10,... | collective-permute-start | bytes 1966088 | tf_op jit(solution)/shard_map/ppermute | solution.py:309
  (53 other events, 1023.0 us)

commit v4 on v0

--- a/solution.py
+++ b/solution.py
@@ -1,16 +1,293 @@
 import jax
 import jax.numpy as jnp
 from jax import lax
+from jax.experimental import pallas as pl
+from jax.experimental.pallas import tpu as pltpu
 from jax.sharding import PartitionSpec as P
 
 HDIM = 128
+AXES = ("mod", "dp", "tensor")
+VMEM = 64 * 1024 * 1024
+F32, BF16, I32 = jnp.float32, jnp.bfloat16, jnp.int32
+
+
+def after(array, *earlier):
+    return lax.optimization_barrier((array,) + earlier)[0]
+
+
+def call(kernel, grid, in_specs, out_specs, out_shape, prefetch, args, flops, aliases=None, moved=0):
+    outs = jax.tree.leaves(out_shape)
+    moved = moved or sum(a.size * a.dtype.itemsize for a in list(args) + outs)
+    return pl.pallas_call(
+        kernel,
+        grid_spec=pltpu.PrefetchScalarGridSpec(
+            num_scalar_prefetch=1, grid=grid, in_specs=in_specs, out_specs=out_specs
+        ),
+        out_shape=out_shape,
+        input_output_aliases=aliases or {},
+        cost_estimate=pl.CostEstimate(flops=flops, bytes_accessed=moved, transcendentals=0),
+        compiler_params=pltpu.CompilerParams(vmem_limit_bytes=VMEM),
+    )(prefetch, *args)
+
+
+def halves(weight, outer, chunk, chunks, *earlier):
+    kinds, depth, width = weight.shape
+    part = width // 2 // chunks
+    tile = min(depth, 128)
+
+    def kernel(o_ref, first_ref, last_ref, low_ref, high_ref, mine_ref, away_ref):
+        low, high = first_ref[...], last_ref[...]
+        first = o_ref[0] == 1
+        low_ref[...] = low
+        high_ref[...] = high
+        mine_ref[...] = jnp.where(first, low, high)
+        away_ref[...] = jnp.where(first, high, low)
+
+    out = jax.ShapeDtypeStruct((kinds, depth, part), weight.dtype)
+    spec = pl.BlockSpec((kinds, tile, part), lambda i, o: (0, i, 0))
+    return call(
+        kernel,
+        (depth // tile,),
+        [
+            pl.BlockSpec((kinds, tile, part), lambda i, o: (0, i, chunk)),
+            pl.BlockSpec((kinds, tile, part), lambda i, o: (0, i, chunks + chunk)),
+        ],
+        [spec] * 4,
+        [out] * 4,
+        after(outer, *earlier).reshape(1),
+        [weight, weight],
+        0,
+        moved=6 * kinds * depth * part,
+    )
+
+
+def normalize(places, held, gains, mine, theirs, shape, start, kept):
+    slots, blocks, length, _ = shape
+    shards = len(mine)
+    count, features = mine[0].shape
+    tile = 80 if count % 80 == 0 else count
+    steps, half = count // tile, length // 2
+    per = features // kept
+
+    def kernel(p_ref, *refs):
+        refs = refs[1:] if held is not None else refs
+        gain_ref, out_ref = refs[0], refs[-1]
+        core, own = p_ref[0], p_ref[1]
+
+        def write(group):
+            wide = [ref[...].astype(F32) for ref in group]
+            total = sum(jnp.sum(w * w, axis=-1, keepdims=True) for w in wide)
+            inverse = lax.rsqrt(total / (shards * features) + 1e-05)
+            for step, w in enumerate(wide):
+                shard = lax.rem(own - step + shards, shards)
+                for i in range(per):
+                    block = shard * per + i
+                    part = w[:, i * kept : (i + 1) * kept] * inverse * gain_ref[block]
+                    out_ref[0, block] = part.astype(BF16)
+
+        @pl.when(pl.program_id(0) == core)
+        def _():
+            write(refs[1 : 1 + shards])
+
+        @pl.when(pl.program_id(0) != core)
+        def _():
+            write(refs[1 + shards : 1 + 2 * shards])
+
+    own_spec = pl.BlockSpec(
+        (tile, features), lambda h, i, p: (jnp.where(h == p[0], i, jnp.where(h == 0, 0, steps - 1)), 0)
+    )
+    other_spec = pl.BlockSpec(
+        (tile, features), lambda h, i, p: (jnp.where(h != p[0], i, jnp.where(h == 0, 0, steps - 1)), 0)
+    )
+    in_specs = [pl.BlockSpec((blocks, 1, kept), lambda h, i, p: (0, 0, 0))]
+    in_specs += [own_spec] * shards + [other_spec] * shards
+    args = [gains] + list(mine) + list(theirs)
+    if held is not None:
+        in_specs = [pl.BlockSpec(memory_space=pl.ANY)] + in_specs
+        args = [held] + args
+    out_spec = pl.BlockSpec(
+        (1, blocks, tile, kept), lambda h, i, p: (p[2], 0, (h * half + start) // tile + i, 0)
+    )
+    return call(
+        kernel,
+        (2, steps),
+        in_specs,
+        out_spec,
+        jax.ShapeDtypeStruct(shape, BF16),
+        places,
+        args,
+        0,
+        {1: 0} if held is not None else None,
+        moved=8 * count * features * shards,
+    )
+
+
+def project(places, normed, blocks, total, final, fresh):
+    slots, _, length, kept = normed.shape
+    kinds, _, width = blocks[0].shape
+    tile = min(width, 256)
+    per = width // tile
+    count = len(blocks)
+
+    def kernel(p_ref, *refs):
+        out_ref = refs[-1]
+        summed = None if fresh else refs[2 * count][0]
+        for i in range(count):
+            part = jnp.dot(refs[i][0, 0], refs[count + i][0], preferred_element_type=F32)
+            summed = part if summed is None else summed + part
+        if final:
+            out_ref[...] = summed.astype(BF16)
+        else:
+            out_ref[0] = summed
+
+    def columns(i):
+        return pl.BlockSpec((1, 1, length, kept), lambda n, p: (p[0], p[1 + i], 0, 0))
+
+    total_spec = pl.BlockSpec((1, length, tile), lambda n, p: (p[0], 0, n))
+    in_specs = [columns(i) for i in range(count)]
+    in_specs += [pl.BlockSpec((1, kept, tile), lambda n, p: (n // per, 0, n % per))] * count
+    args = [normed] * count + list(blocks)
+    if total is not None:
+        in_specs.append(pl.BlockSpec(memory_space=pl.ANY) if fresh else total_spec)
+        args.append(total)
+    aliases = None
+    if final:
+        out_spec = pl.BlockSpec((length, tile), lambda n, p: (0, n))
+        out_shape = jax.ShapeDtypeStruct((length, kinds * width), BF16)
+    else:
+        out_spec, out_shape = total_spec, jax.ShapeDtypeStruct((slots, length, kinds * width), F32)
+        if total is not None:
+            aliases = {1 + 2 * count: 0}
+    return call(
+        kernel,
+        (kinds * per,),
+        in_specs,
+        out_spec,
+        out_shape,
+        places,
+        args,
+        0,
+        aliases,
+        moved=2 * count * kept * (length + kinds * width) + 4 * length * kinds * width,
+    )
+
+
+def attend(own, got, mine):
+    length, width = own.shape[0], own.shape[1] // 3
+    heads = width // HDIM
+    scale = HDIM ** (-0.5)
+    tile = 128 if length % 128 == 0 else length
+
+    def kernel(_, mine_ref, own_ref, got_ref, out_ref):
+        keep = mine_ref[...] != 0
+
+        def pick(j):
+            columns = slice(j * HDIM, (j + 1) * HDIM)
+            return jnp.where(
+                keep, own_ref[:, columns].astype(F32), got_ref[:, columns].astype(F32)
+            ).astype(BF16)
+
+        for h in range(heads):
+            query, key, value = pick(h), pick(heads + h), pick(2 * heads + h)
+            for i in range(length // tile):
+                low, high = i * tile, (i + 1) * tile
+                scores = lax.dot_general(
+                    query[low:high], key[:high], (((1,), (1,)), ((), ())), preferred_element_type=F32
+                )
+                rows = low + lax.broadcasted_iota(I32, (tile, high), 0)
+                cols = lax.broadcasted_iota(I32, (tile, high), 1)
+                scores = jnp.where(cols <= rows, scores * scale, -jnp.inf)
+                top = jnp.max(scores, axis=-1, keepdims=True)
+                raised = jnp.exp(scores - top)
+                share = 1.0 / jnp.sum(raised, axis=-1, keepdims=True)
+                probs = (raised * share).astype(BF16)
+                out = jnp.dot(probs, value[:high], preferred_element_type=F32)
+                out_ref[low:high, h * HDIM : (h + 1) * HDIM] = out.astype(BF16)
+
+    full = pl.BlockSpec((length, 3 * width), lambda i, p: (0, 0))
+    return call(
+        kernel,
+        (1,),
+        [pl.BlockSpec((length, 1), lambda i, p: (0, 0)), full, full],
+        pl.BlockSpec((length, width), lambda i, p: (0, 0)),
+        jax.ShapeDtypeStruct((length, width), BF16),
+        jnp.zeros((1,), I32),
+        [mine, own, got],
+        0,
+    )
+
+
+def combine(places, groups, total, final, slots):
+    _, _, length, held = groups[0][0].shape
+    features = groups[0][2][0][0].shape[2]
+    tile = min(features, 256)
+    terms = [(pieces, parity, pair) for pieces, parity, pairs in groups for pair in pairs]
+    count = len(terms)
+
+    def kernel(p_ref, *refs):
+        out_ref = refs[-1]
+        summed = None if total is None else refs[3 * count][0]
+        for i, (_, parity, _) in enumerate(terms):
+            near, far = refs[count + 2 * i][0], refs[count + 2 * i + 1][0]
+            block = jnp.where(p_ref[1] == parity, near, far)
+            part = jnp.dot(refs[i][0, 0], block, preferred_element_type=F32)
+            summed = part if summed is None else summed + part
+        out_ref[0] = summed.astype(out_ref.dtype)
+
+    def piece(i):
+        return pl.BlockSpec((1, 1, length, held), lambda s, n, p: (p[0] + s, p[2 + i], 0, 0))
+
+    block_spec = pl.BlockSpec((1, held, tile), lambda s, n, p: (0, 0, n))
+    in_specs = [piece(i) for i in range(count)] + [block_spec] * (2 * count)
+    args = [pieces for pieces, _, _ in terms] + [b for _, _, pair in terms for b in pair]
+    if total is not None:
+        in_specs.append(pl.BlockSpec((1, length, tile), lambda s, n, p: (p[0] + s, 0, n)))
+        args.append(total)
+    return call(
+        kernel,
+        (slots, features // tile),
+        in_specs,
+        pl.BlockSpec((1, length, tile), lambda s, n, p: (s, 0, n)),
+        jax.ShapeDtypeStruct((slots, length, features), BF16 if final else F32),
+        places,
+        args,
+        0,
+    )
+
+
+def assemble(places, mine, near, near_other, far, far_other):
+    length, width = near.shape
+    tile = 160 if length % 320 == 0 else length // 2
+    steps = length // 2 // tile
+
+    def kernel(p_ref, mine_ref, a_ref, b_ref, c_ref, d_ref, out_ref):
+        keep = mine_ref[...] != 0
+        own = jnp.where(keep, a_ref[...].astype(F32), b_ref[...].astype(F32)).astype(BF16)
+        held = (pl.program_id(0) // steps) == p_ref[0]
+        other = jnp.where(held, c_ref[...], d_ref[...])
+        first = p_ref[1] == 0
+        out_ref[:, :width] = jnp.where(first, own, other)
+        out_ref[:, width:] = jnp.where(first, other, own)
+
+    rows = pl.BlockSpec((tile, width), lambda i, p: (i, 0))
+    part = pl.BlockSpec((tile, width), lambda i, p: (i % steps, 0))
+    return call(
+        kernel,
+        (2 * steps,),
+        [pl.BlockSpec((tile, 1), lambda i, p: (i, 0)), rows, rows, part, part],
+        pl.BlockSpec((tile, 2 * width), lambda i, p: (i, 0)),
+        jax.ShapeDtypeStruct((length, 2 * width), BF16),
+        places,
+        [mine, near, near_other, far, far_other],
+        0,
+    )
 
 
 def from_partner(x, axis, bit):
     return lax.ppermute(x, axis, [(i, i ^ 1 << bit) for i in range(lax.axis_size(axis))])
 
 
-def on_device(tokens, modality, norm_gains, qkv_weight, out_weight):
+def gathered_plan(tokens, modality, norm_gains, qkv_weight, out_weight):
     tower_id = lax.axis_index("mod")
     own_rows = modality == tower_id
     gathered = lax.all_gather(tokens, "tensor", axis=1, tiled=True)
@@ -62,8 +339,202 @@
 
 
 def solution(mesh):
+    places, shards = mesh.shape["dp"], mesh.shape["tensor"]
+    mods = mesh.shape["mod"]
+
+    def move(array, where, *earlier):
+        pairs = []
+        for m in range(mods):
+            for d in range(places):
+                for x in range(shards):
+                    to = where(m, d, x)
+                    if to is not None:
+                        target = (to[0] * places + to[1]) * shards + to[2]
+                        pairs.append(((m * places + d) * shards + x, target))
+        return lax.ppermute(after(array, *earlier) if earlier else array, AXES, pairs)
+
+    def to_core(array, *earlier):
+        return move(array, lambda m, d, x: (1 - m, d, x), *earlier)
+
+    def over_tensor(array, *earlier):
+        return [array] + [
+            move(array, lambda m, d, x: (m, d, (x + step) % shards), *earlier)
+            for step in range(1, shards)
+        ]
+
+    def edge(m, d, x):
+        return m, d ^ 2, x
+
+    def outward(m, d, x):
+        return (m, d ^ 2, x) if d // 2 in (1, 2) else None
+
+    def across(m, d, x):
+        return (m, (3 - d // 2) * 2 + d % 2, x) if d // 2 in (1, 2) else None
+
+    def across_or_stay(m, d, x):
+        return across(m, d, x) or (m, d, x)
+
+    def pair(m, d, x):
+        return m, d ^ 1, x
+
+    def line_plan(tokens, modality, norm_gains, qkv_weight, out_weight):
+        core = lax.axis_index("mod").astype(I32)
+        place = lax.axis_index("dp").astype(I32)
+        own = lax.axis_index("tensor").astype(I32)
+        z, y = place // 2, place % 2
+        column = (z ^ (z // 2)) & 1
+        outer = 1 - column
+        length, features = tokens.shape
+        kept = qkv_weight.shape[1]
+        half = length // 2
+        which = core ^ (z & 1)
+        at = [z, z ^ 1, jnp.where(z < 2, 2, 1), 3 - 3 * (z // 2)]
+
+        def choose(edge_block, middle_block):
+            return jnp.where(outer == 1, edge_block, middle_block)
+
+        weight = qkv_weight[0].transpose(1, 0, 2)
+        low_a, high_a, mine_a, away_a = halves(weight, outer, 0, 2)
+        e1a = move(away_a, edge)
+        m1a = move(low_a, across_or_stay)
+        p1a = move(mine_a, pair)
+        rows = lax.dynamic_slice_in_dim(tokens, core * half, half, 0)
+        fetched = over_tensor(rows, mine_a)
+        other_modality = move(modality, edge)
+        low_b, high_b, mine_b, away_b = halves(weight, outer, 1, 2, mine_a)
+        rest_rows = lax.dynamic_slice_in_dim(tokens, (1 - core) * half, half, 0)
+
+        ready = (e1a, m1a, p1a, mine_b, other_modality)
+        e2a = move(m1a, edge, *ready)
+        m2a = move(high_a, across, *ready)
+        p2a = move(e1a, pair, *ready)
+        low_o, high_o, mine_o, away_o = halves(out_weight, outer, 0, 1, mine_b, e1a)
+        swapped = [rest_rows] + [to_core(a) for a in fetched[1:]]
+
+        ready = (e2a, m2a, p2a, mine_o, fetched[-1])
+        m3a = move(e2a, across, *ready)
+        passed = move(rows, edge, *ready)
+        third_a = choose(e2a, m2a)
+        p3a = move(third_a, pair, *ready)
+        gains = norm_gains[0].reshape(places, 1, kept)
+        shape = (2, places, length, kept)
+        normed = normalize(
+            jnp.stack([core, own, which]), None, gains, fetched, swapped, shape, 0, kept
+        )
+
+        ready = (m3a, p3a, normed)
+        m4a = move(e1a, across, *ready)
+        p1b = move(mine_b, pair, *ready)
+
+        def add(slot, blocks, total, final=False, fresh=False):
+            found = [slot]
+            for k, _, _ in blocks:
+                found += [2 * k + y, 2 * k + 1 - y]
+            flat = [b for _, near, far in blocks for b in (near, far)]
+            return project(jnp.stack(found).astype(I32), normed, flat, total, final, fresh)
+
+        first_a = [(at[0], mine_a, p1a), (at[1], e1a, p2a), (at[2], third_a, p3a)]
+        total_a = add(which, first_a, None, fresh=True)
+
+        e3a = move(m3a, outward, passed)
+        part = over_tensor(passed)
+        m1b = move(low_b, across_or_stay, m4a, p1b, total_a)
+        part_swapped = [to_core(a) for a in part]
+        fourth_a = choose(e3a, m4a)
+        p4a = move(fourth_a, pair, p1b)
+
+        m2b = move(high_b, across, m1b)
+        e2b = move(m1b, edge, e3a)
+        normed = normalize(
+            jnp.stack([core, own, 1 - which]), normed, gains, part, part_swapped, shape, 0, kept
+        )
+
+        ready = (m2b, e2b, p4a, normed)
+        m3b = move(e2b, across, *ready)
+        e1b = move(away_b, edge, *ready)
+        third_b = choose(e2b, m2b)
+        p3b = move(third_b, pair, *ready)
+        total_a = add(1 - which, first_a, total_a, fresh=True)
+        zero, one = jnp.zeros((), I32), jnp.ones((), I32)
+        last_a = [(at[3], fourth_a, p4a)]
+        theirs_a = add(one, last_a, total_a, final=True)
+        got_a = to_core(theirs_a)
+        ours_a = add(zero, last_a, total_a, final=True)
+        own_rows = (modality == core).astype(I32)[:, None]
+        other_rows = (other_modality == core).astype(I32)[:, None]
+        mine_rows = jnp.where(which == 0, own_rows, other_rows)
+        attended_a = attend(ours_a, got_a, mine_rows)
+
+        ready = (m3b, e1b, p3b, attended_a)
+        m4b = move(e1b, across, *ready)
+        e3b = move(m3b, outward, *ready)
+        p2b = move(e1b, pair, *ready)
+        held_a = over_tensor(attended_a, *ready)
+        first_b = [(at[0], mine_b, p1b), (at[1], e1b, p2b), (at[2], third_b, p3b)]
+        some_b = [first_b[0], first_b[2]]
+        total_b = add(which, some_b, None, fresh=True)
+        total_b = add(1 - which, some_b, total_b, fresh=True)
+
+        ready = (m4b, e3b, p2b, total_b)
+        fourth_b = choose(e3b, m4b)
+        p4b = move(fourth_b, pair, *ready)
+        m1o = move(low_o, across_or_stay, *ready)
+        e1o = move(away_o, edge, *ready)
+        last_b = [(at[1], e1b, p2b), (at[3], fourth_b, p4b)]
+
+        ready = (m1o, e1o)
+        m2o = move(high_o, across, *ready)
+        e2o = move(m1o, edge, *ready)
+        p1o = move(mine_o, pair, p4b)
+        p2o = move(e1o, pair, p1o)
+        theirs_b = add(one, last_b, total_b, final=True)
+        got_b = to_core(theirs_b)
+        ours_b = add(zero, last_b, total_b, final=True)
+        attended_b = attend(ours_b, got_b, mine_rows)
+
+        held_a += over_tensor(move(attended_a, edge, e2o))
+        m3o = move(e2o, across, m2o)
+        m4o = move(e1o, across, m3o)
+        e3o = move(m3o, outward)
+        third_o, fourth_o = choose(e2o, m2o), choose(e3o, m4o)
+        p3o = move(third_o, pair, p2o)
+        p4o = move(fourth_o, pair, p3o)
+        held_b = over_tensor(attended_b)
+        held_b += over_tensor(move(attended_b, edge))
+
+        pieces = [
+            jnp.stack([jnp.stack(held), jnp.stack([to_core(a) for a in held])])
+            for held in (held_a, held_b)
+        ]
+        blocks = [(mine_o, p1o), (e1o, p2o), (third_o, p3o), (fourth_o, p4o)]
+
+        def piece_of(k):
+            shard, part = k // 2, k % 2
+            return jnp.where(part == column, 0, shards) + (own - shard + shards) % shards
+
+        found = [piece_of(k) for k in at]
+        near = [(pieces[0], 0, blocks[:3])]
+        rest = [(pieces[0], 0, blocks[3:]), (pieces[1], 1, blocks)]
+        total = combine(
+            jnp.stack([zero, y] + found[:3]).astype(I32), near, None, False, 2
+        )
+
+        def finish(slot):
+            order = jnp.stack([slot, y, found[3]] + found).astype(I32)
+            return combine(order, rest, total, True, 1)[0]
+
+        away = finish(1 - which)
+        near = finish(which)
+        kept_away = lax.dynamic_slice_in_dim(away, core * half, half, 0)
+        sent_away = to_core(lax.dynamic_slice_in_dim(away, (1 - core) * half, half, 0))
+        keep = lax.dynamic_slice_in_dim(other_rows, core * half, half, 0)
+        far = move(jnp.where(keep != 0, kept_away, sent_away), edge)
+        return assemble(
+            jnp.stack([core, column]), own_rows, near, to_core(near), far, to_core(far)
+        )
+
     return jax.shard_map(
-        on_device,
+        line_plan if places == 8 else gathered_plan,
         mesh=mesh,
         in_specs=(
             P("dp", "tensor"),

time: 771 us -> 359 us (0.47)
  waiting for transfers between devices: 688 us -> 105 us
  Pallas kernels: 0 us -> 126 us
  starting transfers between devices: 0.16 us -> 84.5 us
  matrix products: 46.3 us -> 0 us
  other arithmetic: 7.63 us -> 25.1 us
  between operations: 13.2 us -> 0.34 us
    all_gather x4 -> x0, waiting for transfers between devices: 662 us -> none  [the longest x1 478 us: on_device(): weight_piece = lax.all_gather(qkv_weight, 'dp', axis=1, tiled=True)]
    pallas_call x0 -> x19, Pallas kernels: none -> 126 us  [call(): pl.pallas_call(kernel, grid_spec=pltpu.PrefetchScalarGridSpec(num_scalar_...]
    ppermute x1 -> x60, waiting for transfers between devices: 2.64 us -> 105 us  [move(): lax.ppermute(after(array, *earlier) if earlier else array, AXES, pairs)]
    ppermute x1 -> x60, starting transfers between devices: 0.01 us -> 84.5 us  [move(): lax.ppermute(after(array, *earlier) if earlier else array, AXES, pairs)]
    dot_general x3 -> x0, matrix products: 40 us -> none  [the longest x1 21.7 us: on_device(): jnp.dot(columns, weight_piece[0].reshape(count, 3 * local_width), preferr...]
    psum x1 -> x0, waiting for transfers between devices: 22.3 us -> none  [on_device(): combined = lax.psum(placed.astype(jnp.float32).astype(jnp.bfloat16), 'mod')]
    another operation x0 -> x11, other arithmetic: none -> 12.1 us  [the longest x6 9.06 us: line_plan(): jnp.stack([jnp.stack(held), jnp.stack([to_core(a) for a in held])])]
    unnamed x12 -> x18, local copies, waits for them, and re-layouts: 11.7 us -> 2.56 us
  transfers between devices with their start and end apart: 6 -> 60, of which waited for: 6 -> 18; matrix products, arithmetic and copies ran while one was open for 7% -> 10% of each run, Pallas kernels for 0% -> 31%
where the time goes in v4:
time: 359 us; the launch traced here: 356 us
  Pallas kernels  126 us (35%)
  waiting for transfers between devices  105 us (29%)
  starting transfers between devices  84.5 us (24%)
  other arithmetic  25.1 us (7%)
  local copies, waits for them, and re-layouts  15.6 us (4%)
    pallas_call x19, Pallas kernels, call(): pl.pallas_call(kernel, grid_spec=pltpu.PrefetchScalarGridSpec(num_scalar_...  126 us
    ppermute x60, waiting for transfers between devices, move(): lax.ppermute(after(array, *earlier) if earlier else array, AXES, pairs)  105 us
    ppermute x60, starting transfers between devices, move(): lax.ppermute(after(array, *earlier) if earlier else array, AXES, pairs)  84.5 us
    select_n x6, other arithmetic, choose(): return jnp.where(outer == 1, edge_block, middle_block)  9.58 us
    another operation x6, other arithmetic, line_plan(): jnp.stack([jnp.stack(held), jnp.stack([to_core(a) for a in held])])  9.06 us
  transfers between devices with their start and end apart: 60, of which 18 were waited for; matrix products, arithmetic and copies ran while one was open for 10% of the time, Pallas kernels for 31%

profile of v4, /device:TPU:0, one launch (start us, length us, event | category | flops | bytes accessed | tf_op | source)
XLA Modules:
  0.0 356.2 jit_solution(1290153779937203855)
XLA Ops:
  0.0 4.0 %shard_map.55 = (bf16[3,512,256]{2,1,0:T(8,128)(2,1)}, bf16[3,512,256]{2,1,0:T(8,128)(2,1)}, bf16[3,512,256]{2,1,0:T(8,128)(2,1)}, bf16[3,512,256]{2,1,0:T(8,128)(2,1)}) custom-call(s32[1]{0:T(128)} %bitcast.13.o_ref, bf16[3,512,1024]{2,1,0:T(8,128)(2,1)} %bitcast.54, bf16[3,512,1024]{2,1,0:T(8,128)(2,1)} %bitcast.55), custom_call_target="tpu_custom_call" | custom-call | bytes 2359296 | tf_op jit(solution)/shard_map/pallas_call | solution.py:21
  4.0 3.0 collective-permute-start.4
  7.1 7.4 %collective-permute-start.3 = (bf16[3,512,256]{2,1,0:T(8,128)(2,1)}, bf16[3,512,256]{2,1,0:T(8,128)(2,1)}, u32[]{:S(2)}, u32[]{:S(2)}) collective-permute-start(bf16[3,512,256]{2,1,0:T(8,128)(2,1)} %get-tuple-element.53), channel_id=1, source_target_pairs={{0,0},{1,1},{2,2},{3,3},{4,8},{5,9},{6,10},{7,11},{8,4},{9,5},{10,... | collective-permute-start | bytes 2359304 | tf_op jit(solution)/shard_map/ppermute | solution.py:354
  16.0 3.6 %constant_dynamic-slice_fusion = (bf16[320,2048]{1,0:T(8,128)(2,1)}, bf16[320,2048]{1,0:T(8,128)(2,1)}) fusion(bf16[640,2048]{1,0:T(8,128)(2,1)} %param.5, s32[]{:T(128)S(6)} %select_n.156, s32[]{:T(128)S(6)} %select_n.155), kind=kLoop, calls=%fused_computation.18 | loop fusion | bytes 5242888 | tf_op jit(solution)/shard_map/dynamic_slice | solution.py:405
  21.1 4.0 %shard_map.57 = (bf16[3,512,256]{2,1,0:T(8,128)(2,1)}, bf16[3,512,256]{2,1,0:T(8,128)(2,1)}, bf16[3,512,256]{2,1,0:T(8,128)(2,1)}, bf16[3,512,256]{2,1,0:T(8,128)(2,1)}) custom-call(s32[1]{0:T(128)} %bitcast.16.o_ref, bf16[3,512,1024]{2,1,0:T(8,128)(2,1)} %bitcast.56, bf16[3,512,1024]{2,1,0:T(8,128)(2,1)} %bitcast.57), custom_call_target="tpu_custom_call" | custom-call | bytes 2359296 | tf_op jit(solution)/shard_map/pallas_call | solution.py:21
  25.1 8.7 %collective-permute-done.5.refs_7_ = bf16[3,512,256]{2,1,0:T(8,128)(2,1)} collective-permute-done((bf16[3,512,256]{2,1,0:T(8,128)(2,1)}, bf16[3,512,256]{2,1,0:T(8,128)(2,1)}, u32[]{:S(2)}, u32[]{:S(2)}) %collective-permute-start.5) | collective-permute-done | bytes 786464 | tf_op jit(solution)/shard_map/ppermute | solution.py:354
  36.9 2.4 shard_map.58
  39.3 10.6 %collective-permute-done.1.refs_2_ = bf16[320,2048]{1,0:T(8,128)(2,1)} collective-permute-done((bf16[320,2048]{1,0:T(8,128)(2,1)}, bf16[320,2048]{1,0:T(8,128)(2,1)}, u32[]{:S(2)}, u32[]{:S(2)}) %collective-permute-start.1) | collective-permute-done | bytes 1310752 | tf_op jit(solution)/shard_map/ppermute | solution.py:354
  49.8 2.4 collective-permute-done.6
  53.8 3.4 collective-permute-start.9
  57.2 1.6 collective-permute-start.13
  58.8 2.1 broadcast_select_fusion.3.refs_10_
  62.5 21.2 %collective-permute-done.9.refs_2_ = bf16[320,2048]{1,0:T(8,128)(2,1)} collective-permute-done((bf16[320,2048]{1,0:T(8,128)(2,1)}, bf16[320,2048]{1,0:T(8,128)(2,1)}, u32[]{:S(2)}, u32[]{:S(2)}) %collective-permute-start.9) | collective-permute-done | bytes 1310752 | tf_op jit(solution)/shard_map/ppermute | solution.py:354
  85.8 8.8 %shard_map.56.refs_0_.refs_1_.refs_2_.refs_3_.refs_4_.refs_5_ = bf16[2,8,640,512]{3,2,1,0:T(8,128)(2,1)} custom-call(s32[3]{0:T(128)} %pad_add_fusion.3.p_ref, f32[8,1,512]{2,1,0:T(1,128)} %bitcast.62, bf16[320,2048]{1,0:T(8,128)(2,1)} %get-tuple-element.63.refs_1_, bf16[320,2048]{1,0:T(8,128)(2,1)} %collective-permute-done.1.refs_2_, ...), custom_call_target="tpu_custom_call" | custom-call | bytes 10485760 | tf_op jit(solution)/shard_map/pallas_call | solution.py:21
  99.5 8.3 %shard_map.60.refs_12_ = f32[2,640,768]{2,1,0:T(8,128)} custom-call(s32[7]{0:T(128)} %stack.242.p_ref, bf16[2,8,640,512]{3,2,1,0:T(8,128)(2,1)} %shard_map.56.refs_0_.refs_1_.refs_2_.refs_3_.refs_4_.refs_5_, bf16[2,8,640,512]{3,2,1,0:T(8,128)(2,1)} %shard_map.56.refs_0_.refs_1_.refs_2_.refs_3_.refs_4_.refs_5_, ...), custom_call_target="tpu_custom_call" | custom-call | bytes 10616832 | tf_op jit(solution)/shard_map/pallas_call | solution.py:21
  107.8 4.3 %collective-permute-done.17.refs_5_ = bf16[3,512,256]{2,1,0:T(8,128)(2,1)} collective-permute-done((bf16[3,512,256]{2,1,0:T(8,128)(2,1)}, bf16[3,512,256]{2,1,0:T(8,128)(2,1)}, u32[]{:S(2)}, u32[]{:S(2)}) %collective-permute-start.17) | collective-permute-done | bytes 786464 | tf_op jit(solution)/shard_map/ppermute | solution.py:354
  112.1 7.4 %collective-permute-start.20 = (bf16[3,512,256]{2,1,0:T(8,128)(2,1)}, bf16[3,512,256]{2,1,0:T(8,128)(2,1)}, u32[]{:S(2)}, u32[]{:S(2)}) collective-permute-start(bf16[3,512,256]{2,1,0:T(8,128)(2,1)} %get-tuple-element.71), channel_id=1, source_target_pairs={{0,0},{1,1},{2,2},{3,3},{4,8},{5,9},{6,10},{7,11},{8,4},{9,5},{10,... | collective-permute-start | bytes 2359304 | tf_op jit(solution)/shard_map/ppermute | solution.py:354
  120.0 2.2 broadcast_select_fusion.2.refs_2_
  125.3 10.1 %collective-permute-start.21 = (bf16[3,512,256]{2,1,0:T(8,128)(2,1)}, bf16[3,512,256]{2,1,0:T(8,128)(2,1)}, u32[]{:S(2)}, u32[]{:S(2)}) collective-permute-start(bf16[3,512,256]{2,1,0:T(8,128)(2,1)} %collective-permute-done.20), channel_id=1, source_target_pairs={{0,4},{1,5},{2,6},{3,7},{4,0},{5,1},{6,2},{7,3},{8,12},{9,13},{10,... | collective-permute-start | bytes 2359304 | tf_op jit(solution)/shard_map/ppermute | solution.py:354
  137.2 8.8 %shard_map.59.refs_0_.refs_1_.refs_2_.refs_3_.refs_4_.refs_5_ = bf16[2,8,640,512]{3,2,1,0:T(8,128)(2,1)} custom-call(s32[3]{0:T(128)} %pad_add_fusion.1.p_ref, bf16[2,8,640,512]{3,2,1,0:T(8,128)(2,1)} %shard_map.56.refs_0_.refs_1_.refs_2_.refs_3_.refs_4_.refs_5_, f32[8,1,512]{2,1,0:T(1,128)} %bitcast.63, ...), custom_call_target="tpu_custom_call", output_to_operand_aliasing={{}: (1, {})} | custom-call | bytes 10485760 | tf_op jit(solution)/shard_map/pallas_call | solution.py:21
  146.0 8.3 %shard_map.61.refs_4_ = f32[2,640,768]{2,1,0:T(8,128)} custom-call(s32[7]{0:T(128)} %stack.241.p_ref, bf16[2,8,640,512]{3,2,1,0:T(8,128)(2,1)} %shard_map.59.refs_0_.refs_1_.refs_2_.refs_3_.refs_4_.refs_5_, bf16[2,8,640,512]{3,2,1,0:T(8,128)(2,1)} %shard_map.59.refs_0_.refs_1_.refs_2_.refs_3_.refs_4_.refs_5_, ...), custom_call_target="tpu_custom_call", output_to_operand_aliasing={{}: (13, {})} | custom-call | bytes 10616832 | tf_op jit(solution)/shard_map/pallas_call | solution.py:21
  154.3 5.6 %shard_map.63 = bf16[640,768]{1,0:T(8,128)(2,1)} custom-call(s32[3]{0:T(128)} %add_add_fusion.1.p_ref, bf16[2,8,640,512]{3,2,1,0:T(8,128)(2,1)} %shard_map.59.refs_0_.refs_1_.refs_2_.refs_3_.refs_4_.refs_5_, bf16[2,8,640,512]{3,2,1,0:T(8,128)(2,1)} %shard_map.59.refs_0_.refs_1_.refs_2_.refs_3_.refs_4_.refs_5_, ...), custom_call_target="tpu_custom_call" | custom-call | bytes 4849664 | tf_op jit(solution)/shard_map/pallas_call | solution.py:21
  159.9 2.1 broadcast_select_fusion.1.refs_6_
  167.9 5.5 %shard_map.62.own_ref = bf16[640,768]{1,0:T(8,128)(2,1)} custom-call(s32[3]{0:T(128)} %add_add_fusion.p_ref, bf16[2,8,640,512]{3,2,1,0:T(8,128)(2,1)} %shard_map.59.refs_0_.refs_1_.refs_2_.refs_3_.refs_4_.refs_5_, bf16[2,8,640,512]{3,2,1,0:T(8,128)(2,1)} %shard_map.59.refs_0_.refs_1_.refs_2_.refs_3_.refs_4_.refs_5_, ...), custom_call_target="tpu_custom_call" | custom-call | bytes 4849664 | tf_op jit(solution)/shard_map/pallas_call | solution.py:21
  173.4 5.9 %shard_map.64 = bf16[640,256]{1,0:T(8,128)(2,1)} custom-call(s32[1]{0:T(128)} %constant.118.clone.1._, s32[640,1]{1,0:T(8,128)} %select_n.166.mine_ref, bf16[640,768]{1,0:T(8,128)(2,1)} %shard_map.62.own_ref, bf16[640,768]{1,0:T(8,128)(2,1)} %collective-permute-done.19.got_ref), custom_call_target="tpu_custom_call" | custom-call | bytes 2296320 | tf_op jit(solution)/shard_map/pallas_call | solution.py:21
  179.3 3.0 collective-permute-done.24.refs_4_
  186.7 1.6 collective-permute-start.29
  189.5 6.8 %shard_map.65.refs_8_ = f32[2,640,768]{2,1,0:T(8,128)} custom-call(s32[5]{0:T(128)} %stack.247.p_ref, bf16[2,8,640,512]{3,2,1,0:T(8,128)(2,1)} %shard_map.59.refs_0_.refs_1_.refs_2_.refs_3_.refs_4_.refs_5_, bf16[2,8,640,512]{3,2,1,0:T(8,128)(2,1)} %shard_map.59.refs_0_.refs_1_.refs_2_.refs_3_.refs_4_.refs_5_, ...), custom_call_target="tpu_custom_call" | custom-call | bytes 7733248 | tf_op jit(solution)/shard_map/pallas_call | solution.py:21
  196.3 6.9 %shard_map.66.refs_8_ = f32[2,640,768]{2,1,0:T(8,128)} custom-call(s32[5]{0:T(128)} %stack.246.p_ref, bf16[2,8,640,512]{3,2,1,0:T(8,128)(2,1)} %shard_map.59.refs_0_.refs_1_.refs_2_.refs_3_.refs_4_.refs_5_, bf16[2,8,640,512]{3,2,1,0:T(8,128)(2,1)} %shard_map.59.refs_0_.refs_1_.refs_2_.refs_3_.refs_4_.refs_5_, ...), custom_call_target="tpu_custom_call", output_to_operand_aliasing={{}: (9, {})} | custom-call | bytes 7733248 | tf_op jit(solution)/shard_map/pallas_call | solution.py:21
  203.2 4.6 %collective-permute-done.28 = bf16[3,512,256]{2,1,0:T(8,128)(2,1)} collective-permute-done((bf16[3,512,256]{2,1,0:T(8,128)(2,1)}, bf16[3,512,256]{2,1,0:T(8,128)(2,1)}, u32[]{:S(2)}, u32[]{:S(2)}) %collective-permute-start.28) | collective-permute-done | bytes 786464 | tf_op jit(solution)/shard_map/ppermute | solution.py:354
  214.4 10.3 %collective-permute-done.31.refs_5_.refs_9_ = bf16[1,256,1024]{2,1,0:T(8,128)(2,1)} collective-permute-done((bf16[1,256,1024]{2,1,0:T(8,128)(2,1)S(1)}, bf16[1,256,1024]{2,1,0:T(8,128)(2,1)}, u32[]{:S(2)}, u32[]{:S(2)}) %collective-permute-start.31) | collective-permute-done | bytes 524320 | tf_op jit(solution)/shard_map/ppermute | solution.py:354
  228.3 7.0 %shard_map.68 = bf16[640,768]{1,0:T(8,128)(2,1)} custom-call(s32[5]{0:T(128)} %stack.260.p_ref, bf16[2,8,640,512]{3,2,1,0:T(8,128)(2,1)} %shard_map.59.refs_0_.refs_1_.refs_2_.refs_3_.refs_4_.refs_5_, bf16[2,8,640,512]{3,2,1,0:T(8,128)(2,1)} %shard_map.59.refs_0_.refs_1_.refs_2_.refs_3_.refs_4_.refs_5_, ...), custom_call_target="tpu_custom_call" | custom-call | bytes 7733248 | tf_op jit(solution)/shard_map/pallas_call | solution.py:21
  238.2 3.6 %collective-permute-start.33 = (bf16[640,256]{1,0:T(8,128)(2,1)}, bf16[640,256]{1,0:T(8,128)(2,1)}, u32[]{:S(2)}, u32[]{:S(2)}) collective-permute-start(bf16[640,256]{1,0:T(8,128)(2,1)} %shard_map.64), channel_id=1, source_target_pairs={{0,4},{1,5},{2,6},{3,7},{4,0},{5,1},{6,2},{7,3},{8,12},{9,13},{10,... | collective-permute-start | bytes 983048 | tf_op jit(solution)/shard_map/ppermute | solution.py:354
  241.8 8.2 %collective-permute-done.52.refs_4_.refs_8_ = bf16[1,256,1024]{2,1,0:T(8,128)(2,1)} collective-permute-done((bf16[1,256,1024]{2,1,0:T(8,128)(2,1)}, bf16[1,256,1024]{2,1,0:T(8,128)(2,1)}, u32[]{:S(2)}, u32[]{:S(2)}) %collective-permute-start.52) | collective-permute-done | bytes 524320 | tf_op jit(solution)/shard_map/ppermute | solution.py:354
  253.2 7.0 %shard_map.67.own_ref = bf16[640,768]{1,0:T(8,128)(2,1)} custom-call(s32[5]{0:T(128)} %stack.259.p_ref, bf16[2,8,640,512]{3,2,1,0:T(8,128)(2,1)} %shard_map.59.refs_0_.refs_1_.refs_2_.refs_3_.refs_4_.refs_5_, bf16[2,8,640,512]{3,2,1,0:T(8,128)(2,1)} %shard_map.59.refs_0_.refs_1_.refs_2_.refs_3_.refs_4_.refs_5_, ...), custom_call_target="tpu_custom_call" | custom-call | bytes 7733248 | tf_op jit(solution)/shard_map/pallas_call | solution.py:21
  260.2 5.9 %shard_map.69 = bf16[640,256]{1,0:T(8,128)(2,1)} custom-call(s32[1]{0:T(128)} %constant.118.clone.1._, s32[640,1]{1,0:T(8,128)} %select_n.166.mine_ref, bf16[640,768]{1,0:T(8,128)(2,1)} %shard_map.67.own_ref, bf16[640,768]{1,0:T(8,128)(2,1)} %collective-permute-done.40.got_ref), custom_call_target="tpu_custom_call" | custom-call | bytes 2296320 | tf_op jit(solution)/shard_map/pallas_call | solution.py:21
  266.1 2.1 collective-permute-start.42
  272.6 4.4 %collective-permute-done.42 = bf16[640,256]{1,0:T(8,128)(2,1)} collective-permute-done((bf16[640,256]{1,0:T(8,128)(2,1)}, bf16[640,256]{1,0:T(8,128)(2,1)}, u32[]{:S(2)}, u32[]{:S(2)}) %collective-permute-start.42) | collective-permute-done | bytes 327712 | tf_op jit(solution)/shard_map/ppermute | solution.py:354
  283.1 4.6 %collective-permute-done.50 = bf16[1,256,1024]{2,1,0:T(8,128)(2,1)S(1)} collective-permute-done((bf16[1,256,1024]{2,1,0:T(8,128)(2,1)}, bf16[1,256,1024]{2,1,0:T(8,128)(2,1)S(1)}, u32[]{:S(2)}, u32[]{:S(2)}) %collective-permute-start.50) | collective-permute-done | bytes 524320 | tf_op jit(solution)/shard_map/ppermute | solution.py:354
  289.9 1.6 collective-permute-done.54.refs_8_.refs_12_
  293.5 1.7 pad_maximum_fusion.refs_0_.refs_1_.refs_2_
  295.2 10.4 %shard_map.70.refs_15_ = f32[2,640,1024]{2,1,0:T(8,128)} custom-call(s32[5]{0:T(128)} %stack.274.p_ref, bf16[2,4,640,256]{3,2,1,0:T(8,128)(2,1)} %pad_maximum_fusion.refs_0_.refs_1_.refs_2_, bf16[2,4,640,256]{3,2,1,0:T(8,128)(2,1)} %pad_maximum_fusion.refs_0_.refs_1_.refs_2_, bf16[2,4,640,256]{3,2,1,0:T(8,128)(2,1)} %pad_maximum_fusion.refs_0_.refs_1_.refs_2_, ...), custom_call_target="tpu_custom_call" | custom-call | bytes 16252928 | tf_op jit(solution)/shard_map/pallas_call | solution.py:21
  308.6 1.8 pad_maximum_fusion.1.refs_1_.refs_2_.refs_3_.refs_4_
  310.4 7.5 %shard_map.72 = bf16[1,640,1024]{2,1,0:T(8,128)(2,1)} custom-call(s32[7]{0:T(128)} %stack.275.p_ref, bf16[2,4,640,256]{3,2,1,0:T(8,128)(2,1)} %pad_maximum_fusion.refs_0_.refs_1_.refs_2_, bf16[2,4,640,256]{3,2,1,0:T(8,128)(2,1)} %pad_maximum_fusion.1.refs_1_.refs_2_.refs_3_.refs_4_, ...), custom_call_target="tpu_custom_call" | custom-call | bytes 24903680 | tf_op jit(solution)/shard_map/pallas_call | solution.py:21
  317.9 2.0 dynamic-slice_bitcast_fusion
  321.2 7.6 %shard_map.71 = bf16[1,640,1024]{2,1,0:T(8,128)(2,1)} custom-call(s32[7]{0:T(128)} %stack.227.p_ref, bf16[2,4,640,256]{3,2,1,0:T(8,128)(2,1)} %pad_maximum_fusion.refs_0_.refs_1_.refs_2_, bf16[2,4,640,256]{3,2,1,0:T(8,128)(2,1)} %pad_maximum_fusion.1.refs_1_.refs_2_.refs_3_.refs_4_, ...), custom_call_target="tpu_custom_call" | custom-call | bytes 24903680 | tf_op jit(solution)/shard_map/pallas_call | solution.py:21
  332.4 15.2 %collective-permute-done.58.c_ref = bf16[320,1024]{1,0:T(8,128)(2,1)S(1)} collective-permute-done((bf16[320,1024]{1,0:T(8,128)(2,1)S(1)}, bf16[320,1024]{1,0:T(8,128)(2,1)S(1)}, u32[]{:S(2)}, u32[]{:S(2)}) %collective-permute-start.58) | collective-permute-done | bytes 655392 | tf_op jit(solution)/shard_map/ppermute | solution.py:354
  350.7 5.5 %shard_map.73 = bf16[640,2048]{1,0:T(8,128)(2,1)} custom-call(s32[2]{0:T(128)} %pad_add_fusion.p_ref, s32[640,1]{1,0:T(8,128)} %broadcast_in_dim.14.mine_ref, bf16[640,1024]{1,0:T(8,128)(2,1)} %bitcast.59, bf16[640,1024]{1,0:T(8,128)(2,1)} %collective-permute-done.56.b_ref, bf16[320,1024]{1,0:T(8,128)(2,1)} %copy-done.4, ...), custom_call_target="tpu_custom_call" | custom-call | bytes 6556160 | tf_op jit(solution)/shard_map/pallas_call | solution.py:21
  (142 shorter events, 74.9 us)
Async XLA Ops:
  4.0 21.0 %collective-permute-start.4 = (bf16[3,512,256]{2,1,0:T(8,128)(2,1)}, bf16[3,512,256]{2,1,0:T(8,128)(2,1)}, u32[]{:S(2)}, u32[]{:S(2)}) collective-permute-start(bf16[3,512,256]{2,1,0:T(8,128)(2,1)} %get-tuple-element.54), channel_id=1, source_target_pairs={{0,4},{1,5},{2,6},{3,7},{4,0},{5,1},{6,2},{7,3},{8,12},{9,13},{10,... | collective-permute-start | bytes 2359304 | tf_op jit(solution)/shard_map/ppermute | solution.py:354
  7.1 18.0 %collective-permute-start.3 = (bf16[3,512,256]{2,1,0:T(8,128)(2,1)}, bf16[3,512,256]{2,1,0:T(8,128)(2,1)}, u32[]{:S(2)}, u32[]{:S(2)}) collective-permute-start(bf16[3,512,256]{2,1,0:T(8,128)(2,1)} %get-tuple-element.53), channel_id=1, source_target_pairs={{0,0},{1,1},{2,2},{3,3},{4,8},{5,9},{6,10},{7,11},{8,4},{9,5},{10,... | collective-permute-start | bytes 2359304 | tf_op jit(solution)/shard_map/ppermute | solution.py:354
  14.5 19.3 %collective-permute-start.5 = (bf16[3,512,256]{2,1,0:T(8,128)(2,1)}, bf16[3,512,256]{2,1,0:T(8,128)(2,1)}, u32[]{:S(2)}, u32[]{:S(2)}) collective-permute-start(bf16[3,512,256]{2,1,0:T(8,128)(2,1)} %get-tuple-element.51.refs_6_), channel_id=1, source_target_pairs={{0,2},{1,3},{2,0},{3,1},{4,6},{5,7},{6,4},{7,5},{8,10},{9,11},{10,... | collective-permute-start | bytes 2359304 | tf_op jit(solution)/shard_map/ppermute | solution.py:354
  19.6 30.3 %collective-permute-start.1 = (bf16[320,2048]{1,0:T(8,128)(2,1)}, bf16[320,2048]{1,0:T(8,128)(2,1)}, u32[]{:S(2)}, u32[]{:S(2)}) collective-permute-start(bf16[320,2048]{1,0:T(8,128)(2,1)} %get-tuple-element.63.refs_1_), channel_id=1, source_target_pairs={{0,1},{1,0},{2,3},{3,2},{4,5},{5,4},{6,7},{7,6},{8,9},{9,8},{10,11... | collective-permute-start | bytes 3932168 | tf_op jit(solution)/shard_map/ppermute | solution.py:354
  33.8 18.4 %collective-permute-start.6 = (bf16[3,512,256]{2,1,0:T(8,128)(2,1)}, bf16[3,512,256]{2,1,0:T(8,128)(2,1)}, u32[]{:S(2)}, u32[]{:S(2)}) collective-permute-start(bf16[3,512,256]{2,1,0:T(8,128)(2,1)} %collective-permute-done.3), channel_id=1, source_target_pairs={{0,4},{1,5},{2,6},{3,7},{4,0},{5,1},{6,2},{7,3},{8,12},{9,13},{10,... | collective-permute-start | bytes 2359304 | tf_op jit(solution)/shard_map/ppermute | solution.py:354
  33.8 18.4 %collective-permute-start.7 = (bf16[3,512,256]{2,1,0:T(8,128)(2,1)}, bf16[3,512,256]{2,1,0:T(8,128)(2,1)}, u32[]{:S(2)}, u32[]{:S(2)}) collective-permute-start(bf16[3,512,256]{2,1,0:T(8,128)(2,1)} %get-tuple-element.59), channel_id=1, source_target_pairs={{4,8},{5,9},{6,10},{7,11},{8,4},{9,5},{10,6},{11,7},{20,24},{21,25... | collective-permute-start | bytes 2359304 | tf_op jit(solution)/shard_map/ppermute | solution.py:354
  35.4 18.4 %collective-permute-start.8 = (bf16[3,512,256]{2,1,0:T(8,128)(2,1)}, bf16[3,512,256]{2,1,0:T(8,128)(2,1)}, u32[]{:S(2)}, u32[]{:S(2)}) collective-permute-start(bf16[3,512,256]{2,1,0:T(8,128)(2,1)} %collective-permute-done.4.refs_8_), channel_id=1, source_target_pairs={{0,2},{1,3},{2,0},{3,1},{4,6},{5,7},{6,4},{7,5},{8,10},{9,11},{10,... | collective-permute-start | bytes 2359304 | tf_op jit(solution)/shard_map/ppermute | solution.py:354
  53.8 29.9 %collective-permute-start.9 = (bf16[320,2048]{1,0:T(8,128)(2,1)}, bf16[320,2048]{1,0:T(8,128)(2,1)}, u32[]{:S(2)}, u32[]{:S(2)}) collective-permute-start(bf16[320,2048]{1,0:T(8,128)(2,1)} %get-tuple-element.63.refs_1_), channel_id=1, source_target_pairs={{0,4},{1,5},{2,6},{3,7},{4,0},{5,1},{6,2},{7,3},{8,12},{9,13},{10,... | collective-permute-start | bytes 3932168 | tf_op jit(solution)/shard_map/ppermute | solution.py:354
  57.2 28.6 %collective-permute-start.2 = (bf16[320,2048]{1,0:T(8,128)(2,1)}, bf16[320,2048]{1,0:T(8,128)(2,1)}, u32[]{:S(2)}, u32[]{:S(2)}) collective-permute-start(bf16[320,2048]{1,0:T(8,128)(2,1)} %collective-permute-done.1.refs_2_), channel_id=1, source_target_pairs={{0,16},{1,17},{2,18},{3,19},{4,20},{5,21},{6,22},{7,23},{8,24},{9,... | collective-permute-start | bytes 3932168 | tf_op jit(solution)/shard_map/ppermute | solution.py:354
  57.2 37.3 %collective-permute-start.13 = (bf16[3,512,256]{2,1,0:T(8,128)(2,1)}, bf16[3,512,256]{2,1,0:T(8,128)(2,1)}, u32[]{:S(2)}, u32[]{:S(2)}) collective-permute-start(bf16[3,512,256]{2,1,0:T(8,128)(2,1)} %collective-permute-done.6), channel_id=1, source_target_pairs={{4,8},{5,9},{6,10},{7,11},{8,4},{9,5},{10,6},{11,7},{20,24},{21,25... | collective-permute-start | bytes 2359304 | tf_op jit(solution)/shard_map/ppermute | solution.py:354
  61.0 33.6 %collective-permute-start.15 = (bf16[3,512,256]{2,1,0:T(8,128)(2,1)}, bf16[3,512,256]{2,1,0:T(8,128)(2,1)}, u32[]{:S(2)}, u32[]{:S(2)}) collective-permute-start(bf16[3,512,256]{2,1,0:T(8,128)(2,1)} %broadcast_select_fusion.3.refs_10_), channel_id=1, source_target_pairs={{0,2},{1,3},{2,0},{3,1},{4,6},{5,7},{6,4},{7,5},{8,10},{9,11},{10,... | collective-permute-start | bytes 2359304 | tf_op jit(solution)/shard_map/ppermute | solution.py:354
  83.6 35.9 %collective-permute-start.10 = (bf16[320,2048]{1,0:T(8,128)(2,1)}, bf16[320,2048]{1,0:T(8,128)(2,1)}, u32[]{:S(2)}, u32[]{:S(2)}) collective-permute-start(bf16[320,2048]{1,0:T(8,128)(2,1)} %collective-permute-done.9.refs_2_), channel_id=1, source_target_pairs={{0,1},{1,0},{2,3},{3,2},{4,5},{5,4},{6,7},{7,6},{8,9},{9,8},{10,11... | collective-permute-start | bytes 3932168 | tf_op jit(solution)/shard_map/ppermute | solution.py:354
  94.5 13.3 %collective-permute-start.16 = (bf16[3,512,256]{2,1,0:T(8,128)(2,1)}, bf16[3,512,256]{2,1,0:T(8,128)(2,1)}, u32[]{:S(2)}, u32[]{:S(2)}) collective-permute-start(bf16[3,512,256]{2,1,0:T(8,128)(2,1)} %collective-permute-done.4.refs_8_), channel_id=1, source_target_pairs={{4,8},{5,9},{6,10},{7,11},{8,4},{9,5},{10,6},{11,7},{20,24},{21,25... | collective-permute-start | bytes 2359304 | tf_op jit(solution)/shard_map/ppermute | solution.py:354
  96.1 16.0 %collective-permute-start.17 = (bf16[3,512,256]{2,1,0:T(8,128)(2,1)}, bf16[3,512,256]{2,1,0:T(8,128)(2,1)}, u32[]{:S(2)}, u32[]{:S(2)}) collective-permute-start(bf16[3,512,256]{2,1,0:T(8,128)(2,1)} %get-tuple-element.68.refs_4_), channel_id=1, source_target_pairs={{0,2},{1,3},{2,0},{3,1},{4,6},{5,7},{6,4},{7,5},{8,10},{9,11},{10,... | collective-permute-start | bytes 2359304 | tf_op jit(solution)/shard_map/ppermute | solution.py:354
  97.6 22.4 %collective-permute-start.14 = (bf16[3,512,256]{2,1,0:T(8,128)(2,1)}, bf16[3,512,256]{2,1,0:T(8,128)(2,1)}, u32[]{:S(2)}, u32[]{:S(2)}) collective-permute-start(bf16[3,512,256]{2,1,0:T(8,128)(2,1)} %collective-permute-done.13), channel_id=1, source_target_pairs={{4,0},{5,1},{6,2},{7,3},{8,12},{9,13},{10,14},{11,15},{20,16},{21,... | collective-permute-start | bytes 2359304 | tf_op jit(solution)/shard_map/ppermute | solution.py:354
  119.5 17.8 %collective-permute-start.11 = (bf16[320,2048]{1,0:T(8,128)(2,1)}, bf16[320,2048]{1,0:T(8,128)(2,1)}, u32[]{:S(2)}, u32[]{:S(2)}) collective-permute-start(bf16[320,2048]{1,0:T(8,128)(2,1)} %collective-permute-done.9.refs_2_), channel_id=1, source_target_pairs={{0,16},{1,17},{2,18},{3,19},{4,20},{5,21},{6,22},{7,23},{8,24},{9,... | collective-permute-start | bytes 3932168 | tf_op jit(solution)/shard_map/ppermute | solution.py:354
  119.5 17.7 %collective-permute-start.12 = (bf16[320,2048]{1,0:T(8,128)(2,1)}, bf16[320,2048]{1,0:T(8,128)(2,1)}, u32[]{:S(2)}, u32[]{:S(2)}) collective-permute-start(bf16[320,2048]{1,0:T(8,128)(2,1)} %collective-permute-done.10.refs_3_), channel_id=1, source_target_pairs={{0,16},{1,17},{2,18},{3,19},{4,20},{5,21},{6,22},{7,23},{8,24},{9,... | collective-permute-start | bytes 3932168 | tf_op jit(solution)/shard_map/ppermute | solution.py:354
  122.2 32.1 %collective-permute-start.18 = (bf16[3,512,256]{2,1,0:T(8,128)(2,1)}, bf16[3,512,256]{2,1,0:T(8,128)(2,1)}, u32[]{:S(2)}, u32[]{:S(2)}) collective-permute-start(bf16[3,512,256]{2,1,0:T(8,128)(2,1)} %broadcast_select_fusion.2.refs_2_), channel_id=1, source_target_pairs={{0,2},{1,3},{2,0},{3,1},{4,6},{5,7},{6,4},{7,5},{8,10},{9,11},{10,... | collective-permute-start | bytes 2359304 | tf_op jit(solution)/shard_map/ppermute | solution.py:354
  123.7 36.2 %collective-permute-start.22 = (bf16[3,512,256]{2,1,0:T(8,128)(2,1)}, bf16[3,512,256]{2,1,0:T(8,128)(2,1)}, u32[]{:S(2)}, u32[]{:S(2)}) collective-permute-start(bf16[3,512,256]{2,1,0:T(8,128)(2,1)} %get-tuple-element.74), channel_id=1, source_target_pairs={{4,8},{5,9},{6,10},{7,11},{8,4},{9,5},{10,6},{11,7},{20,24},{21,25... | collective-permute-start | bytes 2359304 | tf_op jit(solution)/shard_map/ppermute | solution.py:354
  125.3 34.7 %collective-permute-start.21 = (bf16[3,512,256]{2,1,0:T(8,128)(2,1)}, bf16[3,512,256]{2,1,0:T(8,128)(2,1)}, u32[]{:S(2)}, u32[]{:S(2)}) collective-permute-start(bf16[3,512,256]{2,1,0:T(8,128)(2,1)} %collective-permute-done.20), channel_id=1, source_target_pairs={{0,4},{1,5},{2,6},{3,7},{4,0},{5,1},{6,2},{7,3},{8,12},{9,13},{10,... | collective-permute-start | bytes 2359304 | tf_op jit(solution)/shard_map/ppermute | solution.py:354
  159.9 13.5 %collective-permute-start.19 = (bf16[640,768]{1,0:T(8,128)(2,1)}, bf16[640,768]{1,0:T(8,128)(2,1)}, u32[]{:S(2)}, u32[]{:S(2)}) collective-permute-start(bf16[640,768]{1,0:T(8,128)(2,1)} %shard_map.63), channel_id=1, source_target_pairs={{0,16},{1,17},{2,18},{3,19},{4,20},{5,21},{6,22},{7,23},{8,24},{9,... | collective-permute-start | bytes 2949128 | tf_op jit(solution)/shard_map/ppermute | solution.py:354
  162.0 20.3 %collective-permute-start.24 = (bf16[3,512,256]{2,1,0:T(8,128)(2,1)}, bf16[3,512,256]{2,1,0:T(8,128)(2,1)}, u32[]{:S(2)}, u32[]{:S(2)}) collective-permute-start(bf16[3,512,256]{2,1,0:T(8,128)(2,1)} %get-tuple-element.77), channel_id=1, source_target_pairs={{0,4},{1,5},{2,6},{3,7},{4,0},{5,1},{6,2},{7,3},{8,12},{9,13},{10,... | collective-permute-start | bytes 2359304 | tf_op jit(solution)/shard_map/ppermute | solution.py:354
  162.0 20.3 %collective-permute-start.23 = (bf16[3,512,256]{2,1,0:T(8,128)(2,1)}, bf16[3,512,256]{2,1,0:T(8,128)(2,1)}, u32[]{:S(2)}, u32[]{:S(2)}) collective-permute-start(bf16[3,512,256]{2,1,0:T(8,128)(2,1)} %collective-permute-done.21), channel_id=1, source_target_pairs={{4,8},{5,9},{6,10},{7,11},{8,4},{9,5},{10,6},{11,7},{20,24},{21,25... | collective-permute-start | bytes 2359304 | tf_op jit(solution)/shard_map/ppermute | solution.py:354
  163.6 20.3 %collective-permute-start.25 = (bf16[3,512,256]{2,1,0:T(8,128)(2,1)}, bf16[3,512,256]{2,1,0:T(8,128)(2,1)}, u32[]{:S(2)}, u32[]{:S(2)}) collective-permute-start(bf16[3,512,256]{2,1,0:T(8,128)(2,1)} %broadcast_select_fusion.1.refs_6_), channel_id=1, source_target_pairs={{0,2},{1,3},{2,0},{3,1},{4,6},{5,7},{6,4},{7,5},{8,10},{9,11},{10,... | collective-permute-start | bytes 2359304 | tf_op jit(solution)/shard_map/ppermute | solution.py:354
  183.8 19.3 %collective-permute-start.27 = (bf16[3,512,256]{2,1,0:T(8,128)(2,1)}, bf16[3,512,256]{2,1,0:T(8,128)(2,1)}, u32[]{:S(2)}, u32[]{:S(2)}) collective-permute-start(bf16[3,512,256]{2,1,0:T(8,128)(2,1)} %collective-permute-done.24.refs_4_), channel_id=1, source_target_pairs={{4,8},{5,9},{6,10},{7,11},{8,4},{9,5},{10,6},{11,7},{20,24},{21,25... | collective-permute-start | bytes 2359304 | tf_op jit(solution)/shard_map/ppermute | solution.py:354
  185.4 22.3 %collective-permute-start.28 = (bf16[3,512,256]{2,1,0:T(8,128)(2,1)}, bf16[3,512,256]{2,1,0:T(8,128)(2,1)}, u32[]{:S(2)}, u32[]{:S(2)}) collective-permute-start(bf16[3,512,256]{2,1,0:T(8,128)(2,1)} %collective-permute-done.23), channel_id=1, source_target_pairs={{4,0},{5,1},{6,2},{7,3},{8,12},{9,13},{10,14},{11,15},{20,16},{21,... | collective-permute-start | bytes 2359304 | tf_op jit(solution)/shard_map/ppermute | solution.py:354
  186.7 22.3 %collective-permute-start.29 = (bf16[3,512,256]{2,1,0:T(8,128)(2,1)}, bf16[3,512,256]{2,1,0:T(8,128)(2,1)}, u32[]{:S(2)}, u32[]{:S(2)}) collective-permute-start(bf16[3,512,256]{2,1,0:T(8,128)(2,1)} %collective-permute-done.24.refs_4_), channel_id=1, source_target_pairs={{0,2},{1,3},{2,0},{3,1},{4,6},{5,7},{6,4},{7,5},{8,10},{9,11},{10,... | collective-permute-start | bytes 2359304 | tf_op jit(solution)/shard_map/ppermute | solution.py:354
  209.9 18.5 %collective-permute-start.39 = (bf16[3,512,256]{2,1,0:T(8,128)(2,1)S(1)}, bf16[3,512,256]{2,1,0:T(8,128)(2,1)}, u32[]{:S(2)}, u32[]{:S(2)}) collective-permute-start(bf16[3,512,256]{2,1,0:T(8,128)(2,1)S(1)} %broadcast_select_fusion.refs_6_), channel_id=1, source_target_pairs={{0,2},{1,3},{2,0},{3,1},{4,6},{5,7},{6,4},{7,5},{8,10},{9,11},{10,... | collective-permute-start | bytes 2359304 | tf_op jit(solution)/shard_map/ppermute | solution.py:354
  235.4 17.4 %collective-permute-start.40 = (bf16[640,768]{1,0:T(8,128)(2,1)}, bf16[640,768]{1,0:T(8,128)(2,1)}, u32[]{:S(2)}, u32[]{:S(2)}) collective-permute-start(bf16[640,768]{1,0:T(8,128)(2,1)} %shard_map.68), channel_id=1, source_target_pairs={{0,16},{1,17},{2,18},{3,19},{4,20},{5,21},{6,22},{7,23},{8,24},{9,... | collective-permute-start | bytes 2949128 | tf_op jit(solution)/shard_map/ppermute | solution.py:354
  235.4 14.6 %collective-permute-start.52 = (bf16[1,256,1024]{2,1,0:T(8,128)(2,1)}, bf16[1,256,1024]{2,1,0:T(8,128)(2,1)}, u32[]{:S(2)}, u32[]{:S(2)}) collective-permute-start(bf16[1,256,1024]{2,1,0:T(8,128)(2,1)} %get-tuple-element.93.refs_3_.refs_7_), channel_id=1, source_target_pairs={{0,2},{1,3},{2,0},{3,1},{4,6},{5,7},{6,4},{7,5},{8,10},{9,11},{10,... | collective-permute-start | bytes 1572872 | tf_op jit(solution)/shard_map/ppermute | solution.py:354
  236.2 13.9 %collective-permute-start.26 = (bf16[640,256]{1,0:T(8,128)(2,1)}, bf16[640,256]{1,0:T(8,128)(2,1)}, u32[]{:S(2)}, u32[]{:S(2)}) collective-permute-start(bf16[640,256]{1,0:T(8,128)(2,1)} %shard_map.64), channel_id=1, source_target_pairs={{0,1},{1,0},{2,3},{3,2},{4,5},{5,4},{6,7},{7,6},{8,9},{9,8},{10,11... | collective-permute-start | bytes 983048 | tf_op jit(solution)/shard_map/ppermute | solution.py:354
  236.7 29.4 %collective-permute-start.49 = (bf16[1,256,1024]{2,1,0:T(8,128)(2,1)}, bf16[1,256,1024]{2,1,0:T(8,128)(2,1)}, u32[]{:S(2)}, u32[]{:S(2)}) collective-permute-start(bf16[1,256,1024]{2,1,0:T(8,128)(2,1)} %collective-permute-done.32), channel_id=1, source_target_pairs={{4,8},{5,9},{6,10},{7,11},{8,4},{9,5},{10,6},{11,7},{20,24},{21,25... | collective-permute-start | bytes 1572872 | tf_op jit(solution)/shard_map/ppermute | solution.py:354
  238.2 12.6 %collective-permute-start.33 = (bf16[640,256]{1,0:T(8,128)(2,1)}, bf16[640,256]{1,0:T(8,128)(2,1)}, u32[]{:S(2)}, u32[]{:S(2)}) collective-permute-start(bf16[640,256]{1,0:T(8,128)(2,1)} %shard_map.64), channel_id=1, source_target_pairs={{0,4},{1,5},{2,6},{3,7},{4,0},{5,1},{6,2},{7,3},{8,12},{9,13},{10,... | collective-permute-start | bytes 983048 | tf_op jit(solution)/shard_map/ppermute | solution.py:354
  250.0 21.5 %collective-permute-start.53 = (bf16[1,256,1024]{2,1,0:T(8,128)(2,1)}, bf16[1,256,1024]{2,1,0:T(8,128)(2,1)}, u32[]{:S(2)}, u32[]{:S(2)}) collective-permute-start(bf16[1,256,1024]{2,1,0:T(8,128)(2,1)} %collective-permute-done.31.refs_5_.refs_9_), channel_id=1, source_target_pairs={{0,2},{1,3},{2,0},{3,1},{4,6},{5,7},{6,4},{7,5},{8,10},{9,11},{10,... | collective-permute-start | bytes 1572872 | tf_op jit(solution)/shard_map/ppermute | solution.py:354
  250.8 17.5 %collective-permute-start.34 = (bf16[640,256]{1,0:T(8,128)(2,1)}, bf16[640,256]{1,0:T(8,128)(2,1)}, u32[]{:S(2)}, u32[]{:S(2)}) collective-permute-start(bf16[640,256]{1,0:T(8,128)(2,1)} %collective-permute-done.33), channel_id=1, source_target_pairs={{0,1},{1,0},{2,3},{3,2},{4,5},{5,4},{6,7},{7,6},{8,9},{9,8},{10,11... | collective-permute-start | bytes 983048 | tf_op jit(solution)/shard_map/ppermute | solution.py:354
  252.0 17.6 %collective-permute-start.36 = (bf16[640,256]{1,0:T(8,128)(2,1)}, bf16[640,256]{1,0:T(8,128)(2,1)}, u32[]{:S(2)}, u32[]{:S(2)}) collective-permute-start(bf16[640,256]{1,0:T(8,128)(2,1)} %collective-permute-done.26), channel_id=1, source_target_pairs={{0,16},{1,17},{2,18},{3,19},{4,20},{5,21},{6,22},{7,23},{8,24},{9,... | collective-permute-start | bytes 983048 | tf_op jit(solution)/shard_map/ppermute | solution.py:354
  252.8 17.5 %collective-permute-start.37 = (bf16[640,256]{1,0:T(8,128)(2,1)}, bf16[640,256]{1,0:T(8,128)(2,1)}, u32[]{:S(2)}, u32[]{:S(2)}) collective-permute-start(bf16[640,256]{1,0:T(8,128)(2,1)} %collective-permute-done.33), channel_id=1, source_target_pairs={{0,16},{1,17},{2,18},{3,19},{4,20},{5,21},{6,22},{7,23},{8,24},{9,... | collective-permute-start | bytes 983048 | tf_op jit(solution)/shard_map/ppermute | solution.py:354
  269.6 18.1 %collective-permute-start.51 = (bf16[1,256,1024]{2,1,0:T(8,128)(2,1)}, bf16[1,256,1024]{2,1,0:T(8,128)(2,1)S(1)}, u32[]{:S(2)}, u32[]{:S(2)}) collective-permute-start(bf16[1,256,1024]{2,1,0:T(8,128)(2,1)} %collective-permute-done.31.refs_5_.refs_9_), channel_id=1, source_target_pairs={{4,8},{5,9},{6,10},{7,11},{8,4},{9,5},{10,6},{11,7},{20,24},{21,25... | collective-permute-start | bytes 1572872 | tf_op jit(solution)/shard_map/ppermute | solution.py:354
  270.3 17.4 %collective-permute-start.50 = (bf16[1,256,1024]{2,1,0:T(8,128)(2,1)}, bf16[1,256,1024]{2,1,0:T(8,128)(2,1)S(1)}, u32[]{:S(2)}, u32[]{:S(2)}) collective-permute-start(bf16[1,256,1024]{2,1,0:T(8,128)(2,1)} %collective-permute-done.49), channel_id=1, source_target_pairs={{4,0},{5,1},{6,2},{7,3},{8,12},{9,13},{10,14},{11,15},{20,16},{21,... | collective-permute-start | bytes 1572872 | tf_op jit(solution)/shard_map/ppermute | solution.py:354
  277.0 12.1 %collective-permute-start.43 = (bf16[640,256]{1,0:T(8,128)(2,1)}, bf16[640,256]{1,0:T(8,128)(2,1)}, u32[]{:S(2)}, u32[]{:S(2)}) collective-permute-start(bf16[640,256]{1,0:T(8,128)(2,1)} %collective-permute-done.42), channel_id=1, source_target_pairs={{0,1},{1,0},{2,3},{3,2},{4,5},{5,4},{6,7},{7,6},{8,9},{9,8},{10,11... | collective-permute-start | bytes 983048 | tf_op jit(solution)/shard_map/ppermute | solution.py:354
  279.1 12.5 %collective-permute-start.54 = (bf16[1,256,1024]{2,1,0:T(8,128)(2,1)S(1)}, bf16[1,256,1024]{2,1,0:T(8,128)(2,1)S(1)}, u32[]{:S(2)}, u32[]{:S(2)}) collective-permute-start(bf16[1,256,1024]{2,1,0:T(8,128)(2,1)S(1)} %broadcast_select_fusion.4.refs_7_.refs_11_), channel_id=1, source_target_pairs={{0,2},{1,3},{2,0},{3,1},{4,6},{5,7},{6,4},{7,5},{8,10},{9,11},{10,... | collective-permute-start | bytes 1572872 | tf_op jit(solution)/shard_map/ppermute | solution.py:354
  283.0 24.1 %collective-permute-start.44 = (bf16[640,256]{1,0:T(8,128)(2,1)}, bf16[640,256]{1,0:T(8,128)(2,1)}, u32[]{:S(2)}, u32[]{:S(2)}) collective-permute-start(bf16[640,256]{1,0:T(8,128)(2,1)} %shard_map.69), channel_id=1, source_target_pairs={{0,16},{1,17},{2,18},{3,19},{4,20},{5,21},{6,22},{7,23},{8,24},{9,... | collective-permute-start | bytes 983048 | tf_op jit(solution)/shard_map/ppermute | solution.py:354
  287.7 19.5 %collective-permute-start.46 = (bf16[640,256]{1,0:T(8,128)(2,1)}, bf16[640,256]{1,0:T(8,128)(2,1)}, u32[]{:S(2)}, u32[]{:S(2)}) collective-permute-start(bf16[640,256]{1,0:T(8,128)(2,1)} %collective-permute-done.42), channel_id=1, source_target_pairs={{0,16},{1,17},{2,18},{3,19},{4,20},{5,21},{6,22},{7,23},{8,24},{9,... | collective-permute-start | bytes 983048 | tf_op jit(solution)/shard_map/ppermute | solution.py:354
  287.7 19.5 %collective-permute-start.45 = (bf16[640,256]{1,0:T(8,128)(2,1)}, bf16[640,256]{1,0:T(8,128)(2,1)}, u32[]{:S(2)}, u32[]{:S(2)}) collective-permute-start(bf16[640,256]{1,0:T(8,128)(2,1)} %collective-permute-done.41), channel_id=1, source_target_pairs={{0,16},{1,17},{2,18},{3,19},{4,20},{5,21},{6,22},{7,23},{8,24},{9,... | collective-permute-start | bytes 983048 | tf_op jit(solution)/shard_map/ppermute | solution.py:354
  289.1 18.0 %collective-permute-start.47 = (bf16[640,256]{1,0:T(8,128)(2,1)}, bf16[640,256]{1,0:T(8,128)(2,1)}, u32[]{:S(2)}, u32[]{:S(2)}) collective-permute-start(bf16[640,256]{1,0:T(8,128)(2,1)} %collective-permute-done.43), channel_id=1, source_target_pairs={{0,16},{1,17},{2,18},{3,19},{4,20},{5,21},{6,22},{7,23},{8,24},{9,... | collective-permute-start | bytes 983048 | tf_op jit(solution)/shard_map/ppermute | solution.py:354
  292.4 18.0 %collective-permute-start.55 = (bf16[1,256,1024]{2,1,0:T(8,128)(2,1)}, bf16[1,256,1024]{2,1,0:T(8,128)(2,1)}, u32[]{:S(2)}, u32[]{:S(2)}) collective-permute-start(bf16[1,256,1024]{2,1,0:T(8,128)(2,1)} %broadcast_select_fusion.5.refs_5_.refs_13_), channel_id=1, source_target_pairs={{0,2},{1,3},{2,0},{3,1},{4,6},{5,7},{6,4},{7,5},{8,10},{9,11},{10,... | collective-permute-start | bytes 1572872 | tf_op jit(solution)/shard_map/ppermute | solution.py:354
  328.8 21.2 %collective-permute-start.56 = (bf16[640,1024]{1,0:T(8,128)(2,1)}, bf16[640,1024]{1,0:T(8,128)(2,1)}, u32[]{:S(2)}, u32[]{:S(2)}) collective-permute-start(bf16[640,1024]{1,0:T(8,128)(2,1)} %bitcast.58), channel_id=1, source_target_pairs={{0,16},{1,17},{2,18},{3,19},{4,20},{5,21},{6,22},{7,23},{8,24},{9,... | collective-permute-start | bytes 3932168 | tf_op jit(solution)/shard_map/ppermute | solution.py:354
  330.9 16.7 %collective-permute-start.58 = (bf16[320,1024]{1,0:T(8,128)(2,1)S(1)}, bf16[320,1024]{1,0:T(8,128)(2,1)S(1)}, u32[]{:S(2)}, u32[]{:S(2)}) collective-permute-start(bf16[320,1024]{1,0:T(8,128)(2,1)S(1)} %bitcast_select_fusion), channel_id=1, source_target_pairs={{0,4},{1,5},{2,6},{3,7},{4,0},{5,1},{6,2},{7,3},{8,12},{9,13},{10,... | collective-permute-start | bytes 1966088 | tf_op jit(solution)/shard_map/ppermute | solution.py:354
  (21 other events, 160.1 us)

commit v5 on v4

--- a/solution.py
+++ b/solution.py
@@ -33,7 +33,7 @@
 def halves(weight, outer, chunk, chunks, *earlier):
     kinds, depth, width = weight.shape
     part = width // 2 // chunks
-    tile = min(depth, 128)
+    tile = min(depth, 256)
 
     def kernel(o_ref, first_ref, last_ref, low_ref, high_ref, mine_ref, away_ref):
         low, high = first_ref[...], last_ref[...]
@@ -65,7 +65,7 @@
     slots, blocks, length, _ = shape
     shards = len(mine)
     count, features = mine[0].shape
-    tile = 80 if count % 80 == 0 else count
+    tile = 160 if count % 160 == 0 else count
     steps, half = count // tile, length // 2
     per = features // kept
 
@@ -217,31 +217,34 @@
     )
 
 
-def combine(places, groups, total, final, slots):
-    _, _, length, held = groups[0][0].shape
-    features = groups[0][2][0][0].shape[2]
+def combine(places, groups, total, final, slots, offset=0):
+    _, length, held = groups[0][0].shape
+    features = groups[0][3][0][0].shape[2]
     tile = min(features, 256)
-    terms = [(pieces, parity, pair) for pieces, parity, pairs in groups for pair in pairs]
+    terms = [group[:3] + (pair,) for group in groups for pair in group[3]]
     count = len(terms)
 
     def kernel(p_ref, *refs):
         out_ref = refs[-1]
-        summed = None if total is None else refs[3 * count][0]
-        for i, (_, parity, _) in enumerate(terms):
-            near, far = refs[count + 2 * i][0], refs[count + 2 * i + 1][0]
+        summed = None if total is None else refs[4 * count][0]
+        slot = (p_ref[0] + pl.program_id(0)) % 2
+        for i, (_, _, parity, _) in enumerate(terms):
+            near, far = refs[2 * count + 2 * i][0], refs[2 * count + 2 * i + 1][0]
             block = jnp.where(p_ref[1] == parity, near, far)
-            part = jnp.dot(refs[i][0, 0], block, preferred_element_type=F32)
+            rows = jnp.where(slot == 0, refs[2 * i][0], refs[2 * i + 1][0])
+            part = jnp.dot(rows, block, preferred_element_type=F32)
             summed = part if summed is None else summed + part
         out_ref[0] = summed.astype(out_ref.dtype)
 
     def piece(i):
-        return pl.BlockSpec((1, 1, length, held), lambda s, n, p: (p[0] + s, p[2 + i], 0, 0))
+        return pl.BlockSpec((1, length, held), lambda s, n, p: (p[2 + i], 0, 0))
 
     block_spec = pl.BlockSpec((1, held, tile), lambda s, n, p: (0, 0, n))
-    in_specs = [piece(i) for i in range(count)] + [block_spec] * (2 * count)
-    args = [pieces for pieces, _, _ in terms] + [b for _, _, pair in terms for b in pair]
+    in_specs = [piece(i) for i in range(count) for _ in range(2)] + [block_spec] * (2 * count)
+    args = [pieces for term in terms for pieces in term[:2]]
+    args += [b for term in terms for b in term[3]]
     if total is not None:
-        in_specs.append(pl.BlockSpec((1, length, tile), lambda s, n, p: (p[0] + s, 0, n)))
+        in_specs.append(pl.BlockSpec((1, length, tile), lambda s, n, p: (offset + s, 0, n)))
         args.append(total)
     return call(
         kernel,
@@ -395,36 +398,36 @@
 
         weight = qkv_weight[0].transpose(1, 0, 2)
         low_a, high_a, mine_a, away_a = halves(weight, outer, 0, 2)
+        m1a = move(low_a, across_or_stay)
         e1a = move(away_a, edge)
-        m1a = move(low_a, across_or_stay)
         p1a = move(mine_a, pair)
         rows = lax.dynamic_slice_in_dim(tokens, core * half, half, 0)
         fetched = over_tensor(rows, mine_a)
-        other_modality = move(modality, edge)
+        other_modality = move(modality, edge, mine_a)
         low_b, high_b, mine_b, away_b = halves(weight, outer, 1, 2, mine_a)
         rest_rows = lax.dynamic_slice_in_dim(tokens, (1 - core) * half, half, 0)
-
-        ready = (e1a, m1a, p1a, mine_b, other_modality)
-        e2a = move(m1a, edge, *ready)
-        m2a = move(high_a, across, *ready)
-        p2a = move(e1a, pair, *ready)
+        top, bottom = rows[: half // 2], rows[half // 2 :]
+
+        m2a = move(high_a, across, m1a)
+        e2a = move(m1a, edge, e1a)
+        p2a = move(e1a, pair, p1a, mine_b, rest_rows)
         low_o, high_o, mine_o, away_o = halves(out_weight, outer, 0, 1, mine_b, e1a)
         swapped = [rest_rows] + [to_core(a) for a in fetched[1:]]
 
-        ready = (e2a, m2a, p2a, mine_o, fetched[-1])
-        m3a = move(e2a, across, *ready)
-        passed = move(rows, edge, *ready)
+        m3a = move(e2a, across, m2a)
+        passed_top = move(top, edge, e2a, other_modality)
         third_a = choose(e2a, m2a)
-        p3a = move(third_a, pair, *ready)
+        p3a = move(third_a, pair, p2a, mine_o)
         gains = norm_gains[0].reshape(places, 1, kept)
         shape = (2, places, length, kept)
         normed = normalize(
             jnp.stack([core, own, which]), None, gains, fetched, swapped, shape, 0, kept
         )
 
-        ready = (m3a, p3a, normed)
-        m4a = move(e1a, across, *ready)
-        p1b = move(mine_b, pair, *ready)
+        m4a = move(e1a, across, m3a)
+        passed_bottom = move(bottom, edge, passed_top)
+        p1b = move(mine_b, pair, p3a, normed)
+        part_top = over_tensor(passed_top, passed_top)
 
         def add(slot, blocks, total, final=False, fresh=False):
             found = [slot]
@@ -436,25 +439,35 @@
         first_a = [(at[0], mine_a, p1a), (at[1], e1a, p2a), (at[2], third_a, p3a)]
         total_a = add(which, first_a, None, fresh=True)
 
-        e3a = move(m3a, outward, passed)
-        part = over_tensor(passed)
-        m1b = move(low_b, across_or_stay, m4a, p1b, total_a)
-        part_swapped = [to_core(a) for a in part]
-        fourth_a = choose(e3a, m4a)
-        p4a = move(fourth_a, pair, p1b)
+        m1b = move(low_b, across_or_stay, m4a)
+        e3a = move(m3a, outward, passed_bottom)
+        part_bottom = over_tensor(passed_bottom, passed_bottom)
+        top_swapped = [to_core(a) for a in part_top]
+        normed = normalize(
+            jnp.stack([core, own, 1 - which]), normed, gains, part_top, top_swapped, shape, 0, kept
+        )
 
         m2b = move(high_b, across, m1b)
         e2b = move(m1b, edge, e3a)
+        fourth_a = choose(e3a, m4a)
+        p4a = move(fourth_a, pair, p1b, total_a, normed)
+        bottom_swapped = [to_core(a) for a in part_bottom]
         normed = normalize(
-            jnp.stack([core, own, 1 - which]), normed, gains, part, part_swapped, shape, 0, kept
+            jnp.stack([core, own, 1 - which]),
+            normed,
+            gains,
+            part_bottom,
+            bottom_swapped,
+            shape,
+            half // 2,
+            kept,
         )
-
-        ready = (m2b, e2b, p4a, normed)
-        m3b = move(e2b, across, *ready)
-        e1b = move(away_b, edge, *ready)
+        total_a = add(1 - which, first_a, total_a, fresh=True)
+
+        m3b = move(e2b, across, m2b)
+        e1b = move(away_b, edge, e2b)
         third_b = choose(e2b, m2b)
-        p3b = move(third_b, pair, *ready)
-        total_a = add(1 - which, first_a, total_a, fresh=True)
+        p3b = move(third_b, pair, p4a, total_a)
         zero, one = jnp.zeros((), I32), jnp.ones((), I32)
         last_a = [(at[3], fourth_a, p4a)]
         theirs_a = add(one, last_a, total_a, final=True)
@@ -463,70 +476,66 @@
         own_rows = (modality == core).astype(I32)[:, None]
         other_rows = (other_modality == core).astype(I32)[:, None]
         mine_rows = jnp.where(which == 0, own_rows, other_rows)
+
+        m4b = move(e1b, across, m3b)
+        e3b = move(m3b, outward, e1b)
+        p2b = move(e1b, pair, p3b, ours_a)
         attended_a = attend(ours_a, got_a, mine_rows)
-
-        ready = (m3b, e1b, p3b, attended_a)
-        m4b = move(e1b, across, *ready)
-        e3b = move(m3b, outward, *ready)
-        p2b = move(e1b, pair, *ready)
-        held_a = over_tensor(attended_a, *ready)
-        first_b = [(at[0], mine_b, p1b), (at[1], e1b, p2b), (at[2], third_b, p3b)]
-        some_b = [first_b[0], first_b[2]]
-        total_b = add(which, some_b, None, fresh=True)
-        total_b = add(1 - which, some_b, total_b, fresh=True)
-
-        ready = (m4b, e3b, p2b, total_b)
+        first_b = [(at[0], mine_b, p1b), (at[2], third_b, p3b)]
+        total_b = add(which, first_b, None, fresh=True)
+        held_a = over_tensor(attended_a)
+
+        m1o = move(low_o, across_or_stay, m4b)
         fourth_b = choose(e3b, m4b)
-        p4b = move(fourth_b, pair, *ready)
-        m1o = move(low_o, across_or_stay, *ready)
-        e1o = move(away_o, edge, *ready)
+        p4b = move(fourth_b, pair, p2b, attended_a)
+        e1o = move(away_o, edge, e3b)
+        total_b = add(1 - which, first_b, total_b, fresh=True)
+        held_a += over_tensor(move(attended_a, edge, e1o))
+
+        m2o = move(high_o, across, m1o)
+        e2o = move(m1o, edge, held_a[shards])
+        p1o = move(mine_o, pair, p4b)
         last_b = [(at[1], e1b, p2b), (at[3], fourth_b, p4b)]
-
-        ready = (m1o, e1o)
-        m2o = move(high_o, across, *ready)
-        e2o = move(m1o, edge, *ready)
-        p1o = move(mine_o, pair, p4b)
-        p2o = move(e1o, pair, p1o)
         theirs_b = add(one, last_b, total_b, final=True)
         got_b = to_core(theirs_b)
         ours_b = add(zero, last_b, total_b, final=True)
+        stack_a = jnp.stack(held_a)
+        pieces_a = (stack_a, to_core(stack_a))
         attended_b = attend(ours_b, got_b, mine_rows)
 
-        held_a += over_tensor(move(attended_a, edge, e2o))
+        p2o = move(e1o, pair, p1o)
         m3o = move(e2o, across, m2o)
         m4o = move(e1o, across, m3o)
+        third_o = choose(e2o, m2o)
+        p3o = move(third_o, pair, p2o)
         e3o = move(m3o, outward)
-        third_o, fourth_o = choose(e2o, m2o), choose(e3o, m4o)
-        p3o = move(third_o, pair, p2o)
-        p4o = move(fourth_o, pair, p3o)
+        fourth_o = choose(e3o, m4o)
         held_b = over_tensor(attended_b)
-        held_b += over_tensor(move(attended_b, edge))
-
-        pieces = [
-            jnp.stack([jnp.stack(held), jnp.stack([to_core(a) for a in held])])
-            for held in (held_a, held_b)
-        ]
-        blocks = [(mine_o, p1o), (e1o, p2o), (third_o, p3o), (fourth_o, p4o)]
+        held_b += over_tensor(move(attended_b, edge, e2o))
+        blocks = [(mine_o, p1o), (e1o, p2o), (third_o, p3o)]
 
         def piece_of(k):
             shard, part = k // 2, k % 2
             return jnp.where(part == column, 0, shards) + (own - shard + shards) % shards
 
         found = [piece_of(k) for k in at]
-        near = [(pieces[0], 0, blocks[:3])]
-        rest = [(pieces[0], 0, blocks[3:]), (pieces[1], 1, blocks)]
         total = combine(
-            jnp.stack([zero, y] + found[:3]).astype(I32), near, None, False, 2
+            jnp.stack([1 - which, y] + found[:3]).astype(I32), [pieces_a + (0, blocks)], None, False, 2
         )
-
-        def finish(slot):
+        p4o = move(fourth_o, pair, p3o)
+        last = [(fourth_o, p4o)]
+        stack_b = jnp.stack(held_b)
+        pieces_b = (stack_b, to_core(stack_b))
+        rest = [pieces_a + (0, last), pieces_b + (1, blocks + last)]
+
+        def finish(slot, offset):
             order = jnp.stack([slot, y, found[3]] + found).astype(I32)
-            return combine(order, rest, total, True, 1)[0]
-
-        away = finish(1 - which)
-        near = finish(which)
+            return combine(order, rest, total, True, 1, offset)[0]
+
+        away = finish(1 - which, 0)
         kept_away = lax.dynamic_slice_in_dim(away, core * half, half, 0)
         sent_away = to_core(lax.dynamic_slice_in_dim(away, (1 - core) * half, half, 0))
+        near = finish(which, 1)
         keep = lax.dynamic_slice_in_dim(other_rows, core * half, half, 0)
         far = move(jnp.where(keep != 0, kept_away, sent_away), edge)
         return assemble(

time: 359 us -> 361 us (level)
  other arithmetic: 25.1 us -> 18.7 us
  waiting for transfers between devices: 105 us -> 111 us
    another operation x6 -> x2, other arithmetic: 9.06 us -> 2.5 us  [the longest x1 1.28 us: line_plan(): stack_a = jnp.stack(held_a)]
    ppermute x60 -> x58, waiting for transfers between devices: 105 us -> 111 us  [move(): lax.ppermute(after(array, *earlier) if earlier else array, AXES, pairs)]
    pallas_call x19 -> x20, Pallas kernels: 126 us -> 124 us  [call(): pl.pallas_call(kernel, grid_spec=pltpu.PrefetchScalarGridSpec(num_scalar_...]
    ppermute x60 -> x58, starting transfers between devices: 84.5 us -> 85.9 us  [move(): lax.ppermute(after(array, *earlier) if earlier else array, AXES, pairs)]
  transfers between devices with their start and end apart: 60 -> 58, of which waited for: 18 -> 23; matrix products, arithmetic and copies ran while one was open for 10% -> 9% of each run, Pallas kernels for 31% -> 30%
where the time goes in v5:
time: 361 us; the launch traced here: 359 us
  Pallas kernels  124 us (34%)
  waiting for transfers between devices  111 us (31%)
  starting transfers between devices  85.9 us (24%)
  local copies, waits for them, and re-layouts  19 us (5%)
  other arithmetic  18.7 us (5%)
    pallas_call x20, Pallas kernels, call(): pl.pallas_call(kernel, grid_spec=pltpu.PrefetchScalarGridSpec(num_scalar_...  124 us
    ppermute x58, waiting for transfers between devices, move(): lax.ppermute(after(array, *earlier) if earlier else array, AXES, pairs)  111 us
    ppermute x58, starting transfers between devices, move(): lax.ppermute(after(array, *earlier) if earlier else array, AXES, pairs)  85.9 us
    select_n x6, other arithmetic, choose(): return jnp.where(outer == 1, edge_block, middle_block)  9.57 us
  transfers between devices with their start and end apart: 58, of which 23 were waited for; matrix products, arithmetic and copies ran while one was open for 9% of the time, Pallas kernels for 30%

profile of v5, /device:TPU:0, one launch (start us, length us, event | category | flops | bytes accessed | tf_op | source)
XLA Modules:
  0.0 358.7 jit_solution(4592966658844852532)
XLA Ops:
  0.0 2.9 shard_map.55
  4.7 4.8 %collective-permute-start.4 = (bf16[3,512,256]{2,1,0:T(8,128)(2,1)}, bf16[3,512,256]{2,1,0:T(8,128)(2,1)S(1)}, u32[]{:S(2)}, u32[]{:S(2)}) collective-permute-start(bf16[3,512,256]{2,1,0:T(8,128)(2,1)} %get-tuple-element.60), channel_id=1, source_target_pairs={{0,4},{1,5},{2,6},{3,7},{4,0},{5,1},{6,2},{7,3},{8,12},{9,13},{10,... | collective-permute-start | bytes 2359304 | tf_op jit(solution)/shard_map/ppermute | solution.py:357
  9.5 17.5 %collective-permute-done.4.refs_8_ = bf16[3,512,256]{2,1,0:T(8,128)(2,1)S(1)} collective-permute-done((bf16[3,512,256]{2,1,0:T(8,128)(2,1)}, bf16[3,512,256]{2,1,0:T(8,128)(2,1)S(1)}, u32[]{:S(2)}, u32[]{:S(2)}) %collective-permute-start.4) | collective-permute-done | bytes 786464 | tf_op jit(solution)/shard_map/ppermute | solution.py:357
  30.4 3.6 constant_dynamic-slice_fusion.2
  37.0 2.2 collective-permute-start
  40.3 5.2 %collective-permute-done = s32[640]{0:T(1024)S(1)} collective-permute-done((s32[640]{0:T(1024)S(1)}, s32[640]{0:T(1024)S(1)}, u32[]{:S(2)}, u32[]{:S(2)}) %collective-permute-start) | collective-permute-done | bytes 2592 | tf_op jit(solution)/shard_map/ppermute | solution.py:357
  49.1 3.0 shard_map.59
  54.8 8.5 %collective-permute-done.1.refs_2_ = bf16[320,2048]{1,0:T(8,128)(2,1)} collective-permute-done((bf16[320,2048]{1,0:T(8,128)(2,1)}, bf16[320,2048]{1,0:T(8,128)(2,1)}, u32[]{:S(2)}, u32[]{:S(2)}) %collective-permute-start.1) | collective-permute-done | bytes 1310752 | tf_op jit(solution)/shard_map/ppermute | solution.py:357
  63.4 2.2 collective-permute-start.10
  65.6 2.6 shard_map.60
  74.0 7.3 %collective-permute-done.10.refs_2_ = bf16[160,2048]{1,0:T(8,128)(2,1)} collective-permute-done((bf16[160,2048]{1,0:T(8,128)(2,1)}, bf16[160,2048]{1,0:T(8,128)(2,1)}, u32[]{:S(2)}, u32[]{:S(2)}) %collective-permute-start.10) | collective-permute-done | bytes 655392 | tf_op jit(solution)/shard_map/ppermute | solution.py:357
  82.6 7.4 %collective-permute-start.25 = (bf16[3,512,256]{2,1,0:T(8,128)(2,1)}, bf16[3,512,256]{2,1,0:T(8,128)(2,1)}, u32[]{:S(2)}, u32[]{:S(2)}) collective-permute-start(bf16[3,512,256]{2,1,0:T(8,128)(2,1)} %get-tuple-element.81), channel_id=1, source_target_pairs={{0,0},{1,1},{2,2},{3,3},{4,8},{5,9},{6,10},{7,11},{8,4},{9,5},{10,... | collective-permute-start | bytes 2359304 | tf_op jit(solution)/shard_map/ppermute | solution.py:357
  94.2 6.9 %shard_map.56.refs_0_.refs_1_.refs_2_.refs_3_.refs_4_.refs_5_ = bf16[2,8,640,512]{3,2,1,0:T(8,128)(2,1)} custom-call(s32[3]{0:T(128)} %pad_add_fusion.3.p_ref, f32[8,1,512]{2,1,0:T(1,128)} %bitcast.51, bf16[320,2048]{1,0:T(8,128)(2,1)} %get-tuple-element.58.refs_1_, bf16[320,2048]{1,0:T(8,128)(2,1)} %collective-permute-done.1.refs_2_, ...), custom_call_target="tpu_custom_call" | custom-call | bytes 10485760 | tf_op jit(solution)/shard_map/pallas_call | solution.py:21
  105.6 4.5 %collective-permute-start.26 = (bf16[3,512,256]{2,1,0:T(8,128)(2,1)}, bf16[3,512,256]{2,1,0:T(8,128)(2,1)}, u32[]{:S(2)}, u32[]{:S(2)}) collective-permute-start(bf16[3,512,256]{2,1,0:T(8,128)(2,1)} %collective-permute-done.25), channel_id=1, source_target_pairs={{0,4},{1,5},{2,6},{3,7},{4,0},{5,1},{6,2},{7,3},{8,12},{9,13},{10,... | collective-permute-start | bytes 2359304 | tf_op jit(solution)/shard_map/ppermute | solution.py:357
  111.7 8.3 %shard_map.61.refs_12_ = f32[2,640,768]{2,1,0:T(8,128)} custom-call(s32[7]{0:T(128)} %stack.198.p_ref, bf16[2,8,640,512]{3,2,1,0:T(8,128)(2,1)} %shard_map.56.refs_0_.refs_1_.refs_2_.refs_3_.refs_4_.refs_5_, bf16[2,8,640,512]{3,2,1,0:T(8,128)(2,1)} %shard_map.56.refs_0_.refs_1_.refs_2_.refs_3_.refs_4_.refs_5_, ...), custom_call_target="tpu_custom_call" | custom-call | bytes 10616832 | tf_op jit(solution)/shard_map/pallas_call | solution.py:21
  120.6 4.5 %shard_map.57.refs_0_ = bf16[2,8,640,512]{3,2,1,0:T(8,128)(2,1)} custom-call(s32[3]{0:T(128)} %pad_add_fusion.1.p_ref, bf16[2,8,640,512]{3,2,1,0:T(8,128)(2,1)} %shard_map.56.refs_0_.refs_1_.refs_2_.refs_3_.refs_4_.refs_5_, f32[8,1,512]{2,1,0:T(1,128)} %bitcast.52, bf16[160,2048]{1,0:T(8,128)(2,1)} %collective-permute-done.6.refs_2_, ...), custom_call_target="tpu_custom_call", output_to_operand_aliasing={{}: (1, {})} | custom-call | bytes 5242880 | tf_op jit(solution)/shard_map/pallas_call | solution.py:21
  125.1 2.1 broadcast_select_fusion.3.refs_2_
  129.5 4.5 %shard_map.58.refs_0_.refs_1_.refs_2_.refs_3_.refs_4_.refs_5_ = bf16[2,8,640,512]{3,2,1,0:T(8,128)(2,1)} custom-call(s32[3]{0:T(128)} %pad_add_fusion.1.p_ref, bf16[2,8,640,512]{3,2,1,0:T(8,128)(2,1)} %shard_map.57.refs_0_, f32[8,1,512]{2,1,0:T(1,128)} %bitcast.53, ...), custom_call_target="tpu_custom_call", output_to_operand_aliasing={{}: (1, {})} | custom-call | bytes 5242880 | tf_op jit(solution)/shard_map/pallas_call | solution.py:21
  135.6 2.8 collective-permute-start.29
  138.3 8.2 %shard_map.62.refs_4_ = f32[2,640,768]{2,1,0:T(8,128)} custom-call(s32[7]{0:T(128)} %stack.199.p_ref, bf16[2,8,640,512]{3,2,1,0:T(8,128)(2,1)} %shard_map.58.refs_0_.refs_1_.refs_2_.refs_3_.refs_4_.refs_5_, bf16[2,8,640,512]{3,2,1,0:T(8,128)(2,1)} %shard_map.58.refs_0_.refs_1_.refs_2_.refs_3_.refs_4_.refs_5_, ...), custom_call_target="tpu_custom_call", output_to_operand_aliasing={{}: (13, {})} | custom-call | bytes 10616832 | tf_op jit(solution)/shard_map/pallas_call | solution.py:21
  149.8 5.6 %shard_map.64 = bf16[640,768]{1,0:T(8,128)(2,1)} custom-call(s32[3]{0:T(128)} %add_add_fusion.1.p_ref, bf16[2,8,640,512]{3,2,1,0:T(8,128)(2,1)} %shard_map.58.refs_0_.refs_1_.refs_2_.refs_3_.refs_4_.refs_5_, bf16[2,8,640,512]{3,2,1,0:T(8,128)(2,1)} %shard_map.58.refs_0_.refs_1_.refs_2_.refs_3_.refs_4_.refs_5_, ...), custom_call_target="tpu_custom_call" | custom-call | bytes 4849664 | tf_op jit(solution)/shard_map/pallas_call | solution.py:21
  159.4 5.5 %shard_map.63.own_ref = bf16[640,768]{1,0:T(8,128)(2,1)} custom-call(s32[3]{0:T(128)} %add_add_fusion.p_ref, bf16[2,8,640,512]{3,2,1,0:T(8,128)(2,1)} %shard_map.58.refs_0_.refs_1_.refs_2_.refs_3_.refs_4_.refs_5_, bf16[2,8,640,512]{3,2,1,0:T(8,128)(2,1)} %shard_map.58.refs_0_.refs_1_.refs_2_.refs_3_.refs_4_.refs_5_, ...), custom_call_target="tpu_custom_call" | custom-call | bytes 4849664 | tf_op jit(solution)/shard_map/pallas_call | solution.py:21
  165.0 2.9 collective-permute-done.35.refs_7_
  170.5 5.9 %shard_map.65 = bf16[640,256]{1,0:T(8,128)(2,1)} custom-call(s32[1]{0:T(128)} %constant.118.clone.1._, s32[640,1]{1,0:T(8,128)} %select_n.166.mine_ref, bf16[640,768]{1,0:T(8,128)(2,1)} %shard_map.63.own_ref, bf16[640,768]{1,0:T(8,128)(2,1)} %collective-permute-done.23.got_ref), custom_call_target="tpu_custom_call" | custom-call | bytes 2296320 | tf_op jit(solution)/shard_map/pallas_call | solution.py:21
  177.5 2.1 broadcast_select_fusion.refs_6_
  179.6 6.4 %collective-permute-done.36.refs_5_ = bf16[3,512,256]{2,1,0:T(8,128)(2,1)} collective-permute-done((bf16[3,512,256]{2,1,0:T(8,128)(2,1)}, bf16[3,512,256]{2,1,0:T(8,128)(2,1)}, u32[]{:S(2)}, u32[]{:S(2)}) %collective-permute-start.36) | collective-permute-done | bytes 786464 | tf_op jit(solution)/shard_map/ppermute | solution.py:357
  186.5 4.8 %collective-permute-start.31 = (bf16[1,256,1024]{2,1,0:T(8,128)(2,1)}, bf16[1,256,1024]{2,1,0:T(8,128)(2,1)}, u32[]{:S(2)}, u32[]{:S(2)}) collective-permute-start(bf16[1,256,1024]{2,1,0:T(8,128)(2,1)} %get-tuple-element.89), channel_id=1, source_target_pairs={{0,4},{1,5},{2,6},{3,7},{4,0},{5,1},{6,2},{7,3},{8,12},{9,13},{10,... | collective-permute-start | bytes 1572872 | tf_op jit(solution)/shard_map/ppermute | solution.py:357
  191.3 5.4 %collective-permute-start.41 = (bf16[1,256,1024]{2,1,0:T(8,128)(2,1)}, bf16[1,256,1024]{2,1,0:T(8,128)(2,1)}, u32[]{:S(2)}, u32[]{:S(2)}) collective-permute-start(bf16[1,256,1024]{2,1,0:T(8,128)(2,1)} %get-tuple-element.96), channel_id=1, source_target_pairs={{0,0},{1,1},{2,2},{3,3},{4,8},{5,9},{6,10},{7,11},{8,4},{9,5},{10,... | collective-permute-start | bytes 1572872 | tf_op jit(solution)/shard_map/ppermute | solution.py:357
  198.6 6.8 %shard_map.66.refs_8_ = f32[2,640,768]{2,1,0:T(8,128)} custom-call(s32[5]{0:T(128)} %stack.208.p_ref, bf16[2,8,640,512]{3,2,1,0:T(8,128)(2,1)} %shard_map.58.refs_0_.refs_1_.refs_2_.refs_3_.refs_4_.refs_5_, bf16[2,8,640,512]{3,2,1,0:T(8,128)(2,1)} %shard_map.58.refs_0_.refs_1_.refs_2_.refs_3_.refs_4_.refs_5_, ...), custom_call_target="tpu_custom_call" | custom-call | bytes 7733248 | tf_op jit(solution)/shard_map/pallas_call | solution.py:21
  205.4 6.8 %shard_map.67.refs_8_ = f32[2,640,768]{2,1,0:T(8,128)} custom-call(s32[5]{0:T(128)} %stack.207.p_ref, bf16[2,8,640,512]{3,2,1,0:T(8,128)(2,1)} %shard_map.58.refs_0_.refs_1_.refs_2_.refs_3_.refs_4_.refs_5_, bf16[2,8,640,512]{3,2,1,0:T(8,128)(2,1)} %shard_map.58.refs_0_.refs_1_.refs_2_.refs_3_.refs_4_.refs_5_, ...), custom_call_target="tpu_custom_call", output_to_operand_aliasing={{}: (9, {})} | custom-call | bytes 7733248 | tf_op jit(solution)/shard_map/pallas_call | solution.py:21
  212.2 7.1 %shard_map.69 = bf16[640,768]{1,0:T(8,128)(2,1)} custom-call(s32[5]{0:T(128)} %stack.209.p_ref, bf16[2,8,640,512]{3,2,1,0:T(8,128)(2,1)} %shard_map.58.refs_0_.refs_1_.refs_2_.refs_3_.refs_4_.refs_5_, bf16[2,8,640,512]{3,2,1,0:T(8,128)(2,1)} %shard_map.58.refs_0_.refs_1_.refs_2_.refs_3_.refs_4_.refs_5_, ...), custom_call_target="tpu_custom_call" | custom-call | bytes 7733248 | tf_op jit(solution)/shard_map/pallas_call | solution.py:21
  219.4 10.4 %collective-permute-done.32 = bf16[640,256]{1,0:T(8,128)(2,1)} collective-permute-done((bf16[640,256]{1,0:T(8,128)(2,1)}, bf16[640,256]{1,0:T(8,128)(2,1)}, u32[]{:S(2)}, u32[]{:S(2)}) %collective-permute-start.32) | collective-permute-done | bytes 327712 | tf_op jit(solution)/shard_map/ppermute | solution.py:357
  232.7 7.0 %shard_map.68.own_ref = bf16[640,768]{1,0:T(8,128)(2,1)} custom-call(s32[5]{0:T(128)} %stack.206.p_ref, bf16[2,8,640,512]{3,2,1,0:T(8,128)(2,1)} %shard_map.58.refs_0_.refs_1_.refs_2_.refs_3_.refs_4_.refs_5_, bf16[2,8,640,512]{3,2,1,0:T(8,128)(2,1)} %shard_map.58.refs_0_.refs_1_.refs_2_.refs_3_.refs_4_.refs_5_, ...), custom_call_target="tpu_custom_call" | custom-call | bytes 7733248 | tf_op jit(solution)/shard_map/pallas_call | solution.py:21
  239.7 5.9 %shard_map.70 = bf16[640,256]{1,0:T(8,128)(2,1)} custom-call(s32[1]{0:T(128)} %constant.118.clone.1._, s32[640,1]{1,0:T(8,128)} %select_n.166.mine_ref, bf16[640,768]{1,0:T(8,128)(2,1)} %shard_map.68.own_ref, bf16[640,768]{1,0:T(8,128)(2,1)} %collective-permute-done.39.got_ref), custom_call_target="tpu_custom_call" | custom-call | bytes 2296320 | tf_op jit(solution)/shard_map/pallas_call | solution.py:21
  245.6 2.7 collective-permute-start.43
  252.6 2.6 collective-permute-done.43
  256.7 3.2 collective-permute-done.24
  261.5 5.5 %collective-permute-done.33 = bf16[640,256]{1,0:T(8,128)(2,1)S(1)} collective-permute-done((bf16[640,256]{1,0:T(8,128)(2,1)}, bf16[640,256]{1,0:T(8,128)(2,1)S(1)}, u32[]{:S(2)}, u32[]{:S(2)}) %collective-permute-start.33) | collective-permute-done | bytes 327712 | tf_op jit(solution)/shard_map/ppermute | solution.py:357
  269.1 4.9 %collective-permute-done.40 = bf16[640,256]{1,0:T(8,128)(2,1)S(1)} collective-permute-done((bf16[640,256]{1,0:T(8,128)(2,1)}, bf16[640,256]{1,0:T(8,128)(2,1)S(1)}, u32[]{:S(2)}, u32[]{:S(2)}) %collective-permute-start.40) | collective-permute-done | bytes 327712 | tf_op jit(solution)/shard_map/ppermute | solution.py:357
  275.5 3.0 collective-permute-done.44
  283.2 3.9 %collective-permute-done.48 = bf16[1,256,1024]{2,1,0:T(8,128)(2,1)S(1)} collective-permute-done((bf16[1,256,1024]{2,1,0:T(8,128)(2,1)S(1)}, bf16[1,256,1024]{2,1,0:T(8,128)(2,1)S(1)}, u32[]{:S(2)}, u32[]{:S(2)}) %collective-permute-start.48) | collective-permute-done | bytes 524320 | tf_op jit(solution)/shard_map/ppermute | solution.py:357
  288.0 8.1 %collective-permute-done.52.refs_11_.refs_17_ = bf16[1,256,1024]{2,1,0:T(8,128)(2,1)S(1)} collective-permute-done((bf16[1,256,1024]{2,1,0:T(8,128)(2,1)S(1)}, bf16[1,256,1024]{2,1,0:T(8,128)(2,1)S(1)}, u32[]{:S(2)}, u32[]{:S(2)}) %collective-permute-start.52) | collective-permute-done | bytes 524320 | tf_op jit(solution)/shard_map/ppermute | solution.py:357
  299.6 10.7 %shard_map.71.refs_20_ = f32[2,640,1024]{2,1,0:T(8,128)} custom-call(s32[5]{0:T(128)} %stack.215.p_ref, bf16[4,640,256]{2,1,0:T(8,128)(2,1)} %copy-done, bf16[4,640,256]{2,1,0:T(8,128)(2,1)} %collective-permute-done.34.refs_1_.refs_3_.refs_5_, bf16[4,640,256]{2,1,0:T(8,128)(2,1)} %copy-done, ...), custom_call_target="tpu_custom_call" | custom-call | bytes 16252928 | tf_op jit(solution)/shard_map/pallas_call | solution.py:21
  310.8 8.1 %shard_map.73 = bf16[1,640,1024]{2,1,0:T(8,128)(2,1)} custom-call(s32[7]{0:T(128)} %stack.216.p_ref, bf16[4,640,256]{2,1,0:T(8,128)(2,1)} %copy-done, bf16[4,640,256]{2,1,0:T(8,128)(2,1)} %collective-permute-done.34.refs_1_.refs_3_.refs_5_, bf16[4,640,256]{2,1,0:T(8,128)(2,1)} %pad_maximum_fusion.1.refs_2_.refs_4_.refs_6_.refs_8_, ...), custom_call_target="tpu_custom_call" | custom-call | bytes 24903680 | tf_op jit(solution)/shard_map/pallas_call | solution.py:21
  322.1 8.1 %shard_map.72 = bf16[1,640,1024]{2,1,0:T(8,128)(2,1)} custom-call(s32[7]{0:T(128)} %stack.184.p_ref, bf16[4,640,256]{2,1,0:T(8,128)(2,1)} %copy-done, bf16[4,640,256]{2,1,0:T(8,128)(2,1)} %collective-permute-done.34.refs_1_.refs_3_.refs_5_, bf16[4,640,256]{2,1,0:T(8,128)(2,1)} %pad_maximum_fusion.1.refs_2_.refs_4_.refs_6_.refs_8_, ...), custom_call_target="tpu_custom_call" | custom-call | bytes 24903680 | tf_op jit(solution)/shard_map/pallas_call | solution.py:21
  332.3 2.9 collective-permute-start.56
  335.2 14.9 %collective-permute-done.56.c_ref = bf16[320,1024]{1,0:T(8,128)(2,1)S(1)} collective-permute-done((bf16[320,1024]{1,0:T(8,128)(2,1)S(1)}, bf16[320,1024]{1,0:T(8,128)(2,1)S(1)}, u32[]{:S(2)}, u32[]{:S(2)}) %collective-permute-start.56) | collective-permute-done | bytes 655392 | tf_op jit(solution)/shard_map/ppermute | solution.py:357
  353.2 5.5 %shard_map.74 = bf16[640,2048]{1,0:T(8,128)(2,1)} custom-call(s32[2]{0:T(128)} %pad_add_fusion.p_ref, s32[640,1]{1,0:T(8,128)} %broadcast_in_dim.14.mine_ref, bf16[640,1024]{1,0:T(8,128)(2,1)} %bitcast.43, bf16[640,1024]{1,0:T(8,128)(2,1)} %collective-permute-done.54.b_ref, bf16[320,1024]{1,0:T(8,128)(2,1)} %copy-done.10, ...), custom_call_target="tpu_custom_call" | custom-call | bytes 6556160 | tf_op jit(solution)/shard_map/pallas_call | solution.py:21
  (148 shorter events, 82.8 us)
Async XLA Ops:
  4.7 22.3 %collective-permute-start.4 = (bf16[3,512,256]{2,1,0:T(8,128)(2,1)}, bf16[3,512,256]{2,1,0:T(8,128)(2,1)S(1)}, u32[]{:S(2)}, u32[]{:S(2)}) collective-permute-start(bf16[3,512,256]{2,1,0:T(8,128)(2,1)} %get-tuple-element.60), channel_id=1, source_target_pairs={{0,4},{1,5},{2,6},{3,7},{4,0},{5,1},{6,2},{7,3},{8,12},{9,13},{10,... | collective-permute-start | bytes 2359304 | tf_op jit(solution)/shard_map/ppermute | solution.py:357
  27.0 19.1 %collective-permute-start.5 = (bf16[3,512,256]{2,1,0:T(8,128)(2,1)S(1)}, bf16[3,512,256]{2,1,0:T(8,128)(2,1)}, u32[]{:S(2)}, u32[]{:S(2)}) collective-permute-start(bf16[3,512,256]{2,1,0:T(8,128)(2,1)S(1)} %collective-permute-done.3), channel_id=1, source_target_pairs={{0,4},{1,5},{2,6},{3,7},{4,0},{5,1},{6,2},{7,3},{8,12},{9,13},{10,... | collective-permute-start | bytes 2359304 | tf_op jit(solution)/shard_map/ppermute | solution.py:357
  28.7 18.8 %collective-permute-start.14 = (bf16[3,512,256]{2,1,0:T(8,128)(2,1)}, bf16[3,512,256]{2,1,0:T(8,128)(2,1)}, u32[]{:S(2)}, u32[]{:S(2)}) collective-permute-start(bf16[3,512,256]{2,1,0:T(8,128)(2,1)} %get-tuple-element.67), channel_id=1, source_target_pairs={{4,8},{5,9},{6,10},{7,11},{8,4},{9,5},{10,6},{11,7},{20,24},{21,25... | collective-permute-start | bytes 2359304 | tf_op jit(solution)/shard_map/ppermute | solution.py:357
  34.0 29.4 %collective-permute-start.1 = (bf16[320,2048]{1,0:T(8,128)(2,1)}, bf16[320,2048]{1,0:T(8,128)(2,1)}, u32[]{:S(2)}, u32[]{:S(2)}) collective-permute-start(bf16[320,2048]{1,0:T(8,128)(2,1)} %get-tuple-element.58.refs_1_), channel_id=1, source_target_pairs={{0,1},{1,0},{2,3},{3,2},{4,5},{5,4},{6,7},{7,6},{8,9},{9,8},{10,11... | collective-permute-start | bytes 3932168 | tf_op jit(solution)/shard_map/ppermute | solution.py:357
  35.5 17.8 %collective-permute-start.18 = (bf16[3,512,256]{2,1,0:T(8,128)(2,1)}, bf16[3,512,256]{2,1,0:T(8,128)(2,1)}, u32[]{:S(2)}, u32[]{:S(2)}) collective-permute-start(bf16[3,512,256]{2,1,0:T(8,128)(2,1)} %get-tuple-element.56.refs_6_), channel_id=1, source_target_pairs={{0,2},{1,3},{2,0},{3,1},{4,6},{5,7},{6,4},{7,5},{8,10},{9,11},{10,... | collective-permute-start | bytes 2359304 | tf_op jit(solution)/shard_map/ppermute | solution.py:357
  46.1 17.2 %collective-permute-start.6 = (bf16[160,2048]{1,0:T(8,128)(2,1)}, bf16[160,2048]{1,0:T(8,128)(2,1)}, u32[]{:S(2)}, u32[]{:S(2)}) collective-permute-start(bf16[160,2048]{1,0:T(8,128)(2,1)} %get-tuple-element.62), channel_id=1, source_target_pairs={{0,4},{1,5},{2,6},{3,7},{4,0},{5,1},{6,2},{7,3},{8,12},{9,13},{10,... | collective-permute-start | bytes 1966088 | tf_op jit(solution)/shard_map/ppermute | solution.py:357
  47.5 20.6 %collective-permute-start.15 = (bf16[3,512,256]{2,1,0:T(8,128)(2,1)}, bf16[3,512,256]{2,1,0:T(8,128)(2,1)}, u32[]{:S(2)}, u32[]{:S(2)}) collective-permute-start(bf16[3,512,256]{2,1,0:T(8,128)(2,1)} %collective-permute-done.5), channel_id=1, source_target_pairs={{4,8},{5,9},{6,10},{7,11},{8,4},{9,5},{10,6},{11,7},{20,24},{21,25... | collective-permute-start | bytes 2359304 | tf_op jit(solution)/shard_map/ppermute | solution.py:357
  53.3 16.9 %collective-permute-start.19 = (bf16[3,512,256]{2,1,0:T(8,128)(2,1)}, bf16[3,512,256]{2,1,0:T(8,128)(2,1)}, u32[]{:S(2)}, u32[]{:S(2)}) collective-permute-start(bf16[3,512,256]{2,1,0:T(8,128)(2,1)} %copy-done.6), channel_id=1, source_target_pairs={{0,2},{1,3},{2,0},{3,1},{4,6},{5,7},{6,4},{7,5},{8,10},{9,11},{10,... | collective-permute-start | bytes 2359304 | tf_op jit(solution)/shard_map/ppermute | solution.py:357
  63.3 28.7 %collective-permute-start.2 = (bf16[320,2048]{1,0:T(8,128)(2,1)}, bf16[320,2048]{1,0:T(8,128)(2,1)}, u32[]{:S(2)}, u32[]{:S(2)}) collective-permute-start(bf16[320,2048]{1,0:T(8,128)(2,1)} %collective-permute-done.1.refs_2_), channel_id=1, source_target_pairs={{0,16},{1,17},{2,18},{3,19},{4,20},{5,21},{6,22},{7,23},{8,24},{9,... | collective-permute-start | bytes 3932168 | tf_op jit(solution)/shard_map/ppermute | solution.py:357
  63.4 17.9 %collective-permute-start.10 = (bf16[160,2048]{1,0:T(8,128)(2,1)}, bf16[160,2048]{1,0:T(8,128)(2,1)}, u32[]{:S(2)}, u32[]{:S(2)}) collective-permute-start(bf16[160,2048]{1,0:T(8,128)(2,1)} %get-tuple-element.64), channel_id=1, source_target_pairs={{0,4},{1,5},{2,6},{3,7},{4,0},{5,1},{6,2},{7,3},{8,12},{9,13},{10,... | collective-permute-start | bytes 1966088 | tf_op jit(solution)/shard_map/ppermute | solution.py:357
  68.2 14.4 %collective-permute-start.17 = (bf16[3,512,256]{2,1,0:T(8,128)(2,1)}, bf16[3,512,256]{2,1,0:T(8,128)(2,1)S(1)}, u32[]{:S(2)}, u32[]{:S(2)}) collective-permute-start(bf16[3,512,256]{2,1,0:T(8,128)(2,1)} %copy-done.6), channel_id=1, source_target_pairs={{4,8},{5,9},{6,10},{7,11},{8,4},{9,5},{10,6},{11,7},{20,24},{21,25... | collective-permute-start | bytes 2359304 | tf_op jit(solution)/shard_map/ppermute | solution.py:357
  71.0 19.7 %collective-permute-start.20 = (bf16[3,512,256]{2,1,0:T(8,128)(2,1)S(1)}, bf16[3,512,256]{2,1,0:T(8,128)(2,1)S(1)}, u32[]{:S(2)}, u32[]{:S(2)}) collective-permute-start(bf16[3,512,256]{2,1,0:T(8,128)(2,1)S(1)} %broadcast_select_fusion.2.refs_10_), channel_id=1, source_target_pairs={{0,2},{1,3},{2,0},{3,1},{4,6},{5,7},{6,4},{7,5},{8,10},{9,11},{10,... | collective-permute-start | bytes 2359304 | tf_op jit(solution)/shard_map/ppermute | solution.py:357
  72.5 19.1 %collective-permute-start.7 = (bf16[160,2048]{1,0:T(8,128)(2,1)}, bf16[160,2048]{1,0:T(8,128)(2,1)}, u32[]{:S(2)}, u32[]{:S(2)}) collective-permute-start(bf16[160,2048]{1,0:T(8,128)(2,1)} %collective-permute-done.6.refs_2_), channel_id=1, source_target_pairs={{0,1},{1,0},{2,3},{3,2},{4,5},{5,4},{6,7},{7,6},{8,9},{9,8},{10,11... | collective-permute-start | bytes 1966088 | tf_op jit(solution)/shard_map/ppermute | solution.py:357
  81.3 21.6 %collective-permute-start.16 = (bf16[3,512,256]{2,1,0:T(8,128)(2,1)}, bf16[3,512,256]{2,1,0:T(8,128)(2,1)}, u32[]{:S(2)}, u32[]{:S(2)}) collective-permute-start(bf16[3,512,256]{2,1,0:T(8,128)(2,1)} %collective-permute-done.15), channel_id=1, source_target_pairs={{4,0},{5,1},{6,2},{7,3},{8,12},{9,13},{10,14},{11,15},{20,16},{21,... | collective-permute-start | bytes 2359304 | tf_op jit(solution)/shard_map/ppermute | solution.py:357
  82.6 23.0 %collective-permute-start.25 = (bf16[3,512,256]{2,1,0:T(8,128)(2,1)}, bf16[3,512,256]{2,1,0:T(8,128)(2,1)}, u32[]{:S(2)}, u32[]{:S(2)}) collective-permute-start(bf16[3,512,256]{2,1,0:T(8,128)(2,1)} %get-tuple-element.81), channel_id=1, source_target_pairs={{0,0},{1,1},{2,2},{3,3},{4,8},{5,9},{6,10},{7,11},{8,4},{9,5},{10,... | collective-permute-start | bytes 2359304 | tf_op jit(solution)/shard_map/ppermute | solution.py:357
  91.6 18.6 %collective-permute-start.8 = (bf16[160,2048]{1,0:T(8,128)(2,1)}, bf16[160,2048]{1,0:T(8,128)(2,1)}, u32[]{:S(2)}, u32[]{:S(2)}) collective-permute-start(bf16[160,2048]{1,0:T(8,128)(2,1)} %collective-permute-done.6.refs_2_), channel_id=1, source_target_pairs={{0,16},{1,17},{2,18},{3,19},{4,20},{5,21},{6,22},{7,23},{8,24},{9,... | collective-permute-start | bytes 1966088 | tf_op jit(solution)/shard_map/ppermute | solution.py:357
  91.6 28.5 %collective-permute-start.9 = (bf16[160,2048]{1,0:T(8,128)(2,1)}, bf16[160,2048]{1,0:T(8,128)(2,1)}, u32[]{:S(2)}, u32[]{:S(2)}) collective-permute-start(bf16[160,2048]{1,0:T(8,128)(2,1)} %collective-permute-done.7.refs_3_), channel_id=1, source_target_pairs={{0,16},{1,17},{2,18},{3,19},{4,20},{5,21},{6,22},{7,23},{8,24},{9,... | collective-permute-start | bytes 1966088 | tf_op jit(solution)/shard_map/ppermute | solution.py:357
  92.1 28.1 %collective-permute-start.11 = (bf16[160,2048]{1,0:T(8,128)(2,1)}, bf16[160,2048]{1,0:T(8,128)(2,1)}, u32[]{:S(2)}, u32[]{:S(2)}) collective-permute-start(bf16[160,2048]{1,0:T(8,128)(2,1)} %collective-permute-done.10.refs_2_), channel_id=1, source_target_pairs={{0,1},{1,0},{2,3},{3,2},{4,5},{5,4},{6,7},{7,6},{8,9},{9,8},{10,11... | collective-permute-start | bytes 1966088 | tf_op jit(solution)/shard_map/ppermute | solution.py:357
  102.8 24.4 %collective-permute-start.21 = (bf16[3,512,256]{2,1,0:T(8,128)(2,1)}, bf16[3,512,256]{2,1,0:T(8,128)(2,1)}, u32[]{:S(2)}, u32[]{:S(2)}) collective-permute-start(bf16[3,512,256]{2,1,0:T(8,128)(2,1)} %get-tuple-element.77.refs_4_), channel_id=1, source_target_pairs={{0,2},{1,3},{2,0},{3,1},{4,6},{5,7},{6,4},{7,5},{8,10},{9,11},{10,... | collective-permute-start | bytes 2359304 | tf_op jit(solution)/shard_map/ppermute | solution.py:357
  105.6 28.3 %collective-permute-start.26 = (bf16[3,512,256]{2,1,0:T(8,128)(2,1)}, bf16[3,512,256]{2,1,0:T(8,128)(2,1)}, u32[]{:S(2)}, u32[]{:S(2)}) collective-permute-start(bf16[3,512,256]{2,1,0:T(8,128)(2,1)} %collective-permute-done.25), channel_id=1, source_target_pairs={{0,4},{1,5},{2,6},{3,7},{4,0},{5,1},{6,2},{7,3},{8,12},{9,13},{10,... | collective-permute-start | bytes 2359304 | tf_op jit(solution)/shard_map/ppermute | solution.py:357
  110.2 23.8 %collective-permute-start.27 = (bf16[3,512,256]{2,1,0:T(8,128)(2,1)}, bf16[3,512,256]{2,1,0:T(8,128)(2,1)}, u32[]{:S(2)}, u32[]{:S(2)}) collective-permute-start(bf16[3,512,256]{2,1,0:T(8,128)(2,1)} %get-tuple-element.84), channel_id=1, source_target_pairs={{4,8},{5,9},{6,10},{7,11},{8,4},{9,5},{10,6},{11,7},{20,24},{21,25... | collective-permute-start | bytes 2359304 | tf_op jit(solution)/shard_map/ppermute | solution.py:357
  127.3 21.4 %collective-permute-start.22 = (bf16[3,512,256]{2,1,0:T(8,128)(2,1)}, bf16[3,512,256]{2,1,0:T(8,128)(2,1)}, u32[]{:S(2)}, u32[]{:S(2)}) collective-permute-start(bf16[3,512,256]{2,1,0:T(8,128)(2,1)} %broadcast_select_fusion.3.refs_2_), channel_id=1, source_target_pairs={{0,2},{1,3},{2,0},{3,1},{4,6},{5,7},{6,4},{7,5},{8,10},{9,11},{10,... | collective-permute-start | bytes 2359304 | tf_op jit(solution)/shard_map/ppermute | solution.py:357
  134.0 21.4 %collective-permute-start.28 = (bf16[3,512,256]{2,1,0:T(8,128)(2,1)}, bf16[3,512,256]{2,1,0:T(8,128)(2,1)}, u32[]{:S(2)}, u32[]{:S(2)}) collective-permute-start(bf16[3,512,256]{2,1,0:T(8,128)(2,1)} %collective-permute-done.26), channel_id=1, source_target_pairs={{4,8},{5,9},{6,10},{7,11},{8,4},{9,5},{10,6},{11,7},{20,24},{21,25... | collective-permute-start | bytes 2359304 | tf_op jit(solution)/shard_map/ppermute | solution.py:357
  135.6 20.4 %collective-permute-start.29 = (bf16[3,512,256]{2,1,0:T(8,128)(2,1)}, bf16[3,512,256]{2,1,0:T(8,128)(2,1)}, u32[]{:S(2)}, u32[]{:S(2)}) collective-permute-start(bf16[3,512,256]{2,1,0:T(8,128)(2,1)} %get-tuple-element.87), channel_id=1, source_target_pairs={{0,4},{1,5},{2,6},{3,7},{4,0},{5,1},{6,2},{7,3},{8,12},{9,13},{10,... | collective-permute-start | bytes 2359304 | tf_op jit(solution)/shard_map/ppermute | solution.py:357
  148.7 19.1 %collective-permute-start.35 = (bf16[3,512,256]{2,1,0:T(8,128)(2,1)}, bf16[3,512,256]{2,1,0:T(8,128)(2,1)}, u32[]{:S(2)}, u32[]{:S(2)}) collective-permute-start(bf16[3,512,256]{2,1,0:T(8,128)(2,1)} %broadcast_select_fusion.1.refs_6_), channel_id=1, source_target_pairs={{0,2},{1,3},{2,0},{3,1},{4,6},{5,7},{6,4},{7,5},{8,10},{9,11},{10,... | collective-permute-start | bytes 2359304 | tf_op jit(solution)/shard_map/ppermute | solution.py:357
  155.3 15.2 %collective-permute-start.23 = (bf16[640,768]{1,0:T(8,128)(2,1)}, bf16[640,768]{1,0:T(8,128)(2,1)}, u32[]{:S(2)}, u32[]{:S(2)}) collective-permute-start(bf16[640,768]{1,0:T(8,128)(2,1)} %shard_map.64), channel_id=1, source_target_pairs={{0,16},{1,17},{2,18},{3,19},{4,20},{5,21},{6,22},{7,23},{8,24},{9,... | collective-permute-start | bytes 2949128 | tf_op jit(solution)/shard_map/ppermute | solution.py:357
  155.9 21.6 %collective-permute-start.30 = (bf16[3,512,256]{2,1,0:T(8,128)(2,1)}, bf16[3,512,256]{2,1,0:T(8,128)(2,1)}, u32[]{:S(2)}, u32[]{:S(2)}) collective-permute-start(bf16[3,512,256]{2,1,0:T(8,128)(2,1)} %collective-permute-done.28), channel_id=1, source_target_pairs={{4,0},{5,1},{6,2},{7,3},{8,12},{9,13},{10,14},{11,15},{20,16},{21,... | collective-permute-start | bytes 2359304 | tf_op jit(solution)/shard_map/ppermute | solution.py:357
  157.2 20.3 %collective-permute-start.37 = (bf16[3,512,256]{2,1,0:T(8,128)(2,1)}, bf16[3,512,256]{2,1,0:T(8,128)(2,1)}, u32[]{:S(2)}, u32[]{:S(2)}) collective-permute-start(bf16[3,512,256]{2,1,0:T(8,128)(2,1)} %collective-permute-done.29.refs_4_), channel_id=1, source_target_pairs={{4,8},{5,9},{6,10},{7,11},{8,4},{9,5},{10,6},{11,7},{20,24},{21,25... | collective-permute-start | bytes 2359304 | tf_op jit(solution)/shard_map/ppermute | solution.py:357
  167.8 18.2 %collective-permute-start.36 = (bf16[3,512,256]{2,1,0:T(8,128)(2,1)}, bf16[3,512,256]{2,1,0:T(8,128)(2,1)}, u32[]{:S(2)}, u32[]{:S(2)}) collective-permute-start(bf16[3,512,256]{2,1,0:T(8,128)(2,1)} %collective-permute-done.29.refs_4_), channel_id=1, source_target_pairs={{0,2},{1,3},{2,0},{3,1},{4,6},{5,7},{6,4},{7,5},{8,10},{9,11},{10,... | collective-permute-start | bytes 2359304 | tf_op jit(solution)/shard_map/ppermute | solution.py:357
  186.0 26.2 %collective-permute-start.38 = (bf16[3,512,256]{2,1,0:T(8,128)(2,1)}, bf16[3,512,256]{2,1,0:T(8,128)(2,1)}, u32[]{:S(2)}, u32[]{:S(2)}) collective-permute-start(bf16[3,512,256]{2,1,0:T(8,128)(2,1)} %broadcast_select_fusion.refs_6_), channel_id=1, source_target_pairs={{0,2},{1,3},{2,0},{3,1},{4,6},{5,7},{6,4},{7,5},{8,10},{9,11},{10,... | collective-permute-start | bytes 2359304 | tf_op jit(solution)/shard_map/ppermute | solution.py:357
  186.5 32.8 %collective-permute-start.31 = (bf16[1,256,1024]{2,1,0:T(8,128)(2,1)}, bf16[1,256,1024]{2,1,0:T(8,128)(2,1)}, u32[]{:S(2)}, u32[]{:S(2)}) collective-permute-start(bf16[1,256,1024]{2,1,0:T(8,128)(2,1)} %get-tuple-element.89), channel_id=1, source_target_pairs={{0,4},{1,5},{2,6},{3,7},{4,0},{5,1},{6,2},{7,3},{8,12},{9,13},{10,... | collective-permute-start | bytes 1572872 | tf_op jit(solution)/shard_map/ppermute | solution.py:357
  191.3 28.1 %collective-permute-start.41 = (bf16[1,256,1024]{2,1,0:T(8,128)(2,1)}, bf16[1,256,1024]{2,1,0:T(8,128)(2,1)}, u32[]{:S(2)}, u32[]{:S(2)}) collective-permute-start(bf16[1,256,1024]{2,1,0:T(8,128)(2,1)} %get-tuple-element.96), channel_id=1, source_target_pairs={{0,0},{1,1},{2,2},{3,3},{4,8},{5,9},{6,10},{7,11},{8,4},{9,5},{10,... | collective-permute-start | bytes 1572872 | tf_op jit(solution)/shard_map/ppermute | solution.py:357
  219.3 20.4 %collective-permute-start.39 = (bf16[640,768]{1,0:T(8,128)(2,1)}, bf16[640,768]{1,0:T(8,128)(2,1)}, u32[]{:S(2)}, u32[]{:S(2)}) collective-permute-start(bf16[640,768]{1,0:T(8,128)(2,1)} %shard_map.69), channel_id=1, source_target_pairs={{0,16},{1,17},{2,18},{3,19},{4,20},{5,21},{6,22},{7,23},{8,24},{9,... | collective-permute-start | bytes 2949128 | tf_op jit(solution)/shard_map/ppermute | solution.py:357
  229.8 15.8 %collective-permute-start.42 = (bf16[1,256,1024]{2,1,0:T(8,128)(2,1)}, bf16[1,256,1024]{2,1,0:T(8,128)(2,1)}, u32[]{:S(2)}, u32[]{:S(2)}) collective-permute-start(bf16[1,256,1024]{2,1,0:T(8,128)(2,1)} %collective-permute-done.41), channel_id=1, source_target_pairs={{0,4},{1,5},{2,6},{3,7},{4,0},{5,1},{6,2},{7,3},{8,12},{9,13},{10,... | collective-permute-start | bytes 1572872 | tf_op jit(solution)/shard_map/ppermute | solution.py:357
  230.0 18.3 %collective-permute-start.46 = (bf16[1,256,1024]{2,1,0:T(8,128)(2,1)}, bf16[1,256,1024]{2,1,0:T(8,128)(2,1)}, u32[]{:S(2)}, u32[]{:S(2)}) collective-permute-start(bf16[1,256,1024]{2,1,0:T(8,128)(2,1)} %get-tuple-element.100), channel_id=1, source_target_pairs={{4,8},{5,9},{6,10},{7,11},{8,4},{9,5},{10,6},{11,7},{20,24},{21,25... | collective-permute-start | bytes 1572872 | tf_op jit(solution)/shard_map/ppermute | solution.py:357
  231.5 19.6 %collective-permute-start.50 = (bf16[1,256,1024]{2,1,0:T(8,128)(2,1)}, bf16[1,256,1024]{2,1,0:T(8,128)(2,1)}, u32[]{:S(2)}, u32[]{:S(2)}) collective-permute-start(bf16[1,256,1024]{2,1,0:T(8,128)(2,1)} %get-tuple-element.103.refs_6_.refs_12_), channel_id=1, source_target_pairs={{0,2},{1,3},{2,0},{3,1},{4,6},{5,7},{6,4},{7,5},{8,10},{9,11},{10,... | collective-permute-start | bytes 1572872 | tf_op jit(solution)/shard_map/ppermute | solution.py:357
  248.3 20.0 %collective-permute-start.47 = (bf16[1,256,1024]{2,1,0:T(8,128)(2,1)}, bf16[1,256,1024]{2,1,0:T(8,128)(2,1)S(1)}, u32[]{:S(2)}, u32[]{:S(2)}) collective-permute-start(bf16[1,256,1024]{2,1,0:T(8,128)(2,1)} %collective-permute-done.42), channel_id=1, source_target_pairs={{4,8},{5,9},{6,10},{7,11},{8,4},{9,5},{10,6},{11,7},{20,24},{21,25... | collective-permute-start | bytes 1572872 | tf_op jit(solution)/shard_map/ppermute | solution.py:357
  250.6 16.4 %collective-permute-start.33 = (bf16[640,256]{1,0:T(8,128)(2,1)}, bf16[640,256]{1,0:T(8,128)(2,1)S(1)}, u32[]{:S(2)}, u32[]{:S(2)}) collective-permute-start(bf16[640,256]{1,0:T(8,128)(2,1)} %collective-permute-done.32), channel_id=1, source_target_pairs={{0,1},{1,0},{2,3},{3,2},{4,5},{5,4},{6,7},{7,6},{8,9},{9,8},{10,11... | collective-permute-start | bytes 983048 | tf_op jit(solution)/shard_map/ppermute | solution.py:357
  251.1 22.9 %collective-permute-start.40 = (bf16[640,256]{1,0:T(8,128)(2,1)}, bf16[640,256]{1,0:T(8,128)(2,1)S(1)}, u32[]{:S(2)}, u32[]{:S(2)}) collective-permute-start(bf16[640,256]{1,0:T(8,128)(2,1)} %shard_map.70), channel_id=1, source_target_pairs={{0,1},{1,0},{2,3},{3,2},{4,5},{5,4},{6,7},{7,6},{8,9},{9,8},{10,11... | collective-permute-start | bytes 983048 | tf_op jit(solution)/shard_map/ppermute | solution.py:357
  255.2 23.3 %collective-permute-start.44 = (bf16[640,256]{1,0:T(8,128)(2,1)S(1)}, bf16[640,256]{1,0:T(8,128)(2,1)S(1)}, u32[]{:S(2)}, u32[]{:S(2)}) collective-permute-start(bf16[640,256]{1,0:T(8,128)(2,1)S(1)} %collective-permute-done.43), channel_id=1, source_target_pairs={{0,1},{1,0},{2,3},{3,2},{4,5},{5,4},{6,7},{7,6},{8,9},{9,8},{10,11... | collective-permute-start | bytes 983048 | tf_op jit(solution)/shard_map/ppermute | solution.py:357
  260.0 20.9 %collective-permute-start.51 = (bf16[1,256,1024]{2,1,0:T(8,128)(2,1)}, bf16[1,256,1024]{2,1,0:T(8,128)(2,1)S(1)}, u32[]{:S(2)}, u32[]{:S(2)}) collective-permute-start(bf16[1,256,1024]{2,1,0:T(8,128)(2,1)} %collective-permute-done.31.refs_8_.refs_14_), channel_id=1, source_target_pairs={{0,2},{1,3},{2,0},{3,1},{4,6},{5,7},{6,4},{7,5},{8,10},{9,11},{10,... | collective-permute-start | bytes 1572872 | tf_op jit(solution)/shard_map/ppermute | solution.py:357
  268.3 31.3 %collective-permute-start.34 = (bf16[4,640,256]{2,1,0:T(8,128)(2,1)S(1)}, bf16[4,640,256]{2,1,0:T(8,128)(2,1)}, u32[]{:S(2)}, u32[]{:S(2)}) collective-permute-start(bf16[4,640,256]{2,1,0:T(8,128)(2,1)S(1)} %pad_maximum_fusion.refs_0_.refs_2_.refs_4_), channel_id=1, source_target_pairs={{0,16},{1,17},{2,18},{3,19},{4,20},{5,21},{6,22},{7,23},{8,24},{9,... | collective-permute-start | bytes 3932168 | tf_op jit(solution)/shard_map/ppermute | solution.py:357
  268.4 18.7 %collective-permute-start.49 = (bf16[1,256,1024]{2,1,0:T(8,128)(2,1)}, bf16[1,256,1024]{2,1,0:T(8,128)(2,1)S(1)}, u32[]{:S(2)}, u32[]{:S(2)}) collective-permute-start(bf16[1,256,1024]{2,1,0:T(8,128)(2,1)} %collective-permute-done.31.refs_8_.refs_14_), channel_id=1, source_target_pairs={{4,8},{5,9},{6,10},{7,11},{8,4},{9,5},{10,6},{11,7},{20,24},{21,25... | collective-permute-start | bytes 1572872 | tf_op jit(solution)/shard_map/ppermute | solution.py:357
  279.7 31.0 %collective-permute-start.45 = (bf16[4,640,256]{2,1,0:T(8,128)(2,1)}, bf16[4,640,256]{2,1,0:T(8,128)(2,1)}, u32[]{:S(2)}, u32[]{:S(2)}) collective-permute-start(bf16[4,640,256]{2,1,0:T(8,128)(2,1)} %pad_maximum_fusion.1.refs_2_.refs_4_.refs_6_.refs_8_), channel_id=1, source_target_pairs={{0,16},{1,17},{2,18},{3,19},{4,20},{5,21},{6,22},{7,23},{8,24},{9,... | collective-permute-start | bytes 3932168 | tf_op jit(solution)/shard_map/ppermute | solution.py:357
  281.7 14.3 %collective-permute-start.52 = (bf16[1,256,1024]{2,1,0:T(8,128)(2,1)S(1)}, bf16[1,256,1024]{2,1,0:T(8,128)(2,1)S(1)}, u32[]{:S(2)}, u32[]{:S(2)}) collective-permute-start(bf16[1,256,1024]{2,1,0:T(8,128)(2,1)S(1)} %broadcast_select_fusion.4.refs_10_.refs_16_), channel_id=1, source_target_pairs={{0,2},{1,3},{2,0},{3,1},{4,6},{5,7},{6,4},{7,5},{8,10},{9,11},{10,... | collective-permute-start | bytes 1572872 | tf_op jit(solution)/shard_map/ppermute | solution.py:357
  296.9 13.9 %collective-permute-start.53 = (bf16[1,256,1024]{2,1,0:T(8,128)(2,1)}, bf16[1,256,1024]{2,1,0:T(8,128)(2,1)}, u32[]{:S(2)}, u32[]{:S(2)}) collective-permute-start(bf16[1,256,1024]{2,1,0:T(8,128)(2,1)} %broadcast_select_fusion.5.refs_10_.refs_18_), channel_id=1, source_target_pairs={{0,2},{1,3},{2,0},{3,1},{4,6},{5,7},{6,4},{7,5},{8,10},{9,11},{10,... | collective-permute-start | bytes 1572872 | tf_op jit(solution)/shard_map/ppermute | solution.py:357
  330.2 22.3 %collective-permute-start.54 = (bf16[640,1024]{1,0:T(8,128)(2,1)}, bf16[640,1024]{1,0:T(8,128)(2,1)}, u32[]{:S(2)}, u32[]{:S(2)}) collective-permute-start(bf16[640,1024]{1,0:T(8,128)(2,1)} %bitcast.42), channel_id=1, source_target_pairs={{0,16},{1,17},{2,18},{3,19},{4,20},{5,21},{6,22},{7,23},{8,24},{9,... | collective-permute-start | bytes 3932168 | tf_op jit(solution)/shard_map/ppermute | solution.py:357
  332.3 17.8 %collective-permute-start.56 = (bf16[320,1024]{1,0:T(8,128)(2,1)S(1)}, bf16[320,1024]{1,0:T(8,128)(2,1)S(1)}, u32[]{:S(2)}, u32[]{:S(2)}) collective-permute-start(bf16[320,1024]{1,0:T(8,128)(2,1)S(1)} %bitcast_select_fusion), channel_id=1, source_target_pairs={{0,4},{1,5},{2,6},{3,7},{4,0},{5,1},{6,2},{7,3},{8,12},{9,13},{10,... | collective-permute-start | bytes 1966088 | tf_op jit(solution)/shard_map/ppermute | solution.py:357
  (25 other events, 185.9 us)

commit v6 on v5

v6 whole, which is shorter than its diff:
```python
import jax
import jax.numpy as jnp
from jax import lax
from jax.experimental import pallas as pl
from jax.experimental.pallas import tpu as pltpu
from jax.sharding import PartitionSpec as P

HDIM = 128
AXES = ("mod", "dp", "tensor")
F32, BF16, I32 = jnp.float32, jnp.bfloat16, jnp.int32
VMEM, SMEM = pltpu.VMEM, pltpu.SMEM


def after(array, *earlier):
    return lax.optimization_barrier((array,) + earlier)[0]


def call(kernel, places, args, out_shape, aliases=None, scratch=8):
    return pl.pallas_call(
        kernel,
        in_specs=[pl.BlockSpec(memory_space=SMEM)] + [pl.BlockSpec(memory_space=VMEM)] * len(args),
        out_specs=jax.tree.map(lambda _: pl.BlockSpec(memory_space=VMEM), out_shape),
        out_shape=jax.tree.map(lambda shape: VMEM(shape.shape, shape.dtype), out_shape),
        input_output_aliases=aliases or {},
        compiler_params=pltpu.CompilerParams(vmem_limit_bytes=scratch * 2**20),
    )(places, *[pltpu.with_memory_space_constraint(a, VMEM) for a in args])


def shaped(shape, dtype=BF16):
    return jax.ShapeDtypeStruct(shape, dtype)


def scalars(*values):
    return jnp.stack([jnp.asarray(v, I32) for v in values])


def halves(weight, outer, chunk, chunks):
    kinds, depth, width = weight.shape
    half = width // 2
    part = half // chunks

    def kernel(p_ref, in_ref, low_ref, high_ref, mine_ref, away_ref):
        first = p_ref[0] == 1
        for kind in range(kinds):
            low = in_ref[kind, :, chunk * part : (chunk + 1) * part]
            high = in_ref[kind, :, half + chunk * part : half + (chunk + 1) * part]
            low_ref[kind] = low
            high_ref[kind] = high
            mine_ref[kind] = jnp.where(first, low, high)
            away_ref[kind] = jnp.where(first, high, low)

    return call(kernel, scalars(outer), [weight], [shaped((kinds, depth, part))] * 4)


def own_rows_of(tokens, core):
    length, features = tokens.shape
    half = length // 2

    def kernel(p_ref, in_ref, rows_ref, top_ref, bottom_ref):
        first = p_ref[0] == 0
        rows = jnp.where(first, in_ref[:half], in_ref[half:])
        rows_ref[...] = rows
        top_ref[...] = rows[: half // 2]
        bottom_ref[...] = rows[half // 2 :]

    part = shaped((half // 2, features))
    return call(kernel, scalars(core), [tokens], [shaped((half, features)), part, part])


def normalize(places, held, gains, whole, mine, theirs, shape, start, count, kept):
    _, _, length, _ = shape
    shards = len(mine) + (whole is not None)
    features = (whole if whole is not None else mine[0]).shape[1]
    tile = 32 if count % 32 == 0 else count
    half = length // 2
    per = features // kept
    args = ([] if held is None else [held]) + [gains] + ([] if whole is None else [whole])
    args += list(mine) + list(theirs)

    def kernel(p_ref, *refs):
        out_ref = refs[-1]
        refs = list(refs[0 if held is None else 1 : -1])
        gain_ref = refs.pop(0)
        whole_ref = None if whole is None else refs.pop(0)
        core, own, slot = p_ref[0], p_ref[1], p_ref[2]
        shard_of = [lax.rem(own - step + shards, shards) for step in range(shards)]

        def step(i, carry):
            for group, first in ((refs[: len(mine)], core), (refs[len(mine) :], 1 - core)):
                row = pl.multiple_of(first * half + start + i * tile, tile)
                at = pl.ds(pl.multiple_of(i * tile, tile), tile)
                found = [(ref, at) for ref in group]
                if whole_ref is not None:
                    found = [(whole_ref, pl.ds(row, tile))] + found
                total = jnp.zeros((tile, 1), F32)
                for ref, rows in found:
                    wide = ref[rows, :].astype(F32)
                    total = total + jnp.sum(wide * wide, axis=-1, keepdims=True)
                inverse = lax.rsqrt(total / (shards * features) + 1e-05)
                for shard, (ref, rows) in zip(shard_of, found):
                    for j in range(per):
                        block = shard * per + j
                        wide = ref[rows, j * kept : (j + 1) * kept].astype(F32)
                        out_ref[slot, block, pl.ds(row, tile), :] = (
                            wide * inverse * gain_ref[block]
                        ).astype(BF16)
            return carry

        lax.fori_loop(0, count // tile, step, 0)

    return call(kernel, places, args, shaped(shape), None if held is None else {1: 0})


def project(places, normed, blocks, total, final, fresh):
    slots, _, length, kept = normed.shape
    kinds, _, width = blocks[0].shape
    count = len(blocks)
    args = [normed] + list(blocks) + ([] if total is None else [total])

    def kernel(p_ref, *refs):
        normed_ref, out_ref = refs[0], refs[-1]
        slot = p_ref[0]
        for kind in range(kinds):
            columns = slice(kind * width, (kind + 1) * width)
            summed = None if fresh else refs[1 + count][slot, :, columns]
            for i in range(count):
                part = jnp.dot(
                    normed_ref[slot, p_ref[1 + i]], refs[1 + i][kind], preferred_element_type=F32
                )
                summed = part if summed is None else summed + part
            if final:
                out_ref[:, columns] = summed.astype(BF16)
            else:
                out_ref[slot, :, columns] = summed

    if final:
        return call(kernel, places, args, shaped((length, kinds * width)))
    aliases = None if total is None else {2 + count: 0}
    return call(kernel, places, args, shaped((slots, length, kinds * width), F32), aliases)


def attend(own, got, mine):
    length, width = own.shape[0], own.shape[1] // 3
    heads = width // HDIM
    scale = HDIM ** (-0.5)
    tile = 128 if length % 128 == 0 else length

    def kernel(_, mine_ref, own_ref, got_ref, out_ref):
        keep = mine_ref[...] != 0

        def pick(j):
            columns = slice(j * HDIM, (j + 1) * HDIM)
            return jnp.where(
                keep, own_ref[:, columns].astype(F32), got_ref[:, columns].astype(F32)
            ).astype(BF16)

        for h in range(heads):
            query, key, value = pick(h), pick(heads + h), pick(2 * heads + h)
            for i in range(length // tile):
                low, high = i * tile, (i + 1) * tile
                scores = lax.dot_general(
                    query[low:high], key[:high], (((1,), (1,)), ((), ())), preferred_element_type=F32
                )
                rows = low + lax.broadcasted_iota(I32, (tile, high), 0)
                cols = lax.broadcasted_iota(I32, (tile, high), 1)
                scores = jnp.where(cols <= rows, scores * scale, -jnp.inf)
                top = jnp.max(scores, axis=-1, keepdims=True)
                raised = jnp.exp(scores - top)
                share = 1.0 / jnp.sum(raised, axis=-1, keepdims=True)
                probs = (raised * share).astype(BF16)
                out = jnp.dot(probs, value[:high], preferred_element_type=F32)
                out_ref[low:high, h * HDIM : (h + 1) * HDIM] = out.astype(BF16)

    return call(kernel, scalars(0), [mine, own, got], shaped((length, width)))


def combine(places, groups, total, slots, offset=0, cut=False):
    _, length, held = groups[0][0].shape
    features = groups[0][3][0][0].shape[2]
    tile = min(features, 256)
    half = length // 2
    terms = [group[:3] + (pair,) for group in groups for pair in group[3]]
    count = len(terms)
    args = [pieces for term in terms for pieces in term[:2]]
    args += [b for term in terms for b in term[3]] + ([] if total is None else [total])

    def kernel(p_ref, *refs):
        outs = refs[-2:] if cut else refs[-1:]
        for s in range(slots):
            slot = (p_ref[0] + s) % 2
            rows = [
                jnp.where(slot == 0, refs[2 * i][p_ref[3 + i]], refs[2 * i + 1][p_ref[3 + i]])
                for i in range(count)
            ]
            for n in range(features // tile):
                columns = slice(n * tile, (n + 1) * tile)
                summed = None if total is None else refs[4 * count][offset + s, :, columns]
                for i, (_, _, parity, _) in enumerate(terms):
                    near = refs[2 * count + 2 * i][0, :, columns]
                    far = refs[2 * count + 2 * i + 1][0, :, columns]
                    block = jnp.where(p_ref[1] == parity, near, far)
                    part = jnp.dot(rows[i], block, preferred_element_type=F32)
                    summed = part if summed is None else summed + part
                if total is None:
                    outs[0][s, :, columns] = summed
                elif cut:
                    result = summed.astype(BF16)
                    first = p_ref[2] == 0
                    outs[0][:, columns] = jnp.where(first, result[:half], result[half:])
                    outs[1][:, columns] = jnp.where(first, result[half:], result[:half])
                else:
                    outs[0][:, columns] = summed.astype(BF16)

    if total is None:
        out_shape = shaped((slots, length, features), F32)
    elif cut:
        out_shape = [shaped((half, features))] * 2
    else:
        out_shape = shaped((length, features))
    return call(kernel, places, args, out_shape, scratch=12)


def assemble(places, mine, near, near_other, far, far_other):
    length, width = near.shape
    steps = 4
    tile = length // steps
    half = length // 2
    args = [mine, near, near_other, far, far_other]

    def kernel(p_ref, mine_ref, a_ref, b_ref, c_ref, d_ref, out_ref, held, sems):
        core, first = p_ref[0], p_ref[1] == 0
        copies = []
        for i in range(steps):
            rows = slice(i * tile, (i + 1) * tile)
            keep = mine_ref[rows] != 0
            own = jnp.where(keep, a_ref[rows].astype(F32), b_ref[rows].astype(F32)).astype(BF16)
            part = slice(i * tile % half, i * tile % half + tile)
            other = jnp.where(core == i * tile // half, c_ref[part], d_ref[part])
            held[i, :, :width] = jnp.where(first, own, other)
            held[i, :, width:] = jnp.where(first, other, own)
            copies.append(pltpu.make_async_copy(held.at[i], out_ref.at[rows], sems.at[i]))
            copies[-1].start()
        for copy in copies:
            copy.wait()

    return pl.pallas_call(
        kernel,
        in_specs=[pl.BlockSpec(memory_space=SMEM)] + [pl.BlockSpec(memory_space=VMEM)] * 5,
        out_specs=pl.BlockSpec(memory_space=pl.ANY),
        out_shape=shaped((length, 2 * width)),
        scratch_shapes=[VMEM((steps, tile, 2 * width), BF16), pltpu.SemaphoreType.DMA((steps,))],
        compiler_params=pltpu.CompilerParams(vmem_limit_bytes=12 * 2**20),
    )(places, *[pltpu.with_memory_space_constraint(a, VMEM) for a in args])


def from_partner(x, axis, bit):
    return lax.ppermute(x, axis, [(i, i ^ 1 << bit) for i in range(lax.axis_size(axis))])


def gathered_plan(tokens, modality, norm_gains, qkv_weight, out_weight):
    tower_id = lax.axis_index("mod")
    own_rows = modality == tower_id
    gathered = lax.all_gather(tokens, "tensor", axis=1, tiled=True)
    length = gathered.shape[0]
    local_width = qkv_weight.shape[3]
    local_heads = local_width // HDIM
    gain_row = norm_gains[0]
    scale = HDIM ** (-0.5)
    wide_rows = gathered.astype(jnp.float32)
    inverse = lax.rsqrt(jnp.mean(wide_rows * wide_rows, axis=-1, keepdims=True) + 1e-05)
    row_block = (wide_rows * inverse * gain_row).astype(jnp.bfloat16)
    weight_piece = lax.all_gather(qkv_weight, "dp", axis=1, tiled=True)
    count = weight_piece.shape[1]
    columns = row_block
    projected = (
        jnp.dot(
            columns,
            weight_piece[0].reshape(count, 3 * local_width),
            preferred_element_type=jnp.float32,
        )
        .astype(jnp.bfloat16)
        .reshape(length, 3, local_heads, HDIM)
    )
    queries = projected[:, 0]
    own_pair = projected[:, 1:]
    other_pair = from_partner(own_pair, "mod", 0)
    key_pairs = jnp.where(own_rows[:, None, None, None], own_pair, other_pair)
    key_pos = jnp.arange(length, dtype=jnp.int32)
    scores = (
        jnp.einsum("qhd,khd->hqk", queries, key_pairs[:, 0], preferred_element_type=jnp.float32)
        * scale
    )
    allowed = key_pos[None, :] <= key_pos[:, None]
    scores = jnp.where(allowed[None], scores, -jnp.inf)
    soft_weights = jax.nn.softmax(scores, axis=-1).astype(jnp.bfloat16)
    attended = jnp.einsum(
        "hqk,khd->qhd", soft_weights, key_pairs[:, 1], preferred_element_type=jnp.float32
    )
    attended = attended.astype(jnp.bfloat16).reshape(queries.shape[0], local_width)
    all_heads = lax.all_gather(attended, "tensor", axis=1, tiled=True)
    weight_piece = lax.all_gather(out_weight, "dp", axis=1, tiled=True)
    columns = all_heads
    projected_out = jnp.dot(columns, weight_piece[0], preferred_element_type=jnp.float32).astype(
        jnp.bfloat16
    )
    placed = jnp.where(own_rows[:, None], projected_out, jnp.zeros_like(projected_out))
    combined = lax.psum(placed.astype(jnp.float32).astype(jnp.bfloat16), "mod")
    return combined


def solution(mesh):
    places, shards = mesh.shape["dp"], mesh.shape["tensor"]
    mods = mesh.shape["mod"]

    def move(array, where, *earlier):
        pairs = []
        for m in range(mods):
            for d in range(places):
                for x in range(shards):
                    to = where(m, d, x)
                    if to is not None:
                        target = (to[0] * places + to[1]) * shards + to[2]
                        pairs.append(((m * places + d) * shards + x, target))
        return lax.ppermute(after(array, *earlier) if earlier else array, AXES, pairs)

    def to_core(array, *earlier):
        return move(array, lambda m, d, x: (1 - m, d, x), *earlier)

    def over_tensor(array, *earlier):
        return [array] + [
            move(array, lambda m, d, x: (m, d, (x + step) % shards), *earlier)
            for step in range(1, shards)
        ]

    def edge(m, d, x):
        return m, d ^ 2, x

    def outward(m, d, x):
        return (m, d ^ 2, x) if d // 2 in (1, 2) else None

    def across(m, d, x):
        return (m, (3 - d // 2) * 2 + d % 2, x) if d // 2 in (1, 2) else None

    def across_or_stay(m, d, x):
        return across(m, d, x) or (m, d, x)

    def pair(m, d, x):
        return m, d ^ 1, x

    def line_plan(tokens, modality, norm_gains, qkv_weight, out_weight):
        core = lax.axis_index("mod").astype(I32)
        place = lax.axis_index("dp").astype(I32)
        own = lax.axis_index("tensor").astype(I32)
        z, y = place // 2, place % 2
        column = (z ^ (z // 2)) & 1
        outer = 1 - column
        length, features = tokens.shape
        kept = qkv_weight.shape[1]
        half = length // 2
        which = core ^ (z & 1)
        at = [z, z ^ 1, jnp.where(z < 2, 2, 1), 3 - 3 * (z // 2)]

        def choose(edge_block, middle_block):
            return jnp.where(outer == 1, edge_block, middle_block)

        weight = qkv_weight[0].transpose(1, 0, 2)
        low_a, high_a, mine_a, away_a = halves(weight, outer, 0, 2)
        m1a = move(low_a, across_or_stay)
        e1a = move(away_a, edge)
        p1a = move(mine_a, pair)
        rows, top, bottom = own_rows_of(after(tokens, mine_a), core)
        fetched = over_tensor(rows)
        other_modality = move(modality, edge, mine_a)
        low_b, high_b, mine_b, away_b = halves(weight, outer, 1, 2)

        m2a = move(high_a, across, m1a)
        e2a = move(m1a, edge, e1a)
        p2a = move(e1a, pair, p1a, mine_b, rows)
        low_o, high_o, mine_o, away_o = halves(out_weight, after(outer, e1a), 0, 1)
        swapped = [to_core(a) for a in fetched[1:]]

        m3a = move(e2a, across, m2a)
        passed_top = move(top, edge, e2a, other_modality)
        third_a = choose(e2a, m2a)
        p3a = move(third_a, pair, p2a, mine_o)
        gains = norm_gains[0].reshape(places, 1, kept)
        shape = (2, places, length, kept)
        normed = normalize(
            scalars(core, own, which), None, gains, tokens, fetched[1:], swapped, shape, 0, half, kept
        )

        m4a = move(e1a, across, m3a)
        passed_bottom = move(bottom, edge, passed_top)
        p1b = move(mine_b, pair, p3a, normed)
        part_top = over_tensor(passed_top, passed_top)

        def add(slot, blocks, total, final=False, fresh=False):
            found = [slot]
            for k, _, _ in blocks:
                found += [2 * k + y, 2 * k + 1 - y]
            flat = [b for _, near, far in blocks for b in (near, far)]
            return project(scalars(*found), normed, flat, total, final, fresh)

        first_a = [(at[0], mine_a, p1a), (at[1], e1a, p2a), (at[2], third_a, p3a)]
        total_a = add(which, first_a, None, fresh=True)

        m1b = move(low_b, across_or_stay, m4a)
        e3a = move(m3a, outward, passed_bottom)
        part_bottom = over_tensor(passed_bottom, passed_bottom)
        top_swapped = [to_core(a) for a in part_top]
        normed = normalize(
            scalars(core, own, 1 - which),
            normed,
            gains,
            None,
            part_top,
            top_swapped,
            shape,
            0,
            half // 2,
            kept,
        )

        m2b = move(high_b, across, m1b)
        e2b = move(m1b, edge, e3a)
        fourth_a = choose(e3a, m4a)
        p4a = move(fourth_a, pair, p1b, total_a, normed)
        bottom_swapped = [to_core(a) for a in part_bottom]
        normed = normalize(
            scalars(core, own, 1 - which),
            normed,
            gains,
            None,
            part_bottom,
            bottom_swapped,
            shape,
            half // 2,
            half // 2,
            kept,
        )
        total_a = add(1 - which, first_a, total_a, fresh=True)

        m3b = move(e2b, across, m2b)
        e1b = move(away_b, edge, e2b)
        third_b = choose(e2b, m2b)
        p3b = move(third_b, pair, p4a, total_a)
        zero, one = jnp.zeros((), I32), jnp.ones((), I32)
        last_a = [(at[3], fourth_a, p4a)]
        theirs_a = add(one, last_a, total_a, final=True)
        got_a = to_core(theirs_a)
        ours_a = add(zero, last_a, total_a, final=True)
        own_rows = (modality == core).astype(I32)[:, None]
        other_rows = (other_modality == core).astype(I32)[:, None]
        mine_rows = jnp.where(which == 0, own_rows, other_rows)

        m4b = move(e1b, across, m3b)
        e3b = move(m3b, outward, e1b)
        p2b = move(e1b, pair, p3b, ours_a)
        attended_a = attend(ours_a, got_a, mine_rows)
        first_b = [(at[0], mine_b, p1b), (at[2], third_b, p3b)]
        total_b = add(which, first_b, None, fresh=True)
        held_a = over_tensor(attended_a)

        m1o = move(low_o, across_or_stay, m4b)
        fourth_b = choose(e3b, m4b)
        p4b = move(fourth_b, pair, p2b, attended_a)
        e1o = move(away_o, edge, e3b)
        total_b = add(1 - which, first_b, total_b, fresh=True)
        held_a += over_tensor(move(attended_a, edge, e1o))

        m2o = move(high_o, across, m1o)
        e2o = move(m1o, edge, held_a[shards])
        p1o = move(mine_o, pair, p4b)
        last_b = [(at[1], e1b, p2b), (at[3], fourth_b, p4b)]
        theirs_b = add(one, last_b, total_b, final=True)
        got_b = to_core(theirs_b)
        ours_b = add(zero, last_b, total_b, final=True)
        stack_a = jnp.stack(held_a)
        pieces_a = (stack_a, to_core(stack_a))
        attended_b = attend(ours_b, got_b, mine_rows)

        p2o = move(e1o, pair, p1o)
        m3o = move(e2o, across, m2o)
        m4o = move(e1o, across, m3o)
        third_o = choose(e2o, m2o)
        p3o = move(third_o, pair, p2o)
        e3o = move(m3o, outward)
        fourth_o = choose(e3o, m4o)
        held_b = over_tensor(attended_b)
        held_b += over_tensor(move(attended_b, edge, e2o))
        blocks = [(mine_o, p1o), (e1o, p2o), (third_o, p3o)]

        def piece_of(k):
            shard, part = k // 2, k % 2
            return jnp.where(part == column, 0, shards) + (own - shard + shards) % shards

        found = [piece_of(k) for k in at]
        total = combine(
            scalars(1 - which, y, core, *found[:3]), [pieces_a + (0, blocks)], None, 2
        )
        p4o = move(fourth_o, pair, p3o)
        last = [(fourth_o, p4o)]
        stack_b = jnp.stack(held_b)
        pieces_b = (stack_b, to_core(stack_b))
        rest = [pieces_a + (0, last), pieces_b + (1, blocks + last)]

        def finish(slot, offset):
            order = scalars(slot, y, core, found[3], *found)
            return combine(order, rest, total, 1, offset, offset == 0)

        kept_away, sent_away = finish(1 - which, 0)
        sent_away = to_core(sent_away)
        near = finish(which, 1)
        keep = lax.dynamic_slice_in_dim(other_rows, core * half, half, 0)
        far = move(jnp.where(keep != 0, kept_away, sent_away), edge)
        return assemble(
            scalars(core, column), own_rows, near, to_core(near), far, to_core(far)
        )

    return jax.shard_map(
        line_plan if places == 8 else gathered_plan,
        mesh=mesh,
        in_specs=(
            P("dp", "tensor"),
            P("dp"),
            P("mod", None),
            P("mod", "dp", None, "tensor"),
            P("mod", "dp", "tensor"),
        ),
        out_specs=P("dp", "tensor"),
        check_vma=False,
    )
```

time: 361 us -> 366 us (1.014)
  local copies, waits for them, and re-layouts: 19 us -> 75.4 us
  Pallas kernels: 124 us -> 75.9 us
  other arithmetic: 18.7 us -> 9.13 us
  waiting for transfers between devices: 111 us -> 119 us
    unnamed x30 -> x146, local copies, waits for them, and re-layouts: 4.78 us -> 74.3 us
    pallas_call x20 -> x21, Pallas kernels: 124 us -> 75.9 us  [the longest x20 73.7 us: call(): pl.pallas_call(kernel, in_specs=[pl.BlockSpec(memory_space=SMEM)] + [pl.B...]
    ppermute x58, waiting for transfers between devices: 111 us -> 119 us  [move(): lax.ppermute(after(array, *earlier) if earlier else array, AXES, pairs)]
    dynamic_slice x2 -> x0, local copies, waits for them, and re-layouts: 5.56 us -> none  [the longest x1 3.57 us: line_plan(): rest_rows = lax.dynamic_slice_in_dim(tokens, (1 - core) * half, half, 0)]
    another operation x9, local copies, waits for them, and re-layouts: 5.73 us -> 0.75 us  [scalars(): return jnp.stack([jnp.asarray(v, I32) for v in values])]
  transfers between devices with their start and end apart: 58 -> 58, of which waited for: 23 -> 21; matrix products, arithmetic and copies ran while one was open for 9% -> 3% of each run, Pallas kernels for 30% -> 18%
where the time goes in v6:
time: 366 us; the launch traced here: 363 us
  waiting for transfers between devices  119 us (33%)
  starting transfers between devices  82.8 us (23%)
  Pallas kernels  75.9 us (21%)
  local copies, waits for them, and re-layouts  75.4 us (21%)
  other arithmetic  9.13 us (2%)
    ppermute x58, waiting for transfers between devices, move(): lax.ppermute(after(array, *earlier) if earlier else array, AXES, pairs)  119 us
    ppermute x58, starting transfers between devices, move(): lax.ppermute(after(array, *earlier) if earlier else array, AXES, pairs)  82.8 us
    unnamed x146, local copies, waits for them, and re-layouts  74.3 us
    pallas_call x20, Pallas kernels, call(): pl.pallas_call(kernel, in_specs=[pl.BlockSpec(memory_space=SMEM)] + [pl.B...  73.7 us
  transfers between devices with their start and end apart: 58, of which 21 were waited for; matrix products, arithmetic and copies ran while one was open for 3% of the time, Pallas kernels for 18%

profile of v6, /device:TPU:0, one launch (start us, length us, event | category | flops | bytes accessed | tf_op | source)
XLA Modules:
  0.0 363.0 jit_solution(977260668434462414)
XLA Ops:
  5.5 5.0 %collective-permute-start.4 = (bf16[3,512,256]{2,1,0:T(8,128)(2,1)S(1)}, bf16[3,512,256]{2,1,0:T(8,128)(2,1)}, u32[]{:S(2)}, u32[]{:S(2)}) collective-permute-start(bf16[3,512,256]{2,1,0:T(8,128)(2,1)S(1)} %get-tuple-element.66), channel_id=1, source_target_pairs={{0,4},{1,5},{2,6},{3,7},{4,0},{5,1},{6,2},{7,3},{8,12},{9,13},{10,... | collective-permute-start | bytes 2359304 | tf_op jit(solution)/shard_map/ppermute | solution.py:324
  10.5 17.4 %collective-permute-done.4.refs_3_ = bf16[3,512,256]{2,1,0:T(8,128)(2,1)} collective-permute-done((bf16[3,512,256]{2,1,0:T(8,128)(2,1)S(1)}, bf16[3,512,256]{2,1,0:T(8,128)(2,1)}, u32[]{:S(2)}, u32[]{:S(2)}) %collective-permute-start.4) | collective-permute-done | bytes 786464 | tf_op jit(solution)/shard_map/ppermute | solution.py:324
  38.7 7.9 %collective-permute-done = s32[640]{0:T(1024)S(1)} collective-permute-done((s32[640]{0:T(1024)S(1)}, s32[640]{0:T(1024)S(1)}, u32[]{:S(2)}, u32[]{:S(2)}) %collective-permute-start) | collective-permute-done | bytes 2592 | tf_op jit(solution)/shard_map/ppermute | solution.py:324
  55.3 7.7 %collective-permute-done.1.refs_2_ = bf16[320,2048]{1,0:T(8,128)(2,1)} collective-permute-done((bf16[320,2048]{1,0:T(8,128)(2,1)S(1)}, bf16[320,2048]{1,0:T(8,128)(2,1)}, u32[]{:S(2)}, u32[]{:S(2)}) %collective-permute-start.1) | collective-permute-done | bytes 1310752 | tf_op jit(solution)/shard_map/ppermute | solution.py:324
  73.4 7.2 %collective-permute-done.10.refs_2_ = bf16[160,2048]{1,0:T(8,128)(2,1)} collective-permute-done((bf16[160,2048]{1,0:T(8,128)(2,1)}, bf16[160,2048]{1,0:T(8,128)(2,1)}, u32[]{:S(2)}, u32[]{:S(2)}) %collective-permute-start.10) | collective-permute-done | bytes 655392 | tf_op jit(solution)/shard_map/ppermute | solution.py:324
  81.9 7.5 %collective-permute-start.25 = (bf16[3,512,256]{2,1,0:T(8,128)(2,1)}, bf16[3,512,256]{2,1,0:T(8,128)(2,1)}, u32[]{:S(2)}, u32[]{:S(2)}) collective-permute-start(bf16[3,512,256]{2,1,0:T(8,128)(2,1)} %get-tuple-element.87), channel_id=1, source_target_pairs={{0,0},{1,1},{2,2},{3,3},{4,8},{5,9},{6,10},{7,11},{8,4},{9,5},{10,... | collective-permute-start | bytes 2359304 | tf_op jit(solution)/shard_map/ppermute | solution.py:324
  93.0 4.3 %shard_map.57.refs_0_ = bf16[2,8,640,512]{3,2,1,0:T(8,128)(2,1)S(1)} custom-call(s32[3]{0:T(128)S(1)} %pad_add_fusion.3.p_ref, f32[8,1,512]{2,1,0:T(1,128)S(1)} %bitcast.36, bf16[640,2048]{1,0:T(8,128)(2,1)S(1)} %copy-done.22, bf16[320,2048]{1,0:T(8,128)(2,1)} %collective-permute-done.1.refs_2_, bf16[320,2048]{1,0:T(8,128)(2,1)} %collective-permute-done.2.refs_3_), custom_call_target="tpu_custom_call" | custom-call | tf_op jit(solution)/shard_map/pallas_call | solution.py:19
  97.4 3.9 %copy-done = bf16[2,8,640,512]{3,2,1,0:T(8,128)(2,1)} copy-done((bf16[2,8,640,512]{3,2,1,0:T(8,128)(2,1)}, bf16[2,8,640,512]{3,2,1,0:T(8,128)(2,1)S(1)}, u32[]{:S(2)}) %copy-start) | copy-done | bytes 10485784
  103.8 4.0 %copy-done.1 = bf16[2,8,640,512]{3,2,1,0:T(8,128)(2,1)S(1)} copy-done((bf16[2,8,640,512]{3,2,1,0:T(8,128)(2,1)S(1)}, bf16[2,8,640,512]{3,2,1,0:T(8,128)(2,1)}, u32[]{:S(2)}) %copy-start.1) | copy-done | bytes 10485784
  111.1 4.7 %shard_map.62.refs_7_ = f32[2,640,768]{2,1,0:T(8,128)S(1)} custom-call(s32[7]{0:T(128)S(1)} %stack.211.p_ref, bf16[2,8,640,512]{3,2,1,0:T(8,128)(2,1)S(1)} %copy-done.1, bf16[3,512,256]{2,1,0:T(8,128)(2,1)S(1)} %copy-done.46, bf16[3,512,256]{2,1,0:T(8,128)(2,1)S(1)} %copy-done.49, bf16[3,512,256]{2,1,0:T(8,128)(2,1)} %collective-permute-done.4.refs_3_, ...), custom_call_target="tpu_custom_call" | custom-call | tf_op jit(solution)/shard_map/pallas_call | solution.py:19
  115.9 2.5 collective-permute-start.26
  120.6 2.9 shard_map.58.refs_0_
  123.5 3.9 %copy-done.3 = bf16[2,8,640,512]{3,2,1,0:T(8,128)(2,1)} copy-done((bf16[2,8,640,512]{3,2,1,0:T(8,128)(2,1)}, bf16[2,8,640,512]{3,2,1,0:T(8,128)(2,1)S(1)}, u32[]{:S(2)}) %copy-start.3) | copy-done | bytes 10485784
  130.2 4.0 %copy-done.4 = bf16[2,8,640,512]{3,2,1,0:T(8,128)(2,1)S(1)} copy-done((bf16[2,8,640,512]{3,2,1,0:T(8,128)(2,1)S(1)}, bf16[2,8,640,512]{3,2,1,0:T(8,128)(2,1)}, u32[]{:S(2)}) %copy-start.4) | copy-done | bytes 10485784
  135.3 2.9 shard_map.59.refs_0_
  138.2 3.9 %copy-done.5 = bf16[2,8,640,512]{3,2,1,0:T(8,128)(2,1)} copy-done((bf16[2,8,640,512]{3,2,1,0:T(8,128)(2,1)}, bf16[2,8,640,512]{3,2,1,0:T(8,128)(2,1)S(1)}, u32[]{:S(2)}) %copy-start.5) | copy-done | bytes 10485784
  142.1 4.0 %copy-done.6 = bf16[2,8,640,512]{3,2,1,0:T(8,128)(2,1)S(1)} copy-done((bf16[2,8,640,512]{3,2,1,0:T(8,128)(2,1)S(1)}, bf16[2,8,640,512]{3,2,1,0:T(8,128)(2,1)}, u32[]{:S(2)}) %copy-start.6) | copy-done | bytes 10485784
  146.1 4.6 %shard_map.63.refs_3_ = f32[2,640,768]{2,1,0:T(8,128)S(1)} custom-call(s32[7]{0:T(128)S(1)} %stack.212.p_ref, bf16[2,8,640,512]{3,2,1,0:T(8,128)(2,1)S(1)} %copy-done.6, bf16[3,512,256]{2,1,0:T(8,128)(2,1)S(1)} %copy-done.47, bf16[3,512,256]{2,1,0:T(8,128)(2,1)S(1)} %copy-done.50, ...), custom_call_target="tpu_custom_call", output_to_operand_aliasing={{}: (8, {})} | custom-call | tf_op jit(solution)/shard_map/pallas_call | solution.py:19
  158.9 4.0 %copy-done.7 = bf16[2,8,640,512]{3,2,1,0:T(8,128)(2,1)S(1)} copy-done((bf16[2,8,640,512]{3,2,1,0:T(8,128)(2,1)S(1)}, bf16[2,8,640,512]{3,2,1,0:T(8,128)(2,1)}, u32[]{:S(2)}) %copy-start.7) | copy-done | bytes 10485784
  165.0 3.4 shard_map.65
  168.4 5.2 %collective-permute-done.29.refs_1_ = bf16[3,512,256]{2,1,0:T(8,128)(2,1)} collective-permute-done((bf16[3,512,256]{2,1,0:T(8,128)(2,1)}, bf16[3,512,256]{2,1,0:T(8,128)(2,1)}, u32[]{:S(2)}, u32[]{:S(2)}) %collective-permute-start.29) | collective-permute-done | bytes 786464 | tf_op jit(solution)/shard_map/ppermute | solution.py:324
  176.6 2.3 shard_map.64.own_ref
  180.7 4.9 %shard_map.66 = bf16[640,256]{1,0:T(8,128)(2,1)S(1)} custom-call(s32[1]{0:T(128)} %constant.116.clone.1._, s32[640,1]{1,0:T(8,128)S(1)} %select_n.159.mine_ref, bf16[640,768]{1,0:T(8,128)(2,1)S(1)} %shard_map.64.own_ref, bf16[640,768]{1,0:T(8,128)(2,1)} %collective-permute-done.23.got_ref), custom_call_target="tpu_custom_call" | custom-call | tf_op jit(solution)/shard_map/pallas_call | solution.py:19
  186.3 7.9 %collective-permute-done.30 = bf16[3,512,256]{2,1,0:T(8,128)(2,1)} collective-permute-done((bf16[3,512,256]{2,1,0:T(8,128)(2,1)}, bf16[3,512,256]{2,1,0:T(8,128)(2,1)}, u32[]{:S(2)}, u32[]{:S(2)}) %collective-permute-start.30) | collective-permute-done | bytes 786464 | tf_op jit(solution)/shard_map/ppermute | solution.py:324
  199.2 4.7 %collective-permute-start.31 = (bf16[1,256,1024]{2,1,0:T(8,128)(2,1)}, bf16[1,256,1024]{2,1,0:T(8,128)(2,1)S(1)}, u32[]{:S(2)}, u32[]{:S(2)}) collective-permute-start(bf16[1,256,1024]{2,1,0:T(8,128)(2,1)} %get-tuple-element.95), channel_id=1, source_target_pairs={{0,4},{1,5},{2,6},{3,7},{4,0},{5,1},{6,2},{7,3},{8,12},{9,13},{10,... | collective-permute-start | bytes 1572872 | tf_op jit(solution)/shard_map/ppermute | solution.py:324
  203.8 5.4 %collective-permute-start.41 = (bf16[1,256,1024]{2,1,0:T(8,128)(2,1)}, bf16[1,256,1024]{2,1,0:T(8,128)(2,1)}, u32[]{:S(2)}, u32[]{:S(2)}) collective-permute-start(bf16[1,256,1024]{2,1,0:T(8,128)(2,1)} %get-tuple-element.102), channel_id=1, source_target_pairs={{0,0},{1,1},{2,2},{3,3},{4,8},{5,9},{6,10},{7,11},{8,4},{9,5},{10,... | collective-permute-start | bytes 1572872 | tf_op jit(solution)/shard_map/ppermute | solution.py:324
  209.5 4.0 %copy-done.9 = bf16[2,8,640,512]{3,2,1,0:T(8,128)(2,1)S(1)} copy-done((bf16[2,8,640,512]{3,2,1,0:T(8,128)(2,1)S(1)}, bf16[2,8,640,512]{3,2,1,0:T(8,128)(2,1)}, u32[]{:S(2)}) %copy-start.9) | copy-done | bytes 10485784
  214.6 3.3 shard_map.67.refs_5_
  217.9 3.3 shard_map.68.refs_5_
  221.3 6.2 %shard_map.70 = bf16[640,768]{1,0:T(8,128)(2,1)} custom-call(s32[5]{0:T(128)S(1)} %stack.222.p_ref, bf16[2,8,640,512]{3,2,1,0:T(8,128)(2,1)S(1)} %copy-done.9, bf16[3,512,256]{2,1,0:T(8,128)(2,1)} %collective-permute-done.29.refs_1_, bf16[3,512,256]{2,1,0:T(8,128)(2,1)} %collective-permute-done.36.refs_2_, ...), custom_call_target="tpu_custom_call" | custom-call | tf_op jit(solution)/shard_map/pallas_call | solution.py:19
  227.6 10.1 %collective-permute-done.32 = bf16[640,256]{1,0:T(8,128)(2,1)S(1)} collective-permute-done((bf16[640,256]{1,0:T(8,128)(2,1)S(1)}, bf16[640,256]{1,0:T(8,128)(2,1)S(1)}, u32[]{:S(2)}, u32[]{:S(2)}) %collective-permute-start.32) | collective-permute-done | bytes 327712 | tf_op jit(solution)/shard_map/ppermute | solution.py:324
  240.5 4.0 %copy-done.10 = bf16[2,8,640,512]{3,2,1,0:T(8,128)(2,1)S(1)} copy-done((bf16[2,8,640,512]{3,2,1,0:T(8,128)(2,1)S(1)}, bf16[2,8,640,512]{3,2,1,0:T(8,128)(2,1)}, u32[]{:S(2)}) %copy-start.10) | copy-done | bytes 10485784
  246.6 3.9 %shard_map.69.own_ref = bf16[640,768]{1,0:T(8,128)(2,1)S(1)} custom-call(s32[5]{0:T(128)S(1)} %stack.219.p_ref, bf16[2,8,640,512]{3,2,1,0:T(8,128)(2,1)S(1)} %copy-done.10, bf16[3,512,256]{2,1,0:T(8,128)(2,1)} %collective-permute-done.29.refs_1_, bf16[3,512,256]{2,1,0:T(8,128)(2,1)} %collective-permute-done.36.refs_2_, ...), custom_call_target="tpu_custom_call" | custom-call | tf_op jit(solution)/shard_map/pallas_call | solution.py:19
  250.5 4.8 %shard_map.71 = bf16[640,256]{1,0:T(8,128)(2,1)S(1)} custom-call(s32[1]{0:T(128)} %constant.116.clone.1._, s32[640,1]{1,0:T(8,128)S(1)} %copy-done.59, bf16[640,768]{1,0:T(8,128)(2,1)S(1)} %shard_map.69.own_ref, bf16[640,768]{1,0:T(8,128)(2,1)} %collective-permute-done.39.got_ref), custom_call_target="tpu_custom_call" | custom-call | tf_op jit(solution)/shard_map/pallas_call | solution.py:19
  255.3 2.8 collective-permute-start.43
  262.1 2.7 collective-permute-done.43
  265.8 3.9 %collective-permute-done.24 = bf16[640,256]{1,0:T(8,128)(2,1)S(1)} collective-permute-done((bf16[640,256]{1,0:T(8,128)(2,1)S(1)}, bf16[640,256]{1,0:T(8,128)(2,1)S(1)}, u32[]{:S(2)}, u32[]{:S(2)}) %collective-permute-start.24) | collective-permute-done | bytes 327712 | tf_op jit(solution)/shard_map/ppermute | solution.py:324
  271.2 5.5 %collective-permute-done.33 = bf16[640,256]{1,0:T(8,128)(2,1)S(1)} collective-permute-done((bf16[640,256]{1,0:T(8,128)(2,1)S(1)}, bf16[640,256]{1,0:T(8,128)(2,1)S(1)}, u32[]{:S(2)}, u32[]{:S(2)}) %collective-permute-start.33) | collective-permute-done | bytes 327712 | tf_op jit(solution)/shard_map/ppermute | solution.py:324
  278.6 5.1 %collective-permute-done.40 = bf16[640,256]{1,0:T(8,128)(2,1)S(1)} collective-permute-done((bf16[640,256]{1,0:T(8,128)(2,1)S(1)}, bf16[640,256]{1,0:T(8,128)(2,1)S(1)}, u32[]{:S(2)}, u32[]{:S(2)}) %collective-permute-start.40) | collective-permute-done | bytes 327712 | tf_op jit(solution)/shard_map/ppermute | solution.py:324
  285.0 3.3 collective-permute-done.44
  291.3 5.4 %collective-permute-done.48 = bf16[1,256,1024]{2,1,0:T(8,128)(2,1)S(1)} collective-permute-done((bf16[1,256,1024]{2,1,0:T(8,128)(2,1)S(1)}, bf16[1,256,1024]{2,1,0:T(8,128)(2,1)S(1)}, u32[]{:S(2)}, u32[]{:S(2)}) %collective-permute-start.48) | collective-permute-done | bytes 524320 | tf_op jit(solution)/shard_map/ppermute | solution.py:324
  296.8 7.3 %collective-permute-done.52.refs_11_.refs_17_ = bf16[1,256,1024]{2,1,0:T(8,128)(2,1)S(1)} collective-permute-done((bf16[1,256,1024]{2,1,0:T(8,128)(2,1)S(1)}, bf16[1,256,1024]{2,1,0:T(8,128)(2,1)S(1)}, u32[]{:S(2)}, u32[]{:S(2)}) %collective-permute-start.52) | collective-permute-done | bytes 524320 | tf_op jit(solution)/shard_map/ppermute | solution.py:324
  312.8 6.0 %shard_map.72.refs_20_ = f32[2,640,1024]{2,1,0:T(8,128)S(1)} custom-call(s32[6]{0:T(128)S(1)} %stack.228.p_ref, bf16[4,640,256]{2,1,0:T(8,128)(2,1)} %pad_maximum_fusion.refs_0_.refs_2_.refs_4_, bf16[4,640,256]{2,1,0:T(8,128)(2,1)} %collective-permute-done.34.refs_1_.refs_3_.refs_5_, bf16[4,640,256]{2,1,0:T(8,128)(2,1)} %pad_maximum_fusion.refs_0_.refs_2_.refs_4_, ...), custom_call_target="tpu_custom_call" | custom-call | tf_op jit(solution)/shard_map/pallas_call | solution.py:19
  318.9 6.7 %shard_map.74 = (bf16[320,1024]{1,0:T(8,128)(2,1)S(1)}, bf16[320,1024]{1,0:T(8,128)(2,1)}) custom-call(s32[8]{0:T(128)S(1)} %stack.229.p_ref, bf16[4,640,256]{2,1,0:T(8,128)(2,1)} %pad_maximum_fusion.refs_0_.refs_2_.refs_4_, bf16[4,640,256]{2,1,0:T(8,128)(2,1)} %collective-permute-done.34.refs_1_.refs_3_.refs_5_, ...), custom_call_target="tpu_custom_call" | custom-call | tf_op jit(solution)/shard_map/pallas_call | solution.py:19
  326.6 2.5 copy-done.18
  335.3 3.9 %shard_map.73.a_ref = bf16[640,1024]{1,0:T(8,128)(2,1)S(1)} custom-call(s32[8]{0:T(128)S(1)} %stack.97.p_ref, bf16[4,640,256]{2,1,0:T(8,128)(2,1)} %pad_maximum_fusion.refs_0_.refs_2_.refs_4_, bf16[4,640,256]{2,1,0:T(8,128)(2,1)} %collective-permute-done.34.refs_1_.refs_3_.refs_5_, ...), custom_call_target="tpu_custom_call" | custom-call | tf_op jit(solution)/shard_map/pallas_call | solution.py:19
  341.1 2.4 collective-permute-start.56
  343.5 14.9 %collective-permute-done.56.c_ref = bf16[320,1024]{1,0:T(8,128)(2,1)S(1)} collective-permute-done((bf16[320,1024]{1,0:T(8,128)(2,1)S(1)}, bf16[320,1024]{1,0:T(8,128)(2,1)S(1)}, u32[]{:S(2)}, u32[]{:S(2)}) %collective-permute-start.56) | collective-permute-done | bytes 655392 | tf_op jit(solution)/shard_map/ppermute | solution.py:324
  (262 shorter events, 114.2 us)
Async XLA Ops:
  5.5 22.4 %collective-permute-start.4 = (bf16[3,512,256]{2,1,0:T(8,128)(2,1)S(1)}, bf16[3,512,256]{2,1,0:T(8,128)(2,1)}, u32[]{:S(2)}, u32[]{:S(2)}) collective-permute-start(bf16[3,512,256]{2,1,0:T(8,128)(2,1)S(1)} %get-tuple-element.66), channel_id=1, source_target_pairs={{0,4},{1,5},{2,6},{3,7},{4,0},{5,1},{6,2},{7,3},{8,12},{9,13},{10,... | collective-permute-start | bytes 2359304 | tf_op jit(solution)/shard_map/ppermute | solution.py:324
  27.9 18.8 %collective-permute-start.5 = (bf16[3,512,256]{2,1,0:T(8,128)(2,1)}, bf16[3,512,256]{2,1,0:T(8,128)(2,1)}, u32[]{:S(2)}, u32[]{:S(2)}) collective-permute-start(bf16[3,512,256]{2,1,0:T(8,128)(2,1)} %collective-permute-done.3), channel_id=1, source_target_pairs={{0,4},{1,5},{2,6},{3,7},{4,0},{5,1},{6,2},{7,3},{8,12},{9,13},{10,... | collective-permute-start | bytes 2359304 | tf_op jit(solution)/shard_map/ppermute | solution.py:324
  29.6 18.5 %collective-permute-start.14 = (bf16[3,512,256]{2,1,0:T(8,128)(2,1)}, bf16[3,512,256]{2,1,0:T(8,128)(2,1)}, u32[]{:S(2)}, u32[]{:S(2)}) collective-permute-start(bf16[3,512,256]{2,1,0:T(8,128)(2,1)} %get-tuple-element.74), channel_id=1, source_target_pairs={{4,8},{5,9},{6,10},{7,11},{8,4},{9,5},{10,6},{11,7},{20,24},{21,25... | collective-permute-start | bytes 2359304 | tf_op jit(solution)/shard_map/ppermute | solution.py:324
  33.9 29.2 %collective-permute-start.1 = (bf16[320,2048]{1,0:T(8,128)(2,1)S(1)}, bf16[320,2048]{1,0:T(8,128)(2,1)}, u32[]{:S(2)}, u32[]{:S(2)}) collective-permute-start(bf16[320,2048]{1,0:T(8,128)(2,1)S(1)} %get-tuple-element.63), channel_id=1, source_target_pairs={{0,1},{1,0},{2,3},{3,2},{4,5},{5,4},{6,7},{7,6},{8,9},{9,8},{10,11... | collective-permute-start | bytes 3932168 | tf_op jit(solution)/shard_map/ppermute | solution.py:324
  35.4 17.5 %collective-permute-start.18 = (bf16[3,512,256]{2,1,0:T(8,128)(2,1)S(1)}, bf16[3,512,256]{2,1,0:T(8,128)(2,1)S(1)}, u32[]{:S(2)}, u32[]{:S(2)}) collective-permute-start(bf16[3,512,256]{2,1,0:T(8,128)(2,1)S(1)} %copy-done.45), channel_id=1, source_target_pairs={{0,2},{1,3},{2,0},{3,1},{4,6},{5,7},{6,4},{7,5},{8,10},{9,11},{10,... | collective-permute-start | bytes 2359304 | tf_op jit(solution)/shard_map/ppermute | solution.py:324
  46.6 16.4 %collective-permute-start.6 = (bf16[160,2048]{1,0:T(8,128)(2,1)S(1)}, bf16[160,2048]{1,0:T(8,128)(2,1)}, u32[]{:S(2)}, u32[]{:S(2)}) collective-permute-start(bf16[160,2048]{1,0:T(8,128)(2,1)S(1)} %get-tuple-element.68), channel_id=1, source_target_pairs={{0,4},{1,5},{2,6},{3,7},{4,0},{5,1},{6,2},{7,3},{8,12},{9,13},{10,... | collective-permute-start | bytes 1966088 | tf_op jit(solution)/shard_map/ppermute | solution.py:324
  48.1 20.2 %collective-permute-start.15 = (bf16[3,512,256]{2,1,0:T(8,128)(2,1)}, bf16[3,512,256]{2,1,0:T(8,128)(2,1)}, u32[]{:S(2)}, u32[]{:S(2)}) collective-permute-start(bf16[3,512,256]{2,1,0:T(8,128)(2,1)} %collective-permute-done.5), channel_id=1, source_target_pairs={{4,8},{5,9},{6,10},{7,11},{8,4},{9,5},{10,6},{11,7},{20,24},{21,25... | collective-permute-start | bytes 2359304 | tf_op jit(solution)/shard_map/ppermute | solution.py:324
  53.8 17.0 %collective-permute-start.19 = (bf16[3,512,256]{2,1,0:T(8,128)(2,1)}, bf16[3,512,256]{2,1,0:T(8,128)(2,1)}, u32[]{:S(2)}, u32[]{:S(2)}) collective-permute-start(bf16[3,512,256]{2,1,0:T(8,128)(2,1)} %collective-permute-done.4.refs_3_), channel_id=1, source_target_pairs={{0,2},{1,3},{2,0},{3,1},{4,6},{5,7},{6,4},{7,5},{8,10},{9,11},{10,... | collective-permute-start | bytes 2359304 | tf_op jit(solution)/shard_map/ppermute | solution.py:324
  63.0 28.4 %collective-permute-start.2 = (bf16[320,2048]{1,0:T(8,128)(2,1)}, bf16[320,2048]{1,0:T(8,128)(2,1)}, u32[]{:S(2)}, u32[]{:S(2)}) collective-permute-start(bf16[320,2048]{1,0:T(8,128)(2,1)} %collective-permute-done.1.refs_2_), channel_id=1, source_target_pairs={{0,16},{1,17},{2,18},{3,19},{4,20},{5,21},{6,22},{7,23},{8,24},{9,... | collective-permute-start | bytes 3932168 | tf_op jit(solution)/shard_map/ppermute | solution.py:324
  63.0 17.6 %collective-permute-start.10 = (bf16[160,2048]{1,0:T(8,128)(2,1)}, bf16[160,2048]{1,0:T(8,128)(2,1)}, u32[]{:S(2)}, u32[]{:S(2)}) collective-permute-start(bf16[160,2048]{1,0:T(8,128)(2,1)} %get-tuple-element.71), channel_id=1, source_target_pairs={{0,4},{1,5},{2,6},{3,7},{4,0},{5,1},{6,2},{7,3},{8,12},{9,13},{10,... | collective-permute-start | bytes 1966088 | tf_op jit(solution)/shard_map/ppermute | solution.py:324
  68.3 13.6 %collective-permute-start.17 = (bf16[3,512,256]{2,1,0:T(8,128)(2,1)}, bf16[3,512,256]{2,1,0:T(8,128)(2,1)S(1)}, u32[]{:S(2)}, u32[]{:S(2)}) collective-permute-start(bf16[3,512,256]{2,1,0:T(8,128)(2,1)} %collective-permute-done.4.refs_3_), channel_id=1, source_target_pairs={{4,8},{5,9},{6,10},{7,11},{8,4},{9,5},{10,6},{11,7},{20,24},{21,25... | collective-permute-start | bytes 2359304 | tf_op jit(solution)/shard_map/ppermute | solution.py:324
  70.8 19.3 %collective-permute-start.20 = (bf16[3,512,256]{2,1,0:T(8,128)(2,1)S(1)}, bf16[3,512,256]{2,1,0:T(8,128)(2,1)S(1)}, u32[]{:S(2)}, u32[]{:S(2)}) collective-permute-start(bf16[3,512,256]{2,1,0:T(8,128)(2,1)S(1)} %broadcast_select_fusion.2.refs_5_), channel_id=1, source_target_pairs={{0,2},{1,3},{2,0},{3,1},{4,6},{5,7},{6,4},{7,5},{8,10},{9,11},{10,... | collective-permute-start | bytes 2359304 | tf_op jit(solution)/shard_map/ppermute | solution.py:324
  72.3 18.6 %collective-permute-start.7 = (bf16[160,2048]{1,0:T(8,128)(2,1)}, bf16[160,2048]{1,0:T(8,128)(2,1)}, u32[]{:S(2)}, u32[]{:S(2)}) collective-permute-start(bf16[160,2048]{1,0:T(8,128)(2,1)} %collective-permute-done.6.refs_2_), channel_id=1, source_target_pairs={{0,1},{1,0},{2,3},{3,2},{4,5},{5,4},{6,7},{7,6},{8,9},{9,8},{10,11... | collective-permute-start | bytes 1966088 | tf_op jit(solution)/shard_map/ppermute | solution.py:324
  80.6 21.5 %collective-permute-start.16 = (bf16[3,512,256]{2,1,0:T(8,128)(2,1)}, bf16[3,512,256]{2,1,0:T(8,128)(2,1)}, u32[]{:S(2)}, u32[]{:S(2)}) collective-permute-start(bf16[3,512,256]{2,1,0:T(8,128)(2,1)} %collective-permute-done.15), channel_id=1, source_target_pairs={{4,0},{5,1},{6,2},{7,3},{8,12},{9,13},{10,14},{11,15},{20,16},{21,... | collective-permute-start | bytes 2359304 | tf_op jit(solution)/shard_map/ppermute | solution.py:324
  81.9 34.0 %collective-permute-start.25 = (bf16[3,512,256]{2,1,0:T(8,128)(2,1)}, bf16[3,512,256]{2,1,0:T(8,128)(2,1)}, u32[]{:S(2)}, u32[]{:S(2)}) collective-permute-start(bf16[3,512,256]{2,1,0:T(8,128)(2,1)} %get-tuple-element.87), channel_id=1, source_target_pairs={{0,0},{1,1},{2,2},{3,3},{4,8},{5,9},{6,10},{7,11},{8,4},{9,5},{10,... | collective-permute-start | bytes 2359304 | tf_op jit(solution)/shard_map/ppermute | solution.py:324
  91.0 27.4 %collective-permute-start.8 = (bf16[160,2048]{1,0:T(8,128)(2,1)}, bf16[160,2048]{1,0:T(8,128)(2,1)}, u32[]{:S(2)}, u32[]{:S(2)}) collective-permute-start(bf16[160,2048]{1,0:T(8,128)(2,1)} %collective-permute-done.6.refs_2_), channel_id=1, source_target_pairs={{0,16},{1,17},{2,18},{3,19},{4,20},{5,21},{6,22},{7,23},{8,24},{9,... | collective-permute-start | bytes 1966088 | tf_op jit(solution)/shard_map/ppermute | solution.py:324
  91.0 29.1 %collective-permute-start.9 = (bf16[160,2048]{1,0:T(8,128)(2,1)}, bf16[160,2048]{1,0:T(8,128)(2,1)}, u32[]{:S(2)}, u32[]{:S(2)}) collective-permute-start(bf16[160,2048]{1,0:T(8,128)(2,1)} %collective-permute-done.7.refs_3_), channel_id=1, source_target_pairs={{0,16},{1,17},{2,18},{3,19},{4,20},{5,21},{6,22},{7,23},{8,24},{9,... | collective-permute-start | bytes 1966088 | tf_op jit(solution)/shard_map/ppermute | solution.py:324
  91.5 28.6 %collective-permute-start.11 = (bf16[160,2048]{1,0:T(8,128)(2,1)}, bf16[160,2048]{1,0:T(8,128)(2,1)}, u32[]{:S(2)}, u32[]{:S(2)}) collective-permute-start(bf16[160,2048]{1,0:T(8,128)(2,1)} %collective-permute-done.10.refs_2_), channel_id=1, source_target_pairs={{0,1},{1,0},{2,3},{3,2},{4,5},{5,4},{6,7},{7,6},{8,9},{9,8},{10,11... | collective-permute-start | bytes 1966088 | tf_op jit(solution)/shard_map/ppermute | solution.py:324
  102.1 26.6 %collective-permute-start.21 = (bf16[3,512,256]{2,1,0:T(8,128)(2,1)}, bf16[3,512,256]{2,1,0:T(8,128)(2,1)S(1)}, u32[]{:S(2)}, u32[]{:S(2)}) collective-permute-start(bf16[3,512,256]{2,1,0:T(8,128)(2,1)} %get-tuple-element.83.refs_1_), channel_id=1, source_target_pairs={{0,2},{1,3},{2,0},{3,1},{4,6},{5,7},{6,4},{7,5},{8,10},{9,11},{10,... | collective-permute-start | bytes 2359304 | tf_op jit(solution)/shard_map/ppermute | solution.py:324
  115.9 36.6 %collective-permute-start.26 = (bf16[3,512,256]{2,1,0:T(8,128)(2,1)}, bf16[3,512,256]{2,1,0:T(8,128)(2,1)}, u32[]{:S(2)}, u32[]{:S(2)}) collective-permute-start(bf16[3,512,256]{2,1,0:T(8,128)(2,1)} %collective-permute-done.25), channel_id=1, source_target_pairs={{0,4},{1,5},{2,6},{3,7},{4,0},{5,1},{6,2},{7,3},{8,12},{9,13},{10,... | collective-permute-start | bytes 2359304 | tf_op jit(solution)/shard_map/ppermute | solution.py:324
  118.4 34.2 %collective-permute-start.27 = (bf16[3,512,256]{2,1,0:T(8,128)(2,1)}, bf16[3,512,256]{2,1,0:T(8,128)(2,1)}, u32[]{:S(2)}, u32[]{:S(2)}) collective-permute-start(bf16[3,512,256]{2,1,0:T(8,128)(2,1)} %get-tuple-element.90), channel_id=1, source_target_pairs={{4,8},{5,9},{6,10},{7,11},{8,4},{9,5},{10,6},{11,7},{20,24},{21,25... | collective-permute-start | bytes 2359304 | tf_op jit(solution)/shard_map/ppermute | solution.py:324
  128.7 28.5 %collective-permute-start.22 = (bf16[3,512,256]{2,1,0:T(8,128)(2,1)S(1)}, bf16[3,512,256]{2,1,0:T(8,128)(2,1)}, u32[]{:S(2)}, u32[]{:S(2)}) collective-permute-start(bf16[3,512,256]{2,1,0:T(8,128)(2,1)S(1)} %broadcast_select_fusion.3.refs_1_), channel_id=1, source_target_pairs={{0,2},{1,3},{2,0},{3,1},{4,6},{5,7},{6,4},{7,5},{8,10},{9,11},{10,... | collective-permute-start | bytes 2359304 | tf_op jit(solution)/shard_map/ppermute | solution.py:324
  152.5 15.9 %collective-permute-start.28 = (bf16[3,512,256]{2,1,0:T(8,128)(2,1)}, bf16[3,512,256]{2,1,0:T(8,128)(2,1)}, u32[]{:S(2)}, u32[]{:S(2)}) collective-permute-start(bf16[3,512,256]{2,1,0:T(8,128)(2,1)} %collective-permute-done.26), channel_id=1, source_target_pairs={{4,8},{5,9},{6,10},{7,11},{8,4},{9,5},{10,6},{11,7},{20,24},{21,25... | collective-permute-start | bytes 2359304 | tf_op jit(solution)/shard_map/ppermute | solution.py:324
  154.1 19.6 %collective-permute-start.29 = (bf16[3,512,256]{2,1,0:T(8,128)(2,1)}, bf16[3,512,256]{2,1,0:T(8,128)(2,1)}, u32[]{:S(2)}, u32[]{:S(2)}) collective-permute-start(bf16[3,512,256]{2,1,0:T(8,128)(2,1)} %get-tuple-element.93), channel_id=1, source_target_pairs={{0,4},{1,5},{2,6},{3,7},{4,0},{5,1},{6,2},{7,3},{8,12},{9,13},{10,... | collective-permute-start | bytes 2359304 | tf_op jit(solution)/shard_map/ppermute | solution.py:324
  157.2 21.6 %collective-permute-start.35 = (bf16[3,512,256]{2,1,0:T(8,128)(2,1)S(1)}, bf16[3,512,256]{2,1,0:T(8,128)(2,1)S(1)}, u32[]{:S(2)}, u32[]{:S(2)}) collective-permute-start(bf16[3,512,256]{2,1,0:T(8,128)(2,1)S(1)} %broadcast_select_fusion.1.refs_3_), channel_id=1, source_target_pairs={{0,2},{1,3},{2,0},{3,1},{4,6},{5,7},{6,4},{7,5},{8,10},{9,11},{10,... | collective-permute-start | bytes 2359304 | tf_op jit(solution)/shard_map/ppermute | solution.py:324
  173.6 20.6 %collective-permute-start.30 = (bf16[3,512,256]{2,1,0:T(8,128)(2,1)}, bf16[3,512,256]{2,1,0:T(8,128)(2,1)}, u32[]{:S(2)}, u32[]{:S(2)}) collective-permute-start(bf16[3,512,256]{2,1,0:T(8,128)(2,1)} %collective-permute-done.28), channel_id=1, source_target_pairs={{4,0},{5,1},{6,2},{7,3},{8,12},{9,13},{10,14},{11,15},{20,16},{21,... | collective-permute-start | bytes 2359304 | tf_op jit(solution)/shard_map/ppermute | solution.py:324
  174.9 19.3 %collective-permute-start.37 = (bf16[3,512,256]{2,1,0:T(8,128)(2,1)}, bf16[3,512,256]{2,1,0:T(8,128)(2,1)}, u32[]{:S(2)}, u32[]{:S(2)}) collective-permute-start(bf16[3,512,256]{2,1,0:T(8,128)(2,1)} %collective-permute-done.29.refs_1_), channel_id=1, source_target_pairs={{4,8},{5,9},{6,10},{7,11},{8,4},{9,5},{10,6},{11,7},{20,24},{21,25... | collective-permute-start | bytes 2359304 | tf_op jit(solution)/shard_map/ppermute | solution.py:324
  178.9 18.7 %collective-permute-start.36 = (bf16[3,512,256]{2,1,0:T(8,128)(2,1)}, bf16[3,512,256]{2,1,0:T(8,128)(2,1)}, u32[]{:S(2)}, u32[]{:S(2)}) collective-permute-start(bf16[3,512,256]{2,1,0:T(8,128)(2,1)} %collective-permute-done.29.refs_1_), channel_id=1, source_target_pairs={{0,2},{1,3},{2,0},{3,1},{4,6},{5,7},{6,4},{7,5},{8,10},{9,11},{10,... | collective-permute-start | bytes 2359304 | tf_op jit(solution)/shard_map/ppermute | solution.py:324
  197.7 23.6 %collective-permute-start.38 = (bf16[3,512,256]{2,1,0:T(8,128)(2,1)S(1)}, bf16[3,512,256]{2,1,0:T(8,128)(2,1)}, u32[]{:S(2)}, u32[]{:S(2)}) collective-permute-start(bf16[3,512,256]{2,1,0:T(8,128)(2,1)S(1)} %broadcast_select_fusion.refs_3_), channel_id=1, source_target_pairs={{0,2},{1,3},{2,0},{3,1},{4,6},{5,7},{6,4},{7,5},{8,10},{9,11},{10,... | collective-permute-start | bytes 2359304 | tf_op jit(solution)/shard_map/ppermute | solution.py:324
  199.2 28.3 %collective-permute-start.31 = (bf16[1,256,1024]{2,1,0:T(8,128)(2,1)}, bf16[1,256,1024]{2,1,0:T(8,128)(2,1)S(1)}, u32[]{:S(2)}, u32[]{:S(2)}) collective-permute-start(bf16[1,256,1024]{2,1,0:T(8,128)(2,1)} %get-tuple-element.95), channel_id=1, source_target_pairs={{0,4},{1,5},{2,6},{3,7},{4,0},{5,1},{6,2},{7,3},{8,12},{9,13},{10,... | collective-permute-start | bytes 1572872 | tf_op jit(solution)/shard_map/ppermute | solution.py:324
  203.8 23.7 %collective-permute-start.41 = (bf16[1,256,1024]{2,1,0:T(8,128)(2,1)}, bf16[1,256,1024]{2,1,0:T(8,128)(2,1)}, u32[]{:S(2)}, u32[]{:S(2)}) collective-permute-start(bf16[1,256,1024]{2,1,0:T(8,128)(2,1)} %get-tuple-element.102), channel_id=1, source_target_pairs={{0,0},{1,1},{2,2},{3,3},{4,8},{5,9},{6,10},{7,11},{8,4},{9,5},{10,... | collective-permute-start | bytes 1572872 | tf_op jit(solution)/shard_map/ppermute | solution.py:324
  227.5 23.0 %collective-permute-start.39 = (bf16[640,768]{1,0:T(8,128)(2,1)}, bf16[640,768]{1,0:T(8,128)(2,1)}, u32[]{:S(2)}, u32[]{:S(2)}) collective-permute-start(bf16[640,768]{1,0:T(8,128)(2,1)} %shard_map.70), channel_id=1, source_target_pairs={{0,16},{1,17},{2,18},{3,19},{4,20},{5,21},{6,22},{7,23},{8,24},{9,... | collective-permute-start | bytes 2949128 | tf_op jit(solution)/shard_map/ppermute | solution.py:324
  237.7 17.6 %collective-permute-start.42 = (bf16[1,256,1024]{2,1,0:T(8,128)(2,1)}, bf16[1,256,1024]{2,1,0:T(8,128)(2,1)}, u32[]{:S(2)}, u32[]{:S(2)}) collective-permute-start(bf16[1,256,1024]{2,1,0:T(8,128)(2,1)} %collective-permute-done.41), channel_id=1, source_target_pairs={{0,4},{1,5},{2,6},{3,7},{4,0},{5,1},{6,2},{7,3},{8,12},{9,13},{10,... | collective-permute-start | bytes 1572872 | tf_op jit(solution)/shard_map/ppermute | solution.py:324
  238.4 19.6 %collective-permute-start.46 = (bf16[1,256,1024]{2,1,0:T(8,128)(2,1)}, bf16[1,256,1024]{2,1,0:T(8,128)(2,1)}, u32[]{:S(2)}, u32[]{:S(2)}) collective-permute-start(bf16[1,256,1024]{2,1,0:T(8,128)(2,1)} %get-tuple-element.106), channel_id=1, source_target_pairs={{4,8},{5,9},{6,10},{7,11},{8,4},{9,5},{10,6},{11,7},{20,24},{21,25... | collective-permute-start | bytes 1572872 | tf_op jit(solution)/shard_map/ppermute | solution.py:324
  239.9 21.2 %collective-permute-start.50 = (bf16[1,256,1024]{2,1,0:T(8,128)(2,1)S(1)}, bf16[1,256,1024]{2,1,0:T(8,128)(2,1)S(1)}, u32[]{:S(2)}, u32[]{:S(2)}) collective-permute-start(bf16[1,256,1024]{2,1,0:T(8,128)(2,1)S(1)} %copy-done.28), channel_id=1, source_target_pairs={{0,2},{1,3},{2,0},{3,1},{4,6},{5,7},{6,4},{7,5},{8,10},{9,11},{10,... | collective-permute-start | bytes 1572872 | tf_op jit(solution)/shard_map/ppermute | solution.py:324
  258.1 19.9 %collective-permute-start.47 = (bf16[1,256,1024]{2,1,0:T(8,128)(2,1)}, bf16[1,256,1024]{2,1,0:T(8,128)(2,1)S(1)}, u32[]{:S(2)}, u32[]{:S(2)}) collective-permute-start(bf16[1,256,1024]{2,1,0:T(8,128)(2,1)} %collective-permute-done.42), channel_id=1, source_target_pairs={{4,8},{5,9},{6,10},{7,11},{8,4},{9,5},{10,6},{11,7},{20,24},{21,25... | collective-permute-start | bytes 1572872 | tf_op jit(solution)/shard_map/ppermute | solution.py:324
  260.1 16.7 %collective-permute-start.33 = (bf16[640,256]{1,0:T(8,128)(2,1)S(1)}, bf16[640,256]{1,0:T(8,128)(2,1)S(1)}, u32[]{:S(2)}, u32[]{:S(2)}) collective-permute-start(bf16[640,256]{1,0:T(8,128)(2,1)S(1)} %copy-done.71), channel_id=1, source_target_pairs={{0,1},{1,0},{2,3},{3,2},{4,5},{5,4},{6,7},{7,6},{8,9},{9,8},{10,11... | collective-permute-start | bytes 983048 | tf_op jit(solution)/shard_map/ppermute | solution.py:324
  261.1 22.7 %collective-permute-start.40 = (bf16[640,256]{1,0:T(8,128)(2,1)S(1)}, bf16[640,256]{1,0:T(8,128)(2,1)S(1)}, u32[]{:S(2)}, u32[]{:S(2)}) collective-permute-start(bf16[640,256]{1,0:T(8,128)(2,1)S(1)} %shard_map.71), channel_id=1, source_target_pairs={{0,1},{1,0},{2,3},{3,2},{4,5},{5,4},{6,7},{7,6},{8,9},{9,8},{10,11... | collective-permute-start | bytes 983048 | tf_op jit(solution)/shard_map/ppermute | solution.py:324
  264.8 23.5 %collective-permute-start.44 = (bf16[640,256]{1,0:T(8,128)(2,1)S(1)}, bf16[640,256]{1,0:T(8,128)(2,1)S(1)}, u32[]{:S(2)}, u32[]{:S(2)}) collective-permute-start(bf16[640,256]{1,0:T(8,128)(2,1)S(1)} %collective-permute-done.43), channel_id=1, source_target_pairs={{0,1},{1,0},{2,3},{3,2},{4,5},{5,4},{6,7},{7,6},{8,9},{9,8},{10,11... | collective-permute-start | bytes 983048 | tf_op jit(solution)/shard_map/ppermute | solution.py:324
  269.7 20.0 %collective-permute-start.51 = (bf16[1,256,1024]{2,1,0:T(8,128)(2,1)S(1)}, bf16[1,256,1024]{2,1,0:T(8,128)(2,1)S(1)}, u32[]{:S(2)}, u32[]{:S(2)}) collective-permute-start(bf16[1,256,1024]{2,1,0:T(8,128)(2,1)S(1)} %collective-permute-done.31.refs_8_.refs_14_), channel_id=1, source_target_pairs={{0,2},{1,3},{2,0},{3,1},{4,6},{5,7},{6,4},{7,5},{8,10},{9,11},{10,... | collective-permute-start | bytes 1572872 | tf_op jit(solution)/shard_map/ppermute | solution.py:324
  277.9 28.6 %collective-permute-start.34 = (bf16[4,640,256]{2,1,0:T(8,128)(2,1)}, bf16[4,640,256]{2,1,0:T(8,128)(2,1)}, u32[]{:S(2)}, u32[]{:S(2)}) collective-permute-start(bf16[4,640,256]{2,1,0:T(8,128)(2,1)} %pad_maximum_fusion.refs_0_.refs_2_.refs_4_), channel_id=1, source_target_pairs={{0,16},{1,17},{2,18},{3,19},{4,20},{5,21},{6,22},{7,23},{8,24},{9,... | collective-permute-start | bytes 3932168 | tf_op jit(solution)/shard_map/ppermute | solution.py:324
  277.9 18.8 %collective-permute-start.49 = (bf16[1,256,1024]{2,1,0:T(8,128)(2,1)S(1)}, bf16[1,256,1024]{2,1,0:T(8,128)(2,1)S(1)}, u32[]{:S(2)}, u32[]{:S(2)}) collective-permute-start(bf16[1,256,1024]{2,1,0:T(8,128)(2,1)S(1)} %collective-permute-done.31.refs_8_.refs_14_), channel_id=1, source_target_pairs={{4,8},{5,9},{6,10},{7,11},{8,4},{9,5},{10,6},{11,7},{20,24},{21,25... | collective-permute-start | bytes 1572872 | tf_op jit(solution)/shard_map/ppermute | solution.py:324
  288.5 30.4 %collective-permute-start.45 = (bf16[4,640,256]{2,1,0:T(8,128)(2,1)S(1)}, bf16[4,640,256]{2,1,0:T(8,128)(2,1)S(1)}, u32[]{:S(2)}, u32[]{:S(2)}) collective-permute-start(bf16[4,640,256]{2,1,0:T(8,128)(2,1)S(1)} %pad_maximum_fusion.1.refs_2_.refs_4_.refs_6_.refs_8_), channel_id=1, source_target_pairs={{0,16},{1,17},{2,18},{3,19},{4,20},{5,21},{6,22},{7,23},{8,24},{9,... | collective-permute-start | bytes 3932168 | tf_op jit(solution)/shard_map/ppermute | solution.py:324
  289.7 14.4 %collective-permute-start.52 = (bf16[1,256,1024]{2,1,0:T(8,128)(2,1)S(1)}, bf16[1,256,1024]{2,1,0:T(8,128)(2,1)S(1)}, u32[]{:S(2)}, u32[]{:S(2)}) collective-permute-start(bf16[1,256,1024]{2,1,0:T(8,128)(2,1)S(1)} %broadcast_select_fusion.5.refs_10_.refs_16_), channel_id=1, source_target_pairs={{0,2},{1,3},{2,0},{3,1},{4,6},{5,7},{6,4},{7,5},{8,10},{9,11},{10,... | collective-permute-start | bytes 1572872 | tf_op jit(solution)/shard_map/ppermute | solution.py:324
  304.9 14.0 %collective-permute-start.53 = (bf16[1,256,1024]{2,1,0:T(8,128)(2,1)S(1)}, bf16[1,256,1024]{2,1,0:T(8,128)(2,1)}, u32[]{:S(2)}, u32[]{:S(2)}) collective-permute-start(bf16[1,256,1024]{2,1,0:T(8,128)(2,1)S(1)} %broadcast_select_fusion.6.refs_10_.refs_18_), channel_id=1, source_target_pairs={{0,2},{1,3},{2,0},{3,1},{4,6},{5,7},{6,4},{7,5},{8,10},{9,11},{10,... | collective-permute-start | bytes 1572872 | tf_op jit(solution)/shard_map/ppermute | solution.py:324
  326.4 13.4 %collective-permute-start.55 = (bf16[320,1024]{1,0:T(8,128)(2,1)}, bf16[320,1024]{1,0:T(8,128)(2,1)}, u32[]{:S(2)}, u32[]{:S(2)}) collective-permute-start(bf16[320,1024]{1,0:T(8,128)(2,1)} %get-tuple-element.114), channel_id=1, source_target_pairs={{0,16},{1,17},{2,18},{3,19},{4,20},{5,21},{6,22},{7,23},{8,24},{9,... | collective-permute-start | bytes 1966088 | tf_op jit(solution)/shard_map/ppermute | solution.py:324
  339.3 19.4 %collective-permute-start.54 = (bf16[640,1024]{1,0:T(8,128)(2,1)S(1)}, bf16[640,1024]{1,0:T(8,128)(2,1)S(1)}, u32[]{:S(2)}, u32[]{:S(2)}) collective-permute-start(bf16[640,1024]{1,0:T(8,128)(2,1)S(1)} %shard_map.73.a_ref), channel_id=1, source_target_pairs={{0,16},{1,17},{2,18},{3,19},{4,20},{5,21},{6,22},{7,23},{8,24},{9,... | collective-permute-start | bytes 3932168 | tf_op jit(solution)/shard_map/ppermute | solution.py:324
  341.1 17.4 %collective-permute-start.56 = (bf16[320,1024]{1,0:T(8,128)(2,1)S(1)}, bf16[320,1024]{1,0:T(8,128)(2,1)S(1)}, u32[]{:S(2)}, u32[]{:S(2)}) collective-permute-start(bf16[320,1024]{1,0:T(8,128)(2,1)S(1)} %broadcast_select_fusion.4), channel_id=1, source_target_pairs={{0,4},{1,5},{2,6},{3,7},{4,0},{5,1},{6,2},{7,3},{8,12},{9,13},{10,... | collective-permute-start | bytes 1966088 | tf_op jit(solution)/shard_map/ppermute | solution.py:324
  (83 other events, 548.2 us)

commit v7 on v6

v7 whole, which is shorter than its diff:
```python
import jax
import jax.numpy as jnp
from jax import lax
from jax.experimental import pallas as pl
from jax.experimental.pallas import tpu as pltpu
from jax.sharding import PartitionSpec as P

HDIM = 128
AXES = ("mod", "dp", "tensor")
F32, BF16, I32 = jnp.float32, jnp.bfloat16, jnp.int32
VMEM, SMEM = pltpu.VMEM, pltpu.SMEM


def after(array, *earlier):
    return lax.optimization_barrier((array,) + earlier)[0]


class Here:
    def __init__(self, ref):
        self.core, place, self.own = ref[0], ref[1], ref[2]
        self.z, self.y = place >> 1, place & 1
        self.column = (self.z ^ (self.z >> 1)) & 1
        self.outer = self.column == 0
        self.which = self.core ^ (self.z & 1)
        self.at = [self.z, self.z ^ 1, jnp.where(self.z < 2, 2, 1), 3 - 3 * (self.z >> 1)]

    def slot(self, name):
        return {"own": self.which, "partner": 1 - self.which}.get(name, name)


def call(kernel, here, args, out_shape, aliases=None, scratch=8):
    return pl.pallas_call(
        kernel,
        in_specs=[pl.BlockSpec(memory_space=SMEM)] + [pl.BlockSpec(memory_space=VMEM)] * len(args),
        out_specs=jax.tree.map(lambda _: pl.BlockSpec(memory_space=VMEM), out_shape),
        out_shape=jax.tree.map(lambda shape: VMEM(shape.shape, shape.dtype), out_shape),
        input_output_aliases=aliases or {},
        compiler_params=pltpu.CompilerParams(vmem_limit_bytes=scratch * 2**20),
    )(here, *[pltpu.with_memory_space_constraint(a, VMEM) for a in args])


def shaped(shape, dtype=BF16):
    return jax.ShapeDtypeStruct(shape, dtype)


def halves(here, weight, chunk, chunks):
    kinds, depth, width = weight.shape
    half = width // 2
    part = half // chunks

    def kernel(h_ref, in_ref, low_ref, high_ref, mine_ref, away_ref):
        outer = Here(h_ref).outer
        for kind in range(kinds):
            low = in_ref[kind, :, chunk * part : (chunk + 1) * part]
            high = in_ref[kind, :, half + chunk * part : half + (chunk + 1) * part]
            low_ref[kind] = low
            high_ref[kind] = high
            mine_ref[kind] = jnp.where(outer, low, high)
            away_ref[kind] = jnp.where(outer, high, low)

    return call(kernel, here, [weight], [shaped((kinds, depth, part))] * 4)


def own_rows_of(here, tokens):
    length, features = tokens.shape
    half = length // 2

    def kernel(h_ref, in_ref, rows_ref, top_ref, bottom_ref):
        rows = jnp.where(h_ref[0] == 0, in_ref[:half], in_ref[half:])
        rows_ref[...] = rows
        top_ref[...] = rows[: half // 2]
        bottom_ref[...] = rows[half // 2 :]

    part = shaped((half // 2, features))
    return call(kernel, here, [tokens], [shaped((half, features)), part, part])


def choose(here, from_edge, from_middle):
    def kernel(h_ref, a_ref, b_ref, out_ref):
        outer = Here(h_ref).outer

        @pl.when(outer)
        def _():
            out_ref[...] = a_ref[...]

        @pl.when(jnp.logical_not(outer))
        def _():
            out_ref[...] = b_ref[...]

    return call(kernel, here, [from_edge, from_middle], shaped(from_edge.shape))


def stack(here, arrays):
    def kernel(_, *refs):
        for i in range(len(arrays)):
            refs[-1][i] = refs[i][...]

    return call(kernel, here, arrays, shaped((len(arrays),) + arrays[0].shape))


def normalize(here, slot, held, gains, whole, mine, theirs, shape, start, count):
    _, _, length, kept = shape
    shards = len(mine) + (whole is not None)
    features = (whole if whole is not None else mine[0]).shape[1]
    tile = 32 if count % 32 == 0 else count
    half = length // 2
    per = features // kept
    args = ([] if held is None else [held]) + [gains] + ([] if whole is None else [whole])
    args += list(mine) + list(theirs)

    def kernel(h_ref, *refs):
        at_place = Here(h_ref)
        core, own, into = at_place.core, at_place.own, at_place.slot(slot)
        out_ref = refs[-1]
        refs = list(refs[0 if held is None else 1 : -1])
        gain_ref = refs.pop(0)
        whole_ref = None if whole is None else refs.pop(0)
        shard_of = [lax.rem(own - step + shards, shards) for step in range(shards)]

        def step(i, carry):
            for group, first in ((refs[: len(mine)], core), (refs[len(mine) :], 1 - core)):
                row = pl.multiple_of(first * half + start + i * tile, tile)
                at = pl.ds(pl.multiple_of(i * tile, tile), tile)
                found = [(ref, at) for ref in group]
                if whole_ref is not None:
                    found = [(whole_ref, pl.ds(row, tile))] + found
                total = jnp.zeros((tile, 1), F32)
                for ref, rows in found:
                    wide = ref[rows, :].astype(F32)
                    total = total + jnp.sum(wide * wide, axis=-1, keepdims=True)
                inverse = lax.rsqrt(total / (shards * features) + 1e-05)
                for shard, (ref, rows) in zip(shard_of, found):
                    for j in range(per):
                        block = shard * per + j
                        wide = ref[rows, j * kept : (j + 1) * kept].astype(F32)
                        out_ref[into, block, pl.ds(row, tile), :] = (
                            wide * inverse * gain_ref[block]
                        ).astype(BF16)
            return carry

        lax.fori_loop(0, count // tile, step, 0)

    return call(kernel, here, args, shaped(shape), None if held is None else {1: 0})


def project(here, slot, normed, blocks, total=None, final=False, fresh=False):
    slots, _, length, kept = normed.shape
    kinds, _, width = blocks[0][1].shape
    count = len(blocks)
    args = [normed] + [b for _, near, far in blocks for b in (near, far)]
    args += [] if total is None else [total]

    def kernel(h_ref, *refs):
        at_place = Here(h_ref)
        into = at_place.slot(slot)
        normed_ref, out_ref = refs[0], refs[-1]
        for kind in range(kinds):
            columns = slice(kind * width, (kind + 1) * width)
            summed = None if fresh else refs[1 + 2 * count][into, :, columns]
            for i, (arrival, _, _) in enumerate(blocks):
                for j, y in enumerate((at_place.y, 1 - at_place.y)):
                    part = jnp.dot(
                        normed_ref[into, at_place.at[arrival] * 2 + y],
                        refs[1 + 2 * i + j][kind],
                        preferred_element_type=F32,
                    )
                    summed = part if summed is None else summed + part
            if final:
                out_ref[:, columns] = summed.astype(BF16)
            else:
                out_ref[into, :, columns] = summed

    if final:
        return call(kernel, here, args, shaped((length, kinds * width)))
    aliases = None if total is None else {2 + 2 * count: 0}
    return call(kernel, here, args, shaped((slots, length, kinds * width), F32), aliases)


def attend(here, own_kind, other_kind, own, got):
    length, width = own.shape[0], own.shape[1] // 3
    heads = width // HDIM
    scale = HDIM ** (-0.5)
    tile = 128 if length % 128 == 0 else length

    def kernel(h_ref, own_kind_ref, other_kind_ref, own_ref, got_ref, out_ref):
        at_place = Here(h_ref)
        kind = jnp.where(at_place.which == 0, own_kind_ref[...], other_kind_ref[...])
        keep = kind == at_place.core

        def pick(j):
            columns = slice(j * HDIM, (j + 1) * HDIM)
            return jnp.where(
                keep, own_ref[:, columns].astype(F32), got_ref[:, columns].astype(F32)
            ).astype(BF16)

        for h in range(heads):
            query, key, value = pick(h), pick(heads + h), pick(2 * heads + h)
            for i in range(length // tile):
                low, high = i * tile, (i + 1) * tile
                scores = lax.dot_general(
                    query[low:high], key[:high], (((1,), (1,)), ((), ())), preferred_element_type=F32
                )
                rows = low + lax.broadcasted_iota(I32, (tile, high), 0)
                cols = lax.broadcasted_iota(I32, (tile, high), 1)
                scores = jnp.where(cols <= rows, scores * scale, -jnp.inf)
                top = jnp.max(scores, axis=-1, keepdims=True)
                raised = jnp.exp(scores - top)
                share = 1.0 / jnp.sum(raised, axis=-1, keepdims=True)
                probs = (raised * share).astype(BF16)
                out = jnp.dot(probs, value[:high], preferred_element_type=F32)
                out_ref[low:high, h * HDIM : (h + 1) * HDIM] = out.astype(BF16)

    return call(kernel, here, [own_kind, other_kind, own, got], shaped((length, width)))


def combine(here, slots, groups, total=None, offset=0, cut=False):
    held_pieces, length, held = groups[0][0].shape
    shards = held_pieces // 2
    features = groups[0][3][0][1].shape[2]
    tile = min(features, 256)
    half = length // 2
    terms = [group[:3] + (pair,) for group in groups for pair in group[3]]
    count = len(terms)
    args = [pieces for term in terms for pieces in term[:2]]
    args += [b for term in terms for b in term[3][1:]] + ([] if total is None else [total])

    def kernel(h_ref, *refs):
        at_place = Here(h_ref)
        outs = refs[-2:] if cut else refs[-1:]
        found = []
        for z in at_place.at:
            shard = lax.rem(at_place.own - (z >> 1) + shards, shards)
            found.append(jnp.where((z & 1) == at_place.column, 0, shards) + shard)
        for s, name in enumerate(slots):
            first_slot = at_place.slot(name) == 0
            rows = [
                jnp.where(
                    first_slot, refs[2 * i][found[arrival]], refs[2 * i + 1][found[arrival]]
                )
                for i, (_, _, _, (arrival, _, _)) in enumerate(terms)
            ]
            for n in range(features // tile):
                columns = slice(n * tile, (n + 1) * tile)
                summed = None if total is None else refs[4 * count][offset + s, :, columns]
                for i, (_, _, parity, _) in enumerate(terms):
                    near = refs[2 * count + 2 * i][0, :, columns]
                    far = refs[2 * count + 2 * i + 1][0, :, columns]
                    block = jnp.where(at_place.y == parity, near, far)
                    part = jnp.dot(rows[i], block, preferred_element_type=F32)
                    summed = part if summed is None else summed + part
                if total is None:
                    outs[0][s, :, columns] = summed
                elif cut:
                    result = summed.astype(BF16)
                    first = at_place.core == 0
                    outs[0][:, columns] = jnp.where(first, result[:half], result[half:])
                    outs[1][:, columns] = jnp.where(first, result[half:], result[:half])
                else:
                    outs[0][:, columns] = summed.astype(BF16)

    if total is None:
        out_shape = shaped((len(slots), length, features), F32)
    elif cut:
        out_shape = [shaped((half, features))] * 2
    else:
        out_shape = shaped((length, features))
    return call(kernel, here, args, out_shape)


def join(here, kind, kept, got):
    half = kept.shape[0]

    def kernel(h_ref, kind_ref, a_ref, b_ref, out_ref):
        core = h_ref[0]
        rows = jnp.where(core == 0, kind_ref[:half], kind_ref[half:])
        out_ref[...] = jnp.where(
            rows == core, a_ref[...].astype(F32), b_ref[...].astype(F32)
        ).astype(BF16)

    return call(kernel, here, [kind, kept, got], shaped(kept.shape))


def assemble(here, kind, near, near_other, far, far_other):
    length, width = near.shape
    steps = 4
    tile = length // steps
    half = length // 2
    args = [kind, near, near_other, far, far_other]

    def kernel(h_ref, kind_ref, a_ref, b_ref, c_ref, d_ref, out_ref, held, sems):
        at_place = Here(h_ref)
        core, first = at_place.core, at_place.column == 0
        copies = []
        for i in range(steps):
            rows = slice(i * tile, (i + 1) * tile)
            keep = kind_ref[rows] == core
            own = jnp.where(keep, a_ref[rows].astype(F32), b_ref[rows].astype(F32)).astype(BF16)
            part = slice(i * tile % half, i * tile % half + tile)
            other = jnp.where(core == i * tile // half, c_ref[part], d_ref[part])
            held[i, :, :width] = jnp.where(first, own, other)
            held[i, :, width:] = jnp.where(first, other, own)
            copies.append(pltpu.make_async_copy(held.at[i], out_ref.at[rows], sems.at[i]))
            copies[-1].start()
        for copy in copies:
            copy.wait()

    return pl.pallas_call(
        kernel,
        in_specs=[pl.BlockSpec(memory_space=SMEM)] + [pl.BlockSpec(memory_space=VMEM)] * 5,
        out_specs=pl.BlockSpec(memory_space=pl.ANY),
        out_shape=shaped((length, 2 * width)),
        scratch_shapes=[VMEM((steps, tile, 2 * width), BF16), pltpu.SemaphoreType.DMA((steps,))],
        compiler_params=pltpu.CompilerParams(vmem_limit_bytes=8 * 2**20),
    )(here, *[pltpu.with_memory_space_constraint(a, VMEM) for a in args])


def from_partner(x, axis, bit):
    return lax.ppermute(x, axis, [(i, i ^ 1 << bit) for i in range(lax.axis_size(axis))])


def gathered_plan(tokens, modality, norm_gains, qkv_weight, out_weight):
    tower_id = lax.axis_index("mod")
    own_rows = modality == tower_id
    gathered = lax.all_gather(tokens, "tensor", axis=1, tiled=True)
    length = gathered.shape[0]
    local_width = qkv_weight.shape[3]
    local_heads = local_width // HDIM
    gain_row = norm_gains[0]
    scale = HDIM ** (-0.5)
    wide_rows = gathered.astype(jnp.float32)
    inverse = lax.rsqrt(jnp.mean(wide_rows * wide_rows, axis=-1, keepdims=True) + 1e-05)
    row_block = (wide_rows * inverse * gain_row).astype(jnp.bfloat16)
    weight_piece = lax.all_gather(qkv_weight, "dp", axis=1, tiled=True)
    count = weight_piece.shape[1]
    columns = row_block
    projected = (
        jnp.dot(
            columns,
            weight_piece[0].reshape(count, 3 * local_width),
            preferred_element_type=jnp.float32,
        )
        .astype(jnp.bfloat16)
        .reshape(length, 3, local_heads, HDIM)
    )
    queries = projected[:, 0]
    own_pair = projected[:, 1:]
    other_pair = from_partner(own_pair, "mod", 0)
    key_pairs = jnp.where(own_rows[:, None, None, None], own_pair, other_pair)
    key_pos = jnp.arange(length, dtype=jnp.int32)
    scores = (
        jnp.einsum("qhd,khd->hqk", queries, key_pairs[:, 0], preferred_element_type=jnp.float32)
        * scale
    )
    allowed = key_pos[None, :] <= key_pos[:, None]
    scores = jnp.where(allowed[None], scores, -jnp.inf)
    soft_weights = jax.nn.softmax(scores, axis=-1).astype(jnp.bfloat16)
    attended = jnp.einsum(
        "hqk,khd->qhd", soft_weights, key_pairs[:, 1], preferred_element_type=jnp.float32
    )
    attended = attended.astype(jnp.bfloat16).reshape(queries.shape[0], local_width)
    all_heads = lax.all_gather(attended, "tensor", axis=1, tiled=True)
    weight_piece = lax.all_gather(out_weight, "dp", axis=1, tiled=True)
    columns = all_heads
    projected_out = jnp.dot(columns, weight_piece[0], preferred_element_type=jnp.float32).astype(
        jnp.bfloat16
    )
    placed = jnp.where(own_rows[:, None], projected_out, jnp.zeros_like(projected_out))
    combined = lax.psum(placed.astype(jnp.float32).astype(jnp.bfloat16), "mod")
    return combined


def solution(mesh):
    places, shards = mesh.shape["dp"], mesh.shape["tensor"]
    mods = mesh.shape["mod"]

    def move(array, where, *earlier):
        pairs = []
        for m in range(mods):
            for d in range(places):
                for x in range(shards):
                    to = where(m, d, x)
                    if to is not None:
                        target = (to[0] * places + to[1]) * shards + to[2]
                        pairs.append(((m * places + d) * shards + x, target))
        return lax.ppermute(after(array, *earlier) if earlier else array, AXES, pairs)

    def to_core(array, *earlier):
        return move(array, lambda m, d, x: (1 - m, d, x), *earlier)

    def over_tensor(array, *earlier):
        return [array] + [
            move(array, lambda m, d, x: (m, d, (x + step) % shards), *earlier)
            for step in range(1, shards)
        ]

    def edge(m, d, x):
        return m, d ^ 2, x

    def outward(m, d, x):
        return (m, d ^ 2, x) if d // 2 in (1, 2) else None

    def across(m, d, x):
        return (m, (3 - d // 2) * 2 + d % 2, x) if d // 2 in (1, 2) else None

    def across_or_stay(m, d, x):
        return across(m, d, x) or (m, d, x)

    def pair(m, d, x):
        return m, d ^ 1, x

    def line_plan(tokens, modality, norm_gains, qkv_weight, out_weight):
        here = jnp.stack([lax.axis_index(name).astype(I32) for name in AXES])
        length = tokens.shape[0]
        kept = qkv_weight.shape[1]
        half = length // 2
        gains = norm_gains[0].reshape(places, 1, kept)
        own_kind = modality[:, None]

        weight = after(qkv_weight[0].transpose(1, 0, 2), here, gains, own_kind)
        low_a, high_a, mine_a, away_a = halves(here, weight, 0, 2)
        m1a = move(low_a, across_or_stay)
        e1a = move(away_a, edge)
        rows, top, bottom = own_rows_of(here, after(tokens, mine_a))
        p1a = move(mine_a, pair, rows)
        fetched = over_tensor(rows)
        other_kind = move(own_kind, edge, rows)
        low_b, high_b, mine_b, away_b = halves(here, after(weight, rows), 1, 2)
        low_o, high_o, mine_o, away_o = halves(here, after(out_weight, mine_b), 0, 1)

        m2a = move(high_a, across, m1a, mine_o)
        e2a = move(m1a, edge, e1a, p1a)
        p2a = move(e1a, pair, p1a)
        swapped = [to_core(a) for a in fetched[1:]]

        m3a = move(e2a, across, m2a)
        passed_top = move(top, edge, e2a, other_kind)
        third_a = choose(here, e2a, m2a)
        p3a = move(third_a, pair, p2a)
        shape = (2, places, length, kept)
        normed = normalize(here, "own", None, gains, tokens, fetched[1:], swapped, shape, 0, half)

        m4a = move(e1a, across, m3a)
        passed_bottom = move(bottom, edge, passed_top)
        p1b = move(mine_b, pair, p3a, normed)
        part_top = over_tensor(passed_top)
        first_a = [(0, mine_a, p1a), (1, e1a, p2a), (2, third_a, p3a)]
        total_a = project(here, "own", normed, first_a, fresh=True)

        m1b = move(low_b, across_or_stay, m4a)
        e3a = move(m3a, outward, passed_bottom)
        p1o = move(mine_o, pair, p1b, total_a)
        part_bottom = over_tensor(passed_bottom)
        top_swapped = [to_core(a) for a in part_top]
        normed = normalize(
            here, "partner", normed, gains, None, part_top, top_swapped, shape, 0, half // 2
        )

        m2b = move(high_b, across, m1b)
        e2b = move(m1b, edge, e3a)
        fourth_a = choose(here, e3a, m4a)
        p4a = move(fourth_a, pair, p1o, normed)
        bottom_swapped = [to_core(a) for a in part_bottom]
        normed = normalize(
            here, "partner", normed, gains, None, part_bottom, bottom_swapped, shape, half // 2, half // 2
        )
        total_a = project(here, "partner", normed, first_a, total_a, fresh=True)

        m3b = move(e2b, across, m2b)
        e1b = move(away_b, edge, e2b)
        third_b = choose(here, e2b, m2b)
        p3b = move(third_b, pair, p4a, total_a)
        last_a = [(3, fourth_a, p4a)]
        theirs_a = project(here, 1, normed, last_a, total_a, final=True)
        got_a = to_core(theirs_a)
        ours_a = project(here, 0, normed, last_a, total_a, final=True)

        m4b = move(e1b, across, m3b)
        e3b = move(m3b, outward, e1b)
        p2b = move(e1b, pair, p3b, ours_a)
        attended_a = attend(here, own_kind, other_kind, ours_a, got_a)
        first_b = [(0, mine_b, p1b), (2, third_b, p3b)]
        total_b = project(here, "own", normed, first_b, fresh=True)
        total_b = project(here, "partner", normed, first_b, total_b, fresh=True)
        held_a = over_tensor(attended_a)

        m1o = move(low_o, across_or_stay, m4b)
        fourth_b = choose(here, e3b, m4b)
        p4b = move(fourth_b, pair, p2b, attended_a, total_b)
        e1o = move(away_o, edge, e3b)
        second_b = [(1, e1b, p2b)]
        total_b = project(here, "own", normed, second_b, total_b)
        total_b = project(here, "partner", normed, second_b, total_b)

        m2o = move(high_o, across, m1o)
        e2o = move(m1o, edge, e1o)
        last_b = [(3, fourth_b, p4b)]
        theirs_b = project(here, 1, normed, last_b, total_b, final=True)
        got_b = to_core(theirs_b)
        ours_b = project(here, 0, normed, last_b, total_b, final=True)
        attended_b = attend(here, own_kind, other_kind, ours_b, got_b)

        p2o = move(e1o, pair, p4b)
        m3o = move(e2o, across, m2o)
        m4o = move(e1o, across, m3o)
        third_o = choose(here, e2o, m2o)
        p3o = move(third_o, pair, p2o)
        passed_a = move(attended_a, edge, e2o)
        held_a += over_tensor(passed_a)
        e3o = move(m3o, outward, passed_a)
        pieces_a = stack(here, held_a)
        pieces_a = (pieces_a, to_core(pieces_a))
        fourth_o = choose(here, e3o, m4o)
        held_b = over_tensor(attended_b)
        held_b += over_tensor(move(attended_b, edge, passed_a))
        blocks = [(0, mine_o, p1o), (1, e1o, p2o), (2, third_o, p3o)]

        total = combine(here, ("partner", "own"), [pieces_a + (0, blocks)])
        p4o = move(fourth_o, pair, p3o)
        last = [(3, fourth_o, p4o)]
        pieces_b = stack(here, held_b)
        pieces_b = (pieces_b, to_core(pieces_b))
        rest = [pieces_a + (0, last), pieces_b + (1, blocks + last)]

        kept_away, sent_away = combine(here, ("partner",), rest, total, 0, True)
        sent_away = to_core(sent_away)
        near = combine(here, ("own",), rest, total, 1)
        far = move(join(here, other_kind, kept_away, sent_away), edge)
        return assemble(here, own_kind, near, to_core(near), far, to_core(far))

    return jax.shard_map(
        line_plan if places == 8 else gathered_plan,
        mesh=mesh,
        in_specs=(
            P("dp", "tensor"),
            P("dp"),
            P("mod", None),
            P("mod", "dp", None, "tensor"),
            P("mod", "dp", "tensor"),
        ),
        out_specs=P("dp", "tensor"),
        check_vma=False,
    )
```

time: 366 us -> 317 us (0.87)
  local copies, waits for them, and re-layouts: 75.4 us -> 23.5 us
  waiting for transfers between devices: 119 us -> 145 us
  Pallas kernels: 75.9 us -> 66.2 us
  other arithmetic: 9.13 us -> 0.08 us
    unnamed x146 -> x78, local copies, waits for them, and re-layouts: 74.3 us -> 21.8 us
    ppermute x58, waiting for transfers between devices: 119 us -> 145 us  [move(): lax.ppermute(after(array, *earlier) if earlier else array, AXES, pairs)]
    pallas_call x20 -> x31, Pallas kernels: 73.7 us -> 64 us  [call(): pl.pallas_call(kernel, in_specs=[pl.BlockSpec(memory_space=SMEM)] + [pl.B...]
    select_n x8 -> x0, other arithmetic: 7.29 us -> none  [the longest x6 6.07 us: choose(): return jnp.where(outer == 1, edge_block, middle_block)]
  transfers between devices with their start and end apart: 58 -> 58, of which waited for: 21 -> 28; matrix products, arithmetic and copies ran while one was open for 3% -> 0% of each run, Pallas kernels for 18% -> 19%
where the time goes in v7:
time: 317 us; the launch traced here: 316 us
  waiting for transfers between devices  145 us (46%)
  starting transfers between devices  80.3 us (25%)
  Pallas kernels  66.2 us (21%)
  local copies, waits for them, and re-layouts  23.5 us (7%)
    ppermute x58, waiting for transfers between devices, move(): lax.ppermute(after(array, *earlier) if earlier else array, AXES, pairs)  145 us
    ppermute x58, starting transfers between devices, move(): lax.ppermute(after(array, *earlier) if earlier else array, AXES, pairs)  80.3 us
    pallas_call x31, Pallas kernels, call(): pl.pallas_call(kernel, in_specs=[pl.BlockSpec(memory_space=SMEM)] + [pl.B...  64 us
    unnamed x78, local copies, waits for them, and re-layouts  21.8 us
  transfers between devices with their start and end apart: 58, of which 28 were waited for; matrix products, arithmetic and copies ran while one was open for 0% of the time, Pallas kernels for 19%

profile of v7, /device:TPU:0, one launch (start us, length us, event | category | flops | bytes accessed | tf_op | source)
XLA Modules:
  0.0 316.4 jit_solution(9195204809766607068)
XLA Ops:
  0.8 1.9 copy-done.2
  7.7 3.0 collective-permute-start.5
  10.7 4.3 %collective-permute-start.4 = (bf16[3,512,256]{2,1,0:T(8,128)(2,1)S(1)}, bf16[3,512,256]{2,1,0:T(8,128)(2,1)}, u32[]{:S(2)}, u32[]{:S(2)}) collective-permute-start(bf16[3,512,256]{2,1,0:T(8,128)(2,1)S(1)} %get-tuple-element.69), channel_id=1, source_target_pairs={{0,4},{1,5},{2,6},{3,7},{4,0},{5,1},{6,2},{7,3},{8,12},{9,13},{10,... | collective-permute-start | bytes 2359304 | tf_op jit(solution)/shard_map/ppermute | solution.py:385
  23.9 4.3 %collective-permute-done.5.refs_2_ = bf16[3,512,256]{2,1,0:T(8,128)(2,1)S(1)} collective-permute-done((bf16[3,512,256]{2,1,0:T(8,128)(2,1)S(1)}, bf16[3,512,256]{2,1,0:T(8,128)(2,1)S(1)}, u32[]{:S(2)}, u32[]{:S(2)}) %collective-permute-start.5) | collective-permute-done | bytes 786464 | tf_op jit(solution)/shard_map/ppermute | solution.py:385
  29.1 3.0 collective-permute-done.4.refs_3_
  34.9 9.9 %collective-permute-done.1.refs_2_ = bf16[320,2048]{1,0:T(8,128)(2,1)} collective-permute-done((bf16[320,2048]{1,0:T(8,128)(2,1)S(1)}, bf16[320,2048]{1,0:T(8,128)(2,1)}, u32[]{:S(2)}, u32[]{:S(2)}) %collective-permute-start.1) | collective-permute-done | bytes 1310752 | tf_op jit(solution)/shard_map/ppermute | solution.py:385
  45.8 4.5 %collective-permute-done.6.a_ref = bf16[3,512,256]{2,1,0:T(8,128)(2,1)} collective-permute-done((bf16[3,512,256]{2,1,0:T(8,128)(2,1)S(1)}, bf16[3,512,256]{2,1,0:T(8,128)(2,1)}, u32[]{:S(2)}, u32[]{:S(2)}) %collective-permute-start.6) | collective-permute-done | bytes 786464 | tf_op jit(solution)/shard_map/ppermute | solution.py:385
  52.8 2.2 collective-permute-start
  55.0 5.8 %collective-permute-done.other_kind_ref.kind_ref = s32[640,1]{1,0:T(8,128)S(1)} collective-permute-done((s32[640,1]{1,0:T(8,128)}, s32[640,1]{1,0:T(8,128)S(1)}, u32[]{:S(2)}, u32[]{:S(2)}) %collective-permute-start) | collective-permute-done | bytes 2592 | tf_op jit(solution)/shard_map/ppermute | solution.py:385
  60.8 2.2 collective-permute-start.7
  67.4 8.2 %collective-permute-done.7.refs_2_ = bf16[160,2048]{1,0:T(8,128)(2,1)S(1)} collective-permute-done((bf16[160,2048]{1,0:T(8,128)(2,1)}, bf16[160,2048]{1,0:T(8,128)(2,1)S(1)}, u32[]{:S(2)}, u32[]{:S(2)}) %collective-permute-start.7) | collective-permute-done | bytes 655392 | tf_op jit(solution)/shard_map/ppermute | solution.py:385
  75.6 2.3 collective-permute-start.11
  79.4 4.4 %shard_map.57.refs_0_ = bf16[2,8,640,512]{3,2,1,0:T(8,128)(2,1)S(1)} custom-call(s32[3]{0:T(128)S(1)} %pad_add_fusion.h_ref._, f32[8,1,512]{2,1,0:T(1,128)S(1)} %bitcast.11, bf16[640,2048]{1,0:T(8,128)(2,1)S(1)} %copy-done.5, bf16[320,2048]{1,0:T(8,128)(2,1)} %collective-permute-done.1.refs_2_, bf16[320,2048]{1,0:T(8,128)(2,1)} %collective-permute-done.2.refs_3_), custom_call_target="tpu_custom_call" | custom-call | tf_op jit(solution)/shard_map/pallas_call | solution.py:32
  85.1 3.3 %collective-permute-done.11.refs_2_ = bf16[160,2048]{1,0:T(8,128)(2,1)S(1)} collective-permute-done((bf16[160,2048]{1,0:T(8,128)(2,1)}, bf16[160,2048]{1,0:T(8,128)(2,1)S(1)}, u32[]{:S(2)}, u32[]{:S(2)}) %collective-permute-start.11) | collective-permute-done | bytes 655392 | tf_op jit(solution)/shard_map/ppermute | solution.py:385
  90.6 4.6 %shard_map.64.refs_7_ = f32[2,640,768]{2,1,0:T(8,128)S(1)} custom-call(s32[3]{0:T(128)S(1)} %pad_add_fusion.h_ref._, bf16[2,8,640,512]{3,2,1,0:T(8,128)(2,1)S(1)} %shard_map.57.refs_0_, bf16[3,512,256]{2,1,0:T(8,128)(2,1)S(1)} %copy-done.10, bf16[3,512,256]{2,1,0:T(8,128)(2,1)S(1)} %copy-done.12, bf16[3,512,256]{2,1,0:T(8,128)(2,1)} %collective-permute-done.4.refs_3_, ...), custom_call_target="tpu_custom_call" | custom-call | tf_op jit(solution)/shard_map/pallas_call | solution.py:32
  95.2 2.1 collective-permute-done.21.refs_2_
  103.2 3.9 %collective-permute-done.17.a_ref = bf16[3,512,256]{2,1,0:T(8,128)(2,1)S(1)} collective-permute-done((bf16[3,512,256]{2,1,0:T(8,128)(2,1)}, bf16[3,512,256]{2,1,0:T(8,128)(2,1)S(1)}, u32[]{:S(2)}, u32[]{:S(2)}) %collective-permute-start.17) | collective-permute-done | bytes 786464 | tf_op jit(solution)/shard_map/ppermute | solution.py:385
  107.8 2.6 collective-permute-done.22.refs_7_.refs_13_
  110.4 5.5 %collective-permute-start.27 = (bf16[3,512,256]{2,1,0:T(8,128)(2,1)S(1)}, bf16[3,512,256]{2,1,0:T(8,128)(2,1)S(1)}, u32[]{:S(2)}, u32[]{:S(2)}) collective-permute-start(bf16[3,512,256]{2,1,0:T(8,128)(2,1)S(1)} %collective-permute-done.26), channel_id=1, source_target_pairs={{0,4},{1,5},{2,6},{3,7},{4,0},{5,1},{6,2},{7,3},{8,12},{9,13},{10,... | collective-permute-start | bytes 2359304 | tf_op jit(solution)/shard_map/ppermute | solution.py:385
  123.3 5.8 %shard_map.65.refs_3_ = f32[2,640,768]{2,1,0:T(8,128)S(1)} custom-call(s32[3]{0:T(128)S(1)} %pad_add_fusion.h_ref._, bf16[2,8,640,512]{3,2,1,0:T(8,128)(2,1)S(1)} %shard_map.59.refs_0_, bf16[3,512,256]{2,1,0:T(8,128)(2,1)S(1)} %copy-done.10, bf16[3,512,256]{2,1,0:T(8,128)(2,1)S(1)} %copy-done.12, ...), custom_call_target="tpu_custom_call", output_to_operand_aliasing={{}: (8, {})} | custom-call | tf_op jit(solution)/shard_map/pallas_call | solution.py:32
  129.1 4.3 %collective-permute-done.27.a_ref = bf16[3,512,256]{2,1,0:T(8,128)(2,1)S(1)} collective-permute-done((bf16[3,512,256]{2,1,0:T(8,128)(2,1)S(1)}, bf16[3,512,256]{2,1,0:T(8,128)(2,1)S(1)}, u32[]{:S(2)}, u32[]{:S(2)}) %collective-permute-start.27) | collective-permute-done | bytes 786464 | tf_op jit(solution)/shard_map/ppermute | solution.py:385
  137.3 2.1 collective-permute-start.28
  140.9 2.7 shard_map.67
  145.3 8.4 %collective-permute-done.39.refs_4_ = bf16[3,512,256]{2,1,0:T(8,128)(2,1)S(1)} collective-permute-done((bf16[3,512,256]{2,1,0:T(8,128)(2,1)S(1)}, bf16[3,512,256]{2,1,0:T(8,128)(2,1)S(1)}, u32[]{:S(2)}, u32[]{:S(2)}) %collective-permute-start.39) | collective-permute-done | bytes 786464 | tf_op jit(solution)/shard_map/ppermute | solution.py:385
  159.3 4.0 %copy-done.1 = bf16[2,8,640,512]{3,2,1,0:T(8,128)(2,1)S(1)} copy-done((bf16[2,8,640,512]{3,2,1,0:T(8,128)(2,1)S(1)}, bf16[2,8,640,512]{3,2,1,0:T(8,128)(2,1)}, u32[]{:S(2)}) %copy-start.1) | copy-done | bytes 10485784
  166.7 2.7 shard_map.72.refs_5_
  169.4 2.7 shard_map.73.refs_3_
  172.2 4.9 %shard_map.68.refs_0_ = bf16[640,256]{1,0:T(8,128)(2,1)S(1)} custom-call(s32[3]{0:T(128)S(1)} %pad_add_fusion.h_ref._, s32[640,1]{1,0:T(8,128)S(1)} %copy.15.own_kind_ref.kind_ref, s32[640,1]{1,0:T(8,128)S(1)} %collective-permute-done.other_kind_ref.kind_ref, bf16[640,768]{1,0:T(8,128)(2,1)S(1)} %shard_map.66.own_ref, ...), custom_call_target="tpu_custom_call" | custom-call | tf_op jit(solution)/shard_map/pallas_call | solution.py:32
  180.1 5.9 %collective-permute-start.34 = (bf16[1,256,1024]{2,1,0:T(8,128)(2,1)S(1)}, bf16[1,256,1024]{2,1,0:T(8,128)(2,1)S(1)}, u32[]{:S(2)}, u32[]{:S(2)}) collective-permute-start(bf16[1,256,1024]{2,1,0:T(8,128)(2,1)S(1)} %copy-done.35), channel_id=1, source_target_pairs={{0,4},{1,5},{2,6},{3,7},{4,0},{5,1},{6,2},{7,3},{8,12},{9,13},{10,... | collective-permute-start | bytes 1572872 | tf_op jit(solution)/shard_map/ppermute | solution.py:385
  186.8 2.7 shard_map.74.refs_3_
  189.5 2.7 shard_map.75.refs_3_
  192.3 3.5 %collective-permute-done.41.refs_2_ = bf16[3,512,256]{2,1,0:T(8,128)(2,1)S(1)} collective-permute-done((bf16[3,512,256]{2,1,0:T(8,128)(2,1)S(1)}, bf16[3,512,256]{2,1,0:T(8,128)(2,1)S(1)}, u32[]{:S(2)}, u32[]{:S(2)}) %collective-permute-start.41) | collective-permute-done | bytes 786464 | tf_op jit(solution)/shard_map/ppermute | solution.py:385
  197.6 5.1 %collective-permute-start.35 = (bf16[1,256,1024]{2,1,0:T(8,128)(2,1)S(1)}, bf16[1,256,1024]{2,1,0:T(8,128)(2,1)S(1)}, u32[]{:S(2)}, u32[]{:S(2)}) collective-permute-start(bf16[1,256,1024]{2,1,0:T(8,128)(2,1)S(1)} %collective-permute-done.32), channel_id=1, source_target_pairs={{0,4},{1,5},{2,6},{3,7},{4,0},{5,1},{6,2},{7,3},{8,12},{9,13},{10,... | collective-permute-start | bytes 1572872 | tf_op jit(solution)/shard_map/ppermute | solution.py:385
  202.7 12.5 %collective-permute-done.35.a_ref = bf16[1,256,1024]{2,1,0:T(8,128)(2,1)S(1)} collective-permute-done((bf16[1,256,1024]{2,1,0:T(8,128)(2,1)S(1)}, bf16[1,256,1024]{2,1,0:T(8,128)(2,1)S(1)}, u32[]{:S(2)}, u32[]{:S(2)}) %collective-permute-start.35) | collective-permute-done | bytes 524320 | tf_op jit(solution)/shard_map/ppermute | solution.py:385
  219.4 4.1 %shard_map.78.refs_0_ = bf16[640,256]{1,0:T(8,128)(2,1)S(1)} custom-call(s32[3]{0:T(128)S(1)} %pad_add_fusion.h_ref._, s32[640,1]{1,0:T(8,128)S(1)} %copy.15.own_kind_ref.kind_ref, s32[640,1]{1,0:T(8,128)S(1)} %collective-permute-done.other_kind_ref.kind_ref, bf16[640,768]{1,0:T(8,128)(2,1)S(1)} %shard_map.76.own_ref, ...), custom_call_target="tpu_custom_call" | custom-call | tf_op jit(solution)/shard_map/pallas_call | solution.py:32
  224.7 1.9 collective-permute-start.44
  230.1 3.6 %collective-permute-done.44.refs_2_ = bf16[640,256]{1,0:T(8,128)(2,1)S(1)} collective-permute-done((bf16[640,256]{1,0:T(8,128)(2,1)S(1)}, bf16[640,256]{1,0:T(8,128)(2,1)S(1)}, u32[]{:S(2)}, u32[]{:S(2)}) %collective-permute-start.44) | collective-permute-done | bytes 327712 | tf_op jit(solution)/shard_map/ppermute | solution.py:385
  238.2 6.1 %collective-permute-done.37.refs_3_ = bf16[640,256]{1,0:T(8,128)(2,1)S(1)} collective-permute-done((bf16[640,256]{1,0:T(8,128)(2,1)S(1)}, bf16[640,256]{1,0:T(8,128)(2,1)S(1)}, u32[]{:S(2)}, u32[]{:S(2)}) %collective-permute-start.37) | collective-permute-done | bytes 327712 | tf_op jit(solution)/shard_map/ppermute | solution.py:385
  245.0 6.3 %collective-permute-done.43.refs_1_ = bf16[640,256]{1,0:T(8,128)(2,1)S(1)} collective-permute-done((bf16[640,256]{1,0:T(8,128)(2,1)S(1)}, bf16[640,256]{1,0:T(8,128)(2,1)S(1)}, u32[]{:S(2)}, u32[]{:S(2)}) %collective-permute-start.43) | collective-permute-done | bytes 327712 | tf_op jit(solution)/shard_map/ppermute | solution.py:385
  251.3 5.0 %collective-permute-done.45.refs_3_ = bf16[640,256]{1,0:T(8,128)(2,1)S(1)} collective-permute-done((bf16[640,256]{1,0:T(8,128)(2,1)S(1)}, bf16[640,256]{1,0:T(8,128)(2,1)S(1)}, u32[]{:S(2)}, u32[]{:S(2)}) %collective-permute-start.45) | collective-permute-done | bytes 327712 | tf_op jit(solution)/shard_map/ppermute | solution.py:385
  261.1 13.5 %collective-permute-done.49.a_ref = bf16[1,256,1024]{2,1,0:T(8,128)(2,1)S(1)} collective-permute-done((bf16[1,256,1024]{2,1,0:T(8,128)(2,1)S(1)}, bf16[1,256,1024]{2,1,0:T(8,128)(2,1)S(1)}, u32[]{:S(2)}, u32[]{:S(2)}) %collective-permute-start.49) | collective-permute-done | bytes 524320 | tf_op jit(solution)/shard_map/ppermute | solution.py:385
  276.6 2.8 shard_map.82.refs_20_
  279.4 9.4 %collective-permute-done.53.refs_11_.refs_19_ = bf16[1,256,1024]{2,1,0:T(8,128)(2,1)S(1)} collective-permute-done((bf16[1,256,1024]{2,1,0:T(8,128)(2,1)S(1)}, bf16[1,256,1024]{2,1,0:T(8,128)(2,1)S(1)}, u32[]{:S(2)}, u32[]{:S(2)}) %collective-permute-start.53) | collective-permute-done | bytes 524320 | tf_op jit(solution)/shard_map/ppermute | solution.py:385
  288.7 2.5 shard_map.84
  291.3 2.5 shard_map.83.a_ref
  296.0 15.8 %collective-permute-done.56.c_ref = bf16[320,1024]{1,0:T(8,128)(2,1)S(1)} collective-permute-done((bf16[320,1024]{1,0:T(8,128)(2,1)S(1)}, bf16[320,1024]{1,0:T(8,128)(2,1)S(1)}, u32[]{:S(2)}, u32[]{:S(2)}) %collective-permute-start.56) | collective-permute-done | bytes 655392 | tf_op jit(solution)/shard_map/ppermute | solution.py:385
  311.8 2.1 collective-permute-done.57.d_ref
  313.9 2.3 shard_map.86
  (183 shorter events, 89.4 us)
Async XLA Ops:
  3.5 19.7 %collective-permute-start.3 = (bf16[3,512,256]{2,1,0:T(8,128)(2,1)S(1)}, bf16[3,512,256]{2,1,0:T(8,128)(2,1)S(1)}, u32[]{:S(2)}, u32[]{:S(2)}) collective-permute-start(bf16[3,512,256]{2,1,0:T(8,128)(2,1)S(1)} %get-tuple-element.68), channel_id=1, source_target_pairs={{0,0},{1,1},{2,2},{3,3},{4,8},{5,9},{6,10},{7,11},{8,4},{9,5},{10,... | collective-permute-start | bytes 2359304 | tf_op jit(solution)/shard_map/ppermute | solution.py:385
  7.7 20.5 %collective-permute-start.5 = (bf16[3,512,256]{2,1,0:T(8,128)(2,1)S(1)}, bf16[3,512,256]{2,1,0:T(8,128)(2,1)S(1)}, u32[]{:S(2)}, u32[]{:S(2)}) collective-permute-start(bf16[3,512,256]{2,1,0:T(8,128)(2,1)S(1)} %get-tuple-element.70.refs_1_), channel_id=1, source_target_pairs={{0,2},{1,3},{2,0},{3,1},{4,6},{5,7},{6,4},{7,5},{8,10},{9,11},{10,... | collective-permute-start | bytes 2359304 | tf_op jit(solution)/shard_map/ppermute | solution.py:385
  10.7 21.4 %collective-permute-start.4 = (bf16[3,512,256]{2,1,0:T(8,128)(2,1)S(1)}, bf16[3,512,256]{2,1,0:T(8,128)(2,1)}, u32[]{:S(2)}, u32[]{:S(2)}) collective-permute-start(bf16[3,512,256]{2,1,0:T(8,128)(2,1)S(1)} %get-tuple-element.69), channel_id=1, source_target_pairs={{0,4},{1,5},{2,6},{3,7},{4,0},{5,1},{6,2},{7,3},{8,12},{9,13},{10,... | collective-permute-start | bytes 2359304 | tf_op jit(solution)/shard_map/ppermute | solution.py:385
  15.0 29.8 %collective-permute-start.1 = (bf16[320,2048]{1,0:T(8,128)(2,1)S(1)}, bf16[320,2048]{1,0:T(8,128)(2,1)}, u32[]{:S(2)}, u32[]{:S(2)}) collective-permute-start(bf16[320,2048]{1,0:T(8,128)(2,1)S(1)} %get-tuple-element.65), channel_id=1, source_target_pairs={{0,1},{1,0},{2,3},{3,2},{4,5},{5,4},{6,7},{7,6},{8,9},{9,8},{10,11... | collective-permute-start | bytes 3932168 | tf_op jit(solution)/shard_map/ppermute | solution.py:385
  23.1 21.7 %collective-permute-start.15 = (bf16[3,512,256]{2,1,0:T(8,128)(2,1)S(1)}, bf16[3,512,256]{2,1,0:T(8,128)(2,1)S(1)}, u32[]{:S(2)}, u32[]{:S(2)}) collective-permute-start(bf16[3,512,256]{2,1,0:T(8,128)(2,1)S(1)} %get-tuple-element.80), channel_id=1, source_target_pairs={{4,8},{5,9},{6,10},{7,11},{8,4},{9,5},{10,6},{11,7},{20,24},{21,25... | collective-permute-start | bytes 2359304 | tf_op jit(solution)/shard_map/ppermute | solution.py:385
  32.1 18.2 %collective-permute-start.6 = (bf16[3,512,256]{2,1,0:T(8,128)(2,1)S(1)}, bf16[3,512,256]{2,1,0:T(8,128)(2,1)}, u32[]{:S(2)}, u32[]{:S(2)}) collective-permute-start(bf16[3,512,256]{2,1,0:T(8,128)(2,1)S(1)} %collective-permute-done.3), channel_id=1, source_target_pairs={{0,4},{1,5},{2,6},{3,7},{4,0},{5,1},{6,2},{7,3},{8,12},{9,13},{10,... | collective-permute-start | bytes 2359304 | tf_op jit(solution)/shard_map/ppermute | solution.py:385
  33.8 31.6 %collective-permute-start.19 = (bf16[3,512,256]{2,1,0:T(8,128)(2,1)}, bf16[3,512,256]{2,1,0:T(8,128)(2,1)}, u32[]{:S(2)}, u32[]{:S(2)}) collective-permute-start(bf16[3,512,256]{2,1,0:T(8,128)(2,1)} %collective-permute-done.4.refs_3_), channel_id=1, source_target_pairs={{0,2},{1,3},{2,0},{3,1},{4,6},{5,7},{6,4},{7,5},{8,10},{9,11},{10,... | collective-permute-start | bytes 2359304 | tf_op jit(solution)/shard_map/ppermute | solution.py:385
  44.8 34.6 %collective-permute-start.2 = (bf16[320,2048]{1,0:T(8,128)(2,1)}, bf16[320,2048]{1,0:T(8,128)(2,1)}, u32[]{:S(2)}, u32[]{:S(2)}) collective-permute-start(bf16[320,2048]{1,0:T(8,128)(2,1)} %collective-permute-done.1.refs_2_), channel_id=1, source_target_pairs={{0,16},{1,17},{2,18},{3,19},{4,20},{5,21},{6,22},{7,23},{8,24},{9,... | collective-permute-start | bytes 3932168 | tf_op jit(solution)/shard_map/ppermute | solution.py:385
  50.3 16.4 %collective-permute-start.16 = (bf16[3,512,256]{2,1,0:T(8,128)(2,1)}, bf16[3,512,256]{2,1,0:T(8,128)(2,1)}, u32[]{:S(2)}, u32[]{:S(2)}) collective-permute-start(bf16[3,512,256]{2,1,0:T(8,128)(2,1)} %collective-permute-done.6.a_ref), channel_id=1, source_target_pairs={{4,8},{5,9},{6,10},{7,11},{8,4},{9,5},{10,6},{11,7},{20,24},{21,25... | collective-permute-start | bytes 2359304 | tf_op jit(solution)/shard_map/ppermute | solution.py:385
  60.8 14.8 %collective-permute-start.7 = (bf16[160,2048]{1,0:T(8,128)(2,1)}, bf16[160,2048]{1,0:T(8,128)(2,1)S(1)}, u32[]{:S(2)}, u32[]{:S(2)}) collective-permute-start(bf16[160,2048]{1,0:T(8,128)(2,1)} %copy-done.29), channel_id=1, source_target_pairs={{0,4},{1,5},{2,6},{3,7},{4,0},{5,1},{6,2},{7,3},{8,12},{9,13},{10,... | collective-permute-start | bytes 1966088 | tf_op jit(solution)/shard_map/ppermute | solution.py:385
  65.4 18.4 %collective-permute-start.20 = (bf16[3,512,256]{2,1,0:T(8,128)(2,1)S(1)}, bf16[3,512,256]{2,1,0:T(8,128)(2,1)S(1)}, u32[]{:S(2)}, u32[]{:S(2)}) collective-permute-start(bf16[3,512,256]{2,1,0:T(8,128)(2,1)S(1)} %shard_map.63.refs_5_), channel_id=1, source_target_pairs={{0,2},{1,3},{2,0},{3,1},{4,6},{5,7},{6,4},{7,5},{8,10},{9,11},{10,... | collective-permute-start | bytes 2359304 | tf_op jit(solution)/shard_map/ppermute | solution.py:385
  66.7 23.0 %collective-permute-start.18 = (bf16[3,512,256]{2,1,0:T(8,128)(2,1)}, bf16[3,512,256]{2,1,0:T(8,128)(2,1)S(1)}, u32[]{:S(2)}, u32[]{:S(2)}) collective-permute-start(bf16[3,512,256]{2,1,0:T(8,128)(2,1)} %collective-permute-done.4.refs_3_), channel_id=1, source_target_pairs={{4,8},{5,9},{6,10},{7,11},{8,4},{9,5},{10,6},{11,7},{20,24},{21,25... | collective-permute-start | bytes 2359304 | tf_op jit(solution)/shard_map/ppermute | solution.py:385
  75.6 12.8 %collective-permute-start.11 = (bf16[160,2048]{1,0:T(8,128)(2,1)}, bf16[160,2048]{1,0:T(8,128)(2,1)S(1)}, u32[]{:S(2)}, u32[]{:S(2)}) collective-permute-start(bf16[160,2048]{1,0:T(8,128)(2,1)} %copy-done.28), channel_id=1, source_target_pairs={{0,4},{1,5},{2,6},{3,7},{4,0},{5,1},{6,2},{7,3},{8,12},{9,13},{10,... | collective-permute-start | bytes 1966088 | tf_op jit(solution)/shard_map/ppermute | solution.py:385
  77.9 12.5 %collective-permute-start.8 = (bf16[160,2048]{1,0:T(8,128)(2,1)S(1)}, bf16[160,2048]{1,0:T(8,128)(2,1)S(1)}, u32[]{:S(2)}, u32[]{:S(2)}) collective-permute-start(bf16[160,2048]{1,0:T(8,128)(2,1)S(1)} %collective-permute-done.7.refs_2_), channel_id=1, source_target_pairs={{0,1},{1,0},{2,3},{3,2},{4,5},{5,4},{6,7},{7,6},{8,9},{9,8},{10,11... | collective-permute-start | bytes 1966088 | tf_op jit(solution)/shard_map/ppermute | solution.py:385
  83.8 13.5 %collective-permute-start.21 = (bf16[3,512,256]{2,1,0:T(8,128)(2,1)S(1)}, bf16[3,512,256]{2,1,0:T(8,128)(2,1)S(1)}, u32[]{:S(2)}, u32[]{:S(2)}) collective-permute-start(bf16[3,512,256]{2,1,0:T(8,128)(2,1)S(1)} %copy-done.7), channel_id=1, source_target_pairs={{0,2},{1,3},{2,0},{3,1},{4,6},{5,7},{6,4},{7,5},{8,10},{9,11},{10,... | collective-permute-start | bytes 2359304 | tf_op jit(solution)/shard_map/ppermute | solution.py:385
  85.1 14.8 %collective-permute-start.9 = (bf16[160,2048]{1,0:T(8,128)(2,1)S(1)}, bf16[160,2048]{1,0:T(8,128)(2,1)S(1)}, u32[]{:S(2)}, u32[]{:S(2)}) collective-permute-start(bf16[160,2048]{1,0:T(8,128)(2,1)S(1)} %collective-permute-done.7.refs_2_), channel_id=1, source_target_pairs={{0,16},{1,17},{2,18},{3,19},{4,20},{5,21},{6,22},{7,23},{8,24},{9,... | collective-permute-start | bytes 1966088 | tf_op jit(solution)/shard_map/ppermute | solution.py:385
  88.4 18.8 %collective-permute-start.17 = (bf16[3,512,256]{2,1,0:T(8,128)(2,1)}, bf16[3,512,256]{2,1,0:T(8,128)(2,1)S(1)}, u32[]{:S(2)}, u32[]{:S(2)}) collective-permute-start(bf16[3,512,256]{2,1,0:T(8,128)(2,1)} %collective-permute-done.16), channel_id=1, source_target_pairs={{4,0},{5,1},{6,2},{7,3},{8,12},{9,13},{10,14},{11,15},{20,16},{21,... | collective-permute-start | bytes 2359304 | tf_op jit(solution)/shard_map/ppermute | solution.py:385
  89.7 20.7 %collective-permute-start.26 = (bf16[3,512,256]{2,1,0:T(8,128)(2,1)S(1)}, bf16[3,512,256]{2,1,0:T(8,128)(2,1)S(1)}, u32[]{:S(2)}, u32[]{:S(2)}) collective-permute-start(bf16[3,512,256]{2,1,0:T(8,128)(2,1)S(1)} %copy-done.27), channel_id=1, source_target_pairs={{0,0},{1,1},{2,2},{3,3},{4,8},{5,9},{6,10},{7,11},{8,4},{9,5},{10,... | collective-permute-start | bytes 2359304 | tf_op jit(solution)/shard_map/ppermute | solution.py:385
  98.2 12.2 %collective-permute-start.22 = (bf16[1,256,1024]{2,1,0:T(8,128)(2,1)S(1)}, bf16[1,256,1024]{2,1,0:T(8,128)(2,1)S(1)}, u32[]{:S(2)}, u32[]{:S(2)}) collective-permute-start(bf16[1,256,1024]{2,1,0:T(8,128)(2,1)S(1)} %get-tuple-element.87.refs_6_.refs_12_), channel_id=1, source_target_pairs={{0,2},{1,3},{2,0},{3,1},{4,6},{5,7},{6,4},{7,5},{8,10},{9,11},{10,... | collective-permute-start | bytes 1572872 | tf_op jit(solution)/shard_map/ppermute | solution.py:385
  99.9 18.5 %collective-permute-start.12 = (bf16[160,2048]{1,0:T(8,128)(2,1)S(1)}, bf16[160,2048]{1,0:T(8,128)(2,1)S(1)}, u32[]{:S(2)}, u32[]{:S(2)}) collective-permute-start(bf16[160,2048]{1,0:T(8,128)(2,1)S(1)} %collective-permute-done.11.refs_2_), channel_id=1, source_target_pairs={{0,1},{1,0},{2,3},{3,2},{4,5},{5,4},{6,7},{7,6},{8,9},{9,8},{10,11... | collective-permute-start | bytes 1966088 | tf_op jit(solution)/shard_map/ppermute | solution.py:385
  110.4 23.0 %collective-permute-start.27 = (bf16[3,512,256]{2,1,0:T(8,128)(2,1)S(1)}, bf16[3,512,256]{2,1,0:T(8,128)(2,1)S(1)}, u32[]{:S(2)}, u32[]{:S(2)}) collective-permute-start(bf16[3,512,256]{2,1,0:T(8,128)(2,1)S(1)} %collective-permute-done.26), channel_id=1, source_target_pairs={{0,4},{1,5},{2,6},{3,7},{4,0},{5,1},{6,2},{7,3},{8,12},{9,13},{10,... | collective-permute-start | bytes 2359304 | tf_op jit(solution)/shard_map/ppermute | solution.py:385
  115.9 17.5 %collective-permute-start.29 = (bf16[3,512,256]{2,1,0:T(8,128)(2,1)S(1)}, bf16[3,512,256]{2,1,0:T(8,128)(2,1)S(1)}, u32[]{:S(2)}, u32[]{:S(2)}) collective-permute-start(bf16[3,512,256]{2,1,0:T(8,128)(2,1)S(1)} %copy-done.25), channel_id=1, source_target_pairs={{4,8},{5,9},{6,10},{7,11},{8,4},{9,5},{10,6},{11,7},{20,24},{21,25... | collective-permute-start | bytes 2359304 | tf_op jit(solution)/shard_map/ppermute | solution.py:385
  116.6 19.0 %collective-permute-start.23 = (bf16[3,512,256]{2,1,0:T(8,128)(2,1)S(1)}, bf16[3,512,256]{2,1,0:T(8,128)(2,1)S(1)}, u32[]{:S(2)}, u32[]{:S(2)}) collective-permute-start(bf16[3,512,256]{2,1,0:T(8,128)(2,1)S(1)} %shard_map.62.refs_1_), channel_id=1, source_target_pairs={{0,2},{1,3},{2,0},{3,1},{4,6},{5,7},{6,4},{7,5},{8,10},{9,11},{10,... | collective-permute-start | bytes 2359304 | tf_op jit(solution)/shard_map/ppermute | solution.py:385
  135.6 18.1 %collective-permute-start.39 = (bf16[3,512,256]{2,1,0:T(8,128)(2,1)S(1)}, bf16[3,512,256]{2,1,0:T(8,128)(2,1)S(1)}, u32[]{:S(2)}, u32[]{:S(2)}) collective-permute-start(bf16[3,512,256]{2,1,0:T(8,128)(2,1)S(1)} %shard_map.71.refs_3_), channel_id=1, source_target_pairs={{0,2},{1,3},{2,0},{3,1},{4,6},{5,7},{6,4},{7,5},{8,10},{9,11},{10,... | collective-permute-start | bytes 2359304 | tf_op jit(solution)/shard_map/ppermute | solution.py:385
  137.3 18.4 %collective-permute-start.28 = (bf16[3,512,256]{2,1,0:T(8,128)(2,1)S(1)}, bf16[3,512,256]{2,1,0:T(8,128)(2,1)}, u32[]{:S(2)}, u32[]{:S(2)}) collective-permute-start(bf16[3,512,256]{2,1,0:T(8,128)(2,1)S(1)} %copy-done.23), channel_id=1, source_target_pairs={{0,4},{1,5},{2,6},{3,7},{4,0},{5,1},{6,2},{7,3},{8,12},{9,13},{10,... | collective-permute-start | bytes 2359304 | tf_op jit(solution)/shard_map/ppermute | solution.py:385
  139.4 16.3 %collective-permute-start.30 = (bf16[3,512,256]{2,1,0:T(8,128)(2,1)S(1)}, bf16[3,512,256]{2,1,0:T(8,128)(2,1)}, u32[]{:S(2)}, u32[]{:S(2)}) collective-permute-start(bf16[3,512,256]{2,1,0:T(8,128)(2,1)S(1)} %collective-permute-done.27.a_ref), channel_id=1, source_target_pairs={{4,8},{5,9},{6,10},{7,11},{8,4},{9,5},{10,6},{11,7},{20,24},{21,25... | collective-permute-start | bytes 2359304 | tf_op jit(solution)/shard_map/ppermute | solution.py:385
  143.6 28.6 %collective-permute-start.24 = (bf16[640,768]{1,0:T(8,128)(2,1)}, bf16[640,768]{1,0:T(8,128)(2,1)}, u32[]{:S(2)}, u32[]{:S(2)}) collective-permute-start(bf16[640,768]{1,0:T(8,128)(2,1)} %shard_map.67), channel_id=1, source_target_pairs={{0,16},{1,17},{2,18},{3,19},{4,20},{5,21},{6,22},{7,23},{8,24},{9,... | collective-permute-start | bytes 2949128 | tf_op jit(solution)/shard_map/ppermute | solution.py:385
  155.7 21.4 %collective-permute-start.33 = (bf16[3,512,256]{2,1,0:T(8,128)(2,1)}, bf16[3,512,256]{2,1,0:T(8,128)(2,1)}, u32[]{:S(2)}, u32[]{:S(2)}) collective-permute-start(bf16[3,512,256]{2,1,0:T(8,128)(2,1)} %collective-permute-done.30), channel_id=1, source_target_pairs={{4,0},{5,1},{6,2},{7,3},{8,12},{9,13},{10,14},{11,15},{20,16},{21,... | collective-permute-start | bytes 2359304 | tf_op jit(solution)/shard_map/ppermute | solution.py:385
  157.0 20.1 %collective-permute-start.31 = (bf16[3,512,256]{2,1,0:T(8,128)(2,1)}, bf16[3,512,256]{2,1,0:T(8,128)(2,1)}, u32[]{:S(2)}, u32[]{:S(2)}) collective-permute-start(bf16[3,512,256]{2,1,0:T(8,128)(2,1)} %collective-permute-done.28.refs_1_), channel_id=1, source_target_pairs={{4,8},{5,9},{6,10},{7,11},{8,4},{9,5},{10,6},{11,7},{20,24},{21,25... | collective-permute-start | bytes 2359304 | tf_op jit(solution)/shard_map/ppermute | solution.py:385
  158.6 20.0 %collective-permute-start.40 = (bf16[3,512,256]{2,1,0:T(8,128)(2,1)}, bf16[3,512,256]{2,1,0:T(8,128)(2,1)}, u32[]{:S(2)}, u32[]{:S(2)}) collective-permute-start(bf16[3,512,256]{2,1,0:T(8,128)(2,1)} %collective-permute-done.28.refs_1_), channel_id=1, source_target_pairs={{0,2},{1,3},{2,0},{3,1},{4,6},{5,7},{6,4},{7,5},{8,10},{9,11},{10,... | collective-permute-start | bytes 2359304 | tf_op jit(solution)/shard_map/ppermute | solution.py:385
  178.5 17.2 %collective-permute-start.41 = (bf16[3,512,256]{2,1,0:T(8,128)(2,1)S(1)}, bf16[3,512,256]{2,1,0:T(8,128)(2,1)S(1)}, u32[]{:S(2)}, u32[]{:S(2)}) collective-permute-start(bf16[3,512,256]{2,1,0:T(8,128)(2,1)S(1)} %shard_map.70.refs_1_), channel_id=1, source_target_pairs={{0,2},{1,3},{2,0},{3,1},{4,6},{5,7},{6,4},{7,5},{8,10},{9,11},{10,... | collective-permute-start | bytes 2359304 | tf_op jit(solution)/shard_map/ppermute | solution.py:385
  180.1 17.5 %collective-permute-start.34 = (bf16[1,256,1024]{2,1,0:T(8,128)(2,1)S(1)}, bf16[1,256,1024]{2,1,0:T(8,128)(2,1)S(1)}, u32[]{:S(2)}, u32[]{:S(2)}) collective-permute-start(bf16[1,256,1024]{2,1,0:T(8,128)(2,1)S(1)} %copy-done.35), channel_id=1, source_target_pairs={{0,4},{1,5},{2,6},{3,7},{4,0},{5,1},{6,2},{7,3},{8,12},{9,13},{10,... | collective-permute-start | bytes 1572872 | tf_op jit(solution)/shard_map/ppermute | solution.py:385
  186.0 11.6 %collective-permute-start.32 = (bf16[1,256,1024]{2,1,0:T(8,128)(2,1)S(1)}, bf16[1,256,1024]{2,1,0:T(8,128)(2,1)S(1)}, u32[]{:S(2)}, u32[]{:S(2)}) collective-permute-start(bf16[1,256,1024]{2,1,0:T(8,128)(2,1)S(1)} %copy-done.33), channel_id=1, source_target_pairs={{0,0},{1,1},{2,2},{3,3},{4,8},{5,9},{6,10},{7,11},{8,4},{9,5},{10,... | collective-permute-start | bytes 1572872 | tf_op jit(solution)/shard_map/ppermute | solution.py:385
  197.5 21.9 %collective-permute-start.42 = (bf16[640,768]{1,0:T(8,128)(2,1)S(1)}, bf16[640,768]{1,0:T(8,128)(2,1)S(1)}, u32[]{:S(2)}, u32[]{:S(2)}) collective-permute-start(bf16[640,768]{1,0:T(8,128)(2,1)S(1)} %shard_map.77), channel_id=1, source_target_pairs={{0,16},{1,17},{2,18},{3,19},{4,20},{5,21},{6,22},{7,23},{8,24},{9,... | collective-permute-start | bytes 2949128 | tf_op jit(solution)/shard_map/ppermute | solution.py:385
  197.6 17.6 %collective-permute-start.35 = (bf16[1,256,1024]{2,1,0:T(8,128)(2,1)S(1)}, bf16[1,256,1024]{2,1,0:T(8,128)(2,1)S(1)}, u32[]{:S(2)}, u32[]{:S(2)}) collective-permute-start(bf16[1,256,1024]{2,1,0:T(8,128)(2,1)S(1)} %collective-permute-done.32), channel_id=1, source_target_pairs={{0,4},{1,5},{2,6},{3,7},{4,0},{5,1},{6,2},{7,3},{8,12},{9,13},{10,... | collective-permute-start | bytes 1572872 | tf_op jit(solution)/shard_map/ppermute | solution.py:385
  217.0 18.3 %collective-permute-start.47 = (bf16[1,256,1024]{2,1,0:T(8,128)(2,1)S(1)}, bf16[1,256,1024]{2,1,0:T(8,128)(2,1)S(1)}, u32[]{:S(2)}, u32[]{:S(2)}) collective-permute-start(bf16[1,256,1024]{2,1,0:T(8,128)(2,1)S(1)} %copy-done.31), channel_id=1, source_target_pairs={{4,8},{5,9},{6,10},{7,11},{8,4},{9,5},{10,6},{11,7},{20,24},{21,25... | collective-permute-start | bytes 1572872 | tf_op jit(solution)/shard_map/ppermute | solution.py:385
  228.1 16.2 %collective-permute-start.37 = (bf16[640,256]{1,0:T(8,128)(2,1)S(1)}, bf16[640,256]{1,0:T(8,128)(2,1)S(1)}, u32[]{:S(2)}, u32[]{:S(2)}) collective-permute-start(bf16[640,256]{1,0:T(8,128)(2,1)S(1)} %collective-permute-done.36.refs_2_), channel_id=1, source_target_pairs={{0,1},{1,0},{2,3},{3,2},{4,5},{5,4},{6,7},{7,6},{8,9},{9,8},{10,11... | collective-permute-start | bytes 983048 | tf_op jit(solution)/shard_map/ppermute | solution.py:385
  228.6 22.7 %collective-permute-start.43 = (bf16[640,256]{1,0:T(8,128)(2,1)S(1)}, bf16[640,256]{1,0:T(8,128)(2,1)S(1)}, u32[]{:S(2)}, u32[]{:S(2)}) collective-permute-start(bf16[640,256]{1,0:T(8,128)(2,1)S(1)} %shard_map.78.refs_0_), channel_id=1, source_target_pairs={{0,1},{1,0},{2,3},{3,2},{4,5},{5,4},{6,7},{7,6},{8,9},{9,8},{10,11... | collective-permute-start | bytes 983048 | tf_op jit(solution)/shard_map/ppermute | solution.py:385
  233.8 22.5 %collective-permute-start.45 = (bf16[640,256]{1,0:T(8,128)(2,1)S(1)}, bf16[640,256]{1,0:T(8,128)(2,1)S(1)}, u32[]{:S(2)}, u32[]{:S(2)}) collective-permute-start(bf16[640,256]{1,0:T(8,128)(2,1)S(1)} %collective-permute-done.44.refs_2_), channel_id=1, source_target_pairs={{0,1},{1,0},{2,3},{3,2},{4,5},{5,4},{6,7},{7,6},{8,9},{9,8},{10,11... | collective-permute-start | bytes 983048 | tf_op jit(solution)/shard_map/ppermute | solution.py:385
  235.3 22.3 %collective-permute-start.51 = (bf16[1,256,1024]{2,1,0:T(8,128)(2,1)S(1)}, bf16[1,256,1024]{2,1,0:T(8,128)(2,1)S(1)}, u32[]{:S(2)}, u32[]{:S(2)}) collective-permute-start(bf16[1,256,1024]{2,1,0:T(8,128)(2,1)S(1)} %collective-permute-done.34.refs_8_.refs_14_), channel_id=1, source_target_pairs={{0,2},{1,3},{2,0},{3,1},{4,6},{5,7},{6,4},{7,5},{8,10},{9,11},{10,... | collective-permute-start | bytes 1572872 | tf_op jit(solution)/shard_map/ppermute | solution.py:385
  237.2 20.4 %collective-permute-start.48 = (bf16[1,256,1024]{2,1,0:T(8,128)(2,1)S(1)}, bf16[1,256,1024]{2,1,0:T(8,128)(2,1)S(1)}, u32[]{:S(2)}, u32[]{:S(2)}) collective-permute-start(bf16[1,256,1024]{2,1,0:T(8,128)(2,1)S(1)} %collective-permute-done.35.a_ref), channel_id=1, source_target_pairs={{4,8},{5,9},{6,10},{7,11},{8,4},{9,5},{10,6},{11,7},{20,24},{21,25... | collective-permute-start | bytes 1572872 | tf_op jit(solution)/shard_map/ppermute | solution.py:385
  244.9 31.7 %collective-permute-start.38 = (bf16[4,640,256]{2,1,0:T(8,128)(2,1)S(1)}, bf16[4,640,256]{2,1,0:T(8,128)(2,1)S(1)}, u32[]{:S(2)}, u32[]{:S(2)}) collective-permute-start(bf16[4,640,256]{2,1,0:T(8,128)(2,1)S(1)} %shard_map.69.refs_0_.refs_2_.refs_4_), channel_id=1, source_target_pairs={{0,16},{1,17},{2,18},{3,19},{4,20},{5,21},{6,22},{7,23},{8,24},{9,... | collective-permute-start | bytes 3932168 | tf_op jit(solution)/shard_map/ppermute | solution.py:385
  256.9 31.8 %collective-permute-start.46 = (bf16[4,640,256]{2,1,0:T(8,128)(2,1)S(1)}, bf16[4,640,256]{2,1,0:T(8,128)(2,1)S(1)}, u32[]{:S(2)}, u32[]{:S(2)}) collective-permute-start(bf16[4,640,256]{2,1,0:T(8,128)(2,1)S(1)} %shard_map.79.refs_2_.refs_4_.refs_6_.refs_8_), channel_id=1, source_target_pairs={{0,16},{1,17},{2,18},{3,19},{4,20},{5,21},{6,22},{7,23},{8,24},{9,... | collective-permute-start | bytes 3932168 | tf_op jit(solution)/shard_map/ppermute | solution.py:385
  258.3 16.2 %collective-permute-start.49 = (bf16[1,256,1024]{2,1,0:T(8,128)(2,1)S(1)}, bf16[1,256,1024]{2,1,0:T(8,128)(2,1)S(1)}, u32[]{:S(2)}, u32[]{:S(2)}) collective-permute-start(bf16[1,256,1024]{2,1,0:T(8,128)(2,1)S(1)} %collective-permute-done.48), channel_id=1, source_target_pairs={{4,0},{5,1},{6,2},{7,3},{8,12},{9,13},{10,14},{11,15},{20,16},{21,... | collective-permute-start | bytes 1572872 | tf_op jit(solution)/shard_map/ppermute | solution.py:385
  259.6 15.5 %collective-permute-start.52 = (bf16[1,256,1024]{2,1,0:T(8,128)(2,1)S(1)}, bf16[1,256,1024]{2,1,0:T(8,128)(2,1)S(1)}, u32[]{:S(2)}, u32[]{:S(2)}) collective-permute-start(bf16[1,256,1024]{2,1,0:T(8,128)(2,1)S(1)} %shard_map.81.refs_10_.refs_16_), channel_id=1, source_target_pairs={{0,2},{1,3},{2,0},{3,1},{4,6},{5,7},{6,4},{7,5},{8,10},{9,11},{10,... | collective-permute-start | bytes 1572872 | tf_op jit(solution)/shard_map/ppermute | solution.py:385
  275.1 13.6 %collective-permute-start.53 = (bf16[1,256,1024]{2,1,0:T(8,128)(2,1)S(1)}, bf16[1,256,1024]{2,1,0:T(8,128)(2,1)S(1)}, u32[]{:S(2)}, u32[]{:S(2)}) collective-permute-start(bf16[1,256,1024]{2,1,0:T(8,128)(2,1)S(1)} %shard_map.80.refs_10_.refs_18_), channel_id=1, source_target_pairs={{0,2},{1,3},{2,0},{3,1},{4,6},{5,7},{6,4},{7,5},{8,10},{9,11},{10,... | collective-permute-start | bytes 1572872 | tf_op jit(solution)/shard_map/ppermute | solution.py:385
  293.8 18.1 %collective-permute-start.54 = (bf16[640,1024]{1,0:T(8,128)(2,1)S(1)}, bf16[640,1024]{1,0:T(8,128)(2,1)S(1)}, u32[]{:S(2)}, u32[]{:S(2)}) collective-permute-start(bf16[640,1024]{1,0:T(8,128)(2,1)S(1)} %shard_map.83.a_ref), channel_id=1, source_target_pairs={{0,16},{1,17},{2,18},{3,19},{4,20},{5,21},{6,22},{7,23},{8,24},{9,... | collective-permute-start | bytes 3932168 | tf_op jit(solution)/shard_map/ppermute | solution.py:385
  295.1 16.7 %collective-permute-start.56 = (bf16[320,1024]{1,0:T(8,128)(2,1)S(1)}, bf16[320,1024]{1,0:T(8,128)(2,1)S(1)}, u32[]{:S(2)}, u32[]{:S(2)}) collective-permute-start(bf16[320,1024]{1,0:T(8,128)(2,1)S(1)} %shard_map.85), channel_id=1, source_target_pairs={{0,4},{1,5},{2,6},{3,7},{4,0},{5,1},{6,2},{7,3},{8,12},{9,13},{10,... | collective-permute-start | bytes 1966088 | tf_op jit(solution)/shard_map/ppermute | solution.py:385
  (49 other events, 512.3 us)

commit v8 on v7

--- a/solution.py
+++ b/solution.py
@@ -399,6 +399,9 @@
     def outward(m, d, x):
         return (m, d ^ 2, x) if d // 2 in (1, 2) else None
 
+    def inward(m, d, x):
+        return (m, d ^ 2, x) if d // 2 in (0, 3) else None
+
     def across(m, d, x):
         return (m, (3 - d // 2) * 2 + d % 2, x) if d // 2 in (1, 2) else None
 
@@ -420,102 +423,127 @@
         low_a, high_a, mine_a, away_a = halves(here, weight, 0, 2)
         m1a = move(low_a, across_or_stay)
         e1a = move(away_a, edge)
+        p1a = move(mine_a, pair)
+        other_kind = move(own_kind, edge)
         rows, top, bottom = own_rows_of(here, after(tokens, mine_a))
-        p1a = move(mine_a, pair, rows)
         fetched = over_tensor(rows)
-        other_kind = move(own_kind, edge, rows)
-        low_b, high_b, mine_b, away_b = halves(here, after(weight, rows), 1, 2)
-        low_o, high_o, mine_o, away_o = halves(here, after(out_weight, mine_b), 0, 1)
-
-        m2a = move(high_a, across, m1a, mine_o)
-        e2a = move(m1a, edge, e1a, p1a)
+
+        m2a = move(high_a, across, m1a)
+        e2a = move(m1a, edge, e1a, p1a, other_kind)
         p2a = move(e1a, pair, p1a)
+        low_b, high_b, mine_b, away_b = halves(here, after(weight, m1a), 1, 2)
         swapped = [to_core(a) for a in fetched[1:]]
 
-        m3a = move(e2a, across, m2a)
-        passed_top = move(top, edge, e2a, other_kind)
+        m3a = move(e2a, across, m2a, mine_b)
+        passed_top = move(top, edge, e2a, m2a)
         third_a = choose(here, e2a, m2a)
         p3a = move(third_a, pair, p2a)
         shape = (2, places, length, kept)
-        normed = normalize(here, "own", None, gains, tokens, fetched[1:], swapped, shape, 0, half)
+        normed = normalize(
+            here, "own", None, gains, after(tokens, m2a), fetched[1:], swapped, shape, 0, half
+        )
 
         m4a = move(e1a, across, m3a)
-        passed_bottom = move(bottom, edge, passed_top)
+        passed_bottom = move(bottom, edge, passed_top, m3a)
         p1b = move(mine_b, pair, p3a, normed)
         part_top = over_tensor(passed_top)
         first_a = [(0, mine_a, p1a), (1, e1a, p2a), (2, third_a, p3a)]
-        total_a = project(here, "own", normed, first_a, fresh=True)
+        total_a = project(here, "own", after(normed, m3a), first_a, fresh=True)
+        low_o, high_o, mine_o, away_o = halves(here, after(out_weight, m3a), 0, 1)
 
         m1b = move(low_b, across_or_stay, m4a)
         e3a = move(m3a, outward, passed_bottom)
+        i1o = move(low_o, inward, passed_bottom)
         p1o = move(mine_o, pair, p1b, total_a)
         part_bottom = over_tensor(passed_bottom)
         top_swapped = [to_core(a) for a in part_top]
         normed = normalize(
-            here, "partner", normed, gains, None, part_top, top_swapped, shape, 0, half // 2
+            here,
+            "partner",
+            normed,
+            gains,
+            None,
+            [after(part_top[0], m4a)] + part_top[1:],
+            top_swapped,
+            shape,
+            0,
+            half // 2,
         )
 
         m2b = move(high_b, across, m1b)
-        e2b = move(m1b, edge, e3a)
+        e2b = move(m1b, edge, e3a, i1o)
         fourth_a = choose(here, e3a, m4a)
         p4a = move(fourth_a, pair, p1o, normed)
         bottom_swapped = [to_core(a) for a in part_bottom]
         normed = normalize(
-            here, "partner", normed, gains, None, part_bottom, bottom_swapped, shape, half // 2, half // 2
+            here,
+            "partner",
+            normed,
+            gains,
+            None,
+            [after(part_bottom[0], m1b)] + part_bottom[1:],
+            bottom_swapped,
+            shape,
+            half // 2,
+            half // 2,
         )
         total_a = project(here, "partner", normed, first_a, total_a, fresh=True)
 
         m3b = move(e2b, across, m2b)
-        e1b = move(away_b, edge, e2b)
+        e1b = move(away_b, edge, e2b, m2b)
         third_b = choose(here, e2b, m2b)
         p3b = move(third_b, pair, p4a, total_a)
         last_a = [(3, fourth_a, p4a)]
-        theirs_a = project(here, 1, normed, last_a, total_a, final=True)
+        theirs_a = project(here, 1, after(normed, m2b), last_a, total_a, final=True)
         got_a = to_core(theirs_a)
         ours_a = project(here, 0, normed, last_a, total_a, final=True)
 
         m4b = move(e1b, across, m3b)
         e3b = move(m3b, outward, e1b)
+        i2o = move(high_o, inward, e1b)
         p2b = move(e1b, pair, p3b, ours_a)
-        attended_a = attend(here, own_kind, other_kind, ours_a, got_a)
+        attended_a = attend(here, own_kind, other_kind, after(ours_a, m3b), got_a)
         first_b = [(0, mine_b, p1b), (2, third_b, p3b)]
-        total_b = project(here, "own", normed, first_b, fresh=True)
-        total_b = project(here, "partner", normed, first_b, total_b, fresh=True)
+        late_normed = after(normed, m3b)
+        total_b = project(here, "own", late_normed, first_b, fresh=True)
+        total_b = project(here, "partner", late_normed, first_b, total_b, fresh=True)
         held_a = over_tensor(attended_a)
 
-        m1o = move(low_o, across_or_stay, m4b)
+        m1o = move(low_o, across, m4b)
+        m3o = move(i1o, across, m4b)
         fourth_b = choose(here, e3b, m4b)
-        p4b = move(fourth_b, pair, p2b, attended_a, total_b)
-        e1o = move(away_o, edge, e3b)
+        p4b = move(fourth_b, pair, p2b)
+        o1o = move(low_o, outward, e3b, m4b)
         second_b = [(1, e1b, p2b)]
-        total_b = project(here, "own", normed, second_b, total_b)
-        total_b = project(here, "partner", normed, second_b, total_b)
-
-        m2o = move(high_o, across, m1o)
-        e2o = move(m1o, edge, e1o)
+        late_normed = after(normed, m4b, attended_a)
+        total_b = project(here, "own", late_normed, second_b, total_b)
+        total_b = project(here, "partner", late_normed, second_b, total_b)
+        passed_a = move(attended_a, edge, o1o)
+        held_a += over_tensor(passed_a)
+
+        second_o = choose(here, o1o, i2o)
+        p2o = move(second_o, pair, p4b)
         last_b = [(3, fourth_b, p4b)]
         theirs_b = project(here, 1, normed, last_b, total_b, final=True)
         got_b = to_core(theirs_b)
         ours_b = project(here, 0, normed, last_b, total_b, final=True)
+        m2o = move(high_o, across, m1o)
+        m4o = move(i2o, across, m3o)
+        o2o = move(m1o, outward, passed_a)
+        o3o = move(m3o, outward, o2o)
         attended_b = attend(here, own_kind, other_kind, ours_b, got_b)
-
-        p2o = move(e1o, pair, p4b)
-        m3o = move(e2o, across, m2o)
-        m4o = move(e1o, across, m3o)
-        third_o = choose(here, e2o, m2o)
+        passed_b = move(attended_b, edge, passed_a)
+        held_b = over_tensor(attended_b)
+        held_b += over_tensor(passed_b)
+
+        third_o = choose(here, o2o, m2o)
         p3o = move(third_o, pair, p2o)
-        passed_a = move(attended_a, edge, e2o)
-        held_a += over_tensor(passed_a)
-        e3o = move(m3o, outward, passed_a)
         pieces_a = stack(here, held_a)
         pieces_a = (pieces_a, to_core(pieces_a))
-        fourth_o = choose(here, e3o, m4o)
-        held_b = over_tensor(attended_b)
-        held_b += over_tensor(move(attended_b, edge, passed_a))
-        blocks = [(0, mine_o, p1o), (1, e1o, p2o), (2, third_o, p3o)]
-
+        fourth_o = choose(here, o3o, m4o)
+        p4o = move(fourth_o, pair, p3o)
+        blocks = [(0, mine_o, p1o), (1, second_o, p2o), (2, third_o, p3o)]
         total = combine(here, ("partner", "own"), [pieces_a + (0, blocks)])
-        p4o = move(fourth_o, pair, p3o)
         last = [(3, fourth_o, p4o)]
         pieces_b = stack(here, held_b)
         pieces_b = (pieces_b, to_core(pieces_b))

time: 317 us -> 317 us (level)
  local copies, waits for them, and re-layouts: 23.5 us -> 6.31 us
  waiting for transfers between devices: 145 us -> 156 us
  starting transfers between devices: 80.3 us -> 88.3 us
    unnamed x78 -> x20, local copies, waits for them, and re-layouts: 21.8 us -> 5.46 us
    ppermute x58 -> x60, waiting for transfers between devices: 145 us -> 156 us  [move(): lax.ppermute(after(array, *earlier) if earlier else array, AXES, pairs)]
    ppermute x58 -> x60, starting transfers between devices: 80.3 us -> 88.3 us  [move(): lax.ppermute(after(array, *earlier) if earlier else array, AXES, pairs)]
    pallas_call x31 -> x32, Pallas kernels: 64 us -> 61.9 us  [call(): pl.pallas_call(kernel, in_specs=[pl.BlockSpec(memory_space=SMEM)] + [pl.B...]
  transfers between devices with their start and end apart: 58 -> 60, of which waited for: 28 -> 25; matrix products, arithmetic and copies ran while one was open for 0% -> 0% of each run, Pallas kernels for 19% -> 18%
where the time goes in v8:
time: 317 us; the launch traced here: 316 us
  waiting for transfers between devices  156 us (49%)
  starting transfers between devices  88.3 us (28%)
  Pallas kernels  64.2 us (20%)
  local copies, waits for them, and re-layouts  6.31 us (2%)
    ppermute x60, waiting for transfers between devices, move(): lax.ppermute(after(array, *earlier) if earlier else array, AXES, pairs)  156 us
    ppermute x60, starting transfers between devices, move(): lax.ppermute(after(array, *earlier) if earlier else array, AXES, pairs)  88.3 us
    pallas_call x32, Pallas kernels, call(): pl.pallas_call(kernel, in_specs=[pl.BlockSpec(memory_space=SMEM)] + [pl.B...  61.9 us
  transfers between devices with their start and end apart: 60, of which 25 were waited for; matrix products, arithmetic and copies ran while one was open for 0% of the time, Pallas kernels for 18%

profile of v8, /device:TPU:0, one launch (start us, length us, event | category | flops | bytes accessed | tf_op | source)
XLA Modules:
  0.0 315.9 jit_solution(4982345859540309536)
XLA Ops:
  0.8 1.9 copy-done
  2.7 2.2 shard_map.55
  4.8 7.5 %collective-permute-start.1 = (bf16[3,512,256]{2,1,0:T(8,128)(2,1)}, bf16[3,512,256]{2,1,0:T(8,128)(2,1)}, u32[]{:S(2)}, u32[]{:S(2)}) collective-permute-start(bf16[3,512,256]{2,1,0:T(8,128)(2,1)} %get-tuple-element.71), channel_id=1, source_target_pairs={{0,0},{1,1},{2,2},{3,3},{4,8},{5,9},{6,10},{7,11},{8,4},{9,5},{10,... | collective-permute-start | bytes 2359304 | tf_op jit(solution)/shard_map/ppermute | solution.py:385
  12.3 3.0 collective-permute-start.6
  22.3 2.1 collective-permute-start
  24.4 15.1 %collective-permute-done.other_kind_ref.kind_ref = s32[640,1]{1,0:T(8,128)S(1)} collective-permute-done((s32[640,1]{1,0:T(8,128)S(1)}, s32[640,1]{1,0:T(8,128)S(1)}, u32[]{:S(2)}, u32[]{:S(2)}) %collective-permute-start) | collective-permute-done | bytes 2592 | tf_op jit(solution)/shard_map/ppermute | solution.py:385
  40.5 2.4 collective-permute-start.20
  43.7 7.4 %collective-permute-done.3.refs_2_ = bf16[320,2048]{1,0:T(8,128)(2,1)} collective-permute-done((bf16[320,2048]{1,0:T(8,128)(2,1)}, bf16[320,2048]{1,0:T(8,128)(2,1)}, u32[]{:S(2)}, u32[]{:S(2)}) %collective-permute-start.3) | collective-permute-done | bytes 1310752 | tf_op jit(solution)/shard_map/ppermute | solution.py:385
  51.1 7.8 %collective-permute-done.7.a_ref = bf16[3,512,256]{2,1,0:T(8,128)(2,1)S(1)} collective-permute-done((bf16[3,512,256]{2,1,0:T(8,128)(2,1)}, bf16[3,512,256]{2,1,0:T(8,128)(2,1)S(1)}, u32[]{:S(2)}, u32[]{:S(2)}) %collective-permute-start.7) | collective-permute-done | bytes 786464 | tf_op jit(solution)/shard_map/ppermute | solution.py:385
  59.6 7.7 %collective-permute-start.8 = (bf16[160,2048]{1,0:T(8,128)(2,1)}, bf16[160,2048]{1,0:T(8,128)(2,1)S(1)}, u32[]{:S(2)}, u32[]{:S(2)}) collective-permute-start(bf16[160,2048]{1,0:T(8,128)(2,1)} %copy-done.9), channel_id=1, source_target_pairs={{0,4},{1,5},{2,6},{3,7},{4,0},{5,1},{6,2},{7,3},{8,12},{9,13},{10,... | collective-permute-start | bytes 1966088 | tf_op jit(solution)/shard_map/ppermute | solution.py:385
  69.6 10.5 %collective-permute-done.8.refs_2_ = bf16[160,2048]{1,0:T(8,128)(2,1)S(1)} collective-permute-done((bf16[160,2048]{1,0:T(8,128)(2,1)}, bf16[160,2048]{1,0:T(8,128)(2,1)S(1)}, u32[]{:S(2)}, u32[]{:S(2)}) %collective-permute-start.8) | collective-permute-done | bytes 655392 | tf_op jit(solution)/shard_map/ppermute | solution.py:385
  80.1 3.1 collective-permute-start.14
  83.9 4.0 %shard_map.57.refs_0_ = bf16[2,8,640,512]{3,2,1,0:T(8,128)(2,1)S(1)} custom-call(s32[3]{0:T(128)S(1)} %pad_add_fusion.h_ref._, f32[8,1,512]{2,1,0:T(1,128)S(1)} %bitcast.9, bf16[640,2048]{1,0:T(8,128)(2,1)S(1)} %copy-done.3, bf16[320,2048]{1,0:T(8,128)(2,1)} %collective-permute-done.3.refs_2_, bf16[320,2048]{1,0:T(8,128)(2,1)S(1)} %collective-permute-done.4.refs_3_), custom_call_target="tpu_custom_call" | custom-call | tf_op jit(solution)/shard_map/pallas_call | solution.py:32
  91.0 4.3 %collective-permute-done.14.refs_2_ = bf16[160,2048]{1,0:T(8,128)(2,1)S(1)} collective-permute-done((bf16[160,2048]{1,0:T(8,128)(2,1)S(1)}, bf16[160,2048]{1,0:T(8,128)(2,1)S(1)}, u32[]{:S(2)}, u32[]{:S(2)}) %collective-permute-start.14) | collective-permute-done | bytes 655392 | tf_op jit(solution)/shard_map/ppermute | solution.py:385
  98.0 4.6 %collective-permute-start.25 = (bf16[1,256,1024]{2,1,0:T(8,128)(2,1)S(1)}, bf16[1,256,1024]{2,1,0:T(8,128)(2,1)S(1)}, u32[]{:S(2)}, u32[]{:S(2)}) collective-permute-start(bf16[1,256,1024]{2,1,0:T(8,128)(2,1)S(1)} %get-tuple-element.121), channel_id=1, source_target_pairs={{0,4},{1,5},{2,6},{3,7},{12,8},{13,9},{14,10},{15,11},{16,20},{17,... | collective-permute-start | bytes 1572872 | tf_op jit(solution)/shard_map/ppermute | solution.py:385
  104.3 4.8 %shard_map.64.refs_7_ = f32[2,640,768]{2,1,0:T(8,128)S(1)} custom-call(s32[3]{0:T(128)S(1)} %pad_add_fusion.h_ref._, bf16[2,8,640,512]{3,2,1,0:T(8,128)(2,1)S(1)} %shard_map.57.refs_0_, bf16[3,512,256]{2,1,0:T(8,128)(2,1)} %get-tuple-element.74.refs_1_, bf16[3,512,256]{2,1,0:T(8,128)(2,1)} %collective-permute-done.6.refs_2_, ...), custom_call_target="tpu_custom_call" | custom-call | tf_op jit(solution)/shard_map/pallas_call | solution.py:32
  114.7 5.1 %collective-permute-start.26 = (bf16[3,512,256]{2,1,0:T(8,128)(2,1)S(1)}, bf16[3,512,256]{2,1,0:T(8,128)(2,1)S(1)}, u32[]{:S(2)}, u32[]{:S(2)}) collective-permute-start(bf16[3,512,256]{2,1,0:T(8,128)(2,1)S(1)} %collective-permute-done.15), channel_id=1, source_target_pairs={{0,4},{1,5},{2,6},{3,7},{4,0},{5,1},{6,2},{7,3},{8,12},{9,13},{10,... | collective-permute-start | bytes 2359304 | tf_op jit(solution)/shard_map/ppermute | solution.py:385
  120.5 1.8 shard_map.59.refs_0_
  122.9 2.4 collective-permute-done.23.refs_7_.refs_13_
  127.3 5.5 %collective-permute-done.26.a_ref = bf16[3,512,256]{2,1,0:T(8,128)(2,1)S(1)} collective-permute-done((bf16[3,512,256]{2,1,0:T(8,128)(2,1)S(1)}, bf16[3,512,256]{2,1,0:T(8,128)(2,1)S(1)}, u32[]{:S(2)}, u32[]{:S(2)}) %collective-permute-start.26) | collective-permute-done | bytes 786464 | tf_op jit(solution)/shard_map/ppermute | solution.py:385
  133.5 7.1 %collective-permute-start.31 = (bf16[3,512,256]{2,1,0:T(8,128)(2,1)S(1)}, bf16[3,512,256]{2,1,0:T(8,128)(2,1)S(1)}, u32[]{:S(2)}, u32[]{:S(2)}) collective-permute-start(bf16[3,512,256]{2,1,0:T(8,128)(2,1)S(1)} %get-tuple-element.109), channel_id=1, source_target_pairs={{0,4},{1,5},{2,6},{3,7},{4,0},{5,1},{6,2},{7,3},{8,12},{9,13},{10,... | collective-permute-start | bytes 2359304 | tf_op jit(solution)/shard_map/ppermute | solution.py:385
  140.6 1.8 shard_map.60.refs_0_
  142.4 4.8 %shard_map.65.refs_3_ = f32[2,640,768]{2,1,0:T(8,128)S(1)} custom-call(s32[3]{0:T(128)S(1)} %pad_add_fusion.h_ref._, bf16[2,8,640,512]{3,2,1,0:T(8,128)(2,1)S(1)} %shard_map.60.refs_0_, bf16[3,512,256]{2,1,0:T(8,128)(2,1)} %get-tuple-element.74.refs_1_, bf16[3,512,256]{2,1,0:T(8,128)(2,1)} %collective-permute-done.6.refs_2_, ...), custom_call_target="tpu_custom_call", output_to_operand_aliasing={{}: (8, {})} | custom-call | tf_op jit(solution)/shard_map/pallas_call | solution.py:32
  154.9 10.7 %collective-permute-done.38.refs_4_ = bf16[3,512,256]{2,1,0:T(8,128)(2,1)S(1)} collective-permute-done((bf16[3,512,256]{2,1,0:T(8,128)(2,1)S(1)}, bf16[3,512,256]{2,1,0:T(8,128)(2,1)S(1)}, u32[]{:S(2)}, u32[]{:S(2)}) %collective-permute-start.38) | collective-permute-done | bytes 786464 | tf_op jit(solution)/shard_map/ppermute | solution.py:385
  169.8 12.5 %collective-permute-done.39.refs_2_ = bf16[3,512,256]{2,1,0:T(8,128)(2,1)S(1)} collective-permute-done((bf16[3,512,256]{2,1,0:T(8,128)(2,1)S(1)}, bf16[3,512,256]{2,1,0:T(8,128)(2,1)S(1)}, u32[]{:S(2)}, u32[]{:S(2)}) %collective-permute-start.39) | collective-permute-done | bytes 786464 | tf_op jit(solution)/shard_map/ppermute | solution.py:385
  182.3 2.5 collective-permute-start.40
  184.8 2.7 shard_map.72.refs_5_
  187.5 2.7 shard_map.73.refs_3_
  190.3 4.1 %shard_map.68.refs_0_ = bf16[640,256]{1,0:T(8,128)(2,1)S(1)} custom-call(s32[3]{0:T(128)S(1)} %pad_add_fusion.h_ref._, s32[640,1]{1,0:T(8,128)S(1)} %copy.15.own_kind_ref.kind_ref, s32[640,1]{1,0:T(8,128)S(1)} %collective-permute-done.other_kind_ref.kind_ref, bf16[640,768]{1,0:T(8,128)(2,1)S(1)} %shard_map.66.own_ref, ...), custom_call_target="tpu_custom_call" | custom-call | tf_op jit(solution)/shard_map/pallas_call | solution.py:32
  194.4 1.9 shard_map.74.refs_3_
  196.3 1.9 shard_map.75.refs_3_
  201.4 4.6 %collective-permute-start.50 = (bf16[1,256,1024]{2,1,0:T(8,128)(2,1)S(1)}, bf16[1,256,1024]{2,1,0:T(8,128)(2,1)S(1)}, u32[]{:S(2)}, u32[]{:S(2)}) collective-permute-start(bf16[1,256,1024]{2,1,0:T(8,128)(2,1)S(1)} %get-tuple-element.127), channel_id=1, source_target_pairs={{0,4},{1,5},{2,6},{3,7},{12,8},{13,9},{14,10},{15,11},{16,20},{17,... | collective-permute-start | bytes 1572872 | tf_op jit(solution)/shard_map/ppermute | solution.py:385
  206.7 9.6 %collective-permute-done.34.a_ref = bf16[1,256,1024]{2,1,0:T(8,128)(2,1)S(1)} collective-permute-done((bf16[1,256,1024]{2,1,0:T(8,128)(2,1)S(1)}, bf16[1,256,1024]{2,1,0:T(8,128)(2,1)S(1)}, u32[]{:S(2)}, u32[]{:S(2)}) %collective-permute-start.34) | collective-permute-done | bytes 524320 | tf_op jit(solution)/shard_map/ppermute | solution.py:385
  218.0 4.1 %shard_map.78.refs_0_ = bf16[640,256]{1,0:T(8,128)(2,1)S(1)} custom-call(s32[3]{0:T(128)S(1)} %pad_add_fusion.h_ref._, s32[640,1]{1,0:T(8,128)S(1)} %copy.15.own_kind_ref.kind_ref, s32[640,1]{1,0:T(8,128)S(1)} %collective-permute-done.other_kind_ref.kind_ref, bf16[640,768]{1,0:T(8,128)(2,1)S(1)} %shard_map.76.own_ref, ...), custom_call_target="tpu_custom_call" | custom-call | tf_op jit(solution)/shard_map/pallas_call | solution.py:32
  222.1 3.4 %collective-permute-done.35.refs_2_ = bf16[640,256]{1,0:T(8,128)(2,1)S(1)} collective-permute-done((bf16[640,256]{1,0:T(8,128)(2,1)S(1)}, bf16[640,256]{1,0:T(8,128)(2,1)S(1)}, u32[]{:S(2)}, u32[]{:S(2)}) %collective-permute-start.35) | collective-permute-done | bytes 327712 | tf_op jit(solution)/shard_map/ppermute | solution.py:385
  231.2 3.0 collective-permute-done.43.refs_2_
  235.7 1.9 collective-permute-done.30.refs_1_
  239.5 5.1 %collective-permute-done.36.refs_3_ = bf16[640,256]{1,0:T(8,128)(2,1)S(1)} collective-permute-done((bf16[640,256]{1,0:T(8,128)(2,1)S(1)}, bf16[640,256]{1,0:T(8,128)(2,1)S(1)}, u32[]{:S(2)}, u32[]{:S(2)}) %collective-permute-start.36) | collective-permute-done | bytes 327712 | tf_op jit(solution)/shard_map/ppermute | solution.py:385
  245.3 6.3 %collective-permute-done.42.refs_1_ = bf16[640,256]{1,0:T(8,128)(2,1)S(1)} collective-permute-done((bf16[640,256]{1,0:T(8,128)(2,1)S(1)}, bf16[640,256]{1,0:T(8,128)(2,1)S(1)}, u32[]{:S(2)}, u32[]{:S(2)}) %collective-permute-start.42) | collective-permute-done | bytes 327712 | tf_op jit(solution)/shard_map/ppermute | solution.py:385
  252.3 4.4 %collective-permute-done.44.refs_3_ = bf16[640,256]{1,0:T(8,128)(2,1)S(1)} collective-permute-done((bf16[640,256]{1,0:T(8,128)(2,1)S(1)}, bf16[640,256]{1,0:T(8,128)(2,1)S(1)}, u32[]{:S(2)}, u32[]{:S(2)}) %collective-permute-start.44) | collective-permute-done | bytes 327712 | tf_op jit(solution)/shard_map/ppermute | solution.py:385
  262.0 12.6 %collective-permute-done.49.a_ref = bf16[1,256,1024]{2,1,0:T(8,128)(2,1)S(1)} collective-permute-done((bf16[1,256,1024]{2,1,0:T(8,128)(2,1)S(1)}, bf16[1,256,1024]{2,1,0:T(8,128)(2,1)S(1)}, u32[]{:S(2)}, u32[]{:S(2)}) %collective-permute-start.49) | collective-permute-done | bytes 524320 | tf_op jit(solution)/shard_map/ppermute | solution.py:385
  275.4 2.8 shard_map.83.refs_20_
  278.1 10.2 %collective-permute-done.55.refs_11_.refs_19_ = bf16[1,256,1024]{2,1,0:T(8,128)(2,1)S(1)} collective-permute-done((bf16[1,256,1024]{2,1,0:T(8,128)(2,1)S(1)}, bf16[1,256,1024]{2,1,0:T(8,128)(2,1)S(1)}, u32[]{:S(2)}, u32[]{:S(2)}) %collective-permute-start.55) | collective-permute-done | bytes 524320 | tf_op jit(solution)/shard_map/ppermute | solution.py:385
  288.3 2.5 shard_map.85
  290.9 2.4 shard_map.84.a_ref
  296.2 15.2 %collective-permute-done.58.c_ref = bf16[320,1024]{1,0:T(8,128)(2,1)S(1)} collective-permute-done((bf16[320,1024]{1,0:T(8,128)(2,1)S(1)}, bf16[320,1024]{1,0:T(8,128)(2,1)S(1)}, u32[]{:S(2)}, u32[]{:S(2)}) %collective-permute-start.58) | collective-permute-done | bytes 655392 | tf_op jit(solution)/shard_map/ppermute | solution.py:385
  311.4 2.1 collective-permute-done.59.d_ref
  313.5 2.3 shard_map.87
  (128 shorter events, 66.6 us)
Async XLA Ops:
  4.8 34.6 %collective-permute-start.1 = (bf16[3,512,256]{2,1,0:T(8,128)(2,1)}, bf16[3,512,256]{2,1,0:T(8,128)(2,1)}, u32[]{:S(2)}, u32[]{:S(2)}) collective-permute-start(bf16[3,512,256]{2,1,0:T(8,128)(2,1)} %get-tuple-element.71), channel_id=1, source_target_pairs={{0,0},{1,1},{2,2},{3,3},{4,8},{5,9},{6,10},{7,11},{8,4},{9,5},{10,... | collective-permute-start | bytes 2359304 | tf_op jit(solution)/shard_map/ppermute | solution.py:385
  12.3 27.1 %collective-permute-start.5 = (bf16[3,512,256]{2,1,0:T(8,128)(2,1)}, bf16[3,512,256]{2,1,0:T(8,128)(2,1)}, u32[]{:S(2)}, u32[]{:S(2)}) collective-permute-start(bf16[3,512,256]{2,1,0:T(8,128)(2,1)} %get-tuple-element.78), channel_id=1, source_target_pairs={{0,4},{1,5},{2,6},{3,7},{4,0},{5,1},{6,2},{7,3},{8,12},{9,13},{10,... | collective-permute-start | bytes 2359304 | tf_op jit(solution)/shard_map/ppermute | solution.py:385
  12.3 27.1 %collective-permute-start.6 = (bf16[3,512,256]{2,1,0:T(8,128)(2,1)}, bf16[3,512,256]{2,1,0:T(8,128)(2,1)}, u32[]{:S(2)}, u32[]{:S(2)}) collective-permute-start(bf16[3,512,256]{2,1,0:T(8,128)(2,1)} %get-tuple-element.74.refs_1_), channel_id=1, source_target_pairs={{0,2},{1,3},{2,0},{3,1},{4,6},{5,7},{6,4},{7,5},{8,10},{9,11},{10,... | collective-permute-start | bytes 2359304 | tf_op jit(solution)/shard_map/ppermute | solution.py:385
  20.6 30.6 %collective-permute-start.3 = (bf16[320,2048]{1,0:T(8,128)(2,1)}, bf16[320,2048]{1,0:T(8,128)(2,1)}, u32[]{:S(2)}, u32[]{:S(2)}) collective-permute-start(bf16[320,2048]{1,0:T(8,128)(2,1)} %get-tuple-element.76), channel_id=1, source_target_pairs={{0,1},{1,0},{2,3},{3,2},{4,5},{5,4},{6,7},{7,6},{8,9},{9,8},{10,11... | collective-permute-start | bytes 3932168 | tf_op jit(solution)/shard_map/ppermute | solution.py:385
  22.3 17.2 %collective-permute-start = (s32[640,1]{1,0:T(8,128)S(1)}, s32[640,1]{1,0:T(8,128)S(1)}, u32[]{:S(2)}, u32[]{:S(2)}) collective-permute-start(s32[640,1]{1,0:T(8,128)S(1)} %copy.15.own_kind_ref.kind_ref), channel_id=1, source_target_pairs={{0,4},{1,5},{2,6},{3,7},{4,0},{5,1},{6,2},{7,3},{8,12},{9,13},{10,... | collective-permute-start | bytes 7688 | tf_op jit(solution)/shard_map/ppermute | solution.py:385
  39.4 19.5 %collective-permute-start.7 = (bf16[3,512,256]{2,1,0:T(8,128)(2,1)}, bf16[3,512,256]{2,1,0:T(8,128)(2,1)S(1)}, u32[]{:S(2)}, u32[]{:S(2)}) collective-permute-start(bf16[3,512,256]{2,1,0:T(8,128)(2,1)} %collective-permute-done.1), channel_id=1, source_target_pairs={{0,4},{1,5},{2,6},{3,7},{4,0},{5,1},{6,2},{7,3},{8,12},{9,13},{10,... | collective-permute-start | bytes 2359304 | tf_op jit(solution)/shard_map/ppermute | solution.py:385
  39.8 19.1 %collective-permute-start.2 = (bf16[3,512,256]{2,1,0:T(8,128)(2,1)}, bf16[3,512,256]{2,1,0:T(8,128)(2,1)S(1)}, u32[]{:S(2)}, u32[]{:S(2)}) collective-permute-start(bf16[3,512,256]{2,1,0:T(8,128)(2,1)} %copy-done.6), channel_id=1, source_target_pairs={{4,8},{5,9},{6,10},{7,11},{8,4},{9,5},{10,6},{11,7},{20,24},{21,25... | collective-permute-start | bytes 2359304 | tf_op jit(solution)/shard_map/ppermute | solution.py:385
  40.5 27.5 %collective-permute-start.20 = (bf16[3,512,256]{2,1,0:T(8,128)(2,1)}, bf16[3,512,256]{2,1,0:T(8,128)(2,1)S(1)}, u32[]{:S(2)}, u32[]{:S(2)}) collective-permute-start(bf16[3,512,256]{2,1,0:T(8,128)(2,1)} %collective-permute-done.5.refs_3_), channel_id=1, source_target_pairs={{0,2},{1,3},{2,0},{3,1},{4,6},{5,7},{6,4},{7,5},{8,10},{9,11},{10,... | collective-permute-start | bytes 2359304 | tf_op jit(solution)/shard_map/ppermute | solution.py:385
  51.1 32.7 %collective-permute-start.4 = (bf16[320,2048]{1,0:T(8,128)(2,1)}, bf16[320,2048]{1,0:T(8,128)(2,1)S(1)}, u32[]{:S(2)}, u32[]{:S(2)}) collective-permute-start(bf16[320,2048]{1,0:T(8,128)(2,1)} %collective-permute-done.3.refs_2_), channel_id=1, source_target_pairs={{0,16},{1,17},{2,18},{3,19},{4,20},{5,21},{6,22},{7,23},{8,24},{9,... | collective-permute-start | bytes 3932168 | tf_op jit(solution)/shard_map/ppermute | solution.py:385
  58.9 21.1 %collective-permute-start.9 = (bf16[3,512,256]{2,1,0:T(8,128)(2,1)S(1)}, bf16[3,512,256]{2,1,0:T(8,128)(2,1)S(1)}, u32[]{:S(2)}, u32[]{:S(2)}) collective-permute-start(bf16[3,512,256]{2,1,0:T(8,128)(2,1)S(1)} %collective-permute-done.7.a_ref), channel_id=1, source_target_pairs={{4,8},{5,9},{6,10},{7,11},{8,4},{9,5},{10,6},{11,7},{20,24},{21,25... | collective-permute-start | bytes 2359304 | tf_op jit(solution)/shard_map/ppermute | solution.py:385
  59.6 20.4 %collective-permute-start.8 = (bf16[160,2048]{1,0:T(8,128)(2,1)}, bf16[160,2048]{1,0:T(8,128)(2,1)S(1)}, u32[]{:S(2)}, u32[]{:S(2)}) collective-permute-start(bf16[160,2048]{1,0:T(8,128)(2,1)} %copy-done.9), channel_id=1, source_target_pairs={{0,4},{1,5},{2,6},{3,7},{4,0},{5,1},{6,2},{7,3},{8,12},{9,13},{10,... | collective-permute-start | bytes 1966088 | tf_op jit(solution)/shard_map/ppermute | solution.py:385
  68.0 19.9 %collective-permute-start.21 = (bf16[3,512,256]{2,1,0:T(8,128)(2,1)S(1)}, bf16[3,512,256]{2,1,0:T(8,128)(2,1)S(1)}, u32[]{:S(2)}, u32[]{:S(2)}) collective-permute-start(bf16[3,512,256]{2,1,0:T(8,128)(2,1)S(1)} %shard_map.63.refs_5_), channel_id=1, source_target_pairs={{0,2},{1,3},{2,0},{3,1},{4,6},{5,7},{6,4},{7,5},{8,10},{9,11},{10,... | collective-permute-start | bytes 2359304 | tf_op jit(solution)/shard_map/ppermute | solution.py:385
  80.1 15.2 %collective-permute-start.14 = (bf16[160,2048]{1,0:T(8,128)(2,1)S(1)}, bf16[160,2048]{1,0:T(8,128)(2,1)S(1)}, u32[]{:S(2)}, u32[]{:S(2)}) collective-permute-start(bf16[160,2048]{1,0:T(8,128)(2,1)S(1)} %copy-done.8), channel_id=1, source_target_pairs={{0,4},{1,5},{2,6},{3,7},{4,0},{5,1},{6,2},{7,3},{8,12},{9,13},{10,... | collective-permute-start | bytes 1966088 | tf_op jit(solution)/shard_map/ppermute | solution.py:385
  83.1 19.5 %collective-permute-start.10 = (bf16[3,512,256]{2,1,0:T(8,128)(2,1)}, bf16[3,512,256]{2,1,0:T(8,128)(2,1)S(1)}, u32[]{:S(2)}, u32[]{:S(2)}) collective-permute-start(bf16[3,512,256]{2,1,0:T(8,128)(2,1)} %collective-permute-done.5.refs_3_), channel_id=1, source_target_pairs={{4,8},{5,9},{6,10},{7,11},{8,4},{9,5},{10,6},{11,7},{20,24},{21,25... | collective-permute-start | bytes 2359304 | tf_op jit(solution)/shard_map/ppermute | solution.py:385
  87.9 16.5 %collective-permute-start.22 = (bf16[3,512,256]{2,1,0:T(8,128)(2,1)S(1)}, bf16[3,512,256]{2,1,0:T(8,128)(2,1)S(1)}, u32[]{:S(2)}, u32[]{:S(2)}) collective-permute-start(bf16[3,512,256]{2,1,0:T(8,128)(2,1)S(1)} %get-tuple-element.96.refs_1_), channel_id=1, source_target_pairs={{0,2},{1,3},{2,0},{3,1},{4,6},{5,7},{6,4},{7,5},{8,10},{9,11},{10,... | collective-permute-start | bytes 2359304 | tf_op jit(solution)/shard_map/ppermute | solution.py:385
  89.5 13.9 %collective-permute-start.11 = (bf16[160,2048]{1,0:T(8,128)(2,1)S(1)}, bf16[160,2048]{1,0:T(8,128)(2,1)S(1)}, u32[]{:S(2)}, u32[]{:S(2)}) collective-permute-start(bf16[160,2048]{1,0:T(8,128)(2,1)S(1)} %collective-permute-done.8.refs_2_), channel_id=1, source_target_pairs={{0,1},{1,0},{2,3},{3,2},{4,5},{5,4},{6,7},{7,6},{8,9},{9,8},{10,11... | collective-permute-start | bytes 1966088 | tf_op jit(solution)/shard_map/ppermute | solution.py:385
  95.3 17.9 %collective-permute-start.19 = (bf16[3,512,256]{2,1,0:T(8,128)(2,1)S(1)}, bf16[3,512,256]{2,1,0:T(8,128)(2,1)S(1)}, u32[]{:S(2)}, u32[]{:S(2)}) collective-permute-start(bf16[3,512,256]{2,1,0:T(8,128)(2,1)S(1)} %collective-permute-done.9), channel_id=1, source_target_pairs={{4,0},{5,1},{6,2},{7,3},{8,12},{9,13},{10,14},{11,15},{20,16},{21,... | collective-permute-start | bytes 2359304 | tf_op jit(solution)/shard_map/ppermute | solution.py:385
  103.4 16.4 %collective-permute-start.12 = (bf16[160,2048]{1,0:T(8,128)(2,1)S(1)}, bf16[160,2048]{1,0:T(8,128)(2,1)S(1)}, u32[]{:S(2)}, u32[]{:S(2)}) collective-permute-start(bf16[160,2048]{1,0:T(8,128)(2,1)S(1)} %collective-permute-done.8.refs_2_), channel_id=1, source_target_pairs={{0,16},{1,17},{2,18},{3,19},{4,20},{5,21},{6,22},{7,23},{8,24},{9,... | collective-permute-start | bytes 1966088 | tf_op jit(solution)/shard_map/ppermute | solution.py:385
  104.3 16.1 %collective-permute-start.13 = (bf16[160,2048]{1,0:T(8,128)(2,1)S(1)}, bf16[160,2048]{1,0:T(8,128)(2,1)S(1)}, u32[]{:S(2)}, u32[]{:S(2)}) collective-permute-start(bf16[160,2048]{1,0:T(8,128)(2,1)S(1)} %collective-permute-done.11.refs_3_), channel_id=1, source_target_pairs={{0,16},{1,17},{2,18},{3,19},{4,20},{5,21},{6,22},{7,23},{8,24},{9,... | collective-permute-start | bytes 1966088 | tf_op jit(solution)/shard_map/ppermute | solution.py:385
  110.3 16.5 %collective-permute-start.16 = (bf16[160,2048]{1,0:T(8,128)(2,1)S(1)}, bf16[160,2048]{1,0:T(8,128)(2,1)S(1)}, u32[]{:S(2)}, u32[]{:S(2)}) collective-permute-start(bf16[160,2048]{1,0:T(8,128)(2,1)S(1)} %collective-permute-done.14.refs_2_), channel_id=1, source_target_pairs={{0,1},{1,0},{2,3},{3,2},{4,5},{5,4},{6,7},{7,6},{8,9},{9,8},{10,11... | collective-permute-start | bytes 1966088 | tf_op jit(solution)/shard_map/ppermute | solution.py:385
  114.7 18.1 %collective-permute-start.26 = (bf16[3,512,256]{2,1,0:T(8,128)(2,1)S(1)}, bf16[3,512,256]{2,1,0:T(8,128)(2,1)S(1)}, u32[]{:S(2)}, u32[]{:S(2)}) collective-permute-start(bf16[3,512,256]{2,1,0:T(8,128)(2,1)S(1)} %collective-permute-done.15), channel_id=1, source_target_pairs={{0,4},{1,5},{2,6},{3,7},{4,0},{5,1},{6,2},{7,3},{8,12},{9,13},{10,... | collective-permute-start | bytes 2359304 | tf_op jit(solution)/shard_map/ppermute | solution.py:385
  125.3 22.6 %collective-permute-start.24 = (bf16[3,512,256]{2,1,0:T(8,128)(2,1)S(1)}, bf16[3,512,256]{2,1,0:T(8,128)(2,1)S(1)}, u32[]{:S(2)}, u32[]{:S(2)}) collective-permute-start(bf16[3,512,256]{2,1,0:T(8,128)(2,1)S(1)} %shard_map.61.refs_1_), channel_id=1, source_target_pairs={{0,2},{1,3},{2,0},{3,1},{4,6},{5,7},{6,4},{7,5},{8,10},{9,11},{10,... | collective-permute-start | bytes 2359304 | tf_op jit(solution)/shard_map/ppermute | solution.py:385
  126.8 13.8 %collective-permute-start.17 = (bf16[160,2048]{1,0:T(8,128)(2,1)S(1)}, bf16[160,2048]{1,0:T(8,128)(2,1)S(1)}, u32[]{:S(2)}, u32[]{:S(2)}) collective-permute-start(bf16[160,2048]{1,0:T(8,128)(2,1)S(1)} %collective-permute-done.14.refs_2_), channel_id=1, source_target_pairs={{0,16},{1,17},{2,18},{3,19},{4,20},{5,21},{6,22},{7,23},{8,24},{9,... | collective-permute-start | bytes 1966088 | tf_op jit(solution)/shard_map/ppermute | solution.py:385
  126.8 13.8 %collective-permute-start.18 = (bf16[160,2048]{1,0:T(8,128)(2,1)S(1)}, bf16[160,2048]{1,0:T(8,128)(2,1)S(1)}, u32[]{:S(2)}, u32[]{:S(2)}) collective-permute-start(bf16[160,2048]{1,0:T(8,128)(2,1)S(1)} %collective-permute-done.16.refs_3_), channel_id=1, source_target_pairs={{0,16},{1,17},{2,18},{3,19},{4,20},{5,21},{6,22},{7,23},{8,24},{9,... | collective-permute-start | bytes 1966088 | tf_op jit(solution)/shard_map/ppermute | solution.py:385
  132.8 18.4 %collective-permute-start.28 = (bf16[3,512,256]{2,1,0:T(8,128)(2,1)S(1)}, bf16[3,512,256]{2,1,0:T(8,128)(2,1)S(1)}, u32[]{:S(2)}, u32[]{:S(2)}) collective-permute-start(bf16[3,512,256]{2,1,0:T(8,128)(2,1)S(1)} %collective-permute-done.26.a_ref), channel_id=1, source_target_pairs={{4,8},{5,9},{6,10},{7,11},{8,4},{9,5},{10,6},{11,7},{20,24},{21,25... | collective-permute-start | bytes 2359304 | tf_op jit(solution)/shard_map/ppermute | solution.py:385
  133.5 19.4 %collective-permute-start.31 = (bf16[3,512,256]{2,1,0:T(8,128)(2,1)S(1)}, bf16[3,512,256]{2,1,0:T(8,128)(2,1)S(1)}, u32[]{:S(2)}, u32[]{:S(2)}) collective-permute-start(bf16[3,512,256]{2,1,0:T(8,128)(2,1)S(1)} %get-tuple-element.109), channel_id=1, source_target_pairs={{0,4},{1,5},{2,6},{3,7},{4,0},{5,1},{6,2},{7,3},{8,12},{9,13},{10,... | collective-permute-start | bytes 2359304 | tf_op jit(solution)/shard_map/ppermute | solution.py:385
  147.9 17.8 %collective-permute-start.38 = (bf16[3,512,256]{2,1,0:T(8,128)(2,1)S(1)}, bf16[3,512,256]{2,1,0:T(8,128)(2,1)S(1)}, u32[]{:S(2)}, u32[]{:S(2)}) collective-permute-start(bf16[3,512,256]{2,1,0:T(8,128)(2,1)S(1)} %shard_map.71.refs_3_), channel_id=1, source_target_pairs={{0,2},{1,3},{2,0},{3,1},{4,6},{5,7},{6,4},{7,5},{8,10},{9,11},{10,... | collective-permute-start | bytes 2359304 | tf_op jit(solution)/shard_map/ppermute | solution.py:385
  152.9 16.1 %collective-permute-start.32 = (bf16[3,512,256]{2,1,0:T(8,128)(2,1)S(1)}, bf16[3,512,256]{2,1,0:T(8,128)(2,1)S(1)}, u32[]{:S(2)}, u32[]{:S(2)}) collective-permute-start(bf16[3,512,256]{2,1,0:T(8,128)(2,1)S(1)} %collective-permute-done.28), channel_id=1, source_target_pairs={{4,0},{5,1},{6,2},{7,3},{8,12},{9,13},{10,14},{11,15},{20,16},{21,... | collective-permute-start | bytes 2359304 | tf_op jit(solution)/shard_map/ppermute | solution.py:385
  154.2 14.8 %collective-permute-start.33 = (bf16[3,512,256]{2,1,0:T(8,128)(2,1)S(1)}, bf16[3,512,256]{2,1,0:T(8,128)(2,1)S(1)}, u32[]{:S(2)}, u32[]{:S(2)}) collective-permute-start(bf16[3,512,256]{2,1,0:T(8,128)(2,1)S(1)} %collective-permute-done.31.refs_1_), channel_id=1, source_target_pairs={{4,8},{5,9},{6,10},{7,11},{8,4},{9,5},{10,6},{11,7},{20,24},{21,25... | collective-permute-start | bytes 2359304 | tf_op jit(solution)/shard_map/ppermute | solution.py:385
  165.7 16.7 %collective-permute-start.39 = (bf16[3,512,256]{2,1,0:T(8,128)(2,1)S(1)}, bf16[3,512,256]{2,1,0:T(8,128)(2,1)S(1)}, u32[]{:S(2)}, u32[]{:S(2)}) collective-permute-start(bf16[3,512,256]{2,1,0:T(8,128)(2,1)S(1)} %collective-permute-done.31.refs_1_), channel_id=1, source_target_pairs={{0,2},{1,3},{2,0},{3,1},{4,6},{5,7},{6,4},{7,5},{8,10},{9,11},{10,... | collective-permute-start | bytes 2359304 | tf_op jit(solution)/shard_map/ppermute | solution.py:385
  168.9 21.4 %collective-permute-start.29 = (bf16[640,768]{1,0:T(8,128)(2,1)S(1)}, bf16[640,768]{1,0:T(8,128)(2,1)S(1)}, u32[]{:S(2)}, u32[]{:S(2)}) collective-permute-start(bf16[640,768]{1,0:T(8,128)(2,1)S(1)} %shard_map.67), channel_id=1, source_target_pairs={{0,16},{1,17},{2,18},{3,19},{4,20},{5,21},{6,22},{7,23},{8,24},{9,... | collective-permute-start | bytes 2949128 | tf_op jit(solution)/shard_map/ppermute | solution.py:385
  182.3 15.9 %collective-permute-start.40 = (bf16[3,512,256]{2,1,0:T(8,128)(2,1)S(1)}, bf16[3,512,256]{2,1,0:T(8,128)(2,1)S(1)}, u32[]{:S(2)}, u32[]{:S(2)}) collective-permute-start(bf16[3,512,256]{2,1,0:T(8,128)(2,1)S(1)} %shard_map.70.refs_1_), channel_id=1, source_target_pairs={{0,2},{1,3},{2,0},{3,1},{4,6},{5,7},{6,4},{7,5},{8,10},{9,11},{10,... | collective-permute-start | bytes 2359304 | tf_op jit(solution)/shard_map/ppermute | solution.py:385
  200.0 18.0 %collective-permute-start.41 = (bf16[640,768]{1,0:T(8,128)(2,1)S(1)}, bf16[640,768]{1,0:T(8,128)(2,1)S(1)}, u32[]{:S(2)}, u32[]{:S(2)}) collective-permute-start(bf16[640,768]{1,0:T(8,128)(2,1)S(1)} %shard_map.77), channel_id=1, source_target_pairs={{0,16},{1,17},{2,18},{3,19},{4,20},{5,21},{6,22},{7,23},{8,24},{9,... | collective-permute-start | bytes 2949128 | tf_op jit(solution)/shard_map/ppermute | solution.py:385
  200.1 16.2 %collective-permute-start.34 = (bf16[1,256,1024]{2,1,0:T(8,128)(2,1)S(1)}, bf16[1,256,1024]{2,1,0:T(8,128)(2,1)S(1)}, u32[]{:S(2)}, u32[]{:S(2)}) collective-permute-start(bf16[1,256,1024]{2,1,0:T(8,128)(2,1)S(1)} %get-tuple-element.121), channel_id=1, source_target_pairs={{4,0},{5,1},{6,2},{7,3},{8,12},{9,13},{10,14},{11,15},{20,16},{21,... | collective-permute-start | bytes 1572872 | tf_op jit(solution)/shard_map/ppermute | solution.py:385
  201.4 27.7 %collective-permute-start.50 = (bf16[1,256,1024]{2,1,0:T(8,128)(2,1)S(1)}, bf16[1,256,1024]{2,1,0:T(8,128)(2,1)S(1)}, u32[]{:S(2)}, u32[]{:S(2)}) collective-permute-start(bf16[1,256,1024]{2,1,0:T(8,128)(2,1)S(1)} %get-tuple-element.127), channel_id=1, source_target_pairs={{0,4},{1,5},{2,6},{3,7},{12,8},{13,9},{14,10},{15,11},{16,20},{17,... | collective-permute-start | bytes 1572872 | tf_op jit(solution)/shard_map/ppermute | solution.py:385
  206.0 24.5 %collective-permute-start.47 = (bf16[1,256,1024]{2,1,0:T(8,128)(2,1)S(1)}, bf16[1,256,1024]{2,1,0:T(8,128)(2,1)S(1)}, u32[]{:S(2)}, u32[]{:S(2)}) collective-permute-start(bf16[1,256,1024]{2,1,0:T(8,128)(2,1)S(1)} %get-tuple-element.121), channel_id=1, source_target_pairs={{4,8},{5,9},{6,10},{7,11},{8,4},{9,5},{10,6},{11,7},{20,24},{21,25... | collective-permute-start | bytes 1572872 | tf_op jit(solution)/shard_map/ppermute | solution.py:385
  228.5 16.2 %collective-permute-start.36 = (bf16[640,256]{1,0:T(8,128)(2,1)S(1)}, bf16[640,256]{1,0:T(8,128)(2,1)S(1)}, u32[]{:S(2)}, u32[]{:S(2)}) collective-permute-start(bf16[640,256]{1,0:T(8,128)(2,1)S(1)} %collective-permute-done.35.refs_2_), channel_id=1, source_target_pairs={{0,1},{1,0},{2,3},{3,2},{4,5},{5,4},{6,7},{7,6},{8,9},{9,8},{10,11... | collective-permute-start | bytes 983048 | tf_op jit(solution)/shard_map/ppermute | solution.py:385
  229.0 22.7 %collective-permute-start.42 = (bf16[640,256]{1,0:T(8,128)(2,1)S(1)}, bf16[640,256]{1,0:T(8,128)(2,1)S(1)}, u32[]{:S(2)}, u32[]{:S(2)}) collective-permute-start(bf16[640,256]{1,0:T(8,128)(2,1)S(1)} %shard_map.78.refs_0_), channel_id=1, source_target_pairs={{0,1},{1,0},{2,3},{3,2},{4,5},{5,4},{6,7},{7,6},{8,9},{9,8},{10,11... | collective-permute-start | bytes 983048 | tf_op jit(solution)/shard_map/ppermute | solution.py:385
  230.5 26.9 %collective-permute-start.46 = (bf16[1,256,1024]{2,1,0:T(8,128)(2,1)S(1)}, bf16[1,256,1024]{2,1,0:T(8,128)(2,1)S(1)}, u32[]{:S(2)}, u32[]{:S(2)}) collective-permute-start(bf16[1,256,1024]{2,1,0:T(8,128)(2,1)S(1)} %collective-permute-done.25), channel_id=1, source_target_pairs={{4,8},{5,9},{6,10},{7,11},{8,4},{9,5},{10,6},{11,7},{20,24},{21,25... | collective-permute-start | bytes 1572872 | tf_op jit(solution)/shard_map/ppermute | solution.py:385
  234.2 22.5 %collective-permute-start.44 = (bf16[640,256]{1,0:T(8,128)(2,1)S(1)}, bf16[640,256]{1,0:T(8,128)(2,1)S(1)}, u32[]{:S(2)}, u32[]{:S(2)}) collective-permute-start(bf16[640,256]{1,0:T(8,128)(2,1)S(1)} %collective-permute-done.43.refs_2_), channel_id=1, source_target_pairs={{0,1},{1,0},{2,3},{3,2},{4,5},{5,4},{6,7},{7,6},{8,9},{9,8},{10,11... | collective-permute-start | bytes 983048 | tf_op jit(solution)/shard_map/ppermute | solution.py:385
  237.6 20.4 %collective-permute-start.48 = (bf16[1,256,1024]{2,1,0:T(8,128)(2,1)S(1)}, bf16[1,256,1024]{2,1,0:T(8,128)(2,1)S(1)}, u32[]{:S(2)}, u32[]{:S(2)}) collective-permute-start(bf16[1,256,1024]{2,1,0:T(8,128)(2,1)S(1)} %collective-permute-done.47), channel_id=1, source_target_pairs={{4,0},{5,1},{6,2},{7,3},{8,12},{9,13},{10,14},{11,15},{20,16},{21,... | collective-permute-start | bytes 1572872 | tf_op jit(solution)/shard_map/ppermute | solution.py:385
  244.7 14.2 %collective-permute-start.52 = (bf16[1,256,1024]{2,1,0:T(8,128)(2,1)S(1)}, bf16[1,256,1024]{2,1,0:T(8,128)(2,1)S(1)}, u32[]{:S(2)}, u32[]{:S(2)}) collective-permute-start(bf16[1,256,1024]{2,1,0:T(8,128)(2,1)S(1)} %get-tuple-element.127), channel_id=1, source_target_pairs={{4,8},{5,9},{6,10},{7,11},{8,4},{9,5},{10,6},{11,7},{20,24},{21,25... | collective-permute-start | bytes 1572872 | tf_op jit(solution)/shard_map/ppermute | solution.py:385
  256.8 18.6 %collective-permute-start.37 = (bf16[4,640,256]{2,1,0:T(8,128)(2,1)S(1)}, bf16[4,640,256]{2,1,0:T(8,128)(2,1)S(1)}, u32[]{:S(2)}, u32[]{:S(2)}) collective-permute-start(bf16[4,640,256]{2,1,0:T(8,128)(2,1)S(1)} %shard_map.69.refs_0_.refs_2_.refs_4_), channel_id=1, source_target_pairs={{0,16},{1,17},{2,18},{3,19},{4,20},{5,21},{6,22},{7,23},{8,24},{9,... | collective-permute-start | bytes 3932168 | tf_op jit(solution)/shard_map/ppermute | solution.py:385
  257.4 30.9 %collective-permute-start.45 = (bf16[4,640,256]{2,1,0:T(8,128)(2,1)S(1)}, bf16[4,640,256]{2,1,0:T(8,128)(2,1)S(1)}, u32[]{:S(2)}, u32[]{:S(2)}) collective-permute-start(bf16[4,640,256]{2,1,0:T(8,128)(2,1)S(1)} %shard_map.79.refs_2_.refs_4_.refs_6_.refs_8_), channel_id=1, source_target_pairs={{0,16},{1,17},{2,18},{3,19},{4,20},{5,21},{6,22},{7,23},{8,24},{9,... | collective-permute-start | bytes 3932168 | tf_op jit(solution)/shard_map/ppermute | solution.py:385
  258.9 15.8 %collective-permute-start.49 = (bf16[1,256,1024]{2,1,0:T(8,128)(2,1)S(1)}, bf16[1,256,1024]{2,1,0:T(8,128)(2,1)S(1)}, u32[]{:S(2)}, u32[]{:S(2)}) collective-permute-start(bf16[1,256,1024]{2,1,0:T(8,128)(2,1)S(1)} %collective-permute-done.46), channel_id=1, source_target_pairs={{4,0},{5,1},{6,2},{7,3},{8,12},{9,13},{10,14},{11,15},{20,16},{21,... | collective-permute-start | bytes 1572872 | tf_op jit(solution)/shard_map/ppermute | solution.py:385
  261.8 13.5 %collective-permute-start.54 = (bf16[1,256,1024]{2,1,0:T(8,128)(2,1)S(1)}, bf16[1,256,1024]{2,1,0:T(8,128)(2,1)S(1)}, u32[]{:S(2)}, u32[]{:S(2)}) collective-permute-start(bf16[1,256,1024]{2,1,0:T(8,128)(2,1)S(1)} %shard_map.81.refs_10_.refs_16_), channel_id=1, source_target_pairs={{0,2},{1,3},{2,0},{3,1},{4,6},{5,7},{6,4},{7,5},{8,10},{9,11},{10,... | collective-permute-start | bytes 1572872 | tf_op jit(solution)/shard_map/ppermute | solution.py:385
  293.3 18.1 %collective-permute-start.56 = (bf16[640,1024]{1,0:T(8,128)(2,1)S(1)}, bf16[640,1024]{1,0:T(8,128)(2,1)S(1)}, u32[]{:S(2)}, u32[]{:S(2)}) collective-permute-start(bf16[640,1024]{1,0:T(8,128)(2,1)S(1)} %shard_map.84.a_ref), channel_id=1, source_target_pairs={{0,16},{1,17},{2,18},{3,19},{4,20},{5,21},{6,22},{7,23},{8,24},{9,... | collective-permute-start | bytes 3932168 | tf_op jit(solution)/shard_map/ppermute | solution.py:385
  294.7 16.7 %collective-permute-start.58 = (bf16[320,1024]{1,0:T(8,128)(2,1)S(1)}, bf16[320,1024]{1,0:T(8,128)(2,1)S(1)}, u32[]{:S(2)}, u32[]{:S(2)}) collective-permute-start(bf16[320,1024]{1,0:T(8,128)(2,1)S(1)} %shard_map.86), channel_id=1, source_target_pairs={{0,4},{1,5},{2,6},{3,7},{4,0},{5,1},{6,2},{7,3},{8,12},{9,13},{10,... | collective-permute-start | bytes 1966088 | tf_op jit(solution)/shard_map/ppermute | solution.py:385
  (22 other events, 362.7 us)

commit v9 on v7

--- a/solution.py
+++ b/solution.py
@@ -28,7 +28,7 @@
         return {"own": self.which, "partner": 1 - self.which}.get(name, name)
 
 
-def call(kernel, here, args, out_shape, aliases=None, scratch=8):
+def call(name, kernel, here, args, out_shape, aliases=None, scratch=8):
     return pl.pallas_call(
         kernel,
         in_specs=[pl.BlockSpec(memory_space=SMEM)] + [pl.BlockSpec(memory_space=VMEM)] * len(args),
@@ -36,11 +36,16 @@
         out_shape=jax.tree.map(lambda shape: VMEM(shape.shape, shape.dtype), out_shape),
         input_output_aliases=aliases or {},
         compiler_params=pltpu.CompilerParams(vmem_limit_bytes=scratch * 2**20),
+        name=name,
     )(here, *[pltpu.with_memory_space_constraint(a, VMEM) for a in args])
 
 
 def shaped(shape, dtype=BF16):
     return jax.ShapeDtypeStruct(shape, dtype)
+
+
+def by_row(kind):
+    return jnp.broadcast_to(kind.astype(F32), (128, kind.shape[1])).T.astype(I32)
 
 
 def halves(here, weight, chunk, chunks):
@@ -58,7 +63,7 @@
             mine_ref[kind] = jnp.where(outer, low, high)
             away_ref[kind] = jnp.where(outer, high, low)
 
-    return call(kernel, here, [weight], [shaped((kinds, depth, part))] * 4)
+    return call("halves", kernel, here, [weight], [shaped((kinds, depth, part))] * 4)
 
 
 def own_rows_of(here, tokens):
@@ -72,7 +77,7 @@
         bottom_ref[...] = rows[half // 2 :]
 
     part = shaped((half // 2, features))
-    return call(kernel, here, [tokens], [shaped((half, features)), part, part])
+    return call("own_rows_of", kernel, here, [tokens], [shaped((half, features)), part, part])
 
 
 def choose(here, from_edge, from_middle):
@@ -87,7 +92,7 @@
         def _():
             out_ref[...] = b_ref[...]
 
-    return call(kernel, here, [from_edge, from_middle], shaped(from_edge.shape))
+    return call("choose", kernel, here, [from_edge, from_middle], shaped(from_edge.shape))
 
 
 def stack(here, arrays):
@@ -95,7 +100,33 @@
         for i in range(len(arrays)):
             refs[-1][i] = refs[i][...]
 
-    return call(kernel, here, arrays, shaped((len(arrays),) + arrays[0].shape))
+    return call("stack", kernel, here, arrays, shaped((len(arrays),) + arrays[0].shape))
+
+
+def pack(here, block, piece):
+    _, depth, features = block.shape
+    length, width = piece.shape
+    cuts = features // width
+
+    def kernel(_, block_ref, piece_ref, out_ref):
+        for i in range(cuts):
+            out_ref[i * depth : (i + 1) * depth] = block_ref[0, :, i * width : (i + 1) * width]
+        out_ref[cuts * depth :] = piece_ref[...]
+
+    return call("pack", kernel, here, [block, piece], shaped((cuts * depth + length, width)))
+
+
+def unpack(here, packed, block, piece):
+    _, depth, features = block.shape
+    _, width = piece.shape
+    cuts = features // width
+
+    def kernel(_, in_ref, block_ref, piece_ref):
+        for i in range(cuts):
+            block_ref[0, :, i * width : (i + 1) * width] = in_ref[i * depth : (i + 1) * depth]
+        piece_ref[...] = in_ref[cuts * depth :]
+
+    return call("unpack", kernel, here, [packed], [shaped(block.shape), shaped(piece.shape)])
 
 
 def normalize(here, slot, held, gains, whole, mine, theirs, shape, start, count):
@@ -140,7 +171,7 @@
 
         lax.fori_loop(0, count // tile, step, 0)
 
-    return call(kernel, here, args, shaped(shape), None if held is None else {1: 0})
+    return call("normalize", kernel, here, args, shaped(shape), None if held is None else {1: 0})
 
 
 def project(here, slot, normed, blocks, total=None, final=False, fresh=False):
@@ -171,9 +202,9 @@
                 out_ref[into, :, columns] = summed
 
     if final:
-        return call(kernel, here, args, shaped((length, kinds * width)))
+        return call("project", kernel, here, args, shaped((length, kinds * width)))
     aliases = None if total is None else {2 + 2 * count: 0}
-    return call(kernel, here, args, shaped((slots, length, kinds * width), F32), aliases)
+    return call("project", kernel, here, args, shaped((slots, length, kinds * width), F32), aliases)
 
 
 def attend(here, own_kind, other_kind, own, got):
@@ -185,7 +216,7 @@
     def kernel(h_ref, own_kind_ref, other_kind_ref, own_ref, got_ref, out_ref):
         at_place = Here(h_ref)
         kind = jnp.where(at_place.which == 0, own_kind_ref[...], other_kind_ref[...])
-        keep = kind == at_place.core
+        keep = by_row(kind) == at_place.core
 
         def pick(j):
             columns = slice(j * HDIM, (j + 1) * HDIM)
@@ -210,7 +241,7 @@
                 out = jnp.dot(probs, value[:high], preferred_element_type=F32)
                 out_ref[low:high, h * HDIM : (h + 1) * HDIM] = out.astype(BF16)
 
-    return call(kernel, here, [own_kind, other_kind, own, got], shaped((length, width)))
+    return call("attend", kernel, here, [own_kind, other_kind, own, got], shaped((length, width)))
 
 
 def combine(here, slots, groups, total=None, offset=0, cut=False):
@@ -264,7 +295,7 @@
         out_shape = [shaped((half, features))] * 2
     else:
         out_shape = shaped((length, features))
-    return call(kernel, here, args, out_shape)
+    return call("combine", kernel, here, args, out_shape)
 
 
 def join(here, kind, kept, got):
@@ -272,12 +303,13 @@
 
     def kernel(h_ref, kind_ref, a_ref, b_ref, out_ref):
         core = h_ref[0]
-        rows = jnp.where(core == 0, kind_ref[:half], kind_ref[half:])
+        rows = by_row(kind_ref[...])[:, :1]
+        rows = jnp.where(core == 0, rows[:half], rows[half:])
         out_ref[...] = jnp.where(
             rows == core, a_ref[...].astype(F32), b_ref[...].astype(F32)
         ).astype(BF16)
 
-    return call(kernel, here, [kind, kept, got], shaped(kept.shape))
+    return call("join", kernel, here, [kind, kept, got], shaped(kept.shape))
 
 
 def assemble(here, kind, near, near_other, far, far_other):
@@ -291,9 +323,10 @@
         at_place = Here(h_ref)
         core, first = at_place.core, at_place.column == 0
         copies = []
+        kind = by_row(kind_ref[...])[:, :1]
         for i in range(steps):
             rows = slice(i * tile, (i + 1) * tile)
-            keep = kind_ref[rows] == core
+            keep = kind[rows] == core
             own = jnp.where(keep, a_ref[rows].astype(F32), b_ref[rows].astype(F32)).astype(BF16)
             part = slice(i * tile % half, i * tile % half + tile)
             other = jnp.where(core == i * tile // half, c_ref[part], d_ref[part])
@@ -399,6 +432,9 @@
     def outward(m, d, x):
         return (m, d ^ 2, x) if d // 2 in (1, 2) else None
 
+    def inward(m, d, x):
+        return (m, d ^ 2, x) if d // 2 in (0, 3) else None
+
     def across(m, d, x):
         return (m, (3 - d // 2) * 2 + d % 2, x) if d // 2 in (1, 2) else None
 
@@ -414,112 +450,135 @@
         kept = qkv_weight.shape[1]
         half = length // 2
         gains = norm_gains[0].reshape(places, 1, kept)
-        own_kind = modality[:, None]
+        own_kind = modality[None, :]
 
         weight = after(qkv_weight[0].transpose(1, 0, 2), here, gains, own_kind)
         low_a, high_a, mine_a, away_a = halves(here, weight, 0, 2)
         m1a = move(low_a, across_or_stay)
         e1a = move(away_a, edge)
-        rows, top, bottom = own_rows_of(here, after(tokens, mine_a))
-        p1a = move(mine_a, pair, rows)
+        p1a = move(mine_a, pair)
+
+        begun = (m1a,)
+        m2a = move(high_a, across, e1a, p1a, *begun)
+        e2a = move(m1a, edge, e1a, p1a)
+        p2a = move(e1a, pair, p1a, *begun)
+        rows, top, bottom = own_rows_of(here, after(tokens, *begun))
         fetched = over_tensor(rows)
-        other_kind = move(own_kind, edge, rows)
-        low_b, high_b, mine_b, away_b = halves(here, after(weight, rows), 1, 2)
-        low_o, high_o, mine_o, away_o = halves(here, after(out_weight, mine_b), 0, 1)
-
-        m2a = move(high_a, across, m1a, mine_o)
-        e2a = move(m1a, edge, e1a, p1a)
-        p2a = move(e1a, pair, p1a)
-        swapped = [to_core(a) for a in fetched[1:]]
-
-        m3a = move(e2a, across, m2a)
-        passed_top = move(top, edge, e2a, other_kind)
-        third_a = choose(here, e2a, m2a)
+        low_b, high_b, mine_b, away_b = halves(here, after(weight, *begun), 1, 2)
+
+        begun = (m2a, mine_b)
+        m3a = move(e2a, across, p2a, *begun)
+        other_kind = move(own_kind, edge, e2a, p2a, *begun)
+        passed_top = move(top, edge, e2a, p2a, *begun)
+        third_a = choose(here, after(e2a, *begun), m2a)
         p3a = move(third_a, pair, p2a)
+
+        begun = (m3a,)
+        swapped = [to_core(a, *begun) for a in fetched[1:]]
         shape = (2, places, length, kept)
-        normed = normalize(here, "own", None, gains, tokens, fetched[1:], swapped, shape, 0, half)
-
-        m4a = move(e1a, across, m3a)
-        passed_bottom = move(bottom, edge, passed_top)
-        p1b = move(mine_b, pair, p3a, normed)
-        part_top = over_tensor(passed_top)
+        normed = normalize(
+            here, "own", None, gains, after(tokens, *begun), fetched[1:], swapped, shape, 0, half
+        )
+        m4a = move(e1a, across, passed_top, p3a, *begun)
+        passed_bottom = move(bottom, edge, passed_top, p3a, *begun)
+        p1b = move(mine_b, pair, p3a, *begun)
+        part_top = over_tensor(after(passed_top, *begun))
+        low_o, high_o, mine_o, away_o = halves(here, after(out_weight, *begun), 0, 1)
+
+        begun = (m4a, normed, mine_o)
+        m1b = move(low_b, across_or_stay, *begun)
+        e3a = move(m3a, outward, passed_bottom, p1b, part_top[-1], *begun)
+        i1o = move(low_o, inward, passed_bottom, p1b, part_top[-1], *begun)
+        p1o = move(mine_o, pair, p1b, *begun)
+        part_bottom = over_tensor(after(passed_bottom, *begun))
+        top_swapped = [to_core(a, *begun) for a in part_top]
         first_a = [(0, mine_a, p1a), (1, e1a, p2a), (2, third_a, p3a)]
-        total_a = project(here, "own", normed, first_a, fresh=True)
-
-        m1b = move(low_b, across_or_stay, m4a)
-        e3a = move(m3a, outward, passed_bottom)
-        p1o = move(mine_o, pair, p1b, total_a)
-        part_bottom = over_tensor(passed_bottom)
-        top_swapped = [to_core(a) for a in part_top]
+        total_a = project(here, "own", after(normed, *begun), first_a, fresh=True)
         normed = normalize(
             here, "partner", normed, gains, None, part_top, top_swapped, shape, 0, half // 2
         )
 
-        m2b = move(high_b, across, m1b)
-        e2b = move(m1b, edge, e3a)
-        fourth_a = choose(here, e3a, m4a)
-        p4a = move(fourth_a, pair, p1o, normed)
-        bottom_swapped = [to_core(a) for a in part_bottom]
+        begun = (m1b, normed, total_a)
+        m2b = move(high_b, across, *begun)
+        e2b = move(m1b, edge, e3a, i1o, p1o, part_bottom[-1], *begun)
+        fourth_a = choose(here, after(e3a, *begun), m4a)
+        p4a = move(fourth_a, pair, p1o)
+        bottom_swapped = [to_core(a, *begun) for a in part_bottom]
         normed = normalize(
             here, "partner", normed, gains, None, part_bottom, bottom_swapped, shape, half // 2, half // 2
         )
         total_a = project(here, "partner", normed, first_a, total_a, fresh=True)
 
-        m3b = move(e2b, across, m2b)
-        e1b = move(away_b, edge, e2b)
-        third_b = choose(here, e2b, m2b)
-        p3b = move(third_b, pair, p4a, total_a)
+        begun = (m2b, total_a)
+        m3b = move(e2b, across, *begun)
+        e1b = move(away_b, edge, e2b, p4a, *begun)
+        third_b = choose(here, after(e2b, *begun), m2b)
+        p3b = move(third_b, pair, p4a)
         last_a = [(3, fourth_a, p4a)]
-        theirs_a = project(here, 1, normed, last_a, total_a, final=True)
+        late_normed = after(normed, *begun)
+        theirs_a = project(here, 1, late_normed, last_a, total_a, final=True)
         got_a = to_core(theirs_a)
-        ours_a = project(here, 0, normed, last_a, total_a, final=True)
-
-        m4b = move(e1b, across, m3b)
-        e3b = move(m3b, outward, e1b)
-        p2b = move(e1b, pair, p3b, ours_a)
-        attended_a = attend(here, own_kind, other_kind, ours_a, got_a)
+        ours_a = project(here, 0, late_normed, last_a, total_a, final=True)
+
+        begun = (m3b, theirs_a, ours_a)
+        m4b = move(e1b, across, *begun)
+        e3b = move(m3b, outward, e1b, p3b, *begun)
+        i2o = move(high_o, inward, e1b, p3b, *begun)
+        p2b = move(e1b, pair, p3b, *begun)
+        attended_a = attend(here, own_kind, other_kind, after(ours_a, *begun), got_a)
         first_b = [(0, mine_b, p1b), (2, third_b, p3b)]
-        total_b = project(here, "own", normed, first_b, fresh=True)
-        total_b = project(here, "partner", normed, first_b, total_b, fresh=True)
-        held_a = over_tensor(attended_a)
-
-        m1o = move(low_o, across_or_stay, m4b)
-        fourth_b = choose(here, e3b, m4b)
-        p4b = move(fourth_b, pair, p2b, attended_a, total_b)
-        e1o = move(away_o, edge, e3b)
+        late_normed = after(normed, *begun)
+        total_b = project(here, "own", late_normed, first_b, fresh=True)
+        total_b = project(here, "partner", late_normed, first_b, total_b, fresh=True)
+
+        begun = (m4b, attended_a, total_b)
+        m1o = move(low_o, across, *begun)
+        m2o = move(high_o, across, *begun)
+        fourth_b = choose(here, after(e3b, *begun), m4b)
+        p4b = move(fourth_b, pair, p2b)
+        packed_a = move(pack(here, after(low_o, *begun), attended_a), edge, e3b, i2o, p2b)
+        held_a = over_tensor(after(attended_a, *begun))
         second_b = [(1, e1b, p2b)]
-        total_b = project(here, "own", normed, second_b, total_b)
-        total_b = project(here, "partner", normed, second_b, total_b)
-
-        m2o = move(high_o, across, m1o)
-        e2o = move(m1o, edge, e1o)
+        late_normed = after(normed, *begun)
+        total_b = project(here, "own", late_normed, second_b, total_b)
+        total_b = project(here, "partner", late_normed, second_b, total_b)
+
         last_b = [(3, fourth_b, p4b)]
         theirs_b = project(here, 1, normed, last_b, total_b, final=True)
         got_b = to_core(theirs_b)
         ours_b = project(here, 0, normed, last_b, total_b, final=True)
-        attended_b = attend(here, own_kind, other_kind, ours_b, got_b)
-
-        p2o = move(e1o, pair, p4b)
-        m3o = move(e2o, across, m2o)
-        m4o = move(e1o, across, m3o)
-        third_o = choose(here, e2o, m2o)
+        o1o, passed_a = unpack(here, after(packed_a, theirs_b), low_o, attended_a)
+        second_o = choose(here, o1o, i2o)
+        p2o = move(second_o, pair, p4b)
+        held_a += over_tensor(passed_a)
+
+        begun = (m1o, m2o, ours_b, second_o)
+        m3o = move(i1o, across, *begun)
+        o2o = move(m1o, outward, *begun)
+        attended_b = attend(here, own_kind, other_kind, after(ours_b, *begun), got_b)
+
+        begun = (m3o, attended_b)
+        m4o = move(i2o, across, *begun)
+        packed_b = move(pack(here, m3o, attended_b), edge, o2o, p2o, held_a[-1], *begun)
+        held_b = over_tensor(attended_b)
+        third_o = choose(here, after(o2o, *begun), m2o)
         p3o = move(third_o, pair, p2o)
-        passed_a = move(attended_a, edge, e2o)
-        held_a += over_tensor(passed_a)
-        e3o = move(m3o, outward, passed_a)
-        pieces_a = stack(here, held_a)
+        pieces_a = stack(here, [after(held_a[0], *begun)] + held_a[1:])
         pieces_a = (pieces_a, to_core(pieces_a))
-        fourth_o = choose(here, e3o, m4o)
-        held_b = over_tensor(attended_b)
-        held_b += over_tensor(move(attended_b, edge, passed_a))
-        blocks = [(0, mine_o, p1o), (1, e1o, p2o), (2, third_o, p3o)]
-
-        total = combine(here, ("partner", "own"), [pieces_a + (0, blocks)])
+
+        begun = (m4o, pieces_a[0])
+        o3o, passed_b = unpack(here, after(packed_b, p3o, held_b[-1], *begun), low_o, attended_b)
+        held_b += over_tensor(passed_b)
+        fourth_o = choose(here, o3o, m4o)
         p4o = move(fourth_o, pair, p3o)
-        last = [(3, fourth_o, p4o)]
+        blocks = [(0, mine_o, p1o), (1, second_o, p2o), (2, third_o, p3o)]
         pieces_b = stack(here, held_b)
         pieces_b = (pieces_b, to_core(pieces_b))
-        rest = [pieces_a + (0, last), pieces_b + (1, blocks + last)]
+        total = combine(
+            here, ("partner", "own"), [pieces_a + (0, blocks), pieces_b + (1, blocks)]
+        )
+        last = [(3, fourth_o, p4o)]
+        rest = [pieces_a + (0, last), pieces_b + (1, last)]
 
         kept_away, sent_away = combine(here, ("partner",), rest, total, 0, True)
         sent_away = to_core(sent_away)

time: 317 us -> 294 us (0.927)
  local copies, waits for them, and re-layouts: 23.5 us -> 4.34 us
  starting transfers between devices: 80.3 us -> 92.7 us
  waiting for transfers between devices: 145 us -> 135 us
  Pallas kernels: 66.2 us -> 61.3 us
    unnamed x78 -> x12, local copies, waits for them, and re-layouts: 21.8 us -> 3.65 us
    ppermute x58, starting transfers between devices: 80.3 us -> 92.7 us  [move(): lax.ppermute(after(array, *earlier) if earlier else array, AXES, pairs)]
    ppermute x58, waiting for transfers between devices: 145 us -> 135 us  [move(): lax.ppermute(after(array, *earlier) if earlier else array, AXES, pairs)]
    pallas_call x31 -> x36, Pallas kernels: 64 us -> 59 us  [call(): pl.pallas_call(kernel, in_specs=[pl.BlockSpec(memory_space=SMEM)] + [pl.B...]
  transfers between devices with their start and end apart: 58 -> 58, of which waited for: 28 -> 27; matrix products, arithmetic and copies ran while one was open for 0% -> 0% of each run, Pallas kernels for 19% -> 19%
where the time goes in v9:
time: 294 us
  waiting for transfers between devices  135 us (46%)
  starting transfers between devices  92.7 us (32%)
  Pallas kernels  61.3 us (21%)
  local copies, waits for them, and re-layouts  4.34 us (1%)
    ppermute x58, waiting for transfers between devices, move(): lax.ppermute(after(array, *earlier) if earlier else array, AXES, pairs)  135 us
    ppermute x58, starting transfers between devices, move(): lax.ppermute(after(array, *earlier) if earlier else array, AXES, pairs)  92.7 us
    pallas_call x36, Pallas kernels, call(): pl.pallas_call(kernel, in_specs=[pl.BlockSpec(memory_space=SMEM)] + [pl.B...  59 us
  transfers between devices with their start and end apart: 58, of which 27 were waited for; matrix products, arithmetic and copies ran while one was open for 0% of the time, Pallas kernels for 19%

profile of v9, /device:TPU:0, one launch (start us, length us, event | category | flops | bytes accessed | tf_op | source)
XLA Modules:
  0.0 293.8 jit_solution(8578990892351866416)
XLA Ops:
  0.8 1.9 copy-done
  4.3 5.9 %collective-permute-start.1 = (bf16[3,512,256]{2,1,0:T(8,128)(2,1)S(1)}, bf16[3,512,256]{2,1,0:T(8,128)(2,1)S(1)}, u32[]{:S(2)}, u32[]{:S(2)}) collective-permute-start(bf16[3,512,256]{2,1,0:T(8,128)(2,1)S(1)} %get-tuple-element.88), channel_id=1, source_target_pairs={{0,4},{1,5},{2,6},{3,7},{4,0},{5,1},{6,2},{7,3},{8,12},{9,13},{10,... | collective-permute-start | bytes 2359304 | tf_op jit(solution)/shard_map/ppermute | solution.py:418
  11.7 15.7 %collective-permute-done.1.refs_3_ = bf16[3,512,256]{2,1,0:T(8,128)(2,1)S(1)} collective-permute-done((bf16[3,512,256]{2,1,0:T(8,128)(2,1)S(1)}, bf16[3,512,256]{2,1,0:T(8,128)(2,1)S(1)}, u32[]{:S(2)}, u32[]{:S(2)}) %collective-permute-start.1) | collective-permute-done | bytes 786464 | tf_op jit(solution)/shard_map/ppermute | solution.py:418
  31.5 1.7 copy-done.2
  36.4 10.3 %collective-permute-done.3.a_ref = bf16[3,512,256]{2,1,0:T(8,128)(2,1)S(1)} collective-permute-done((bf16[3,512,256]{2,1,0:T(8,128)(2,1)S(1)}, bf16[3,512,256]{2,1,0:T(8,128)(2,1)S(1)}, u32[]{:S(2)}, u32[]{:S(2)}) %collective-permute-start.3) | collective-permute-done | bytes 786464 | tf_op jit(solution)/shard_map/ppermute | solution.py:418
  50.0 5.1 %collective-permute-start.10 = (bf16[160,2048]{1,0:T(8,128)(2,1)S(1)}, bf16[160,2048]{1,0:T(8,128)(2,1)S(1)}, u32[]{:S(2)}, u32[]{:S(2)}) collective-permute-start(bf16[160,2048]{1,0:T(8,128)(2,1)S(1)} %get-tuple-element.103), channel_id=1, source_target_pairs={{0,4},{1,5},{2,6},{3,7},{4,0},{5,1},{6,2},{7,3},{8,12},{9,13},{10,... | collective-permute-start | bytes 1966088 | tf_op jit(solution)/shard_map/ppermute | solution.py:418
  55.1 7.7 %collective-permute-done.8.refs_2_ = bf16[320,2048]{1,0:T(8,128)(2,1)S(1)} collective-permute-done((bf16[320,2048]{1,0:T(8,128)(2,1)S(1)}, bf16[320,2048]{1,0:T(8,128)(2,1)S(1)}, u32[]{:S(2)}, u32[]{:S(2)}) %collective-permute-start.8) | collective-permute-done | bytes 1310752 | tf_op jit(solution)/shard_map/ppermute | solution.py:418
  62.8 3.5 %collective-permute-done.10.refs_2_ = bf16[160,2048]{1,0:T(8,128)(2,1)S(1)} collective-permute-done((bf16[160,2048]{1,0:T(8,128)(2,1)S(1)}, bf16[160,2048]{1,0:T(8,128)(2,1)S(1)}, u32[]{:S(2)}, u32[]{:S(2)}) %collective-permute-start.10) | collective-permute-done | bytes 655392 | tf_op jit(solution)/shard_map/ppermute | solution.py:418
  70.1 6.1 %collective-permute-start.16 = (bf16[160,2048]{1,0:T(8,128)(2,1)S(1)}, bf16[160,2048]{1,0:T(8,128)(2,1)S(1)}, u32[]{:S(2)}, u32[]{:S(2)}) collective-permute-start(bf16[160,2048]{1,0:T(8,128)(2,1)S(1)} %get-tuple-element.113), channel_id=1, source_target_pairs={{0,4},{1,5},{2,6},{3,7},{4,0},{5,1},{6,2},{7,3},{8,12},{9,13},{10,... | collective-permute-start | bytes 1966088 | tf_op jit(solution)/shard_map/ppermute | solution.py:418
  77.7 3.2 %normalize.3.refs_0_ = bf16[2,8,640,512]{3,2,1,0:T(8,128)(2,1)S(1)} custom-call(s32[3]{0:T(128)S(1)} %pad_add_fusion.h_ref._, f32[8,1,512]{2,1,0:T(1,128)S(1)} %bitcast.9, bf16[640,2048]{1,0:T(8,128)(2,1)S(1)} %copy-done.3, bf16[320,2048]{1,0:T(8,128)(2,1)S(1)} %collective-permute-done.8.refs_2_, bf16[320,2048]{1,0:T(8,128)(2,1)S(1)} %collective-permute-done.9.refs_3_), custom_call_target="tpu_custom_call" | custom-call | tf_op jit(solution)/shard_map/normalize/pallas_call | solution.py:32
  81.5 7.3 %collective-permute-done.16.refs_2_ = bf16[160,2048]{1,0:T(8,128)(2,1)S(1)} collective-permute-done((bf16[160,2048]{1,0:T(8,128)(2,1)S(1)}, bf16[160,2048]{1,0:T(8,128)(2,1)S(1)}, u32[]{:S(2)}, u32[]{:S(2)}) %collective-permute-start.16) | collective-permute-done | bytes 655392 | tf_op jit(solution)/shard_map/ppermute | solution.py:418
  92.9 8.1 %collective-permute-start.26 = (bf16[1,256,1024]{2,1,0:T(8,128)(2,1)S(1)}, bf16[1,256,1024]{2,1,0:T(8,128)(2,1)S(1)}, u32[]{:S(2)}, u32[]{:S(2)}) collective-permute-start(bf16[1,256,1024]{2,1,0:T(8,128)(2,1)S(1)} %get-tuple-element.139.block_ref), channel_id=1, source_target_pairs={{0,4},{1,5},{2,6},{3,7},{12,8},{13,9},{14,10},{15,11},{16,20},{17,... | collective-permute-start | bytes 1572872 | tf_op jit(solution)/shard_map/ppermute | solution.py:418
  101.0 3.7 %project.10.refs_7_ = f32[2,640,768]{2,1,0:T(8,128)S(1)} custom-call(s32[3]{0:T(128)S(1)} %pad_add_fusion.h_ref._, bf16[2,8,640,512]{3,2,1,0:T(8,128)(2,1)S(1)} %normalize.3.refs_0_, bf16[3,512,256]{2,1,0:T(8,128)(2,1)S(1)} %get-tuple-element.89.refs_1_, bf16[3,512,256]{2,1,0:T(8,128)(2,1)S(1)} %collective-permute-done.2.refs_2_, ...), custom_call_target="tpu_custom_call" | custom-call | tf_op jit(solution)/shard_map/project/pallas_call | solution.py:32
  104.7 1.8 normalize.4.refs_0_
  106.5 3.8 %collective-permute-done.26 = bf16[1,256,1024]{2,1,0:T(8,128)(2,1)S(1)} collective-permute-done((bf16[1,256,1024]{2,1,0:T(8,128)(2,1)S(1)}, bf16[1,256,1024]{2,1,0:T(8,128)(2,1)S(1)}, u32[]{:S(2)}, u32[]{:S(2)}) %collective-permute-start.26) | collective-permute-done | bytes 524320 | tf_op jit(solution)/shard_map/ppermute | solution.py:418
  110.3 3.1 %collective-permute-done.23.a_ref = bf16[3,512,256]{2,1,0:T(8,128)(2,1)S(1)} collective-permute-done((bf16[3,512,256]{2,1,0:T(8,128)(2,1)S(1)}, bf16[3,512,256]{2,1,0:T(8,128)(2,1)S(1)}, u32[]{:S(2)}, u32[]{:S(2)}) %collective-permute-start.23) | collective-permute-done | bytes 786464 | tf_op jit(solution)/shard_map/ppermute | solution.py:418
  115.3 3.2 %collective-permute-start.27 = (bf16[3,512,256]{2,1,0:T(8,128)(2,1)S(1)}, bf16[3,512,256]{2,1,0:T(8,128)(2,1)S(1)}, u32[]{:S(2)}, u32[]{:S(2)}) collective-permute-start(bf16[3,512,256]{2,1,0:T(8,128)(2,1)S(1)} %collective-permute-done.18), channel_id=1, source_target_pairs={{0,4},{1,5},{2,6},{3,7},{4,0},{5,1},{6,2},{7,3},{8,12},{9,13},{10,... | collective-permute-start | bytes 2359304 | tf_op jit(solution)/shard_map/ppermute | solution.py:418
  121.5 1.8 normalize.5.refs_0_
  123.3 3.7 %project.11.refs_3_ = f32[2,640,768]{2,1,0:T(8,128)S(1)} custom-call(s32[3]{0:T(128)S(1)} %pad_add_fusion.h_ref._, bf16[2,8,640,512]{3,2,1,0:T(8,128)(2,1)S(1)} %normalize.5.refs_0_, bf16[3,512,256]{2,1,0:T(8,128)(2,1)S(1)} %get-tuple-element.89.refs_1_, bf16[3,512,256]{2,1,0:T(8,128)(2,1)S(1)} %collective-permute-done.2.refs_2_, ...), custom_call_target="tpu_custom_call", output_to_operand_aliasing={{}: (8, {})} | custom-call | tf_op jit(solution)/shard_map/project/pallas_call | solution.py:32
  127.1 4.4 %collective-permute-done.25.refs_2_ = bf16[3,512,256]{2,1,0:T(8,128)(2,1)S(1)} collective-permute-done((bf16[3,512,256]{2,1,0:T(8,128)(2,1)S(1)}, bf16[3,512,256]{2,1,0:T(8,128)(2,1)S(1)}, u32[]{:S(2)}, u32[]{:S(2)}) %collective-permute-start.25) | collective-permute-done | bytes 786464 | tf_op jit(solution)/shard_map/ppermute | solution.py:418
  131.5 2.4 collective-permute-done.27.a_ref
  135.8 4.0 %collective-permute-start.30 = (bf16[3,512,256]{2,1,0:T(8,128)(2,1)S(1)}, bf16[3,512,256]{2,1,0:T(8,128)(2,1)S(1)}, u32[]{:S(2)}, u32[]{:S(2)}) collective-permute-start(bf16[3,512,256]{2,1,0:T(8,128)(2,1)S(1)} %get-tuple-element.134), channel_id=1, source_target_pairs={{0,4},{1,5},{2,6},{3,7},{4,0},{5,1},{6,2},{7,3},{8,12},{9,13},{10,... | collective-permute-start | bytes 2359304 | tf_op jit(solution)/shard_map/ppermute | solution.py:418
  143.3 8.5 %collective-permute-done.32.refs_4_ = bf16[3,512,256]{2,1,0:T(8,128)(2,1)S(1)} collective-permute-done((bf16[3,512,256]{2,1,0:T(8,128)(2,1)S(1)}, bf16[3,512,256]{2,1,0:T(8,128)(2,1)S(1)}, u32[]{:S(2)}, u32[]{:S(2)}) %collective-permute-start.32) | collective-permute-done | bytes 786464 | tf_op jit(solution)/shard_map/ppermute | solution.py:418
  151.8 1.8 collective-permute-done.30.refs_1_
  156.5 4.7 %collective-permute-start.6 = (s32[1,640]{1,0:T(1,128)S(1)}, s32[1,640]{1,0:T(1,128)S(1)}, u32[]{:S(2)}, u32[]{:S(2)}) collective-permute-start(s32[1,640]{1,0:T(1,128)S(1)} %broadcast_in_dim.3.own_kind_ref.kind_ref), channel_id=1, source_target_pairs={{0,4},{1,5},{2,6},{3,7},{4,0},{5,1},{6,2},{7,3},{8,12},{9,13},{10,... | collective-permute-start | bytes 7688 | tf_op jit(solution)/shard_map/ppermute | solution.py:418
  161.3 11.2 %collective-permute-done.6.other_kind_ref.kind_ref = s32[1,640]{1,0:T(1,128)S(1)} collective-permute-done((s32[1,640]{1,0:T(1,128)S(1)}, s32[1,640]{1,0:T(1,128)S(1)}, u32[]{:S(2)}, u32[]{:S(2)}) %collective-permute-start.6) | collective-permute-done | bytes 2592 | tf_op jit(solution)/shard_map/ppermute | solution.py:418
  174.2 2.7 project.14.refs_5_
  176.9 2.7 project.15.refs_3_
  179.6 4.2 %attend.2.piece_ref.refs_0_ = bf16[640,256]{1,0:T(8,128)(2,1)S(1)} custom-call(s32[3]{0:T(128)S(1)} %pad_add_fusion.h_ref._, s32[1,640]{1,0:T(1,128)S(1)} %broadcast_in_dim.3.own_kind_ref.kind_ref, s32[1,640]{1,0:T(1,128)S(1)} %collective-permute-done.6.other_kind_ref.kind_ref, bf16[640,768]{1,0:T(8,128)(2,1)S(1)} %project.12.own_ref, ...), custom_call_target="tpu_custom_call" | custom-call | tf_op jit(solution)/shard_map/attend/pallas_call | solution.py:32
  188.0 1.9 project.16.refs_3_
  189.9 1.9 project.17.refs_3_
  191.8 6.4 %collective-permute-done.37.refs_2_ = bf16[3,512,256]{2,1,0:T(8,128)(2,1)S(1)} collective-permute-done((bf16[3,512,256]{2,1,0:T(8,128)(2,1)S(1)}, bf16[3,512,256]{2,1,0:T(8,128)(2,1)S(1)}, u32[]{:S(2)}, u32[]{:S(2)}) %collective-permute-start.37) | collective-permute-done | bytes 786464 | tf_op jit(solution)/shard_map/ppermute | solution.py:418
  206.4 4.3 %collective-permute-start.43 = (bf16[640,256]{1,0:T(8,128)(2,1)S(1)}, bf16[640,256]{1,0:T(8,128)(2,1)S(1)}, u32[]{:S(2)}, u32[]{:S(2)}) collective-permute-start(bf16[640,256]{1,0:T(8,128)(2,1)S(1)} %get-tuple-element.154.refs_2_), channel_id=1, source_target_pairs={{0,1},{1,0},{2,3},{3,2},{4,5},{5,4},{6,7},{7,6},{8,9},{9,8},{10,11... | collective-permute-start | bytes 983048 | tf_op jit(solution)/shard_map/ppermute | solution.py:418
  210.7 4.1 %attend.3.piece_ref.refs_0_ = bf16[640,256]{1,0:T(8,128)(2,1)S(1)} custom-call(s32[3]{0:T(128)S(1)} %pad_add_fusion.h_ref._, s32[1,640]{1,0:T(1,128)S(1)} %broadcast_in_dim.3.own_kind_ref.kind_ref, s32[1,640]{1,0:T(1,128)S(1)} %collective-permute-done.6.other_kind_ref.kind_ref, bf16[640,768]{1,0:T(8,128)(2,1)S(1)} %project.18.own_ref, ...), custom_call_target="tpu_custom_call" | custom-call | tf_op jit(solution)/shard_map/attend/pallas_call | solution.py:32
  215.5 3.3 %collective-permute-done.43.refs_3_ = bf16[640,256]{1,0:T(8,128)(2,1)S(1)} collective-permute-done((bf16[640,256]{1,0:T(8,128)(2,1)S(1)}, bf16[640,256]{1,0:T(8,128)(2,1)S(1)}, u32[]{:S(2)}, u32[]{:S(2)}) %collective-permute-start.43) | collective-permute-done | bytes 327712 | tf_op jit(solution)/shard_map/ppermute | solution.py:418
  218.8 2.1 collective-permute-done.46.a_ref
  220.9 5.1 %collective-permute-start.48 = (bf16[1664,256]{1,0:T(8,128)(2,1)S(1)}, bf16[1664,256]{1,0:T(8,128)(2,1)S(1)}, u32[]{:S(2)}, u32[]{:S(2)}) collective-permute-start(bf16[1664,256]{1,0:T(8,128)(2,1)S(1)} %pack.3), channel_id=1, source_target_pairs={{0,4},{1,5},{2,6},{3,7},{4,0},{5,1},{6,2},{7,3},{8,12},{9,13},{10,... | collective-permute-start | bytes 2555912 | tf_op jit(solution)/shard_map/ppermute | solution.py:418
  227.7 4.4 %collective-permute-start.42 = (bf16[640,256]{1,0:T(8,128)(2,1)S(1)}, bf16[640,256]{1,0:T(8,128)(2,1)S(1)}, u32[]{:S(2)}, u32[]{:S(2)}) collective-permute-start(bf16[640,256]{1,0:T(8,128)(2,1)S(1)} %attend.2.piece_ref.refs_0_), channel_id=1, source_target_pairs={{0,1},{1,0},{2,3},{3,2},{4,5},{5,4},{6,7},{7,6},{8,9},{9,8},{10,11... | collective-permute-start | bytes 983048 | tf_op jit(solution)/shard_map/ppermute | solution.py:418
  232.2 5.3 %collective-permute-done.42.refs_1_ = bf16[640,256]{1,0:T(8,128)(2,1)S(1)} collective-permute-done((bf16[640,256]{1,0:T(8,128)(2,1)S(1)}, bf16[640,256]{1,0:T(8,128)(2,1)S(1)}, u32[]{:S(2)}, u32[]{:S(2)}) %collective-permute-start.42) | collective-permute-done | bytes 327712 | tf_op jit(solution)/shard_map/ppermute | solution.py:418
  238.1 2.9 collective-permute-done.45.refs_1_
  241.6 4.0 %collective-permute-start.51 = (bf16[640,256]{1,0:T(8,128)(2,1)S(1)}, bf16[640,256]{1,0:T(8,128)(2,1)S(1)}, u32[]{:S(2)}, u32[]{:S(2)}) collective-permute-start(bf16[640,256]{1,0:T(8,128)(2,1)S(1)} %get-tuple-element.162.refs_2_), channel_id=1, source_target_pairs={{0,1},{1,0},{2,3},{3,2},{4,5},{5,4},{6,7},{7,6},{8,9},{9,8},{10,11... | collective-permute-start | bytes 983048 | tf_op jit(solution)/shard_map/ppermute | solution.py:418
  245.6 5.1 %collective-permute-done.51.refs_3_ = bf16[640,256]{1,0:T(8,128)(2,1)S(1)} collective-permute-done((bf16[640,256]{1,0:T(8,128)(2,1)S(1)}, bf16[640,256]{1,0:T(8,128)(2,1)S(1)}, u32[]{:S(2)}, u32[]{:S(2)}) %collective-permute-start.51) | collective-permute-done | bytes 327712 | tf_op jit(solution)/shard_map/ppermute | solution.py:418
  254.4 4.8 %combine.3.refs_8_ = f32[2,640,1024]{2,1,0:T(8,128)S(1)} custom-call(s32[3]{0:T(128)S(1)} %pad_add_fusion.h_ref._, bf16[4,640,256]{2,1,0:T(8,128)(2,1)S(1)} %stack.18.refs_0_.refs_2_.refs_4_, bf16[4,640,256]{2,1,0:T(8,128)(2,1)S(1)} %collective-permute-done.44.refs_1_.refs_3_.refs_5_, bf16[4,640,256]{2,1,0:T(8,128)(2,1)S(1)} %stack.18.refs_0_.refs_2_.refs_4_, ...), custom_call_target="tpu_custom_call" | custom-call | tf_op jit(solution)/shard_map/combine/pallas_call | solution.py:32
  259.2 7.1 %collective-permute-done.53.refs_5_.refs_7_ = bf16[1,256,1024]{2,1,0:T(8,128)(2,1)S(1)} collective-permute-done((bf16[1,256,1024]{2,1,0:T(8,128)(2,1)S(1)}, bf16[1,256,1024]{2,1,0:T(8,128)(2,1)S(1)}, u32[]{:S(2)}, u32[]{:S(2)}) %collective-permute-start.53) | collective-permute-done | bytes 524320 | tf_op jit(solution)/shard_map/ppermute | solution.py:418
  270.8 3.3 %collective-permute-start.56 = (bf16[320,1024]{1,0:T(8,128)(2,1)S(1)}, bf16[320,1024]{1,0:T(8,128)(2,1)S(1)}, u32[]{:S(2)}, u32[]{:S(2)}) collective-permute-start(bf16[320,1024]{1,0:T(8,128)(2,1)S(1)} %join.1), channel_id=1, source_target_pairs={{0,4},{1,5},{2,6},{3,7},{4,0},{5,1},{6,2},{7,3},{8,12},{9,13},{10,... | collective-permute-start | bytes 1966088 | tf_op jit(solution)/shard_map/ppermute | solution.py:418
  274.2 15.0 %collective-permute-done.56.c_ref = bf16[320,1024]{1,0:T(8,128)(2,1)S(1)} collective-permute-done((bf16[320,1024]{1,0:T(8,128)(2,1)S(1)}, bf16[320,1024]{1,0:T(8,128)(2,1)S(1)}, u32[]{:S(2)}, u32[]{:S(2)}) %collective-permute-start.56) | collective-permute-done | bytes 655392 | tf_op jit(solution)/shard_map/ppermute | solution.py:418
  289.2 2.1 collective-permute-done.57.d_ref
  291.3 2.4 shard_map.55
  (119 shorter events, 63.2 us)
Async XLA Ops:
  4.3 23.1 %collective-permute-start.1 = (bf16[3,512,256]{2,1,0:T(8,128)(2,1)S(1)}, bf16[3,512,256]{2,1,0:T(8,128)(2,1)S(1)}, u32[]{:S(2)}, u32[]{:S(2)}) collective-permute-start(bf16[3,512,256]{2,1,0:T(8,128)(2,1)S(1)} %get-tuple-element.88), channel_id=1, source_target_pairs={{0,4},{1,5},{2,6},{3,7},{4,0},{5,1},{6,2},{7,3},{8,12},{9,13},{10,... | collective-permute-start | bytes 2359304 | tf_op jit(solution)/shard_map/ppermute | solution.py:418
  10.2 18.7 %collective-permute-start.2 = (bf16[3,512,256]{2,1,0:T(8,128)(2,1)S(1)}, bf16[3,512,256]{2,1,0:T(8,128)(2,1)S(1)}, u32[]{:S(2)}, u32[]{:S(2)}) collective-permute-start(bf16[3,512,256]{2,1,0:T(8,128)(2,1)S(1)} %get-tuple-element.89.refs_1_), channel_id=1, source_target_pairs={{0,2},{1,3},{2,0},{3,1},{4,6},{5,7},{6,4},{7,5},{8,10},{9,11},{10,... | collective-permute-start | bytes 2359304 | tf_op jit(solution)/shard_map/ppermute | solution.py:418
  28.9 17.8 %collective-permute-start.3 = (bf16[3,512,256]{2,1,0:T(8,128)(2,1)S(1)}, bf16[3,512,256]{2,1,0:T(8,128)(2,1)S(1)}, u32[]{:S(2)}, u32[]{:S(2)}) collective-permute-start(bf16[3,512,256]{2,1,0:T(8,128)(2,1)S(1)} %collective-permute-done), channel_id=1, source_target_pairs={{0,4},{1,5},{2,6},{3,7},{4,0},{5,1},{6,2},{7,3},{8,12},{9,13},{10,... | collective-permute-start | bytes 2359304 | tf_op jit(solution)/shard_map/ppermute | solution.py:418
  29.3 17.8 %collective-permute-start.4 = (bf16[3,512,256]{2,1,0:T(8,128)(2,1)S(1)}, bf16[3,512,256]{2,1,0:T(8,128)(2,1)S(1)}, u32[]{:S(2)}, u32[]{:S(2)}) collective-permute-start(bf16[3,512,256]{2,1,0:T(8,128)(2,1)S(1)} %collective-permute-done.1.refs_3_), channel_id=1, source_target_pairs={{0,2},{1,3},{2,0},{3,1},{4,6},{5,7},{6,4},{7,5},{8,10},{9,11},{10,... | collective-permute-start | bytes 2359304 | tf_op jit(solution)/shard_map/ppermute | solution.py:418
  30.8 16.3 %collective-permute-start.5 = (bf16[3,512,256]{2,1,0:T(8,128)(2,1)S(1)}, bf16[3,512,256]{2,1,0:T(8,128)(2,1)S(1)}, u32[]{:S(2)}, u32[]{:S(2)}) collective-permute-start(bf16[3,512,256]{2,1,0:T(8,128)(2,1)S(1)} %get-tuple-element.93), channel_id=1, source_target_pairs={{4,8},{5,9},{6,10},{7,11},{8,4},{9,5},{10,6},{11,7},{20,24},{21,25... | collective-permute-start | bytes 2359304 | tf_op jit(solution)/shard_map/ppermute | solution.py:418
  34.0 28.8 %collective-permute-start.8 = (bf16[320,2048]{1,0:T(8,128)(2,1)S(1)}, bf16[320,2048]{1,0:T(8,128)(2,1)S(1)}, u32[]{:S(2)}, u32[]{:S(2)}) collective-permute-start(bf16[320,2048]{1,0:T(8,128)(2,1)S(1)} %get-tuple-element.100), channel_id=1, source_target_pairs={{0,1},{1,0},{2,3},{3,2},{4,5},{5,4},{6,7},{7,6},{8,9},{9,8},{10,11... | collective-permute-start | bytes 3932168 | tf_op jit(solution)/shard_map/ppermute | solution.py:418
  47.1 15.8 %collective-permute-start.7 = (bf16[3,512,256]{2,1,0:T(8,128)(2,1)S(1)}, bf16[3,512,256]{2,1,0:T(8,128)(2,1)S(1)}, u32[]{:S(2)}, u32[]{:S(2)}) collective-permute-start(bf16[3,512,256]{2,1,0:T(8,128)(2,1)S(1)} %collective-permute-done.3.a_ref), channel_id=1, source_target_pairs={{4,8},{5,9},{6,10},{7,11},{8,4},{9,5},{10,6},{11,7},{20,24},{21,25... | collective-permute-start | bytes 2359304 | tf_op jit(solution)/shard_map/ppermute | solution.py:418
  48.4 17.9 %collective-permute-start.12 = (bf16[3,512,256]{2,1,0:T(8,128)(2,1)S(1)}, bf16[3,512,256]{2,1,0:T(8,128)(2,1)S(1)}, u32[]{:S(2)}, u32[]{:S(2)}) collective-permute-start(bf16[3,512,256]{2,1,0:T(8,128)(2,1)S(1)} %choose.7.refs_5_), channel_id=1, source_target_pairs={{0,2},{1,3},{2,0},{3,1},{4,6},{5,7},{6,4},{7,5},{8,10},{9,11},{10,... | collective-permute-start | bytes 2359304 | tf_op jit(solution)/shard_map/ppermute | solution.py:418
  50.0 16.3 %collective-permute-start.10 = (bf16[160,2048]{1,0:T(8,128)(2,1)S(1)}, bf16[160,2048]{1,0:T(8,128)(2,1)S(1)}, u32[]{:S(2)}, u32[]{:S(2)}) collective-permute-start(bf16[160,2048]{1,0:T(8,128)(2,1)S(1)} %get-tuple-element.103), channel_id=1, source_target_pairs={{0,4},{1,5},{2,6},{3,7},{4,0},{5,1},{6,2},{7,3},{8,12},{9,13},{10,... | collective-permute-start | bytes 1966088 | tf_op jit(solution)/shard_map/ppermute | solution.py:418
  62.8 14.8 %collective-permute-start.9 = (bf16[320,2048]{1,0:T(8,128)(2,1)S(1)}, bf16[320,2048]{1,0:T(8,128)(2,1)S(1)}, u32[]{:S(2)}, u32[]{:S(2)}) collective-permute-start(bf16[320,2048]{1,0:T(8,128)(2,1)S(1)} %collective-permute-done.8.refs_2_), channel_id=1, source_target_pairs={{0,16},{1,17},{2,18},{3,19},{4,20},{5,21},{6,22},{7,23},{8,24},{9,... | collective-permute-start | bytes 3932168 | tf_op jit(solution)/shard_map/ppermute | solution.py:418
  66.3 14.6 %collective-permute-start.13 = (bf16[3,512,256]{2,1,0:T(8,128)(2,1)S(1)}, bf16[3,512,256]{2,1,0:T(8,128)(2,1)S(1)}, u32[]{:S(2)}, u32[]{:S(2)}) collective-permute-start(bf16[3,512,256]{2,1,0:T(8,128)(2,1)S(1)} %collective-permute-done.1.refs_3_), channel_id=1, source_target_pairs={{4,8},{5,9},{6,10},{7,11},{8,4},{9,5},{10,6},{11,7},{20,24},{21,25... | collective-permute-start | bytes 2359304 | tf_op jit(solution)/shard_map/ppermute | solution.py:418
  67.0 13.9 %collective-permute-start.11 = (bf16[160,2048]{1,0:T(8,128)(2,1)S(1)}, bf16[160,2048]{1,0:T(8,128)(2,1)S(1)}, u32[]{:S(2)}, u32[]{:S(2)}) collective-permute-start(bf16[160,2048]{1,0:T(8,128)(2,1)S(1)} %collective-permute-done.10.refs_2_), channel_id=1, source_target_pairs={{0,1},{1,0},{2,3},{3,2},{4,5},{5,4},{6,7},{7,6},{8,9},{9,8},{10,11... | collective-permute-start | bytes 1966088 | tf_op jit(solution)/shard_map/ppermute | solution.py:418
  68.6 20.2 %collective-permute-start.22 = (bf16[3,512,256]{2,1,0:T(8,128)(2,1)S(1)}, bf16[3,512,256]{2,1,0:T(8,128)(2,1)S(1)}, u32[]{:S(2)}, u32[]{:S(2)}) collective-permute-start(bf16[3,512,256]{2,1,0:T(8,128)(2,1)S(1)} %get-tuple-element.123.refs_1_), channel_id=1, source_target_pairs={{0,2},{1,3},{2,0},{3,1},{4,6},{5,7},{6,4},{7,5},{8,10},{9,11},{10,... | collective-permute-start | bytes 2359304 | tf_op jit(solution)/shard_map/ppermute | solution.py:418
  70.1 18.7 %collective-permute-start.16 = (bf16[160,2048]{1,0:T(8,128)(2,1)S(1)}, bf16[160,2048]{1,0:T(8,128)(2,1)S(1)}, u32[]{:S(2)}, u32[]{:S(2)}) collective-permute-start(bf16[160,2048]{1,0:T(8,128)(2,1)S(1)} %get-tuple-element.113), channel_id=1, source_target_pairs={{0,4},{1,5},{2,6},{3,7},{4,0},{5,1},{6,2},{7,3},{8,12},{9,13},{10,... | collective-permute-start | bytes 1966088 | tf_op jit(solution)/shard_map/ppermute | solution.py:418
  80.9 10.5 %collective-permute-start.14 = (bf16[160,2048]{1,0:T(8,128)(2,1)S(1)}, bf16[160,2048]{1,0:T(8,128)(2,1)S(1)}, u32[]{:S(2)}, u32[]{:S(2)}) collective-permute-start(bf16[160,2048]{1,0:T(8,128)(2,1)S(1)} %collective-permute-done.10.refs_2_), channel_id=1, source_target_pairs={{0,16},{1,17},{2,18},{3,19},{4,20},{5,21},{6,22},{7,23},{8,24},{9,... | collective-permute-start | bytes 1966088 | tf_op jit(solution)/shard_map/ppermute | solution.py:418
  81.0 11.9 %collective-permute-start.15 = (bf16[160,2048]{1,0:T(8,128)(2,1)S(1)}, bf16[160,2048]{1,0:T(8,128)(2,1)S(1)}, u32[]{:S(2)}, u32[]{:S(2)}) collective-permute-start(bf16[160,2048]{1,0:T(8,128)(2,1)S(1)} %collective-permute-done.11.refs_3_), channel_id=1, source_target_pairs={{0,16},{1,17},{2,18},{3,19},{4,20},{5,21},{6,22},{7,23},{8,24},{9,... | collective-permute-start | bytes 1966088 | tf_op jit(solution)/shard_map/ppermute | solution.py:418
  88.8 21.6 %collective-permute-start.18 = (bf16[3,512,256]{2,1,0:T(8,128)(2,1)S(1)}, bf16[3,512,256]{2,1,0:T(8,128)(2,1)S(1)}, u32[]{:S(2)}, u32[]{:S(2)}) collective-permute-start(bf16[3,512,256]{2,1,0:T(8,128)(2,1)S(1)} %get-tuple-element.116), channel_id=1, source_target_pairs={{0,0},{1,1},{2,2},{3,3},{4,8},{5,9},{6,10},{7,11},{8,4},{9,5},{10,... | collective-permute-start | bytes 2359304 | tf_op jit(solution)/shard_map/ppermute | solution.py:418
  89.5 24.0 %collective-permute-start.23 = (bf16[3,512,256]{2,1,0:T(8,128)(2,1)S(1)}, bf16[3,512,256]{2,1,0:T(8,128)(2,1)S(1)}, u32[]{:S(2)}, u32[]{:S(2)}) collective-permute-start(bf16[3,512,256]{2,1,0:T(8,128)(2,1)S(1)} %collective-permute-done.7), channel_id=1, source_target_pairs={{4,0},{5,1},{6,2},{7,3},{8,12},{9,13},{10,14},{11,15},{20,16},{21,... | collective-permute-start | bytes 2359304 | tf_op jit(solution)/shard_map/ppermute | solution.py:418
  90.8 19.6 %collective-permute-start.17 = (bf16[160,2048]{1,0:T(8,128)(2,1)S(1)}, bf16[160,2048]{1,0:T(8,128)(2,1)S(1)}, u32[]{:S(2)}, u32[]{:S(2)}) collective-permute-start(bf16[160,2048]{1,0:T(8,128)(2,1)S(1)} %collective-permute-done.16.refs_2_), channel_id=1, source_target_pairs={{0,1},{1,0},{2,3},{3,2},{4,5},{5,4},{6,7},{7,6},{8,9},{9,8},{10,11... | collective-permute-start | bytes 1966088 | tf_op jit(solution)/shard_map/ppermute | solution.py:418
  91.4 15.1 %collective-permute-start.24 = (bf16[1,256,1024]{2,1,0:T(8,128)(2,1)S(1)}, bf16[1,256,1024]{2,1,0:T(8,128)(2,1)S(1)}, u32[]{:S(2)}, u32[]{:S(2)}) collective-permute-start(bf16[1,256,1024]{2,1,0:T(8,128)(2,1)S(1)} %get-tuple-element.126.refs_12_.refs_18_), channel_id=1, source_target_pairs={{0,2},{1,3},{2,0},{3,1},{4,6},{5,7},{6,4},{7,5},{8,10},{9,11},{10,... | collective-permute-start | bytes 1572872 | tf_op jit(solution)/shard_map/ppermute | solution.py:418
  92.9 17.4 %collective-permute-start.26 = (bf16[1,256,1024]{2,1,0:T(8,128)(2,1)S(1)}, bf16[1,256,1024]{2,1,0:T(8,128)(2,1)S(1)}, u32[]{:S(2)}, u32[]{:S(2)}) collective-permute-start(bf16[1,256,1024]{2,1,0:T(8,128)(2,1)S(1)} %get-tuple-element.139.block_ref), channel_id=1, source_target_pairs={{0,4},{1,5},{2,6},{3,7},{12,8},{13,9},{14,10},{15,11},{16,20},{17,... | collective-permute-start | bytes 1572872 | tf_op jit(solution)/shard_map/ppermute | solution.py:418
  114.0 13.1 %collective-permute-start.21 = (bf16[3,512,256]{2,1,0:T(8,128)(2,1)S(1)}, bf16[3,512,256]{2,1,0:T(8,128)(2,1)S(1)}, u32[]{:S(2)}, u32[]{:S(2)}) collective-permute-start(bf16[3,512,256]{2,1,0:T(8,128)(2,1)S(1)} %get-tuple-element.121), channel_id=1, source_target_pairs={{4,8},{5,9},{6,10},{7,11},{8,4},{9,5},{10,6},{11,7},{20,24},{21,25... | collective-permute-start | bytes 2359304 | tf_op jit(solution)/shard_map/ppermute | solution.py:418
  114.8 16.8 %collective-permute-start.25 = (bf16[3,512,256]{2,1,0:T(8,128)(2,1)S(1)}, bf16[3,512,256]{2,1,0:T(8,128)(2,1)S(1)}, u32[]{:S(2)}, u32[]{:S(2)}) collective-permute-start(bf16[3,512,256]{2,1,0:T(8,128)(2,1)S(1)} %choose.8.refs_1_), channel_id=1, source_target_pairs={{0,2},{1,3},{2,0},{3,1},{4,6},{5,7},{6,4},{7,5},{8,10},{9,11},{10,... | collective-permute-start | bytes 2359304 | tf_op jit(solution)/shard_map/ppermute | solution.py:418
  115.3 18.6 %collective-permute-start.27 = (bf16[3,512,256]{2,1,0:T(8,128)(2,1)S(1)}, bf16[3,512,256]{2,1,0:T(8,128)(2,1)S(1)}, u32[]{:S(2)}, u32[]{:S(2)}) collective-permute-start(bf16[3,512,256]{2,1,0:T(8,128)(2,1)S(1)} %collective-permute-done.18), channel_id=1, source_target_pairs={{0,4},{1,5},{2,6},{3,7},{4,0},{5,1},{6,2},{7,3},{8,12},{9,13},{10,... | collective-permute-start | bytes 2359304 | tf_op jit(solution)/shard_map/ppermute | solution.py:418
  133.9 17.9 %collective-permute-start.28 = (bf16[3,512,256]{2,1,0:T(8,128)(2,1)S(1)}, bf16[3,512,256]{2,1,0:T(8,128)(2,1)S(1)}, u32[]{:S(2)}, u32[]{:S(2)}) collective-permute-start(bf16[3,512,256]{2,1,0:T(8,128)(2,1)S(1)} %collective-permute-done.27.a_ref), channel_id=1, source_target_pairs={{4,8},{5,9},{6,10},{7,11},{8,4},{9,5},{10,6},{11,7},{20,24},{21,25... | collective-permute-start | bytes 2359304 | tf_op jit(solution)/shard_map/ppermute | solution.py:418
  135.2 16.6 %collective-permute-start.32 = (bf16[3,512,256]{2,1,0:T(8,128)(2,1)S(1)}, bf16[3,512,256]{2,1,0:T(8,128)(2,1)S(1)}, u32[]{:S(2)}, u32[]{:S(2)}) collective-permute-start(bf16[3,512,256]{2,1,0:T(8,128)(2,1)S(1)} %choose.9.refs_3_), channel_id=1, source_target_pairs={{0,2},{1,3},{2,0},{3,1},{4,6},{5,7},{6,4},{7,5},{8,10},{9,11},{10,... | collective-permute-start | bytes 2359304 | tf_op jit(solution)/shard_map/ppermute | solution.py:418
  135.8 17.8 %collective-permute-start.30 = (bf16[3,512,256]{2,1,0:T(8,128)(2,1)S(1)}, bf16[3,512,256]{2,1,0:T(8,128)(2,1)S(1)}, u32[]{:S(2)}, u32[]{:S(2)}) collective-permute-start(bf16[3,512,256]{2,1,0:T(8,128)(2,1)S(1)} %get-tuple-element.134), channel_id=1, source_target_pairs={{0,4},{1,5},{2,6},{3,7},{4,0},{5,1},{6,2},{7,3},{8,12},{9,13},{10,... | collective-permute-start | bytes 2359304 | tf_op jit(solution)/shard_map/ppermute | solution.py:418
  141.5 38.2 %collective-permute-start.29 = (bf16[640,768]{1,0:T(8,128)(2,1)S(1)}, bf16[640,768]{1,0:T(8,128)(2,1)S(1)}, u32[]{:S(2)}, u32[]{:S(2)}) collective-permute-start(bf16[640,768]{1,0:T(8,128)(2,1)S(1)} %project.13), channel_id=1, source_target_pairs={{0,16},{1,17},{2,18},{3,19},{4,20},{5,21},{6,22},{7,23},{8,24},{9,... | collective-permute-start | bytes 2949128 | tf_op jit(solution)/shard_map/ppermute | solution.py:418
  153.6 30.2 %collective-permute-start.31 = (bf16[3,512,256]{2,1,0:T(8,128)(2,1)S(1)}, bf16[3,512,256]{2,1,0:T(8,128)(2,1)S(1)}, u32[]{:S(2)}, u32[]{:S(2)}) collective-permute-start(bf16[3,512,256]{2,1,0:T(8,128)(2,1)S(1)} %collective-permute-done.30.refs_1_), channel_id=1, source_target_pairs={{4,8},{5,9},{6,10},{7,11},{8,4},{9,5},{10,6},{11,7},{20,24},{21,25... | collective-permute-start | bytes 2359304 | tf_op jit(solution)/shard_map/ppermute | solution.py:418
  154.3 29.5 %collective-permute-start.35 = (bf16[3,512,256]{2,1,0:T(8,128)(2,1)S(1)}, bf16[3,512,256]{2,1,0:T(8,128)(2,1)S(1)}, u32[]{:S(2)}, u32[]{:S(2)}) collective-permute-start(bf16[3,512,256]{2,1,0:T(8,128)(2,1)S(1)} %collective-permute-done.28), channel_id=1, source_target_pairs={{4,0},{5,1},{6,2},{7,3},{8,12},{9,13},{10,14},{11,15},{20,16},{21,... | collective-permute-start | bytes 2359304 | tf_op jit(solution)/shard_map/ppermute | solution.py:418
  155.6 28.9 %collective-permute-start.36 = (bf16[3,512,256]{2,1,0:T(8,128)(2,1)S(1)}, bf16[3,512,256]{2,1,0:T(8,128)(2,1)S(1)}, u32[]{:S(2)}, u32[]{:S(2)}) collective-permute-start(bf16[3,512,256]{2,1,0:T(8,128)(2,1)S(1)} %collective-permute-done.30.refs_1_), channel_id=1, source_target_pairs={{0,2},{1,3},{2,0},{3,1},{4,6},{5,7},{6,4},{7,5},{8,10},{9,11},{10,... | collective-permute-start | bytes 2359304 | tf_op jit(solution)/shard_map/ppermute | solution.py:418
  156.5 16.0 %collective-permute-start.6 = (s32[1,640]{1,0:T(1,128)S(1)}, s32[1,640]{1,0:T(1,128)S(1)}, u32[]{:S(2)}, u32[]{:S(2)}) collective-permute-start(s32[1,640]{1,0:T(1,128)S(1)} %broadcast_in_dim.3.own_kind_ref.kind_ref), channel_id=1, source_target_pairs={{0,4},{1,5},{2,6},{3,7},{4,0},{5,1},{6,2},{7,3},{8,12},{9,13},{10,... | collective-permute-start | bytes 7688 | tf_op jit(solution)/shard_map/ppermute | solution.py:418
  172.5 14.0 %collective-permute-start.38 = (bf16[1,256,1024]{2,1,0:T(8,128)(2,1)S(1)}, bf16[1,256,1024]{2,1,0:T(8,128)(2,1)S(1)}, u32[]{:S(2)}, u32[]{:S(2)}) collective-permute-start(bf16[1,256,1024]{2,1,0:T(8,128)(2,1)S(1)} %get-tuple-element.147), channel_id=1, source_target_pairs={{0,4},{1,5},{2,6},{3,7},{12,8},{13,9},{14,10},{15,11},{16,20},{17,... | collective-permute-start | bytes 1572872 | tf_op jit(solution)/shard_map/ppermute | solution.py:418
  184.4 13.8 %collective-permute-start.37 = (bf16[3,512,256]{2,1,0:T(8,128)(2,1)S(1)}, bf16[3,512,256]{2,1,0:T(8,128)(2,1)S(1)}, u32[]{:S(2)}, u32[]{:S(2)}) collective-permute-start(bf16[3,512,256]{2,1,0:T(8,128)(2,1)S(1)} %choose.10.refs_1_), channel_id=1, source_target_pairs={{0,2},{1,3},{2,0},{3,1},{4,6},{5,7},{6,4},{7,5},{8,10},{9,11},{10,... | collective-permute-start | bytes 2359304 | tf_op jit(solution)/shard_map/ppermute | solution.py:418
  186.5 15.2 %collective-permute-start.39 = (bf16[1664,256]{1,0:T(8,128)(2,1)S(1)}, bf16[1664,256]{1,0:T(8,128)(2,1)S(1)}, u32[]{:S(2)}, u32[]{:S(2)}) collective-permute-start(bf16[1664,256]{1,0:T(8,128)(2,1)S(1)} %pack.2), channel_id=1, source_target_pairs={{0,4},{1,5},{2,6},{3,7},{4,0},{5,1},{6,2},{7,3},{8,12},{9,13},{10,... | collective-permute-start | bytes 2555912 | tf_op jit(solution)/shard_map/ppermute | solution.py:418
  186.6 16.4 %collective-permute-start.33 = (bf16[1,256,1024]{2,1,0:T(8,128)(2,1)S(1)}, bf16[1,256,1024]{2,1,0:T(8,128)(2,1)S(1)}, u32[]{:S(2)}, u32[]{:S(2)}) collective-permute-start(bf16[1,256,1024]{2,1,0:T(8,128)(2,1)S(1)} %get-tuple-element.139.block_ref), channel_id=1, source_target_pairs={{4,8},{5,9},{6,10},{7,11},{8,4},{9,5},{10,6},{11,7},{20,24},{21,25... | collective-permute-start | bytes 1572872 | tf_op jit(solution)/shard_map/ppermute | solution.py:418
  187.3 15.7 %collective-permute-start.34 = (bf16[1,256,1024]{2,1,0:T(8,128)(2,1)S(1)}, bf16[1,256,1024]{2,1,0:T(8,128)(2,1)S(1)}, u32[]{:S(2)}, u32[]{:S(2)}) collective-permute-start(bf16[1,256,1024]{2,1,0:T(8,128)(2,1)S(1)} %get-tuple-element.147), channel_id=1, source_target_pairs={{4,8},{5,9},{6,10},{7,11},{8,4},{9,5},{10,6},{11,7},{20,24},{21,25... | collective-permute-start | bytes 1572872 | tf_op jit(solution)/shard_map/ppermute | solution.py:418
  199.9 10.7 %collective-permute-start.41 = (bf16[640,768]{1,0:T(8,128)(2,1)S(1)}, bf16[640,768]{1,0:T(8,128)(2,1)S(1)}, u32[]{:S(2)}, u32[]{:S(2)}) collective-permute-start(bf16[640,768]{1,0:T(8,128)(2,1)S(1)} %project.19), channel_id=1, source_target_pairs={{0,16},{1,17},{2,18},{3,19},{4,20},{5,21},{6,22},{7,23},{8,24},{9,... | collective-permute-start | bytes 2949128 | tf_op jit(solution)/shard_map/ppermute | solution.py:418
  203.0 11.8 %collective-permute-start.40 = (bf16[1,256,1024]{2,1,0:T(8,128)(2,1)S(1)}, bf16[1,256,1024]{2,1,0:T(8,128)(2,1)S(1)}, u32[]{:S(2)}, u32[]{:S(2)}) collective-permute-start(bf16[1,256,1024]{2,1,0:T(8,128)(2,1)S(1)} %collective-permute-done.26), channel_id=1, source_target_pairs={{4,8},{5,9},{6,10},{7,11},{8,4},{9,5},{10,6},{11,7},{20,24},{21,25... | collective-permute-start | bytes 1572872 | tf_op jit(solution)/shard_map/ppermute | solution.py:418
  203.7 17.2 %collective-permute-start.46 = (bf16[1,256,1024]{2,1,0:T(8,128)(2,1)S(1)}, bf16[1,256,1024]{2,1,0:T(8,128)(2,1)S(1)}, u32[]{:S(2)}, u32[]{:S(2)}) collective-permute-start(bf16[1,256,1024]{2,1,0:T(8,128)(2,1)S(1)} %collective-permute-done.33), channel_id=1, source_target_pairs={{4,0},{5,1},{6,2},{7,3},{8,12},{9,13},{10,14},{11,15},{20,16},{21,... | collective-permute-start | bytes 1572872 | tf_op jit(solution)/shard_map/ppermute | solution.py:418
  205.0 15.9 %collective-permute-start.47 = (bf16[1,256,1024]{2,1,0:T(8,128)(2,1)S(1)}, bf16[1,256,1024]{2,1,0:T(8,128)(2,1)S(1)}, u32[]{:S(2)}, u32[]{:S(2)}) collective-permute-start(bf16[1,256,1024]{2,1,0:T(8,128)(2,1)S(1)} %choose.11.refs_14_.refs_20_), channel_id=1, source_target_pairs={{0,2},{1,3},{2,0},{3,1},{4,6},{5,7},{6,4},{7,5},{8,10},{9,11},{10,... | collective-permute-start | bytes 1572872 | tf_op jit(solution)/shard_map/ppermute | solution.py:418
  206.4 12.3 %collective-permute-start.43 = (bf16[640,256]{1,0:T(8,128)(2,1)S(1)}, bf16[640,256]{1,0:T(8,128)(2,1)S(1)}, u32[]{:S(2)}, u32[]{:S(2)}) collective-permute-start(bf16[640,256]{1,0:T(8,128)(2,1)S(1)} %get-tuple-element.154.refs_2_), channel_id=1, source_target_pairs={{0,1},{1,0},{2,3},{3,2},{4,5},{5,4},{6,7},{7,6},{8,9},{9,8},{10,11... | collective-permute-start | bytes 983048 | tf_op jit(solution)/shard_map/ppermute | solution.py:418
  220.9 20.1 %collective-permute-start.48 = (bf16[1664,256]{1,0:T(8,128)(2,1)S(1)}, bf16[1664,256]{1,0:T(8,128)(2,1)S(1)}, u32[]{:S(2)}, u32[]{:S(2)}) collective-permute-start(bf16[1664,256]{1,0:T(8,128)(2,1)S(1)} %pack.3), channel_id=1, source_target_pairs={{0,4},{1,5},{2,6},{3,7},{4,0},{5,1},{6,2},{7,3},{8,12},{9,13},{10,... | collective-permute-start | bytes 2555912 | tf_op jit(solution)/shard_map/ppermute | solution.py:418
  226.6 14.4 %collective-permute-start.49 = (bf16[1,256,1024]{2,1,0:T(8,128)(2,1)S(1)}, bf16[1,256,1024]{2,1,0:T(8,128)(2,1)S(1)}, u32[]{:S(2)}, u32[]{:S(2)}) collective-permute-start(bf16[1,256,1024]{2,1,0:T(8,128)(2,1)S(1)} %choose.12.refs_16_.refs_22_), channel_id=1, source_target_pairs={{0,2},{1,3},{2,0},{3,1},{4,6},{5,7},{6,4},{7,5},{8,10},{9,11},{10,... | collective-permute-start | bytes 1572872 | tf_op jit(solution)/shard_map/ppermute | solution.py:418
  226.7 14.2 %collective-permute-start.50 = (bf16[1,256,1024]{2,1,0:T(8,128)(2,1)S(1)}, bf16[1,256,1024]{2,1,0:T(8,128)(2,1)S(1)}, u32[]{:S(2)}, u32[]{:S(2)}) collective-permute-start(bf16[1,256,1024]{2,1,0:T(8,128)(2,1)S(1)} %collective-permute-done.38.b_ref), channel_id=1, source_target_pairs={{4,8},{5,9},{6,10},{7,11},{8,4},{9,5},{10,6},{11,7},{20,24},{21,25... | collective-permute-start | bytes 1572872 | tf_op jit(solution)/shard_map/ppermute | solution.py:418
  252.0 14.4 %collective-permute-start.53 = (bf16[1,256,1024]{2,1,0:T(8,128)(2,1)S(1)}, bf16[1,256,1024]{2,1,0:T(8,128)(2,1)S(1)}, u32[]{:S(2)}, u32[]{:S(2)}) collective-permute-start(bf16[1,256,1024]{2,1,0:T(8,128)(2,1)S(1)} %choose.13.refs_4_.refs_6_), channel_id=1, source_target_pairs={{0,2},{1,3},{2,0},{3,1},{4,6},{5,7},{6,4},{7,5},{8,10},{9,11},{10,... | collective-permute-start | bytes 1572872 | tf_op jit(solution)/shard_map/ppermute | solution.py:418
  269.3 19.9 %collective-permute-start.54 = (bf16[640,1024]{1,0:T(8,128)(2,1)S(1)}, bf16[640,1024]{1,0:T(8,128)(2,1)S(1)}, u32[]{:S(2)}, u32[]{:S(2)}) collective-permute-start(bf16[640,1024]{1,0:T(8,128)(2,1)S(1)} %combine.4.a_ref), channel_id=1, source_target_pairs={{0,16},{1,17},{2,18},{3,19},{4,20},{5,21},{6,22},{7,23},{8,24},{9,... | collective-permute-start | bytes 3932168 | tf_op jit(solution)/shard_map/ppermute | solution.py:418
  270.8 18.4 %collective-permute-start.56 = (bf16[320,1024]{1,0:T(8,128)(2,1)S(1)}, bf16[320,1024]{1,0:T(8,128)(2,1)S(1)}, u32[]{:S(2)}, u32[]{:S(2)}) collective-permute-start(bf16[320,1024]{1,0:T(8,128)(2,1)S(1)} %join.1), channel_id=1, source_target_pairs={{0,4},{1,5},{2,6},{3,7},{4,0},{5,1},{6,2},{7,3},{8,12},{9,13},{10,... | collective-permute-start | bytes 1966088 | tf_op jit(solution)/shard_map/ppermute | solution.py:418
  (16 other events, 222.4 us)

commit v10 on v9

--- a/solution.py
+++ b/solution.py
@@ -66,18 +66,30 @@
     return call("halves", kernel, here, [weight], [shaped((kinds, depth, part))] * 4)
 
 
-def own_rows_of(here, tokens):
+def own_rows_of(here, tokens, kind):
     length, features = tokens.shape
     half = length // 2
-
-    def kernel(h_ref, in_ref, rows_ref, top_ref, bottom_ref):
+    extra = 16
+
+    def kernel(h_ref, in_ref, kind_ref, rows_ref, top_ref, bottom_ref):
         rows = jnp.where(h_ref[0] == 0, in_ref[:half], in_ref[half:])
         rows_ref[...] = rows
         top_ref[...] = rows[: half // 2]
-        bottom_ref[...] = rows[half // 2 :]
-
-    part = shaped((half // 2, features))
-    return call("own_rows_of", kernel, here, [tokens], [shaped((half, features)), part, part])
+        bottom_ref[: half // 2] = rows[half // 2 :]
+        bottom_ref[half // 2 :, :length] = jnp.broadcast_to(
+            kind_ref[...].astype(F32), (extra, length)
+        ).astype(BF16)
+        bottom_ref[half // 2 :, length:] = jnp.zeros((extra, features - length), BF16)
+
+    outs = [shaped((rows, features)) for rows in (half, half // 2, half // 2 + extra)]
+    return call("own_rows_of", kernel, here, [tokens, kind], outs)
+
+
+def kinds_behind(here, part, length):
+    def kernel(_, in_ref, out_ref):
+        out_ref[...] = in_ref[length // 4 :, :length].astype(F32)[:1].astype(I32)
+
+    return call("kinds_behind", kernel, here, [part], shaped((1, length), I32))
 
 
 def choose(here, from_edge, from_middle):
@@ -244,7 +256,7 @@
     return call("attend", kernel, here, [own_kind, other_kind, own, got], shaped((length, width)))
 
 
-def combine(here, slots, groups, total=None, offset=0, cut=False):
+def combine(here, slots, groups, total=None, final=False, offset=0, cut=False):
     held_pieces, length, held = groups[0][0].shape
     shards = held_pieces // 2
     features = groups[0][3][0][1].shape[2]
@@ -279,7 +291,7 @@
                     block = jnp.where(at_place.y == parity, near, far)
                     part = jnp.dot(rows[i], block, preferred_element_type=F32)
                     summed = part if summed is None else summed + part
-                if total is None:
+                if not final:
                     outs[0][s, :, columns] = summed
                 elif cut:
                     result = summed.astype(BF16)
@@ -289,7 +301,7 @@
                 else:
                     outs[0][:, columns] = summed.astype(BF16)
 
-    if total is None:
+    if not final:
         out_shape = shaped((len(slots), length, features), F32)
     elif cut:
         out_shape = [shaped((half, features))] * 2
@@ -462,13 +474,12 @@
         m2a = move(high_a, across, e1a, p1a, *begun)
         e2a = move(m1a, edge, e1a, p1a)
         p2a = move(e1a, pair, p1a, *begun)
-        rows, top, bottom = own_rows_of(here, after(tokens, *begun))
+        rows, top, bottom = own_rows_of(here, after(tokens, *begun), own_kind)
         fetched = over_tensor(rows)
         low_b, high_b, mine_b, away_b = halves(here, after(weight, *begun), 1, 2)
 
         begun = (m2a, mine_b)
         m3a = move(e2a, across, p2a, *begun)
-        other_kind = move(own_kind, edge, e2a, p2a, *begun)
         passed_top = move(top, edge, e2a, p2a, *begun)
         third_a = choose(here, after(e2a, *begun), m2a)
         p3a = move(third_a, pair, p2a)
@@ -480,16 +491,17 @@
             here, "own", None, gains, after(tokens, *begun), fetched[1:], swapped, shape, 0, half
         )
         m4a = move(e1a, across, passed_top, p3a, *begun)
+        m1b = move(low_b, across_or_stay, passed_top, p3a, *begun)
         passed_bottom = move(bottom, edge, passed_top, p3a, *begun)
         p1b = move(mine_b, pair, p3a, *begun)
         part_top = over_tensor(after(passed_top, *begun))
         low_o, high_o, mine_o, away_o = halves(here, after(out_weight, *begun), 0, 1)
 
-        begun = (m4a, normed, mine_o)
-        m1b = move(low_b, across_or_stay, *begun)
-        e3a = move(m3a, outward, passed_bottom, p1b, part_top[-1], *begun)
-        i1o = move(low_o, inward, passed_bottom, p1b, part_top[-1], *begun)
+        begun = (passed_bottom, normed, mine_o)
+        e3a = move(m3a, outward, part_top[-1], *begun)
+        i1o = move(low_o, inward, part_top[-1], *begun)
         p1o = move(mine_o, pair, p1b, *begun)
+        other_kind = kinds_behind(here, after(passed_bottom, *begun), length)
         part_bottom = over_tensor(after(passed_bottom, *begun))
         top_swapped = [to_core(a, *begun) for a in part_top]
         first_a = [(0, mine_a, p1a), (1, e1a, p2a), (2, third_a, p3a)]
@@ -498,7 +510,7 @@
             here, "partner", normed, gains, None, part_top, top_swapped, shape, 0, half // 2
         )
 
-        begun = (m1b, normed, total_a)
+        begun = (m4a, m1b, normed, total_a, other_kind)
         m2b = move(high_b, across, *begun)
         e2b = move(m1b, edge, e3a, i1o, p1o, part_bottom[-1], *begun)
         fourth_a = choose(here, after(e3a, *begun), m4a)
@@ -553,36 +565,35 @@
         held_a += over_tensor(passed_a)
 
         begun = (m1o, m2o, ours_b, second_o)
-        m3o = move(i1o, across, *begun)
+        m3o = move(i1o, across, held_a[1], *begun)
         o2o = move(m1o, outward, *begun)
         attended_b = attend(here, own_kind, other_kind, after(ours_b, *begun), got_b)
 
-        begun = (m3o, attended_b)
+        passed_b = move(attended_b, edge, o2o, p2o, held_a[-1])
+        begun = (m3o, passed_b)
         m4o = move(i2o, across, *begun)
-        packed_b = move(pack(here, m3o, attended_b), edge, o2o, p2o, held_a[-1], *begun)
-        held_b = over_tensor(attended_b)
+        o3o = move(m3o, outward, *begun)
+        held_b = over_tensor(after(attended_b, *begun)) + over_tensor(after(passed_b, *begun))
         third_o = choose(here, after(o2o, *begun), m2o)
         p3o = move(third_o, pair, p2o)
         pieces_a = stack(here, [after(held_a[0], *begun)] + held_a[1:])
         pieces_a = (pieces_a, to_core(pieces_a))
-
-        begun = (m4o, pieces_a[0])
-        o3o, passed_b = unpack(here, after(packed_b, p3o, held_b[-1], *begun), low_o, attended_b)
-        held_b += over_tensor(passed_b)
-        fourth_o = choose(here, o3o, m4o)
-        p4o = move(fourth_o, pair, p3o)
+        both = ("partner", "own")
         blocks = [(0, mine_o, p1o), (1, second_o, p2o), (2, third_o, p3o)]
-        pieces_b = stack(here, held_b)
+        total = combine(here, both, [pieces_a + (0, blocks[:2])])
+
+        begun = (o3o, m4o, p3o, total)
+        fourth_o = choose(here, after(o3o, *begun), m4o)
+        p4o = move(fourth_o, pair)
+        pieces_b = stack(here, [after(held_b[0], fourth_o)] + held_b[1:])
         pieces_b = (pieces_b, to_core(pieces_b))
-        total = combine(
-            here, ("partner", "own"), [pieces_a + (0, blocks), pieces_b + (1, blocks)]
-        )
+        total = combine(here, both, [pieces_b + (1, blocks)], total)
         last = [(3, fourth_o, p4o)]
-        rest = [pieces_a + (0, last), pieces_b + (1, last)]
-
-        kept_away, sent_away = combine(here, ("partner",), rest, total, 0, True)
+        rest = [pieces_a + (0, blocks[2:] + last), pieces_b + (1, last)]
+
+        kept_away, sent_away = combine(here, ("partner",), rest, total, True, 0, True)
         sent_away = to_core(sent_away)
-        near = combine(here, ("own",), rest, total, 1)
+        near = combine(here, ("own",), rest, total, True, 1)
         far = move(join(here, other_kind, kept_away, sent_away), edge)
         return assemble(here, own_kind, near, to_core(near), far, to_core(far))
 

time: 294 us -> 283 us (0.963)
  starting transfers between devices: 92.7 us -> 73 us
  waiting for transfers between devices: 135 us -> 142 us
    ppermute x58, starting transfers between devices: 92.7 us -> 73 us  [move(): lax.ppermute(after(array, *earlier) if earlier else array, AXES, pairs)]
    ppermute x58, waiting for transfers between devices: 135 us -> 142 us  [move(): lax.ppermute(after(array, *earlier) if earlier else array, AXES, pairs)]
  transfers between devices with their start and end apart: 58 -> 58, of which waited for: 27 -> 29; matrix products, arithmetic and copies ran while one was open for 0% -> 0% of each run, Pallas kernels for 19% -> 20%
where the time goes in v10:
time: 283 us; the launch traced here: 282 us
  waiting for transfers between devices  142 us (50%)
  starting transfers between devices  73 us (26%)
  Pallas kernels  61.4 us (22%)
  local copies, waits for them, and re-layouts  4.34 us (2%)
    ppermute x58, waiting for transfers between devices, move(): lax.ppermute(after(array, *earlier) if earlier else array, AXES, pairs)  142 us
    ppermute x58, starting transfers between devices, move(): lax.ppermute(after(array, *earlier) if earlier else array, AXES, pairs)  73 us
    pallas_call x36, Pallas kernels, call(): pl.pallas_call(kernel, in_specs=[pl.BlockSpec(memory_space=SMEM)] + [pl.B...  59 us
  transfers between devices with their start and end apart: 58, of which 29 were waited for; matrix products, arithmetic and copies ran while one was open for 0% of the time, Pallas kernels for 20%

profile of v10, /device:TPU:0, one launch (start us, length us, event | category | flops | bytes accessed | tf_op | source)
XLA Modules:
  0.0 282.1 jit_solution(7694505196162889572)
XLA Ops:
  0.8 1.9 copy-done
  3.5 3.0 %collective-permute-start.2 = (bf16[3,512,256]{2,1,0:T(8,128)(2,1)S(1)}, bf16[3,512,256]{2,1,0:T(8,128)(2,1)S(1)}, u32[]{:S(2)}, u32[]{:S(2)}) collective-permute-start(bf16[3,512,256]{2,1,0:T(8,128)(2,1)S(1)} %get-tuple-element.92.refs_1_), channel_id=1, source_target_pairs={{0,2},{1,3},{2,0},{3,1},{4,6},{5,7},{6,4},{7,5},{8,10},{9,11},{10,... | collective-permute-start | bytes 2359304 | tf_op jit(solution)/shard_map/ppermute | solution.py:430
  8.8 15.3 %collective-permute-done.2.refs_2_ = bf16[3,512,256]{2,1,0:T(8,128)(2,1)S(1)} collective-permute-done((bf16[3,512,256]{2,1,0:T(8,128)(2,1)S(1)}, bf16[3,512,256]{2,1,0:T(8,128)(2,1)S(1)}, u32[]{:S(2)}, u32[]{:S(2)}) %collective-permute-start.2) | collective-permute-done | bytes 786464 | tf_op jit(solution)/shard_map/ppermute | solution.py:430
  26.6 7.7 %collective-permute-start.3 = (bf16[3,512,256]{2,1,0:T(8,128)(2,1)S(1)}, bf16[3,512,256]{2,1,0:T(8,128)(2,1)S(1)}, u32[]{:S(2)}, u32[]{:S(2)}) collective-permute-start(bf16[3,512,256]{2,1,0:T(8,128)(2,1)S(1)} %collective-permute-done), channel_id=1, source_target_pairs={{0,4},{1,5},{2,6},{3,7},{4,0},{5,1},{6,2},{7,3},{8,12},{9,13},{10,... | collective-permute-start | bytes 2359304 | tf_op jit(solution)/shard_map/ppermute | solution.py:430
  39.2 5.2 %collective-permute-done.4.refs_4_ = bf16[3,512,256]{2,1,0:T(8,128)(2,1)S(1)} collective-permute-done((bf16[3,512,256]{2,1,0:T(8,128)(2,1)S(1)}, bf16[3,512,256]{2,1,0:T(8,128)(2,1)S(1)}, u32[]{:S(2)}, u32[]{:S(2)}) %collective-permute-start.4) | collective-permute-done | bytes 786464 | tf_op jit(solution)/shard_map/ppermute | solution.py:430
  44.4 5.4 %collective-permute-done.3.a_ref = bf16[3,512,256]{2,1,0:T(8,128)(2,1)S(1)} collective-permute-done((bf16[3,512,256]{2,1,0:T(8,128)(2,1)S(1)}, bf16[3,512,256]{2,1,0:T(8,128)(2,1)S(1)}, u32[]{:S(2)}, u32[]{:S(2)}) %collective-permute-start.3) | collective-permute-done | bytes 786464 | tf_op jit(solution)/shard_map/ppermute | solution.py:430
  52.7 3.5 %collective-permute-start.6 = (bf16[160,2048]{1,0:T(8,128)(2,1)S(1)}, bf16[160,2048]{1,0:T(8,128)(2,1)S(1)}, u32[]{:S(2)}, u32[]{:S(2)}) collective-permute-start(bf16[160,2048]{1,0:T(8,128)(2,1)S(1)} %get-tuple-element.99), channel_id=1, source_target_pairs={{0,4},{1,5},{2,6},{3,7},{4,0},{5,1},{6,2},{7,3},{8,12},{9,13},{10,... | collective-permute-start | bytes 1966088 | tf_op jit(solution)/shard_map/ppermute | solution.py:430
  56.2 8.8 %collective-permute-done.10.refs_2_ = bf16[320,2048]{1,0:T(8,128)(2,1)S(1)} collective-permute-done((bf16[320,2048]{1,0:T(8,128)(2,1)S(1)}, bf16[320,2048]{1,0:T(8,128)(2,1)S(1)}, u32[]{:S(2)}, u32[]{:S(2)}) %collective-permute-start.10) | collective-permute-done | bytes 1310752 | tf_op jit(solution)/shard_map/ppermute | solution.py:430
  65.1 2.7 collective-permute-done.6.refs_2_
  67.8 3.3 %collective-permute-start.9 = (bf16[176,2048]{1,0:T(8,128)(2,1)S(1)}, bf16[176,2048]{1,0:T(8,128)(2,1)S(1)}, u32[]{:S(2)}, u32[]{:S(2)}) collective-permute-start(bf16[176,2048]{1,0:T(8,128)(2,1)S(1)} %get-tuple-element.103), channel_id=1, source_target_pairs={{0,4},{1,5},{2,6},{3,7},{4,0},{5,1},{6,2},{7,3},{8,12},{9,13},{10,... | collective-permute-start | bytes 2162696 | tf_op jit(solution)/shard_map/ppermute | solution.py:430
  76.3 3.2 %normalize.3.refs_0_ = bf16[2,8,640,512]{3,2,1,0:T(8,128)(2,1)S(1)} custom-call(s32[3]{0:T(128)S(1)} %pad_add_fusion.h_ref._, f32[8,1,512]{2,1,0:T(1,128)S(1)} %bitcast.9, bf16[640,2048]{1,0:T(8,128)(2,1)S(1)} %copy-done.3, bf16[320,2048]{1,0:T(8,128)(2,1)S(1)} %collective-permute-done.10.refs_2_, bf16[320,2048]{1,0:T(8,128)(2,1)S(1)} %collective-permute-done.11.refs_3_), custom_call_target="tpu_custom_call" | custom-call | tf_op jit(solution)/shard_map/normalize/pallas_call | solution.py:32
  79.5 7.2 %collective-permute-done.12.refs_3_ = bf16[160,2048]{1,0:T(8,128)(2,1)S(1)} collective-permute-done((bf16[160,2048]{1,0:T(8,128)(2,1)S(1)}, bf16[160,2048]{1,0:T(8,128)(2,1)S(1)}, u32[]{:S(2)}, u32[]{:S(2)}) %collective-permute-start.12) | collective-permute-done | bytes 655392 | tf_op jit(solution)/shard_map/ppermute | solution.py:430
  87.9 2.8 collective-permute-done.22.refs_2_
  94.1 4.6 %collective-permute-start.25 = (bf16[1,256,1024]{2,1,0:T(8,128)(2,1)S(1)}, bf16[1,256,1024]{2,1,0:T(8,128)(2,1)S(1)}, u32[]{:S(2)}, u32[]{:S(2)}) collective-permute-start(bf16[1,256,1024]{2,1,0:T(8,128)(2,1)S(1)} %get-tuple-element.138.block_ref), channel_id=1, source_target_pairs={{0,4},{1,5},{2,6},{3,7},{12,8},{13,9},{14,10},{15,11},{16,20},{17,... | collective-permute-start | bytes 1572872 | tf_op jit(solution)/shard_map/ppermute | solution.py:430
  99.2 3.7 %project.10.refs_7_ = f32[2,640,768]{2,1,0:T(8,128)S(1)} custom-call(s32[3]{0:T(128)S(1)} %pad_add_fusion.h_ref._, bf16[2,8,640,512]{3,2,1,0:T(8,128)(2,1)S(1)} %normalize.3.refs_0_, bf16[3,512,256]{2,1,0:T(8,128)(2,1)S(1)} %get-tuple-element.92.refs_1_, bf16[3,512,256]{2,1,0:T(8,128)(2,1)S(1)} %collective-permute-done.2.refs_2_, ...), custom_call_target="tpu_custom_call" | custom-call | tf_op jit(solution)/shard_map/project/pallas_call | solution.py:32
  103.0 1.8 normalize.4.refs_0_
  105.5 4.8 %collective-permute-done.21.a_ref = bf16[3,512,256]{2,1,0:T(8,128)(2,1)S(1)} collective-permute-done((bf16[3,512,256]{2,1,0:T(8,128)(2,1)S(1)}, bf16[3,512,256]{2,1,0:T(8,128)(2,1)S(1)}, u32[]{:S(2)}, u32[]{:S(2)}) %collective-permute-start.21) | collective-permute-done | bytes 786464 | tf_op jit(solution)/shard_map/ppermute | solution.py:430
  110.4 3.5 %collective-permute-start.26 = (bf16[3,512,256]{2,1,0:T(8,128)(2,1)S(1)}, bf16[3,512,256]{2,1,0:T(8,128)(2,1)S(1)}, u32[]{:S(2)}, u32[]{:S(2)}) collective-permute-start(bf16[3,512,256]{2,1,0:T(8,128)(2,1)S(1)} %collective-permute-done.17), channel_id=1, source_target_pairs={{0,4},{1,5},{2,6},{3,7},{4,0},{5,1},{6,2},{7,3},{8,12},{9,13},{10,... | collective-permute-start | bytes 2359304 | tf_op jit(solution)/shard_map/ppermute | solution.py:430
  118.5 1.8 normalize.5.refs_0_
  120.3 3.7 %project.11.refs_3_ = f32[2,640,768]{2,1,0:T(8,128)S(1)} custom-call(s32[3]{0:T(128)S(1)} %pad_add_fusion.h_ref._, bf16[2,8,640,512]{3,2,1,0:T(8,128)(2,1)S(1)} %normalize.5.refs_0_, bf16[3,512,256]{2,1,0:T(8,128)(2,1)S(1)} %get-tuple-element.92.refs_1_, bf16[3,512,256]{2,1,0:T(8,128)(2,1)S(1)} %collective-permute-done.2.refs_2_, ...), custom_call_target="tpu_custom_call", output_to_operand_aliasing={{}: (8, {})} | custom-call | tf_op jit(solution)/shard_map/project/pallas_call | solution.py:32
  124.0 6.7 %collective-permute-done.26.a_ref = bf16[3,512,256]{2,1,0:T(8,128)(2,1)S(1)} collective-permute-done((bf16[3,512,256]{2,1,0:T(8,128)(2,1)S(1)}, bf16[3,512,256]{2,1,0:T(8,128)(2,1)S(1)}, u32[]{:S(2)}, u32[]{:S(2)}) %collective-permute-start.26) | collective-permute-done | bytes 786464 | tf_op jit(solution)/shard_map/ppermute | solution.py:430
  132.8 2.7 collective-permute-start.29
  140.2 11.0 %collective-permute-done.29.refs_1_ = bf16[3,512,256]{2,1,0:T(8,128)(2,1)S(1)} collective-permute-done((bf16[3,512,256]{2,1,0:T(8,128)(2,1)S(1)}, bf16[3,512,256]{2,1,0:T(8,128)(2,1)S(1)}, u32[]{:S(2)}, u32[]{:S(2)}) %collective-permute-start.29) | collective-permute-done | bytes 786464 | tf_op jit(solution)/shard_map/ppermute | solution.py:430
  155.0 4.8 %collective-permute-start.38 = (bf16[1,256,1024]{2,1,0:T(8,128)(2,1)S(1)}, bf16[1,256,1024]{2,1,0:T(8,128)(2,1)S(1)}, u32[]{:S(2)}, u32[]{:S(2)}) collective-permute-start(bf16[1,256,1024]{2,1,0:T(8,128)(2,1)S(1)} %get-tuple-element.146), channel_id=1, source_target_pairs={{0,4},{1,5},{2,6},{3,7},{12,8},{13,9},{14,10},{15,11},{16,20},{17,... | collective-permute-start | bytes 1572872 | tf_op jit(solution)/shard_map/ppermute | solution.py:430
  159.8 2.7 project.14.refs_5_
  162.5 2.7 project.15.refs_3_
  165.3 4.2 %attend.2.piece_ref.refs_0_ = bf16[640,256]{1,0:T(8,128)(2,1)S(1)} custom-call(s32[3]{0:T(128)S(1)} %pad_add_fusion.h_ref._, s32[1,640]{1,0:T(1,128)S(1)} %broadcast_in_dim.3.kind_ref.own_kind_ref, s32[1,640]{1,0:T(1,128)S(1)} %kinds_behind.1.other_kind_ref.kind_ref, bf16[640,768]{1,0:T(8,128)(2,1)S(1)} %project.12.own_ref, ...), custom_call_target="tpu_custom_call" | custom-call | tf_op jit(solution)/shard_map/attend/pallas_call | solution.py:32
  169.4 2.1 collective-permute-done.35.a_ref
  172.9 3.2 %collective-permute-start.39 = (bf16[1664,256]{1,0:T(8,128)(2,1)S(1)}, bf16[1664,256]{1,0:T(8,128)(2,1)S(1)}, u32[]{:S(2)}, u32[]{:S(2)}) collective-permute-start(bf16[1664,256]{1,0:T(8,128)(2,1)S(1)} %pack.1), channel_id=1, source_target_pairs={{0,4},{1,5},{2,6},{3,7},{4,0},{5,1},{6,2},{7,3},{8,12},{9,13},{10,... | collective-permute-start | bytes 2555912 | tf_op jit(solution)/shard_map/ppermute | solution.py:430
  177.4 1.9 project.16.refs_3_
  179.4 1.9 project.17.refs_3_
  181.3 6.4 %collective-permute-done.37.refs_2_ = bf16[3,512,256]{2,1,0:T(8,128)(2,1)S(1)} collective-permute-done((bf16[3,512,256]{2,1,0:T(8,128)(2,1)S(1)}, bf16[3,512,256]{2,1,0:T(8,128)(2,1)S(1)}, u32[]{:S(2)}, u32[]{:S(2)}) %collective-permute-start.37) | collective-permute-done | bytes 786464 | tf_op jit(solution)/shard_map/ppermute | solution.py:430
  196.3 3.8 %collective-permute-done.32.refs_1_ = bf16[640,256]{1,0:T(8,128)(2,1)S(1)} collective-permute-done((bf16[640,256]{1,0:T(8,128)(2,1)S(1)}, bf16[640,256]{1,0:T(8,128)(2,1)S(1)}, u32[]{:S(2)}, u32[]{:S(2)}) %collective-permute-start.32) | collective-permute-done | bytes 327712 | tf_op jit(solution)/shard_map/ppermute | solution.py:430
  200.8 4.2 %attend.3.refs_0_ = bf16[640,256]{1,0:T(8,128)(2,1)S(1)} custom-call(s32[3]{0:T(128)S(1)} %pad_add_fusion.h_ref._, s32[1,640]{1,0:T(1,128)S(1)} %broadcast_in_dim.3.kind_ref.own_kind_ref, s32[1,640]{1,0:T(1,128)S(1)} %kinds_behind.1.other_kind_ref.kind_ref, bf16[640,768]{1,0:T(8,128)(2,1)S(1)} %project.18.own_ref, ...), custom_call_target="tpu_custom_call" | custom-call | tf_op jit(solution)/shard_map/attend/pallas_call | solution.py:32
  206.9 2.8 %collective-permute-done.42.a_ref = bf16[1,256,1024]{2,1,0:T(8,128)(2,1)S(1)} collective-permute-done((bf16[1,256,1024]{2,1,0:T(8,128)(2,1)S(1)}, bf16[1,256,1024]{2,1,0:T(8,128)(2,1)S(1)}, u32[]{:S(2)}, u32[]{:S(2)}) %collective-permute-start.42) | collective-permute-done | bytes 524320 | tf_op jit(solution)/shard_map/ppermute | solution.py:430
  209.9 7.8 %collective-permute-done.45.refs_2_ = bf16[640,256]{1,0:T(8,128)(2,1)S(1)} collective-permute-done((bf16[640,256]{1,0:T(8,128)(2,1)S(1)}, bf16[640,256]{1,0:T(8,128)(2,1)S(1)}, u32[]{:S(2)}, u32[]{:S(2)}) %collective-permute-start.45) | collective-permute-done | bytes 327712 | tf_op jit(solution)/shard_map/ppermute | solution.py:430
  221.4 3.4 %collective-permute-start.51 = (bf16[640,256]{1,0:T(8,128)(2,1)S(1)}, bf16[640,256]{1,0:T(8,128)(2,1)S(1)}, u32[]{:S(2)}, u32[]{:S(2)}) collective-permute-start(bf16[640,256]{1,0:T(8,128)(2,1)S(1)} %collective-permute-done.45.refs_2_), channel_id=1, source_target_pairs={{0,1},{1,0},{2,3},{3,2},{4,5},{5,4},{6,7},{7,6},{8,9},{9,8},{10,11... | collective-permute-start | bytes 983048 | tf_op jit(solution)/shard_map/ppermute | solution.py:430
  224.9 2.1 combine.4.refs_12_
  226.9 6.4 %collective-permute-done.49.refs_11_.refs_7_ = bf16[1,256,1024]{2,1,0:T(8,128)(2,1)S(1)} collective-permute-done((bf16[1,256,1024]{2,1,0:T(8,128)(2,1)S(1)}, bf16[1,256,1024]{2,1,0:T(8,128)(2,1)S(1)}, u32[]{:S(2)}, u32[]{:S(2)}) %collective-permute-start.49) | collective-permute-done | bytes 524320 | tf_op jit(solution)/shard_map/ppermute | solution.py:430
  233.4 3.8 %collective-permute-done.47.a_ref = bf16[1,256,1024]{2,1,0:T(8,128)(2,1)S(1)} collective-permute-done((bf16[1,256,1024]{2,1,0:T(8,128)(2,1)S(1)}, bf16[1,256,1024]{2,1,0:T(8,128)(2,1)S(1)}, u32[]{:S(2)}, u32[]{:S(2)}) %collective-permute-start.47) | collective-permute-done | bytes 524320 | tf_op jit(solution)/shard_map/ppermute | solution.py:430
  237.8 2.1 collective-permute-done.50.refs_1_
  241.0 2.6 collective-permute-done.52.refs_1_.refs_3_.refs_5_
  243.6 2.8 combine.5.refs_12_
  246.4 8.5 %collective-permute-done.53.refs_9_.refs_11_ = bf16[1,256,1024]{2,1,0:T(8,128)(2,1)S(1)} collective-permute-done((bf16[1,256,1024]{2,1,0:T(8,128)(2,1)S(1)}, bf16[1,256,1024]{2,1,0:T(8,128)(2,1)S(1)}, u32[]{:S(2)}, u32[]{:S(2)}) %collective-permute-start.53) | collective-permute-done | bytes 524320 | tf_op jit(solution)/shard_map/ppermute | solution.py:430
  260.0 2.5 collective-permute-start.56
  262.5 14.9 %collective-permute-done.56.c_ref = bf16[320,1024]{1,0:T(8,128)(2,1)S(1)} collective-permute-done((bf16[320,1024]{1,0:T(8,128)(2,1)S(1)}, bf16[320,1024]{1,0:T(8,128)(2,1)S(1)}, u32[]{:S(2)}, u32[]{:S(2)}) %collective-permute-start.56) | collective-permute-done | bytes 655392 | tf_op jit(solution)/shard_map/ppermute | solution.py:430
  277.4 2.1 collective-permute-done.57.d_ref
  279.5 2.4 shard_map.55
  (119 shorter events, 64.6 us)
Async XLA Ops:
  3.5 20.6 %collective-permute-start.2 = (bf16[3,512,256]{2,1,0:T(8,128)(2,1)S(1)}, bf16[3,512,256]{2,1,0:T(8,128)(2,1)S(1)}, u32[]{:S(2)}, u32[]{:S(2)}) collective-permute-start(bf16[3,512,256]{2,1,0:T(8,128)(2,1)S(1)} %get-tuple-element.92.refs_1_), channel_id=1, source_target_pairs={{0,2},{1,3},{2,0},{3,1},{4,6},{5,7},{6,4},{7,5},{8,10},{9,11},{10,... | collective-permute-start | bytes 2359304 | tf_op jit(solution)/shard_map/ppermute | solution.py:430
  6.5 19.0 %collective-permute-start.1 = (bf16[3,512,256]{2,1,0:T(8,128)(2,1)S(1)}, bf16[3,512,256]{2,1,0:T(8,128)(2,1)S(1)}, u32[]{:S(2)}, u32[]{:S(2)}) collective-permute-start(bf16[3,512,256]{2,1,0:T(8,128)(2,1)S(1)} %get-tuple-element.91), channel_id=1, source_target_pairs={{0,4},{1,5},{2,6},{3,7},{4,0},{5,1},{6,2},{7,3},{8,12},{9,13},{10,... | collective-permute-start | bytes 2359304 | tf_op jit(solution)/shard_map/ppermute | solution.py:430
  8.1 17.4 %collective-permute-start = (bf16[3,512,256]{2,1,0:T(8,128)(2,1)S(1)}, bf16[3,512,256]{2,1,0:T(8,128)(2,1)S(1)}, u32[]{:S(2)}, u32[]{:S(2)}) collective-permute-start(bf16[3,512,256]{2,1,0:T(8,128)(2,1)S(1)} %get-tuple-element.87), channel_id=1, source_target_pairs={{0,0},{1,1},{2,2},{3,3},{4,8},{5,9},{6,10},{7,11},{8,4},{9,5},{10,... | collective-permute-start | bytes 2359304 | tf_op jit(solution)/shard_map/ppermute | solution.py:430
  25.5 13.7 %collective-permute-start.5 = (bf16[3,512,256]{2,1,0:T(8,128)(2,1)S(1)}, bf16[3,512,256]{2,1,0:T(8,128)(2,1)S(1)}, u32[]{:S(2)}, u32[]{:S(2)}) collective-permute-start(bf16[3,512,256]{2,1,0:T(8,128)(2,1)S(1)} %get-tuple-element.96), channel_id=1, source_target_pairs={{4,8},{5,9},{6,10},{7,11},{8,4},{9,5},{10,6},{11,7},{20,24},{21,25... | collective-permute-start | bytes 2359304 | tf_op jit(solution)/shard_map/ppermute | solution.py:430
  26.2 18.2 %collective-permute-start.4 = (bf16[3,512,256]{2,1,0:T(8,128)(2,1)S(1)}, bf16[3,512,256]{2,1,0:T(8,128)(2,1)S(1)}, u32[]{:S(2)}, u32[]{:S(2)}) collective-permute-start(bf16[3,512,256]{2,1,0:T(8,128)(2,1)S(1)} %collective-permute-done.1.refs_3_), channel_id=1, source_target_pairs={{0,2},{1,3},{2,0},{3,1},{4,6},{5,7},{6,4},{7,5},{8,10},{9,11},{10,... | collective-permute-start | bytes 2359304 | tf_op jit(solution)/shard_map/ppermute | solution.py:430
  26.6 23.2 %collective-permute-start.3 = (bf16[3,512,256]{2,1,0:T(8,128)(2,1)S(1)}, bf16[3,512,256]{2,1,0:T(8,128)(2,1)S(1)}, u32[]{:S(2)}, u32[]{:S(2)}) collective-permute-start(bf16[3,512,256]{2,1,0:T(8,128)(2,1)S(1)} %collective-permute-done), channel_id=1, source_target_pairs={{0,4},{1,5},{2,6},{3,7},{4,0},{5,1},{6,2},{7,3},{8,12},{9,13},{10,... | collective-permute-start | bytes 2359304 | tf_op jit(solution)/shard_map/ppermute | solution.py:430
  36.8 28.3 %collective-permute-start.10 = (bf16[320,2048]{1,0:T(8,128)(2,1)S(1)}, bf16[320,2048]{1,0:T(8,128)(2,1)S(1)}, u32[]{:S(2)}, u32[]{:S(2)}) collective-permute-start(bf16[320,2048]{1,0:T(8,128)(2,1)S(1)} %get-tuple-element.105), channel_id=1, source_target_pairs={{0,1},{1,0},{2,3},{3,2},{4,5},{5,4},{6,7},{7,6},{8,9},{9,8},{10,11... | collective-permute-start | bytes 3932168 | tf_op jit(solution)/shard_map/ppermute | solution.py:430
  49.8 15.3 %collective-permute-start.8 = (bf16[3,512,256]{2,1,0:T(8,128)(2,1)S(1)}, bf16[3,512,256]{2,1,0:T(8,128)(2,1)S(1)}, u32[]{:S(2)}, u32[]{:S(2)}) collective-permute-start(bf16[3,512,256]{2,1,0:T(8,128)(2,1)S(1)} %collective-permute-done.3.a_ref), channel_id=1, source_target_pairs={{4,8},{5,9},{6,10},{7,11},{8,4},{9,5},{10,6},{11,7},{20,24},{21,25... | collective-permute-start | bytes 2359304 | tf_op jit(solution)/shard_map/ppermute | solution.py:430
  51.1 16.7 %collective-permute-start.7 = (bf16[3,512,256]{2,1,0:T(8,128)(2,1)S(1)}, bf16[3,512,256]{2,1,0:T(8,128)(2,1)S(1)}, u32[]{:S(2)}, u32[]{:S(2)}) collective-permute-start(bf16[3,512,256]{2,1,0:T(8,128)(2,1)S(1)} %choose.7.refs_5_), channel_id=1, source_target_pairs={{0,2},{1,3},{2,0},{3,1},{4,6},{5,7},{6,4},{7,5},{8,10},{9,11},{10,... | collective-permute-start | bytes 2359304 | tf_op jit(solution)/shard_map/ppermute | solution.py:430
  52.7 15.0 %collective-permute-start.6 = (bf16[160,2048]{1,0:T(8,128)(2,1)S(1)}, bf16[160,2048]{1,0:T(8,128)(2,1)S(1)}, u32[]{:S(2)}, u32[]{:S(2)}) collective-permute-start(bf16[160,2048]{1,0:T(8,128)(2,1)S(1)} %get-tuple-element.99), channel_id=1, source_target_pairs={{0,4},{1,5},{2,6},{3,7},{4,0},{5,1},{6,2},{7,3},{8,12},{9,13},{10,... | collective-permute-start | bytes 1966088 | tf_op jit(solution)/shard_map/ppermute | solution.py:430
  65.1 11.2 %collective-permute-start.11 = (bf16[320,2048]{1,0:T(8,128)(2,1)S(1)}, bf16[320,2048]{1,0:T(8,128)(2,1)S(1)}, u32[]{:S(2)}, u32[]{:S(2)}) collective-permute-start(bf16[320,2048]{1,0:T(8,128)(2,1)S(1)} %collective-permute-done.10.refs_2_), channel_id=1, source_target_pairs={{0,16},{1,17},{2,18},{3,19},{4,20},{5,21},{6,22},{7,23},{8,24},{9,... | collective-permute-start | bytes 3932168 | tf_op jit(solution)/shard_map/ppermute | solution.py:430
  67.8 18.9 %collective-permute-start.9 = (bf16[176,2048]{1,0:T(8,128)(2,1)S(1)}, bf16[176,2048]{1,0:T(8,128)(2,1)S(1)}, u32[]{:S(2)}, u32[]{:S(2)}) collective-permute-start(bf16[176,2048]{1,0:T(8,128)(2,1)S(1)} %get-tuple-element.103), channel_id=1, source_target_pairs={{0,4},{1,5},{2,6},{3,7},{4,0},{5,1},{6,2},{7,3},{8,12},{9,13},{10,... | collective-permute-start | bytes 2162696 | tf_op jit(solution)/shard_map/ppermute | solution.py:430
  71.1 15.6 %collective-permute-start.12 = (bf16[160,2048]{1,0:T(8,128)(2,1)S(1)}, bf16[160,2048]{1,0:T(8,128)(2,1)S(1)}, u32[]{:S(2)}, u32[]{:S(2)}) collective-permute-start(bf16[160,2048]{1,0:T(8,128)(2,1)S(1)} %collective-permute-done.6.refs_2_), channel_id=1, source_target_pairs={{0,1},{1,0},{2,3},{3,2},{4,5},{5,4},{6,7},{7,6},{8,9},{9,8},{10,11... | collective-permute-start | bytes 1966088 | tf_op jit(solution)/shard_map/ppermute | solution.py:430
  72.6 18.1 %collective-permute-start.22 = (bf16[3,512,256]{2,1,0:T(8,128)(2,1)S(1)}, bf16[3,512,256]{2,1,0:T(8,128)(2,1)S(1)}, u32[]{:S(2)}, u32[]{:S(2)}) collective-permute-start(bf16[3,512,256]{2,1,0:T(8,128)(2,1)S(1)} %get-tuple-element.124.refs_1_), channel_id=1, source_target_pairs={{0,2},{1,3},{2,0},{3,1},{4,6},{5,7},{6,4},{7,5},{8,10},{9,11},{10,... | collective-permute-start | bytes 2359304 | tf_op jit(solution)/shard_map/ppermute | solution.py:430
  74.1 17.9 %collective-permute-start.16 = (bf16[3,512,256]{2,1,0:T(8,128)(2,1)S(1)}, bf16[3,512,256]{2,1,0:T(8,128)(2,1)S(1)}, u32[]{:S(2)}, u32[]{:S(2)}) collective-permute-start(bf16[3,512,256]{2,1,0:T(8,128)(2,1)S(1)} %collective-permute-done.1.refs_3_), channel_id=1, source_target_pairs={{4,8},{5,9},{6,10},{7,11},{8,4},{9,5},{10,6},{11,7},{20,24},{21,25... | collective-permute-start | bytes 2359304 | tf_op jit(solution)/shard_map/ppermute | solution.py:430
  87.2 17.6 %collective-permute-start.17 = (bf16[3,512,256]{2,1,0:T(8,128)(2,1)S(1)}, bf16[3,512,256]{2,1,0:T(8,128)(2,1)S(1)}, u32[]{:S(2)}, u32[]{:S(2)}) collective-permute-start(bf16[3,512,256]{2,1,0:T(8,128)(2,1)S(1)} %get-tuple-element.115), channel_id=1, source_target_pairs={{0,0},{1,1},{2,2},{3,3},{4,8},{5,9},{6,10},{7,11},{8,4},{9,5},{10,... | collective-permute-start | bytes 2359304 | tf_op jit(solution)/shard_map/ppermute | solution.py:430
  90.7 19.7 %collective-permute-start.21 = (bf16[3,512,256]{2,1,0:T(8,128)(2,1)S(1)}, bf16[3,512,256]{2,1,0:T(8,128)(2,1)S(1)}, u32[]{:S(2)}, u32[]{:S(2)}) collective-permute-start(bf16[3,512,256]{2,1,0:T(8,128)(2,1)S(1)} %collective-permute-done.8), channel_id=1, source_target_pairs={{4,0},{5,1},{6,2},{7,3},{8,12},{9,13},{10,14},{11,15},{20,16},{21,... | collective-permute-start | bytes 2359304 | tf_op jit(solution)/shard_map/ppermute | solution.py:430
  92.0 18.4 %collective-permute-start.15 = (bf16[176,2048]{1,0:T(8,128)(2,1)S(1)}, bf16[176,2048]{1,0:T(8,128)(2,1)S(1)}, u32[]{:S(2)}, u32[]{:S(2)}) collective-permute-start(bf16[176,2048]{1,0:T(8,128)(2,1)S(1)} %collective-permute-done.9.in_ref.refs_2_), channel_id=1, source_target_pairs={{0,1},{1,0},{2,3},{3,2},{4,5},{5,4},{6,7},{7,6},{8,9},{9,8},{10,11... | collective-permute-start | bytes 2162696 | tf_op jit(solution)/shard_map/ppermute | solution.py:430
  92.6 17.8 %collective-permute-start.23 = (bf16[1,256,1024]{2,1,0:T(8,128)(2,1)S(1)}, bf16[1,256,1024]{2,1,0:T(8,128)(2,1)S(1)}, u32[]{:S(2)}, u32[]{:S(2)}) collective-permute-start(bf16[1,256,1024]{2,1,0:T(8,128)(2,1)S(1)} %get-tuple-element.125.refs_4_.refs_6_), channel_id=1, source_target_pairs={{0,2},{1,3},{2,0},{3,1},{4,6},{5,7},{6,4},{7,5},{8,10},{9,11},{10,... | collective-permute-start | bytes 1572872 | tf_op jit(solution)/shard_map/ppermute | solution.py:430
  94.1 16.3 %collective-permute-start.25 = (bf16[1,256,1024]{2,1,0:T(8,128)(2,1)S(1)}, bf16[1,256,1024]{2,1,0:T(8,128)(2,1)S(1)}, u32[]{:S(2)}, u32[]{:S(2)}) collective-permute-start(bf16[1,256,1024]{2,1,0:T(8,128)(2,1)S(1)} %get-tuple-element.138.block_ref), channel_id=1, source_target_pairs={{0,4},{1,5},{2,6},{3,7},{12,8},{13,9},{14,10},{15,11},{16,20},{17,... | collective-permute-start | bytes 1572872 | tf_op jit(solution)/shard_map/ppermute | solution.py:430
  104.8 19.2 %collective-permute-start.20 = (bf16[3,512,256]{2,1,0:T(8,128)(2,1)S(1)}, bf16[3,512,256]{2,1,0:T(8,128)(2,1)S(1)}, u32[]{:S(2)}, u32[]{:S(2)}) collective-permute-start(bf16[3,512,256]{2,1,0:T(8,128)(2,1)S(1)} %get-tuple-element.120), channel_id=1, source_target_pairs={{4,8},{5,9},{6,10},{7,11},{8,4},{9,5},{10,6},{11,7},{20,24},{21,25... | collective-permute-start | bytes 2359304 | tf_op jit(solution)/shard_map/ppermute | solution.py:430
  110.4 20.3 %collective-permute-start.26 = (bf16[3,512,256]{2,1,0:T(8,128)(2,1)S(1)}, bf16[3,512,256]{2,1,0:T(8,128)(2,1)S(1)}, u32[]{:S(2)}, u32[]{:S(2)}) collective-permute-start(bf16[3,512,256]{2,1,0:T(8,128)(2,1)S(1)} %collective-permute-done.17), channel_id=1, source_target_pairs={{0,4},{1,5},{2,6},{3,7},{4,0},{5,1},{6,2},{7,3},{8,12},{9,13},{10,... | collective-permute-start | bytes 2359304 | tf_op jit(solution)/shard_map/ppermute | solution.py:430
  114.5 18.4 %collective-permute-start.24 = (bf16[3,512,256]{2,1,0:T(8,128)(2,1)S(1)}, bf16[3,512,256]{2,1,0:T(8,128)(2,1)S(1)}, u32[]{:S(2)}, u32[]{:S(2)}) collective-permute-start(bf16[3,512,256]{2,1,0:T(8,128)(2,1)S(1)} %choose.8.refs_1_), channel_id=1, source_target_pairs={{0,2},{1,3},{2,0},{3,1},{4,6},{5,7},{6,4},{7,5},{8,10},{9,11},{10,... | collective-permute-start | bytes 2359304 | tf_op jit(solution)/shard_map/ppermute | solution.py:430
  132.8 18.4 %collective-permute-start.29 = (bf16[3,512,256]{2,1,0:T(8,128)(2,1)S(1)}, bf16[3,512,256]{2,1,0:T(8,128)(2,1)S(1)}, u32[]{:S(2)}, u32[]{:S(2)}) collective-permute-start(bf16[3,512,256]{2,1,0:T(8,128)(2,1)S(1)} %get-tuple-element.133), channel_id=1, source_target_pairs={{0,4},{1,5},{2,6},{3,7},{4,0},{5,1},{6,2},{7,3},{8,12},{9,13},{10,... | collective-permute-start | bytes 2359304 | tf_op jit(solution)/shard_map/ppermute | solution.py:430
  136.2 17.2 %collective-permute-start.31 = (bf16[3,512,256]{2,1,0:T(8,128)(2,1)S(1)}, bf16[3,512,256]{2,1,0:T(8,128)(2,1)S(1)}, u32[]{:S(2)}, u32[]{:S(2)}) collective-permute-start(bf16[3,512,256]{2,1,0:T(8,128)(2,1)S(1)} %choose.9.refs_3_), channel_id=1, source_target_pairs={{0,2},{1,3},{2,0},{3,1},{4,6},{5,7},{6,4},{7,5},{8,10},{9,11},{10,... | collective-permute-start | bytes 2359304 | tf_op jit(solution)/shard_map/ppermute | solution.py:430
  138.4 26.9 %collective-permute-start.28 = (bf16[640,768]{1,0:T(8,128)(2,1)S(1)}, bf16[640,768]{1,0:T(8,128)(2,1)S(1)}, u32[]{:S(2)}, u32[]{:S(2)}) collective-permute-start(bf16[640,768]{1,0:T(8,128)(2,1)S(1)} %project.13), channel_id=1, source_target_pairs={{0,16},{1,17},{2,18},{3,19},{4,20},{5,21},{6,22},{7,23},{8,24},{9,... | collective-permute-start | bytes 2949128 | tf_op jit(solution)/shard_map/ppermute | solution.py:430
  151.2 18.2 %collective-permute-start.30 = (bf16[3,512,256]{2,1,0:T(8,128)(2,1)S(1)}, bf16[3,512,256]{2,1,0:T(8,128)(2,1)S(1)}, u32[]{:S(2)}, u32[]{:S(2)}) collective-permute-start(bf16[3,512,256]{2,1,0:T(8,128)(2,1)S(1)} %collective-permute-done.29.refs_1_), channel_id=1, source_target_pairs={{4,8},{5,9},{6,10},{7,11},{8,4},{9,5},{10,6},{11,7},{20,24},{21,25... | collective-permute-start | bytes 2359304 | tf_op jit(solution)/shard_map/ppermute | solution.py:430
  153.3 18.2 %collective-permute-start.35 = (bf16[3,512,256]{2,1,0:T(8,128)(2,1)S(1)}, bf16[3,512,256]{2,1,0:T(8,128)(2,1)S(1)}, u32[]{:S(2)}, u32[]{:S(2)}) collective-permute-start(bf16[3,512,256]{2,1,0:T(8,128)(2,1)S(1)} %collective-permute-done.27), channel_id=1, source_target_pairs={{4,0},{5,1},{6,2},{7,3},{8,12},{9,13},{10,14},{11,15},{20,16},{21,... | collective-permute-start | bytes 2359304 | tf_op jit(solution)/shard_map/ppermute | solution.py:430
  154.6 17.5 %collective-permute-start.36 = (bf16[3,512,256]{2,1,0:T(8,128)(2,1)S(1)}, bf16[3,512,256]{2,1,0:T(8,128)(2,1)S(1)}, u32[]{:S(2)}, u32[]{:S(2)}) collective-permute-start(bf16[3,512,256]{2,1,0:T(8,128)(2,1)S(1)} %collective-permute-done.29.refs_1_), channel_id=1, source_target_pairs={{0,2},{1,3},{2,0},{3,1},{4,6},{5,7},{6,4},{7,5},{8,10},{9,11},{10,... | collective-permute-start | bytes 2359304 | tf_op jit(solution)/shard_map/ppermute | solution.py:430
  155.0 17.9 %collective-permute-start.38 = (bf16[1,256,1024]{2,1,0:T(8,128)(2,1)S(1)}, bf16[1,256,1024]{2,1,0:T(8,128)(2,1)S(1)}, u32[]{:S(2)}, u32[]{:S(2)}) collective-permute-start(bf16[1,256,1024]{2,1,0:T(8,128)(2,1)S(1)} %get-tuple-element.146), channel_id=1, source_target_pairs={{0,4},{1,5},{2,6},{3,7},{12,8},{13,9},{14,10},{15,11},{16,20},{17,... | collective-permute-start | bytes 1572872 | tf_op jit(solution)/shard_map/ppermute | solution.py:430
  172.2 15.6 %collective-permute-start.37 = (bf16[3,512,256]{2,1,0:T(8,128)(2,1)S(1)}, bf16[3,512,256]{2,1,0:T(8,128)(2,1)S(1)}, u32[]{:S(2)}, u32[]{:S(2)}) collective-permute-start(bf16[3,512,256]{2,1,0:T(8,128)(2,1)S(1)} %choose.10.refs_1_), channel_id=1, source_target_pairs={{0,2},{1,3},{2,0},{3,1},{4,6},{5,7},{6,4},{7,5},{8,10},{9,11},{10,... | collective-permute-start | bytes 2359304 | tf_op jit(solution)/shard_map/ppermute | solution.py:430
  172.9 18.5 %collective-permute-start.39 = (bf16[1664,256]{1,0:T(8,128)(2,1)S(1)}, bf16[1664,256]{1,0:T(8,128)(2,1)S(1)}, u32[]{:S(2)}, u32[]{:S(2)}) collective-permute-start(bf16[1664,256]{1,0:T(8,128)(2,1)S(1)} %pack.1), channel_id=1, source_target_pairs={{0,4},{1,5},{2,6},{3,7},{4,0},{5,1},{6,2},{7,3},{8,12},{9,13},{10,... | collective-permute-start | bytes 2555912 | tf_op jit(solution)/shard_map/ppermute | solution.py:430
  176.1 18.0 %collective-permute-start.34 = (bf16[1,256,1024]{2,1,0:T(8,128)(2,1)S(1)}, bf16[1,256,1024]{2,1,0:T(8,128)(2,1)S(1)}, u32[]{:S(2)}, u32[]{:S(2)}) collective-permute-start(bf16[1,256,1024]{2,1,0:T(8,128)(2,1)S(1)} %get-tuple-element.146), channel_id=1, source_target_pairs={{4,8},{5,9},{6,10},{7,11},{8,4},{9,5},{10,6},{11,7},{20,24},{21,25... | collective-permute-start | bytes 1572872 | tf_op jit(solution)/shard_map/ppermute | solution.py:430
  176.7 17.3 %collective-permute-start.33 = (bf16[1,256,1024]{2,1,0:T(8,128)(2,1)S(1)}, bf16[1,256,1024]{2,1,0:T(8,128)(2,1)S(1)}, u32[]{:S(2)}, u32[]{:S(2)}) collective-permute-start(bf16[1,256,1024]{2,1,0:T(8,128)(2,1)S(1)} %get-tuple-element.138.block_ref), channel_id=1, source_target_pairs={{4,8},{5,9},{6,10},{7,11},{8,4},{9,5},{10,6},{11,7},{20,24},{21,25... | collective-permute-start | bytes 1572872 | tf_op jit(solution)/shard_map/ppermute | solution.py:430
  189.4 11.3 %collective-permute-start.41 = (bf16[640,768]{1,0:T(8,128)(2,1)S(1)}, bf16[640,768]{1,0:T(8,128)(2,1)S(1)}, u32[]{:S(2)}, u32[]{:S(2)}) collective-permute-start(bf16[640,768]{1,0:T(8,128)(2,1)S(1)} %project.19), channel_id=1, source_target_pairs={{0,16},{1,17},{2,18},{3,19},{4,20},{5,21},{6,22},{7,23},{8,24},{9,... | collective-permute-start | bytes 2949128 | tf_op jit(solution)/shard_map/ppermute | solution.py:430
  189.5 10.6 %collective-permute-start.32 = (bf16[640,256]{1,0:T(8,128)(2,1)S(1)}, bf16[640,256]{1,0:T(8,128)(2,1)S(1)}, u32[]{:S(2)}, u32[]{:S(2)}) collective-permute-start(bf16[640,256]{1,0:T(8,128)(2,1)S(1)} %attend.2.piece_ref.refs_0_), channel_id=1, source_target_pairs={{0,1},{1,0},{2,3},{3,2},{4,5},{5,4},{6,7},{7,6},{8,9},{9,8},{10,11... | collective-permute-start | bytes 983048 | tf_op jit(solution)/shard_map/ppermute | solution.py:430
  192.6 14.3 %collective-permute-start.43 = (bf16[1,256,1024]{2,1,0:T(8,128)(2,1)S(1)}, bf16[1,256,1024]{2,1,0:T(8,128)(2,1)S(1)}, u32[]{:S(2)}, u32[]{:S(2)}) collective-permute-start(bf16[1,256,1024]{2,1,0:T(8,128)(2,1)S(1)} %choose.11.refs_6_.refs_8_), channel_id=1, source_target_pairs={{0,2},{1,3},{2,0},{3,1},{4,6},{5,7},{6,4},{7,5},{8,10},{9,11},{10,... | collective-permute-start | bytes 1572872 | tf_op jit(solution)/shard_map/ppermute | solution.py:430
  194.0 15.7 %collective-permute-start.42 = (bf16[1,256,1024]{2,1,0:T(8,128)(2,1)S(1)}, bf16[1,256,1024]{2,1,0:T(8,128)(2,1)S(1)}, u32[]{:S(2)}, u32[]{:S(2)}) collective-permute-start(bf16[1,256,1024]{2,1,0:T(8,128)(2,1)S(1)} %collective-permute-done.33), channel_id=1, source_target_pairs={{4,0},{5,1},{6,2},{7,3},{8,12},{9,13},{10,14},{11,15},{20,16},{21,... | collective-permute-start | bytes 1572872 | tf_op jit(solution)/shard_map/ppermute | solution.py:430
  195.3 11.4 %collective-permute-start.44 = (bf16[640,256]{1,0:T(8,128)(2,1)S(1)}, bf16[640,256]{1,0:T(8,128)(2,1)S(1)}, u32[]{:S(2)}, u32[]{:S(2)}) collective-permute-start(bf16[640,256]{1,0:T(8,128)(2,1)S(1)} %get-tuple-element.154.refs_2_), channel_id=1, source_target_pairs={{0,1},{1,0},{2,3},{3,2},{4,5},{5,4},{6,7},{7,6},{8,9},{9,8},{10,11... | collective-permute-start | bytes 983048 | tf_op jit(solution)/shard_map/ppermute | solution.py:430
  200.1 9.8 %collective-permute-start.40 = (bf16[1,256,1024]{2,1,0:T(8,128)(2,1)S(1)}, bf16[1,256,1024]{2,1,0:T(8,128)(2,1)S(1)}, u32[]{:S(2)}, u32[]{:S(2)}) collective-permute-start(bf16[1,256,1024]{2,1,0:T(8,128)(2,1)S(1)} %collective-permute-done.25), channel_id=1, source_target_pairs={{4,8},{5,9},{6,10},{7,11},{8,4},{9,5},{10,6},{11,7},{20,24},{21,25... | collective-permute-start | bytes 1572872 | tf_op jit(solution)/shard_map/ppermute | solution.py:430
  219.0 14.4 %collective-permute-start.49 = (bf16[1,256,1024]{2,1,0:T(8,128)(2,1)S(1)}, bf16[1,256,1024]{2,1,0:T(8,128)(2,1)S(1)}, u32[]{:S(2)}, u32[]{:S(2)}) collective-permute-start(bf16[1,256,1024]{2,1,0:T(8,128)(2,1)S(1)} %choose.12.refs_10_.refs_6_), channel_id=1, source_target_pairs={{0,2},{1,3},{2,0},{3,1},{4,6},{5,7},{6,4},{7,5},{8,10},{9,11},{10,... | collective-permute-start | bytes 1572872 | tf_op jit(solution)/shard_map/ppermute | solution.py:430
  219.1 14.2 %collective-permute-start.48 = (bf16[1,256,1024]{2,1,0:T(8,128)(2,1)S(1)}, bf16[1,256,1024]{2,1,0:T(8,128)(2,1)S(1)}, u32[]{:S(2)}, u32[]{:S(2)}) collective-permute-start(bf16[1,256,1024]{2,1,0:T(8,128)(2,1)S(1)} %collective-permute-done.38.b_ref), channel_id=1, source_target_pairs={{4,8},{5,9},{6,10},{7,11},{8,4},{9,5},{10,6},{11,7},{20,24},{21,25... | collective-permute-start | bytes 1572872 | tf_op jit(solution)/shard_map/ppermute | solution.py:430
  219.8 17.3 %collective-permute-start.47 = (bf16[1,256,1024]{2,1,0:T(8,128)(2,1)S(1)}, bf16[1,256,1024]{2,1,0:T(8,128)(2,1)S(1)}, u32[]{:S(2)}, u32[]{:S(2)}) collective-permute-start(bf16[1,256,1024]{2,1,0:T(8,128)(2,1)S(1)} %collective-permute-done.40), channel_id=1, source_target_pairs={{4,0},{5,1},{6,2},{7,3},{8,12},{9,13},{10,14},{11,15},{20,16},{21,... | collective-permute-start | bytes 1572872 | tf_op jit(solution)/shard_map/ppermute | solution.py:430
  221.4 16.4 %collective-permute-start.51 = (bf16[640,256]{1,0:T(8,128)(2,1)S(1)}, bf16[640,256]{1,0:T(8,128)(2,1)S(1)}, u32[]{:S(2)}, u32[]{:S(2)}) collective-permute-start(bf16[640,256]{1,0:T(8,128)(2,1)S(1)} %collective-permute-done.45.refs_2_), channel_id=1, source_target_pairs={{0,1},{1,0},{2,3},{3,2},{4,5},{5,4},{6,7},{7,6},{8,9},{9,8},{10,11... | collective-permute-start | bytes 983048 | tf_op jit(solution)/shard_map/ppermute | solution.py:430
  224.8 15.1 %collective-permute-start.50 = (bf16[640,256]{1,0:T(8,128)(2,1)S(1)}, bf16[640,256]{1,0:T(8,128)(2,1)S(1)}, u32[]{:S(2)}, u32[]{:S(2)}) collective-permute-start(bf16[640,256]{1,0:T(8,128)(2,1)S(1)} %attend.3.refs_0_), channel_id=1, source_target_pairs={{0,1},{1,0},{2,3},{3,2},{4,5},{5,4},{6,7},{7,6},{8,9},{9,8},{10,11... | collective-permute-start | bytes 983048 | tf_op jit(solution)/shard_map/ppermute | solution.py:430
  240.6 14.3 %collective-permute-start.53 = (bf16[1,256,1024]{2,1,0:T(8,128)(2,1)S(1)}, bf16[1,256,1024]{2,1,0:T(8,128)(2,1)S(1)}, u32[]{:S(2)}, u32[]{:S(2)}) collective-permute-start(bf16[1,256,1024]{2,1,0:T(8,128)(2,1)S(1)} %choose.13.refs_8_.refs_10_), channel_id=1, source_target_pairs={{0,2},{1,3},{2,0},{3,1},{4,6},{5,7},{6,4},{7,5},{8,10},{9,11},{10,... | collective-permute-start | bytes 1572872 | tf_op jit(solution)/shard_map/ppermute | solution.py:430
  258.6 18.9 %collective-permute-start.54 = (bf16[640,1024]{1,0:T(8,128)(2,1)S(1)}, bf16[640,1024]{1,0:T(8,128)(2,1)S(1)}, u32[]{:S(2)}, u32[]{:S(2)}) collective-permute-start(bf16[640,1024]{1,0:T(8,128)(2,1)S(1)} %combine.6.a_ref), channel_id=1, source_target_pairs={{0,16},{1,17},{2,18},{3,19},{4,20},{5,21},{6,22},{7,23},{8,24},{9,... | collective-permute-start | bytes 3932168 | tf_op jit(solution)/shard_map/ppermute | solution.py:430
  260.0 17.4 %collective-permute-start.56 = (bf16[320,1024]{1,0:T(8,128)(2,1)S(1)}, bf16[320,1024]{1,0:T(8,128)(2,1)S(1)}, u32[]{:S(2)}, u32[]{:S(2)}) collective-permute-start(bf16[320,1024]{1,0:T(8,128)(2,1)S(1)} %join.1), channel_id=1, source_target_pairs={{0,4},{1,5},{2,6},{3,7},{4,0},{5,1},{6,2},{7,3},{8,12},{9,13},{10,... | collective-permute-start | bytes 1966088 | tf_op jit(solution)/shard_map/ppermute | solution.py:430
  (16 other events, 206.5 us)

commit v11 on v10

--- a/solution.py
+++ b/solution.py
@@ -92,6 +92,17 @@
     return call("kinds_behind", kernel, here, [part], shaped((1, length), I32))
 
 
+def split(here, block):
+    kinds, depth, width = block.shape
+    half = width // 2
+
+    def kernel(_, in_ref, low_ref, high_ref):
+        low_ref[...] = in_ref[:, :, :half]
+        high_ref[...] = in_ref[:, :, half:]
+
+    return call("split", kernel, here, [block], [shaped((kinds, depth, half))] * 2)
+
+
 def choose(here, from_edge, from_middle):
     def kernel(h_ref, a_ref, b_ref, out_ref):
         outer = Here(h_ref).outer
@@ -113,32 +124,6 @@
             refs[-1][i] = refs[i][...]
 
     return call("stack", kernel, here, arrays, shaped((len(arrays),) + arrays[0].shape))
-
-
-def pack(here, block, piece):
-    _, depth, features = block.shape
-    length, width = piece.shape
-    cuts = features // width
-
-    def kernel(_, block_ref, piece_ref, out_ref):
-        for i in range(cuts):
-            out_ref[i * depth : (i + 1) * depth] = block_ref[0, :, i * width : (i + 1) * width]
-        out_ref[cuts * depth :] = piece_ref[...]
-
-    return call("pack", kernel, here, [block, piece], shaped((cuts * depth + length, width)))
-
-
-def unpack(here, packed, block, piece):
-    _, depth, features = block.shape
-    _, width = piece.shape
-    cuts = features // width
-
-    def kernel(_, in_ref, block_ref, piece_ref):
-        for i in range(cuts):
-            block_ref[0, :, i * width : (i + 1) * width] = in_ref[i * depth : (i + 1) * depth]
-        piece_ref[...] = in_ref[cuts * depth :]
-
-    return call("unpack", kernel, here, [packed], [shaped(block.shape), shaped(piece.shape)])
 
 
 def normalize(here, slot, held, gains, whole, mine, theirs, shape, start, count):
@@ -481,10 +466,11 @@
         begun = (m2a, mine_b)
         m3a = move(e2a, across, p2a, *begun)
         passed_top = move(top, edge, e2a, p2a, *begun)
+        low_o, high_o, mine_o, away_o = halves(here, after(out_weight, *begun), 0, 1)
         third_a = choose(here, after(e2a, *begun), m2a)
         p3a = move(third_a, pair, p2a)
 
-        begun = (m3a,)
+        begun = (m3a, mine_o)
         swapped = [to_core(a, *begun) for a in fetched[1:]]
         shape = (2, places, length, kept)
         normed = normalize(
@@ -493,11 +479,11 @@
         m4a = move(e1a, across, passed_top, p3a, *begun)
         m1b = move(low_b, across_or_stay, passed_top, p3a, *begun)
         passed_bottom = move(bottom, edge, passed_top, p3a, *begun)
+        o1o = move(low_o, outward, passed_top, p3a, *begun)
         p1b = move(mine_b, pair, p3a, *begun)
         part_top = over_tensor(after(passed_top, *begun))
-        low_o, high_o, mine_o, away_o = halves(here, after(out_weight, *begun), 0, 1)
-
-        begun = (passed_bottom, normed, mine_o)
+
+        begun = (passed_bottom, o1o, normed)
         e3a = move(m3a, outward, part_top[-1], *begun)
         i1o = move(low_o, inward, part_top[-1], *begun)
         p1o = move(mine_o, pair, p1b, *begun)
@@ -544,38 +530,37 @@
         total_b = project(here, "partner", late_normed, first_b, total_b, fresh=True)
 
         begun = (m4b, attended_a, total_b)
-        m1o = move(low_o, across, *begun)
-        m2o = move(high_o, across, *begun)
+        m12o = move(out_weight, across, i2o, *begun)
         fourth_b = choose(here, after(e3b, *begun), m4b)
         p4b = move(fourth_b, pair, p2b)
-        packed_a = move(pack(here, after(low_o, *begun), attended_a), edge, e3b, i2o, p2b)
+        passed_a = move(attended_a, edge, e3b, p2b, *begun)
         held_a = over_tensor(after(attended_a, *begun))
+        second_o = choose(here, after(o1o, *begun), i2o)
         second_b = [(1, e1b, p2b)]
         late_normed = after(normed, *begun)
         total_b = project(here, "own", late_normed, second_b, total_b)
         total_b = project(here, "partner", late_normed, second_b, total_b)
 
+        begun = (m12o, total_b, passed_a, held_a[1], second_o)
+        m3o = move(i1o, across, *begun)
+        m1o, m2o = split(here, after(m12o, *begun))
+        o2o = move(m1o, outward)
+        p2o = move(second_o, pair, p4b, *begun)
+        held_a += over_tensor(after(passed_a, *begun))
         last_b = [(3, fourth_b, p4b)]
-        theirs_b = project(here, 1, normed, last_b, total_b, final=True)
+        late_normed = after(normed, *begun)
+        theirs_b = project(here, 1, late_normed, last_b, total_b, final=True)
         got_b = to_core(theirs_b)
-        ours_b = project(here, 0, normed, last_b, total_b, final=True)
-        o1o, passed_a = unpack(here, after(packed_a, theirs_b), low_o, attended_a)
-        second_o = choose(here, o1o, i2o)
-        p2o = move(second_o, pair, p4b)
-        held_a += over_tensor(passed_a)
-
-        begun = (m1o, m2o, ours_b, second_o)
-        m3o = move(i1o, across, held_a[1], *begun)
-        o2o = move(m1o, outward, *begun)
-        attended_b = attend(here, own_kind, other_kind, after(ours_b, *begun), got_b)
-
-        passed_b = move(attended_b, edge, o2o, p2o, held_a[-1])
-        begun = (m3o, passed_b)
+        ours_b = project(here, 0, late_normed, last_b, total_b, final=True)
+        attended_b = attend(here, own_kind, other_kind, ours_b, got_b)
+
+        passed_b = move(attended_b, edge, o2o, m3o, p2o)
+        begun = (passed_b, held_a[-1])
         m4o = move(i2o, across, *begun)
         o3o = move(m3o, outward, *begun)
-        held_b = over_tensor(after(attended_b, *begun)) + over_tensor(after(passed_b, *begun))
         third_o = choose(here, after(o2o, *begun), m2o)
         p3o = move(third_o, pair, p2o)
+        held_b = over_tensor(after(attended_b, *begun)) + over_tensor(after(passed_b, *begun))
         pieces_a = stack(here, [after(held_a[0], *begun)] + held_a[1:])
         pieces_a = (pieces_a, to_core(pieces_a))
         both = ("partner", "own")

time: 283 us -> 314 us (1.11)
  waiting for transfers between devices: 142 us -> 171 us
  starting transfers between devices: 73 us -> 77.4 us
    ppermute x58, waiting for transfers between devices: 142 us -> 171 us  [move(): lax.ppermute(after(array, *earlier) if earlier else array, AXES, pairs)]
    ppermute x58, starting transfers between devices: 73 us -> 77.4 us  [move(): lax.ppermute(after(array, *earlier) if earlier else array, AXES, pairs)]
    pallas_call x36 -> x35, Pallas kernels: 59 us -> 58.4 us  [call(): pl.pallas_call(kernel, in_specs=[pl.BlockSpec(memory_space=SMEM)] + [pl.B...]
  transfers between devices with their start and end apart: 58 -> 58, of which waited for: 29 -> 27; matrix products, arithmetic and copies ran while one was open for 0% -> 0% of each run, Pallas kernels for 20% -> 17%
where the time goes in v11:
time: 314 us
  waiting for transfers between devices  171 us (54%)
  starting transfers between devices  77.4 us (25%)
  Pallas kernels  60.8 us (19%)
  local copies, waits for them, and re-layouts  4.34 us (1%)
    ppermute x58, waiting for transfers between devices, move(): lax.ppermute(after(array, *earlier) if earlier else array, AXES, pairs)  171 us
    ppermute x58, starting transfers between devices, move(): lax.ppermute(after(array, *earlier) if earlier else array, AXES, pairs)  77.4 us
    pallas_call x35, Pallas kernels, call(): pl.pallas_call(kernel, in_specs=[pl.BlockSpec(memory_space=SMEM)] + [pl.B...  58.4 us
  transfers between devices with their start and end apart: 58, of which 27 were waited for; matrix products, arithmetic and copies ran while one was open for 0% of the time, Pallas kernels for 17%

profile of v11, /device:TPU:0, one launch (start us, length us, event | category | flops | bytes accessed | tf_op | source)
XLA Modules:
  0.0 313.9 jit_solution(4076061517143249853)
XLA Ops:
  0.8 1.9 copy-done
  3.5 3.0 collective-permute-start.2
  8.8 15.3 %collective-permute-done.2.refs_2_ = bf16[3,512,256]{2,1,0:T(8,128)(2,1)S(1)} collective-permute-done((bf16[3,512,256]{2,1,0:T(8,128)(2,1)S(1)}, bf16[3,512,256]{2,1,0:T(8,128)(2,1)S(1)}, u32[]{:S(2)}, u32[]{:S(2)}) %collective-permute-start.2) | collective-permute-done | bytes 786464 | tf_op jit(solution)/shard_map/ppermute | solution.py:415
  26.6 7.7 %collective-permute-start.3 = (bf16[3,512,256]{2,1,0:T(8,128)(2,1)S(1)}, bf16[3,512,256]{2,1,0:T(8,128)(2,1)S(1)}, u32[]{:S(2)}, u32[]{:S(2)}) collective-permute-start(bf16[3,512,256]{2,1,0:T(8,128)(2,1)S(1)} %collective-permute-done), channel_id=1, source_target_pairs={{0,4},{1,5},{2,6},{3,7},{4,0},{5,1},{6,2},{7,3},{8,12},{9,13},{10,... | collective-permute-start | bytes 2359304 | tf_op jit(solution)/shard_map/ppermute | solution.py:415
  34.3 1.7 copy-done.2
  39.2 5.2 %collective-permute-done.4.refs_4_ = bf16[3,512,256]{2,1,0:T(8,128)(2,1)S(1)} collective-permute-done((bf16[3,512,256]{2,1,0:T(8,128)(2,1)S(1)}, bf16[3,512,256]{2,1,0:T(8,128)(2,1)S(1)}, u32[]{:S(2)}, u32[]{:S(2)}) %collective-permute-start.4) | collective-permute-done | bytes 786464 | tf_op jit(solution)/shard_map/ppermute | solution.py:415
  44.4 5.4 %collective-permute-done.3.a_ref = bf16[3,512,256]{2,1,0:T(8,128)(2,1)S(1)} collective-permute-done((bf16[3,512,256]{2,1,0:T(8,128)(2,1)S(1)}, bf16[3,512,256]{2,1,0:T(8,128)(2,1)S(1)}, u32[]{:S(2)}, u32[]{:S(2)}) %collective-permute-start.3) | collective-permute-done | bytes 786464 | tf_op jit(solution)/shard_map/ppermute | solution.py:415
  52.0 13.1 %collective-permute-done.11.refs_2_ = bf16[320,2048]{1,0:T(8,128)(2,1)S(1)} collective-permute-done((bf16[320,2048]{1,0:T(8,128)(2,1)S(1)}, bf16[320,2048]{1,0:T(8,128)(2,1)S(1)}, u32[]{:S(2)}, u32[]{:S(2)}) %collective-permute-start.11) | collective-permute-done | bytes 1310752 | tf_op jit(solution)/shard_map/ppermute | solution.py:415
  67.3 4.7 %collective-permute-start.6 = (bf16[160,2048]{1,0:T(8,128)(2,1)S(1)}, bf16[160,2048]{1,0:T(8,128)(2,1)S(1)}, u32[]{:S(2)}, u32[]{:S(2)}) collective-permute-start(bf16[160,2048]{1,0:T(8,128)(2,1)S(1)} %get-tuple-element.100), channel_id=1, source_target_pairs={{0,4},{1,5},{2,6},{3,7},{4,0},{5,1},{6,2},{7,3},{8,12},{9,13},{10,... | collective-permute-start | bytes 1966088 | tf_op jit(solution)/shard_map/ppermute | solution.py:415
  71.9 15.1 %collective-permute-done.6.refs_2_ = bf16[160,2048]{1,0:T(8,128)(2,1)S(1)} collective-permute-done((bf16[160,2048]{1,0:T(8,128)(2,1)S(1)}, bf16[160,2048]{1,0:T(8,128)(2,1)S(1)}, u32[]{:S(2)}, u32[]{:S(2)}) %collective-permute-start.6) | collective-permute-done | bytes 655392 | tf_op jit(solution)/shard_map/ppermute | solution.py:415
  87.1 3.4 %collective-permute-start.9 = (bf16[176,2048]{1,0:T(8,128)(2,1)S(1)}, bf16[176,2048]{1,0:T(8,128)(2,1)S(1)}, u32[]{:S(2)}, u32[]{:S(2)}) collective-permute-start(bf16[176,2048]{1,0:T(8,128)(2,1)S(1)} %get-tuple-element.106), channel_id=1, source_target_pairs={{0,4},{1,5},{2,6},{3,7},{4,0},{5,1},{6,2},{7,3},{8,12},{9,13},{10,... | collective-permute-start | bytes 2162696 | tf_op jit(solution)/shard_map/ppermute | solution.py:415
  95.5 3.2 %normalize.3.refs_0_ = bf16[2,8,640,512]{3,2,1,0:T(8,128)(2,1)S(1)} custom-call(s32[3]{0:T(128)S(1)} %pad_add_fusion.h_ref._, f32[8,1,512]{2,1,0:T(1,128)S(1)} %bitcast.9, bf16[640,2048]{1,0:T(8,128)(2,1)S(1)} %copy-done.3, bf16[320,2048]{1,0:T(8,128)(2,1)S(1)} %collective-permute-done.11.refs_2_, bf16[320,2048]{1,0:T(8,128)(2,1)S(1)} %collective-permute-done.12.refs_3_), custom_call_target="tpu_custom_call" | custom-call | tf_op jit(solution)/shard_map/normalize/pallas_call | solution.py:32
  98.7 19.0 %collective-permute-done.10.a_ref = bf16[1,256,1024]{2,1,0:T(8,128)(2,1)S(1)} collective-permute-done((bf16[1,256,1024]{2,1,0:T(8,128)(2,1)S(1)}, bf16[1,256,1024]{2,1,0:T(8,128)(2,1)S(1)}, u32[]{:S(2)}, u32[]{:S(2)}) %collective-permute-start.10) | collective-permute-done | bytes 524320 | tf_op jit(solution)/shard_map/ppermute | solution.py:415
  123.3 4.6 %collective-permute-start.26 = (bf16[1,256,1024]{2,1,0:T(8,128)(2,1)S(1)}, bf16[1,256,1024]{2,1,0:T(8,128)(2,1)S(1)}, u32[]{:S(2)}, u32[]{:S(2)}) collective-permute-start(bf16[1,256,1024]{2,1,0:T(8,128)(2,1)S(1)} %get-tuple-element.130), channel_id=1, source_target_pairs={{0,4},{1,5},{2,6},{3,7},{12,8},{13,9},{14,10},{15,11},{16,20},{17,... | collective-permute-start | bytes 1572872 | tf_op jit(solution)/shard_map/ppermute | solution.py:415
  128.4 3.7 %project.10.refs_7_ = f32[2,640,768]{2,1,0:T(8,128)S(1)} custom-call(s32[3]{0:T(128)S(1)} %pad_add_fusion.h_ref._, bf16[2,8,640,512]{3,2,1,0:T(8,128)(2,1)S(1)} %normalize.3.refs_0_, bf16[3,512,256]{2,1,0:T(8,128)(2,1)S(1)} %get-tuple-element.93.refs_1_, bf16[3,512,256]{2,1,0:T(8,128)(2,1)S(1)} %collective-permute-done.2.refs_2_, ...), custom_call_target="tpu_custom_call" | custom-call | tf_op jit(solution)/shard_map/project/pallas_call | solution.py:32
  132.2 1.8 normalize.4.refs_0_
  134.7 5.6 %collective-permute-done.22.a_ref = bf16[3,512,256]{2,1,0:T(8,128)(2,1)S(1)} collective-permute-done((bf16[3,512,256]{2,1,0:T(8,128)(2,1)S(1)}, bf16[3,512,256]{2,1,0:T(8,128)(2,1)S(1)}, u32[]{:S(2)}, u32[]{:S(2)}) %collective-permute-start.22) | collective-permute-done | bytes 786464 | tf_op jit(solution)/shard_map/ppermute | solution.py:415
  147.4 1.8 normalize.5.refs_0_
  149.2 3.7 %project.11.refs_3_ = f32[2,640,768]{2,1,0:T(8,128)S(1)} custom-call(s32[3]{0:T(128)S(1)} %pad_add_fusion.h_ref._, bf16[2,8,640,512]{3,2,1,0:T(8,128)(2,1)S(1)} %normalize.5.refs_0_, bf16[3,512,256]{2,1,0:T(8,128)(2,1)S(1)} %get-tuple-element.93.refs_1_, bf16[3,512,256]{2,1,0:T(8,128)(2,1)S(1)} %collective-permute-done.2.refs_2_, ...), custom_call_target="tpu_custom_call", output_to_operand_aliasing={{}: (8, {})} | custom-call | tf_op jit(solution)/shard_map/project/pallas_call | solution.py:32
  153.0 6.1 %collective-permute-done.27.a_ref = bf16[3,512,256]{2,1,0:T(8,128)(2,1)S(1)} collective-permute-done((bf16[3,512,256]{2,1,0:T(8,128)(2,1)S(1)}, bf16[3,512,256]{2,1,0:T(8,128)(2,1)S(1)}, u32[]{:S(2)}, u32[]{:S(2)}) %collective-permute-start.27) | collective-permute-done | bytes 786464 | tf_op jit(solution)/shard_map/ppermute | solution.py:415
  160.8 2.7 collective-permute-start.30
  167.5 1.7 project.12.own_ref
  169.2 9.8 %collective-permute-done.30.refs_1_ = bf16[3,512,256]{2,1,0:T(8,128)(2,1)S(1)} collective-permute-done((bf16[3,512,256]{2,1,0:T(8,128)(2,1)S(1)}, bf16[3,512,256]{2,1,0:T(8,128)(2,1)S(1)}, u32[]{:S(2)}, u32[]{:S(2)}) %collective-permute-start.30) | collective-permute-done | bytes 786464 | tf_op jit(solution)/shard_map/ppermute | solution.py:415
  182.4 4.8 %collective-permute-start.33 = (bf16[1,256,1024]{2,1,0:T(8,128)(2,1)S(1)}, bf16[1,256,1024]{2,1,0:T(8,128)(2,1)S(1)}, u32[]{:S(2)}, u32[]{:S(2)}) collective-permute-start(bf16[1,256,1024]{2,1,0:T(8,128)(2,1)S(1)} %get-tuple-element.141), channel_id=1, source_target_pairs={{0,4},{1,5},{2,6},{3,7},{12,8},{13,9},{14,10},{15,11},{16,20},{17,... | collective-permute-start | bytes 1572872 | tf_op jit(solution)/shard_map/ppermute | solution.py:415
  188.8 2.7 project.14.refs_5_
  191.5 2.7 project.15.refs_3_
  194.3 4.2 %attend.2.refs_0_ = bf16[640,256]{1,0:T(8,128)(2,1)S(1)} custom-call(s32[3]{0:T(128)S(1)} %pad_add_fusion.h_ref._, s32[1,640]{1,0:T(1,128)S(1)} %broadcast_in_dim.3.kind_ref.own_kind_ref, s32[1,640]{1,0:T(1,128)S(1)} %kinds_behind.1.other_kind_ref.kind_ref, bf16[640,768]{1,0:T(8,128)(2,1)S(1)} %project.12.own_ref, ...), custom_call_target="tpu_custom_call" | custom-call | tf_op jit(solution)/shard_map/attend/pallas_call | solution.py:32
  199.8 5.2 %collective-permute-done.35.refs_2_ = bf16[3,512,256]{2,1,0:T(8,128)(2,1)S(1)} collective-permute-done((bf16[3,512,256]{2,1,0:T(8,128)(2,1)S(1)}, bf16[3,512,256]{2,1,0:T(8,128)(2,1)S(1)}, u32[]{:S(2)}, u32[]{:S(2)}) %collective-permute-start.35) | collective-permute-done | bytes 786464 | tf_op jit(solution)/shard_map/ppermute | solution.py:415
  208.6 1.9 project.16.refs_3_
  210.5 1.9 project.17.refs_3_
  213.6 6.1 %collective-permute-done.39.refs_2_ = bf16[3,512,256]{2,1,0:T(8,128)(2,1)S(1)} collective-permute-done((bf16[3,512,256]{2,1,0:T(8,128)(2,1)S(1)}, bf16[3,512,256]{2,1,0:T(8,128)(2,1)S(1)}, u32[]{:S(2)}, u32[]{:S(2)}) %collective-permute-start.39) | collective-permute-done | bytes 786464 | tf_op jit(solution)/shard_map/ppermute | solution.py:415
  227.2 1.7 project.18.own_ref
  228.9 4.2 %attend.3.refs_0_ = bf16[640,256]{1,0:T(8,128)(2,1)S(1)} custom-call(s32[3]{0:T(128)S(1)} %pad_add_fusion.h_ref._, s32[1,640]{1,0:T(1,128)S(1)} %broadcast_in_dim.3.kind_ref.own_kind_ref, s32[1,640]{1,0:T(1,128)S(1)} %kinds_behind.1.other_kind_ref.kind_ref, bf16[640,768]{1,0:T(8,128)(2,1)S(1)} %project.18.own_ref, ...), custom_call_target="tpu_custom_call" | custom-call | tf_op jit(solution)/shard_map/attend/pallas_call | solution.py:32
  233.1 2.7 collective-permute-done.43.refs_7_.refs_9_
  235.8 5.9 %collective-permute-done.41.a_ref = bf16[1,256,1024]{2,1,0:T(8,128)(2,1)S(1)} collective-permute-done((bf16[1,256,1024]{2,1,0:T(8,128)(2,1)S(1)}, bf16[1,256,1024]{2,1,0:T(8,128)(2,1)S(1)}, u32[]{:S(2)}, u32[]{:S(2)}) %collective-permute-start.41) | collective-permute-done | bytes 524320 | tf_op jit(solution)/shard_map/ppermute | solution.py:415
  241.8 8.9 %collective-permute-done.44.refs_2_ = bf16[640,256]{1,0:T(8,128)(2,1)S(1)} collective-permute-done((bf16[640,256]{1,0:T(8,128)(2,1)S(1)}, bf16[640,256]{1,0:T(8,128)(2,1)S(1)}, u32[]{:S(2)}, u32[]{:S(2)}) %collective-permute-start.44) | collective-permute-done | bytes 327712 | tf_op jit(solution)/shard_map/ppermute | solution.py:415
  256.9 2.1 combine.4.refs_12_
  259.0 7.4 %collective-permute-done.49.refs_11_.refs_7_ = bf16[1,256,1024]{2,1,0:T(8,128)(2,1)S(1)} collective-permute-done((bf16[1,256,1024]{2,1,0:T(8,128)(2,1)S(1)}, bf16[1,256,1024]{2,1,0:T(8,128)(2,1)S(1)}, u32[]{:S(2)}, u32[]{:S(2)}) %collective-permute-start.49) | collective-permute-done | bytes 524320 | tf_op jit(solution)/shard_map/ppermute | solution.py:415
  266.4 2.9 collective-permute-done.47.a_ref
  269.9 1.9 collective-permute-done.50.refs_1_
  275.5 2.8 combine.5.refs_12_
  278.3 8.5 %collective-permute-done.53.refs_9_.refs_11_ = bf16[1,256,1024]{2,1,0:T(8,128)(2,1)S(1)} collective-permute-done((bf16[1,256,1024]{2,1,0:T(8,128)(2,1)S(1)}, bf16[1,256,1024]{2,1,0:T(8,128)(2,1)S(1)}, u32[]{:S(2)}, u32[]{:S(2)}) %collective-permute-start.53) | collective-permute-done | bytes 524320 | tf_op jit(solution)/shard_map/ppermute | solution.py:415
  286.8 1.8 combine.7
  288.7 1.7 combine.6.a_ref
  291.9 2.5 collective-permute-start.56
  294.3 14.9 %collective-permute-done.56.c_ref = bf16[320,1024]{1,0:T(8,128)(2,1)S(1)} collective-permute-done((bf16[320,1024]{1,0:T(8,128)(2,1)S(1)}, bf16[320,1024]{1,0:T(8,128)(2,1)S(1)}, u32[]{:S(2)}, u32[]{:S(2)}) %collective-permute-start.56) | collective-permute-done | bytes 655392 | tf_op jit(solution)/shard_map/ppermute | solution.py:415
  309.3 2.1 collective-permute-done.57.d_ref
  311.4 2.4 shard_map.55
  (118 shorter events, 68.9 us)
Async XLA Ops:
  3.5 20.6 %collective-permute-start.2 = (bf16[3,512,256]{2,1,0:T(8,128)(2,1)S(1)}, bf16[3,512,256]{2,1,0:T(8,128)(2,1)S(1)}, u32[]{:S(2)}, u32[]{:S(2)}) collective-permute-start(bf16[3,512,256]{2,1,0:T(8,128)(2,1)S(1)} %get-tuple-element.93.refs_1_), channel_id=1, source_target_pairs={{0,2},{1,3},{2,0},{3,1},{4,6},{5,7},{6,4},{7,5},{8,10},{9,11},{10,... | collective-permute-start | bytes 2359304 | tf_op jit(solution)/shard_map/ppermute | solution.py:415
  6.5 19.0 %collective-permute-start.1 = (bf16[3,512,256]{2,1,0:T(8,128)(2,1)S(1)}, bf16[3,512,256]{2,1,0:T(8,128)(2,1)S(1)}, u32[]{:S(2)}, u32[]{:S(2)}) collective-permute-start(bf16[3,512,256]{2,1,0:T(8,128)(2,1)S(1)} %get-tuple-element.92), channel_id=1, source_target_pairs={{0,4},{1,5},{2,6},{3,7},{4,0},{5,1},{6,2},{7,3},{8,12},{9,13},{10,... | collective-permute-start | bytes 2359304 | tf_op jit(solution)/shard_map/ppermute | solution.py:415
  8.1 17.4 %collective-permute-start = (bf16[3,512,256]{2,1,0:T(8,128)(2,1)S(1)}, bf16[3,512,256]{2,1,0:T(8,128)(2,1)S(1)}, u32[]{:S(2)}, u32[]{:S(2)}) collective-permute-start(bf16[3,512,256]{2,1,0:T(8,128)(2,1)S(1)} %get-tuple-element.88), channel_id=1, source_target_pairs={{0,0},{1,1},{2,2},{3,3},{4,8},{5,9},{6,10},{7,11},{8,4},{9,5},{10,... | collective-permute-start | bytes 2359304 | tf_op jit(solution)/shard_map/ppermute | solution.py:415
  25.5 13.7 %collective-permute-start.5 = (bf16[3,512,256]{2,1,0:T(8,128)(2,1)S(1)}, bf16[3,512,256]{2,1,0:T(8,128)(2,1)S(1)}, u32[]{:S(2)}, u32[]{:S(2)}) collective-permute-start(bf16[3,512,256]{2,1,0:T(8,128)(2,1)S(1)} %get-tuple-element.97), channel_id=1, source_target_pairs={{4,8},{5,9},{6,10},{7,11},{8,4},{9,5},{10,6},{11,7},{20,24},{21,25... | collective-permute-start | bytes 2359304 | tf_op jit(solution)/shard_map/ppermute | solution.py:415
  26.2 18.2 %collective-permute-start.4 = (bf16[3,512,256]{2,1,0:T(8,128)(2,1)S(1)}, bf16[3,512,256]{2,1,0:T(8,128)(2,1)S(1)}, u32[]{:S(2)}, u32[]{:S(2)}) collective-permute-start(bf16[3,512,256]{2,1,0:T(8,128)(2,1)S(1)} %collective-permute-done.1.refs_3_), channel_id=1, source_target_pairs={{0,2},{1,3},{2,0},{3,1},{4,6},{5,7},{6,4},{7,5},{8,10},{9,11},{10,... | collective-permute-start | bytes 2359304 | tf_op jit(solution)/shard_map/ppermute | solution.py:415
  26.6 23.2 %collective-permute-start.3 = (bf16[3,512,256]{2,1,0:T(8,128)(2,1)S(1)}, bf16[3,512,256]{2,1,0:T(8,128)(2,1)S(1)}, u32[]{:S(2)}, u32[]{:S(2)}) collective-permute-start(bf16[3,512,256]{2,1,0:T(8,128)(2,1)S(1)} %collective-permute-done), channel_id=1, source_target_pairs={{0,4},{1,5},{2,6},{3,7},{4,0},{5,1},{6,2},{7,3},{8,12},{9,13},{10,... | collective-permute-start | bytes 2359304 | tf_op jit(solution)/shard_map/ppermute | solution.py:415
  36.8 28.3 %collective-permute-start.11 = (bf16[320,2048]{1,0:T(8,128)(2,1)S(1)}, bf16[320,2048]{1,0:T(8,128)(2,1)S(1)}, u32[]{:S(2)}, u32[]{:S(2)}) collective-permute-start(bf16[320,2048]{1,0:T(8,128)(2,1)S(1)} %get-tuple-element.110), channel_id=1, source_target_pairs={{0,1},{1,0},{2,3},{3,2},{4,5},{5,4},{6,7},{7,6},{8,9},{9,8},{10,11... | collective-permute-start | bytes 3932168 | tf_op jit(solution)/shard_map/ppermute | solution.py:415
  49.8 15.3 %collective-permute-start.8 = (bf16[3,512,256]{2,1,0:T(8,128)(2,1)S(1)}, bf16[3,512,256]{2,1,0:T(8,128)(2,1)S(1)}, u32[]{:S(2)}, u32[]{:S(2)}) collective-permute-start(bf16[3,512,256]{2,1,0:T(8,128)(2,1)S(1)} %collective-permute-done.3.a_ref), channel_id=1, source_target_pairs={{4,8},{5,9},{6,10},{7,11},{8,4},{9,5},{10,6},{11,7},{20,24},{21,25... | collective-permute-start | bytes 2359304 | tf_op jit(solution)/shard_map/ppermute | solution.py:415
  65.1 29.7 %collective-permute-start.12 = (bf16[320,2048]{1,0:T(8,128)(2,1)S(1)}, bf16[320,2048]{1,0:T(8,128)(2,1)S(1)}, u32[]{:S(2)}, u32[]{:S(2)}) collective-permute-start(bf16[320,2048]{1,0:T(8,128)(2,1)S(1)} %collective-permute-done.11.refs_2_), channel_id=1, source_target_pairs={{0,16},{1,17},{2,18},{3,19},{4,20},{5,21},{6,22},{7,23},{8,24},{9,... | collective-permute-start | bytes 3932168 | tf_op jit(solution)/shard_map/ppermute | solution.py:415
  65.7 21.4 %collective-permute-start.7 = (bf16[3,512,256]{2,1,0:T(8,128)(2,1)S(1)}, bf16[3,512,256]{2,1,0:T(8,128)(2,1)S(1)}, u32[]{:S(2)}, u32[]{:S(2)}) collective-permute-start(bf16[3,512,256]{2,1,0:T(8,128)(2,1)S(1)} %choose.7.refs_5_), channel_id=1, source_target_pairs={{0,2},{1,3},{2,0},{3,1},{4,6},{5,7},{6,4},{7,5},{8,10},{9,11},{10,... | collective-permute-start | bytes 2359304 | tf_op jit(solution)/shard_map/ppermute | solution.py:415
  67.3 19.8 %collective-permute-start.6 = (bf16[160,2048]{1,0:T(8,128)(2,1)S(1)}, bf16[160,2048]{1,0:T(8,128)(2,1)S(1)}, u32[]{:S(2)}, u32[]{:S(2)}) collective-permute-start(bf16[160,2048]{1,0:T(8,128)(2,1)S(1)} %get-tuple-element.100), channel_id=1, source_target_pairs={{0,4},{1,5},{2,6},{3,7},{4,0},{5,1},{6,2},{7,3},{8,12},{9,13},{10,... | collective-permute-start | bytes 1966088 | tf_op jit(solution)/shard_map/ppermute | solution.py:415
  87.1 30.6 %collective-permute-start.9 = (bf16[176,2048]{1,0:T(8,128)(2,1)S(1)}, bf16[176,2048]{1,0:T(8,128)(2,1)S(1)}, u32[]{:S(2)}, u32[]{:S(2)}) collective-permute-start(bf16[176,2048]{1,0:T(8,128)(2,1)S(1)} %get-tuple-element.106), channel_id=1, source_target_pairs={{0,4},{1,5},{2,6},{3,7},{4,0},{5,1},{6,2},{7,3},{8,12},{9,13},{10,... | collective-permute-start | bytes 2162696 | tf_op jit(solution)/shard_map/ppermute | solution.py:415
  90.4 27.3 %collective-permute-start.13 = (bf16[160,2048]{1,0:T(8,128)(2,1)S(1)}, bf16[160,2048]{1,0:T(8,128)(2,1)S(1)}, u32[]{:S(2)}, u32[]{:S(2)}) collective-permute-start(bf16[160,2048]{1,0:T(8,128)(2,1)S(1)} %collective-permute-done.6.refs_2_), channel_id=1, source_target_pairs={{0,1},{1,0},{2,3},{3,2},{4,5},{5,4},{6,7},{7,6},{8,9},{9,8},{10,11... | collective-permute-start | bytes 1966088 | tf_op jit(solution)/shard_map/ppermute | solution.py:415
  91.9 25.8 %collective-permute-start.10 = (bf16[1,256,1024]{2,1,0:T(8,128)(2,1)S(1)}, bf16[1,256,1024]{2,1,0:T(8,128)(2,1)S(1)}, u32[]{:S(2)}, u32[]{:S(2)}) collective-permute-start(bf16[1,256,1024]{2,1,0:T(8,128)(2,1)S(1)} %get-tuple-element.130), channel_id=1, source_target_pairs={{4,0},{5,1},{6,2},{7,3},{8,12},{9,13},{10,14},{11,15},{20,16},{21,... | collective-permute-start | bytes 1572872 | tf_op jit(solution)/shard_map/ppermute | solution.py:415
  93.2 25.7 %collective-permute-start.23 = (bf16[3,512,256]{2,1,0:T(8,128)(2,1)S(1)}, bf16[3,512,256]{2,1,0:T(8,128)(2,1)S(1)}, u32[]{:S(2)}, u32[]{:S(2)}) collective-permute-start(bf16[3,512,256]{2,1,0:T(8,128)(2,1)S(1)} %get-tuple-element.127.refs_1_), channel_id=1, source_target_pairs={{0,2},{1,3},{2,0},{3,1},{4,6},{5,7},{6,4},{7,5},{8,10},{9,11},{10,... | collective-permute-start | bytes 2359304 | tf_op jit(solution)/shard_map/ppermute | solution.py:415
  94.7 25.5 %collective-permute-start.17 = (bf16[3,512,256]{2,1,0:T(8,128)(2,1)S(1)}, bf16[3,512,256]{2,1,0:T(8,128)(2,1)S(1)}, u32[]{:S(2)}, u32[]{:S(2)}) collective-permute-start(bf16[3,512,256]{2,1,0:T(8,128)(2,1)S(1)} %collective-permute-done.1.refs_3_), channel_id=1, source_target_pairs={{4,8},{5,9},{6,10},{7,11},{8,4},{9,5},{10,6},{11,7},{20,24},{21,25... | collective-permute-start | bytes 2359304 | tf_op jit(solution)/shard_map/ppermute | solution.py:415
  118.2 15.8 %collective-permute-start.18 = (bf16[3,512,256]{2,1,0:T(8,128)(2,1)S(1)}, bf16[3,512,256]{2,1,0:T(8,128)(2,1)S(1)}, u32[]{:S(2)}, u32[]{:S(2)}) collective-permute-start(bf16[3,512,256]{2,1,0:T(8,128)(2,1)S(1)} %get-tuple-element.118), channel_id=1, source_target_pairs={{0,0},{1,1},{2,2},{3,3},{4,8},{5,9},{6,10},{7,11},{8,4},{9,5},{10,... | collective-permute-start | bytes 2359304 | tf_op jit(solution)/shard_map/ppermute | solution.py:415
  118.9 21.4 %collective-permute-start.22 = (bf16[3,512,256]{2,1,0:T(8,128)(2,1)S(1)}, bf16[3,512,256]{2,1,0:T(8,128)(2,1)S(1)}, u32[]{:S(2)}, u32[]{:S(2)}) collective-permute-start(bf16[3,512,256]{2,1,0:T(8,128)(2,1)S(1)} %collective-permute-done.8), channel_id=1, source_target_pairs={{4,0},{5,1},{6,2},{7,3},{8,12},{9,13},{10,14},{11,15},{20,16},{21,... | collective-permute-start | bytes 2359304 | tf_op jit(solution)/shard_map/ppermute | solution.py:415
  120.2 20.1 %collective-permute-start.16 = (bf16[176,2048]{1,0:T(8,128)(2,1)S(1)}, bf16[176,2048]{1,0:T(8,128)(2,1)S(1)}, u32[]{:S(2)}, u32[]{:S(2)}) collective-permute-start(bf16[176,2048]{1,0:T(8,128)(2,1)S(1)} %collective-permute-done.9.in_ref.refs_2_), channel_id=1, source_target_pairs={{0,1},{1,0},{2,3},{3,2},{4,5},{5,4},{6,7},{7,6},{8,9},{9,8},{10,11... | collective-permute-start | bytes 2162696 | tf_op jit(solution)/shard_map/ppermute | solution.py:415
  121.8 18.5 %collective-permute-start.24 = (bf16[1,256,1024]{2,1,0:T(8,128)(2,1)S(1)}, bf16[1,256,1024]{2,1,0:T(8,128)(2,1)S(1)}, u32[]{:S(2)}, u32[]{:S(2)}) collective-permute-start(bf16[1,256,1024]{2,1,0:T(8,128)(2,1)S(1)} %get-tuple-element.128.refs_4_.refs_6_), channel_id=1, source_target_pairs={{0,2},{1,3},{2,0},{3,1},{4,6},{5,7},{6,4},{7,5},{8,10},{9,11},{10,... | collective-permute-start | bytes 1572872 | tf_op jit(solution)/shard_map/ppermute | solution.py:415
  123.3 17.1 %collective-permute-start.26 = (bf16[1,256,1024]{2,1,0:T(8,128)(2,1)S(1)}, bf16[1,256,1024]{2,1,0:T(8,128)(2,1)S(1)}, u32[]{:S(2)}, u32[]{:S(2)}) collective-permute-start(bf16[1,256,1024]{2,1,0:T(8,128)(2,1)S(1)} %get-tuple-element.130), channel_id=1, source_target_pairs={{0,4},{1,5},{2,6},{3,7},{12,8},{13,9},{14,10},{15,11},{16,20},{17,... | collective-permute-start | bytes 1572872 | tf_op jit(solution)/shard_map/ppermute | solution.py:415
  134.0 19.0 %collective-permute-start.21 = (bf16[3,512,256]{2,1,0:T(8,128)(2,1)S(1)}, bf16[3,512,256]{2,1,0:T(8,128)(2,1)S(1)}, u32[]{:S(2)}, u32[]{:S(2)}) collective-permute-start(bf16[3,512,256]{2,1,0:T(8,128)(2,1)S(1)} %get-tuple-element.123), channel_id=1, source_target_pairs={{4,8},{5,9},{6,10},{7,11},{8,4},{9,5},{10,6},{11,7},{20,24},{21,25... | collective-permute-start | bytes 2359304 | tf_op jit(solution)/shard_map/ppermute | solution.py:415
  140.4 18.7 %collective-permute-start.27 = (bf16[3,512,256]{2,1,0:T(8,128)(2,1)S(1)}, bf16[3,512,256]{2,1,0:T(8,128)(2,1)S(1)}, u32[]{:S(2)}, u32[]{:S(2)}) collective-permute-start(bf16[3,512,256]{2,1,0:T(8,128)(2,1)S(1)} %collective-permute-done.18), channel_id=1, source_target_pairs={{0,4},{1,5},{2,6},{3,7},{4,0},{5,1},{6,2},{7,3},{8,12},{9,13},{10,... | collective-permute-start | bytes 2359304 | tf_op jit(solution)/shard_map/ppermute | solution.py:415
  142.7 18.2 %collective-permute-start.25 = (bf16[3,512,256]{2,1,0:T(8,128)(2,1)S(1)}, bf16[3,512,256]{2,1,0:T(8,128)(2,1)S(1)}, u32[]{:S(2)}, u32[]{:S(2)}) collective-permute-start(bf16[3,512,256]{2,1,0:T(8,128)(2,1)S(1)} %choose.8.refs_1_), channel_id=1, source_target_pairs={{0,2},{1,3},{2,0},{3,1},{4,6},{5,7},{6,4},{7,5},{8,10},{9,11},{10,... | collective-permute-start | bytes 2359304 | tf_op jit(solution)/shard_map/ppermute | solution.py:415
  159.1 10.1 %collective-permute-start.28 = (bf16[3,512,256]{2,1,0:T(8,128)(2,1)S(1)}, bf16[3,512,256]{2,1,0:T(8,128)(2,1)S(1)}, u32[]{:S(2)}, u32[]{:S(2)}) collective-permute-start(bf16[3,512,256]{2,1,0:T(8,128)(2,1)S(1)} %collective-permute-done.27.a_ref), channel_id=1, source_target_pairs={{4,8},{5,9},{6,10},{7,11},{8,4},{9,5},{10,6},{11,7},{20,24},{21,25... | collective-permute-start | bytes 2359304 | tf_op jit(solution)/shard_map/ppermute | solution.py:415
  160.8 18.2 %collective-permute-start.30 = (bf16[3,512,256]{2,1,0:T(8,128)(2,1)S(1)}, bf16[3,512,256]{2,1,0:T(8,128)(2,1)S(1)}, u32[]{:S(2)}, u32[]{:S(2)}) collective-permute-start(bf16[3,512,256]{2,1,0:T(8,128)(2,1)S(1)} %get-tuple-element.135), channel_id=1, source_target_pairs={{0,4},{1,5},{2,6},{3,7},{4,0},{5,1},{6,2},{7,3},{8,12},{9,13},{10,... | collective-permute-start | bytes 2359304 | tf_op jit(solution)/shard_map/ppermute | solution.py:415
  164.2 17.0 %collective-permute-start.32 = (bf16[3,512,256]{2,1,0:T(8,128)(2,1)S(1)}, bf16[3,512,256]{2,1,0:T(8,128)(2,1)S(1)}, u32[]{:S(2)}, u32[]{:S(2)}) collective-permute-start(bf16[3,512,256]{2,1,0:T(8,128)(2,1)S(1)} %choose.9.refs_3_), channel_id=1, source_target_pairs={{0,2},{1,3},{2,0},{3,1},{4,6},{5,7},{6,4},{7,5},{8,10},{9,11},{10,... | collective-permute-start | bytes 2359304 | tf_op jit(solution)/shard_map/ppermute | solution.py:415
  167.4 26.8 %collective-permute-start.29 = (bf16[640,768]{1,0:T(8,128)(2,1)S(1)}, bf16[640,768]{1,0:T(8,128)(2,1)S(1)}, u32[]{:S(2)}, u32[]{:S(2)}) collective-permute-start(bf16[640,768]{1,0:T(8,128)(2,1)S(1)} %project.13), channel_id=1, source_target_pairs={{0,16},{1,17},{2,18},{3,19},{4,20},{5,21},{6,22},{7,23},{8,24},{9,... | collective-permute-start | bytes 2949128 | tf_op jit(solution)/shard_map/ppermute | solution.py:415
  179.0 19.4 %collective-permute-start.31 = (bf16[3,512,256]{2,1,0:T(8,128)(2,1)S(1)}, bf16[3,512,256]{2,1,0:T(8,128)(2,1)S(1)}, u32[]{:S(2)}, u32[]{:S(2)}) collective-permute-start(bf16[3,512,256]{2,1,0:T(8,128)(2,1)S(1)} %collective-permute-done.30.refs_1_), channel_id=1, source_target_pairs={{4,8},{5,9},{6,10},{7,11},{8,4},{9,5},{10,6},{11,7},{20,24},{21,25... | collective-permute-start | bytes 2359304 | tf_op jit(solution)/shard_map/ppermute | solution.py:415
  181.2 18.0 %collective-permute-start.36 = (bf16[3,512,256]{2,1,0:T(8,128)(2,1)S(1)}, bf16[3,512,256]{2,1,0:T(8,128)(2,1)S(1)}, u32[]{:S(2)}, u32[]{:S(2)}) collective-permute-start(bf16[3,512,256]{2,1,0:T(8,128)(2,1)S(1)} %collective-permute-done.28), channel_id=1, source_target_pairs={{4,0},{5,1},{6,2},{7,3},{8,12},{9,13},{10,14},{11,15},{20,16},{21,... | collective-permute-start | bytes 2359304 | tf_op jit(solution)/shard_map/ppermute | solution.py:415
  182.4 16.0 %collective-permute-start.33 = (bf16[1,256,1024]{2,1,0:T(8,128)(2,1)S(1)}, bf16[1,256,1024]{2,1,0:T(8,128)(2,1)S(1)}, u32[]{:S(2)}, u32[]{:S(2)}) collective-permute-start(bf16[1,256,1024]{2,1,0:T(8,128)(2,1)S(1)} %get-tuple-element.141), channel_id=1, source_target_pairs={{0,4},{1,5},{2,6},{3,7},{12,8},{13,9},{14,10},{15,11},{16,20},{17,... | collective-permute-start | bytes 1572872 | tf_op jit(solution)/shard_map/ppermute | solution.py:415
  187.3 17.8 %collective-permute-start.35 = (bf16[3,512,256]{2,1,0:T(8,128)(2,1)S(1)}, bf16[3,512,256]{2,1,0:T(8,128)(2,1)S(1)}, u32[]{:S(2)}, u32[]{:S(2)}) collective-permute-start(bf16[3,512,256]{2,1,0:T(8,128)(2,1)S(1)} %collective-permute-done.30.refs_1_), channel_id=1, source_target_pairs={{0,2},{1,3},{2,0},{3,1},{4,6},{5,7},{6,4},{7,5},{8,10},{9,11},{10,... | collective-permute-start | bytes 2359304 | tf_op jit(solution)/shard_map/ppermute | solution.py:415
  198.4 15.1 %collective-permute-start.34 = (bf16[1,256,2048]{2,1,0:T(8,128)(2,1)S(1)}, bf16[1,256,2048]{2,1,0:T(8,128)(2,1)S(1)}, u32[]{:S(2)}, u32[]{:S(2)}) collective-permute-start(bf16[1,256,2048]{2,1,0:T(8,128)(2,1)S(1)} %copy-done.4), channel_id=1, source_target_pairs={{4,8},{5,9},{6,10},{7,11},{8,4},{9,5},{10,6},{11,7},{20,24},{21,25... | collective-permute-start | bytes 3145736 | tf_op jit(solution)/shard_map/ppermute | solution.py:415
  205.0 14.6 %collective-permute-start.39 = (bf16[3,512,256]{2,1,0:T(8,128)(2,1)S(1)}, bf16[3,512,256]{2,1,0:T(8,128)(2,1)S(1)}, u32[]{:S(2)}, u32[]{:S(2)}) collective-permute-start(bf16[3,512,256]{2,1,0:T(8,128)(2,1)S(1)} %choose.11.refs_1_), channel_id=1, source_target_pairs={{0,2},{1,3},{2,0},{3,1},{4,6},{5,7},{6,4},{7,5},{8,10},{9,11},{10,... | collective-permute-start | bytes 2359304 | tf_op jit(solution)/shard_map/ppermute | solution.py:415
  221.4 7.5 %collective-permute-start.40 = (bf16[640,768]{1,0:T(8,128)(2,1)S(1)}, bf16[640,768]{1,0:T(8,128)(2,1)S(1)}, u32[]{:S(2)}, u32[]{:S(2)}) collective-permute-start(bf16[640,768]{1,0:T(8,128)(2,1)S(1)} %project.19), channel_id=1, source_target_pairs={{0,16},{1,17},{2,18},{3,19},{4,20},{5,21},{6,22},{7,23},{8,24},{9,... | collective-permute-start | bytes 2949128 | tf_op jit(solution)/shard_map/ppermute | solution.py:415
  221.5 14.3 %collective-permute-start.43 = (bf16[1,256,1024]{2,1,0:T(8,128)(2,1)S(1)}, bf16[1,256,1024]{2,1,0:T(8,128)(2,1)S(1)}, u32[]{:S(2)}, u32[]{:S(2)}) collective-permute-start(bf16[1,256,1024]{2,1,0:T(8,128)(2,1)S(1)} %choose.10.refs_6_.refs_8_), channel_id=1, source_target_pairs={{0,2},{1,3},{2,0},{3,1},{4,6},{5,7},{6,4},{7,5},{8,10},{9,11},{10,... | collective-permute-start | bytes 1572872 | tf_op jit(solution)/shard_map/ppermute | solution.py:415
  223.0 12.8 %collective-permute-start.42 = (bf16[1,256,1024]{2,1,0:T(8,128)(2,1)S(1)}, bf16[1,256,1024]{2,1,0:T(8,128)(2,1)S(1)}, u32[]{:S(2)}, u32[]{:S(2)}) collective-permute-start(bf16[1,256,1024]{2,1,0:T(8,128)(2,1)S(1)} %collective-permute-done.26), channel_id=1, source_target_pairs={{4,8},{5,9},{6,10},{7,11},{8,4},{9,5},{10,6},{11,7},{20,24},{21,25... | collective-permute-start | bytes 1572872 | tf_op jit(solution)/shard_map/ppermute | solution.py:415
  224.3 17.5 %collective-permute-start.41 = (bf16[1,256,1024]{2,1,0:T(8,128)(2,1)S(1)}, bf16[1,256,1024]{2,1,0:T(8,128)(2,1)S(1)}, u32[]{:S(2)}, u32[]{:S(2)}) collective-permute-start(bf16[1,256,1024]{2,1,0:T(8,128)(2,1)S(1)} %get-tuple-element.152), channel_id=1, source_target_pairs={{4,0},{5,1},{6,2},{7,3},{8,12},{9,13},{10,14},{11,15},{20,16},{21,... | collective-permute-start | bytes 1572872 | tf_op jit(solution)/shard_map/ppermute | solution.py:415
  225.6 16.2 %collective-permute-start.45 = (bf16[640,256]{1,0:T(8,128)(2,1)S(1)}, bf16[640,256]{1,0:T(8,128)(2,1)S(1)}, u32[]{:S(2)}, u32[]{:S(2)}) collective-permute-start(bf16[640,256]{1,0:T(8,128)(2,1)S(1)} %collective-permute-done.37.refs_2_), channel_id=1, source_target_pairs={{0,1},{1,0},{2,3},{3,2},{4,5},{5,4},{6,7},{7,6},{8,9},{9,8},{10,11... | collective-permute-start | bytes 983048 | tf_op jit(solution)/shard_map/ppermute | solution.py:415
  241.8 9.0 %collective-permute-start.44 = (bf16[640,256]{1,0:T(8,128)(2,1)S(1)}, bf16[640,256]{1,0:T(8,128)(2,1)S(1)}, u32[]{:S(2)}, u32[]{:S(2)}) collective-permute-start(bf16[640,256]{1,0:T(8,128)(2,1)S(1)} %attend.3.refs_0_), channel_id=1, source_target_pairs={{0,4},{1,5},{2,6},{3,7},{4,0},{5,1},{6,2},{7,3},{8,12},{9,13},{10,... | collective-permute-start | bytes 983048 | tf_op jit(solution)/shard_map/ppermute | solution.py:415
  252.0 14.4 %collective-permute-start.49 = (bf16[1,256,1024]{2,1,0:T(8,128)(2,1)S(1)}, bf16[1,256,1024]{2,1,0:T(8,128)(2,1)S(1)}, u32[]{:S(2)}, u32[]{:S(2)}) collective-permute-start(bf16[1,256,1024]{2,1,0:T(8,128)(2,1)S(1)} %choose.12.refs_10_.refs_6_), channel_id=1, source_target_pairs={{0,2},{1,3},{2,0},{3,1},{4,6},{5,7},{6,4},{7,5},{8,10},{9,11},{10,... | collective-permute-start | bytes 1572872 | tf_op jit(solution)/shard_map/ppermute | solution.py:415
  252.6 13.8 %collective-permute-start.48 = (bf16[1,256,1024]{2,1,0:T(8,128)(2,1)S(1)}, bf16[1,256,1024]{2,1,0:T(8,128)(2,1)S(1)}, u32[]{:S(2)}, u32[]{:S(2)}) collective-permute-start(bf16[1,256,1024]{2,1,0:T(8,128)(2,1)S(1)} %collective-permute-done.33.b_ref), channel_id=1, source_target_pairs={{4,8},{5,9},{6,10},{7,11},{8,4},{9,5},{10,6},{11,7},{20,24},{21,25... | collective-permute-start | bytes 1572872 | tf_op jit(solution)/shard_map/ppermute | solution.py:415
  253.3 15.9 %collective-permute-start.47 = (bf16[1,256,1024]{2,1,0:T(8,128)(2,1)S(1)}, bf16[1,256,1024]{2,1,0:T(8,128)(2,1)S(1)}, u32[]{:S(2)}, u32[]{:S(2)}) collective-permute-start(bf16[1,256,1024]{2,1,0:T(8,128)(2,1)S(1)} %collective-permute-done.42), channel_id=1, source_target_pairs={{4,0},{5,1},{6,2},{7,3},{8,12},{9,13},{10,14},{11,15},{20,16},{21,... | collective-permute-start | bytes 1572872 | tf_op jit(solution)/shard_map/ppermute | solution.py:415
  254.8 15.0 %collective-permute-start.51 = (bf16[640,256]{1,0:T(8,128)(2,1)S(1)}, bf16[640,256]{1,0:T(8,128)(2,1)S(1)}, u32[]{:S(2)}, u32[]{:S(2)}) collective-permute-start(bf16[640,256]{1,0:T(8,128)(2,1)S(1)} %collective-permute-done.44.refs_2_), channel_id=1, source_target_pairs={{0,1},{1,0},{2,3},{3,2},{4,5},{5,4},{6,7},{7,6},{8,9},{9,8},{10,11... | collective-permute-start | bytes 983048 | tf_op jit(solution)/shard_map/ppermute | solution.py:415
  256.4 15.4 %collective-permute-start.50 = (bf16[640,256]{1,0:T(8,128)(2,1)S(1)}, bf16[640,256]{1,0:T(8,128)(2,1)S(1)}, u32[]{:S(2)}, u32[]{:S(2)}) collective-permute-start(bf16[640,256]{1,0:T(8,128)(2,1)S(1)} %attend.3.refs_0_), channel_id=1, source_target_pairs={{0,1},{1,0},{2,3},{3,2},{4,5},{5,4},{6,7},{7,6},{8,9},{9,8},{10,11... | collective-permute-start | bytes 983048 | tf_op jit(solution)/shard_map/ppermute | solution.py:415
  272.5 14.3 %collective-permute-start.53 = (bf16[1,256,1024]{2,1,0:T(8,128)(2,1)S(1)}, bf16[1,256,1024]{2,1,0:T(8,128)(2,1)S(1)}, u32[]{:S(2)}, u32[]{:S(2)}) collective-permute-start(bf16[1,256,1024]{2,1,0:T(8,128)(2,1)S(1)} %choose.13.refs_8_.refs_10_), channel_id=1, source_target_pairs={{0,2},{1,3},{2,0},{3,1},{4,6},{5,7},{6,4},{7,5},{8,10},{9,11},{10,... | collective-permute-start | bytes 1572872 | tf_op jit(solution)/shard_map/ppermute | solution.py:415
  290.4 18.8 %collective-permute-start.54 = (bf16[640,1024]{1,0:T(8,128)(2,1)S(1)}, bf16[640,1024]{1,0:T(8,128)(2,1)S(1)}, u32[]{:S(2)}, u32[]{:S(2)}) collective-permute-start(bf16[640,1024]{1,0:T(8,128)(2,1)S(1)} %combine.6.a_ref), channel_id=1, source_target_pairs={{0,16},{1,17},{2,18},{3,19},{4,20},{5,21},{6,22},{7,23},{8,24},{9,... | collective-permute-start | bytes 3932168 | tf_op jit(solution)/shard_map/ppermute | solution.py:415
  291.9 17.4 %collective-permute-start.56 = (bf16[320,1024]{1,0:T(8,128)(2,1)S(1)}, bf16[320,1024]{1,0:T(8,128)(2,1)S(1)}, u32[]{:S(2)}, u32[]{:S(2)}) collective-permute-start(bf16[320,1024]{1,0:T(8,128)(2,1)S(1)} %join.1), channel_id=1, source_target_pairs={{0,4},{1,5},{2,6},{3,7},{4,0},{5,1},{6,2},{7,3},{8,12},{9,13},{10,... | collective-permute-start | bytes 1966088 | tf_op jit(solution)/shard_map/ppermute | solution.py:415
  (16 other events, 213.0 us)

commit v12 on v11

--- a/solution.py
+++ b/solution.py
@@ -462,16 +462,17 @@
         rows, top, bottom = own_rows_of(here, after(tokens, *begun), own_kind)
         fetched = over_tensor(rows)
         low_b, high_b, mine_b, away_b = halves(here, after(weight, *begun), 1, 2)
-
-        begun = (m2a, mine_b)
+        low_o, high_o, mine_o, away_o = halves(here, after(out_weight, *begun), 0, 1)
+
+        begun = (m2a, mine_b, mine_o)
         m3a = move(e2a, across, p2a, *begun)
         passed_top = move(top, edge, e2a, p2a, *begun)
-        low_o, high_o, mine_o, away_o = halves(here, after(out_weight, *begun), 0, 1)
+        o1o = move(low_o, outward, e2a, p2a, *begun)
         third_a = choose(here, after(e2a, *begun), m2a)
         p3a = move(third_a, pair, p2a)
 
-        begun = (m3a, mine_o)
-        swapped = [to_core(a, *begun) for a in fetched[1:]]
+        begun = (m3a,)
+        swapped = [to_core(a, passed_top, p3a, *begun) for a in fetched[1:]]
         shape = (2, places, length, kept)
         normed = normalize(
             here, "own", None, gains, after(tokens, *begun), fetched[1:], swapped, shape, 0, half
@@ -479,12 +480,11 @@
         m4a = move(e1a, across, passed_top, p3a, *begun)
         m1b = move(low_b, across_or_stay, passed_top, p3a, *begun)
         passed_bottom = move(bottom, edge, passed_top, p3a, *begun)
-        o1o = move(low_o, outward, passed_top, p3a, *begun)
         p1b = move(mine_b, pair, p3a, *begun)
         part_top = over_tensor(after(passed_top, *begun))
 
-        begun = (passed_bottom, o1o, normed)
-        e3a = move(m3a, outward, part_top[-1], *begun)
+        begun = (passed_bottom, normed)
+        e3a = move(m3a, outward, part_top[-1], o1o, *begun)
         i1o = move(low_o, inward, part_top[-1], *begun)
         p1o = move(mine_o, pair, p1b, *begun)
         other_kind = kinds_behind(here, after(passed_bottom, *begun), length)
@@ -554,13 +554,14 @@
         ours_b = project(here, 0, late_normed, last_b, total_b, final=True)
         attended_b = attend(here, own_kind, other_kind, ours_b, got_b)
 
-        passed_b = move(attended_b, edge, o2o, m3o, p2o)
-        begun = (passed_b, held_a[-1])
-        m4o = move(i2o, across, *begun)
+        begun = (m3o, o2o, p2o, attended_b, held_a[-1])
+        passed_b = move(attended_b, edge, *begun)
+        held_b = over_tensor(after(attended_b, *begun))
+        m4o = move(i2o, across, held_b[1], *begun)
         o3o = move(m3o, outward, *begun)
         third_o = choose(here, after(o2o, *begun), m2o)
         p3o = move(third_o, pair, p2o)
-        held_b = over_tensor(after(attended_b, *begun)) + over_tensor(after(passed_b, *begun))
+        held_b += over_tensor(after(passed_b, *begun))
         pieces_a = stack(here, [after(held_a[0], *begun)] + held_a[1:])
         pieces_a = (pieces_a, to_core(pieces_a))
         both = ("partner", "own")

time: 314 us -> 290 us (0.924)
  waiting for transfers between devices: 171 us -> 143 us
  starting transfers between devices: 77.4 us -> 80.9 us
    ppermute x58, waiting for transfers between devices: 171 us -> 143 us  [move(): lax.ppermute(after(array, *earlier) if earlier else array, AXES, pairs)]
    ppermute x58, starting transfers between devices: 77.4 us -> 80.9 us  [move(): lax.ppermute(after(array, *earlier) if earlier else array, AXES, pairs)]
  transfers between devices with their start and end apart: 58 -> 58, of which waited for: 27 -> 30; matrix products, arithmetic and copies ran while one was open for 0% -> 0% of each run, Pallas kernels for 17% -> 18%
where the time goes in v12:
time: 290 us
  waiting for transfers between devices  143 us (49%)
  starting transfers between devices  80.9 us (28%)
  Pallas kernels  60.7 us (21%)
  local copies, waits for them, and re-layouts  4.34 us (1%)
    ppermute x58, waiting for transfers between devices, move(): lax.ppermute(after(array, *earlier) if earlier else array, AXES, pairs)  143 us
    ppermute x58, starting transfers between devices, move(): lax.ppermute(after(array, *earlier) if earlier else array, AXES, pairs)  80.9 us
    pallas_call x35, Pallas kernels, call(): pl.pallas_call(kernel, in_specs=[pl.BlockSpec(memory_space=SMEM)] + [pl.B...  58.4 us
  transfers between devices with their start and end apart: 58, of which 30 were waited for; matrix products, arithmetic and copies ran while one was open for 0% of the time, Pallas kernels for 18%

profile of v12, /device:TPU:0, one launch (start us, length us, event | category | flops | bytes accessed | tf_op | source)
XLA Modules:
  0.0 289.6 jit_solution(5132877312409791943)
XLA Ops:
  0.8 1.9 copy-done
  3.5 3.0 %collective-permute-start.2 = (bf16[3,512,256]{2,1,0:T(8,128)(2,1)S(1)}, bf16[3,512,256]{2,1,0:T(8,128)(2,1)S(1)}, u32[]{:S(2)}, u32[]{:S(2)}) collective-permute-start(bf16[3,512,256]{2,1,0:T(8,128)(2,1)S(1)} %get-tuple-element.92.refs_1_), channel_id=1, source_target_pairs={{0,2},{1,3},{2,0},{3,1},{4,6},{5,7},{6,4},{7,5},{8,10},{9,11},{10,... | collective-permute-start | bytes 2359304 | tf_op jit(solution)/shard_map/ppermute | solution.py:415
  7.2 4.4 %collective-permute-start.1 = (bf16[3,512,256]{2,1,0:T(8,128)(2,1)S(1)}, bf16[3,512,256]{2,1,0:T(8,128)(2,1)S(1)}, u32[]{:S(2)}, u32[]{:S(2)}) collective-permute-start(bf16[3,512,256]{2,1,0:T(8,128)(2,1)S(1)} %get-tuple-element.91), channel_id=1, source_target_pairs={{0,4},{1,5},{2,6},{3,7},{4,0},{5,1},{6,2},{7,3},{8,12},{9,13},{10,... | collective-permute-start | bytes 2359304 | tf_op jit(solution)/shard_map/ppermute | solution.py:415
  11.6 12.4 %collective-permute-done.2.refs_2_ = bf16[3,512,256]{2,1,0:T(8,128)(2,1)S(1)} collective-permute-done((bf16[3,512,256]{2,1,0:T(8,128)(2,1)S(1)}, bf16[3,512,256]{2,1,0:T(8,128)(2,1)S(1)}, u32[]{:S(2)}, u32[]{:S(2)}) %collective-permute-start.2) | collective-permute-done | bytes 786464 | tf_op jit(solution)/shard_map/ppermute | solution.py:415
  24.0 4.6 %collective-permute-done.1.refs_3_ = bf16[3,512,256]{2,1,0:T(8,128)(2,1)S(1)} collective-permute-done((bf16[3,512,256]{2,1,0:T(8,128)(2,1)S(1)}, bf16[3,512,256]{2,1,0:T(8,128)(2,1)S(1)}, u32[]{:S(2)}, u32[]{:S(2)}) %collective-permute-start.1) | collective-permute-done | bytes 786464 | tf_op jit(solution)/shard_map/ppermute | solution.py:415
  29.9 3.4 %collective-permute-start.3 = (bf16[3,512,256]{2,1,0:T(8,128)(2,1)S(1)}, bf16[3,512,256]{2,1,0:T(8,128)(2,1)S(1)}, u32[]{:S(2)}, u32[]{:S(2)}) collective-permute-start(bf16[3,512,256]{2,1,0:T(8,128)(2,1)S(1)} %collective-permute-done), channel_id=1, source_target_pairs={{0,4},{1,5},{2,6},{3,7},{4,0},{5,1},{6,2},{7,3},{8,12},{9,13},{10,... | collective-permute-start | bytes 2359304 | tf_op jit(solution)/shard_map/ppermute | solution.py:415
  39.6 7.8 %collective-permute-done.4.refs_4_ = bf16[3,512,256]{2,1,0:T(8,128)(2,1)S(1)} collective-permute-done((bf16[3,512,256]{2,1,0:T(8,128)(2,1)S(1)}, bf16[3,512,256]{2,1,0:T(8,128)(2,1)S(1)}, u32[]{:S(2)}, u32[]{:S(2)}) %collective-permute-start.4) | collective-permute-done | bytes 786464 | tf_op jit(solution)/shard_map/ppermute | solution.py:415
  51.7 4.5 %collective-permute-start.6 = (bf16[160,2048]{1,0:T(8,128)(2,1)S(1)}, bf16[160,2048]{1,0:T(8,128)(2,1)S(1)}, u32[]{:S(2)}, u32[]{:S(2)}) collective-permute-start(bf16[160,2048]{1,0:T(8,128)(2,1)S(1)} %get-tuple-element.101), channel_id=1, source_target_pairs={{0,4},{1,5},{2,6},{3,7},{4,0},{5,1},{6,2},{7,3},{8,12},{9,13},{10,... | collective-permute-start | bytes 1966088 | tf_op jit(solution)/shard_map/ppermute | solution.py:415
  56.2 7.9 %collective-permute-done.10.refs_2_ = bf16[320,2048]{1,0:T(8,128)(2,1)S(1)} collective-permute-done((bf16[320,2048]{1,0:T(8,128)(2,1)S(1)}, bf16[320,2048]{1,0:T(8,128)(2,1)S(1)}, u32[]{:S(2)}, u32[]{:S(2)}) %collective-permute-start.10) | collective-permute-done | bytes 1310752 | tf_op jit(solution)/shard_map/ppermute | solution.py:415
  64.1 3.3 %collective-permute-done.6.refs_2_ = bf16[160,2048]{1,0:T(8,128)(2,1)S(1)} collective-permute-done((bf16[160,2048]{1,0:T(8,128)(2,1)S(1)}, bf16[160,2048]{1,0:T(8,128)(2,1)S(1)}, u32[]{:S(2)}, u32[]{:S(2)}) %collective-permute-start.6) | collective-permute-done | bytes 655392 | tf_op jit(solution)/shard_map/ppermute | solution.py:415
  67.4 3.4 %collective-permute-start.9 = (bf16[176,2048]{1,0:T(8,128)(2,1)S(1)}, bf16[176,2048]{1,0:T(8,128)(2,1)S(1)}, u32[]{:S(2)}, u32[]{:S(2)}) collective-permute-start(bf16[176,2048]{1,0:T(8,128)(2,1)S(1)} %get-tuple-element.105), channel_id=1, source_target_pairs={{0,4},{1,5},{2,6},{3,7},{4,0},{5,1},{6,2},{7,3},{8,12},{9,13},{10,... | collective-permute-start | bytes 2162696 | tf_op jit(solution)/shard_map/ppermute | solution.py:415
  75.8 3.2 %normalize.3.refs_0_ = bf16[2,8,640,512]{3,2,1,0:T(8,128)(2,1)S(1)} custom-call(s32[3]{0:T(128)S(1)} %pad_add_fusion.h_ref._, f32[8,1,512]{2,1,0:T(1,128)S(1)} %bitcast.9, bf16[640,2048]{1,0:T(8,128)(2,1)S(1)} %copy-done.3, bf16[320,2048]{1,0:T(8,128)(2,1)S(1)} %collective-permute-done.10.refs_2_, bf16[320,2048]{1,0:T(8,128)(2,1)S(1)} %collective-permute-done.11.refs_3_), custom_call_target="tpu_custom_call" | custom-call | tf_op jit(solution)/shard_map/normalize/pallas_call | solution.py:32
  79.0 8.7 %collective-permute-done.12.refs_3_ = bf16[160,2048]{1,0:T(8,128)(2,1)S(1)} collective-permute-done((bf16[160,2048]{1,0:T(8,128)(2,1)S(1)}, bf16[160,2048]{1,0:T(8,128)(2,1)S(1)}, u32[]{:S(2)}, u32[]{:S(2)}) %collective-permute-start.12) | collective-permute-done | bytes 655392 | tf_op jit(solution)/shard_map/ppermute | solution.py:415
  88.3 10.5 %collective-permute-done.21.a_ref = bf16[1,256,1024]{2,1,0:T(8,128)(2,1)S(1)} collective-permute-done((bf16[1,256,1024]{2,1,0:T(8,128)(2,1)S(1)}, bf16[1,256,1024]{2,1,0:T(8,128)(2,1)S(1)}, u32[]{:S(2)}, u32[]{:S(2)}) %collective-permute-start.21) | collective-permute-done | bytes 524320 | tf_op jit(solution)/shard_map/ppermute | solution.py:415
  103.9 4.6 %collective-permute-start.26 = (bf16[1,256,1024]{2,1,0:T(8,128)(2,1)S(1)}, bf16[1,256,1024]{2,1,0:T(8,128)(2,1)S(1)}, u32[]{:S(2)}, u32[]{:S(2)}) collective-permute-start(bf16[1,256,1024]{2,1,0:T(8,128)(2,1)S(1)} %get-tuple-element.129), channel_id=1, source_target_pairs={{0,4},{1,5},{2,6},{3,7},{12,8},{13,9},{14,10},{15,11},{16,20},{17,... | collective-permute-start | bytes 1572872 | tf_op jit(solution)/shard_map/ppermute | solution.py:415
  109.0 3.7 %project.10.refs_7_ = f32[2,640,768]{2,1,0:T(8,128)S(1)} custom-call(s32[3]{0:T(128)S(1)} %pad_add_fusion.h_ref._, bf16[2,8,640,512]{3,2,1,0:T(8,128)(2,1)S(1)} %normalize.3.refs_0_, bf16[3,512,256]{2,1,0:T(8,128)(2,1)S(1)} %get-tuple-element.92.refs_1_, bf16[3,512,256]{2,1,0:T(8,128)(2,1)S(1)} %collective-permute-done.2.refs_2_, ...), custom_call_target="tpu_custom_call" | custom-call | tf_op jit(solution)/shard_map/project/pallas_call | solution.py:32
  112.8 1.8 normalize.4.refs_0_
  115.3 5.5 %collective-permute-done.22.a_ref = bf16[3,512,256]{2,1,0:T(8,128)(2,1)S(1)} collective-permute-done((bf16[3,512,256]{2,1,0:T(8,128)(2,1)S(1)}, bf16[3,512,256]{2,1,0:T(8,128)(2,1)S(1)}, u32[]{:S(2)}, u32[]{:S(2)}) %collective-permute-start.22) | collective-permute-done | bytes 786464 | tf_op jit(solution)/shard_map/ppermute | solution.py:415
  127.5 1.8 normalize.5.refs_0_
  129.3 3.7 %project.11.refs_3_ = f32[2,640,768]{2,1,0:T(8,128)S(1)} custom-call(s32[3]{0:T(128)S(1)} %pad_add_fusion.h_ref._, bf16[2,8,640,512]{3,2,1,0:T(8,128)(2,1)S(1)} %normalize.5.refs_0_, bf16[3,512,256]{2,1,0:T(8,128)(2,1)S(1)} %get-tuple-element.92.refs_1_, bf16[3,512,256]{2,1,0:T(8,128)(2,1)S(1)} %collective-permute-done.2.refs_2_, ...), custom_call_target="tpu_custom_call", output_to_operand_aliasing={{}: (8, {})} | custom-call | tf_op jit(solution)/shard_map/project/pallas_call | solution.py:32
  133.1 6.3 %collective-permute-done.27.a_ref = bf16[3,512,256]{2,1,0:T(8,128)(2,1)S(1)} collective-permute-done((bf16[3,512,256]{2,1,0:T(8,128)(2,1)S(1)}, bf16[3,512,256]{2,1,0:T(8,128)(2,1)S(1)}, u32[]{:S(2)}, u32[]{:S(2)}) %collective-permute-start.27) | collective-permute-done | bytes 786464 | tf_op jit(solution)/shard_map/ppermute | solution.py:415
  140.8 3.1 %collective-permute-start.30 = (bf16[3,512,256]{2,1,0:T(8,128)(2,1)S(1)}, bf16[3,512,256]{2,1,0:T(8,128)(2,1)S(1)}, u32[]{:S(2)}, u32[]{:S(2)}) collective-permute-start(bf16[3,512,256]{2,1,0:T(8,128)(2,1)S(1)} %get-tuple-element.134), channel_id=1, source_target_pairs={{0,4},{1,5},{2,6},{3,7},{4,0},{5,1},{6,2},{7,3},{8,12},{9,13},{10,... | collective-permute-start | bytes 2359304 | tf_op jit(solution)/shard_map/ppermute | solution.py:415
  149.5 9.6 %collective-permute-done.30.refs_1_ = bf16[3,512,256]{2,1,0:T(8,128)(2,1)S(1)} collective-permute-done((bf16[3,512,256]{2,1,0:T(8,128)(2,1)S(1)}, bf16[3,512,256]{2,1,0:T(8,128)(2,1)S(1)}, u32[]{:S(2)}, u32[]{:S(2)}) %collective-permute-start.30) | collective-permute-done | bytes 786464 | tf_op jit(solution)/shard_map/ppermute | solution.py:415
  162.6 4.8 %collective-permute-start.33 = (bf16[1,256,1024]{2,1,0:T(8,128)(2,1)S(1)}, bf16[1,256,1024]{2,1,0:T(8,128)(2,1)S(1)}, u32[]{:S(2)}, u32[]{:S(2)}) collective-permute-start(bf16[1,256,1024]{2,1,0:T(8,128)(2,1)S(1)} %get-tuple-element.140), channel_id=1, source_target_pairs={{0,4},{1,5},{2,6},{3,7},{12,8},{13,9},{14,10},{15,11},{16,20},{17,... | collective-permute-start | bytes 1572872 | tf_op jit(solution)/shard_map/ppermute | solution.py:415
  168.9 2.7 project.14.refs_5_
  171.6 2.7 project.15.refs_3_
  174.4 4.2 %attend.2.refs_0_ = bf16[640,256]{1,0:T(8,128)(2,1)S(1)} custom-call(s32[3]{0:T(128)S(1)} %pad_add_fusion.h_ref._, s32[1,640]{1,0:T(1,128)S(1)} %broadcast_in_dim.3.kind_ref.own_kind_ref, s32[1,640]{1,0:T(1,128)S(1)} %kinds_behind.1.other_kind_ref.kind_ref, bf16[640,768]{1,0:T(8,128)(2,1)S(1)} %project.12.own_ref, ...), custom_call_target="tpu_custom_call" | custom-call | tf_op jit(solution)/shard_map/attend/pallas_call | solution.py:32
  179.9 5.2 %collective-permute-done.35.refs_2_ = bf16[3,512,256]{2,1,0:T(8,128)(2,1)S(1)} collective-permute-done((bf16[3,512,256]{2,1,0:T(8,128)(2,1)S(1)}, bf16[3,512,256]{2,1,0:T(8,128)(2,1)S(1)}, u32[]{:S(2)}, u32[]{:S(2)}) %collective-permute-start.35) | collective-permute-done | bytes 786464 | tf_op jit(solution)/shard_map/ppermute | solution.py:415
  188.7 1.9 project.16.refs_3_
  190.6 1.9 project.17.refs_3_
  193.7 5.9 %collective-permute-done.41.refs_2_ = bf16[3,512,256]{2,1,0:T(8,128)(2,1)S(1)} collective-permute-done((bf16[3,512,256]{2,1,0:T(8,128)(2,1)S(1)}, bf16[3,512,256]{2,1,0:T(8,128)(2,1)S(1)}, u32[]{:S(2)}, u32[]{:S(2)}) %collective-permute-start.41) | collective-permute-done | bytes 786464 | tf_op jit(solution)/shard_map/ppermute | solution.py:415
  208.8 4.2 %attend.3.refs_0_ = bf16[640,256]{1,0:T(8,128)(2,1)S(1)} custom-call(s32[3]{0:T(128)S(1)} %pad_add_fusion.h_ref._, s32[1,640]{1,0:T(1,128)S(1)} %broadcast_in_dim.3.kind_ref.own_kind_ref, s32[1,640]{1,0:T(1,128)S(1)} %kinds_behind.1.other_kind_ref.kind_ref, bf16[640,768]{1,0:T(8,128)(2,1)S(1)} %project.18.own_ref, ...), custom_call_target="tpu_custom_call" | custom-call | tf_op jit(solution)/shard_map/attend/pallas_call | solution.py:32
  213.0 2.4 collective-permute-done.44.refs_3_
  215.7 3.7 %collective-permute-done.40.a_ref = bf16[1,256,1024]{2,1,0:T(8,128)(2,1)S(1)} collective-permute-done((bf16[1,256,1024]{2,1,0:T(8,128)(2,1)S(1)}, bf16[1,256,1024]{2,1,0:T(8,128)(2,1)S(1)}, u32[]{:S(2)}, u32[]{:S(2)}) %collective-permute-start.40) | collective-permute-done | bytes 524320 | tf_op jit(solution)/shard_map/ppermute | solution.py:415
  221.7 3.7 %collective-permute-start.50 = (bf16[640,256]{1,0:T(8,128)(2,1)S(1)}, bf16[640,256]{1,0:T(8,128)(2,1)S(1)}, u32[]{:S(2)}, u32[]{:S(2)}) collective-permute-start(bf16[640,256]{1,0:T(8,128)(2,1)S(1)} %attend.3.refs_0_), channel_id=1, source_target_pairs={{0,4},{1,5},{2,6},{3,7},{4,0},{5,1},{6,2},{7,3},{8,12},{9,13},{10,... | collective-permute-start | bytes 983048 | tf_op jit(solution)/shard_map/ppermute | solution.py:415
  227.9 2.4 collective-permute-done.47.refs_1_
  231.2 2.7 collective-permute-done.50.refs_2_
  234.4 2.1 combine.4.refs_12_
  236.5 3.3 %collective-permute-done.49.refs_11_.refs_7_ = bf16[1,256,1024]{2,1,0:T(8,128)(2,1)S(1)} collective-permute-done((bf16[1,256,1024]{2,1,0:T(8,128)(2,1)S(1)}, bf16[1,256,1024]{2,1,0:T(8,128)(2,1)S(1)}, u32[]{:S(2)}, u32[]{:S(2)}) %collective-permute-start.49) | collective-permute-done | bytes 524320 | tf_op jit(solution)/shard_map/ppermute | solution.py:415
  239.7 4.9 %collective-permute-done.46.a_ref = bf16[1,256,1024]{2,1,0:T(8,128)(2,1)S(1)} collective-permute-done((bf16[1,256,1024]{2,1,0:T(8,128)(2,1)S(1)}, bf16[1,256,1024]{2,1,0:T(8,128)(2,1)S(1)}, u32[]{:S(2)}, u32[]{:S(2)}) %collective-permute-start.46) | collective-permute-done | bytes 524320 | tf_op jit(solution)/shard_map/ppermute | solution.py:415
  246.6 2.4 collective-permute-done.52.refs_1_.refs_3_.refs_5_
  249.0 2.8 combine.5.refs_12_
  251.8 8.5 %collective-permute-done.53.refs_9_.refs_11_ = bf16[1,256,1024]{2,1,0:T(8,128)(2,1)S(1)} collective-permute-done((bf16[1,256,1024]{2,1,0:T(8,128)(2,1)S(1)}, bf16[1,256,1024]{2,1,0:T(8,128)(2,1)S(1)}, u32[]{:S(2)}, u32[]{:S(2)}) %collective-permute-start.53) | collective-permute-done | bytes 524320 | tf_op jit(solution)/shard_map/ppermute | solution.py:415
  260.3 1.8 combine.7
  265.4 4.7 %collective-permute-start.56 = (bf16[320,1024]{1,0:T(8,128)(2,1)S(1)}, bf16[320,1024]{1,0:T(8,128)(2,1)S(1)}, u32[]{:S(2)}, u32[]{:S(2)}) collective-permute-start(bf16[320,1024]{1,0:T(8,128)(2,1)S(1)} %join.1), channel_id=1, source_target_pairs={{0,4},{1,5},{2,6},{3,7},{4,0},{5,1},{6,2},{7,3},{8,12},{9,13},{10,... | collective-permute-start | bytes 1966088 | tf_op jit(solution)/shard_map/ppermute | solution.py:415
  270.1 14.9 %collective-permute-done.56.c_ref = bf16[320,1024]{1,0:T(8,128)(2,1)S(1)} collective-permute-done((bf16[320,1024]{1,0:T(8,128)(2,1)S(1)}, bf16[320,1024]{1,0:T(8,128)(2,1)S(1)}, u32[]{:S(2)}, u32[]{:S(2)}) %collective-permute-start.56) | collective-permute-done | bytes 655392 | tf_op jit(solution)/shard_map/ppermute | solution.py:415
  285.0 2.1 collective-permute-done.57.d_ref
  287.1 2.4 shard_map.55
  (118 shorter events, 71.6 us)
Async XLA Ops:
  3.5 20.6 %collective-permute-start.2 = (bf16[3,512,256]{2,1,0:T(8,128)(2,1)S(1)}, bf16[3,512,256]{2,1,0:T(8,128)(2,1)S(1)}, u32[]{:S(2)}, u32[]{:S(2)}) collective-permute-start(bf16[3,512,256]{2,1,0:T(8,128)(2,1)S(1)} %get-tuple-element.92.refs_1_), channel_id=1, source_target_pairs={{0,2},{1,3},{2,0},{3,1},{4,6},{5,7},{6,4},{7,5},{8,10},{9,11},{10,... | collective-permute-start | bytes 2359304 | tf_op jit(solution)/shard_map/ppermute | solution.py:415
  6.5 17.5 %collective-permute-start = (bf16[3,512,256]{2,1,0:T(8,128)(2,1)S(1)}, bf16[3,512,256]{2,1,0:T(8,128)(2,1)S(1)}, u32[]{:S(2)}, u32[]{:S(2)}) collective-permute-start(bf16[3,512,256]{2,1,0:T(8,128)(2,1)S(1)} %get-tuple-element.87), channel_id=1, source_target_pairs={{0,0},{1,1},{2,2},{3,3},{4,8},{5,9},{6,10},{7,11},{8,4},{9,5},{10,... | collective-permute-start | bytes 2359304 | tf_op jit(solution)/shard_map/ppermute | solution.py:415
  7.2 21.4 %collective-permute-start.1 = (bf16[3,512,256]{2,1,0:T(8,128)(2,1)S(1)}, bf16[3,512,256]{2,1,0:T(8,128)(2,1)S(1)}, u32[]{:S(2)}, u32[]{:S(2)}) collective-permute-start(bf16[3,512,256]{2,1,0:T(8,128)(2,1)S(1)} %get-tuple-element.91), channel_id=1, source_target_pairs={{0,4},{1,5},{2,6},{3,7},{4,0},{5,1},{6,2},{7,3},{8,12},{9,13},{10,... | collective-permute-start | bytes 2359304 | tf_op jit(solution)/shard_map/ppermute | solution.py:415
  28.6 11.0 %collective-permute-start.5 = (bf16[3,512,256]{2,1,0:T(8,128)(2,1)S(1)}, bf16[3,512,256]{2,1,0:T(8,128)(2,1)S(1)}, u32[]{:S(2)}, u32[]{:S(2)}) collective-permute-start(bf16[3,512,256]{2,1,0:T(8,128)(2,1)S(1)} %get-tuple-element.96), channel_id=1, source_target_pairs={{4,8},{5,9},{6,10},{7,11},{8,4},{9,5},{10,6},{11,7},{20,24},{21,25... | collective-permute-start | bytes 2359304 | tf_op jit(solution)/shard_map/ppermute | solution.py:415
  29.3 18.2 %collective-permute-start.4 = (bf16[3,512,256]{2,1,0:T(8,128)(2,1)S(1)}, bf16[3,512,256]{2,1,0:T(8,128)(2,1)S(1)}, u32[]{:S(2)}, u32[]{:S(2)}) collective-permute-start(bf16[3,512,256]{2,1,0:T(8,128)(2,1)S(1)} %collective-permute-done.1.refs_3_), channel_id=1, source_target_pairs={{0,2},{1,3},{2,0},{3,1},{4,6},{5,7},{6,4},{7,5},{8,10},{9,11},{10,... | collective-permute-start | bytes 2359304 | tf_op jit(solution)/shard_map/ppermute | solution.py:415
  29.9 18.9 %collective-permute-start.3 = (bf16[3,512,256]{2,1,0:T(8,128)(2,1)S(1)}, bf16[3,512,256]{2,1,0:T(8,128)(2,1)S(1)}, u32[]{:S(2)}, u32[]{:S(2)}) collective-permute-start(bf16[3,512,256]{2,1,0:T(8,128)(2,1)S(1)} %collective-permute-done), channel_id=1, source_target_pairs={{0,4},{1,5},{2,6},{3,7},{4,0},{5,1},{6,2},{7,3},{8,12},{9,13},{10,... | collective-permute-start | bytes 2359304 | tf_op jit(solution)/shard_map/ppermute | solution.py:415
  35.8 28.3 %collective-permute-start.10 = (bf16[320,2048]{1,0:T(8,128)(2,1)S(1)}, bf16[320,2048]{1,0:T(8,128)(2,1)S(1)}, u32[]{:S(2)}, u32[]{:S(2)}) collective-permute-start(bf16[320,2048]{1,0:T(8,128)(2,1)S(1)} %get-tuple-element.107), channel_id=1, source_target_pairs={{0,1},{1,0},{2,3},{3,2},{4,5},{5,4},{6,7},{7,6},{8,9},{9,8},{10,11... | collective-permute-start | bytes 3932168 | tf_op jit(solution)/shard_map/ppermute | solution.py:415
  48.8 18.6 %collective-permute-start.8 = (bf16[3,512,256]{2,1,0:T(8,128)(2,1)S(1)}, bf16[3,512,256]{2,1,0:T(8,128)(2,1)S(1)}, u32[]{:S(2)}, u32[]{:S(2)}) collective-permute-start(bf16[3,512,256]{2,1,0:T(8,128)(2,1)S(1)} %collective-permute-done.3.a_ref), channel_id=1, source_target_pairs={{4,8},{5,9},{6,10},{7,11},{8,4},{9,5},{10,6},{11,7},{20,24},{21,25... | collective-permute-start | bytes 2359304 | tf_op jit(solution)/shard_map/ppermute | solution.py:415
  50.1 17.3 %collective-permute-start.7 = (bf16[3,512,256]{2,1,0:T(8,128)(2,1)S(1)}, bf16[3,512,256]{2,1,0:T(8,128)(2,1)S(1)}, u32[]{:S(2)}, u32[]{:S(2)}) collective-permute-start(bf16[3,512,256]{2,1,0:T(8,128)(2,1)S(1)} %choose.7.refs_5_), channel_id=1, source_target_pairs={{0,2},{1,3},{2,0},{3,1},{4,6},{5,7},{6,4},{7,5},{8,10},{9,11},{10,... | collective-permute-start | bytes 2359304 | tf_op jit(solution)/shard_map/ppermute | solution.py:415
  51.7 15.7 %collective-permute-start.6 = (bf16[160,2048]{1,0:T(8,128)(2,1)S(1)}, bf16[160,2048]{1,0:T(8,128)(2,1)S(1)}, u32[]{:S(2)}, u32[]{:S(2)}) collective-permute-start(bf16[160,2048]{1,0:T(8,128)(2,1)S(1)} %get-tuple-element.101), channel_id=1, source_target_pairs={{0,4},{1,5},{2,6},{3,7},{4,0},{5,1},{6,2},{7,3},{8,12},{9,13},{10,... | collective-permute-start | bytes 1966088 | tf_op jit(solution)/shard_map/ppermute | solution.py:415
  67.4 20.3 %collective-permute-start.9 = (bf16[176,2048]{1,0:T(8,128)(2,1)S(1)}, bf16[176,2048]{1,0:T(8,128)(2,1)S(1)}, u32[]{:S(2)}, u32[]{:S(2)}) collective-permute-start(bf16[176,2048]{1,0:T(8,128)(2,1)S(1)} %get-tuple-element.105), channel_id=1, source_target_pairs={{0,4},{1,5},{2,6},{3,7},{4,0},{5,1},{6,2},{7,3},{8,12},{9,13},{10,... | collective-permute-start | bytes 2162696 | tf_op jit(solution)/shard_map/ppermute | solution.py:415
  70.8 16.9 %collective-permute-start.12 = (bf16[160,2048]{1,0:T(8,128)(2,1)S(1)}, bf16[160,2048]{1,0:T(8,128)(2,1)S(1)}, u32[]{:S(2)}, u32[]{:S(2)}) collective-permute-start(bf16[160,2048]{1,0:T(8,128)(2,1)S(1)} %collective-permute-done.6.refs_2_), channel_id=1, source_target_pairs={{0,1},{1,0},{2,3},{3,2},{4,5},{5,4},{6,7},{7,6},{8,9},{9,8},{10,11... | collective-permute-start | bytes 1966088 | tf_op jit(solution)/shard_map/ppermute | solution.py:415
  72.2 27.3 %collective-permute-start.23 = (bf16[3,512,256]{2,1,0:T(8,128)(2,1)S(1)}, bf16[3,512,256]{2,1,0:T(8,128)(2,1)S(1)}, u32[]{:S(2)}, u32[]{:S(2)}) collective-permute-start(bf16[3,512,256]{2,1,0:T(8,128)(2,1)S(1)} %get-tuple-element.126.refs_1_), channel_id=1, source_target_pairs={{0,2},{1,3},{2,0},{3,1},{4,6},{5,7},{6,4},{7,5},{8,10},{9,11},{10,... | collective-permute-start | bytes 2359304 | tf_op jit(solution)/shard_map/ppermute | solution.py:415
  73.7 27.1 %collective-permute-start.16 = (bf16[3,512,256]{2,1,0:T(8,128)(2,1)S(1)}, bf16[3,512,256]{2,1,0:T(8,128)(2,1)S(1)}, u32[]{:S(2)}, u32[]{:S(2)}) collective-permute-start(bf16[3,512,256]{2,1,0:T(8,128)(2,1)S(1)} %collective-permute-done.1.refs_3_), channel_id=1, source_target_pairs={{4,8},{5,9},{6,10},{7,11},{8,4},{9,5},{10,6},{11,7},{20,24},{21,25... | collective-permute-start | bytes 2359304 | tf_op jit(solution)/shard_map/ppermute | solution.py:415
  74.4 24.4 %collective-permute-start.21 = (bf16[1,256,1024]{2,1,0:T(8,128)(2,1)S(1)}, bf16[1,256,1024]{2,1,0:T(8,128)(2,1)S(1)}, u32[]{:S(2)}, u32[]{:S(2)}) collective-permute-start(bf16[1,256,1024]{2,1,0:T(8,128)(2,1)S(1)} %get-tuple-element.129), channel_id=1, source_target_pairs={{4,0},{5,1},{6,2},{7,3},{8,12},{9,13},{10,14},{11,15},{20,16},{21,... | collective-permute-start | bytes 1572872 | tf_op jit(solution)/shard_map/ppermute | solution.py:415
  87.7 14.6 %collective-permute-start.14 = (bf16[160,2048]{1,0:T(8,128)(2,1)S(1)}, bf16[160,2048]{1,0:T(8,128)(2,1)S(1)}, u32[]{:S(2)}, u32[]{:S(2)}) collective-permute-start(bf16[160,2048]{1,0:T(8,128)(2,1)S(1)} %collective-permute-done.12.refs_3_), channel_id=1, source_target_pairs={{0,16},{1,17},{2,18},{3,19},{4,20},{5,21},{6,22},{7,23},{8,24},{9,... | collective-permute-start | bytes 1966088 | tf_op jit(solution)/shard_map/ppermute | solution.py:415
  87.7 16.1 %collective-permute-start.13 = (bf16[160,2048]{1,0:T(8,128)(2,1)S(1)}, bf16[160,2048]{1,0:T(8,128)(2,1)S(1)}, u32[]{:S(2)}, u32[]{:S(2)}) collective-permute-start(bf16[160,2048]{1,0:T(8,128)(2,1)S(1)} %collective-permute-done.6.refs_2_), channel_id=1, source_target_pairs={{0,16},{1,17},{2,18},{3,19},{4,20},{5,21},{6,22},{7,23},{8,24},{9,... | collective-permute-start | bytes 1966088 | tf_op jit(solution)/shard_map/ppermute | solution.py:415
  98.8 15.8 %collective-permute-start.17 = (bf16[3,512,256]{2,1,0:T(8,128)(2,1)S(1)}, bf16[3,512,256]{2,1,0:T(8,128)(2,1)S(1)}, u32[]{:S(2)}, u32[]{:S(2)}) collective-permute-start(bf16[3,512,256]{2,1,0:T(8,128)(2,1)S(1)} %get-tuple-element.115), channel_id=1, source_target_pairs={{0,0},{1,1},{2,2},{3,3},{4,8},{5,9},{6,10},{7,11},{8,4},{9,5},{10,... | collective-permute-start | bytes 2359304 | tf_op jit(solution)/shard_map/ppermute | solution.py:415
  99.5 21.3 %collective-permute-start.22 = (bf16[3,512,256]{2,1,0:T(8,128)(2,1)S(1)}, bf16[3,512,256]{2,1,0:T(8,128)(2,1)S(1)}, u32[]{:S(2)}, u32[]{:S(2)}) collective-permute-start(bf16[3,512,256]{2,1,0:T(8,128)(2,1)S(1)} %collective-permute-done.8), channel_id=1, source_target_pairs={{4,0},{5,1},{6,2},{7,3},{8,12},{9,13},{10,14},{11,15},{20,16},{21,... | collective-permute-start | bytes 2359304 | tf_op jit(solution)/shard_map/ppermute | solution.py:415
  100.8 20.0 %collective-permute-start.15 = (bf16[176,2048]{1,0:T(8,128)(2,1)S(1)}, bf16[176,2048]{1,0:T(8,128)(2,1)S(1)}, u32[]{:S(2)}, u32[]{:S(2)}) collective-permute-start(bf16[176,2048]{1,0:T(8,128)(2,1)S(1)} %collective-permute-done.9.in_ref.refs_2_), channel_id=1, source_target_pairs={{0,1},{1,0},{2,3},{3,2},{4,5},{5,4},{6,7},{7,6},{8,9},{9,8},{10,11... | collective-permute-start | bytes 2162696 | tf_op jit(solution)/shard_map/ppermute | solution.py:415
  102.4 18.4 %collective-permute-start.24 = (bf16[1,256,1024]{2,1,0:T(8,128)(2,1)S(1)}, bf16[1,256,1024]{2,1,0:T(8,128)(2,1)S(1)}, u32[]{:S(2)}, u32[]{:S(2)}) collective-permute-start(bf16[1,256,1024]{2,1,0:T(8,128)(2,1)S(1)} %get-tuple-element.127.refs_4_.refs_6_), channel_id=1, source_target_pairs={{0,2},{1,3},{2,0},{3,1},{4,6},{5,7},{6,4},{7,5},{8,10},{9,11},{10,... | collective-permute-start | bytes 1572872 | tf_op jit(solution)/shard_map/ppermute | solution.py:415
  103.9 16.9 %collective-permute-start.26 = (bf16[1,256,1024]{2,1,0:T(8,128)(2,1)S(1)}, bf16[1,256,1024]{2,1,0:T(8,128)(2,1)S(1)}, u32[]{:S(2)}, u32[]{:S(2)}) collective-permute-start(bf16[1,256,1024]{2,1,0:T(8,128)(2,1)S(1)} %get-tuple-element.129), channel_id=1, source_target_pairs={{0,4},{1,5},{2,6},{3,7},{12,8},{13,9},{14,10},{15,11},{16,20},{17,... | collective-permute-start | bytes 1572872 | tf_op jit(solution)/shard_map/ppermute | solution.py:415
  114.6 18.5 %collective-permute-start.20 = (bf16[3,512,256]{2,1,0:T(8,128)(2,1)S(1)}, bf16[3,512,256]{2,1,0:T(8,128)(2,1)S(1)}, u32[]{:S(2)}, u32[]{:S(2)}) collective-permute-start(bf16[3,512,256]{2,1,0:T(8,128)(2,1)S(1)} %get-tuple-element.120), channel_id=1, source_target_pairs={{4,8},{5,9},{6,10},{7,11},{8,4},{9,5},{10,6},{11,7},{20,24},{21,25... | collective-permute-start | bytes 2359304 | tf_op jit(solution)/shard_map/ppermute | solution.py:415
  120.8 18.6 %collective-permute-start.27 = (bf16[3,512,256]{2,1,0:T(8,128)(2,1)S(1)}, bf16[3,512,256]{2,1,0:T(8,128)(2,1)S(1)}, u32[]{:S(2)}, u32[]{:S(2)}) collective-permute-start(bf16[3,512,256]{2,1,0:T(8,128)(2,1)S(1)} %collective-permute-done.17), channel_id=1, source_target_pairs={{0,4},{1,5},{2,6},{3,7},{4,0},{5,1},{6,2},{7,3},{8,12},{9,13},{10,... | collective-permute-start | bytes 2359304 | tf_op jit(solution)/shard_map/ppermute | solution.py:415
  122.8 18.0 %collective-permute-start.25 = (bf16[3,512,256]{2,1,0:T(8,128)(2,1)S(1)}, bf16[3,512,256]{2,1,0:T(8,128)(2,1)S(1)}, u32[]{:S(2)}, u32[]{:S(2)}) collective-permute-start(bf16[3,512,256]{2,1,0:T(8,128)(2,1)S(1)} %choose.8.refs_1_), channel_id=1, source_target_pairs={{0,2},{1,3},{2,0},{3,1},{4,6},{5,7},{6,4},{7,5},{8,10},{9,11},{10,... | collective-permute-start | bytes 2359304 | tf_op jit(solution)/shard_map/ppermute | solution.py:415
  139.4 10.2 %collective-permute-start.28 = (bf16[3,512,256]{2,1,0:T(8,128)(2,1)S(1)}, bf16[3,512,256]{2,1,0:T(8,128)(2,1)S(1)}, u32[]{:S(2)}, u32[]{:S(2)}) collective-permute-start(bf16[3,512,256]{2,1,0:T(8,128)(2,1)S(1)} %collective-permute-done.27.a_ref), channel_id=1, source_target_pairs={{4,8},{5,9},{6,10},{7,11},{8,4},{9,5},{10,6},{11,7},{20,24},{21,25... | collective-permute-start | bytes 2359304 | tf_op jit(solution)/shard_map/ppermute | solution.py:415
  140.8 18.4 %collective-permute-start.30 = (bf16[3,512,256]{2,1,0:T(8,128)(2,1)S(1)}, bf16[3,512,256]{2,1,0:T(8,128)(2,1)S(1)}, u32[]{:S(2)}, u32[]{:S(2)}) collective-permute-start(bf16[3,512,256]{2,1,0:T(8,128)(2,1)S(1)} %get-tuple-element.134), channel_id=1, source_target_pairs={{0,4},{1,5},{2,6},{3,7},{4,0},{5,1},{6,2},{7,3},{8,12},{9,13},{10,... | collective-permute-start | bytes 2359304 | tf_op jit(solution)/shard_map/ppermute | solution.py:415
  144.5 16.8 %collective-permute-start.32 = (bf16[3,512,256]{2,1,0:T(8,128)(2,1)S(1)}, bf16[3,512,256]{2,1,0:T(8,128)(2,1)S(1)}, u32[]{:S(2)}, u32[]{:S(2)}) collective-permute-start(bf16[3,512,256]{2,1,0:T(8,128)(2,1)S(1)} %choose.9.refs_3_), channel_id=1, source_target_pairs={{0,2},{1,3},{2,0},{3,1},{4,6},{5,7},{6,4},{7,5},{8,10},{9,11},{10,... | collective-permute-start | bytes 2359304 | tf_op jit(solution)/shard_map/ppermute | solution.py:415
  147.7 26.7 %collective-permute-start.29 = (bf16[640,768]{1,0:T(8,128)(2,1)S(1)}, bf16[640,768]{1,0:T(8,128)(2,1)S(1)}, u32[]{:S(2)}, u32[]{:S(2)}) collective-permute-start(bf16[640,768]{1,0:T(8,128)(2,1)S(1)} %project.13), channel_id=1, source_target_pairs={{0,16},{1,17},{2,18},{3,19},{4,20},{5,21},{6,22},{7,23},{8,24},{9,... | collective-permute-start | bytes 2949128 | tf_op jit(solution)/shard_map/ppermute | solution.py:415
  159.1 19.4 %collective-permute-start.31 = (bf16[3,512,256]{2,1,0:T(8,128)(2,1)S(1)}, bf16[3,512,256]{2,1,0:T(8,128)(2,1)S(1)}, u32[]{:S(2)}, u32[]{:S(2)}) collective-permute-start(bf16[3,512,256]{2,1,0:T(8,128)(2,1)S(1)} %collective-permute-done.30.refs_1_), channel_id=1, source_target_pairs={{4,8},{5,9},{6,10},{7,11},{8,4},{9,5},{10,6},{11,7},{20,24},{21,25... | collective-permute-start | bytes 2359304 | tf_op jit(solution)/shard_map/ppermute | solution.py:415
  161.3 18.0 %collective-permute-start.36 = (bf16[3,512,256]{2,1,0:T(8,128)(2,1)S(1)}, bf16[3,512,256]{2,1,0:T(8,128)(2,1)S(1)}, u32[]{:S(2)}, u32[]{:S(2)}) collective-permute-start(bf16[3,512,256]{2,1,0:T(8,128)(2,1)S(1)} %collective-permute-done.28), channel_id=1, source_target_pairs={{4,0},{5,1},{6,2},{7,3},{8,12},{9,13},{10,14},{11,15},{20,16},{21,... | collective-permute-start | bytes 2359304 | tf_op jit(solution)/shard_map/ppermute | solution.py:415
  162.6 16.0 %collective-permute-start.33 = (bf16[1,256,1024]{2,1,0:T(8,128)(2,1)S(1)}, bf16[1,256,1024]{2,1,0:T(8,128)(2,1)S(1)}, u32[]{:S(2)}, u32[]{:S(2)}) collective-permute-start(bf16[1,256,1024]{2,1,0:T(8,128)(2,1)S(1)} %get-tuple-element.140), channel_id=1, source_target_pairs={{0,4},{1,5},{2,6},{3,7},{12,8},{13,9},{14,10},{15,11},{16,20},{17,... | collective-permute-start | bytes 1572872 | tf_op jit(solution)/shard_map/ppermute | solution.py:415
  167.4 17.8 %collective-permute-start.35 = (bf16[3,512,256]{2,1,0:T(8,128)(2,1)S(1)}, bf16[3,512,256]{2,1,0:T(8,128)(2,1)S(1)}, u32[]{:S(2)}, u32[]{:S(2)}) collective-permute-start(bf16[3,512,256]{2,1,0:T(8,128)(2,1)S(1)} %collective-permute-done.30.refs_1_), channel_id=1, source_target_pairs={{0,2},{1,3},{2,0},{3,1},{4,6},{5,7},{6,4},{7,5},{8,10},{9,11},{10,... | collective-permute-start | bytes 2359304 | tf_op jit(solution)/shard_map/ppermute | solution.py:415
  178.6 15.1 %collective-permute-start.34 = (bf16[1,256,2048]{2,1,0:T(8,128)(2,1)S(1)}, bf16[1,256,2048]{2,1,0:T(8,128)(2,1)S(1)}, u32[]{:S(2)}, u32[]{:S(2)}) collective-permute-start(bf16[1,256,2048]{2,1,0:T(8,128)(2,1)S(1)} %copy-done.4), channel_id=1, source_target_pairs={{4,8},{5,9},{6,10},{7,11},{8,4},{9,5},{10,6},{11,7},{20,24},{21,25... | collective-permute-start | bytes 3145736 | tf_op jit(solution)/shard_map/ppermute | solution.py:415
  185.2 14.4 %collective-permute-start.41 = (bf16[3,512,256]{2,1,0:T(8,128)(2,1)S(1)}, bf16[3,512,256]{2,1,0:T(8,128)(2,1)S(1)}, u32[]{:S(2)}, u32[]{:S(2)}) collective-permute-start(bf16[3,512,256]{2,1,0:T(8,128)(2,1)S(1)} %choose.11.refs_1_), channel_id=1, source_target_pairs={{0,2},{1,3},{2,0},{3,1},{4,6},{5,7},{6,4},{7,5},{8,10},{9,11},{10,... | collective-permute-start | bytes 2359304 | tf_op jit(solution)/shard_map/ppermute | solution.py:415
  201.4 14.3 %collective-permute-start.42 = (bf16[1,256,1024]{2,1,0:T(8,128)(2,1)S(1)}, bf16[1,256,1024]{2,1,0:T(8,128)(2,1)S(1)}, u32[]{:S(2)}, u32[]{:S(2)}) collective-permute-start(bf16[1,256,1024]{2,1,0:T(8,128)(2,1)S(1)} %choose.10.refs_6_.refs_8_), channel_id=1, source_target_pairs={{0,2},{1,3},{2,0},{3,1},{4,6},{5,7},{6,4},{7,5},{8,10},{9,11},{10,... | collective-permute-start | bytes 1572872 | tf_op jit(solution)/shard_map/ppermute | solution.py:415
  203.5 15.9 %collective-permute-start.40 = (bf16[1,256,1024]{2,1,0:T(8,128)(2,1)S(1)}, bf16[1,256,1024]{2,1,0:T(8,128)(2,1)S(1)}, u32[]{:S(2)}, u32[]{:S(2)}) collective-permute-start(bf16[1,256,1024]{2,1,0:T(8,128)(2,1)S(1)} %get-tuple-element.149), channel_id=1, source_target_pairs={{4,0},{5,1},{6,2},{7,3},{8,12},{9,13},{10,14},{11,15},{20,16},{21,... | collective-permute-start | bytes 1572872 | tf_op jit(solution)/shard_map/ppermute | solution.py:415
  204.8 14.6 %collective-permute-start.39 = (bf16[1,256,1024]{2,1,0:T(8,128)(2,1)S(1)}, bf16[1,256,1024]{2,1,0:T(8,128)(2,1)S(1)}, u32[]{:S(2)}, u32[]{:S(2)}) collective-permute-start(bf16[1,256,1024]{2,1,0:T(8,128)(2,1)S(1)} %collective-permute-done.26), channel_id=1, source_target_pairs={{4,8},{5,9},{6,10},{7,11},{8,4},{9,5},{10,6},{11,7},{20,24},{21,25... | collective-permute-start | bytes 1572872 | tf_op jit(solution)/shard_map/ppermute | solution.py:415
  220.0 14.3 %collective-permute-start.45 = (bf16[4,640,256]{2,1,0:T(8,128)(2,1)S(1)}, bf16[4,640,256]{2,1,0:T(8,128)(2,1)S(1)}, u32[]{:S(2)}, u32[]{:S(2)}) collective-permute-start(bf16[4,640,256]{2,1,0:T(8,128)(2,1)S(1)} %stack.18.refs_0_.refs_2_), channel_id=1, source_target_pairs={{0,16},{1,17},{2,18},{3,19},{4,20},{5,21},{6,22},{7,23},{8,24},{9,... | collective-permute-start | bytes 3932168 | tf_op jit(solution)/shard_map/ppermute | solution.py:415
  220.1 10.1 %collective-permute-start.47 = (bf16[640,256]{1,0:T(8,128)(2,1)S(1)}, bf16[640,256]{1,0:T(8,128)(2,1)S(1)}, u32[]{:S(2)}, u32[]{:S(2)}) collective-permute-start(bf16[640,256]{1,0:T(8,128)(2,1)S(1)} %attend.3.refs_0_), channel_id=1, source_target_pairs={{0,1},{1,0},{2,3},{3,2},{4,5},{5,4},{6,7},{7,6},{8,9},{9,8},{10,11... | collective-permute-start | bytes 983048 | tf_op jit(solution)/shard_map/ppermute | solution.py:415
  221.7 12.2 %collective-permute-start.50 = (bf16[640,256]{1,0:T(8,128)(2,1)S(1)}, bf16[640,256]{1,0:T(8,128)(2,1)S(1)}, u32[]{:S(2)}, u32[]{:S(2)}) collective-permute-start(bf16[640,256]{1,0:T(8,128)(2,1)S(1)} %attend.3.refs_0_), channel_id=1, source_target_pairs={{0,4},{1,5},{2,6},{3,7},{4,0},{5,1},{6,2},{7,3},{8,12},{9,13},{10,... | collective-permute-start | bytes 983048 | tf_op jit(solution)/shard_map/ppermute | solution.py:415
  226.0 13.8 %collective-permute-start.49 = (bf16[1,256,1024]{2,1,0:T(8,128)(2,1)S(1)}, bf16[1,256,1024]{2,1,0:T(8,128)(2,1)S(1)}, u32[]{:S(2)}, u32[]{:S(2)}) collective-permute-start(bf16[1,256,1024]{2,1,0:T(8,128)(2,1)S(1)} %choose.12.refs_10_.refs_6_), channel_id=1, source_target_pairs={{0,2},{1,3},{2,0},{3,1},{4,6},{5,7},{6,4},{7,5},{8,10},{9,11},{10,... | collective-permute-start | bytes 1572872 | tf_op jit(solution)/shard_map/ppermute | solution.py:415
  226.6 18.1 %collective-permute-start.46 = (bf16[1,256,1024]{2,1,0:T(8,128)(2,1)S(1)}, bf16[1,256,1024]{2,1,0:T(8,128)(2,1)S(1)}, u32[]{:S(2)}, u32[]{:S(2)}) collective-permute-start(bf16[1,256,1024]{2,1,0:T(8,128)(2,1)S(1)} %collective-permute-done.39), channel_id=1, source_target_pairs={{4,0},{5,1},{6,2},{7,3},{8,12},{9,13},{10,14},{11,15},{20,16},{21,... | collective-permute-start | bytes 1572872 | tf_op jit(solution)/shard_map/ppermute | solution.py:415
  230.3 14.4 %collective-permute-start.48 = (bf16[1,256,1024]{2,1,0:T(8,128)(2,1)S(1)}, bf16[1,256,1024]{2,1,0:T(8,128)(2,1)S(1)}, u32[]{:S(2)}, u32[]{:S(2)}) collective-permute-start(bf16[1,256,1024]{2,1,0:T(8,128)(2,1)S(1)} %collective-permute-done.33.b_ref), channel_id=1, source_target_pairs={{4,8},{5,9},{6,10},{7,11},{8,4},{9,5},{10,6},{11,7},{20,24},{21,25... | collective-permute-start | bytes 1572872 | tf_op jit(solution)/shard_map/ppermute | solution.py:415
  233.9 11.4 %collective-permute-start.51 = (bf16[640,256]{1,0:T(8,128)(2,1)S(1)}, bf16[640,256]{1,0:T(8,128)(2,1)S(1)}, u32[]{:S(2)}, u32[]{:S(2)}) collective-permute-start(bf16[640,256]{1,0:T(8,128)(2,1)S(1)} %collective-permute-done.50.refs_2_), channel_id=1, source_target_pairs={{0,1},{1,0},{2,3},{3,2},{4,5},{5,4},{6,7},{7,6},{8,9},{9,8},{10,11... | collective-permute-start | bytes 983048 | tf_op jit(solution)/shard_map/ppermute | solution.py:415
  246.0 14.3 %collective-permute-start.53 = (bf16[1,256,1024]{2,1,0:T(8,128)(2,1)S(1)}, bf16[1,256,1024]{2,1,0:T(8,128)(2,1)S(1)}, u32[]{:S(2)}, u32[]{:S(2)}) collective-permute-start(bf16[1,256,1024]{2,1,0:T(8,128)(2,1)S(1)} %choose.13.refs_8_.refs_10_), channel_id=1, source_target_pairs={{0,2},{1,3},{2,0},{3,1},{4,6},{5,7},{6,4},{7,5},{8,10},{9,11},{10,... | collective-permute-start | bytes 1572872 | tf_op jit(solution)/shard_map/ppermute | solution.py:415
  263.9 21.1 %collective-permute-start.54 = (bf16[640,1024]{1,0:T(8,128)(2,1)S(1)}, bf16[640,1024]{1,0:T(8,128)(2,1)S(1)}, u32[]{:S(2)}, u32[]{:S(2)}) collective-permute-start(bf16[640,1024]{1,0:T(8,128)(2,1)S(1)} %combine.6.a_ref), channel_id=1, source_target_pairs={{0,16},{1,17},{2,18},{3,19},{4,20},{5,21},{6,22},{7,23},{8,24},{9,... | collective-permute-start | bytes 3932168 | tf_op jit(solution)/shard_map/ppermute | solution.py:415
  265.4 19.7 %collective-permute-start.56 = (bf16[320,1024]{1,0:T(8,128)(2,1)S(1)}, bf16[320,1024]{1,0:T(8,128)(2,1)S(1)}, u32[]{:S(2)}, u32[]{:S(2)}) collective-permute-start(bf16[320,1024]{1,0:T(8,128)(2,1)S(1)} %join.1), channel_id=1, source_target_pairs={{0,4},{1,5},{2,6},{3,7},{4,0},{5,1},{6,2},{7,3},{8,12},{9,13},{10,... | collective-permute-start | bytes 1966088 | tf_op jit(solution)/shard_map/ppermute | solution.py:415
  (16 other events, 172.9 us)

commit v13 on v10

--- a/solution.py
+++ b/solution.py
@@ -259,13 +259,13 @@
 def combine(here, slots, groups, total=None, final=False, offset=0, cut=False):
     held_pieces, length, held = groups[0][0].shape
     shards = held_pieces // 2
-    features = groups[0][3][0][1].shape[2]
+    features = groups[0][3][0][1].shape[-1]
     tile = min(features, 256)
     half = length // 2
     terms = [group[:3] + (pair,) for group in groups for pair in group[3]]
     count = len(terms)
     args = [pieces for term in terms for pieces in term[:2]]
-    args += [b for term in terms for b in term[3][1:]] + ([] if total is None else [total])
+    args += [b for term in terms for b in term[3][1:3]] + ([] if total is None else [total])
 
     def kernel(h_ref, *refs):
         at_place = Here(h_ref)
@@ -280,14 +280,14 @@
                 jnp.where(
                     first_slot, refs[2 * i][found[arrival]], refs[2 * i + 1][found[arrival]]
                 )
-                for i, (_, _, _, (arrival, _, _)) in enumerate(terms)
+                for i, (_, _, _, (arrival, *_)) in enumerate(terms)
             ]
             for n in range(features // tile):
                 columns = slice(n * tile, (n + 1) * tile)
                 summed = None if total is None else refs[4 * count][offset + s, :, columns]
-                for i, (_, _, parity, _) in enumerate(terms):
-                    near = refs[2 * count + 2 * i][0, :, columns]
-                    far = refs[2 * count + 2 * i + 1][0, :, columns]
+                for i, (_, _, parity, (_, _, _, *index)) in enumerate(terms):
+                    near = refs[2 * count + 2 * i][(*index, 0, slice(None), columns)]
+                    far = refs[2 * count + 2 * i + 1][(*index, 0, slice(None), columns)]
                     block = jnp.where(at_place.y == parity, near, far)
                     part = jnp.dot(rows[i], block, preferred_element_type=F32)
                     summed = part if summed is None else summed + part
@@ -542,54 +542,49 @@
         late_normed = after(normed, *begun)
         total_b = project(here, "own", late_normed, first_b, fresh=True)
         total_b = project(here, "partner", late_normed, first_b, total_b, fresh=True)
-
-        begun = (m4b, attended_a, total_b)
-        m1o = move(low_o, across, *begun)
-        m2o = move(high_o, across, *begun)
+        lows = stack(here, [after(low_o, *begun), i1o])
+
+        begun = (m4b, attended_a, total_b, lows)
+        m13o = move(lows, across, i2o, *begun)
         fourth_b = choose(here, after(e3b, *begun), m4b)
         p4b = move(fourth_b, pair, p2b)
-        packed_a = move(pack(here, after(low_o, *begun), attended_a), edge, e3b, i2o, p2b)
+        packed_a = move(pack(here, after(low_o, *begun), attended_a), edge, e3b, p2b)
         held_a = over_tensor(after(attended_a, *begun))
+        highs = stack(here, [after(high_o, *begun), i2o])
         second_b = [(1, e1b, p2b)]
         late_normed = after(normed, *begun)
         total_b = project(here, "own", late_normed, second_b, total_b)
         total_b = project(here, "partner", late_normed, second_b, total_b)
 
+        begun = (m13o, total_b, packed_a, held_a[1], highs)
+        m24o = move(highs, across, *begun)
+        o23o = move(m13o, outward, *begun)
         last_b = [(3, fourth_b, p4b)]
-        theirs_b = project(here, 1, normed, last_b, total_b, final=True)
+        late_normed = after(normed, *begun)
+        theirs_b = project(here, 1, late_normed, last_b, total_b, final=True)
         got_b = to_core(theirs_b)
-        ours_b = project(here, 0, normed, last_b, total_b, final=True)
-        o1o, passed_a = unpack(here, after(packed_a, theirs_b), low_o, attended_a)
+        ours_b = project(here, 0, late_normed, last_b, total_b, final=True)
+        o1o, passed_a = unpack(here, after(packed_a, ours_b), low_o, attended_a)
         second_o = choose(here, o1o, i2o)
         p2o = move(second_o, pair, p4b)
         held_a += over_tensor(passed_a)
-
-        begun = (m1o, m2o, ours_b, second_o)
-        m3o = move(i1o, across, held_a[1], *begun)
-        o2o = move(m1o, outward, *begun)
-        attended_b = attend(here, own_kind, other_kind, after(ours_b, *begun), got_b)
-
-        passed_b = move(attended_b, edge, o2o, p2o, held_a[-1])
-        begun = (m3o, passed_b)
-        m4o = move(i2o, across, *begun)
-        o3o = move(m3o, outward, *begun)
-        held_b = over_tensor(after(attended_b, *begun)) + over_tensor(after(passed_b, *begun))
-        third_o = choose(here, after(o2o, *begun), m2o)
-        p3o = move(third_o, pair, p2o)
-        pieces_a = stack(here, [after(held_a[0], *begun)] + held_a[1:])
+        attended_b = attend(here, own_kind, other_kind, ours_b, got_b)
+        held_b = over_tensor(attended_b)
+
+        begun = (m24o, o23o, held_b[1], held_a[-1], p2o)
+        late_o = choose(here, after(o23o, *begun), m24o)
+        p34o = move(late_o, pair)
+        passed_b = move(attended_b, edge, o23o)
+        held_b += over_tensor(after(passed_b, late_o))
+        pieces_a = stack(here, [after(held_a[0], late_o)] + held_a[1:])
         pieces_a = (pieces_a, to_core(pieces_a))
         both = ("partner", "own")
-        blocks = [(0, mine_o, p1o), (1, second_o, p2o), (2, third_o, p3o)]
-        total = combine(here, both, [pieces_a + (0, blocks[:2])])
-
-        begun = (o3o, m4o, p3o, total)
-        fourth_o = choose(here, after(o3o, *begun), m4o)
-        p4o = move(fourth_o, pair)
-        pieces_b = stack(here, [after(held_b[0], fourth_o)] + held_b[1:])
+        near = [(0, mine_o, p1o), (1, second_o, p2o)]
+        last = [(2, late_o, p34o, 0), (3, late_o, p34o, 1)]
+        total = combine(here, both, [pieces_a + (0, near)])
+        pieces_b = stack(here, [after(held_b[0], total, p34o)] + held_b[1:])
         pieces_b = (pieces_b, to_core(pieces_b))
-        total = combine(here, both, [pieces_b + (1, blocks)], total)
-        last = [(3, fourth_o, p4o)]
-        rest = [pieces_a + (0, blocks[2:] + last), pieces_b + (1, last)]
+        rest = [pieces_a + (0, last), pieces_b + (1, near + last)]
 
         kept_away, sent_away = combine(here, ("partner",), rest, total, True, 0, True)
         sent_away = to_core(sent_away)

time: 283 us -> 284 us (level)
    ppermute x58 -> x54, waiting for transfers between devices: 142 us -> 143 us  [move(): lax.ppermute(after(array, *earlier) if earlier else array, AXES, pairs)]
    ppermute x58 -> x54, starting transfers between devices: 73 us -> 73.3 us  [move(): lax.ppermute(after(array, *earlier) if earlier else array, AXES, pairs)]
  transfers between devices with their start and end apart: 58 -> 54, of which waited for: 29 -> 27; matrix products, arithmetic and copies ran while one was open for 0% -> 0% of each run, Pallas kernels for 20% -> 18%
where the time goes in v13:
time: 284 us; the launch traced here: 283 us
  waiting for transfers between devices  143 us (50%)
  starting transfers between devices  73.3 us (26%)
  Pallas kernels  61.5 us (22%)
  local copies, waits for them, and re-layouts  4.34 us (2%)
    ppermute x54, waiting for transfers between devices, move(): lax.ppermute(after(array, *earlier) if earlier else array, AXES, pairs)  143 us
    ppermute x54, starting transfers between devices, move(): lax.ppermute(after(array, *earlier) if earlier else array, AXES, pairs)  73.3 us
    pallas_call x36, Pallas kernels, call(): pl.pallas_call(kernel, in_specs=[pl.BlockSpec(memory_space=SMEM)] + [pl.B...  59.1 us
  transfers between devices with their start and end apart: 54, of which 27 were waited for; matrix products, arithmetic and copies ran while one was open for 0% of the time, Pallas kernels for 18%

profile of v13, /device:TPU:0, one launch (start us, length us, event | category | flops | bytes accessed | tf_op | source)
XLA Modules:
  0.0 283.0 jit_solution(7326613009176935347)
XLA Ops:
  0.8 1.9 copy-done
  3.5 3.0 %collective-permute-start.2 = (bf16[3,512,256]{2,1,0:T(8,128)(2,1)S(1)}, bf16[3,512,256]{2,1,0:T(8,128)(2,1)S(1)}, u32[]{:S(2)}, u32[]{:S(2)}) collective-permute-start(bf16[3,512,256]{2,1,0:T(8,128)(2,1)S(1)} %get-tuple-element.89.refs_1_), channel_id=1, source_target_pairs={{0,2},{1,3},{2,0},{3,1},{4,6},{5,7},{6,4},{7,5},{8,10},{9,11},{10,... | collective-permute-start | bytes 2359304 | tf_op jit(solution)/shard_map/ppermute | solution.py:430
  8.8 15.3 %collective-permute-done.2.refs_2_ = bf16[3,512,256]{2,1,0:T(8,128)(2,1)S(1)} collective-permute-done((bf16[3,512,256]{2,1,0:T(8,128)(2,1)S(1)}, bf16[3,512,256]{2,1,0:T(8,128)(2,1)S(1)}, u32[]{:S(2)}, u32[]{:S(2)}) %collective-permute-start.2) | collective-permute-done | bytes 786464 | tf_op jit(solution)/shard_map/ppermute | solution.py:430
  26.6 7.7 %collective-permute-start.3 = (bf16[3,512,256]{2,1,0:T(8,128)(2,1)S(1)}, bf16[3,512,256]{2,1,0:T(8,128)(2,1)S(1)}, u32[]{:S(2)}, u32[]{:S(2)}) collective-permute-start(bf16[3,512,256]{2,1,0:T(8,128)(2,1)S(1)} %collective-permute-done), channel_id=1, source_target_pairs={{0,4},{1,5},{2,6},{3,7},{4,0},{5,1},{6,2},{7,3},{8,12},{9,13},{10,... | collective-permute-start | bytes 2359304 | tf_op jit(solution)/shard_map/ppermute | solution.py:430
  34.3 1.7 copy-done.2
  39.2 5.2 %collective-permute-done.4.refs_4_ = bf16[3,512,256]{2,1,0:T(8,128)(2,1)S(1)} collective-permute-done((bf16[3,512,256]{2,1,0:T(8,128)(2,1)S(1)}, bf16[3,512,256]{2,1,0:T(8,128)(2,1)S(1)}, u32[]{:S(2)}, u32[]{:S(2)}) %collective-permute-start.4) | collective-permute-done | bytes 786464 | tf_op jit(solution)/shard_map/ppermute | solution.py:430
  44.4 5.4 %collective-permute-done.3.a_ref = bf16[3,512,256]{2,1,0:T(8,128)(2,1)S(1)} collective-permute-done((bf16[3,512,256]{2,1,0:T(8,128)(2,1)S(1)}, bf16[3,512,256]{2,1,0:T(8,128)(2,1)S(1)}, u32[]{:S(2)}, u32[]{:S(2)}) %collective-permute-start.3) | collective-permute-done | bytes 786464 | tf_op jit(solution)/shard_map/ppermute | solution.py:430
  52.7 3.5 %collective-permute-start.6 = (bf16[160,2048]{1,0:T(8,128)(2,1)S(1)}, bf16[160,2048]{1,0:T(8,128)(2,1)S(1)}, u32[]{:S(2)}, u32[]{:S(2)}) collective-permute-start(bf16[160,2048]{1,0:T(8,128)(2,1)S(1)} %get-tuple-element.96), channel_id=1, source_target_pairs={{0,4},{1,5},{2,6},{3,7},{4,0},{5,1},{6,2},{7,3},{8,12},{9,13},{10,... | collective-permute-start | bytes 1966088 | tf_op jit(solution)/shard_map/ppermute | solution.py:430
  56.2 8.8 %collective-permute-done.10.refs_2_ = bf16[320,2048]{1,0:T(8,128)(2,1)S(1)} collective-permute-done((bf16[320,2048]{1,0:T(8,128)(2,1)S(1)}, bf16[320,2048]{1,0:T(8,128)(2,1)S(1)}, u32[]{:S(2)}, u32[]{:S(2)}) %collective-permute-start.10) | collective-permute-done | bytes 1310752 | tf_op jit(solution)/shard_map/ppermute | solution.py:430
  65.1 2.7 collective-permute-done.6.refs_2_
  67.8 3.3 %collective-permute-start.9 = (bf16[176,2048]{1,0:T(8,128)(2,1)S(1)}, bf16[176,2048]{1,0:T(8,128)(2,1)S(1)}, u32[]{:S(2)}, u32[]{:S(2)}) collective-permute-start(bf16[176,2048]{1,0:T(8,128)(2,1)S(1)} %get-tuple-element.100), channel_id=1, source_target_pairs={{0,4},{1,5},{2,6},{3,7},{4,0},{5,1},{6,2},{7,3},{8,12},{9,13},{10,... | collective-permute-start | bytes 2162696 | tf_op jit(solution)/shard_map/ppermute | solution.py:430
  76.3 3.2 %normalize.3.refs_0_ = bf16[2,8,640,512]{3,2,1,0:T(8,128)(2,1)S(1)} custom-call(s32[3]{0:T(128)S(1)} %pad_add_fusion.h_ref._, f32[8,1,512]{2,1,0:T(1,128)S(1)} %bitcast.9, bf16[640,2048]{1,0:T(8,128)(2,1)S(1)} %copy-done.3, bf16[320,2048]{1,0:T(8,128)(2,1)S(1)} %collective-permute-done.10.refs_2_, bf16[320,2048]{1,0:T(8,128)(2,1)S(1)} %collective-permute-done.11.refs_3_), custom_call_target="tpu_custom_call" | custom-call | tf_op jit(solution)/shard_map/normalize/pallas_call | solution.py:32
  79.5 7.2 %collective-permute-done.12.refs_3_ = bf16[160,2048]{1,0:T(8,128)(2,1)S(1)} collective-permute-done((bf16[160,2048]{1,0:T(8,128)(2,1)S(1)}, bf16[160,2048]{1,0:T(8,128)(2,1)S(1)}, u32[]{:S(2)}, u32[]{:S(2)}) %collective-permute-start.12) | collective-permute-done | bytes 655392 | tf_op jit(solution)/shard_map/ppermute | solution.py:430
  87.9 2.8 collective-permute-done.22.refs_2_
  94.1 4.6 %collective-permute-start.25 = (bf16[1,256,1024]{2,1,0:T(8,128)(2,1)S(1)}, bf16[1,256,1024]{2,1,0:T(8,128)(2,1)S(1)}, u32[]{:S(2)}, u32[]{:S(2)}) collective-permute-start(bf16[1,256,1024]{2,1,0:T(8,128)(2,1)S(1)} %get-tuple-element.141.refs_0_.block_ref), channel_id=1, source_target_pairs={{0,4},{1,5},{2,6},{3,7},{12,8},{13,9},{14,10},{15,11},{16,20},{17,... | collective-permute-start | bytes 1572872 | tf_op jit(solution)/shard_map/ppermute | solution.py:430
  99.2 3.7 %project.10.refs_7_ = f32[2,640,768]{2,1,0:T(8,128)S(1)} custom-call(s32[3]{0:T(128)S(1)} %pad_add_fusion.h_ref._, bf16[2,8,640,512]{3,2,1,0:T(8,128)(2,1)S(1)} %normalize.3.refs_0_, bf16[3,512,256]{2,1,0:T(8,128)(2,1)S(1)} %get-tuple-element.89.refs_1_, bf16[3,512,256]{2,1,0:T(8,128)(2,1)S(1)} %collective-permute-done.2.refs_2_, ...), custom_call_target="tpu_custom_call" | custom-call | tf_op jit(solution)/shard_map/project/pallas_call | solution.py:32
  103.0 1.8 normalize.4.refs_0_
  105.5 4.8 %collective-permute-done.21.a_ref = bf16[3,512,256]{2,1,0:T(8,128)(2,1)S(1)} collective-permute-done((bf16[3,512,256]{2,1,0:T(8,128)(2,1)S(1)}, bf16[3,512,256]{2,1,0:T(8,128)(2,1)S(1)}, u32[]{:S(2)}, u32[]{:S(2)}) %collective-permute-start.21) | collective-permute-done | bytes 786464 | tf_op jit(solution)/shard_map/ppermute | solution.py:430
  110.4 3.5 %collective-permute-start.26 = (bf16[3,512,256]{2,1,0:T(8,128)(2,1)S(1)}, bf16[3,512,256]{2,1,0:T(8,128)(2,1)S(1)}, u32[]{:S(2)}, u32[]{:S(2)}) collective-permute-start(bf16[3,512,256]{2,1,0:T(8,128)(2,1)S(1)} %collective-permute-done.17), channel_id=1, source_target_pairs={{0,4},{1,5},{2,6},{3,7},{4,0},{5,1},{6,2},{7,3},{8,12},{9,13},{10,... | collective-permute-start | bytes 2359304 | tf_op jit(solution)/shard_map/ppermute | solution.py:430
  118.5 1.8 normalize.5.refs_0_
  120.3 3.7 %project.11.refs_3_ = f32[2,640,768]{2,1,0:T(8,128)S(1)} custom-call(s32[3]{0:T(128)S(1)} %pad_add_fusion.h_ref._, bf16[2,8,640,512]{3,2,1,0:T(8,128)(2,1)S(1)} %normalize.5.refs_0_, bf16[3,512,256]{2,1,0:T(8,128)(2,1)S(1)} %get-tuple-element.89.refs_1_, bf16[3,512,256]{2,1,0:T(8,128)(2,1)S(1)} %collective-permute-done.2.refs_2_, ...), custom_call_target="tpu_custom_call", output_to_operand_aliasing={{}: (8, {})} | custom-call | tf_op jit(solution)/shard_map/project/pallas_call | solution.py:32
  124.0 6.7 %collective-permute-done.26.a_ref = bf16[3,512,256]{2,1,0:T(8,128)(2,1)S(1)} collective-permute-done((bf16[3,512,256]{2,1,0:T(8,128)(2,1)S(1)}, bf16[3,512,256]{2,1,0:T(8,128)(2,1)S(1)}, u32[]{:S(2)}, u32[]{:S(2)}) %collective-permute-start.26) | collective-permute-done | bytes 786464 | tf_op jit(solution)/shard_map/ppermute | solution.py:430
  130.7 2.1 collective-permute-done.24.refs_2_
  135.0 1.7 project.13
  138.5 11.7 %collective-permute-done.29.refs_1_ = bf16[3,512,256]{2,1,0:T(8,128)(2,1)S(1)} collective-permute-done((bf16[3,512,256]{2,1,0:T(8,128)(2,1)S(1)}, bf16[3,512,256]{2,1,0:T(8,128)(2,1)S(1)}, u32[]{:S(2)}, u32[]{:S(2)}) %collective-permute-start.29) | collective-permute-done | bytes 786464 | tf_op jit(solution)/shard_map/ppermute | solution.py:430
  153.5 7.1 %collective-permute-start.32 = (bf16[1,256,1024]{2,1,0:T(8,128)(2,1)S(1)}, bf16[1,256,1024]{2,1,0:T(8,128)(2,1)S(1)}, u32[]{:S(2)}, u32[]{:S(2)}) collective-permute-start(bf16[1,256,1024]{2,1,0:T(8,128)(2,1)S(1)} %get-tuple-element.144.refs_0_), channel_id=1, source_target_pairs={{0,4},{1,5},{2,6},{3,7},{12,8},{13,9},{14,10},{15,11},{16,20},{17,... | collective-permute-start | bytes 1572872 | tf_op jit(solution)/shard_map/ppermute | solution.py:430
  161.2 2.7 project.14.refs_5_
  164.0 2.7 project.15.refs_3_
  166.7 4.2 %attend.2.piece_ref.refs_0_ = bf16[640,256]{1,0:T(8,128)(2,1)S(1)} custom-call(s32[3]{0:T(128)S(1)} %pad_add_fusion.h_ref._, s32[1,640]{1,0:T(1,128)S(1)} %broadcast_in_dim.3.kind_ref.own_kind_ref, s32[1,640]{1,0:T(1,128)S(1)} %kinds_behind.1.other_kind_ref.kind_ref, bf16[640,768]{1,0:T(8,128)(2,1)S(1)} %project.12.own_ref, ...), custom_call_target="tpu_custom_call" | custom-call | tf_op jit(solution)/shard_map/attend/pallas_call | solution.py:32
  172.6 3.1 %collective-permute-start.36 = (bf16[1664,256]{1,0:T(8,128)(2,1)S(1)}, bf16[1664,256]{1,0:T(8,128)(2,1)S(1)}, u32[]{:S(2)}, u32[]{:S(2)}) collective-permute-start(bf16[1664,256]{1,0:T(8,128)(2,1)S(1)} %pack.1), channel_id=1, source_target_pairs={{0,4},{1,5},{2,6},{3,7},{4,0},{5,1},{6,2},{7,3},{8,12},{9,13},{10,... | collective-permute-start | bytes 2555912 | tf_op jit(solution)/shard_map/ppermute | solution.py:430
  178.3 1.9 project.16.refs_3_
  180.3 1.9 project.17.refs_3_
  183.5 7.1 %collective-permute-done.36.in_ref = bf16[1664,256]{1,0:T(8,128)(2,1)S(1)} collective-permute-done((bf16[1664,256]{1,0:T(8,128)(2,1)S(1)}, bf16[1664,256]{1,0:T(8,128)(2,1)S(1)}, u32[]{:S(2)}, u32[]{:S(2)}) %collective-permute-start.36) | collective-permute-done | bytes 852000 | tf_op jit(solution)/shard_map/ppermute | solution.py:430
  199.0 4.1 %attend.3.refs_0_ = bf16[640,256]{1,0:T(8,128)(2,1)S(1)} custom-call(s32[3]{0:T(128)S(1)} %pad_add_fusion.h_ref._, s32[1,640]{1,0:T(1,128)S(1)} %broadcast_in_dim.3.kind_ref.own_kind_ref, s32[1,640]{1,0:T(1,128)S(1)} %kinds_behind.1.other_kind_ref.kind_ref, bf16[640,768]{1,0:T(8,128)(2,1)S(1)} %project.18.own_ref, ...), custom_call_target="tpu_custom_call" | custom-call | tf_op jit(solution)/shard_map/attend/pallas_call | solution.py:32
  204.4 4.3 %collective-permute-done.43.refs_3_ = bf16[640,256]{1,0:T(8,128)(2,1)S(1)} collective-permute-done((bf16[640,256]{1,0:T(8,128)(2,1)S(1)}, bf16[640,256]{1,0:T(8,128)(2,1)S(1)}, u32[]{:S(2)}, u32[]{:S(2)}) %collective-permute-start.43) | collective-permute-done | bytes 327712 | tf_op jit(solution)/shard_map/ppermute | solution.py:430
  208.7 3.5 %collective-permute-done.44.refs_7_.refs_19_ = bf16[1,256,1024]{2,1,0:T(8,128)(2,1)S(1)} collective-permute-done((bf16[1,256,1024]{2,1,0:T(8,128)(2,1)S(1)}, bf16[1,256,1024]{2,1,0:T(8,128)(2,1)S(1)}, u32[]{:S(2)}, u32[]{:S(2)}) %collective-permute-start.44) | collective-permute-done | bytes 524320 | tf_op jit(solution)/shard_map/ppermute | solution.py:430
  212.2 9.4 %collective-permute-done.38.a_ref = bf16[2,1,256,1024]{3,2,1,0:T(8,128)(2,1)S(1)} collective-permute-done((bf16[2,1,256,1024]{3,2,1,0:T(8,128)(2,1)S(1)}, bf16[2,1,256,1024]{3,2,1,0:T(8,128)(2,1)S(1)}, u32[]{:S(2)}, u32[]{:S(2)}) %collective-permute-start.38) | collective-permute-done | bytes 1048608 | tf_op jit(solution)/shard_map/ppermute | solution.py:430
  223.7 3.7 %collective-permute-start.47 = (bf16[640,256]{1,0:T(8,128)(2,1)S(1)}, bf16[640,256]{1,0:T(8,128)(2,1)S(1)}, u32[]{:S(2)}, u32[]{:S(2)}) collective-permute-start(bf16[640,256]{1,0:T(8,128)(2,1)S(1)} %attend.3.refs_0_), channel_id=1, source_target_pairs={{0,4},{1,5},{2,6},{3,7},{4,0},{5,1},{6,2},{7,3},{8,12},{9,13},{10,... | collective-permute-start | bytes 983048 | tf_op jit(solution)/shard_map/ppermute | solution.py:430
  227.5 8.0 %collective-permute-done.47.refs_2_ = bf16[640,256]{1,0:T(8,128)(2,1)S(1)} collective-permute-done((bf16[640,256]{1,0:T(8,128)(2,1)S(1)}, bf16[640,256]{1,0:T(8,128)(2,1)S(1)}, u32[]{:S(2)}, u32[]{:S(2)}) %collective-permute-start.47) | collective-permute-done | bytes 327712 | tf_op jit(solution)/shard_map/ppermute | solution.py:430
  236.1 2.1 combine.3.refs_24_
  238.2 10.5 %collective-permute-done.46.refs_13_.refs_15_.refs_21_.refs_23_ = bf16[2,1,256,1024]{3,2,1,0:T(8,128)(2,1)S(1)} collective-permute-done((bf16[2,1,256,1024]{3,2,1,0:T(8,128)(2,1)S(1)}, bf16[2,1,256,1024]{3,2,1,0:T(8,128)(2,1)S(1)}, u32[]{:S(2)}, u32[]{:S(2)}) %collective-permute-start.46) | collective-permute-done | bytes 1048608 | tf_op jit(solution)/shard_map/ppermute | solution.py:430
  249.4 3.0 %collective-permute-done.49.refs_5_.refs_7_.refs_9_.refs_11_ = bf16[4,640,256]{2,1,0:T(8,128)(2,1)S(1)} collective-permute-done((bf16[4,640,256]{2,1,0:T(8,128)(2,1)S(1)}, bf16[4,640,256]{2,1,0:T(8,128)(2,1)S(1)}, u32[]{:S(2)}, u32[]{:S(2)}) %collective-permute-start.49) | collective-permute-done | bytes 1310752 | tf_op jit(solution)/shard_map/ppermute | solution.py:430
  252.4 2.8 combine.5
  255.4 2.8 combine.4.a_ref
  259.5 3.8 %collective-permute-start.52 = (bf16[320,1024]{1,0:T(8,128)(2,1)S(1)}, bf16[320,1024]{1,0:T(8,128)(2,1)S(1)}, u32[]{:S(2)}, u32[]{:S(2)}) collective-permute-start(bf16[320,1024]{1,0:T(8,128)(2,1)S(1)} %join.1), channel_id=1, source_target_pairs={{0,4},{1,5},{2,6},{3,7},{4,0},{5,1},{6,2},{7,3},{8,12},{9,13},{10,... | collective-permute-start | bytes 1966088 | tf_op jit(solution)/shard_map/ppermute | solution.py:430
  263.3 15.0 %collective-permute-done.52.c_ref = bf16[320,1024]{1,0:T(8,128)(2,1)S(1)} collective-permute-done((bf16[320,1024]{1,0:T(8,128)(2,1)S(1)}, bf16[320,1024]{1,0:T(8,128)(2,1)S(1)}, u32[]{:S(2)}, u32[]{:S(2)}) %collective-permute-start.52) | collective-permute-done | bytes 655392 | tf_op jit(solution)/shard_map/ppermute | solution.py:430
  278.4 2.1 collective-permute-done.53.d_ref
  280.5 2.4 shard_map.55
  (111 shorter events, 56.1 us)
Async XLA Ops:
  3.5 20.6 %collective-permute-start.2 = (bf16[3,512,256]{2,1,0:T(8,128)(2,1)S(1)}, bf16[3,512,256]{2,1,0:T(8,128)(2,1)S(1)}, u32[]{:S(2)}, u32[]{:S(2)}) collective-permute-start(bf16[3,512,256]{2,1,0:T(8,128)(2,1)S(1)} %get-tuple-element.89.refs_1_), channel_id=1, source_target_pairs={{0,2},{1,3},{2,0},{3,1},{4,6},{5,7},{6,4},{7,5},{8,10},{9,11},{10,... | collective-permute-start | bytes 2359304 | tf_op jit(solution)/shard_map/ppermute | solution.py:430
  6.5 19.0 %collective-permute-start.1 = (bf16[3,512,256]{2,1,0:T(8,128)(2,1)S(1)}, bf16[3,512,256]{2,1,0:T(8,128)(2,1)S(1)}, u32[]{:S(2)}, u32[]{:S(2)}) collective-permute-start(bf16[3,512,256]{2,1,0:T(8,128)(2,1)S(1)} %get-tuple-element.88), channel_id=1, source_target_pairs={{0,4},{1,5},{2,6},{3,7},{4,0},{5,1},{6,2},{7,3},{8,12},{9,13},{10,... | collective-permute-start | bytes 2359304 | tf_op jit(solution)/shard_map/ppermute | solution.py:430
  8.1 17.4 %collective-permute-start = (bf16[3,512,256]{2,1,0:T(8,128)(2,1)S(1)}, bf16[3,512,256]{2,1,0:T(8,128)(2,1)S(1)}, u32[]{:S(2)}, u32[]{:S(2)}) collective-permute-start(bf16[3,512,256]{2,1,0:T(8,128)(2,1)S(1)} %get-tuple-element.84), channel_id=1, source_target_pairs={{0,0},{1,1},{2,2},{3,3},{4,8},{5,9},{6,10},{7,11},{8,4},{9,5},{10,... | collective-permute-start | bytes 2359304 | tf_op jit(solution)/shard_map/ppermute | solution.py:430
  25.5 13.7 %collective-permute-start.5 = (bf16[3,512,256]{2,1,0:T(8,128)(2,1)S(1)}, bf16[3,512,256]{2,1,0:T(8,128)(2,1)S(1)}, u32[]{:S(2)}, u32[]{:S(2)}) collective-permute-start(bf16[3,512,256]{2,1,0:T(8,128)(2,1)S(1)} %get-tuple-element.93), channel_id=1, source_target_pairs={{4,8},{5,9},{6,10},{7,11},{8,4},{9,5},{10,6},{11,7},{20,24},{21,25... | collective-permute-start | bytes 2359304 | tf_op jit(solution)/shard_map/ppermute | solution.py:430
  26.2 18.2 %collective-permute-start.4 = (bf16[3,512,256]{2,1,0:T(8,128)(2,1)S(1)}, bf16[3,512,256]{2,1,0:T(8,128)(2,1)S(1)}, u32[]{:S(2)}, u32[]{:S(2)}) collective-permute-start(bf16[3,512,256]{2,1,0:T(8,128)(2,1)S(1)} %collective-permute-done.1.refs_3_), channel_id=1, source_target_pairs={{0,2},{1,3},{2,0},{3,1},{4,6},{5,7},{6,4},{7,5},{8,10},{9,11},{10,... | collective-permute-start | bytes 2359304 | tf_op jit(solution)/shard_map/ppermute | solution.py:430
  26.6 23.2 %collective-permute-start.3 = (bf16[3,512,256]{2,1,0:T(8,128)(2,1)S(1)}, bf16[3,512,256]{2,1,0:T(8,128)(2,1)S(1)}, u32[]{:S(2)}, u32[]{:S(2)}) collective-permute-start(bf16[3,512,256]{2,1,0:T(8,128)(2,1)S(1)} %collective-permute-done), channel_id=1, source_target_pairs={{0,4},{1,5},{2,6},{3,7},{4,0},{5,1},{6,2},{7,3},{8,12},{9,13},{10,... | collective-permute-start | bytes 2359304 | tf_op jit(solution)/shard_map/ppermute | solution.py:430
  36.8 28.3 %collective-permute-start.10 = (bf16[320,2048]{1,0:T(8,128)(2,1)S(1)}, bf16[320,2048]{1,0:T(8,128)(2,1)S(1)}, u32[]{:S(2)}, u32[]{:S(2)}) collective-permute-start(bf16[320,2048]{1,0:T(8,128)(2,1)S(1)} %get-tuple-element.102), channel_id=1, source_target_pairs={{0,1},{1,0},{2,3},{3,2},{4,5},{5,4},{6,7},{7,6},{8,9},{9,8},{10,11... | collective-permute-start | bytes 3932168 | tf_op jit(solution)/shard_map/ppermute | solution.py:430
  49.8 15.3 %collective-permute-start.8 = (bf16[3,512,256]{2,1,0:T(8,128)(2,1)S(1)}, bf16[3,512,256]{2,1,0:T(8,128)(2,1)S(1)}, u32[]{:S(2)}, u32[]{:S(2)}) collective-permute-start(bf16[3,512,256]{2,1,0:T(8,128)(2,1)S(1)} %collective-permute-done.3.a_ref), channel_id=1, source_target_pairs={{4,8},{5,9},{6,10},{7,11},{8,4},{9,5},{10,6},{11,7},{20,24},{21,25... | collective-permute-start | bytes 2359304 | tf_op jit(solution)/shard_map/ppermute | solution.py:430
  51.1 16.7 %collective-permute-start.7 = (bf16[3,512,256]{2,1,0:T(8,128)(2,1)S(1)}, bf16[3,512,256]{2,1,0:T(8,128)(2,1)S(1)}, u32[]{:S(2)}, u32[]{:S(2)}) collective-permute-start(bf16[3,512,256]{2,1,0:T(8,128)(2,1)S(1)} %choose.6.refs_5_), channel_id=1, source_target_pairs={{0,2},{1,3},{2,0},{3,1},{4,6},{5,7},{6,4},{7,5},{8,10},{9,11},{10,... | collective-permute-start | bytes 2359304 | tf_op jit(solution)/shard_map/ppermute | solution.py:430
  52.7 15.0 %collective-permute-start.6 = (bf16[160,2048]{1,0:T(8,128)(2,1)S(1)}, bf16[160,2048]{1,0:T(8,128)(2,1)S(1)}, u32[]{:S(2)}, u32[]{:S(2)}) collective-permute-start(bf16[160,2048]{1,0:T(8,128)(2,1)S(1)} %get-tuple-element.96), channel_id=1, source_target_pairs={{0,4},{1,5},{2,6},{3,7},{4,0},{5,1},{6,2},{7,3},{8,12},{9,13},{10,... | collective-permute-start | bytes 1966088 | tf_op jit(solution)/shard_map/ppermute | solution.py:430
  65.1 11.2 %collective-permute-start.11 = (bf16[320,2048]{1,0:T(8,128)(2,1)S(1)}, bf16[320,2048]{1,0:T(8,128)(2,1)S(1)}, u32[]{:S(2)}, u32[]{:S(2)}) collective-permute-start(bf16[320,2048]{1,0:T(8,128)(2,1)S(1)} %collective-permute-done.10.refs_2_), channel_id=1, source_target_pairs={{0,16},{1,17},{2,18},{3,19},{4,20},{5,21},{6,22},{7,23},{8,24},{9,... | collective-permute-start | bytes 3932168 | tf_op jit(solution)/shard_map/ppermute | solution.py:430
  67.8 18.9 %collective-permute-start.9 = (bf16[176,2048]{1,0:T(8,128)(2,1)S(1)}, bf16[176,2048]{1,0:T(8,128)(2,1)S(1)}, u32[]{:S(2)}, u32[]{:S(2)}) collective-permute-start(bf16[176,2048]{1,0:T(8,128)(2,1)S(1)} %get-tuple-element.100), channel_id=1, source_target_pairs={{0,4},{1,5},{2,6},{3,7},{4,0},{5,1},{6,2},{7,3},{8,12},{9,13},{10,... | collective-permute-start | bytes 2162696 | tf_op jit(solution)/shard_map/ppermute | solution.py:430
  71.1 15.6 %collective-permute-start.12 = (bf16[160,2048]{1,0:T(8,128)(2,1)S(1)}, bf16[160,2048]{1,0:T(8,128)(2,1)S(1)}, u32[]{:S(2)}, u32[]{:S(2)}) collective-permute-start(bf16[160,2048]{1,0:T(8,128)(2,1)S(1)} %collective-permute-done.6.refs_2_), channel_id=1, source_target_pairs={{0,1},{1,0},{2,3},{3,2},{4,5},{5,4},{6,7},{7,6},{8,9},{9,8},{10,11... | collective-permute-start | bytes 1966088 | tf_op jit(solution)/shard_map/ppermute | solution.py:430
  72.6 18.1 %collective-permute-start.22 = (bf16[3,512,256]{2,1,0:T(8,128)(2,1)S(1)}, bf16[3,512,256]{2,1,0:T(8,128)(2,1)S(1)}, u32[]{:S(2)}, u32[]{:S(2)}) collective-permute-start(bf16[3,512,256]{2,1,0:T(8,128)(2,1)S(1)} %get-tuple-element.121.refs_1_), channel_id=1, source_target_pairs={{0,2},{1,3},{2,0},{3,1},{4,6},{5,7},{6,4},{7,5},{8,10},{9,11},{10,... | collective-permute-start | bytes 2359304 | tf_op jit(solution)/shard_map/ppermute | solution.py:430
  74.1 17.9 %collective-permute-start.16 = (bf16[3,512,256]{2,1,0:T(8,128)(2,1)S(1)}, bf16[3,512,256]{2,1,0:T(8,128)(2,1)S(1)}, u32[]{:S(2)}, u32[]{:S(2)}) collective-permute-start(bf16[3,512,256]{2,1,0:T(8,128)(2,1)S(1)} %collective-permute-done.1.refs_3_), channel_id=1, source_target_pairs={{4,8},{5,9},{6,10},{7,11},{8,4},{9,5},{10,6},{11,7},{20,24},{21,25... | collective-permute-start | bytes 2359304 | tf_op jit(solution)/shard_map/ppermute | solution.py:430
  86.7 7.4 %collective-permute-start.13 = (bf16[160,2048]{1,0:T(8,128)(2,1)S(1)}, bf16[160,2048]{1,0:T(8,128)(2,1)S(1)}, u32[]{:S(2)}, u32[]{:S(2)}) collective-permute-start(bf16[160,2048]{1,0:T(8,128)(2,1)S(1)} %collective-permute-done.6.refs_2_), channel_id=1, source_target_pairs={{0,16},{1,17},{2,18},{3,19},{4,20},{5,21},{6,22},{7,23},{8,24},{9,... | collective-permute-start | bytes 1966088 | tf_op jit(solution)/shard_map/ppermute | solution.py:430
  87.2 17.6 %collective-permute-start.17 = (bf16[3,512,256]{2,1,0:T(8,128)(2,1)S(1)}, bf16[3,512,256]{2,1,0:T(8,128)(2,1)S(1)}, u32[]{:S(2)}, u32[]{:S(2)}) collective-permute-start(bf16[3,512,256]{2,1,0:T(8,128)(2,1)S(1)} %get-tuple-element.112), channel_id=1, source_target_pairs={{0,0},{1,1},{2,2},{3,3},{4,8},{5,9},{6,10},{7,11},{8,4},{9,5},{10,... | collective-permute-start | bytes 2359304 | tf_op jit(solution)/shard_map/ppermute | solution.py:430
  90.7 19.7 %collective-permute-start.21 = (bf16[3,512,256]{2,1,0:T(8,128)(2,1)S(1)}, bf16[3,512,256]{2,1,0:T(8,128)(2,1)S(1)}, u32[]{:S(2)}, u32[]{:S(2)}) collective-permute-start(bf16[3,512,256]{2,1,0:T(8,128)(2,1)S(1)} %collective-permute-done.8), channel_id=1, source_target_pairs={{4,0},{5,1},{6,2},{7,3},{8,12},{9,13},{10,14},{11,15},{20,16},{21,... | collective-permute-start | bytes 2359304 | tf_op jit(solution)/shard_map/ppermute | solution.py:430
  92.0 18.4 %collective-permute-start.15 = (bf16[176,2048]{1,0:T(8,128)(2,1)S(1)}, bf16[176,2048]{1,0:T(8,128)(2,1)S(1)}, u32[]{:S(2)}, u32[]{:S(2)}) collective-permute-start(bf16[176,2048]{1,0:T(8,128)(2,1)S(1)} %collective-permute-done.9.in_ref.refs_2_), channel_id=1, source_target_pairs={{0,1},{1,0},{2,3},{3,2},{4,5},{5,4},{6,7},{7,6},{8,9},{9,8},{10,11... | collective-permute-start | bytes 2162696 | tf_op jit(solution)/shard_map/ppermute | solution.py:430
  92.6 17.8 %collective-permute-start.23 = (bf16[1,256,1024]{2,1,0:T(8,128)(2,1)S(1)}, bf16[1,256,1024]{2,1,0:T(8,128)(2,1)S(1)}, u32[]{:S(2)}, u32[]{:S(2)}) collective-permute-start(bf16[1,256,1024]{2,1,0:T(8,128)(2,1)S(1)} %get-tuple-element.122.refs_4_.refs_16_), channel_id=1, source_target_pairs={{0,2},{1,3},{2,0},{3,1},{4,6},{5,7},{6,4},{7,5},{8,10},{9,11},{10,... | collective-permute-start | bytes 1572872 | tf_op jit(solution)/shard_map/ppermute | solution.py:430
  94.1 16.3 %collective-permute-start.25 = (bf16[1,256,1024]{2,1,0:T(8,128)(2,1)S(1)}, bf16[1,256,1024]{2,1,0:T(8,128)(2,1)S(1)}, u32[]{:S(2)}, u32[]{:S(2)}) collective-permute-start(bf16[1,256,1024]{2,1,0:T(8,128)(2,1)S(1)} %get-tuple-element.141.refs_0_.block_ref), channel_id=1, source_target_pairs={{0,4},{1,5},{2,6},{3,7},{12,8},{13,9},{14,10},{15,11},{16,20},{17,... | collective-permute-start | bytes 1572872 | tf_op jit(solution)/shard_map/ppermute | solution.py:430
  104.8 19.2 %collective-permute-start.20 = (bf16[3,512,256]{2,1,0:T(8,128)(2,1)S(1)}, bf16[3,512,256]{2,1,0:T(8,128)(2,1)S(1)}, u32[]{:S(2)}, u32[]{:S(2)}) collective-permute-start(bf16[3,512,256]{2,1,0:T(8,128)(2,1)S(1)} %get-tuple-element.117), channel_id=1, source_target_pairs={{4,8},{5,9},{6,10},{7,11},{8,4},{9,5},{10,6},{11,7},{20,24},{21,25... | collective-permute-start | bytes 2359304 | tf_op jit(solution)/shard_map/ppermute | solution.py:430
  110.4 20.3 %collective-permute-start.26 = (bf16[3,512,256]{2,1,0:T(8,128)(2,1)S(1)}, bf16[3,512,256]{2,1,0:T(8,128)(2,1)S(1)}, u32[]{:S(2)}, u32[]{:S(2)}) collective-permute-start(bf16[3,512,256]{2,1,0:T(8,128)(2,1)S(1)} %collective-permute-done.17), channel_id=1, source_target_pairs={{0,4},{1,5},{2,6},{3,7},{4,0},{5,1},{6,2},{7,3},{8,12},{9,13},{10,... | collective-permute-start | bytes 2359304 | tf_op jit(solution)/shard_map/ppermute | solution.py:430
  114.5 18.4 %collective-permute-start.24 = (bf16[3,512,256]{2,1,0:T(8,128)(2,1)S(1)}, bf16[3,512,256]{2,1,0:T(8,128)(2,1)S(1)}, u32[]{:S(2)}, u32[]{:S(2)}) collective-permute-start(bf16[3,512,256]{2,1,0:T(8,128)(2,1)S(1)} %choose.7.refs_1_), channel_id=1, source_target_pairs={{0,2},{1,3},{2,0},{3,1},{4,6},{5,7},{6,4},{7,5},{8,10},{9,11},{10,... | collective-permute-start | bytes 2359304 | tf_op jit(solution)/shard_map/ppermute | solution.py:430
  132.8 17.4 %collective-permute-start.29 = (bf16[3,512,256]{2,1,0:T(8,128)(2,1)S(1)}, bf16[3,512,256]{2,1,0:T(8,128)(2,1)S(1)}, u32[]{:S(2)}, u32[]{:S(2)}) collective-permute-start(bf16[3,512,256]{2,1,0:T(8,128)(2,1)S(1)} %get-tuple-element.130), channel_id=1, source_target_pairs={{0,4},{1,5},{2,6},{3,7},{4,0},{5,1},{6,2},{7,3},{8,12},{9,13},{10,... | collective-permute-start | bytes 2359304 | tf_op jit(solution)/shard_map/ppermute | solution.py:430
  133.1 17.1 %collective-permute-start.27 = (bf16[3,512,256]{2,1,0:T(8,128)(2,1)S(1)}, bf16[3,512,256]{2,1,0:T(8,128)(2,1)S(1)}, u32[]{:S(2)}, u32[]{:S(2)}) collective-permute-start(bf16[3,512,256]{2,1,0:T(8,128)(2,1)S(1)} %collective-permute-done.26.a_ref), channel_id=1, source_target_pairs={{4,8},{5,9},{6,10},{7,11},{8,4},{9,5},{10,6},{11,7},{20,24},{21,25... | collective-permute-start | bytes 2359304 | tf_op jit(solution)/shard_map/ppermute | solution.py:430
  134.5 17.4 %collective-permute-start.31 = (bf16[3,512,256]{2,1,0:T(8,128)(2,1)S(1)}, bf16[3,512,256]{2,1,0:T(8,128)(2,1)S(1)}, u32[]{:S(2)}, u32[]{:S(2)}) collective-permute-start(bf16[3,512,256]{2,1,0:T(8,128)(2,1)S(1)} %choose.8.refs_3_), channel_id=1, source_target_pairs={{0,2},{1,3},{2,0},{3,1},{4,6},{5,7},{6,4},{7,5},{8,10},{9,11},{10,... | collective-permute-start | bytes 2359304 | tf_op jit(solution)/shard_map/ppermute | solution.py:430
  136.7 30.0 %collective-permute-start.28 = (bf16[640,768]{1,0:T(8,128)(2,1)S(1)}, bf16[640,768]{1,0:T(8,128)(2,1)S(1)}, u32[]{:S(2)}, u32[]{:S(2)}) collective-permute-start(bf16[640,768]{1,0:T(8,128)(2,1)S(1)} %project.13), channel_id=1, source_target_pairs={{0,16},{1,17},{2,18},{3,19},{4,20},{5,21},{6,22},{7,23},{8,24},{9,... | collective-permute-start | bytes 2949128 | tf_op jit(solution)/shard_map/ppermute | solution.py:430
  150.2 20.6 %collective-permute-start.30 = (bf16[3,512,256]{2,1,0:T(8,128)(2,1)S(1)}, bf16[3,512,256]{2,1,0:T(8,128)(2,1)S(1)}, u32[]{:S(2)}, u32[]{:S(2)}) collective-permute-start(bf16[3,512,256]{2,1,0:T(8,128)(2,1)S(1)} %collective-permute-done.29.refs_1_), channel_id=1, source_target_pairs={{4,8},{5,9},{6,10},{7,11},{8,4},{9,5},{10,6},{11,7},{20,24},{21,25... | collective-permute-start | bytes 2359304 | tf_op jit(solution)/shard_map/ppermute | solution.py:430
  151.9 20.7 %collective-permute-start.35 = (bf16[3,512,256]{2,1,0:T(8,128)(2,1)S(1)}, bf16[3,512,256]{2,1,0:T(8,128)(2,1)S(1)}, u32[]{:S(2)}, u32[]{:S(2)}) collective-permute-start(bf16[3,512,256]{2,1,0:T(8,128)(2,1)S(1)} %collective-permute-done.27), channel_id=1, source_target_pairs={{4,0},{5,1},{6,2},{7,3},{8,12},{9,13},{10,14},{11,15},{20,16},{21,... | collective-permute-start | bytes 2359304 | tf_op jit(solution)/shard_map/ppermute | solution.py:430
  153.2 19.4 %collective-permute-start.34 = (bf16[3,512,256]{2,1,0:T(8,128)(2,1)S(1)}, bf16[3,512,256]{2,1,0:T(8,128)(2,1)S(1)}, u32[]{:S(2)}, u32[]{:S(2)}) collective-permute-start(bf16[3,512,256]{2,1,0:T(8,128)(2,1)S(1)} %collective-permute-done.29.refs_1_), channel_id=1, source_target_pairs={{0,2},{1,3},{2,0},{3,1},{4,6},{5,7},{6,4},{7,5},{8,10},{9,11},{10,... | collective-permute-start | bytes 2359304 | tf_op jit(solution)/shard_map/ppermute | solution.py:430
  153.5 17.3 %collective-permute-start.32 = (bf16[1,256,1024]{2,1,0:T(8,128)(2,1)S(1)}, bf16[1,256,1024]{2,1,0:T(8,128)(2,1)S(1)}, u32[]{:S(2)}, u32[]{:S(2)}) collective-permute-start(bf16[1,256,1024]{2,1,0:T(8,128)(2,1)S(1)} %get-tuple-element.144.refs_0_), channel_id=1, source_target_pairs={{0,4},{1,5},{2,6},{3,7},{12,8},{13,9},{14,10},{15,11},{16,20},{17,... | collective-permute-start | bytes 1572872 | tf_op jit(solution)/shard_map/ppermute | solution.py:430
  170.9 19.7 %collective-permute-start.33 = (bf16[2,1,256,1024]{3,2,1,0:T(8,128)(2,1)S(1)}, bf16[2,1,256,1024]{3,2,1,0:T(8,128)(2,1)S(1)}, u32[]{:S(2)}, u32[]{:S(2)}) collective-permute-start(bf16[2,1,256,1024]{3,2,1,0:T(8,128)(2,1)S(1)} %stack.20), channel_id=1, source_target_pairs={{4,8},{5,9},{6,10},{7,11},{8,4},{9,5},{10,6},{11,7},{20,24},{21,25... | collective-permute-start | bytes 3145736 | tf_op jit(solution)/shard_map/ppermute | solution.py:430
  172.6 18.0 %collective-permute-start.36 = (bf16[1664,256]{1,0:T(8,128)(2,1)S(1)}, bf16[1664,256]{1,0:T(8,128)(2,1)S(1)}, u32[]{:S(2)}, u32[]{:S(2)}) collective-permute-start(bf16[1664,256]{1,0:T(8,128)(2,1)S(1)} %pack.1), channel_id=1, source_target_pairs={{0,4},{1,5},{2,6},{3,7},{4,0},{5,1},{6,2},{7,3},{8,12},{9,13},{10,... | collective-permute-start | bytes 2555912 | tf_op jit(solution)/shard_map/ppermute | solution.py:430
  176.3 14.8 %collective-permute-start.40 = (bf16[3,512,256]{2,1,0:T(8,128)(2,1)S(1)}, bf16[3,512,256]{2,1,0:T(8,128)(2,1)S(1)}, u32[]{:S(2)}, u32[]{:S(2)}) collective-permute-start(bf16[3,512,256]{2,1,0:T(8,128)(2,1)S(1)} %choose.9.refs_1_), channel_id=1, source_target_pairs={{0,2},{1,3},{2,0},{3,1},{4,6},{5,7},{6,4},{7,5},{8,10},{9,11},{10,... | collective-permute-start | bytes 2359304 | tf_op jit(solution)/shard_map/ppermute | solution.py:430
  176.4 7.1 %collective-permute-start.37 = (bf16[640,256]{1,0:T(8,128)(2,1)S(1)}, bf16[640,256]{1,0:T(8,128)(2,1)S(1)}, u32[]{:S(2)}, u32[]{:S(2)}) collective-permute-start(bf16[640,256]{1,0:T(8,128)(2,1)S(1)} %attend.2.piece_ref.refs_0_), channel_id=1, source_target_pairs={{0,1},{1,0},{2,3},{3,2},{4,5},{5,4},{6,7},{7,6},{8,9},{9,8},{10,11... | collective-permute-start | bytes 983048 | tf_op jit(solution)/shard_map/ppermute | solution.py:430
  192.7 6.3 %collective-permute-start.41 = (bf16[640,768]{1,0:T(8,128)(2,1)S(1)}, bf16[640,768]{1,0:T(8,128)(2,1)S(1)}, u32[]{:S(2)}, u32[]{:S(2)}) collective-permute-start(bf16[640,768]{1,0:T(8,128)(2,1)S(1)} %project.19), channel_id=1, source_target_pairs={{0,16},{1,17},{2,18},{3,19},{4,20},{5,21},{6,22},{7,23},{8,24},{9,... | collective-permute-start | bytes 2949128 | tf_op jit(solution)/shard_map/ppermute | solution.py:430
  192.8 28.7 %collective-permute-start.38 = (bf16[2,1,256,1024]{3,2,1,0:T(8,128)(2,1)S(1)}, bf16[2,1,256,1024]{3,2,1,0:T(8,128)(2,1)S(1)}, u32[]{:S(2)}, u32[]{:S(2)}) collective-permute-start(bf16[2,1,256,1024]{3,2,1,0:T(8,128)(2,1)S(1)} %collective-permute-done.33), channel_id=1, source_target_pairs={{4,0},{5,1},{6,2},{7,3},{8,12},{9,13},{10,14},{11,15},{20,16},{21,... | collective-permute-start | bytes 3145736 | tf_op jit(solution)/shard_map/ppermute | solution.py:430
  194.1 27.4 %collective-permute-start.39 = (bf16[2,1,256,1024]{3,2,1,0:T(8,128)(2,1)S(1)}, bf16[2,1,256,1024]{3,2,1,0:T(8,128)(2,1)S(1)}, u32[]{:S(2)}, u32[]{:S(2)}) collective-permute-start(bf16[2,1,256,1024]{3,2,1,0:T(8,128)(2,1)S(1)} %stack.21), channel_id=1, source_target_pairs={{4,8},{5,9},{6,10},{7,11},{8,4},{9,5},{10,6},{11,7},{20,24},{21,25... | collective-permute-start | bytes 3145736 | tf_op jit(solution)/shard_map/ppermute | solution.py:430
  197.8 14.4 %collective-permute-start.44 = (bf16[1,256,1024]{2,1,0:T(8,128)(2,1)S(1)}, bf16[1,256,1024]{2,1,0:T(8,128)(2,1)S(1)}, u32[]{:S(2)}, u32[]{:S(2)}) collective-permute-start(bf16[1,256,1024]{2,1,0:T(8,128)(2,1)S(1)} %choose.10.refs_6_.refs_18_), channel_id=1, source_target_pairs={{0,2},{1,3},{2,0},{3,1},{4,6},{5,7},{6,4},{7,5},{8,10},{9,11},{10,... | collective-permute-start | bytes 1572872 | tf_op jit(solution)/shard_map/ppermute | solution.py:430
  198.2 10.5 %collective-permute-start.43 = (bf16[640,256]{1,0:T(8,128)(2,1)S(1)}, bf16[640,256]{1,0:T(8,128)(2,1)S(1)}, u32[]{:S(2)}, u32[]{:S(2)}) collective-permute-start(bf16[640,256]{1,0:T(8,128)(2,1)S(1)} %get-tuple-element.151.refs_2_), channel_id=1, source_target_pairs={{0,1},{1,0},{2,3},{3,2},{4,5},{5,4},{6,7},{7,6},{8,9},{9,8},{10,11... | collective-permute-start | bytes 983048 | tf_op jit(solution)/shard_map/ppermute | solution.py:430
  203.2 18.4 %collective-permute-start.42 = (bf16[640,256]{1,0:T(8,128)(2,1)S(1)}, bf16[640,256]{1,0:T(8,128)(2,1)S(1)}, u32[]{:S(2)}, u32[]{:S(2)}) collective-permute-start(bf16[640,256]{1,0:T(8,128)(2,1)S(1)} %attend.3.refs_0_), channel_id=1, source_target_pairs={{0,1},{1,0},{2,3},{3,2},{4,5},{5,4},{6,7},{7,6},{8,9},{9,8},{10,11... | collective-permute-start | bytes 983048 | tf_op jit(solution)/shard_map/ppermute | solution.py:430
  223.0 13.0 %collective-permute-start.45 = (bf16[4,640,256]{2,1,0:T(8,128)(2,1)S(1)}, bf16[4,640,256]{2,1,0:T(8,128)(2,1)S(1)}, u32[]{:S(2)}, u32[]{:S(2)}) collective-permute-start(bf16[4,640,256]{2,1,0:T(8,128)(2,1)S(1)} %stack.22.refs_0_.refs_2_), channel_id=1, source_target_pairs={{0,16},{1,17},{2,18},{3,19},{4,20},{5,21},{6,22},{7,23},{8,24},{9,... | collective-permute-start | bytes 3932168 | tf_op jit(solution)/shard_map/ppermute | solution.py:430
  223.1 25.6 %collective-permute-start.46 = (bf16[2,1,256,1024]{3,2,1,0:T(8,128)(2,1)S(1)}, bf16[2,1,256,1024]{3,2,1,0:T(8,128)(2,1)S(1)}, u32[]{:S(2)}, u32[]{:S(2)}) collective-permute-start(bf16[2,1,256,1024]{3,2,1,0:T(8,128)(2,1)S(1)} %choose.11.refs_12_.refs_14_.refs_20_.refs_22_), channel_id=1, source_target_pairs={{0,2},{1,3},{2,0},{3,1},{4,6},{5,7},{6,4},{7,5},{8,10},{9,11},{10,... | collective-permute-start | bytes 3145736 | tf_op jit(solution)/shard_map/ppermute | solution.py:430
  223.7 11.8 %collective-permute-start.47 = (bf16[640,256]{1,0:T(8,128)(2,1)S(1)}, bf16[640,256]{1,0:T(8,128)(2,1)S(1)}, u32[]{:S(2)}, u32[]{:S(2)}) collective-permute-start(bf16[640,256]{1,0:T(8,128)(2,1)S(1)} %attend.3.refs_0_), channel_id=1, source_target_pairs={{0,4},{1,5},{2,6},{3,7},{4,0},{5,1},{6,2},{7,3},{8,12},{9,13},{10,... | collective-permute-start | bytes 983048 | tf_op jit(solution)/shard_map/ppermute | solution.py:430
  235.5 13.2 %collective-permute-start.48 = (bf16[640,256]{1,0:T(8,128)(2,1)S(1)}, bf16[640,256]{1,0:T(8,128)(2,1)S(1)}, u32[]{:S(2)}, u32[]{:S(2)}) collective-permute-start(bf16[640,256]{1,0:T(8,128)(2,1)S(1)} %collective-permute-done.47.refs_2_), channel_id=1, source_target_pairs={{0,1},{1,0},{2,3},{3,2},{4,5},{5,4},{6,7},{7,6},{8,9},{9,8},{10,11... | collective-permute-start | bytes 983048 | tf_op jit(solution)/shard_map/ppermute | solution.py:430
  258.2 20.2 %collective-permute-start.50 = (bf16[640,1024]{1,0:T(8,128)(2,1)S(1)}, bf16[640,1024]{1,0:T(8,128)(2,1)S(1)}, u32[]{:S(2)}, u32[]{:S(2)}) collective-permute-start(bf16[640,1024]{1,0:T(8,128)(2,1)S(1)} %combine.4.a_ref), channel_id=1, source_target_pairs={{0,16},{1,17},{2,18},{3,19},{4,20},{5,21},{6,22},{7,23},{8,24},{9,... | collective-permute-start | bytes 3932168 | tf_op jit(solution)/shard_map/ppermute | solution.py:430
  259.5 18.8 %collective-permute-start.52 = (bf16[320,1024]{1,0:T(8,128)(2,1)S(1)}, bf16[320,1024]{1,0:T(8,128)(2,1)S(1)}, u32[]{:S(2)}, u32[]{:S(2)}) collective-permute-start(bf16[320,1024]{1,0:T(8,128)(2,1)S(1)} %join.1), channel_id=1, source_target_pairs={{0,4},{1,5},{2,6},{3,7},{4,0},{5,1},{6,2},{7,3},{8,12},{9,13},{10,... | collective-permute-start | bytes 1966088 | tf_op jit(solution)/shard_map/ppermute | solution.py:430
  (12 other events, 176.2 us)

commit v14 on v13

--- a/solution.py
+++ b/solution.py
@@ -105,6 +105,24 @@
             out_ref[...] = b_ref[...]
 
     return call("choose", kernel, here, [from_edge, from_middle], shaped(from_edge.shape))
+
+
+def choose_halves(here, from_edge, from_middle):
+    shape = from_edge.shape
+    half = shape[-1] // 2
+
+    def kernel(h_ref, a_ref, b_ref, low_ref, high_ref):
+        outer = Here(h_ref).outer
+        for ref, wanted in ((a_ref, outer), (b_ref, jnp.logical_not(outer))):
+
+            @pl.when(wanted)
+            def _(ref=ref):
+                for i in range(shape[0]):
+                    low_ref[i] = ref[i, :, :, :half]
+                    high_ref[i] = ref[i, :, :, half:]
+
+    outs = [shaped(shape[:-1] + (half,))] * 2
+    return call("choose_halves", kernel, here, [from_edge, from_middle], outs)
 
 
 def stack(here, arrays):
@@ -256,11 +274,14 @@
     return call("attend", kernel, here, [own_kind, other_kind, own, got], shaped((length, width)))
 
 
-def combine(here, slots, groups, total=None, final=False, offset=0, cut=False):
+def combine(here, slots, groups, total=None, part=None, cut=False):
     held_pieces, length, held = groups[0][0].shape
     shards = held_pieces // 2
-    features = groups[0][3][0][1].shape[-1]
-    tile = min(features, 256)
+    plain = [pair for group in groups for pair in group[3] if len(pair) == 3]
+    features = plain[0][1].shape[-1]
+    offset, side = (0, 0) if part is None else part
+    wide = features if part is None else features // 2
+    tile = min(wide, 256)
     half = length // 2
     terms = [group[:3] + (pair,) for group in groups for pair in group[3]]
     count = len(terms)
@@ -282,16 +303,18 @@
                 )
                 for i, (_, _, _, (arrival, *_)) in enumerate(terms)
             ]
-            for n in range(features // tile):
+            for n in range(wide // tile):
                 columns = slice(n * tile, (n + 1) * tile)
-                summed = None if total is None else refs[4 * count][offset + s, :, columns]
+                whole = slice(side * wide + n * tile, side * wide + (n + 1) * tile)
+                summed = None if total is None else refs[4 * count][offset + s, :, whole]
                 for i, (_, _, parity, (_, _, _, *index)) in enumerate(terms):
-                    near = refs[2 * count + 2 * i][(*index, 0, slice(None), columns)]
-                    far = refs[2 * count + 2 * i + 1][(*index, 0, slice(None), columns)]
+                    place = (*index, 0, slice(None), columns if index else whole)
+                    near = refs[2 * count + 2 * i][place]
+                    far = refs[2 * count + 2 * i + 1][place]
                     block = jnp.where(at_place.y == parity, near, far)
-                    part = jnp.dot(rows[i], block, preferred_element_type=F32)
-                    summed = part if summed is None else summed + part
-                if not final:
+                    product = jnp.dot(rows[i], block, preferred_element_type=F32)
+                    summed = product if summed is None else summed + product
+                if part is None:
                     outs[0][s, :, columns] = summed
                 elif cut:
                     result = summed.astype(BF16)
@@ -301,12 +324,12 @@
                 else:
                     outs[0][:, columns] = summed.astype(BF16)
 
-    if not final:
-        out_shape = shaped((len(slots), length, features), F32)
+    if part is None:
+        out_shape = shaped((len(slots), length, wide), F32)
     elif cut:
-        out_shape = [shaped((half, features))] * 2
+        out_shape = [shaped((half, wide))] * 2
     else:
-        out_shape = shaped((length, features))
+        out_shape = shaped((length, wide))
     return call("combine", kernel, here, args, out_shape)
 
 
@@ -324,14 +347,16 @@
     return call("join", kernel, here, [kind, kept, got], shaped(kept.shape))
 
 
-def assemble(here, kind, near, near_other, far, far_other):
-    length, width = near.shape
+def assemble(here, kind, parts):
+    length, wide = parts[0][0].shape
+    width = wide * len(parts)
     steps = 4
     tile = length // steps
     half = length // 2
-    args = [kind, near, near_other, far, far_other]
-
-    def kernel(h_ref, kind_ref, a_ref, b_ref, c_ref, d_ref, out_ref, held, sems):
+    args = [kind] + [array for part in parts for array in part]
+
+    def kernel(h_ref, kind_ref, *refs):
+        out_ref, held, sems = refs[-3:]
         at_place = Here(h_ref)
         core, first = at_place.core, at_place.column == 0
         copies = []
@@ -339,11 +364,15 @@
         for i in range(steps):
             rows = slice(i * tile, (i + 1) * tile)
             keep = kind[rows] == core
-            own = jnp.where(keep, a_ref[rows].astype(F32), b_ref[rows].astype(F32)).astype(BF16)
             part = slice(i * tile % half, i * tile % half + tile)
-            other = jnp.where(core == i * tile // half, c_ref[part], d_ref[part])
-            held[i, :, :width] = jnp.where(first, own, other)
-            held[i, :, width:] = jnp.where(first, other, own)
+            for j in range(len(parts)):
+                a_ref, b_ref, c_ref, d_ref = refs[4 * j : 4 * j + 4]
+                own = jnp.where(keep, a_ref[rows].astype(F32), b_ref[rows].astype(F32)).astype(BF16)
+                other = jnp.where(core == i * tile // half, c_ref[part], d_ref[part])
+                low = slice(j * wide, (j + 1) * wide)
+                high = slice(width + j * wide, width + (j + 1) * wide)
+                held[i, :, low] = jnp.where(first, own, other)
+                held[i, :, high] = jnp.where(first, other, own)
             copies.append(pltpu.make_async_copy(held.at[i], out_ref.at[rows], sems.at[i]))
             copies[-1].start()
         for copy in copies:
@@ -351,11 +380,12 @@
 
     return pl.pallas_call(
         kernel,
-        in_specs=[pl.BlockSpec(memory_space=SMEM)] + [pl.BlockSpec(memory_space=VMEM)] * 5,
+        in_specs=[pl.BlockSpec(memory_space=SMEM)] + [pl.BlockSpec(memory_space=VMEM)] * len(args),
         out_specs=pl.BlockSpec(memory_space=pl.ANY),
         out_shape=shaped((length, 2 * width)),
         scratch_shapes=[VMEM((steps, tile, 2 * width), BF16), pltpu.SemaphoreType.DMA((steps,))],
         compiler_params=pltpu.CompilerParams(vmem_limit_bytes=8 * 2**20),
+        name="assemble",
     )(here, *[pltpu.with_memory_space_constraint(a, VMEM) for a in args])
 
 
@@ -572,25 +602,31 @@
         held_b = over_tensor(attended_b)
 
         begun = (m24o, o23o, held_b[1], held_a[-1], p2o)
-        late_o = choose(here, after(o23o, *begun), m24o)
-        p34o = move(late_o, pair)
+        late_o = choose_halves(here, after(o23o, *begun), m24o)
         passed_b = move(attended_b, edge, o23o)
-        held_b += over_tensor(after(passed_b, late_o))
-        pieces_a = stack(here, [after(held_a[0], late_o)] + held_a[1:])
+        held_b += over_tensor(after(passed_b, late_o[0]))
+        p34o = [move(late_o[0], pair)]
+        p34o.append(move(late_o[1], pair, p34o[0]))
+        pieces_a = stack(here, [after(held_a[0], late_o[0])] + held_a[1:])
         pieces_a = (pieces_a, to_core(pieces_a))
-        both = ("partner", "own")
         near = [(0, mine_o, p1o), (1, second_o, p2o)]
-        last = [(2, late_o, p34o, 0), (3, late_o, p34o, 1)]
-        total = combine(here, both, [pieces_a + (0, near)])
-        pieces_b = stack(here, [after(held_b[0], total, p34o)] + held_b[1:])
+        total = combine(here, ("partner", "own"), [pieces_a + (0, near)])
+        pieces_b = stack(here, [after(held_b[0], total, p34o[0])] + held_b[1:])
         pieces_b = (pieces_b, to_core(pieces_b))
-        rest = [pieces_a + (0, last), pieces_b + (1, near + last)]
-
-        kept_away, sent_away = combine(here, ("partner",), rest, total, True, 0, True)
-        sent_away = to_core(sent_away)
-        near = combine(here, ("own",), rest, total, True, 1)
-        far = move(join(here, other_kind, kept_away, sent_away), edge)
-        return assemble(here, own_kind, near, to_core(near), far, to_core(far))
+
+        fars, rests = [], []
+        for side in range(2):
+            last = [(2, late_o[side], p34o[side], 0), (3, late_o[side], p34o[side], 1)]
+            rests.append([pieces_a + (0, last), pieces_b + (1, near + last)])
+            ready = after(total, fars[-1]) if fars else total
+            kept_away, sent_away = combine(here, ("partner",), rests[side], ready, (0, side), True)
+            joined = join(here, other_kind, kept_away, to_core(sent_away))
+            fars.append(move(joined, edge))
+        parts = []
+        for side in range(2):
+            near_part = combine(here, ("own",), rests[side], after(total, joined), (1, side))
+            parts.append((near_part, to_core(near_part), fars[side], to_core(fars[side])))
+        return assemble(here, own_kind, parts)
 
     return jax.shard_map(
         line_plan if places == 8 else gathered_plan,

time: 284 us -> 283 us (level)
    pallas_call x36 -> x39, Pallas kernels: 59.1 us -> 61.3 us  [call(): pl.pallas_call(kernel, in_specs=[pl.BlockSpec(memory_space=SMEM)] + [pl.B...]
    ppermute x54 -> x59, waiting for transfers between devices: 143 us -> 141 us  [move(): lax.ppermute(after(array, *earlier) if earlier else array, AXES, pairs)]
    ppermute x54 -> x59, starting transfers between devices: 73.3 us -> 73.1 us  [move(): lax.ppermute(after(array, *earlier) if earlier else array, AXES, pairs)]
  transfers between devices with their start and end apart: 54 -> 59, of which waited for: 27 -> 32; matrix products, arithmetic and copies ran while one was open for 0% -> 0% of each run, Pallas kernels for 18% -> 19%
where the time goes in v14:
time: 283 us
  waiting for transfers between devices  141 us (50%)
  starting transfers between devices  73.1 us (26%)
  Pallas kernels  63.6 us (22%)
  local copies, waits for them, and re-layouts  4.34 us (2%)
    ppermute x59, waiting for transfers between devices, move(): lax.ppermute(after(array, *earlier) if earlier else array, AXES, pairs)  141 us
    ppermute x59, starting transfers between devices, move(): lax.ppermute(after(array, *earlier) if earlier else array, AXES, pairs)  73.1 us
    pallas_call x39, Pallas kernels, call(): pl.pallas_call(kernel, in_specs=[pl.BlockSpec(memory_space=SMEM)] + [pl.B...  61.3 us
  transfers between devices with their start and end apart: 59, of which 32 were waited for; matrix products, arithmetic and copies ran while one was open for 0% of the time, Pallas kernels for 19%

profile of v14, /device:TPU:0, one launch (start us, length us, event | category | flops | bytes accessed | tf_op | source)
XLA Modules:
  0.0 282.8 jit_solution(3340702448103175857)
XLA Ops:
  0.8 1.9 copy-done
  3.5 3.0 %collective-permute-start.2 = (bf16[3,512,256]{2,1,0:T(8,128)(2,1)S(1)}, bf16[3,512,256]{2,1,0:T(8,128)(2,1)S(1)}, u32[]{:S(2)}, u32[]{:S(2)}) collective-permute-start(bf16[3,512,256]{2,1,0:T(8,128)(2,1)S(1)} %get-tuple-element.96.refs_1_), channel_id=1, source_target_pairs={{0,2},{1,3},{2,0},{3,1},{4,6},{5,7},{6,4},{7,5},{8,10},{9,11},{10,... | collective-permute-start | bytes 2359304 | tf_op jit(solution)/shard_map/ppermute | solution.py:460
  8.8 15.3 %collective-permute-done.2.refs_2_ = bf16[3,512,256]{2,1,0:T(8,128)(2,1)S(1)} collective-permute-done((bf16[3,512,256]{2,1,0:T(8,128)(2,1)S(1)}, bf16[3,512,256]{2,1,0:T(8,128)(2,1)S(1)}, u32[]{:S(2)}, u32[]{:S(2)}) %collective-permute-start.2) | collective-permute-done | bytes 786464 | tf_op jit(solution)/shard_map/ppermute | solution.py:460
  26.6 7.7 %collective-permute-start.3 = (bf16[3,512,256]{2,1,0:T(8,128)(2,1)S(1)}, bf16[3,512,256]{2,1,0:T(8,128)(2,1)S(1)}, u32[]{:S(2)}, u32[]{:S(2)}) collective-permute-start(bf16[3,512,256]{2,1,0:T(8,128)(2,1)S(1)} %collective-permute-done), channel_id=1, source_target_pairs={{0,4},{1,5},{2,6},{3,7},{4,0},{5,1},{6,2},{7,3},{8,12},{9,13},{10,... | collective-permute-start | bytes 2359304 | tf_op jit(solution)/shard_map/ppermute | solution.py:460
  34.3 1.7 copy-done.2
  39.2 5.2 %collective-permute-done.4.refs_4_ = bf16[3,512,256]{2,1,0:T(8,128)(2,1)S(1)} collective-permute-done((bf16[3,512,256]{2,1,0:T(8,128)(2,1)S(1)}, bf16[3,512,256]{2,1,0:T(8,128)(2,1)S(1)}, u32[]{:S(2)}, u32[]{:S(2)}) %collective-permute-start.4) | collective-permute-done | bytes 786464 | tf_op jit(solution)/shard_map/ppermute | solution.py:460
  44.4 5.4 %collective-permute-done.3.a_ref = bf16[3,512,256]{2,1,0:T(8,128)(2,1)S(1)} collective-permute-done((bf16[3,512,256]{2,1,0:T(8,128)(2,1)S(1)}, bf16[3,512,256]{2,1,0:T(8,128)(2,1)S(1)}, u32[]{:S(2)}, u32[]{:S(2)}) %collective-permute-start.3) | collective-permute-done | bytes 786464 | tf_op jit(solution)/shard_map/ppermute | solution.py:460
  52.7 3.5 %collective-permute-start.6 = (bf16[160,2048]{1,0:T(8,128)(2,1)S(1)}, bf16[160,2048]{1,0:T(8,128)(2,1)S(1)}, u32[]{:S(2)}, u32[]{:S(2)}) collective-permute-start(bf16[160,2048]{1,0:T(8,128)(2,1)S(1)} %get-tuple-element.103), channel_id=1, source_target_pairs={{0,4},{1,5},{2,6},{3,7},{4,0},{5,1},{6,2},{7,3},{8,12},{9,13},{10,... | collective-permute-start | bytes 1966088 | tf_op jit(solution)/shard_map/ppermute | solution.py:460
  56.2 8.8 %collective-permute-done.10.refs_2_ = bf16[320,2048]{1,0:T(8,128)(2,1)S(1)} collective-permute-done((bf16[320,2048]{1,0:T(8,128)(2,1)S(1)}, bf16[320,2048]{1,0:T(8,128)(2,1)S(1)}, u32[]{:S(2)}, u32[]{:S(2)}) %collective-permute-start.10) | collective-permute-done | bytes 1310752 | tf_op jit(solution)/shard_map/ppermute | solution.py:460
  65.1 2.7 collective-permute-done.6.refs_2_
  67.8 3.3 %collective-permute-start.9 = (bf16[176,2048]{1,0:T(8,128)(2,1)S(1)}, bf16[176,2048]{1,0:T(8,128)(2,1)S(1)}, u32[]{:S(2)}, u32[]{:S(2)}) collective-permute-start(bf16[176,2048]{1,0:T(8,128)(2,1)S(1)} %get-tuple-element.107), channel_id=1, source_target_pairs={{0,4},{1,5},{2,6},{3,7},{4,0},{5,1},{6,2},{7,3},{8,12},{9,13},{10,... | collective-permute-start | bytes 2162696 | tf_op jit(solution)/shard_map/ppermute | solution.py:460
  76.3 3.2 %normalize.3.refs_0_ = bf16[2,8,640,512]{3,2,1,0:T(8,128)(2,1)S(1)} custom-call(s32[3]{0:T(128)S(1)} %pad_add_fusion.h_ref._, f32[8,1,512]{2,1,0:T(1,128)S(1)} %bitcast.9, bf16[640,2048]{1,0:T(8,128)(2,1)S(1)} %copy-done.3, bf16[320,2048]{1,0:T(8,128)(2,1)S(1)} %collective-permute-done.10.refs_2_, bf16[320,2048]{1,0:T(8,128)(2,1)S(1)} %collective-permute-done.11.refs_3_), custom_call_target="tpu_custom_call" | custom-call | tf_op jit(solution)/shard_map/normalize/pallas_call | solution.py:32
  79.5 7.2 %collective-permute-done.12.refs_3_ = bf16[160,2048]{1,0:T(8,128)(2,1)S(1)} collective-permute-done((bf16[160,2048]{1,0:T(8,128)(2,1)S(1)}, bf16[160,2048]{1,0:T(8,128)(2,1)S(1)}, u32[]{:S(2)}, u32[]{:S(2)}) %collective-permute-start.12) | collective-permute-done | bytes 655392 | tf_op jit(solution)/shard_map/ppermute | solution.py:460
  87.9 2.8 collective-permute-done.22.refs_2_
  94.1 4.6 %collective-permute-start.25 = (bf16[1,256,1024]{2,1,0:T(8,128)(2,1)S(1)}, bf16[1,256,1024]{2,1,0:T(8,128)(2,1)S(1)}, u32[]{:S(2)}, u32[]{:S(2)}) collective-permute-start(bf16[1,256,1024]{2,1,0:T(8,128)(2,1)S(1)} %get-tuple-element.148.refs_0_.block_ref), channel_id=1, source_target_pairs={{0,4},{1,5},{2,6},{3,7},{12,8},{13,9},{14,10},{15,11},{16,20},{17,... | collective-permute-start | bytes 1572872 | tf_op jit(solution)/shard_map/ppermute | solution.py:460
  99.2 3.7 %project.10.refs_7_ = f32[2,640,768]{2,1,0:T(8,128)S(1)} custom-call(s32[3]{0:T(128)S(1)} %pad_add_fusion.h_ref._, bf16[2,8,640,512]{3,2,1,0:T(8,128)(2,1)S(1)} %normalize.3.refs_0_, bf16[3,512,256]{2,1,0:T(8,128)(2,1)S(1)} %get-tuple-element.96.refs_1_, bf16[3,512,256]{2,1,0:T(8,128)(2,1)S(1)} %collective-permute-done.2.refs_2_, ...), custom_call_target="tpu_custom_call" | custom-call | tf_op jit(solution)/shard_map/project/pallas_call | solution.py:32
  103.0 1.8 normalize.4.refs_0_
  105.5 4.8 %collective-permute-done.21.a_ref = bf16[3,512,256]{2,1,0:T(8,128)(2,1)S(1)} collective-permute-done((bf16[3,512,256]{2,1,0:T(8,128)(2,1)S(1)}, bf16[3,512,256]{2,1,0:T(8,128)(2,1)S(1)}, u32[]{:S(2)}, u32[]{:S(2)}) %collective-permute-start.21) | collective-permute-done | bytes 786464 | tf_op jit(solution)/shard_map/ppermute | solution.py:460
  110.4 3.5 %collective-permute-start.26 = (bf16[3,512,256]{2,1,0:T(8,128)(2,1)S(1)}, bf16[3,512,256]{2,1,0:T(8,128)(2,1)S(1)}, u32[]{:S(2)}, u32[]{:S(2)}) collective-permute-start(bf16[3,512,256]{2,1,0:T(8,128)(2,1)S(1)} %collective-permute-done.17), channel_id=1, source_target_pairs={{0,4},{1,5},{2,6},{3,7},{4,0},{5,1},{6,2},{7,3},{8,12},{9,13},{10,... | collective-permute-start | bytes 2359304 | tf_op jit(solution)/shard_map/ppermute | solution.py:460
  118.5 1.8 normalize.5.refs_0_
  120.3 3.7 %project.11.refs_3_ = f32[2,640,768]{2,1,0:T(8,128)S(1)} custom-call(s32[3]{0:T(128)S(1)} %pad_add_fusion.h_ref._, bf16[2,8,640,512]{3,2,1,0:T(8,128)(2,1)S(1)} %normalize.5.refs_0_, bf16[3,512,256]{2,1,0:T(8,128)(2,1)S(1)} %get-tuple-element.96.refs_1_, bf16[3,512,256]{2,1,0:T(8,128)(2,1)S(1)} %collective-permute-done.2.refs_2_, ...), custom_call_target="tpu_custom_call", output_to_operand_aliasing={{}: (8, {})} | custom-call | tf_op jit(solution)/shard_map/project/pallas_call | solution.py:32
  124.0 6.7 %collective-permute-done.26.a_ref = bf16[3,512,256]{2,1,0:T(8,128)(2,1)S(1)} collective-permute-done((bf16[3,512,256]{2,1,0:T(8,128)(2,1)S(1)}, bf16[3,512,256]{2,1,0:T(8,128)(2,1)S(1)}, u32[]{:S(2)}, u32[]{:S(2)}) %collective-permute-start.26) | collective-permute-done | bytes 786464 | tf_op jit(solution)/shard_map/ppermute | solution.py:460
  130.7 2.1 collective-permute-done.24.refs_2_
  138.5 11.7 %collective-permute-done.29.refs_1_ = bf16[3,512,256]{2,1,0:T(8,128)(2,1)S(1)} collective-permute-done((bf16[3,512,256]{2,1,0:T(8,128)(2,1)S(1)}, bf16[3,512,256]{2,1,0:T(8,128)(2,1)S(1)}, u32[]{:S(2)}, u32[]{:S(2)}) %collective-permute-start.29) | collective-permute-done | bytes 786464 | tf_op jit(solution)/shard_map/ppermute | solution.py:460
  153.5 7.1 %collective-permute-start.32 = (bf16[1,256,1024]{2,1,0:T(8,128)(2,1)S(1)}, bf16[1,256,1024]{2,1,0:T(8,128)(2,1)S(1)}, u32[]{:S(2)}, u32[]{:S(2)}) collective-permute-start(bf16[1,256,1024]{2,1,0:T(8,128)(2,1)S(1)} %get-tuple-element.151.refs_0_), channel_id=1, source_target_pairs={{0,4},{1,5},{2,6},{3,7},{12,8},{13,9},{14,10},{15,11},{16,20},{17,... | collective-permute-start | bytes 1572872 | tf_op jit(solution)/shard_map/ppermute | solution.py:460
  161.2 2.7 project.14.refs_5_
  164.0 2.7 project.15.refs_3_
  166.7 4.2 %attend.2.piece_ref.refs_0_ = bf16[640,256]{1,0:T(8,128)(2,1)S(1)} custom-call(s32[3]{0:T(128)S(1)} %pad_add_fusion.h_ref._, s32[1,640]{1,0:T(1,128)S(1)} %broadcast_in_dim.3.kind_ref.own_kind_ref, s32[1,640]{1,0:T(1,128)S(1)} %kinds_behind.1.other_kind_ref.kind_ref, bf16[640,768]{1,0:T(8,128)(2,1)S(1)} %project.12.own_ref, ...), custom_call_target="tpu_custom_call" | custom-call | tf_op jit(solution)/shard_map/attend/pallas_call | solution.py:32
  172.6 3.1 %collective-permute-start.36 = (bf16[1664,256]{1,0:T(8,128)(2,1)S(1)}, bf16[1664,256]{1,0:T(8,128)(2,1)S(1)}, u32[]{:S(2)}, u32[]{:S(2)}) collective-permute-start(bf16[1664,256]{1,0:T(8,128)(2,1)S(1)} %pack.1), channel_id=1, source_target_pairs={{0,4},{1,5},{2,6},{3,7},{4,0},{5,1},{6,2},{7,3},{8,12},{9,13},{10,... | collective-permute-start | bytes 2555912 | tf_op jit(solution)/shard_map/ppermute | solution.py:460
  178.3 1.9 project.16.refs_3_
  180.3 1.9 project.17.refs_3_
  183.5 7.1 %collective-permute-done.36.in_ref = bf16[1664,256]{1,0:T(8,128)(2,1)S(1)} collective-permute-done((bf16[1664,256]{1,0:T(8,128)(2,1)S(1)}, bf16[1664,256]{1,0:T(8,128)(2,1)S(1)}, u32[]{:S(2)}, u32[]{:S(2)}) %collective-permute-start.36) | collective-permute-done | bytes 852000 | tf_op jit(solution)/shard_map/ppermute | solution.py:460
  199.0 4.1 %attend.3.refs_0_ = bf16[640,256]{1,0:T(8,128)(2,1)S(1)} custom-call(s32[3]{0:T(128)S(1)} %pad_add_fusion.h_ref._, s32[1,640]{1,0:T(1,128)S(1)} %broadcast_in_dim.3.kind_ref.own_kind_ref, s32[1,640]{1,0:T(1,128)S(1)} %kinds_behind.1.other_kind_ref.kind_ref, bf16[640,768]{1,0:T(8,128)(2,1)S(1)} %project.18.own_ref, ...), custom_call_target="tpu_custom_call" | custom-call | tf_op jit(solution)/shard_map/attend/pallas_call | solution.py:32
  204.4 4.3 %collective-permute-done.43.refs_3_ = bf16[640,256]{1,0:T(8,128)(2,1)S(1)} collective-permute-done((bf16[640,256]{1,0:T(8,128)(2,1)S(1)}, bf16[640,256]{1,0:T(8,128)(2,1)S(1)}, u32[]{:S(2)}, u32[]{:S(2)}) %collective-permute-start.43) | collective-permute-done | bytes 327712 | tf_op jit(solution)/shard_map/ppermute | solution.py:460
  208.7 3.5 %collective-permute-done.44.refs_7_.refs_19_ = bf16[1,256,1024]{2,1,0:T(8,128)(2,1)S(1)} collective-permute-done((bf16[1,256,1024]{2,1,0:T(8,128)(2,1)S(1)}, bf16[1,256,1024]{2,1,0:T(8,128)(2,1)S(1)}, u32[]{:S(2)}, u32[]{:S(2)}) %collective-permute-start.44) | collective-permute-done | bytes 524320 | tf_op jit(solution)/shard_map/ppermute | solution.py:460
  212.2 9.4 %collective-permute-done.38.a_ref = bf16[2,1,256,1024]{3,2,1,0:T(8,128)(2,1)S(1)} collective-permute-done((bf16[2,1,256,1024]{3,2,1,0:T(8,128)(2,1)S(1)}, bf16[2,1,256,1024]{3,2,1,0:T(8,128)(2,1)S(1)}, u32[]{:S(2)}, u32[]{:S(2)}) %collective-permute-start.38) | collective-permute-done | bytes 1048608 | tf_op jit(solution)/shard_map/ppermute | solution.py:460
  223.1 3.8 %collective-permute-start.47 = (bf16[640,256]{1,0:T(8,128)(2,1)S(1)}, bf16[640,256]{1,0:T(8,128)(2,1)S(1)}, u32[]{:S(2)}, u32[]{:S(2)}) collective-permute-start(bf16[640,256]{1,0:T(8,128)(2,1)S(1)} %attend.3.refs_0_), channel_id=1, source_target_pairs={{0,4},{1,5},{2,6},{3,7},{4,0},{5,1},{6,2},{7,3},{8,12},{9,13},{10,... | collective-permute-start | bytes 983048 | tf_op jit(solution)/shard_map/ppermute | solution.py:460
  227.5 7.8 %collective-permute-done.47.refs_2_ = bf16[640,256]{1,0:T(8,128)(2,1)S(1)} collective-permute-done((bf16[640,256]{1,0:T(8,128)(2,1)S(1)}, bf16[640,256]{1,0:T(8,128)(2,1)S(1)}, u32[]{:S(2)}, u32[]{:S(2)}) %collective-permute-start.47) | collective-permute-done | bytes 327712 | tf_op jit(solution)/shard_map/ppermute | solution.py:460
  235.2 2.1 combine.5.refs_24_
  237.3 3.6 %collective-permute-done.46.refs_13_.refs_15_.refs_21_.refs_23_ = bf16[2,1,256,512]{3,2,1,0:T(8,128)(2,1)S(1)} collective-permute-done((bf16[2,1,256,512]{3,2,1,0:T(8,128)(2,1)S(1)}, bf16[2,1,256,512]{3,2,1,0:T(8,128)(2,1)S(1)}, u32[]{:S(2)}, u32[]{:S(2)}) %collective-permute-start.46) | collective-permute-done | bytes 524320 | tf_op jit(solution)/shard_map/ppermute | solution.py:460
  240.9 3.8 %collective-permute-done.48.refs_3_ = bf16[640,256]{1,0:T(8,128)(2,1)S(1)} collective-permute-done((bf16[640,256]{1,0:T(8,128)(2,1)S(1)}, bf16[640,256]{1,0:T(8,128)(2,1)S(1)}, u32[]{:S(2)}, u32[]{:S(2)}) %collective-permute-start.48) | collective-permute-done | bytes 327712 | tf_op jit(solution)/shard_map/ppermute | solution.py:460
  245.4 3.0 %collective-permute-done.49.refs_5_.refs_7_.refs_9_.refs_11_ = bf16[4,640,256]{2,1,0:T(8,128)(2,1)S(1)} collective-permute-done((bf16[4,640,256]{2,1,0:T(8,128)(2,1)S(1)}, bf16[4,640,256]{2,1,0:T(8,128)(2,1)S(1)}, u32[]{:S(2)}, u32[]{:S(2)}) %collective-permute-start.49) | collective-permute-done | bytes 1310752 | tf_op jit(solution)/shard_map/ppermute | solution.py:460
  248.4 1.7 combine.6
  254.3 8.2 %collective-permute-done.52.refs_2_ = bf16[320,512]{1,0:T(8,128)(2,1)S(1)} collective-permute-done((bf16[320,512]{1,0:T(8,128)(2,1)S(1)}, bf16[320,512]{1,0:T(8,128)(2,1)S(1)}, u32[]{:S(2)}, u32[]{:S(2)}) %collective-permute-start.52) | collective-permute-done | bytes 327712 | tf_op jit(solution)/shard_map/ppermute | solution.py:460
  262.5 2.1 collective-permute-done.50.refs_13_.refs_15_.refs_21_.refs_23_
  272.3 1.7 combine.8.refs_0_
  274.6 4.0 %collective-permute-done.57.refs_6_ = bf16[320,512]{1,0:T(8,128)(2,1)S(1)} collective-permute-done((bf16[320,512]{1,0:T(8,128)(2,1)S(1)}, bf16[320,512]{1,0:T(8,128)(2,1)S(1)}, u32[]{:S(2)}, u32[]{:S(2)}) %collective-permute-start.57) | collective-permute-done | bytes 327712 | tf_op jit(solution)/shard_map/ppermute | solution.py:460
  280.3 2.4 assemble.1
  (124 shorter events, 69.7 us)
Async XLA Ops:
  3.5 20.6 %collective-permute-start.2 = (bf16[3,512,256]{2,1,0:T(8,128)(2,1)S(1)}, bf16[3,512,256]{2,1,0:T(8,128)(2,1)S(1)}, u32[]{:S(2)}, u32[]{:S(2)}) collective-permute-start(bf16[3,512,256]{2,1,0:T(8,128)(2,1)S(1)} %get-tuple-element.96.refs_1_), channel_id=1, source_target_pairs={{0,2},{1,3},{2,0},{3,1},{4,6},{5,7},{6,4},{7,5},{8,10},{9,11},{10,... | collective-permute-start | bytes 2359304 | tf_op jit(solution)/shard_map/ppermute | solution.py:460
  6.5 19.0 %collective-permute-start.1 = (bf16[3,512,256]{2,1,0:T(8,128)(2,1)S(1)}, bf16[3,512,256]{2,1,0:T(8,128)(2,1)S(1)}, u32[]{:S(2)}, u32[]{:S(2)}) collective-permute-start(bf16[3,512,256]{2,1,0:T(8,128)(2,1)S(1)} %get-tuple-element.95), channel_id=1, source_target_pairs={{0,4},{1,5},{2,6},{3,7},{4,0},{5,1},{6,2},{7,3},{8,12},{9,13},{10,... | collective-permute-start | bytes 2359304 | tf_op jit(solution)/shard_map/ppermute | solution.py:460
  8.1 17.4 %collective-permute-start = (bf16[3,512,256]{2,1,0:T(8,128)(2,1)S(1)}, bf16[3,512,256]{2,1,0:T(8,128)(2,1)S(1)}, u32[]{:S(2)}, u32[]{:S(2)}) collective-permute-start(bf16[3,512,256]{2,1,0:T(8,128)(2,1)S(1)} %get-tuple-element.91), channel_id=1, source_target_pairs={{0,0},{1,1},{2,2},{3,3},{4,8},{5,9},{6,10},{7,11},{8,4},{9,5},{10,... | collective-permute-start | bytes 2359304 | tf_op jit(solution)/shard_map/ppermute | solution.py:460
  25.5 13.7 %collective-permute-start.5 = (bf16[3,512,256]{2,1,0:T(8,128)(2,1)S(1)}, bf16[3,512,256]{2,1,0:T(8,128)(2,1)S(1)}, u32[]{:S(2)}, u32[]{:S(2)}) collective-permute-start(bf16[3,512,256]{2,1,0:T(8,128)(2,1)S(1)} %get-tuple-element.100), channel_id=1, source_target_pairs={{4,8},{5,9},{6,10},{7,11},{8,4},{9,5},{10,6},{11,7},{20,24},{21,25... | collective-permute-start | bytes 2359304 | tf_op jit(solution)/shard_map/ppermute | solution.py:460
  26.2 18.2 %collective-permute-start.4 = (bf16[3,512,256]{2,1,0:T(8,128)(2,1)S(1)}, bf16[3,512,256]{2,1,0:T(8,128)(2,1)S(1)}, u32[]{:S(2)}, u32[]{:S(2)}) collective-permute-start(bf16[3,512,256]{2,1,0:T(8,128)(2,1)S(1)} %collective-permute-done.1.refs_3_), channel_id=1, source_target_pairs={{0,2},{1,3},{2,0},{3,1},{4,6},{5,7},{6,4},{7,5},{8,10},{9,11},{10,... | collective-permute-start | bytes 2359304 | tf_op jit(solution)/shard_map/ppermute | solution.py:460
  26.6 23.2 %collective-permute-start.3 = (bf16[3,512,256]{2,1,0:T(8,128)(2,1)S(1)}, bf16[3,512,256]{2,1,0:T(8,128)(2,1)S(1)}, u32[]{:S(2)}, u32[]{:S(2)}) collective-permute-start(bf16[3,512,256]{2,1,0:T(8,128)(2,1)S(1)} %collective-permute-done), channel_id=1, source_target_pairs={{0,4},{1,5},{2,6},{3,7},{4,0},{5,1},{6,2},{7,3},{8,12},{9,13},{10,... | collective-permute-start | bytes 2359304 | tf_op jit(solution)/shard_map/ppermute | solution.py:460
  36.8 28.3 %collective-permute-start.10 = (bf16[320,2048]{1,0:T(8,128)(2,1)S(1)}, bf16[320,2048]{1,0:T(8,128)(2,1)S(1)}, u32[]{:S(2)}, u32[]{:S(2)}) collective-permute-start(bf16[320,2048]{1,0:T(8,128)(2,1)S(1)} %get-tuple-element.109), channel_id=1, source_target_pairs={{0,1},{1,0},{2,3},{3,2},{4,5},{5,4},{6,7},{7,6},{8,9},{9,8},{10,11... | collective-permute-start | bytes 3932168 | tf_op jit(solution)/shard_map/ppermute | solution.py:460
  49.8 15.3 %collective-permute-start.8 = (bf16[3,512,256]{2,1,0:T(8,128)(2,1)S(1)}, bf16[3,512,256]{2,1,0:T(8,128)(2,1)S(1)}, u32[]{:S(2)}, u32[]{:S(2)}) collective-permute-start(bf16[3,512,256]{2,1,0:T(8,128)(2,1)S(1)} %collective-permute-done.3.a_ref), channel_id=1, source_target_pairs={{4,8},{5,9},{6,10},{7,11},{8,4},{9,5},{10,6},{11,7},{20,24},{21,25... | collective-permute-start | bytes 2359304 | tf_op jit(solution)/shard_map/ppermute | solution.py:460
  51.1 16.7 %collective-permute-start.7 = (bf16[3,512,256]{2,1,0:T(8,128)(2,1)S(1)}, bf16[3,512,256]{2,1,0:T(8,128)(2,1)S(1)}, u32[]{:S(2)}, u32[]{:S(2)}) collective-permute-start(bf16[3,512,256]{2,1,0:T(8,128)(2,1)S(1)} %choose.5.refs_5_), channel_id=1, source_target_pairs={{0,2},{1,3},{2,0},{3,1},{4,6},{5,7},{6,4},{7,5},{8,10},{9,11},{10,... | collective-permute-start | bytes 2359304 | tf_op jit(solution)/shard_map/ppermute | solution.py:460
  52.7 15.0 %collective-permute-start.6 = (bf16[160,2048]{1,0:T(8,128)(2,1)S(1)}, bf16[160,2048]{1,0:T(8,128)(2,1)S(1)}, u32[]{:S(2)}, u32[]{:S(2)}) collective-permute-start(bf16[160,2048]{1,0:T(8,128)(2,1)S(1)} %get-tuple-element.103), channel_id=1, source_target_pairs={{0,4},{1,5},{2,6},{3,7},{4,0},{5,1},{6,2},{7,3},{8,12},{9,13},{10,... | collective-permute-start | bytes 1966088 | tf_op jit(solution)/shard_map/ppermute | solution.py:460
  65.1 11.2 %collective-permute-start.11 = (bf16[320,2048]{1,0:T(8,128)(2,1)S(1)}, bf16[320,2048]{1,0:T(8,128)(2,1)S(1)}, u32[]{:S(2)}, u32[]{:S(2)}) collective-permute-start(bf16[320,2048]{1,0:T(8,128)(2,1)S(1)} %collective-permute-done.10.refs_2_), channel_id=1, source_target_pairs={{0,16},{1,17},{2,18},{3,19},{4,20},{5,21},{6,22},{7,23},{8,24},{9,... | collective-permute-start | bytes 3932168 | tf_op jit(solution)/shard_map/ppermute | solution.py:460
  67.8 18.9 %collective-permute-start.9 = (bf16[176,2048]{1,0:T(8,128)(2,1)S(1)}, bf16[176,2048]{1,0:T(8,128)(2,1)S(1)}, u32[]{:S(2)}, u32[]{:S(2)}) collective-permute-start(bf16[176,2048]{1,0:T(8,128)(2,1)S(1)} %get-tuple-element.107), channel_id=1, source_target_pairs={{0,4},{1,5},{2,6},{3,7},{4,0},{5,1},{6,2},{7,3},{8,12},{9,13},{10,... | collective-permute-start | bytes 2162696 | tf_op jit(solution)/shard_map/ppermute | solution.py:460
  71.1 15.6 %collective-permute-start.12 = (bf16[160,2048]{1,0:T(8,128)(2,1)S(1)}, bf16[160,2048]{1,0:T(8,128)(2,1)S(1)}, u32[]{:S(2)}, u32[]{:S(2)}) collective-permute-start(bf16[160,2048]{1,0:T(8,128)(2,1)S(1)} %collective-permute-done.6.refs_2_), channel_id=1, source_target_pairs={{0,1},{1,0},{2,3},{3,2},{4,5},{5,4},{6,7},{7,6},{8,9},{9,8},{10,11... | collective-permute-start | bytes 1966088 | tf_op jit(solution)/shard_map/ppermute | solution.py:460
  72.6 18.1 %collective-permute-start.22 = (bf16[3,512,256]{2,1,0:T(8,128)(2,1)S(1)}, bf16[3,512,256]{2,1,0:T(8,128)(2,1)S(1)}, u32[]{:S(2)}, u32[]{:S(2)}) collective-permute-start(bf16[3,512,256]{2,1,0:T(8,128)(2,1)S(1)} %get-tuple-element.128.refs_1_), channel_id=1, source_target_pairs={{0,2},{1,3},{2,0},{3,1},{4,6},{5,7},{6,4},{7,5},{8,10},{9,11},{10,... | collective-permute-start | bytes 2359304 | tf_op jit(solution)/shard_map/ppermute | solution.py:460
  74.1 17.9 %collective-permute-start.16 = (bf16[3,512,256]{2,1,0:T(8,128)(2,1)S(1)}, bf16[3,512,256]{2,1,0:T(8,128)(2,1)S(1)}, u32[]{:S(2)}, u32[]{:S(2)}) collective-permute-start(bf16[3,512,256]{2,1,0:T(8,128)(2,1)S(1)} %collective-permute-done.1.refs_3_), channel_id=1, source_target_pairs={{4,8},{5,9},{6,10},{7,11},{8,4},{9,5},{10,6},{11,7},{20,24},{21,25... | collective-permute-start | bytes 2359304 | tf_op jit(solution)/shard_map/ppermute | solution.py:460
  86.7 7.4 %collective-permute-start.13 = (bf16[160,2048]{1,0:T(8,128)(2,1)S(1)}, bf16[160,2048]{1,0:T(8,128)(2,1)S(1)}, u32[]{:S(2)}, u32[]{:S(2)}) collective-permute-start(bf16[160,2048]{1,0:T(8,128)(2,1)S(1)} %collective-permute-done.6.refs_2_), channel_id=1, source_target_pairs={{0,16},{1,17},{2,18},{3,19},{4,20},{5,21},{6,22},{7,23},{8,24},{9,... | collective-permute-start | bytes 1966088 | tf_op jit(solution)/shard_map/ppermute | solution.py:460
  87.2 17.6 %collective-permute-start.17 = (bf16[3,512,256]{2,1,0:T(8,128)(2,1)S(1)}, bf16[3,512,256]{2,1,0:T(8,128)(2,1)S(1)}, u32[]{:S(2)}, u32[]{:S(2)}) collective-permute-start(bf16[3,512,256]{2,1,0:T(8,128)(2,1)S(1)} %get-tuple-element.119), channel_id=1, source_target_pairs={{0,0},{1,1},{2,2},{3,3},{4,8},{5,9},{6,10},{7,11},{8,4},{9,5},{10,... | collective-permute-start | bytes 2359304 | tf_op jit(solution)/shard_map/ppermute | solution.py:460
  90.7 19.7 %collective-permute-start.21 = (bf16[3,512,256]{2,1,0:T(8,128)(2,1)S(1)}, bf16[3,512,256]{2,1,0:T(8,128)(2,1)S(1)}, u32[]{:S(2)}, u32[]{:S(2)}) collective-permute-start(bf16[3,512,256]{2,1,0:T(8,128)(2,1)S(1)} %collective-permute-done.8), channel_id=1, source_target_pairs={{4,0},{5,1},{6,2},{7,3},{8,12},{9,13},{10,14},{11,15},{20,16},{21,... | collective-permute-start | bytes 2359304 | tf_op jit(solution)/shard_map/ppermute | solution.py:460
  92.0 18.4 %collective-permute-start.15 = (bf16[176,2048]{1,0:T(8,128)(2,1)S(1)}, bf16[176,2048]{1,0:T(8,128)(2,1)S(1)}, u32[]{:S(2)}, u32[]{:S(2)}) collective-permute-start(bf16[176,2048]{1,0:T(8,128)(2,1)S(1)} %collective-permute-done.9.in_ref.refs_2_), channel_id=1, source_target_pairs={{0,1},{1,0},{2,3},{3,2},{4,5},{5,4},{6,7},{7,6},{8,9},{9,8},{10,11... | collective-permute-start | bytes 2162696 | tf_op jit(solution)/shard_map/ppermute | solution.py:460
  92.6 17.8 %collective-permute-start.23 = (bf16[1,256,1024]{2,1,0:T(8,128)(2,1)S(1)}, bf16[1,256,1024]{2,1,0:T(8,128)(2,1)S(1)}, u32[]{:S(2)}, u32[]{:S(2)}) collective-permute-start(bf16[1,256,1024]{2,1,0:T(8,128)(2,1)S(1)} %get-tuple-element.129.refs_4_.refs_16_), channel_id=1, source_target_pairs={{0,2},{1,3},{2,0},{3,1},{4,6},{5,7},{6,4},{7,5},{8,10},{9,11},{10,... | collective-permute-start | bytes 1572872 | tf_op jit(solution)/shard_map/ppermute | solution.py:460
  94.1 16.3 %collective-permute-start.25 = (bf16[1,256,1024]{2,1,0:T(8,128)(2,1)S(1)}, bf16[1,256,1024]{2,1,0:T(8,128)(2,1)S(1)}, u32[]{:S(2)}, u32[]{:S(2)}) collective-permute-start(bf16[1,256,1024]{2,1,0:T(8,128)(2,1)S(1)} %get-tuple-element.148.refs_0_.block_ref), channel_id=1, source_target_pairs={{0,4},{1,5},{2,6},{3,7},{12,8},{13,9},{14,10},{15,11},{16,20},{17,... | collective-permute-start | bytes 1572872 | tf_op jit(solution)/shard_map/ppermute | solution.py:460
  104.8 19.2 %collective-permute-start.20 = (bf16[3,512,256]{2,1,0:T(8,128)(2,1)S(1)}, bf16[3,512,256]{2,1,0:T(8,128)(2,1)S(1)}, u32[]{:S(2)}, u32[]{:S(2)}) collective-permute-start(bf16[3,512,256]{2,1,0:T(8,128)(2,1)S(1)} %get-tuple-element.124), channel_id=1, source_target_pairs={{4,8},{5,9},{6,10},{7,11},{8,4},{9,5},{10,6},{11,7},{20,24},{21,25... | collective-permute-start | bytes 2359304 | tf_op jit(solution)/shard_map/ppermute | solution.py:460
  110.4 20.3 %collective-permute-start.26 = (bf16[3,512,256]{2,1,0:T(8,128)(2,1)S(1)}, bf16[3,512,256]{2,1,0:T(8,128)(2,1)S(1)}, u32[]{:S(2)}, u32[]{:S(2)}) collective-permute-start(bf16[3,512,256]{2,1,0:T(8,128)(2,1)S(1)} %collective-permute-done.17), channel_id=1, source_target_pairs={{0,4},{1,5},{2,6},{3,7},{4,0},{5,1},{6,2},{7,3},{8,12},{9,13},{10,... | collective-permute-start | bytes 2359304 | tf_op jit(solution)/shard_map/ppermute | solution.py:460
  114.5 18.4 %collective-permute-start.24 = (bf16[3,512,256]{2,1,0:T(8,128)(2,1)S(1)}, bf16[3,512,256]{2,1,0:T(8,128)(2,1)S(1)}, u32[]{:S(2)}, u32[]{:S(2)}) collective-permute-start(bf16[3,512,256]{2,1,0:T(8,128)(2,1)S(1)} %choose.6.refs_1_), channel_id=1, source_target_pairs={{0,2},{1,3},{2,0},{3,1},{4,6},{5,7},{6,4},{7,5},{8,10},{9,11},{10,... | collective-permute-start | bytes 2359304 | tf_op jit(solution)/shard_map/ppermute | solution.py:460
  132.8 17.4 %collective-permute-start.29 = (bf16[3,512,256]{2,1,0:T(8,128)(2,1)S(1)}, bf16[3,512,256]{2,1,0:T(8,128)(2,1)S(1)}, u32[]{:S(2)}, u32[]{:S(2)}) collective-permute-start(bf16[3,512,256]{2,1,0:T(8,128)(2,1)S(1)} %get-tuple-element.137), channel_id=1, source_target_pairs={{0,4},{1,5},{2,6},{3,7},{4,0},{5,1},{6,2},{7,3},{8,12},{9,13},{10,... | collective-permute-start | bytes 2359304 | tf_op jit(solution)/shard_map/ppermute | solution.py:460
  133.1 17.1 %collective-permute-start.27 = (bf16[3,512,256]{2,1,0:T(8,128)(2,1)S(1)}, bf16[3,512,256]{2,1,0:T(8,128)(2,1)S(1)}, u32[]{:S(2)}, u32[]{:S(2)}) collective-permute-start(bf16[3,512,256]{2,1,0:T(8,128)(2,1)S(1)} %collective-permute-done.26.a_ref), channel_id=1, source_target_pairs={{4,8},{5,9},{6,10},{7,11},{8,4},{9,5},{10,6},{11,7},{20,24},{21,25... | collective-permute-start | bytes 2359304 | tf_op jit(solution)/shard_map/ppermute | solution.py:460
  134.5 17.4 %collective-permute-start.31 = (bf16[3,512,256]{2,1,0:T(8,128)(2,1)S(1)}, bf16[3,512,256]{2,1,0:T(8,128)(2,1)S(1)}, u32[]{:S(2)}, u32[]{:S(2)}) collective-permute-start(bf16[3,512,256]{2,1,0:T(8,128)(2,1)S(1)} %choose.7.refs_3_), channel_id=1, source_target_pairs={{0,2},{1,3},{2,0},{3,1},{4,6},{5,7},{6,4},{7,5},{8,10},{9,11},{10,... | collective-permute-start | bytes 2359304 | tf_op jit(solution)/shard_map/ppermute | solution.py:460
  136.7 30.0 %collective-permute-start.28 = (bf16[640,768]{1,0:T(8,128)(2,1)S(1)}, bf16[640,768]{1,0:T(8,128)(2,1)S(1)}, u32[]{:S(2)}, u32[]{:S(2)}) collective-permute-start(bf16[640,768]{1,0:T(8,128)(2,1)S(1)} %project.13), channel_id=1, source_target_pairs={{0,16},{1,17},{2,18},{3,19},{4,20},{5,21},{6,22},{7,23},{8,24},{9,... | collective-permute-start | bytes 2949128 | tf_op jit(solution)/shard_map/ppermute | solution.py:460
  150.2 20.6 %collective-permute-start.30 = (bf16[3,512,256]{2,1,0:T(8,128)(2,1)S(1)}, bf16[3,512,256]{2,1,0:T(8,128)(2,1)S(1)}, u32[]{:S(2)}, u32[]{:S(2)}) collective-permute-start(bf16[3,512,256]{2,1,0:T(8,128)(2,1)S(1)} %collective-permute-done.29.refs_1_), channel_id=1, source_target_pairs={{4,8},{5,9},{6,10},{7,11},{8,4},{9,5},{10,6},{11,7},{20,24},{21,25... | collective-permute-start | bytes 2359304 | tf_op jit(solution)/shard_map/ppermute | solution.py:460
  151.9 20.7 %collective-permute-start.35 = (bf16[3,512,256]{2,1,0:T(8,128)(2,1)S(1)}, bf16[3,512,256]{2,1,0:T(8,128)(2,1)S(1)}, u32[]{:S(2)}, u32[]{:S(2)}) collective-permute-start(bf16[3,512,256]{2,1,0:T(8,128)(2,1)S(1)} %collective-permute-done.27), channel_id=1, source_target_pairs={{4,0},{5,1},{6,2},{7,3},{8,12},{9,13},{10,14},{11,15},{20,16},{21,... | collective-permute-start | bytes 2359304 | tf_op jit(solution)/shard_map/ppermute | solution.py:460
  153.2 19.4 %collective-permute-start.34 = (bf16[3,512,256]{2,1,0:T(8,128)(2,1)S(1)}, bf16[3,512,256]{2,1,0:T(8,128)(2,1)S(1)}, u32[]{:S(2)}, u32[]{:S(2)}) collective-permute-start(bf16[3,512,256]{2,1,0:T(8,128)(2,1)S(1)} %collective-permute-done.29.refs_1_), channel_id=1, source_target_pairs={{0,2},{1,3},{2,0},{3,1},{4,6},{5,7},{6,4},{7,5},{8,10},{9,11},{10,... | collective-permute-start | bytes 2359304 | tf_op jit(solution)/shard_map/ppermute | solution.py:460
  153.5 17.3 %collective-permute-start.32 = (bf16[1,256,1024]{2,1,0:T(8,128)(2,1)S(1)}, bf16[1,256,1024]{2,1,0:T(8,128)(2,1)S(1)}, u32[]{:S(2)}, u32[]{:S(2)}) collective-permute-start(bf16[1,256,1024]{2,1,0:T(8,128)(2,1)S(1)} %get-tuple-element.151.refs_0_), channel_id=1, source_target_pairs={{0,4},{1,5},{2,6},{3,7},{12,8},{13,9},{14,10},{15,11},{16,20},{17,... | collective-permute-start | bytes 1572872 | tf_op jit(solution)/shard_map/ppermute | solution.py:460
  170.9 19.7 %collective-permute-start.33 = (bf16[2,1,256,1024]{3,2,1,0:T(8,128)(2,1)S(1)}, bf16[2,1,256,1024]{3,2,1,0:T(8,128)(2,1)S(1)}, u32[]{:S(2)}, u32[]{:S(2)}) collective-permute-start(bf16[2,1,256,1024]{3,2,1,0:T(8,128)(2,1)S(1)} %stack.20), channel_id=1, source_target_pairs={{4,8},{5,9},{6,10},{7,11},{8,4},{9,5},{10,6},{11,7},{20,24},{21,25... | collective-permute-start | bytes 3145736 | tf_op jit(solution)/shard_map/ppermute | solution.py:460
  172.6 18.0 %collective-permute-start.36 = (bf16[1664,256]{1,0:T(8,128)(2,1)S(1)}, bf16[1664,256]{1,0:T(8,128)(2,1)S(1)}, u32[]{:S(2)}, u32[]{:S(2)}) collective-permute-start(bf16[1664,256]{1,0:T(8,128)(2,1)S(1)} %pack.1), channel_id=1, source_target_pairs={{0,4},{1,5},{2,6},{3,7},{4,0},{5,1},{6,2},{7,3},{8,12},{9,13},{10,... | collective-permute-start | bytes 2555912 | tf_op jit(solution)/shard_map/ppermute | solution.py:460
  176.3 14.8 %collective-permute-start.40 = (bf16[3,512,256]{2,1,0:T(8,128)(2,1)S(1)}, bf16[3,512,256]{2,1,0:T(8,128)(2,1)S(1)}, u32[]{:S(2)}, u32[]{:S(2)}) collective-permute-start(bf16[3,512,256]{2,1,0:T(8,128)(2,1)S(1)} %choose.8.refs_1_), channel_id=1, source_target_pairs={{0,2},{1,3},{2,0},{3,1},{4,6},{5,7},{6,4},{7,5},{8,10},{9,11},{10,... | collective-permute-start | bytes 2359304 | tf_op jit(solution)/shard_map/ppermute | solution.py:460
  192.8 28.7 %collective-permute-start.38 = (bf16[2,1,256,1024]{3,2,1,0:T(8,128)(2,1)S(1)}, bf16[2,1,256,1024]{3,2,1,0:T(8,128)(2,1)S(1)}, u32[]{:S(2)}, u32[]{:S(2)}) collective-permute-start(bf16[2,1,256,1024]{3,2,1,0:T(8,128)(2,1)S(1)} %collective-permute-done.33), channel_id=1, source_target_pairs={{4,0},{5,1},{6,2},{7,3},{8,12},{9,13},{10,14},{11,15},{20,16},{21,... | collective-permute-start | bytes 3145736 | tf_op jit(solution)/shard_map/ppermute | solution.py:460
  194.1 27.4 %collective-permute-start.39 = (bf16[2,1,256,1024]{3,2,1,0:T(8,128)(2,1)S(1)}, bf16[2,1,256,1024]{3,2,1,0:T(8,128)(2,1)S(1)}, u32[]{:S(2)}, u32[]{:S(2)}) collective-permute-start(bf16[2,1,256,1024]{3,2,1,0:T(8,128)(2,1)S(1)} %stack.21), channel_id=1, source_target_pairs={{4,8},{5,9},{6,10},{7,11},{8,4},{9,5},{10,6},{11,7},{20,24},{21,25... | collective-permute-start | bytes 3145736 | tf_op jit(solution)/shard_map/ppermute | solution.py:460
  197.8 14.4 %collective-permute-start.44 = (bf16[1,256,1024]{2,1,0:T(8,128)(2,1)S(1)}, bf16[1,256,1024]{2,1,0:T(8,128)(2,1)S(1)}, u32[]{:S(2)}, u32[]{:S(2)}) collective-permute-start(bf16[1,256,1024]{2,1,0:T(8,128)(2,1)S(1)} %choose.9.refs_6_.refs_18_), channel_id=1, source_target_pairs={{0,2},{1,3},{2,0},{3,1},{4,6},{5,7},{6,4},{7,5},{8,10},{9,11},{10,... | collective-permute-start | bytes 1572872 | tf_op jit(solution)/shard_map/ppermute | solution.py:460
  198.2 10.5 %collective-permute-start.43 = (bf16[640,256]{1,0:T(8,128)(2,1)S(1)}, bf16[640,256]{1,0:T(8,128)(2,1)S(1)}, u32[]{:S(2)}, u32[]{:S(2)}) collective-permute-start(bf16[640,256]{1,0:T(8,128)(2,1)S(1)} %get-tuple-element.158.refs_2_), channel_id=1, source_target_pairs={{0,1},{1,0},{2,3},{3,2},{4,5},{5,4},{6,7},{7,6},{8,9},{9,8},{10,11... | collective-permute-start | bytes 983048 | tf_op jit(solution)/shard_map/ppermute | solution.py:460
  203.2 18.4 %collective-permute-start.42 = (bf16[640,256]{1,0:T(8,128)(2,1)S(1)}, bf16[640,256]{1,0:T(8,128)(2,1)S(1)}, u32[]{:S(2)}, u32[]{:S(2)}) collective-permute-start(bf16[640,256]{1,0:T(8,128)(2,1)S(1)} %attend.3.refs_0_), channel_id=1, source_target_pairs={{0,1},{1,0},{2,3},{3,2},{4,5},{5,4},{6,7},{7,6},{8,9},{9,8},{10,11... | collective-permute-start | bytes 983048 | tf_op jit(solution)/shard_map/ppermute | solution.py:460
  223.0 12.2 %collective-permute-start.45 = (bf16[4,640,256]{2,1,0:T(8,128)(2,1)S(1)}, bf16[4,640,256]{2,1,0:T(8,128)(2,1)S(1)}, u32[]{:S(2)}, u32[]{:S(2)}) collective-permute-start(bf16[4,640,256]{2,1,0:T(8,128)(2,1)S(1)} %stack.22.refs_0_.refs_2_), channel_id=1, source_target_pairs={{0,16},{1,17},{2,18},{3,19},{4,20},{5,21},{6,22},{7,23},{8,24},{9,... | collective-permute-start | bytes 3932168 | tf_op jit(solution)/shard_map/ppermute | solution.py:460
  223.1 12.1 %collective-permute-start.47 = (bf16[640,256]{1,0:T(8,128)(2,1)S(1)}, bf16[640,256]{1,0:T(8,128)(2,1)S(1)}, u32[]{:S(2)}, u32[]{:S(2)}) collective-permute-start(bf16[640,256]{1,0:T(8,128)(2,1)S(1)} %attend.3.refs_0_), channel_id=1, source_target_pairs={{0,4},{1,5},{2,6},{3,7},{4,0},{5,1},{6,2},{7,3},{8,12},{9,13},{10,... | collective-permute-start | bytes 983048 | tf_op jit(solution)/shard_map/ppermute | solution.py:460
  226.9 14.0 %collective-permute-start.46 = (bf16[2,1,256,512]{3,2,1,0:T(8,128)(2,1)S(1)}, bf16[2,1,256,512]{3,2,1,0:T(8,128)(2,1)S(1)}, u32[]{:S(2)}, u32[]{:S(2)}) collective-permute-start(bf16[2,1,256,512]{3,2,1,0:T(8,128)(2,1)S(1)} %get-tuple-element.162.refs_12_.refs_14_.refs_20_.refs_22_), channel_id=1, source_target_pairs={{0,2},{1,3},{2,0},{3,1},{4,6},{5,7},{6,4},{7,5},{8,10},{9,11},{10,... | collective-permute-start | bytes 1572872 | tf_op jit(solution)/shard_map/ppermute | solution.py:460
  235.2 9.5 %collective-permute-start.48 = (bf16[640,256]{1,0:T(8,128)(2,1)S(1)}, bf16[640,256]{1,0:T(8,128)(2,1)S(1)}, u32[]{:S(2)}, u32[]{:S(2)}) collective-permute-start(bf16[640,256]{1,0:T(8,128)(2,1)S(1)} %collective-permute-done.47.refs_2_), channel_id=1, source_target_pairs={{0,1},{1,0},{2,3},{3,2},{4,5},{5,4},{6,7},{7,6},{8,9},{9,8},{10,11... | collective-permute-start | bytes 983048 | tf_op jit(solution)/shard_map/ppermute | solution.py:460
  250.4 14.2 %collective-permute-start.50 = (bf16[2,1,256,512]{3,2,1,0:T(8,128)(2,1)S(1)}, bf16[2,1,256,512]{3,2,1,0:T(8,128)(2,1)S(1)}, u32[]{:S(2)}, u32[]{:S(2)}) collective-permute-start(bf16[2,1,256,512]{3,2,1,0:T(8,128)(2,1)S(1)} %get-tuple-element.168.refs_12_.refs_14_.refs_20_.refs_22_), channel_id=1, source_target_pairs={{0,2},{1,3},{2,0},{3,1},{4,6},{5,7},{6,4},{7,5},{8,10},{9,11},{10,... | collective-permute-start | bytes 1572872 | tf_op jit(solution)/shard_map/ppermute | solution.py:460
  252.7 9.8 %collective-permute-start.52 = (bf16[320,512]{1,0:T(8,128)(2,1)S(1)}, bf16[320,512]{1,0:T(8,128)(2,1)S(1)}, u32[]{:S(2)}, u32[]{:S(2)}) collective-permute-start(bf16[320,512]{1,0:T(8,128)(2,1)S(1)} %join.2), channel_id=1, source_target_pairs={{0,4},{1,5},{2,6},{3,7},{4,0},{5,1},{6,2},{7,3},{8,12},{9,13},{10,... | collective-permute-start | bytes 983048 | tf_op jit(solution)/shard_map/ppermute | solution.py:460
  268.8 9.8 %collective-permute-start.57 = (bf16[320,512]{1,0:T(8,128)(2,1)S(1)}, bf16[320,512]{1,0:T(8,128)(2,1)S(1)}, u32[]{:S(2)}, u32[]{:S(2)}) collective-permute-start(bf16[320,512]{1,0:T(8,128)(2,1)S(1)} %join.3), channel_id=1, source_target_pairs={{0,4},{1,5},{2,6},{3,7},{4,0},{5,1},{6,2},{7,3},{8,12},{9,13},{10,... | collective-permute-start | bytes 983048 | tf_op jit(solution)/shard_map/ppermute | solution.py:460
  272.2 8.1 %collective-permute-start.56 = (bf16[640,512]{1,0:T(8,128)(2,1)S(1)}, bf16[640,512]{1,0:T(8,128)(2,1)S(1)}, u32[]{:S(2)}, u32[]{:S(2)}) collective-permute-start(bf16[640,512]{1,0:T(8,128)(2,1)S(1)} %combine.9.refs_4_), channel_id=1, source_target_pairs={{0,16},{1,17},{2,18},{3,19},{4,20},{5,21},{6,22},{7,23},{8,24},{9,... | collective-permute-start | bytes 1966088 | tf_op jit(solution)/shard_map/ppermute | solution.py:460
  (17 other events, 200.2 us)

commit v15 on v14

--- a/solution.py
+++ b/solution.py
@@ -601,9 +601,9 @@
         attended_b = attend(here, own_kind, other_kind, ours_b, got_b)
         held_b = over_tensor(attended_b)
 
-        begun = (m24o, o23o, held_b[1], held_a[-1], p2o)
+        passed_b = move(attended_b, edge)
+        begun = (m24o, o23o, held_b[1], held_a[-1], p2o, passed_b)
         late_o = choose_halves(here, after(o23o, *begun), m24o)
-        passed_b = move(attended_b, edge, o23o)
         held_b += over_tensor(after(passed_b, late_o[0]))
         p34o = [move(late_o[0], pair)]
         p34o.append(move(late_o[1], pair, p34o[0]))

time: 283 us -> 286 us (1.011)
  waiting for transfers between devices: 141 us -> 144 us
  transfers between devices with their start and end apart: 59 -> 59, of which waited for: 32 -> 31; matrix products, arithmetic and copies ran while one was open for 0% -> 0% of each run, Pallas kernels for 19% -> 18%
where the time goes in v15:
time: 286 us; the launch traced here: 285 us
  waiting for transfers between devices  144 us (50%)
  starting transfers between devices  72.8 us (25%)
  Pallas kernels  63.6 us (22%)
  local copies, waits for them, and re-layouts  4.34 us (2%)
    ppermute x59, waiting for transfers between devices, move(): lax.ppermute(after(array, *earlier) if earlier else array, AXES, pairs)  144 us
    ppermute x59, starting transfers between devices, move(): lax.ppermute(after(array, *earlier) if earlier else array, AXES, pairs)  72.8 us
    pallas_call x39, Pallas kernels, call(): pl.pallas_call(kernel, in_specs=[pl.BlockSpec(memory_space=SMEM)] + [pl.B...  61.3 us
  transfers between devices with their start and end apart: 59, of which 31 were waited for; matrix products, arithmetic and copies ran while one was open for 0% of the time, Pallas kernels for 18%

profile of v15, /device:TPU:0, one launch (start us, length us, event | category | flops | bytes accessed | tf_op | source)
XLA Modules:
  0.0 285.4 jit_solution(624345025703658032)
XLA Ops:
  0.8 1.9 copy-done
  3.5 3.0 %collective-permute-start.2 = (bf16[3,512,256]{2,1,0:T(8,128)(2,1)S(1)}, bf16[3,512,256]{2,1,0:T(8,128)(2,1)S(1)}, u32[]{:S(2)}, u32[]{:S(2)}) collective-permute-start(bf16[3,512,256]{2,1,0:T(8,128)(2,1)S(1)} %get-tuple-element.95.refs_1_), channel_id=1, source_target_pairs={{0,2},{1,3},{2,0},{3,1},{4,6},{5,7},{6,4},{7,5},{8,10},{9,11},{10,... | collective-permute-start | bytes 2359304 | tf_op jit(solution)/shard_map/ppermute | solution.py:460
  8.8 15.3 %collective-permute-done.2.refs_2_ = bf16[3,512,256]{2,1,0:T(8,128)(2,1)S(1)} collective-permute-done((bf16[3,512,256]{2,1,0:T(8,128)(2,1)S(1)}, bf16[3,512,256]{2,1,0:T(8,128)(2,1)S(1)}, u32[]{:S(2)}, u32[]{:S(2)}) %collective-permute-start.2) | collective-permute-done | bytes 786464 | tf_op jit(solution)/shard_map/ppermute | solution.py:460
  26.6 7.7 %collective-permute-start.3 = (bf16[3,512,256]{2,1,0:T(8,128)(2,1)S(1)}, bf16[3,512,256]{2,1,0:T(8,128)(2,1)S(1)}, u32[]{:S(2)}, u32[]{:S(2)}) collective-permute-start(bf16[3,512,256]{2,1,0:T(8,128)(2,1)S(1)} %collective-permute-done), channel_id=1, source_target_pairs={{0,4},{1,5},{2,6},{3,7},{4,0},{5,1},{6,2},{7,3},{8,12},{9,13},{10,... | collective-permute-start | bytes 2359304 | tf_op jit(solution)/shard_map/ppermute | solution.py:460
  34.3 1.7 copy-done.2
  39.2 5.2 %collective-permute-done.4.refs_4_ = bf16[3,512,256]{2,1,0:T(8,128)(2,1)S(1)} collective-permute-done((bf16[3,512,256]{2,1,0:T(8,128)(2,1)S(1)}, bf16[3,512,256]{2,1,0:T(8,128)(2,1)S(1)}, u32[]{:S(2)}, u32[]{:S(2)}) %collective-permute-start.4) | collective-permute-done | bytes 786464 | tf_op jit(solution)/shard_map/ppermute | solution.py:460
  44.4 5.4 %collective-permute-done.3.a_ref = bf16[3,512,256]{2,1,0:T(8,128)(2,1)S(1)} collective-permute-done((bf16[3,512,256]{2,1,0:T(8,128)(2,1)S(1)}, bf16[3,512,256]{2,1,0:T(8,128)(2,1)S(1)}, u32[]{:S(2)}, u32[]{:S(2)}) %collective-permute-start.3) | collective-permute-done | bytes 786464 | tf_op jit(solution)/shard_map/ppermute | solution.py:460
  52.7 3.5 %collective-permute-start.6 = (bf16[160,2048]{1,0:T(8,128)(2,1)S(1)}, bf16[160,2048]{1,0:T(8,128)(2,1)S(1)}, u32[]{:S(2)}, u32[]{:S(2)}) collective-permute-start(bf16[160,2048]{1,0:T(8,128)(2,1)S(1)} %get-tuple-element.102), channel_id=1, source_target_pairs={{0,4},{1,5},{2,6},{3,7},{4,0},{5,1},{6,2},{7,3},{8,12},{9,13},{10,... | collective-permute-start | bytes 1966088 | tf_op jit(solution)/shard_map/ppermute | solution.py:460
  56.2 8.8 %collective-permute-done.10.refs_2_ = bf16[320,2048]{1,0:T(8,128)(2,1)S(1)} collective-permute-done((bf16[320,2048]{1,0:T(8,128)(2,1)S(1)}, bf16[320,2048]{1,0:T(8,128)(2,1)S(1)}, u32[]{:S(2)}, u32[]{:S(2)}) %collective-permute-start.10) | collective-permute-done | bytes 1310752 | tf_op jit(solution)/shard_map/ppermute | solution.py:460
  65.1 2.7 collective-permute-done.6.refs_2_
  67.8 3.3 %collective-permute-start.9 = (bf16[176,2048]{1,0:T(8,128)(2,1)S(1)}, bf16[176,2048]{1,0:T(8,128)(2,1)S(1)}, u32[]{:S(2)}, u32[]{:S(2)}) collective-permute-start(bf16[176,2048]{1,0:T(8,128)(2,1)S(1)} %get-tuple-element.106), channel_id=1, source_target_pairs={{0,4},{1,5},{2,6},{3,7},{4,0},{5,1},{6,2},{7,3},{8,12},{9,13},{10,... | collective-permute-start | bytes 2162696 | tf_op jit(solution)/shard_map/ppermute | solution.py:460
  76.3 3.2 %normalize.3.refs_0_ = bf16[2,8,640,512]{3,2,1,0:T(8,128)(2,1)S(1)} custom-call(s32[3]{0:T(128)S(1)} %pad_add_fusion.h_ref._, f32[8,1,512]{2,1,0:T(1,128)S(1)} %bitcast.9, bf16[640,2048]{1,0:T(8,128)(2,1)S(1)} %copy-done.3, bf16[320,2048]{1,0:T(8,128)(2,1)S(1)} %collective-permute-done.10.refs_2_, bf16[320,2048]{1,0:T(8,128)(2,1)S(1)} %collective-permute-done.11.refs_3_), custom_call_target="tpu_custom_call" | custom-call | tf_op jit(solution)/shard_map/normalize/pallas_call | solution.py:32
  79.5 7.2 %collective-permute-done.12.refs_3_ = bf16[160,2048]{1,0:T(8,128)(2,1)S(1)} collective-permute-done((bf16[160,2048]{1,0:T(8,128)(2,1)S(1)}, bf16[160,2048]{1,0:T(8,128)(2,1)S(1)}, u32[]{:S(2)}, u32[]{:S(2)}) %collective-permute-start.12) | collective-permute-done | bytes 655392 | tf_op jit(solution)/shard_map/ppermute | solution.py:460
  87.9 2.8 collective-permute-done.22.refs_2_
  94.1 4.6 %collective-permute-start.25 = (bf16[1,256,1024]{2,1,0:T(8,128)(2,1)S(1)}, bf16[1,256,1024]{2,1,0:T(8,128)(2,1)S(1)}, u32[]{:S(2)}, u32[]{:S(2)}) collective-permute-start(bf16[1,256,1024]{2,1,0:T(8,128)(2,1)S(1)} %get-tuple-element.147.refs_0_.block_ref), channel_id=1, source_target_pairs={{0,4},{1,5},{2,6},{3,7},{12,8},{13,9},{14,10},{15,11},{16,20},{17,... | collective-permute-start | bytes 1572872 | tf_op jit(solution)/shard_map/ppermute | solution.py:460
  99.2 3.7 %project.10.refs_7_ = f32[2,640,768]{2,1,0:T(8,128)S(1)} custom-call(s32[3]{0:T(128)S(1)} %pad_add_fusion.h_ref._, bf16[2,8,640,512]{3,2,1,0:T(8,128)(2,1)S(1)} %normalize.3.refs_0_, bf16[3,512,256]{2,1,0:T(8,128)(2,1)S(1)} %get-tuple-element.95.refs_1_, bf16[3,512,256]{2,1,0:T(8,128)(2,1)S(1)} %collective-permute-done.2.refs_2_, ...), custom_call_target="tpu_custom_call" | custom-call | tf_op jit(solution)/shard_map/project/pallas_call | solution.py:32
  103.0 1.8 normalize.4.refs_0_
  105.5 4.8 %collective-permute-done.21.a_ref = bf16[3,512,256]{2,1,0:T(8,128)(2,1)S(1)} collective-permute-done((bf16[3,512,256]{2,1,0:T(8,128)(2,1)S(1)}, bf16[3,512,256]{2,1,0:T(8,128)(2,1)S(1)}, u32[]{:S(2)}, u32[]{:S(2)}) %collective-permute-start.21) | collective-permute-done | bytes 786464 | tf_op jit(solution)/shard_map/ppermute | solution.py:460
  110.4 3.5 %collective-permute-start.26 = (bf16[3,512,256]{2,1,0:T(8,128)(2,1)S(1)}, bf16[3,512,256]{2,1,0:T(8,128)(2,1)S(1)}, u32[]{:S(2)}, u32[]{:S(2)}) collective-permute-start(bf16[3,512,256]{2,1,0:T(8,128)(2,1)S(1)} %collective-permute-done.17), channel_id=1, source_target_pairs={{0,4},{1,5},{2,6},{3,7},{4,0},{5,1},{6,2},{7,3},{8,12},{9,13},{10,... | collective-permute-start | bytes 2359304 | tf_op jit(solution)/shard_map/ppermute | solution.py:460
  118.5 1.8 normalize.5.refs_0_
  120.3 3.7 %project.11.refs_3_ = f32[2,640,768]{2,1,0:T(8,128)S(1)} custom-call(s32[3]{0:T(128)S(1)} %pad_add_fusion.h_ref._, bf16[2,8,640,512]{3,2,1,0:T(8,128)(2,1)S(1)} %normalize.5.refs_0_, bf16[3,512,256]{2,1,0:T(8,128)(2,1)S(1)} %get-tuple-element.95.refs_1_, bf16[3,512,256]{2,1,0:T(8,128)(2,1)S(1)} %collective-permute-done.2.refs_2_, ...), custom_call_target="tpu_custom_call", output_to_operand_aliasing={{}: (8, {})} | custom-call | tf_op jit(solution)/shard_map/project/pallas_call | solution.py:32
  124.0 6.7 %collective-permute-done.26.a_ref = bf16[3,512,256]{2,1,0:T(8,128)(2,1)S(1)} collective-permute-done((bf16[3,512,256]{2,1,0:T(8,128)(2,1)S(1)}, bf16[3,512,256]{2,1,0:T(8,128)(2,1)S(1)}, u32[]{:S(2)}, u32[]{:S(2)}) %collective-permute-start.26) | collective-permute-done | bytes 786464 | tf_op jit(solution)/shard_map/ppermute | solution.py:460
  130.7 2.1 collective-permute-done.24.refs_2_
  138.5 11.7 %collective-permute-done.29.refs_1_ = bf16[3,512,256]{2,1,0:T(8,128)(2,1)S(1)} collective-permute-done((bf16[3,512,256]{2,1,0:T(8,128)(2,1)S(1)}, bf16[3,512,256]{2,1,0:T(8,128)(2,1)S(1)}, u32[]{:S(2)}, u32[]{:S(2)}) %collective-permute-start.29) | collective-permute-done | bytes 786464 | tf_op jit(solution)/shard_map/ppermute | solution.py:460
  153.5 7.1 %collective-permute-start.32 = (bf16[1,256,1024]{2,1,0:T(8,128)(2,1)S(1)}, bf16[1,256,1024]{2,1,0:T(8,128)(2,1)S(1)}, u32[]{:S(2)}, u32[]{:S(2)}) collective-permute-start(bf16[1,256,1024]{2,1,0:T(8,128)(2,1)S(1)} %get-tuple-element.150.refs_0_), channel_id=1, source_target_pairs={{0,4},{1,5},{2,6},{3,7},{12,8},{13,9},{14,10},{15,11},{16,20},{17,... | collective-permute-start | bytes 1572872 | tf_op jit(solution)/shard_map/ppermute | solution.py:460
  161.2 2.7 project.14.refs_5_
  164.0 2.7 project.15.refs_3_
  166.7 4.2 %attend.2.piece_ref.refs_0_ = bf16[640,256]{1,0:T(8,128)(2,1)S(1)} custom-call(s32[3]{0:T(128)S(1)} %pad_add_fusion.h_ref._, s32[1,640]{1,0:T(1,128)S(1)} %broadcast_in_dim.3.kind_ref.own_kind_ref, s32[1,640]{1,0:T(1,128)S(1)} %kinds_behind.1.other_kind_ref.kind_ref, bf16[640,768]{1,0:T(8,128)(2,1)S(1)} %project.12.own_ref, ...), custom_call_target="tpu_custom_call" | custom-call | tf_op jit(solution)/shard_map/attend/pallas_call | solution.py:32
  172.6 3.1 %collective-permute-start.36 = (bf16[1664,256]{1,0:T(8,128)(2,1)S(1)}, bf16[1664,256]{1,0:T(8,128)(2,1)S(1)}, u32[]{:S(2)}, u32[]{:S(2)}) collective-permute-start(bf16[1664,256]{1,0:T(8,128)(2,1)S(1)} %pack.1), channel_id=1, source_target_pairs={{0,4},{1,5},{2,6},{3,7},{4,0},{5,1},{6,2},{7,3},{8,12},{9,13},{10,... | collective-permute-start | bytes 2555912 | tf_op jit(solution)/shard_map/ppermute | solution.py:460
  178.3 1.9 project.16.refs_3_
  180.3 1.9 project.17.refs_3_
  183.5 7.1 %collective-permute-done.36.in_ref = bf16[1664,256]{1,0:T(8,128)(2,1)S(1)} collective-permute-done((bf16[1664,256]{1,0:T(8,128)(2,1)S(1)}, bf16[1664,256]{1,0:T(8,128)(2,1)S(1)}, u32[]{:S(2)}, u32[]{:S(2)}) %collective-permute-start.36) | collective-permute-done | bytes 852000 | tf_op jit(solution)/shard_map/ppermute | solution.py:460
  199.1 4.2 %attend.3.refs_0_ = bf16[640,256]{1,0:T(8,128)(2,1)S(1)} custom-call(s32[3]{0:T(128)S(1)} %pad_add_fusion.h_ref._, s32[1,640]{1,0:T(1,128)S(1)} %broadcast_in_dim.3.kind_ref.own_kind_ref, s32[1,640]{1,0:T(1,128)S(1)} %kinds_behind.1.other_kind_ref.kind_ref, bf16[640,768]{1,0:T(8,128)(2,1)S(1)} %project.18.own_ref, ...), custom_call_target="tpu_custom_call" | custom-call | tf_op jit(solution)/shard_map/attend/pallas_call | solution.py:32
  204.5 3.3 %collective-permute-done.43.refs_3_ = bf16[640,256]{1,0:T(8,128)(2,1)S(1)} collective-permute-done((bf16[640,256]{1,0:T(8,128)(2,1)S(1)}, bf16[640,256]{1,0:T(8,128)(2,1)S(1)}, u32[]{:S(2)}, u32[]{:S(2)}) %collective-permute-start.43) | collective-permute-done | bytes 327712 | tf_op jit(solution)/shard_map/ppermute | solution.py:460
  207.8 6.1 %collective-permute-start.45 = (bf16[640,256]{1,0:T(8,128)(2,1)S(1)}, bf16[640,256]{1,0:T(8,128)(2,1)S(1)}, u32[]{:S(2)}, u32[]{:S(2)}) collective-permute-start(bf16[640,256]{1,0:T(8,128)(2,1)S(1)} %attend.3.refs_0_), channel_id=1, source_target_pairs={{0,4},{1,5},{2,6},{3,7},{4,0},{5,1},{6,2},{7,3},{8,12},{9,13},{10,... | collective-permute-start | bytes 983048 | tf_op jit(solution)/shard_map/ppermute | solution.py:460
  213.9 10.9 %collective-permute-done.38.a_ref = bf16[2,1,256,1024]{3,2,1,0:T(8,128)(2,1)S(1)} collective-permute-done((bf16[2,1,256,1024]{3,2,1,0:T(8,128)(2,1)S(1)}, bf16[2,1,256,1024]{3,2,1,0:T(8,128)(2,1)S(1)}, u32[]{:S(2)}, u32[]{:S(2)}) %collective-permute-start.38) | collective-permute-done | bytes 1048608 | tf_op jit(solution)/shard_map/ppermute | solution.py:460
  224.7 6.6 %collective-permute-done.45.refs_2_ = bf16[640,256]{1,0:T(8,128)(2,1)S(1)} collective-permute-done((bf16[640,256]{1,0:T(8,128)(2,1)S(1)}, bf16[640,256]{1,0:T(8,128)(2,1)S(1)}, u32[]{:S(2)}, u32[]{:S(2)}) %collective-permute-start.45) | collective-permute-done | bytes 327712 | tf_op jit(solution)/shard_map/ppermute | solution.py:460
  234.1 1.8 collective-permute-done.46.refs_1_.refs_3_
  235.9 2.1 combine.5.refs_24_
  238.0 9.2 %collective-permute-done.47.refs_13_.refs_15_.refs_21_.refs_23_ = bf16[2,1,256,512]{3,2,1,0:T(8,128)(2,1)S(1)} collective-permute-done((bf16[2,1,256,512]{3,2,1,0:T(8,128)(2,1)S(1)}, bf16[2,1,256,512]{3,2,1,0:T(8,128)(2,1)S(1)}, u32[]{:S(2)}, u32[]{:S(2)}) %collective-permute-start.47) | collective-permute-done | bytes 524320 | tf_op jit(solution)/shard_map/ppermute | solution.py:460
  248.0 3.0 %collective-permute-done.49.refs_5_.refs_7_.refs_9_.refs_11_ = bf16[4,640,256]{2,1,0:T(8,128)(2,1)S(1)} collective-permute-done((bf16[4,640,256]{2,1,0:T(8,128)(2,1)S(1)}, bf16[4,640,256]{2,1,0:T(8,128)(2,1)S(1)}, u32[]{:S(2)}, u32[]{:S(2)}) %collective-permute-start.49) | collective-permute-done | bytes 1310752 | tf_op jit(solution)/shard_map/ppermute | solution.py:460
  251.0 1.7 combine.6
  255.3 9.7 %collective-permute-done.52.refs_2_ = bf16[320,512]{1,0:T(8,128)(2,1)S(1)} collective-permute-done((bf16[320,512]{1,0:T(8,128)(2,1)S(1)}, bf16[320,512]{1,0:T(8,128)(2,1)S(1)}, u32[]{:S(2)}, u32[]{:S(2)}) %collective-permute-start.52) | collective-permute-done | bytes 327712 | tf_op jit(solution)/shard_map/ppermute | solution.py:460
  265.1 2.1 collective-permute-done.50.refs_13_.refs_15_.refs_21_.refs_23_
  267.1 1.7 combine.7
  271.5 1.7 combine.9.refs_4_
  275.7 5.5 %collective-permute-done.57.refs_6_ = bf16[320,512]{1,0:T(8,128)(2,1)S(1)} collective-permute-done((bf16[320,512]{1,0:T(8,128)(2,1)S(1)}, bf16[320,512]{1,0:T(8,128)(2,1)S(1)}, u32[]{:S(2)}, u32[]{:S(2)}) %collective-permute-start.57) | collective-permute-done | bytes 327712 | tf_op jit(solution)/shard_map/ppermute | solution.py:460
  282.8 2.4 assemble.1
  (124 shorter events, 65.6 us)
Async XLA Ops:
  3.5 20.6 %collective-permute-start.2 = (bf16[3,512,256]{2,1,0:T(8,128)(2,1)S(1)}, bf16[3,512,256]{2,1,0:T(8,128)(2,1)S(1)}, u32[]{:S(2)}, u32[]{:S(2)}) collective-permute-start(bf16[3,512,256]{2,1,0:T(8,128)(2,1)S(1)} %get-tuple-element.95.refs_1_), channel_id=1, source_target_pairs={{0,2},{1,3},{2,0},{3,1},{4,6},{5,7},{6,4},{7,5},{8,10},{9,11},{10,... | collective-permute-start | bytes 2359304 | tf_op jit(solution)/shard_map/ppermute | solution.py:460
  6.5 19.0 %collective-permute-start.1 = (bf16[3,512,256]{2,1,0:T(8,128)(2,1)S(1)}, bf16[3,512,256]{2,1,0:T(8,128)(2,1)S(1)}, u32[]{:S(2)}, u32[]{:S(2)}) collective-permute-start(bf16[3,512,256]{2,1,0:T(8,128)(2,1)S(1)} %get-tuple-element.94), channel_id=1, source_target_pairs={{0,4},{1,5},{2,6},{3,7},{4,0},{5,1},{6,2},{7,3},{8,12},{9,13},{10,... | collective-permute-start | bytes 2359304 | tf_op jit(solution)/shard_map/ppermute | solution.py:460
  8.1 17.4 %collective-permute-start = (bf16[3,512,256]{2,1,0:T(8,128)(2,1)S(1)}, bf16[3,512,256]{2,1,0:T(8,128)(2,1)S(1)}, u32[]{:S(2)}, u32[]{:S(2)}) collective-permute-start(bf16[3,512,256]{2,1,0:T(8,128)(2,1)S(1)} %get-tuple-element.90), channel_id=1, source_target_pairs={{0,0},{1,1},{2,2},{3,3},{4,8},{5,9},{6,10},{7,11},{8,4},{9,5},{10,... | collective-permute-start | bytes 2359304 | tf_op jit(solution)/shard_map/ppermute | solution.py:460
  25.5 13.7 %collective-permute-start.5 = (bf16[3,512,256]{2,1,0:T(8,128)(2,1)S(1)}, bf16[3,512,256]{2,1,0:T(8,128)(2,1)S(1)}, u32[]{:S(2)}, u32[]{:S(2)}) collective-permute-start(bf16[3,512,256]{2,1,0:T(8,128)(2,1)S(1)} %get-tuple-element.99), channel_id=1, source_target_pairs={{4,8},{5,9},{6,10},{7,11},{8,4},{9,5},{10,6},{11,7},{20,24},{21,25... | collective-permute-start | bytes 2359304 | tf_op jit(solution)/shard_map/ppermute | solution.py:460
  26.2 18.2 %collective-permute-start.4 = (bf16[3,512,256]{2,1,0:T(8,128)(2,1)S(1)}, bf16[3,512,256]{2,1,0:T(8,128)(2,1)S(1)}, u32[]{:S(2)}, u32[]{:S(2)}) collective-permute-start(bf16[3,512,256]{2,1,0:T(8,128)(2,1)S(1)} %collective-permute-done.1.refs_3_), channel_id=1, source_target_pairs={{0,2},{1,3},{2,0},{3,1},{4,6},{5,7},{6,4},{7,5},{8,10},{9,11},{10,... | collective-permute-start | bytes 2359304 | tf_op jit(solution)/shard_map/ppermute | solution.py:460
  26.6 23.2 %collective-permute-start.3 = (bf16[3,512,256]{2,1,0:T(8,128)(2,1)S(1)}, bf16[3,512,256]{2,1,0:T(8,128)(2,1)S(1)}, u32[]{:S(2)}, u32[]{:S(2)}) collective-permute-start(bf16[3,512,256]{2,1,0:T(8,128)(2,1)S(1)} %collective-permute-done), channel_id=1, source_target_pairs={{0,4},{1,5},{2,6},{3,7},{4,0},{5,1},{6,2},{7,3},{8,12},{9,13},{10,... | collective-permute-start | bytes 2359304 | tf_op jit(solution)/shard_map/ppermute | solution.py:460
  36.8 28.3 %collective-permute-start.10 = (bf16[320,2048]{1,0:T(8,128)(2,1)S(1)}, bf16[320,2048]{1,0:T(8,128)(2,1)S(1)}, u32[]{:S(2)}, u32[]{:S(2)}) collective-permute-start(bf16[320,2048]{1,0:T(8,128)(2,1)S(1)} %get-tuple-element.108), channel_id=1, source_target_pairs={{0,1},{1,0},{2,3},{3,2},{4,5},{5,4},{6,7},{7,6},{8,9},{9,8},{10,11... | collective-permute-start | bytes 3932168 | tf_op jit(solution)/shard_map/ppermute | solution.py:460
  49.8 15.3 %collective-permute-start.8 = (bf16[3,512,256]{2,1,0:T(8,128)(2,1)S(1)}, bf16[3,512,256]{2,1,0:T(8,128)(2,1)S(1)}, u32[]{:S(2)}, u32[]{:S(2)}) collective-permute-start(bf16[3,512,256]{2,1,0:T(8,128)(2,1)S(1)} %collective-permute-done.3.a_ref), channel_id=1, source_target_pairs={{4,8},{5,9},{6,10},{7,11},{8,4},{9,5},{10,6},{11,7},{20,24},{21,25... | collective-permute-start | bytes 2359304 | tf_op jit(solution)/shard_map/ppermute | solution.py:460
  51.1 16.7 %collective-permute-start.7 = (bf16[3,512,256]{2,1,0:T(8,128)(2,1)S(1)}, bf16[3,512,256]{2,1,0:T(8,128)(2,1)S(1)}, u32[]{:S(2)}, u32[]{:S(2)}) collective-permute-start(bf16[3,512,256]{2,1,0:T(8,128)(2,1)S(1)} %choose.5.refs_5_), channel_id=1, source_target_pairs={{0,2},{1,3},{2,0},{3,1},{4,6},{5,7},{6,4},{7,5},{8,10},{9,11},{10,... | collective-permute-start | bytes 2359304 | tf_op jit(solution)/shard_map/ppermute | solution.py:460
  52.7 15.0 %collective-permute-start.6 = (bf16[160,2048]{1,0:T(8,128)(2,1)S(1)}, bf16[160,2048]{1,0:T(8,128)(2,1)S(1)}, u32[]{:S(2)}, u32[]{:S(2)}) collective-permute-start(bf16[160,2048]{1,0:T(8,128)(2,1)S(1)} %get-tuple-element.102), channel_id=1, source_target_pairs={{0,4},{1,5},{2,6},{3,7},{4,0},{5,1},{6,2},{7,3},{8,12},{9,13},{10,... | collective-permute-start | bytes 1966088 | tf_op jit(solution)/shard_map/ppermute | solution.py:460
  65.1 11.2 %collective-permute-start.11 = (bf16[320,2048]{1,0:T(8,128)(2,1)S(1)}, bf16[320,2048]{1,0:T(8,128)(2,1)S(1)}, u32[]{:S(2)}, u32[]{:S(2)}) collective-permute-start(bf16[320,2048]{1,0:T(8,128)(2,1)S(1)} %collective-permute-done.10.refs_2_), channel_id=1, source_target_pairs={{0,16},{1,17},{2,18},{3,19},{4,20},{5,21},{6,22},{7,23},{8,24},{9,... | collective-permute-start | bytes 3932168 | tf_op jit(solution)/shard_map/ppermute | solution.py:460
  67.8 18.9 %collective-permute-start.9 = (bf16[176,2048]{1,0:T(8,128)(2,1)S(1)}, bf16[176,2048]{1,0:T(8,128)(2,1)S(1)}, u32[]{:S(2)}, u32[]{:S(2)}) collective-permute-start(bf16[176,2048]{1,0:T(8,128)(2,1)S(1)} %get-tuple-element.106), channel_id=1, source_target_pairs={{0,4},{1,5},{2,6},{3,7},{4,0},{5,1},{6,2},{7,3},{8,12},{9,13},{10,... | collective-permute-start | bytes 2162696 | tf_op jit(solution)/shard_map/ppermute | solution.py:460
  71.1 15.6 %collective-permute-start.12 = (bf16[160,2048]{1,0:T(8,128)(2,1)S(1)}, bf16[160,2048]{1,0:T(8,128)(2,1)S(1)}, u32[]{:S(2)}, u32[]{:S(2)}) collective-permute-start(bf16[160,2048]{1,0:T(8,128)(2,1)S(1)} %collective-permute-done.6.refs_2_), channel_id=1, source_target_pairs={{0,1},{1,0},{2,3},{3,2},{4,5},{5,4},{6,7},{7,6},{8,9},{9,8},{10,11... | collective-permute-start | bytes 1966088 | tf_op jit(solution)/shard_map/ppermute | solution.py:460
  72.6 18.1 %collective-permute-start.22 = (bf16[3,512,256]{2,1,0:T(8,128)(2,1)S(1)}, bf16[3,512,256]{2,1,0:T(8,128)(2,1)S(1)}, u32[]{:S(2)}, u32[]{:S(2)}) collective-permute-start(bf16[3,512,256]{2,1,0:T(8,128)(2,1)S(1)} %get-tuple-element.127.refs_1_), channel_id=1, source_target_pairs={{0,2},{1,3},{2,0},{3,1},{4,6},{5,7},{6,4},{7,5},{8,10},{9,11},{10,... | collective-permute-start | bytes 2359304 | tf_op jit(solution)/shard_map/ppermute | solution.py:460
  74.1 17.9 %collective-permute-start.16 = (bf16[3,512,256]{2,1,0:T(8,128)(2,1)S(1)}, bf16[3,512,256]{2,1,0:T(8,128)(2,1)S(1)}, u32[]{:S(2)}, u32[]{:S(2)}) collective-permute-start(bf16[3,512,256]{2,1,0:T(8,128)(2,1)S(1)} %collective-permute-done.1.refs_3_), channel_id=1, source_target_pairs={{4,8},{5,9},{6,10},{7,11},{8,4},{9,5},{10,6},{11,7},{20,24},{21,25... | collective-permute-start | bytes 2359304 | tf_op jit(solution)/shard_map/ppermute | solution.py:460
  86.7 7.4 %collective-permute-start.13 = (bf16[160,2048]{1,0:T(8,128)(2,1)S(1)}, bf16[160,2048]{1,0:T(8,128)(2,1)S(1)}, u32[]{:S(2)}, u32[]{:S(2)}) collective-permute-start(bf16[160,2048]{1,0:T(8,128)(2,1)S(1)} %collective-permute-done.6.refs_2_), channel_id=1, source_target_pairs={{0,16},{1,17},{2,18},{3,19},{4,20},{5,21},{6,22},{7,23},{8,24},{9,... | collective-permute-start | bytes 1966088 | tf_op jit(solution)/shard_map/ppermute | solution.py:460
  87.2 17.6 %collective-permute-start.17 = (bf16[3,512,256]{2,1,0:T(8,128)(2,1)S(1)}, bf16[3,512,256]{2,1,0:T(8,128)(2,1)S(1)}, u32[]{:S(2)}, u32[]{:S(2)}) collective-permute-start(bf16[3,512,256]{2,1,0:T(8,128)(2,1)S(1)} %get-tuple-element.118), channel_id=1, source_target_pairs={{0,0},{1,1},{2,2},{3,3},{4,8},{5,9},{6,10},{7,11},{8,4},{9,5},{10,... | collective-permute-start | bytes 2359304 | tf_op jit(solution)/shard_map/ppermute | solution.py:460
  90.7 19.7 %collective-permute-start.21 = (bf16[3,512,256]{2,1,0:T(8,128)(2,1)S(1)}, bf16[3,512,256]{2,1,0:T(8,128)(2,1)S(1)}, u32[]{:S(2)}, u32[]{:S(2)}) collective-permute-start(bf16[3,512,256]{2,1,0:T(8,128)(2,1)S(1)} %collective-permute-done.8), channel_id=1, source_target_pairs={{4,0},{5,1},{6,2},{7,3},{8,12},{9,13},{10,14},{11,15},{20,16},{21,... | collective-permute-start | bytes 2359304 | tf_op jit(solution)/shard_map/ppermute | solution.py:460
  92.0 18.4 %collective-permute-start.15 = (bf16[176,2048]{1,0:T(8,128)(2,1)S(1)}, bf16[176,2048]{1,0:T(8,128)(2,1)S(1)}, u32[]{:S(2)}, u32[]{:S(2)}) collective-permute-start(bf16[176,2048]{1,0:T(8,128)(2,1)S(1)} %collective-permute-done.9.in_ref.refs_2_), channel_id=1, source_target_pairs={{0,1},{1,0},{2,3},{3,2},{4,5},{5,4},{6,7},{7,6},{8,9},{9,8},{10,11... | collective-permute-start | bytes 2162696 | tf_op jit(solution)/shard_map/ppermute | solution.py:460
  92.6 17.8 %collective-permute-start.23 = (bf16[1,256,1024]{2,1,0:T(8,128)(2,1)S(1)}, bf16[1,256,1024]{2,1,0:T(8,128)(2,1)S(1)}, u32[]{:S(2)}, u32[]{:S(2)}) collective-permute-start(bf16[1,256,1024]{2,1,0:T(8,128)(2,1)S(1)} %get-tuple-element.128.refs_4_.refs_16_), channel_id=1, source_target_pairs={{0,2},{1,3},{2,0},{3,1},{4,6},{5,7},{6,4},{7,5},{8,10},{9,11},{10,... | collective-permute-start | bytes 1572872 | tf_op jit(solution)/shard_map/ppermute | solution.py:460
  94.1 16.3 %collective-permute-start.25 = (bf16[1,256,1024]{2,1,0:T(8,128)(2,1)S(1)}, bf16[1,256,1024]{2,1,0:T(8,128)(2,1)S(1)}, u32[]{:S(2)}, u32[]{:S(2)}) collective-permute-start(bf16[1,256,1024]{2,1,0:T(8,128)(2,1)S(1)} %get-tuple-element.147.refs_0_.block_ref), channel_id=1, source_target_pairs={{0,4},{1,5},{2,6},{3,7},{12,8},{13,9},{14,10},{15,11},{16,20},{17,... | collective-permute-start | bytes 1572872 | tf_op jit(solution)/shard_map/ppermute | solution.py:460
  104.8 19.2 %collective-permute-start.20 = (bf16[3,512,256]{2,1,0:T(8,128)(2,1)S(1)}, bf16[3,512,256]{2,1,0:T(8,128)(2,1)S(1)}, u32[]{:S(2)}, u32[]{:S(2)}) collective-permute-start(bf16[3,512,256]{2,1,0:T(8,128)(2,1)S(1)} %get-tuple-element.123), channel_id=1, source_target_pairs={{4,8},{5,9},{6,10},{7,11},{8,4},{9,5},{10,6},{11,7},{20,24},{21,25... | collective-permute-start | bytes 2359304 | tf_op jit(solution)/shard_map/ppermute | solution.py:460
  110.4 20.3 %collective-permute-start.26 = (bf16[3,512,256]{2,1,0:T(8,128)(2,1)S(1)}, bf16[3,512,256]{2,1,0:T(8,128)(2,1)S(1)}, u32[]{:S(2)}, u32[]{:S(2)}) collective-permute-start(bf16[3,512,256]{2,1,0:T(8,128)(2,1)S(1)} %collective-permute-done.17), channel_id=1, source_target_pairs={{0,4},{1,5},{2,6},{3,7},{4,0},{5,1},{6,2},{7,3},{8,12},{9,13},{10,... | collective-permute-start | bytes 2359304 | tf_op jit(solution)/shard_map/ppermute | solution.py:460
  114.5 18.4 %collective-permute-start.24 = (bf16[3,512,256]{2,1,0:T(8,128)(2,1)S(1)}, bf16[3,512,256]{2,1,0:T(8,128)(2,1)S(1)}, u32[]{:S(2)}, u32[]{:S(2)}) collective-permute-start(bf16[3,512,256]{2,1,0:T(8,128)(2,1)S(1)} %choose.6.refs_1_), channel_id=1, source_target_pairs={{0,2},{1,3},{2,0},{3,1},{4,6},{5,7},{6,4},{7,5},{8,10},{9,11},{10,... | collective-permute-start | bytes 2359304 | tf_op jit(solution)/shard_map/ppermute | solution.py:460
  132.8 17.4 %collective-permute-start.29 = (bf16[3,512,256]{2,1,0:T(8,128)(2,1)S(1)}, bf16[3,512,256]{2,1,0:T(8,128)(2,1)S(1)}, u32[]{:S(2)}, u32[]{:S(2)}) collective-permute-start(bf16[3,512,256]{2,1,0:T(8,128)(2,1)S(1)} %get-tuple-element.136), channel_id=1, source_target_pairs={{0,4},{1,5},{2,6},{3,7},{4,0},{5,1},{6,2},{7,3},{8,12},{9,13},{10,... | collective-permute-start | bytes 2359304 | tf_op jit(solution)/shard_map/ppermute | solution.py:460
  133.1 17.1 %collective-permute-start.27 = (bf16[3,512,256]{2,1,0:T(8,128)(2,1)S(1)}, bf16[3,512,256]{2,1,0:T(8,128)(2,1)S(1)}, u32[]{:S(2)}, u32[]{:S(2)}) collective-permute-start(bf16[3,512,256]{2,1,0:T(8,128)(2,1)S(1)} %collective-permute-done.26.a_ref), channel_id=1, source_target_pairs={{4,8},{5,9},{6,10},{7,11},{8,4},{9,5},{10,6},{11,7},{20,24},{21,25... | collective-permute-start | bytes 2359304 | tf_op jit(solution)/shard_map/ppermute | solution.py:460
  134.5 17.4 %collective-permute-start.31 = (bf16[3,512,256]{2,1,0:T(8,128)(2,1)S(1)}, bf16[3,512,256]{2,1,0:T(8,128)(2,1)S(1)}, u32[]{:S(2)}, u32[]{:S(2)}) collective-permute-start(bf16[3,512,256]{2,1,0:T(8,128)(2,1)S(1)} %choose.7.refs_3_), channel_id=1, source_target_pairs={{0,2},{1,3},{2,0},{3,1},{4,6},{5,7},{6,4},{7,5},{8,10},{9,11},{10,... | collective-permute-start | bytes 2359304 | tf_op jit(solution)/shard_map/ppermute | solution.py:460
  136.7 30.0 %collective-permute-start.28 = (bf16[640,768]{1,0:T(8,128)(2,1)S(1)}, bf16[640,768]{1,0:T(8,128)(2,1)S(1)}, u32[]{:S(2)}, u32[]{:S(2)}) collective-permute-start(bf16[640,768]{1,0:T(8,128)(2,1)S(1)} %project.13), channel_id=1, source_target_pairs={{0,16},{1,17},{2,18},{3,19},{4,20},{5,21},{6,22},{7,23},{8,24},{9,... | collective-permute-start | bytes 2949128 | tf_op jit(solution)/shard_map/ppermute | solution.py:460
  150.2 20.6 %collective-permute-start.30 = (bf16[3,512,256]{2,1,0:T(8,128)(2,1)S(1)}, bf16[3,512,256]{2,1,0:T(8,128)(2,1)S(1)}, u32[]{:S(2)}, u32[]{:S(2)}) collective-permute-start(bf16[3,512,256]{2,1,0:T(8,128)(2,1)S(1)} %collective-permute-done.29.refs_1_), channel_id=1, source_target_pairs={{4,8},{5,9},{6,10},{7,11},{8,4},{9,5},{10,6},{11,7},{20,24},{21,25... | collective-permute-start | bytes 2359304 | tf_op jit(solution)/shard_map/ppermute | solution.py:460
  151.9 20.7 %collective-permute-start.35 = (bf16[3,512,256]{2,1,0:T(8,128)(2,1)S(1)}, bf16[3,512,256]{2,1,0:T(8,128)(2,1)S(1)}, u32[]{:S(2)}, u32[]{:S(2)}) collective-permute-start(bf16[3,512,256]{2,1,0:T(8,128)(2,1)S(1)} %collective-permute-done.27), channel_id=1, source_target_pairs={{4,0},{5,1},{6,2},{7,3},{8,12},{9,13},{10,14},{11,15},{20,16},{21,... | collective-permute-start | bytes 2359304 | tf_op jit(solution)/shard_map/ppermute | solution.py:460
  153.2 19.4 %collective-permute-start.34 = (bf16[3,512,256]{2,1,0:T(8,128)(2,1)S(1)}, bf16[3,512,256]{2,1,0:T(8,128)(2,1)S(1)}, u32[]{:S(2)}, u32[]{:S(2)}) collective-permute-start(bf16[3,512,256]{2,1,0:T(8,128)(2,1)S(1)} %collective-permute-done.29.refs_1_), channel_id=1, source_target_pairs={{0,2},{1,3},{2,0},{3,1},{4,6},{5,7},{6,4},{7,5},{8,10},{9,11},{10,... | collective-permute-start | bytes 2359304 | tf_op jit(solution)/shard_map/ppermute | solution.py:460
  153.5 17.3 %collective-permute-start.32 = (bf16[1,256,1024]{2,1,0:T(8,128)(2,1)S(1)}, bf16[1,256,1024]{2,1,0:T(8,128)(2,1)S(1)}, u32[]{:S(2)}, u32[]{:S(2)}) collective-permute-start(bf16[1,256,1024]{2,1,0:T(8,128)(2,1)S(1)} %get-tuple-element.150.refs_0_), channel_id=1, source_target_pairs={{0,4},{1,5},{2,6},{3,7},{12,8},{13,9},{14,10},{15,11},{16,20},{17,... | collective-permute-start | bytes 1572872 | tf_op jit(solution)/shard_map/ppermute | solution.py:460
  170.9 19.7 %collective-permute-start.33 = (bf16[2,1,256,1024]{3,2,1,0:T(8,128)(2,1)S(1)}, bf16[2,1,256,1024]{3,2,1,0:T(8,128)(2,1)S(1)}, u32[]{:S(2)}, u32[]{:S(2)}) collective-permute-start(bf16[2,1,256,1024]{3,2,1,0:T(8,128)(2,1)S(1)} %stack.20), channel_id=1, source_target_pairs={{4,8},{5,9},{6,10},{7,11},{8,4},{9,5},{10,6},{11,7},{20,24},{21,25... | collective-permute-start | bytes 3145736 | tf_op jit(solution)/shard_map/ppermute | solution.py:460
  172.6 18.0 %collective-permute-start.36 = (bf16[1664,256]{1,0:T(8,128)(2,1)S(1)}, bf16[1664,256]{1,0:T(8,128)(2,1)S(1)}, u32[]{:S(2)}, u32[]{:S(2)}) collective-permute-start(bf16[1664,256]{1,0:T(8,128)(2,1)S(1)} %pack.1), channel_id=1, source_target_pairs={{0,4},{1,5},{2,6},{3,7},{4,0},{5,1},{6,2},{7,3},{8,12},{9,13},{10,... | collective-permute-start | bytes 2555912 | tf_op jit(solution)/shard_map/ppermute | solution.py:460
  176.3 14.8 %collective-permute-start.40 = (bf16[3,512,256]{2,1,0:T(8,128)(2,1)S(1)}, bf16[3,512,256]{2,1,0:T(8,128)(2,1)S(1)}, u32[]{:S(2)}, u32[]{:S(2)}) collective-permute-start(bf16[3,512,256]{2,1,0:T(8,128)(2,1)S(1)} %choose.8.refs_1_), channel_id=1, source_target_pairs={{0,2},{1,3},{2,0},{3,1},{4,6},{5,7},{6,4},{7,5},{8,10},{9,11},{10,... | collective-permute-start | bytes 2359304 | tf_op jit(solution)/shard_map/ppermute | solution.py:460
  192.8 21.1 %collective-permute-start.39 = (bf16[2,1,256,1024]{3,2,1,0:T(8,128)(2,1)S(1)}, bf16[2,1,256,1024]{3,2,1,0:T(8,128)(2,1)S(1)}, u32[]{:S(2)}, u32[]{:S(2)}) collective-permute-start(bf16[2,1,256,1024]{3,2,1,0:T(8,128)(2,1)S(1)} %stack.21), channel_id=1, source_target_pairs={{4,8},{5,9},{6,10},{7,11},{8,4},{9,5},{10,6},{11,7},{20,24},{21,25... | collective-permute-start | bytes 3145736 | tf_op jit(solution)/shard_map/ppermute | solution.py:460
  193.6 31.2 %collective-permute-start.38 = (bf16[2,1,256,1024]{3,2,1,0:T(8,128)(2,1)S(1)}, bf16[2,1,256,1024]{3,2,1,0:T(8,128)(2,1)S(1)}, u32[]{:S(2)}, u32[]{:S(2)}) collective-permute-start(bf16[2,1,256,1024]{3,2,1,0:T(8,128)(2,1)S(1)} %collective-permute-done.33), channel_id=1, source_target_pairs={{4,0},{5,1},{6,2},{7,3},{8,12},{9,13},{10,14},{11,15},{20,16},{21,... | collective-permute-start | bytes 3145736 | tf_op jit(solution)/shard_map/ppermute | solution.py:460
  197.2 10.6 %collective-permute-start.43 = (bf16[640,256]{1,0:T(8,128)(2,1)S(1)}, bf16[640,256]{1,0:T(8,128)(2,1)S(1)}, u32[]{:S(2)}, u32[]{:S(2)}) collective-permute-start(bf16[640,256]{1,0:T(8,128)(2,1)S(1)} %get-tuple-element.157.refs_2_), channel_id=1, source_target_pairs={{0,1},{1,0},{2,3},{3,2},{4,5},{5,4},{6,7},{7,6},{8,9},{9,8},{10,11... | collective-permute-start | bytes 983048 | tf_op jit(solution)/shard_map/ppermute | solution.py:460
  197.9 16.0 %collective-permute-start.44 = (bf16[1,256,1024]{2,1,0:T(8,128)(2,1)S(1)}, bf16[1,256,1024]{2,1,0:T(8,128)(2,1)S(1)}, u32[]{:S(2)}, u32[]{:S(2)}) collective-permute-start(bf16[1,256,1024]{2,1,0:T(8,128)(2,1)S(1)} %choose.9.refs_6_.refs_18_), channel_id=1, source_target_pairs={{0,2},{1,3},{2,0},{3,1},{4,6},{5,7},{6,4},{7,5},{8,10},{9,11},{10,... | collective-permute-start | bytes 1572872 | tf_op jit(solution)/shard_map/ppermute | solution.py:460
  203.2 21.5 %collective-permute-start.42 = (bf16[640,256]{1,0:T(8,128)(2,1)S(1)}, bf16[640,256]{1,0:T(8,128)(2,1)S(1)}, u32[]{:S(2)}, u32[]{:S(2)}) collective-permute-start(bf16[640,256]{1,0:T(8,128)(2,1)S(1)} %attend.3.refs_0_), channel_id=1, source_target_pairs={{0,1},{1,0},{2,3},{3,2},{4,5},{5,4},{6,7},{7,6},{8,9},{9,8},{10,11... | collective-permute-start | bytes 983048 | tf_op jit(solution)/shard_map/ppermute | solution.py:460
  207.8 23.6 %collective-permute-start.45 = (bf16[640,256]{1,0:T(8,128)(2,1)S(1)}, bf16[640,256]{1,0:T(8,128)(2,1)S(1)}, u32[]{:S(2)}, u32[]{:S(2)}) collective-permute-start(bf16[640,256]{1,0:T(8,128)(2,1)S(1)} %attend.3.refs_0_), channel_id=1, source_target_pairs={{0,4},{1,5},{2,6},{3,7},{4,0},{5,1},{6,2},{7,3},{8,12},{9,13},{10,... | collective-permute-start | bytes 983048 | tf_op jit(solution)/shard_map/ppermute | solution.py:460
  232.9 14.3 %collective-permute-start.47 = (bf16[2,1,256,512]{3,2,1,0:T(8,128)(2,1)S(1)}, bf16[2,1,256,512]{3,2,1,0:T(8,128)(2,1)S(1)}, u32[]{:S(2)}, u32[]{:S(2)}) collective-permute-start(bf16[2,1,256,512]{3,2,1,0:T(8,128)(2,1)S(1)} %get-tuple-element.161.refs_12_.refs_14_.refs_20_.refs_22_), channel_id=1, source_target_pairs={{0,2},{1,3},{2,0},{3,1},{4,6},{5,7},{6,4},{7,5},{8,10},{9,11},{10,... | collective-permute-start | bytes 1572872 | tf_op jit(solution)/shard_map/ppermute | solution.py:460
  233.3 14.0 %collective-permute-start.48 = (bf16[640,256]{1,0:T(8,128)(2,1)S(1)}, bf16[640,256]{1,0:T(8,128)(2,1)S(1)}, u32[]{:S(2)}, u32[]{:S(2)}) collective-permute-start(bf16[640,256]{1,0:T(8,128)(2,1)S(1)} %collective-permute-done.45.refs_2_), channel_id=1, source_target_pairs={{0,1},{1,0},{2,3},{3,2},{4,5},{5,4},{6,7},{7,6},{8,9},{9,8},{10,11... | collective-permute-start | bytes 983048 | tf_op jit(solution)/shard_map/ppermute | solution.py:460
  252.9 14.2 %collective-permute-start.50 = (bf16[2,1,256,512]{3,2,1,0:T(8,128)(2,1)S(1)}, bf16[2,1,256,512]{3,2,1,0:T(8,128)(2,1)S(1)}, u32[]{:S(2)}, u32[]{:S(2)}) collective-permute-start(bf16[2,1,256,512]{3,2,1,0:T(8,128)(2,1)S(1)} %get-tuple-element.166.refs_12_.refs_14_.refs_20_.refs_22_), channel_id=1, source_target_pairs={{0,2},{1,3},{2,0},{3,1},{4,6},{5,7},{6,4},{7,5},{8,10},{9,11},{10,... | collective-permute-start | bytes 1572872 | tf_op jit(solution)/shard_map/ppermute | solution.py:460
  255.2 9.8 %collective-permute-start.52 = (bf16[320,512]{1,0:T(8,128)(2,1)S(1)}, bf16[320,512]{1,0:T(8,128)(2,1)S(1)}, u32[]{:S(2)}, u32[]{:S(2)}) collective-permute-start(bf16[320,512]{1,0:T(8,128)(2,1)S(1)} %join.2), channel_id=1, source_target_pairs={{0,4},{1,5},{2,6},{3,7},{4,0},{5,1},{6,2},{7,3},{8,12},{9,13},{10,... | collective-permute-start | bytes 983048 | tf_op jit(solution)/shard_map/ppermute | solution.py:460
  271.4 9.8 %collective-permute-start.57 = (bf16[320,512]{1,0:T(8,128)(2,1)S(1)}, bf16[320,512]{1,0:T(8,128)(2,1)S(1)}, u32[]{:S(2)}, u32[]{:S(2)}) collective-permute-start(bf16[320,512]{1,0:T(8,128)(2,1)S(1)} %join.3), channel_id=1, source_target_pairs={{0,4},{1,5},{2,6},{3,7},{4,0},{5,1},{6,2},{7,3},{8,12},{9,13},{10,... | collective-permute-start | bytes 983048 | tf_op jit(solution)/shard_map/ppermute | solution.py:460
  273.2 9.6 %collective-permute-start.56 = (bf16[640,512]{1,0:T(8,128)(2,1)S(1)}, bf16[640,512]{1,0:T(8,128)(2,1)S(1)}, u32[]{:S(2)}, u32[]{:S(2)}) collective-permute-start(bf16[640,512]{1,0:T(8,128)(2,1)S(1)} %combine.9.refs_4_), channel_id=1, source_target_pairs={{0,16},{1,17},{2,18},{3,19},{4,20},{5,21},{6,22},{7,23},{8,24},{9,... | collective-permute-start | bytes 1966088 | tf_op jit(solution)/shard_map/ppermute | solution.py:460
  275.2 7.7 %collective-permute-start.54 = (bf16[640,512]{1,0:T(8,128)(2,1)S(1)}, bf16[640,512]{1,0:T(8,128)(2,1)S(1)}, u32[]{:S(2)}, u32[]{:S(2)}) collective-permute-start(bf16[640,512]{1,0:T(8,128)(2,1)S(1)} %combine.8.refs_0_), channel_id=1, source_target_pairs={{0,16},{1,17},{2,18},{3,19},{4,20},{5,21},{6,22},{7,23},{8,24},{9,... | collective-permute-start | bytes 1966088 | tf_op jit(solution)/shard_map/ppermute | solution.py:460
  (17 other events, 198.6 us)

commit v16 on v15

--- a/solution.py
+++ b/solution.py
@@ -601,7 +601,7 @@
         attended_b = attend(here, own_kind, other_kind, ours_b, got_b)
         held_b = over_tensor(attended_b)
 
-        passed_b = move(attended_b, edge)
+        passed_b = move(attended_b, edge, o23o)
         begun = (m24o, o23o, held_b[1], held_a[-1], p2o, passed_b)
         late_o = choose_halves(here, after(o23o, *begun), m24o)
         held_b += over_tensor(after(passed_b, late_o[0]))

time: 286 us -> 279 us (0.976)
  starting transfers between devices: 72.8 us -> 67.5 us
    ppermute x59, starting transfers between devices: 72.8 us -> 67.5 us  [move(): lax.ppermute(after(array, *earlier) if earlier else array, AXES, pairs)]
  transfers between devices with their start and end apart: 59 -> 59, of which waited for: 31 -> 29; matrix products, arithmetic and copies ran while one was open for 0% -> 0% of each run, Pallas kernels for 18% -> 19%
where the time goes in v16:
time: 279 us; the launch traced here: 278 us
  waiting for transfers between devices  142 us (51%)
  starting transfers between devices  67.5 us (24%)
  Pallas kernels  63.6 us (23%)
  local copies, waits for them, and re-layouts  4.34 us (2%)
    ppermute x59, waiting for transfers between devices, move(): lax.ppermute(after(array, *earlier) if earlier else array, AXES, pairs)  142 us
    ppermute x59, starting transfers between devices, move(): lax.ppermute(after(array, *earlier) if earlier else array, AXES, pairs)  67.5 us
    pallas_call x39, Pallas kernels, call(): pl.pallas_call(kernel, in_specs=[pl.BlockSpec(memory_space=SMEM)] + [pl.B...  61.3 us
  transfers between devices with their start and end apart: 59, of which 29 were waited for; matrix products, arithmetic and copies ran while one was open for 0% of the time, Pallas kernels for 19%

profile of v16, /device:TPU:0, one launch (start us, length us, event | category | flops | bytes accessed | tf_op | source)
XLA Modules:
  0.0 278.3 jit_solution(610164494571657154)
XLA Ops:
  0.8 1.9 copy-done
  3.5 3.0 %collective-permute-start.2 = (bf16[3,512,256]{2,1,0:T(8,128)(2,1)S(1)}, bf16[3,512,256]{2,1,0:T(8,128)(2,1)S(1)}, u32[]{:S(2)}, u32[]{:S(2)}) collective-permute-start(bf16[3,512,256]{2,1,0:T(8,128)(2,1)S(1)} %get-tuple-element.96.refs_1_), channel_id=1, source_target_pairs={{0,2},{1,3},{2,0},{3,1},{4,6},{5,7},{6,4},{7,5},{8,10},{9,11},{10,... | collective-permute-start | bytes 2359304 | tf_op jit(solution)/shard_map/ppermute | solution.py:460
  8.8 15.3 %collective-permute-done.2.refs_2_ = bf16[3,512,256]{2,1,0:T(8,128)(2,1)S(1)} collective-permute-done((bf16[3,512,256]{2,1,0:T(8,128)(2,1)S(1)}, bf16[3,512,256]{2,1,0:T(8,128)(2,1)S(1)}, u32[]{:S(2)}, u32[]{:S(2)}) %collective-permute-start.2) | collective-permute-done | bytes 786464 | tf_op jit(solution)/shard_map/ppermute | solution.py:460
  26.6 7.7 %collective-permute-start.3 = (bf16[3,512,256]{2,1,0:T(8,128)(2,1)S(1)}, bf16[3,512,256]{2,1,0:T(8,128)(2,1)S(1)}, u32[]{:S(2)}, u32[]{:S(2)}) collective-permute-start(bf16[3,512,256]{2,1,0:T(8,128)(2,1)S(1)} %collective-permute-done), channel_id=1, source_target_pairs={{0,4},{1,5},{2,6},{3,7},{4,0},{5,1},{6,2},{7,3},{8,12},{9,13},{10,... | collective-permute-start | bytes 2359304 | tf_op jit(solution)/shard_map/ppermute | solution.py:460
  34.3 1.7 copy-done.2
  39.2 5.2 %collective-permute-done.4.refs_4_ = bf16[3,512,256]{2,1,0:T(8,128)(2,1)S(1)} collective-permute-done((bf16[3,512,256]{2,1,0:T(8,128)(2,1)S(1)}, bf16[3,512,256]{2,1,0:T(8,128)(2,1)S(1)}, u32[]{:S(2)}, u32[]{:S(2)}) %collective-permute-start.4) | collective-permute-done | bytes 786464 | tf_op jit(solution)/shard_map/ppermute | solution.py:460
  44.4 5.4 %collective-permute-done.3.a_ref = bf16[3,512,256]{2,1,0:T(8,128)(2,1)S(1)} collective-permute-done((bf16[3,512,256]{2,1,0:T(8,128)(2,1)S(1)}, bf16[3,512,256]{2,1,0:T(8,128)(2,1)S(1)}, u32[]{:S(2)}, u32[]{:S(2)}) %collective-permute-start.3) | collective-permute-done | bytes 786464 | tf_op jit(solution)/shard_map/ppermute | solution.py:460
  52.7 3.5 %collective-permute-start.6 = (bf16[160,2048]{1,0:T(8,128)(2,1)S(1)}, bf16[160,2048]{1,0:T(8,128)(2,1)S(1)}, u32[]{:S(2)}, u32[]{:S(2)}) collective-permute-start(bf16[160,2048]{1,0:T(8,128)(2,1)S(1)} %get-tuple-element.103), channel_id=1, source_target_pairs={{0,4},{1,5},{2,6},{3,7},{4,0},{5,1},{6,2},{7,3},{8,12},{9,13},{10,... | collective-permute-start | bytes 1966088 | tf_op jit(solution)/shard_map/ppermute | solution.py:460
  56.2 8.8 %collective-permute-done.10.refs_2_ = bf16[320,2048]{1,0:T(8,128)(2,1)S(1)} collective-permute-done((bf16[320,2048]{1,0:T(8,128)(2,1)S(1)}, bf16[320,2048]{1,0:T(8,128)(2,1)S(1)}, u32[]{:S(2)}, u32[]{:S(2)}) %collective-permute-start.10) | collective-permute-done | bytes 1310752 | tf_op jit(solution)/shard_map/ppermute | solution.py:460
  65.1 2.7 collective-permute-done.6.refs_2_
  67.8 3.3 %collective-permute-start.9 = (bf16[176,2048]{1,0:T(8,128)(2,1)S(1)}, bf16[176,2048]{1,0:T(8,128)(2,1)S(1)}, u32[]{:S(2)}, u32[]{:S(2)}) collective-permute-start(bf16[176,2048]{1,0:T(8,128)(2,1)S(1)} %get-tuple-element.107), channel_id=1, source_target_pairs={{0,4},{1,5},{2,6},{3,7},{4,0},{5,1},{6,2},{7,3},{8,12},{9,13},{10,... | collective-permute-start | bytes 2162696 | tf_op jit(solution)/shard_map/ppermute | solution.py:460
  76.3 3.2 %normalize.3.refs_0_ = bf16[2,8,640,512]{3,2,1,0:T(8,128)(2,1)S(1)} custom-call(s32[3]{0:T(128)S(1)} %pad_add_fusion.h_ref._, f32[8,1,512]{2,1,0:T(1,128)S(1)} %bitcast.9, bf16[640,2048]{1,0:T(8,128)(2,1)S(1)} %copy-done.3, bf16[320,2048]{1,0:T(8,128)(2,1)S(1)} %collective-permute-done.10.refs_2_, bf16[320,2048]{1,0:T(8,128)(2,1)S(1)} %collective-permute-done.11.refs_3_), custom_call_target="tpu_custom_call" | custom-call | tf_op jit(solution)/shard_map/normalize/pallas_call | solution.py:32
  79.5 7.2 %collective-permute-done.12.refs_3_ = bf16[160,2048]{1,0:T(8,128)(2,1)S(1)} collective-permute-done((bf16[160,2048]{1,0:T(8,128)(2,1)S(1)}, bf16[160,2048]{1,0:T(8,128)(2,1)S(1)}, u32[]{:S(2)}, u32[]{:S(2)}) %collective-permute-start.12) | collective-permute-done | bytes 655392 | tf_op jit(solution)/shard_map/ppermute | solution.py:460
  87.9 2.8 %collective-permute-done.22.refs_2_ = bf16[3,512,256]{2,1,0:T(8,128)(2,1)S(1)} collective-permute-done((bf16[3,512,256]{2,1,0:T(8,128)(2,1)S(1)}, bf16[3,512,256]{2,1,0:T(8,128)(2,1)S(1)}, u32[]{:S(2)}, u32[]{:S(2)}) %collective-permute-start.22) | collective-permute-done | bytes 786464 | tf_op jit(solution)/shard_map/ppermute | solution.py:460
  94.1 4.6 %collective-permute-start.25 = (bf16[1,256,1024]{2,1,0:T(8,128)(2,1)S(1)}, bf16[1,256,1024]{2,1,0:T(8,128)(2,1)S(1)}, u32[]{:S(2)}, u32[]{:S(2)}) collective-permute-start(bf16[1,256,1024]{2,1,0:T(8,128)(2,1)S(1)} %get-tuple-element.148.refs_0_.block_ref), channel_id=1, source_target_pairs={{0,4},{1,5},{2,6},{3,7},{12,8},{13,9},{14,10},{15,11},{16,20},{17,... | collective-permute-start | bytes 1572872 | tf_op jit(solution)/shard_map/ppermute | solution.py:460
  99.2 3.7 %project.10.refs_7_ = f32[2,640,768]{2,1,0:T(8,128)S(1)} custom-call(s32[3]{0:T(128)S(1)} %pad_add_fusion.h_ref._, bf16[2,8,640,512]{3,2,1,0:T(8,128)(2,1)S(1)} %normalize.3.refs_0_, bf16[3,512,256]{2,1,0:T(8,128)(2,1)S(1)} %get-tuple-element.96.refs_1_, bf16[3,512,256]{2,1,0:T(8,128)(2,1)S(1)} %collective-permute-done.2.refs_2_, ...), custom_call_target="tpu_custom_call" | custom-call | tf_op jit(solution)/shard_map/project/pallas_call | solution.py:32
  103.0 1.8 normalize.4.refs_0_
  105.5 4.8 %collective-permute-done.21.a_ref = bf16[3,512,256]{2,1,0:T(8,128)(2,1)S(1)} collective-permute-done((bf16[3,512,256]{2,1,0:T(8,128)(2,1)S(1)}, bf16[3,512,256]{2,1,0:T(8,128)(2,1)S(1)}, u32[]{:S(2)}, u32[]{:S(2)}) %collective-permute-start.21) | collective-permute-done | bytes 786464 | tf_op jit(solution)/shard_map/ppermute | solution.py:460
  110.4 3.5 %collective-permute-start.26 = (bf16[3,512,256]{2,1,0:T(8,128)(2,1)S(1)}, bf16[3,512,256]{2,1,0:T(8,128)(2,1)S(1)}, u32[]{:S(2)}, u32[]{:S(2)}) collective-permute-start(bf16[3,512,256]{2,1,0:T(8,128)(2,1)S(1)} %collective-permute-done.17), channel_id=1, source_target_pairs={{0,4},{1,5},{2,6},{3,7},{4,0},{5,1},{6,2},{7,3},{8,12},{9,13},{10,... | collective-permute-start | bytes 2359304 | tf_op jit(solution)/shard_map/ppermute | solution.py:460
  118.5 1.8 normalize.5.refs_0_
  120.3 3.7 %project.11.refs_3_ = f32[2,640,768]{2,1,0:T(8,128)S(1)} custom-call(s32[3]{0:T(128)S(1)} %pad_add_fusion.h_ref._, bf16[2,8,640,512]{3,2,1,0:T(8,128)(2,1)S(1)} %normalize.5.refs_0_, bf16[3,512,256]{2,1,0:T(8,128)(2,1)S(1)} %get-tuple-element.96.refs_1_, bf16[3,512,256]{2,1,0:T(8,128)(2,1)S(1)} %collective-permute-done.2.refs_2_, ...), custom_call_target="tpu_custom_call", output_to_operand_aliasing={{}: (8, {})} | custom-call | tf_op jit(solution)/shard_map/project/pallas_call | solution.py:32
  124.0 6.7 %collective-permute-done.26.a_ref = bf16[3,512,256]{2,1,0:T(8,128)(2,1)S(1)} collective-permute-done((bf16[3,512,256]{2,1,0:T(8,128)(2,1)S(1)}, bf16[3,512,256]{2,1,0:T(8,128)(2,1)S(1)}, u32[]{:S(2)}, u32[]{:S(2)}) %collective-permute-start.26) | collective-permute-done | bytes 786464 | tf_op jit(solution)/shard_map/ppermute | solution.py:460
  130.7 2.1 collective-permute-done.24.refs_2_
  138.5 11.7 %collective-permute-done.29.refs_1_ = bf16[3,512,256]{2,1,0:T(8,128)(2,1)S(1)} collective-permute-done((bf16[3,512,256]{2,1,0:T(8,128)(2,1)S(1)}, bf16[3,512,256]{2,1,0:T(8,128)(2,1)S(1)}, u32[]{:S(2)}, u32[]{:S(2)}) %collective-permute-start.29) | collective-permute-done | bytes 786464 | tf_op jit(solution)/shard_map/ppermute | solution.py:460
  153.5 7.1 %collective-permute-start.32 = (bf16[1,256,1024]{2,1,0:T(8,128)(2,1)S(1)}, bf16[1,256,1024]{2,1,0:T(8,128)(2,1)S(1)}, u32[]{:S(2)}, u32[]{:S(2)}) collective-permute-start(bf16[1,256,1024]{2,1,0:T(8,128)(2,1)S(1)} %get-tuple-element.151.refs_0_), channel_id=1, source_target_pairs={{0,4},{1,5},{2,6},{3,7},{12,8},{13,9},{14,10},{15,11},{16,20},{17,... | collective-permute-start | bytes 1572872 | tf_op jit(solution)/shard_map/ppermute | solution.py:460
  161.2 2.7 project.14.refs_5_
  164.0 2.7 project.15.refs_3_
  166.7 4.2 %attend.2.piece_ref.refs_0_ = bf16[640,256]{1,0:T(8,128)(2,1)S(1)} custom-call(s32[3]{0:T(128)S(1)} %pad_add_fusion.h_ref._, s32[1,640]{1,0:T(1,128)S(1)} %broadcast_in_dim.3.kind_ref.own_kind_ref, s32[1,640]{1,0:T(1,128)S(1)} %kinds_behind.1.other_kind_ref.kind_ref, bf16[640,768]{1,0:T(8,128)(2,1)S(1)} %project.12.own_ref, ...), custom_call_target="tpu_custom_call" | custom-call | tf_op jit(solution)/shard_map/attend/pallas_call | solution.py:32
  172.6 3.1 %collective-permute-start.36 = (bf16[1664,256]{1,0:T(8,128)(2,1)S(1)}, bf16[1664,256]{1,0:T(8,128)(2,1)S(1)}, u32[]{:S(2)}, u32[]{:S(2)}) collective-permute-start(bf16[1664,256]{1,0:T(8,128)(2,1)S(1)} %pack.1), channel_id=1, source_target_pairs={{0,4},{1,5},{2,6},{3,7},{4,0},{5,1},{6,2},{7,3},{8,12},{9,13},{10,... | collective-permute-start | bytes 2555912 | tf_op jit(solution)/shard_map/ppermute | solution.py:460
  178.3 1.9 project.16.refs_3_
  180.3 1.9 project.17.refs_3_
  183.5 7.1 %collective-permute-done.36.in_ref = bf16[1664,256]{1,0:T(8,128)(2,1)S(1)} collective-permute-done((bf16[1664,256]{1,0:T(8,128)(2,1)S(1)}, bf16[1664,256]{1,0:T(8,128)(2,1)S(1)}, u32[]{:S(2)}, u32[]{:S(2)}) %collective-permute-start.36) | collective-permute-done | bytes 852000 | tf_op jit(solution)/shard_map/ppermute | solution.py:460
  191.9 1.7 project.19
  198.9 4.1 %attend.3.refs_0_ = bf16[640,256]{1,0:T(8,128)(2,1)S(1)} custom-call(s32[3]{0:T(128)S(1)} %pad_add_fusion.h_ref._, s32[1,640]{1,0:T(1,128)S(1)} %broadcast_in_dim.3.kind_ref.own_kind_ref, s32[1,640]{1,0:T(1,128)S(1)} %kinds_behind.1.other_kind_ref.kind_ref, bf16[640,768]{1,0:T(8,128)(2,1)S(1)} %project.18.own_ref, ...), custom_call_target="tpu_custom_call" | custom-call | tf_op jit(solution)/shard_map/attend/pallas_call | solution.py:32
  204.0 13.2 %collective-permute-done.38.a_ref = bf16[2,1,256,1024]{3,2,1,0:T(8,128)(2,1)S(1)} collective-permute-done((bf16[2,1,256,1024]{3,2,1,0:T(8,128)(2,1)S(1)}, bf16[2,1,256,1024]{3,2,1,0:T(8,128)(2,1)S(1)}, u32[]{:S(2)}, u32[]{:S(2)}) %collective-permute-start.38) | collective-permute-done | bytes 1048608 | tf_op jit(solution)/shard_map/ppermute | solution.py:460
  217.3 7.0 %collective-permute-done.45.refs_2_ = bf16[640,256]{1,0:T(8,128)(2,1)S(1)} collective-permute-done((bf16[640,256]{1,0:T(8,128)(2,1)S(1)}, bf16[640,256]{1,0:T(8,128)(2,1)S(1)}, u32[]{:S(2)}, u32[]{:S(2)}) %collective-permute-start.45) | collective-permute-done | bytes 327712 | tf_op jit(solution)/shard_map/ppermute | solution.py:460
  226.1 2.8 %collective-permute-done.46.refs_1_.refs_3_ = bf16[4,640,256]{2,1,0:T(8,128)(2,1)S(1)} collective-permute-done((bf16[4,640,256]{2,1,0:T(8,128)(2,1)S(1)}, bf16[4,640,256]{2,1,0:T(8,128)(2,1)S(1)}, u32[]{:S(2)}, u32[]{:S(2)}) %collective-permute-start.46) | collective-permute-done | bytes 1310752 | tf_op jit(solution)/shard_map/ppermute | solution.py:460
  228.9 2.1 combine.5.refs_24_
  231.0 9.2 %collective-permute-done.47.refs_13_.refs_15_.refs_21_.refs_23_ = bf16[2,1,256,512]{3,2,1,0:T(8,128)(2,1)S(1)} collective-permute-done((bf16[2,1,256,512]{3,2,1,0:T(8,128)(2,1)S(1)}, bf16[2,1,256,512]{3,2,1,0:T(8,128)(2,1)S(1)}, u32[]{:S(2)}, u32[]{:S(2)}) %collective-permute-start.47) | collective-permute-done | bytes 524320 | tf_op jit(solution)/shard_map/ppermute | solution.py:460
  240.9 3.0 %collective-permute-done.49.refs_5_.refs_7_.refs_9_.refs_11_ = bf16[4,640,256]{2,1,0:T(8,128)(2,1)S(1)} collective-permute-done((bf16[4,640,256]{2,1,0:T(8,128)(2,1)S(1)}, bf16[4,640,256]{2,1,0:T(8,128)(2,1)S(1)}, u32[]{:S(2)}, u32[]{:S(2)}) %collective-permute-start.49) | collective-permute-done | bytes 1310752 | tf_op jit(solution)/shard_map/ppermute | solution.py:460
  243.9 1.7 combine.6
  249.2 8.8 %collective-permute-done.52.refs_2_ = bf16[320,512]{1,0:T(8,128)(2,1)S(1)} collective-permute-done((bf16[320,512]{1,0:T(8,128)(2,1)S(1)}, bf16[320,512]{1,0:T(8,128)(2,1)S(1)}, u32[]{:S(2)}, u32[]{:S(2)}) %collective-permute-start.52) | collective-permute-done | bytes 327712 | tf_op jit(solution)/shard_map/ppermute | solution.py:460
  258.0 2.1 collective-permute-done.50.refs_13_.refs_15_.refs_21_.refs_23_
  260.1 1.7 combine.7
  265.4 1.7 combine.9.refs_4_
  267.2 1.7 combine.8.refs_0_
  269.6 4.6 %collective-permute-done.57.refs_6_ = bf16[320,512]{1,0:T(8,128)(2,1)S(1)} collective-permute-done((bf16[320,512]{1,0:T(8,128)(2,1)S(1)}, bf16[320,512]{1,0:T(8,128)(2,1)S(1)}, u32[]{:S(2)}, u32[]{:S(2)}) %collective-permute-start.57) | collective-permute-done | bytes 327712 | tf_op jit(solution)/shard_map/ppermute | solution.py:460
  275.8 2.4 assemble.1
  (124 shorter events, 62.6 us)
Async XLA Ops:
  3.5 20.6 %collective-permute-start.2 = (bf16[3,512,256]{2,1,0:T(8,128)(2,1)S(1)}, bf16[3,512,256]{2,1,0:T(8,128)(2,1)S(1)}, u32[]{:S(2)}, u32[]{:S(2)}) collective-permute-start(bf16[3,512,256]{2,1,0:T(8,128)(2,1)S(1)} %get-tuple-element.96.refs_1_), channel_id=1, source_target_pairs={{0,2},{1,3},{2,0},{3,1},{4,6},{5,7},{6,4},{7,5},{8,10},{9,11},{10,... | collective-permute-start | bytes 2359304 | tf_op jit(solution)/shard_map/ppermute | solution.py:460
  6.5 19.0 %collective-permute-start.1 = (bf16[3,512,256]{2,1,0:T(8,128)(2,1)S(1)}, bf16[3,512,256]{2,1,0:T(8,128)(2,1)S(1)}, u32[]{:S(2)}, u32[]{:S(2)}) collective-permute-start(bf16[3,512,256]{2,1,0:T(8,128)(2,1)S(1)} %get-tuple-element.95), channel_id=1, source_target_pairs={{0,4},{1,5},{2,6},{3,7},{4,0},{5,1},{6,2},{7,3},{8,12},{9,13},{10,... | collective-permute-start | bytes 2359304 | tf_op jit(solution)/shard_map/ppermute | solution.py:460
  8.1 17.4 %collective-permute-start = (bf16[3,512,256]{2,1,0:T(8,128)(2,1)S(1)}, bf16[3,512,256]{2,1,0:T(8,128)(2,1)S(1)}, u32[]{:S(2)}, u32[]{:S(2)}) collective-permute-start(bf16[3,512,256]{2,1,0:T(8,128)(2,1)S(1)} %get-tuple-element.91), channel_id=1, source_target_pairs={{0,0},{1,1},{2,2},{3,3},{4,8},{5,9},{6,10},{7,11},{8,4},{9,5},{10,... | collective-permute-start | bytes 2359304 | tf_op jit(solution)/shard_map/ppermute | solution.py:460
  25.5 13.7 %collective-permute-start.5 = (bf16[3,512,256]{2,1,0:T(8,128)(2,1)S(1)}, bf16[3,512,256]{2,1,0:T(8,128)(2,1)S(1)}, u32[]{:S(2)}, u32[]{:S(2)}) collective-permute-start(bf16[3,512,256]{2,1,0:T(8,128)(2,1)S(1)} %get-tuple-element.100), channel_id=1, source_target_pairs={{4,8},{5,9},{6,10},{7,11},{8,4},{9,5},{10,6},{11,7},{20,24},{21,25... | collective-permute-start | bytes 2359304 | tf_op jit(solution)/shard_map/ppermute | solution.py:460
  26.2 18.2 %collective-permute-start.4 = (bf16[3,512,256]{2,1,0:T(8,128)(2,1)S(1)}, bf16[3,512,256]{2,1,0:T(8,128)(2,1)S(1)}, u32[]{:S(2)}, u32[]{:S(2)}) collective-permute-start(bf16[3,512,256]{2,1,0:T(8,128)(2,1)S(1)} %collective-permute-done.1.refs_3_), channel_id=1, source_target_pairs={{0,2},{1,3},{2,0},{3,1},{4,6},{5,7},{6,4},{7,5},{8,10},{9,11},{10,... | collective-permute-start | bytes 2359304 | tf_op jit(solution)/shard_map/ppermute | solution.py:460
  26.6 23.2 %collective-permute-start.3 = (bf16[3,512,256]{2,1,0:T(8,128)(2,1)S(1)}, bf16[3,512,256]{2,1,0:T(8,128)(2,1)S(1)}, u32[]{:S(2)}, u32[]{:S(2)}) collective-permute-start(bf16[3,512,256]{2,1,0:T(8,128)(2,1)S(1)} %collective-permute-done), channel_id=1, source_target_pairs={{0,4},{1,5},{2,6},{3,7},{4,0},{5,1},{6,2},{7,3},{8,12},{9,13},{10,... | collective-permute-start | bytes 2359304 | tf_op jit(solution)/shard_map/ppermute | solution.py:460
  36.8 28.3 %collective-permute-start.10 = (bf16[320,2048]{1,0:T(8,128)(2,1)S(1)}, bf16[320,2048]{1,0:T(8,128)(2,1)S(1)}, u32[]{:S(2)}, u32[]{:S(2)}) collective-permute-start(bf16[320,2048]{1,0:T(8,128)(2,1)S(1)} %get-tuple-element.109), channel_id=1, source_target_pairs={{0,1},{1,0},{2,3},{3,2},{4,5},{5,4},{6,7},{7,6},{8,9},{9,8},{10,11... | collective-permute-start | bytes 3932168 | tf_op jit(solution)/shard_map/ppermute | solution.py:460
  49.8 15.3 %collective-permute-start.8 = (bf16[3,512,256]{2,1,0:T(8,128)(2,1)S(1)}, bf16[3,512,256]{2,1,0:T(8,128)(2,1)S(1)}, u32[]{:S(2)}, u32[]{:S(2)}) collective-permute-start(bf16[3,512,256]{2,1,0:T(8,128)(2,1)S(1)} %collective-permute-done.3.a_ref), channel_id=1, source_target_pairs={{4,8},{5,9},{6,10},{7,11},{8,4},{9,5},{10,6},{11,7},{20,24},{21,25... | collective-permute-start | bytes 2359304 | tf_op jit(solution)/shard_map/ppermute | solution.py:460
  51.1 16.7 %collective-permute-start.7 = (bf16[3,512,256]{2,1,0:T(8,128)(2,1)S(1)}, bf16[3,512,256]{2,1,0:T(8,128)(2,1)S(1)}, u32[]{:S(2)}, u32[]{:S(2)}) collective-permute-start(bf16[3,512,256]{2,1,0:T(8,128)(2,1)S(1)} %choose.5.refs_5_), channel_id=1, source_target_pairs={{0,2},{1,3},{2,0},{3,1},{4,6},{5,7},{6,4},{7,5},{8,10},{9,11},{10,... | collective-permute-start | bytes 2359304 | tf_op jit(solution)/shard_map/ppermute | solution.py:460
  52.7 15.0 %collective-permute-start.6 = (bf16[160,2048]{1,0:T(8,128)(2,1)S(1)}, bf16[160,2048]{1,0:T(8,128)(2,1)S(1)}, u32[]{:S(2)}, u32[]{:S(2)}) collective-permute-start(bf16[160,2048]{1,0:T(8,128)(2,1)S(1)} %get-tuple-element.103), channel_id=1, source_target_pairs={{0,4},{1,5},{2,6},{3,7},{4,0},{5,1},{6,2},{7,3},{8,12},{9,13},{10,... | collective-permute-start | bytes 1966088 | tf_op jit(solution)/shard_map/ppermute | solution.py:460
  65.1 11.2 %collective-permute-start.11 = (bf16[320,2048]{1,0:T(8,128)(2,1)S(1)}, bf16[320,2048]{1,0:T(8,128)(2,1)S(1)}, u32[]{:S(2)}, u32[]{:S(2)}) collective-permute-start(bf16[320,2048]{1,0:T(8,128)(2,1)S(1)} %collective-permute-done.10.refs_2_), channel_id=1, source_target_pairs={{0,16},{1,17},{2,18},{3,19},{4,20},{5,21},{6,22},{7,23},{8,24},{9,... | collective-permute-start | bytes 3932168 | tf_op jit(solution)/shard_map/ppermute | solution.py:460
  67.8 18.9 %collective-permute-start.9 = (bf16[176,2048]{1,0:T(8,128)(2,1)S(1)}, bf16[176,2048]{1,0:T(8,128)(2,1)S(1)}, u32[]{:S(2)}, u32[]{:S(2)}) collective-permute-start(bf16[176,2048]{1,0:T(8,128)(2,1)S(1)} %get-tuple-element.107), channel_id=1, source_target_pairs={{0,4},{1,5},{2,6},{3,7},{4,0},{5,1},{6,2},{7,3},{8,12},{9,13},{10,... | collective-permute-start | bytes 2162696 | tf_op jit(solution)/shard_map/ppermute | solution.py:460
  71.1 15.6 %collective-permute-start.12 = (bf16[160,2048]{1,0:T(8,128)(2,1)S(1)}, bf16[160,2048]{1,0:T(8,128)(2,1)S(1)}, u32[]{:S(2)}, u32[]{:S(2)}) collective-permute-start(bf16[160,2048]{1,0:T(8,128)(2,1)S(1)} %collective-permute-done.6.refs_2_), channel_id=1, source_target_pairs={{0,1},{1,0},{2,3},{3,2},{4,5},{5,4},{6,7},{7,6},{8,9},{9,8},{10,11... | collective-permute-start | bytes 1966088 | tf_op jit(solution)/shard_map/ppermute | solution.py:460
  72.6 18.1 %collective-permute-start.22 = (bf16[3,512,256]{2,1,0:T(8,128)(2,1)S(1)}, bf16[3,512,256]{2,1,0:T(8,128)(2,1)S(1)}, u32[]{:S(2)}, u32[]{:S(2)}) collective-permute-start(bf16[3,512,256]{2,1,0:T(8,128)(2,1)S(1)} %get-tuple-element.128.refs_1_), channel_id=1, source_target_pairs={{0,2},{1,3},{2,0},{3,1},{4,6},{5,7},{6,4},{7,5},{8,10},{9,11},{10,... | collective-permute-start | bytes 2359304 | tf_op jit(solution)/shard_map/ppermute | solution.py:460
  74.1 17.9 %collective-permute-start.16 = (bf16[3,512,256]{2,1,0:T(8,128)(2,1)S(1)}, bf16[3,512,256]{2,1,0:T(8,128)(2,1)S(1)}, u32[]{:S(2)}, u32[]{:S(2)}) collective-permute-start(bf16[3,512,256]{2,1,0:T(8,128)(2,1)S(1)} %collective-permute-done.1.refs_3_), channel_id=1, source_target_pairs={{4,8},{5,9},{6,10},{7,11},{8,4},{9,5},{10,6},{11,7},{20,24},{21,25... | collective-permute-start | bytes 2359304 | tf_op jit(solution)/shard_map/ppermute | solution.py:460
  86.7 7.4 %collective-permute-start.13 = (bf16[160,2048]{1,0:T(8,128)(2,1)S(1)}, bf16[160,2048]{1,0:T(8,128)(2,1)S(1)}, u32[]{:S(2)}, u32[]{:S(2)}) collective-permute-start(bf16[160,2048]{1,0:T(8,128)(2,1)S(1)} %collective-permute-done.6.refs_2_), channel_id=1, source_target_pairs={{0,16},{1,17},{2,18},{3,19},{4,20},{5,21},{6,22},{7,23},{8,24},{9,... | collective-permute-start | bytes 1966088 | tf_op jit(solution)/shard_map/ppermute | solution.py:460
  87.2 17.6 %collective-permute-start.17 = (bf16[3,512,256]{2,1,0:T(8,128)(2,1)S(1)}, bf16[3,512,256]{2,1,0:T(8,128)(2,1)S(1)}, u32[]{:S(2)}, u32[]{:S(2)}) collective-permute-start(bf16[3,512,256]{2,1,0:T(8,128)(2,1)S(1)} %get-tuple-element.119), channel_id=1, source_target_pairs={{0,0},{1,1},{2,2},{3,3},{4,8},{5,9},{6,10},{7,11},{8,4},{9,5},{10,... | collective-permute-start | bytes 2359304 | tf_op jit(solution)/shard_map/ppermute | solution.py:460
  90.7 19.7 %collective-permute-start.21 = (bf16[3,512,256]{2,1,0:T(8,128)(2,1)S(1)}, bf16[3,512,256]{2,1,0:T(8,128)(2,1)S(1)}, u32[]{:S(2)}, u32[]{:S(2)}) collective-permute-start(bf16[3,512,256]{2,1,0:T(8,128)(2,1)S(1)} %collective-permute-done.8), channel_id=1, source_target_pairs={{4,0},{5,1},{6,2},{7,3},{8,12},{9,13},{10,14},{11,15},{20,16},{21,... | collective-permute-start | bytes 2359304 | tf_op jit(solution)/shard_map/ppermute | solution.py:460
  92.0 18.4 %collective-permute-start.15 = (bf16[176,2048]{1,0:T(8,128)(2,1)S(1)}, bf16[176,2048]{1,0:T(8,128)(2,1)S(1)}, u32[]{:S(2)}, u32[]{:S(2)}) collective-permute-start(bf16[176,2048]{1,0:T(8,128)(2,1)S(1)} %collective-permute-done.9.in_ref.refs_2_), channel_id=1, source_target_pairs={{0,1},{1,0},{2,3},{3,2},{4,5},{5,4},{6,7},{7,6},{8,9},{9,8},{10,11... | collective-permute-start | bytes 2162696 | tf_op jit(solution)/shard_map/ppermute | solution.py:460
  92.6 17.8 %collective-permute-start.23 = (bf16[1,256,1024]{2,1,0:T(8,128)(2,1)S(1)}, bf16[1,256,1024]{2,1,0:T(8,128)(2,1)S(1)}, u32[]{:S(2)}, u32[]{:S(2)}) collective-permute-start(bf16[1,256,1024]{2,1,0:T(8,128)(2,1)S(1)} %get-tuple-element.129.refs_4_.refs_16_), channel_id=1, source_target_pairs={{0,2},{1,3},{2,0},{3,1},{4,6},{5,7},{6,4},{7,5},{8,10},{9,11},{10,... | collective-permute-start | bytes 1572872 | tf_op jit(solution)/shard_map/ppermute | solution.py:460
  94.1 16.3 %collective-permute-start.25 = (bf16[1,256,1024]{2,1,0:T(8,128)(2,1)S(1)}, bf16[1,256,1024]{2,1,0:T(8,128)(2,1)S(1)}, u32[]{:S(2)}, u32[]{:S(2)}) collective-permute-start(bf16[1,256,1024]{2,1,0:T(8,128)(2,1)S(1)} %get-tuple-element.148.refs_0_.block_ref), channel_id=1, source_target_pairs={{0,4},{1,5},{2,6},{3,7},{12,8},{13,9},{14,10},{15,11},{16,20},{17,... | collective-permute-start | bytes 1572872 | tf_op jit(solution)/shard_map/ppermute | solution.py:460
  104.8 19.2 %collective-permute-start.20 = (bf16[3,512,256]{2,1,0:T(8,128)(2,1)S(1)}, bf16[3,512,256]{2,1,0:T(8,128)(2,1)S(1)}, u32[]{:S(2)}, u32[]{:S(2)}) collective-permute-start(bf16[3,512,256]{2,1,0:T(8,128)(2,1)S(1)} %get-tuple-element.124), channel_id=1, source_target_pairs={{4,8},{5,9},{6,10},{7,11},{8,4},{9,5},{10,6},{11,7},{20,24},{21,25... | collective-permute-start | bytes 2359304 | tf_op jit(solution)/shard_map/ppermute | solution.py:460
  110.4 20.3 %collective-permute-start.26 = (bf16[3,512,256]{2,1,0:T(8,128)(2,1)S(1)}, bf16[3,512,256]{2,1,0:T(8,128)(2,1)S(1)}, u32[]{:S(2)}, u32[]{:S(2)}) collective-permute-start(bf16[3,512,256]{2,1,0:T(8,128)(2,1)S(1)} %collective-permute-done.17), channel_id=1, source_target_pairs={{0,4},{1,5},{2,6},{3,7},{4,0},{5,1},{6,2},{7,3},{8,12},{9,13},{10,... | collective-permute-start | bytes 2359304 | tf_op jit(solution)/shard_map/ppermute | solution.py:460
  114.5 18.4 %collective-permute-start.24 = (bf16[3,512,256]{2,1,0:T(8,128)(2,1)S(1)}, bf16[3,512,256]{2,1,0:T(8,128)(2,1)S(1)}, u32[]{:S(2)}, u32[]{:S(2)}) collective-permute-start(bf16[3,512,256]{2,1,0:T(8,128)(2,1)S(1)} %choose.6.refs_1_), channel_id=1, source_target_pairs={{0,2},{1,3},{2,0},{3,1},{4,6},{5,7},{6,4},{7,5},{8,10},{9,11},{10,... | collective-permute-start | bytes 2359304 | tf_op jit(solution)/shard_map/ppermute | solution.py:460
  132.8 17.4 %collective-permute-start.29 = (bf16[3,512,256]{2,1,0:T(8,128)(2,1)S(1)}, bf16[3,512,256]{2,1,0:T(8,128)(2,1)S(1)}, u32[]{:S(2)}, u32[]{:S(2)}) collective-permute-start(bf16[3,512,256]{2,1,0:T(8,128)(2,1)S(1)} %get-tuple-element.137), channel_id=1, source_target_pairs={{0,4},{1,5},{2,6},{3,7},{4,0},{5,1},{6,2},{7,3},{8,12},{9,13},{10,... | collective-permute-start | bytes 2359304 | tf_op jit(solution)/shard_map/ppermute | solution.py:460
  133.1 17.1 %collective-permute-start.27 = (bf16[3,512,256]{2,1,0:T(8,128)(2,1)S(1)}, bf16[3,512,256]{2,1,0:T(8,128)(2,1)S(1)}, u32[]{:S(2)}, u32[]{:S(2)}) collective-permute-start(bf16[3,512,256]{2,1,0:T(8,128)(2,1)S(1)} %collective-permute-done.26.a_ref), channel_id=1, source_target_pairs={{4,8},{5,9},{6,10},{7,11},{8,4},{9,5},{10,6},{11,7},{20,24},{21,25... | collective-permute-start | bytes 2359304 | tf_op jit(solution)/shard_map/ppermute | solution.py:460
  134.5 17.4 %collective-permute-start.31 = (bf16[3,512,256]{2,1,0:T(8,128)(2,1)S(1)}, bf16[3,512,256]{2,1,0:T(8,128)(2,1)S(1)}, u32[]{:S(2)}, u32[]{:S(2)}) collective-permute-start(bf16[3,512,256]{2,1,0:T(8,128)(2,1)S(1)} %choose.7.refs_3_), channel_id=1, source_target_pairs={{0,2},{1,3},{2,0},{3,1},{4,6},{5,7},{6,4},{7,5},{8,10},{9,11},{10,... | collective-permute-start | bytes 2359304 | tf_op jit(solution)/shard_map/ppermute | solution.py:460
  136.7 30.0 %collective-permute-start.28 = (bf16[640,768]{1,0:T(8,128)(2,1)S(1)}, bf16[640,768]{1,0:T(8,128)(2,1)S(1)}, u32[]{:S(2)}, u32[]{:S(2)}) collective-permute-start(bf16[640,768]{1,0:T(8,128)(2,1)S(1)} %project.13), channel_id=1, source_target_pairs={{0,16},{1,17},{2,18},{3,19},{4,20},{5,21},{6,22},{7,23},{8,24},{9,... | collective-permute-start | bytes 2949128 | tf_op jit(solution)/shard_map/ppermute | solution.py:460
  150.2 20.6 %collective-permute-start.30 = (bf16[3,512,256]{2,1,0:T(8,128)(2,1)S(1)}, bf16[3,512,256]{2,1,0:T(8,128)(2,1)S(1)}, u32[]{:S(2)}, u32[]{:S(2)}) collective-permute-start(bf16[3,512,256]{2,1,0:T(8,128)(2,1)S(1)} %collective-permute-done.29.refs_1_), channel_id=1, source_target_pairs={{4,8},{5,9},{6,10},{7,11},{8,4},{9,5},{10,6},{11,7},{20,24},{21,25... | collective-permute-start | bytes 2359304 | tf_op jit(solution)/shard_map/ppermute | solution.py:460
  151.9 20.7 %collective-permute-start.35 = (bf16[3,512,256]{2,1,0:T(8,128)(2,1)S(1)}, bf16[3,512,256]{2,1,0:T(8,128)(2,1)S(1)}, u32[]{:S(2)}, u32[]{:S(2)}) collective-permute-start(bf16[3,512,256]{2,1,0:T(8,128)(2,1)S(1)} %collective-permute-done.27), channel_id=1, source_target_pairs={{4,0},{5,1},{6,2},{7,3},{8,12},{9,13},{10,14},{11,15},{20,16},{21,... | collective-permute-start | bytes 2359304 | tf_op jit(solution)/shard_map/ppermute | solution.py:460
  153.2 19.4 %collective-permute-start.34 = (bf16[3,512,256]{2,1,0:T(8,128)(2,1)S(1)}, bf16[3,512,256]{2,1,0:T(8,128)(2,1)S(1)}, u32[]{:S(2)}, u32[]{:S(2)}) collective-permute-start(bf16[3,512,256]{2,1,0:T(8,128)(2,1)S(1)} %collective-permute-done.29.refs_1_), channel_id=1, source_target_pairs={{0,2},{1,3},{2,0},{3,1},{4,6},{5,7},{6,4},{7,5},{8,10},{9,11},{10,... | collective-permute-start | bytes 2359304 | tf_op jit(solution)/shard_map/ppermute | solution.py:460
  153.5 17.3 %collective-permute-start.32 = (bf16[1,256,1024]{2,1,0:T(8,128)(2,1)S(1)}, bf16[1,256,1024]{2,1,0:T(8,128)(2,1)S(1)}, u32[]{:S(2)}, u32[]{:S(2)}) collective-permute-start(bf16[1,256,1024]{2,1,0:T(8,128)(2,1)S(1)} %get-tuple-element.151.refs_0_), channel_id=1, source_target_pairs={{0,4},{1,5},{2,6},{3,7},{12,8},{13,9},{14,10},{15,11},{16,20},{17,... | collective-permute-start | bytes 1572872 | tf_op jit(solution)/shard_map/ppermute | solution.py:460
  170.9 19.7 %collective-permute-start.33 = (bf16[2,1,256,1024]{3,2,1,0:T(8,128)(2,1)S(1)}, bf16[2,1,256,1024]{3,2,1,0:T(8,128)(2,1)S(1)}, u32[]{:S(2)}, u32[]{:S(2)}) collective-permute-start(bf16[2,1,256,1024]{3,2,1,0:T(8,128)(2,1)S(1)} %stack.20), channel_id=1, source_target_pairs={{4,8},{5,9},{6,10},{7,11},{8,4},{9,5},{10,6},{11,7},{20,24},{21,25... | collective-permute-start | bytes 3145736 | tf_op jit(solution)/shard_map/ppermute | solution.py:460
  172.6 18.0 %collective-permute-start.36 = (bf16[1664,256]{1,0:T(8,128)(2,1)S(1)}, bf16[1664,256]{1,0:T(8,128)(2,1)S(1)}, u32[]{:S(2)}, u32[]{:S(2)}) collective-permute-start(bf16[1664,256]{1,0:T(8,128)(2,1)S(1)} %pack.1), channel_id=1, source_target_pairs={{0,4},{1,5},{2,6},{3,7},{4,0},{5,1},{6,2},{7,3},{8,12},{9,13},{10,... | collective-permute-start | bytes 2555912 | tf_op jit(solution)/shard_map/ppermute | solution.py:460
  176.3 15.6 %collective-permute-start.40 = (bf16[3,512,256]{2,1,0:T(8,128)(2,1)S(1)}, bf16[3,512,256]{2,1,0:T(8,128)(2,1)S(1)}, u32[]{:S(2)}, u32[]{:S(2)}) collective-permute-start(bf16[3,512,256]{2,1,0:T(8,128)(2,1)S(1)} %choose.8.refs_1_), channel_id=1, source_target_pairs={{0,2},{1,3},{2,0},{3,1},{4,6},{5,7},{6,4},{7,5},{8,10},{9,11},{10,... | collective-permute-start | bytes 2359304 | tf_op jit(solution)/shard_map/ppermute | solution.py:460
  176.4 7.1 %collective-permute-start.37 = (bf16[640,256]{1,0:T(8,128)(2,1)S(1)}, bf16[640,256]{1,0:T(8,128)(2,1)S(1)}, u32[]{:S(2)}, u32[]{:S(2)}) collective-permute-start(bf16[640,256]{1,0:T(8,128)(2,1)S(1)} %attend.2.piece_ref.refs_0_), channel_id=1, source_target_pairs={{0,1},{1,0},{2,3},{3,2},{4,5},{5,4},{6,7},{7,6},{8,9},{9,8},{10,11... | collective-permute-start | bytes 983048 | tf_op jit(solution)/shard_map/ppermute | solution.py:460
  190.6 26.6 %collective-permute-start.38 = (bf16[2,1,256,1024]{3,2,1,0:T(8,128)(2,1)S(1)}, bf16[2,1,256,1024]{3,2,1,0:T(8,128)(2,1)S(1)}, u32[]{:S(2)}, u32[]{:S(2)}) collective-permute-start(bf16[2,1,256,1024]{3,2,1,0:T(8,128)(2,1)S(1)} %collective-permute-done.33), channel_id=1, source_target_pairs={{4,0},{5,1},{6,2},{7,3},{8,12},{9,13},{10,14},{11,15},{20,16},{21,... | collective-permute-start | bytes 3145736 | tf_op jit(solution)/shard_map/ppermute | solution.py:460
  193.7 23.5 %collective-permute-start.39 = (bf16[2,1,256,1024]{3,2,1,0:T(8,128)(2,1)S(1)}, bf16[2,1,256,1024]{3,2,1,0:T(8,128)(2,1)S(1)}, u32[]{:S(2)}, u32[]{:S(2)}) collective-permute-start(bf16[2,1,256,1024]{3,2,1,0:T(8,128)(2,1)S(1)} %stack.21), channel_id=1, source_target_pairs={{4,8},{5,9},{6,10},{7,11},{8,4},{9,5},{10,6},{11,7},{20,24},{21,25... | collective-permute-start | bytes 3145736 | tf_op jit(solution)/shard_map/ppermute | solution.py:460
  197.4 19.8 %collective-permute-start.44 = (bf16[1,256,1024]{2,1,0:T(8,128)(2,1)S(1)}, bf16[1,256,1024]{2,1,0:T(8,128)(2,1)S(1)}, u32[]{:S(2)}, u32[]{:S(2)}) collective-permute-start(bf16[1,256,1024]{2,1,0:T(8,128)(2,1)S(1)} %choose.9.refs_6_.refs_18_), channel_id=1, source_target_pairs={{0,2},{1,3},{2,0},{3,1},{4,6},{5,7},{6,4},{7,5},{8,10},{9,11},{10,... | collective-permute-start | bytes 1572872 | tf_op jit(solution)/shard_map/ppermute | solution.py:460
  197.8 19.5 %collective-permute-start.43 = (bf16[640,256]{1,0:T(8,128)(2,1)S(1)}, bf16[640,256]{1,0:T(8,128)(2,1)S(1)}, u32[]{:S(2)}, u32[]{:S(2)}) collective-permute-start(bf16[640,256]{1,0:T(8,128)(2,1)S(1)} %get-tuple-element.158.refs_2_), channel_id=1, source_target_pairs={{0,1},{1,0},{2,3},{3,2},{4,5},{5,4},{6,7},{7,6},{8,9},{9,8},{10,11... | collective-permute-start | bytes 983048 | tf_op jit(solution)/shard_map/ppermute | solution.py:460
  203.0 14.2 %collective-permute-start.42 = (bf16[640,256]{1,0:T(8,128)(2,1)S(1)}, bf16[640,256]{1,0:T(8,128)(2,1)S(1)}, u32[]{:S(2)}, u32[]{:S(2)}) collective-permute-start(bf16[640,256]{1,0:T(8,128)(2,1)S(1)} %attend.3.refs_0_), channel_id=1, source_target_pairs={{0,1},{1,0},{2,3},{3,2},{4,5},{5,4},{6,7},{7,6},{8,9},{9,8},{10,11... | collective-permute-start | bytes 983048 | tf_op jit(solution)/shard_map/ppermute | solution.py:460
  217.2 7.1 %collective-permute-start.45 = (bf16[640,256]{1,0:T(8,128)(2,1)S(1)}, bf16[640,256]{1,0:T(8,128)(2,1)S(1)}, u32[]{:S(2)}, u32[]{:S(2)}) collective-permute-start(bf16[640,256]{1,0:T(8,128)(2,1)S(1)} %attend.3.refs_0_), channel_id=1, source_target_pairs={{0,4},{1,5},{2,6},{3,7},{4,0},{5,1},{6,2},{7,3},{8,12},{9,13},{10,... | collective-permute-start | bytes 983048 | tf_op jit(solution)/shard_map/ppermute | solution.py:460
  225.9 14.3 %collective-permute-start.47 = (bf16[2,1,256,512]{3,2,1,0:T(8,128)(2,1)S(1)}, bf16[2,1,256,512]{3,2,1,0:T(8,128)(2,1)S(1)}, u32[]{:S(2)}, u32[]{:S(2)}) collective-permute-start(bf16[2,1,256,512]{3,2,1,0:T(8,128)(2,1)S(1)} %get-tuple-element.163.refs_12_.refs_14_.refs_20_.refs_22_), channel_id=1, source_target_pairs={{0,2},{1,3},{2,0},{3,1},{4,6},{5,7},{6,4},{7,5},{8,10},{9,11},{10,... | collective-permute-start | bytes 1572872 | tf_op jit(solution)/shard_map/ppermute | solution.py:460
  226.0 14.2 %collective-permute-start.48 = (bf16[640,256]{1,0:T(8,128)(2,1)S(1)}, bf16[640,256]{1,0:T(8,128)(2,1)S(1)}, u32[]{:S(2)}, u32[]{:S(2)}) collective-permute-start(bf16[640,256]{1,0:T(8,128)(2,1)S(1)} %collective-permute-done.45.refs_2_), channel_id=1, source_target_pairs={{0,1},{1,0},{2,3},{3,2},{4,5},{5,4},{6,7},{7,6},{8,9},{9,8},{10,11... | collective-permute-start | bytes 983048 | tf_op jit(solution)/shard_map/ppermute | solution.py:460
  245.9 14.2 %collective-permute-start.50 = (bf16[2,1,256,512]{3,2,1,0:T(8,128)(2,1)S(1)}, bf16[2,1,256,512]{3,2,1,0:T(8,128)(2,1)S(1)}, u32[]{:S(2)}, u32[]{:S(2)}) collective-permute-start(bf16[2,1,256,512]{3,2,1,0:T(8,128)(2,1)S(1)} %get-tuple-element.168.refs_12_.refs_14_.refs_20_.refs_22_), channel_id=1, source_target_pairs={{0,2},{1,3},{2,0},{3,1},{4,6},{5,7},{6,4},{7,5},{8,10},{9,11},{10,... | collective-permute-start | bytes 1572872 | tf_op jit(solution)/shard_map/ppermute | solution.py:460
  248.2 9.8 %collective-permute-start.52 = (bf16[320,512]{1,0:T(8,128)(2,1)S(1)}, bf16[320,512]{1,0:T(8,128)(2,1)S(1)}, u32[]{:S(2)}, u32[]{:S(2)}) collective-permute-start(bf16[320,512]{1,0:T(8,128)(2,1)S(1)} %join.2), channel_id=1, source_target_pairs={{0,4},{1,5},{2,6},{3,7},{4,0},{5,1},{6,2},{7,3},{8,12},{9,13},{10,... | collective-permute-start | bytes 983048 | tf_op jit(solution)/shard_map/ppermute | solution.py:460
  264.3 9.8 %collective-permute-start.57 = (bf16[320,512]{1,0:T(8,128)(2,1)S(1)}, bf16[320,512]{1,0:T(8,128)(2,1)S(1)}, u32[]{:S(2)}, u32[]{:S(2)}) collective-permute-start(bf16[320,512]{1,0:T(8,128)(2,1)S(1)} %join.3), channel_id=1, source_target_pairs={{0,4},{1,5},{2,6},{3,7},{4,0},{5,1},{6,2},{7,3},{8,12},{9,13},{10,... | collective-permute-start | bytes 983048 | tf_op jit(solution)/shard_map/ppermute | solution.py:460
  267.1 8.7 %collective-permute-start.56 = (bf16[640,512]{1,0:T(8,128)(2,1)S(1)}, bf16[640,512]{1,0:T(8,128)(2,1)S(1)}, u32[]{:S(2)}, u32[]{:S(2)}) collective-permute-start(bf16[640,512]{1,0:T(8,128)(2,1)S(1)} %combine.9.refs_4_), channel_id=1, source_target_pairs={{0,16},{1,17},{2,18},{3,19},{4,20},{5,21},{6,22},{7,23},{8,24},{9,... | collective-permute-start | bytes 1966088 | tf_op jit(solution)/shard_map/ppermute | solution.py:460
  (17 other events, 196.3 us)

commit v17 on v16

--- a/solution.py
+++ b/solution.py
@@ -610,9 +610,11 @@
         pieces_a = stack(here, [after(held_a[0], late_o[0])] + held_a[1:])
         pieces_a = (pieces_a, to_core(pieces_a))
         near = [(0, mine_o, p1o), (1, second_o, p2o)]
-        total = combine(here, ("partner", "own"), [pieces_a + (0, near)])
+        swapped = [to_core(a, late_o[0]) for a in held_b[:-1]]
+        total = combine(here, ("partner", "own"), [(after(pieces_a[0], *swapped), pieces_a[1], 0, near)])
+        swapped.append(to_core(held_b[-1], total, p34o[0]))
         pieces_b = stack(here, [after(held_b[0], total, p34o[0])] + held_b[1:])
-        pieces_b = (pieces_b, to_core(pieces_b))
+        pieces_b = (pieces_b, stack(here, swapped))
 
         fars, rests = [], []
         for side in range(2):

time: 279 us -> 277 us (level)
  waiting for transfers between devices: 142 us -> 139 us
    ppermute x59 -> x62, waiting for transfers between devices: 142 us -> 139 us  [move(): lax.ppermute(after(array, *earlier) if earlier else array, AXES, pairs)]
    ppermute x59 -> x62, starting transfers between devices: 67.5 us -> 68.4 us  [move(): lax.ppermute(after(array, *earlier) if earlier else array, AXES, pairs)]
    pallas_call x39 -> x40, Pallas kernels: 61.3 us -> 61.9 us  [call(): pl.pallas_call(kernel, in_specs=[pl.BlockSpec(memory_space=SMEM)] + [pl.B...]
  transfers between devices with their start and end apart: 59 -> 62, of which waited for: 29 -> 32; matrix products, arithmetic and copies ran while one was open for 0% -> 0% of each run, Pallas kernels for 19% -> 20%
where the time goes in v17:
time: 277 us
  waiting for transfers between devices  139 us (50%)
  starting transfers between devices  68.4 us (25%)
  Pallas kernels  64.3 us (23%)
  local copies, waits for them, and re-layouts  4.34 us (2%)
    ppermute x62, waiting for transfers between devices, move(): lax.ppermute(after(array, *earlier) if earlier else array, AXES, pairs)  139 us
    ppermute x62, starting transfers between devices, move(): lax.ppermute(after(array, *earlier) if earlier else array, AXES, pairs)  68.4 us
    pallas_call x40, Pallas kernels, call(): pl.pallas_call(kernel, in_specs=[pl.BlockSpec(memory_space=SMEM)] + [pl.B...  61.9 us
  transfers between devices with their start and end apart: 62, of which 32 were waited for; matrix products, arithmetic and copies ran while one was open for 0% of the time, Pallas kernels for 20%

profile of v17, /device:TPU:0, one launch (start us, length us, event | category | flops | bytes accessed | tf_op | source)
XLA Modules:
  0.0 276.9 jit_solution(16186751448134838283)
XLA Ops:
  0.8 1.9 copy-done
  3.5 3.0 %collective-permute-start.2 = (bf16[3,512,256]{2,1,0:T(8,128)(2,1)S(1)}, bf16[3,512,256]{2,1,0:T(8,128)(2,1)S(1)}, u32[]{:S(2)}, u32[]{:S(2)}) collective-permute-start(bf16[3,512,256]{2,1,0:T(8,128)(2,1)S(1)} %get-tuple-element.101.refs_1_), channel_id=1, source_target_pairs={{0,2},{1,3},{2,0},{3,1},{4,6},{5,7},{6,4},{7,5},{8,10},{9,11},{10,... | collective-permute-start | bytes 2359304 | tf_op jit(solution)/shard_map/ppermute | solution.py:460
  8.8 15.3 %collective-permute-done.2.refs_2_ = bf16[3,512,256]{2,1,0:T(8,128)(2,1)S(1)} collective-permute-done((bf16[3,512,256]{2,1,0:T(8,128)(2,1)S(1)}, bf16[3,512,256]{2,1,0:T(8,128)(2,1)S(1)}, u32[]{:S(2)}, u32[]{:S(2)}) %collective-permute-start.2) | collective-permute-done | bytes 786464 | tf_op jit(solution)/shard_map/ppermute | solution.py:460
  26.6 7.7 %collective-permute-start.3 = (bf16[3,512,256]{2,1,0:T(8,128)(2,1)S(1)}, bf16[3,512,256]{2,1,0:T(8,128)(2,1)S(1)}, u32[]{:S(2)}, u32[]{:S(2)}) collective-permute-start(bf16[3,512,256]{2,1,0:T(8,128)(2,1)S(1)} %collective-permute-done), channel_id=1, source_target_pairs={{0,4},{1,5},{2,6},{3,7},{4,0},{5,1},{6,2},{7,3},{8,12},{9,13},{10,... | collective-permute-start | bytes 2359304 | tf_op jit(solution)/shard_map/ppermute | solution.py:460
  34.3 1.7 copy-done.2
  39.2 5.2 %collective-permute-done.4.refs_4_ = bf16[3,512,256]{2,1,0:T(8,128)(2,1)S(1)} collective-permute-done((bf16[3,512,256]{2,1,0:T(8,128)(2,1)S(1)}, bf16[3,512,256]{2,1,0:T(8,128)(2,1)S(1)}, u32[]{:S(2)}, u32[]{:S(2)}) %collective-permute-start.4) | collective-permute-done | bytes 786464 | tf_op jit(solution)/shard_map/ppermute | solution.py:460
  44.4 5.4 %collective-permute-done.3.a_ref = bf16[3,512,256]{2,1,0:T(8,128)(2,1)S(1)} collective-permute-done((bf16[3,512,256]{2,1,0:T(8,128)(2,1)S(1)}, bf16[3,512,256]{2,1,0:T(8,128)(2,1)S(1)}, u32[]{:S(2)}, u32[]{:S(2)}) %collective-permute-start.3) | collective-permute-done | bytes 786464 | tf_op jit(solution)/shard_map/ppermute | solution.py:460
  52.7 3.5 %collective-permute-start.6 = (bf16[160,2048]{1,0:T(8,128)(2,1)S(1)}, bf16[160,2048]{1,0:T(8,128)(2,1)S(1)}, u32[]{:S(2)}, u32[]{:S(2)}) collective-permute-start(bf16[160,2048]{1,0:T(8,128)(2,1)S(1)} %get-tuple-element.108), channel_id=1, source_target_pairs={{0,4},{1,5},{2,6},{3,7},{4,0},{5,1},{6,2},{7,3},{8,12},{9,13},{10,... | collective-permute-start | bytes 1966088 | tf_op jit(solution)/shard_map/ppermute | solution.py:460
  56.2 8.8 %collective-permute-done.10.refs_2_ = bf16[320,2048]{1,0:T(8,128)(2,1)S(1)} collective-permute-done((bf16[320,2048]{1,0:T(8,128)(2,1)S(1)}, bf16[320,2048]{1,0:T(8,128)(2,1)S(1)}, u32[]{:S(2)}, u32[]{:S(2)}) %collective-permute-start.10) | collective-permute-done | bytes 1310752 | tf_op jit(solution)/shard_map/ppermute | solution.py:460
  65.1 2.7 collective-permute-done.6.refs_2_
  67.8 3.3 %collective-permute-start.9 = (bf16[176,2048]{1,0:T(8,128)(2,1)S(1)}, bf16[176,2048]{1,0:T(8,128)(2,1)S(1)}, u32[]{:S(2)}, u32[]{:S(2)}) collective-permute-start(bf16[176,2048]{1,0:T(8,128)(2,1)S(1)} %get-tuple-element.112), channel_id=1, source_target_pairs={{0,4},{1,5},{2,6},{3,7},{4,0},{5,1},{6,2},{7,3},{8,12},{9,13},{10,... | collective-permute-start | bytes 2162696 | tf_op jit(solution)/shard_map/ppermute | solution.py:460
  76.3 3.2 %normalize.3.refs_0_ = bf16[2,8,640,512]{3,2,1,0:T(8,128)(2,1)S(1)} custom-call(s32[3]{0:T(128)S(1)} %pad_add_fusion.h_ref._, f32[8,1,512]{2,1,0:T(1,128)S(1)} %bitcast.9, bf16[640,2048]{1,0:T(8,128)(2,1)S(1)} %copy-done.3, bf16[320,2048]{1,0:T(8,128)(2,1)S(1)} %collective-permute-done.10.refs_2_, bf16[320,2048]{1,0:T(8,128)(2,1)S(1)} %collective-permute-done.11.refs_3_), custom_call_target="tpu_custom_call" | custom-call | tf_op jit(solution)/shard_map/normalize/pallas_call | solution.py:32
  79.5 7.2 %collective-permute-done.12.refs_3_ = bf16[160,2048]{1,0:T(8,128)(2,1)S(1)} collective-permute-done((bf16[160,2048]{1,0:T(8,128)(2,1)S(1)}, bf16[160,2048]{1,0:T(8,128)(2,1)S(1)}, u32[]{:S(2)}, u32[]{:S(2)}) %collective-permute-start.12) | collective-permute-done | bytes 655392 | tf_op jit(solution)/shard_map/ppermute | solution.py:460
  87.9 2.8 %collective-permute-done.22.refs_2_ = bf16[3,512,256]{2,1,0:T(8,128)(2,1)S(1)} collective-permute-done((bf16[3,512,256]{2,1,0:T(8,128)(2,1)S(1)}, bf16[3,512,256]{2,1,0:T(8,128)(2,1)S(1)}, u32[]{:S(2)}, u32[]{:S(2)}) %collective-permute-start.22) | collective-permute-done | bytes 786464 | tf_op jit(solution)/shard_map/ppermute | solution.py:460
  94.1 4.6 %collective-permute-start.25 = (bf16[1,256,1024]{2,1,0:T(8,128)(2,1)S(1)}, bf16[1,256,1024]{2,1,0:T(8,128)(2,1)S(1)}, u32[]{:S(2)}, u32[]{:S(2)}) collective-permute-start(bf16[1,256,1024]{2,1,0:T(8,128)(2,1)S(1)} %get-tuple-element.153.refs_0_.block_ref), channel_id=1, source_target_pairs={{0,4},{1,5},{2,6},{3,7},{12,8},{13,9},{14,10},{15,11},{16,20},{17,... | collective-permute-start | bytes 1572872 | tf_op jit(solution)/shard_map/ppermute | solution.py:460
  99.2 3.7 %project.10.refs_7_ = f32[2,640,768]{2,1,0:T(8,128)S(1)} custom-call(s32[3]{0:T(128)S(1)} %pad_add_fusion.h_ref._, bf16[2,8,640,512]{3,2,1,0:T(8,128)(2,1)S(1)} %normalize.3.refs_0_, bf16[3,512,256]{2,1,0:T(8,128)(2,1)S(1)} %get-tuple-element.101.refs_1_, bf16[3,512,256]{2,1,0:T(8,128)(2,1)S(1)} %collective-permute-done.2.refs_2_, ...), custom_call_target="tpu_custom_call" | custom-call | tf_op jit(solution)/shard_map/project/pallas_call | solution.py:32
  103.0 1.8 normalize.4.refs_0_
  105.5 4.8 %collective-permute-done.21.a_ref = bf16[3,512,256]{2,1,0:T(8,128)(2,1)S(1)} collective-permute-done((bf16[3,512,256]{2,1,0:T(8,128)(2,1)S(1)}, bf16[3,512,256]{2,1,0:T(8,128)(2,1)S(1)}, u32[]{:S(2)}, u32[]{:S(2)}) %collective-permute-start.21) | collective-permute-done | bytes 786464 | tf_op jit(solution)/shard_map/ppermute | solution.py:460
  110.4 3.5 %collective-permute-start.26 = (bf16[3,512,256]{2,1,0:T(8,128)(2,1)S(1)}, bf16[3,512,256]{2,1,0:T(8,128)(2,1)S(1)}, u32[]{:S(2)}, u32[]{:S(2)}) collective-permute-start(bf16[3,512,256]{2,1,0:T(8,128)(2,1)S(1)} %collective-permute-done.17), channel_id=1, source_target_pairs={{0,4},{1,5},{2,6},{3,7},{4,0},{5,1},{6,2},{7,3},{8,12},{9,13},{10,... | collective-permute-start | bytes 2359304 | tf_op jit(solution)/shard_map/ppermute | solution.py:460
  118.5 1.8 normalize.5.refs_0_
  120.3 3.7 %project.11.refs_3_ = f32[2,640,768]{2,1,0:T(8,128)S(1)} custom-call(s32[3]{0:T(128)S(1)} %pad_add_fusion.h_ref._, bf16[2,8,640,512]{3,2,1,0:T(8,128)(2,1)S(1)} %normalize.5.refs_0_, bf16[3,512,256]{2,1,0:T(8,128)(2,1)S(1)} %get-tuple-element.101.refs_1_, bf16[3,512,256]{2,1,0:T(8,128)(2,1)S(1)} %collective-permute-done.2.refs_2_, ...), custom_call_target="tpu_custom_call", output_to_operand_aliasing={{}: (8, {})} | custom-call | tf_op jit(solution)/shard_map/project/pallas_call | solution.py:32
  124.0 6.7 %collective-permute-done.26.a_ref = bf16[3,512,256]{2,1,0:T(8,128)(2,1)S(1)} collective-permute-done((bf16[3,512,256]{2,1,0:T(8,128)(2,1)S(1)}, bf16[3,512,256]{2,1,0:T(8,128)(2,1)S(1)}, u32[]{:S(2)}, u32[]{:S(2)}) %collective-permute-start.26) | collective-permute-done | bytes 786464 | tf_op jit(solution)/shard_map/ppermute | solution.py:460
  130.7 2.1 collective-permute-done.24.refs_2_
  135.0 1.7 project.13
  138.5 11.7 %collective-permute-done.29.refs_1_ = bf16[3,512,256]{2,1,0:T(8,128)(2,1)S(1)} collective-permute-done((bf16[3,512,256]{2,1,0:T(8,128)(2,1)S(1)}, bf16[3,512,256]{2,1,0:T(8,128)(2,1)S(1)}, u32[]{:S(2)}, u32[]{:S(2)}) %collective-permute-start.29) | collective-permute-done | bytes 786464 | tf_op jit(solution)/shard_map/ppermute | solution.py:460
  153.5 7.1 %collective-permute-start.32 = (bf16[1,256,1024]{2,1,0:T(8,128)(2,1)S(1)}, bf16[1,256,1024]{2,1,0:T(8,128)(2,1)S(1)}, u32[]{:S(2)}, u32[]{:S(2)}) collective-permute-start(bf16[1,256,1024]{2,1,0:T(8,128)(2,1)S(1)} %get-tuple-element.156.refs_0_), channel_id=1, source_target_pairs={{0,4},{1,5},{2,6},{3,7},{12,8},{13,9},{14,10},{15,11},{16,20},{17,... | collective-permute-start | bytes 1572872 | tf_op jit(solution)/shard_map/ppermute | solution.py:460
  161.2 2.7 project.14.refs_5_
  164.0 2.7 project.15.refs_3_
  166.7 4.2 %attend.2.piece_ref.refs_0_ = bf16[640,256]{1,0:T(8,128)(2,1)S(1)} custom-call(s32[3]{0:T(128)S(1)} %pad_add_fusion.h_ref._, s32[1,640]{1,0:T(1,128)S(1)} %broadcast_in_dim.3.kind_ref.own_kind_ref, s32[1,640]{1,0:T(1,128)S(1)} %kinds_behind.1.other_kind_ref.kind_ref, bf16[640,768]{1,0:T(8,128)(2,1)S(1)} %project.12.own_ref, ...), custom_call_target="tpu_custom_call" | custom-call | tf_op jit(solution)/shard_map/attend/pallas_call | solution.py:32
  172.6 3.1 %collective-permute-start.36 = (bf16[1664,256]{1,0:T(8,128)(2,1)S(1)}, bf16[1664,256]{1,0:T(8,128)(2,1)S(1)}, u32[]{:S(2)}, u32[]{:S(2)}) collective-permute-start(bf16[1664,256]{1,0:T(8,128)(2,1)S(1)} %pack.1), channel_id=1, source_target_pairs={{0,4},{1,5},{2,6},{3,7},{4,0},{5,1},{6,2},{7,3},{8,12},{9,13},{10,... | collective-permute-start | bytes 2555912 | tf_op jit(solution)/shard_map/ppermute | solution.py:460
  178.3 1.9 project.16.refs_3_
  180.3 1.9 project.17.refs_3_
  183.5 7.1 %collective-permute-done.36.in_ref = bf16[1664,256]{1,0:T(8,128)(2,1)S(1)} collective-permute-done((bf16[1664,256]{1,0:T(8,128)(2,1)S(1)}, bf16[1664,256]{1,0:T(8,128)(2,1)S(1)}, u32[]{:S(2)}, u32[]{:S(2)}) %collective-permute-start.36) | collective-permute-done | bytes 852000 | tf_op jit(solution)/shard_map/ppermute | solution.py:460
  191.9 1.7 project.19
  198.9 4.1 %attend.3.refs_0_ = bf16[640,256]{1,0:T(8,128)(2,1)S(1)} custom-call(s32[3]{0:T(128)S(1)} %pad_add_fusion.h_ref._, s32[1,640]{1,0:T(1,128)S(1)} %broadcast_in_dim.3.kind_ref.own_kind_ref, s32[1,640]{1,0:T(1,128)S(1)} %kinds_behind.1.other_kind_ref.kind_ref, bf16[640,768]{1,0:T(8,128)(2,1)S(1)} %project.18.own_ref, ...), custom_call_target="tpu_custom_call" | custom-call | tf_op jit(solution)/shard_map/attend/pallas_call | solution.py:32
  204.0 13.2 %collective-permute-done.38.a_ref = bf16[2,1,256,1024]{3,2,1,0:T(8,128)(2,1)S(1)} collective-permute-done((bf16[2,1,256,1024]{3,2,1,0:T(8,128)(2,1)S(1)}, bf16[2,1,256,1024]{3,2,1,0:T(8,128)(2,1)S(1)}, u32[]{:S(2)}, u32[]{:S(2)}) %collective-permute-start.38) | collective-permute-done | bytes 1048608 | tf_op jit(solution)/shard_map/ppermute | solution.py:460
  217.3 7.0 %collective-permute-done.45.refs_2_ = bf16[640,256]{1,0:T(8,128)(2,1)S(1)} collective-permute-done((bf16[640,256]{1,0:T(8,128)(2,1)S(1)}, bf16[640,256]{1,0:T(8,128)(2,1)S(1)}, u32[]{:S(2)}, u32[]{:S(2)}) %collective-permute-start.45) | collective-permute-done | bytes 327712 | tf_op jit(solution)/shard_map/ppermute | solution.py:460
  227.0 2.4 collective-permute-done.49.refs_2_
  230.3 2.1 combine.5.refs_24_
  232.4 6.7 %collective-permute-done.51.refs_3_ = bf16[640,256]{1,0:T(8,128)(2,1)S(1)} collective-permute-done((bf16[640,256]{1,0:T(8,128)(2,1)S(1)}, bf16[640,256]{1,0:T(8,128)(2,1)S(1)}, u32[]{:S(2)}, u32[]{:S(2)}) %collective-permute-start.51) | collective-permute-done | bytes 327712 | tf_op jit(solution)/shard_map/ppermute | solution.py:460
  242.5 1.8 combine.6
  247.9 8.8 %collective-permute-done.55.refs_2_ = bf16[320,512]{1,0:T(8,128)(2,1)S(1)} collective-permute-done((bf16[320,512]{1,0:T(8,128)(2,1)S(1)}, bf16[320,512]{1,0:T(8,128)(2,1)S(1)}, u32[]{:S(2)}, u32[]{:S(2)}) %collective-permute-start.55) | collective-permute-done | bytes 327712 | tf_op jit(solution)/shard_map/ppermute | solution.py:460
  256.6 2.1 collective-permute-done.53.refs_13_.refs_15_.refs_21_.refs_23_
  258.7 1.7 combine.7
  264.0 1.7 combine.9.refs_4_
  265.8 1.7 combine.8.refs_0_
  268.2 4.6 %collective-permute-done.60.refs_6_ = bf16[320,512]{1,0:T(8,128)(2,1)S(1)} collective-permute-done((bf16[320,512]{1,0:T(8,128)(2,1)S(1)}, bf16[320,512]{1,0:T(8,128)(2,1)S(1)}, u32[]{:S(2)}, u32[]{:S(2)}) %collective-permute-start.60) | collective-permute-done | bytes 327712 | tf_op jit(solution)/shard_map/ppermute | solution.py:460
  274.4 2.4 assemble.1
  (131 shorter events, 65.4 us)
Async XLA Ops:
  3.5 20.6 %collective-permute-start.2 = (bf16[3,512,256]{2,1,0:T(8,128)(2,1)S(1)}, bf16[3,512,256]{2,1,0:T(8,128)(2,1)S(1)}, u32[]{:S(2)}, u32[]{:S(2)}) collective-permute-start(bf16[3,512,256]{2,1,0:T(8,128)(2,1)S(1)} %get-tuple-element.101.refs_1_), channel_id=1, source_target_pairs={{0,2},{1,3},{2,0},{3,1},{4,6},{5,7},{6,4},{7,5},{8,10},{9,11},{10,... | collective-permute-start | bytes 2359304 | tf_op jit(solution)/shard_map/ppermute | solution.py:460
  6.5 19.0 %collective-permute-start.1 = (bf16[3,512,256]{2,1,0:T(8,128)(2,1)S(1)}, bf16[3,512,256]{2,1,0:T(8,128)(2,1)S(1)}, u32[]{:S(2)}, u32[]{:S(2)}) collective-permute-start(bf16[3,512,256]{2,1,0:T(8,128)(2,1)S(1)} %get-tuple-element.100), channel_id=1, source_target_pairs={{0,4},{1,5},{2,6},{3,7},{4,0},{5,1},{6,2},{7,3},{8,12},{9,13},{10,... | collective-permute-start | bytes 2359304 | tf_op jit(solution)/shard_map/ppermute | solution.py:460
  8.1 17.4 %collective-permute-start = (bf16[3,512,256]{2,1,0:T(8,128)(2,1)S(1)}, bf16[3,512,256]{2,1,0:T(8,128)(2,1)S(1)}, u32[]{:S(2)}, u32[]{:S(2)}) collective-permute-start(bf16[3,512,256]{2,1,0:T(8,128)(2,1)S(1)} %get-tuple-element.96), channel_id=1, source_target_pairs={{0,0},{1,1},{2,2},{3,3},{4,8},{5,9},{6,10},{7,11},{8,4},{9,5},{10,... | collective-permute-start | bytes 2359304 | tf_op jit(solution)/shard_map/ppermute | solution.py:460
  25.5 13.7 %collective-permute-start.5 = (bf16[3,512,256]{2,1,0:T(8,128)(2,1)S(1)}, bf16[3,512,256]{2,1,0:T(8,128)(2,1)S(1)}, u32[]{:S(2)}, u32[]{:S(2)}) collective-permute-start(bf16[3,512,256]{2,1,0:T(8,128)(2,1)S(1)} %get-tuple-element.105), channel_id=1, source_target_pairs={{4,8},{5,9},{6,10},{7,11},{8,4},{9,5},{10,6},{11,7},{20,24},{21,25... | collective-permute-start | bytes 2359304 | tf_op jit(solution)/shard_map/ppermute | solution.py:460
  26.2 18.2 %collective-permute-start.4 = (bf16[3,512,256]{2,1,0:T(8,128)(2,1)S(1)}, bf16[3,512,256]{2,1,0:T(8,128)(2,1)S(1)}, u32[]{:S(2)}, u32[]{:S(2)}) collective-permute-start(bf16[3,512,256]{2,1,0:T(8,128)(2,1)S(1)} %collective-permute-done.1.refs_3_), channel_id=1, source_target_pairs={{0,2},{1,3},{2,0},{3,1},{4,6},{5,7},{6,4},{7,5},{8,10},{9,11},{10,... | collective-permute-start | bytes 2359304 | tf_op jit(solution)/shard_map/ppermute | solution.py:460
  26.6 23.2 %collective-permute-start.3 = (bf16[3,512,256]{2,1,0:T(8,128)(2,1)S(1)}, bf16[3,512,256]{2,1,0:T(8,128)(2,1)S(1)}, u32[]{:S(2)}, u32[]{:S(2)}) collective-permute-start(bf16[3,512,256]{2,1,0:T(8,128)(2,1)S(1)} %collective-permute-done), channel_id=1, source_target_pairs={{0,4},{1,5},{2,6},{3,7},{4,0},{5,1},{6,2},{7,3},{8,12},{9,13},{10,... | collective-permute-start | bytes 2359304 | tf_op jit(solution)/shard_map/ppermute | solution.py:460
  36.8 28.3 %collective-permute-start.10 = (bf16[320,2048]{1,0:T(8,128)(2,1)S(1)}, bf16[320,2048]{1,0:T(8,128)(2,1)S(1)}, u32[]{:S(2)}, u32[]{:S(2)}) collective-permute-start(bf16[320,2048]{1,0:T(8,128)(2,1)S(1)} %get-tuple-element.114), channel_id=1, source_target_pairs={{0,1},{1,0},{2,3},{3,2},{4,5},{5,4},{6,7},{7,6},{8,9},{9,8},{10,11... | collective-permute-start | bytes 3932168 | tf_op jit(solution)/shard_map/ppermute | solution.py:460
  49.8 15.3 %collective-permute-start.8 = (bf16[3,512,256]{2,1,0:T(8,128)(2,1)S(1)}, bf16[3,512,256]{2,1,0:T(8,128)(2,1)S(1)}, u32[]{:S(2)}, u32[]{:S(2)}) collective-permute-start(bf16[3,512,256]{2,1,0:T(8,128)(2,1)S(1)} %collective-permute-done.3.a_ref), channel_id=1, source_target_pairs={{4,8},{5,9},{6,10},{7,11},{8,4},{9,5},{10,6},{11,7},{20,24},{21,25... | collective-permute-start | bytes 2359304 | tf_op jit(solution)/shard_map/ppermute | solution.py:460
  51.1 16.7 %collective-permute-start.7 = (bf16[3,512,256]{2,1,0:T(8,128)(2,1)S(1)}, bf16[3,512,256]{2,1,0:T(8,128)(2,1)S(1)}, u32[]{:S(2)}, u32[]{:S(2)}) collective-permute-start(bf16[3,512,256]{2,1,0:T(8,128)(2,1)S(1)} %choose.5.refs_5_), channel_id=1, source_target_pairs={{0,2},{1,3},{2,0},{3,1},{4,6},{5,7},{6,4},{7,5},{8,10},{9,11},{10,... | collective-permute-start | bytes 2359304 | tf_op jit(solution)/shard_map/ppermute | solution.py:460
  52.7 15.0 %collective-permute-start.6 = (bf16[160,2048]{1,0:T(8,128)(2,1)S(1)}, bf16[160,2048]{1,0:T(8,128)(2,1)S(1)}, u32[]{:S(2)}, u32[]{:S(2)}) collective-permute-start(bf16[160,2048]{1,0:T(8,128)(2,1)S(1)} %get-tuple-element.108), channel_id=1, source_target_pairs={{0,4},{1,5},{2,6},{3,7},{4,0},{5,1},{6,2},{7,3},{8,12},{9,13},{10,... | collective-permute-start | bytes 1966088 | tf_op jit(solution)/shard_map/ppermute | solution.py:460
  65.1 11.2 %collective-permute-start.11 = (bf16[320,2048]{1,0:T(8,128)(2,1)S(1)}, bf16[320,2048]{1,0:T(8,128)(2,1)S(1)}, u32[]{:S(2)}, u32[]{:S(2)}) collective-permute-start(bf16[320,2048]{1,0:T(8,128)(2,1)S(1)} %collective-permute-done.10.refs_2_), channel_id=1, source_target_pairs={{0,16},{1,17},{2,18},{3,19},{4,20},{5,21},{6,22},{7,23},{8,24},{9,... | collective-permute-start | bytes 3932168 | tf_op jit(solution)/shard_map/ppermute | solution.py:460
  67.8 18.9 %collective-permute-start.9 = (bf16[176,2048]{1,0:T(8,128)(2,1)S(1)}, bf16[176,2048]{1,0:T(8,128)(2,1)S(1)}, u32[]{:S(2)}, u32[]{:S(2)}) collective-permute-start(bf16[176,2048]{1,0:T(8,128)(2,1)S(1)} %get-tuple-element.112), channel_id=1, source_target_pairs={{0,4},{1,5},{2,6},{3,7},{4,0},{5,1},{6,2},{7,3},{8,12},{9,13},{10,... | collective-permute-start | bytes 2162696 | tf_op jit(solution)/shard_map/ppermute | solution.py:460
  71.1 15.6 %collective-permute-start.12 = (bf16[160,2048]{1,0:T(8,128)(2,1)S(1)}, bf16[160,2048]{1,0:T(8,128)(2,1)S(1)}, u32[]{:S(2)}, u32[]{:S(2)}) collective-permute-start(bf16[160,2048]{1,0:T(8,128)(2,1)S(1)} %collective-permute-done.6.refs_2_), channel_id=1, source_target_pairs={{0,1},{1,0},{2,3},{3,2},{4,5},{5,4},{6,7},{7,6},{8,9},{9,8},{10,11... | collective-permute-start | bytes 1966088 | tf_op jit(solution)/shard_map/ppermute | solution.py:460
  72.6 18.1 %collective-permute-start.22 = (bf16[3,512,256]{2,1,0:T(8,128)(2,1)S(1)}, bf16[3,512,256]{2,1,0:T(8,128)(2,1)S(1)}, u32[]{:S(2)}, u32[]{:S(2)}) collective-permute-start(bf16[3,512,256]{2,1,0:T(8,128)(2,1)S(1)} %get-tuple-element.133.refs_1_), channel_id=1, source_target_pairs={{0,2},{1,3},{2,0},{3,1},{4,6},{5,7},{6,4},{7,5},{8,10},{9,11},{10,... | collective-permute-start | bytes 2359304 | tf_op jit(solution)/shard_map/ppermute | solution.py:460
  74.1 17.9 %collective-permute-start.16 = (bf16[3,512,256]{2,1,0:T(8,128)(2,1)S(1)}, bf16[3,512,256]{2,1,0:T(8,128)(2,1)S(1)}, u32[]{:S(2)}, u32[]{:S(2)}) collective-permute-start(bf16[3,512,256]{2,1,0:T(8,128)(2,1)S(1)} %collective-permute-done.1.refs_3_), channel_id=1, source_target_pairs={{4,8},{5,9},{6,10},{7,11},{8,4},{9,5},{10,6},{11,7},{20,24},{21,25... | collective-permute-start | bytes 2359304 | tf_op jit(solution)/shard_map/ppermute | solution.py:460
  86.7 7.4 %collective-permute-start.13 = (bf16[160,2048]{1,0:T(8,128)(2,1)S(1)}, bf16[160,2048]{1,0:T(8,128)(2,1)S(1)}, u32[]{:S(2)}, u32[]{:S(2)}) collective-permute-start(bf16[160,2048]{1,0:T(8,128)(2,1)S(1)} %collective-permute-done.6.refs_2_), channel_id=1, source_target_pairs={{0,16},{1,17},{2,18},{3,19},{4,20},{5,21},{6,22},{7,23},{8,24},{9,... | collective-permute-start | bytes 1966088 | tf_op jit(solution)/shard_map/ppermute | solution.py:460
  87.2 17.6 %collective-permute-start.17 = (bf16[3,512,256]{2,1,0:T(8,128)(2,1)S(1)}, bf16[3,512,256]{2,1,0:T(8,128)(2,1)S(1)}, u32[]{:S(2)}, u32[]{:S(2)}) collective-permute-start(bf16[3,512,256]{2,1,0:T(8,128)(2,1)S(1)} %get-tuple-element.124), channel_id=1, source_target_pairs={{0,0},{1,1},{2,2},{3,3},{4,8},{5,9},{6,10},{7,11},{8,4},{9,5},{10,... | collective-permute-start | bytes 2359304 | tf_op jit(solution)/shard_map/ppermute | solution.py:460
  90.7 19.7 %collective-permute-start.21 = (bf16[3,512,256]{2,1,0:T(8,128)(2,1)S(1)}, bf16[3,512,256]{2,1,0:T(8,128)(2,1)S(1)}, u32[]{:S(2)}, u32[]{:S(2)}) collective-permute-start(bf16[3,512,256]{2,1,0:T(8,128)(2,1)S(1)} %collective-permute-done.8), channel_id=1, source_target_pairs={{4,0},{5,1},{6,2},{7,3},{8,12},{9,13},{10,14},{11,15},{20,16},{21,... | collective-permute-start | bytes 2359304 | tf_op jit(solution)/shard_map/ppermute | solution.py:460
  92.0 18.4 %collective-permute-start.15 = (bf16[176,2048]{1,0:T(8,128)(2,1)S(1)}, bf16[176,2048]{1,0:T(8,128)(2,1)S(1)}, u32[]{:S(2)}, u32[]{:S(2)}) collective-permute-start(bf16[176,2048]{1,0:T(8,128)(2,1)S(1)} %collective-permute-done.9.in_ref.refs_2_), channel_id=1, source_target_pairs={{0,1},{1,0},{2,3},{3,2},{4,5},{5,4},{6,7},{7,6},{8,9},{9,8},{10,11... | collective-permute-start | bytes 2162696 | tf_op jit(solution)/shard_map/ppermute | solution.py:460
  92.6 17.8 %collective-permute-start.23 = (bf16[1,256,1024]{2,1,0:T(8,128)(2,1)S(1)}, bf16[1,256,1024]{2,1,0:T(8,128)(2,1)S(1)}, u32[]{:S(2)}, u32[]{:S(2)}) collective-permute-start(bf16[1,256,1024]{2,1,0:T(8,128)(2,1)S(1)} %get-tuple-element.134.refs_4_.refs_16_), channel_id=1, source_target_pairs={{0,2},{1,3},{2,0},{3,1},{4,6},{5,7},{6,4},{7,5},{8,10},{9,11},{10,... | collective-permute-start | bytes 1572872 | tf_op jit(solution)/shard_map/ppermute | solution.py:460
  94.1 16.3 %collective-permute-start.25 = (bf16[1,256,1024]{2,1,0:T(8,128)(2,1)S(1)}, bf16[1,256,1024]{2,1,0:T(8,128)(2,1)S(1)}, u32[]{:S(2)}, u32[]{:S(2)}) collective-permute-start(bf16[1,256,1024]{2,1,0:T(8,128)(2,1)S(1)} %get-tuple-element.153.refs_0_.block_ref), channel_id=1, source_target_pairs={{0,4},{1,5},{2,6},{3,7},{12,8},{13,9},{14,10},{15,11},{16,20},{17,... | collective-permute-start | bytes 1572872 | tf_op jit(solution)/shard_map/ppermute | solution.py:460
  104.8 19.2 %collective-permute-start.20 = (bf16[3,512,256]{2,1,0:T(8,128)(2,1)S(1)}, bf16[3,512,256]{2,1,0:T(8,128)(2,1)S(1)}, u32[]{:S(2)}, u32[]{:S(2)}) collective-permute-start(bf16[3,512,256]{2,1,0:T(8,128)(2,1)S(1)} %get-tuple-element.129), channel_id=1, source_target_pairs={{4,8},{5,9},{6,10},{7,11},{8,4},{9,5},{10,6},{11,7},{20,24},{21,25... | collective-permute-start | bytes 2359304 | tf_op jit(solution)/shard_map/ppermute | solution.py:460
  110.4 20.3 %collective-permute-start.26 = (bf16[3,512,256]{2,1,0:T(8,128)(2,1)S(1)}, bf16[3,512,256]{2,1,0:T(8,128)(2,1)S(1)}, u32[]{:S(2)}, u32[]{:S(2)}) collective-permute-start(bf16[3,512,256]{2,1,0:T(8,128)(2,1)S(1)} %collective-permute-done.17), channel_id=1, source_target_pairs={{0,4},{1,5},{2,6},{3,7},{4,0},{5,1},{6,2},{7,3},{8,12},{9,13},{10,... | collective-permute-start | bytes 2359304 | tf_op jit(solution)/shard_map/ppermute | solution.py:460
  114.5 18.4 %collective-permute-start.24 = (bf16[3,512,256]{2,1,0:T(8,128)(2,1)S(1)}, bf16[3,512,256]{2,1,0:T(8,128)(2,1)S(1)}, u32[]{:S(2)}, u32[]{:S(2)}) collective-permute-start(bf16[3,512,256]{2,1,0:T(8,128)(2,1)S(1)} %choose.6.refs_1_), channel_id=1, source_target_pairs={{0,2},{1,3},{2,0},{3,1},{4,6},{5,7},{6,4},{7,5},{8,10},{9,11},{10,... | collective-permute-start | bytes 2359304 | tf_op jit(solution)/shard_map/ppermute | solution.py:460
  132.8 17.4 %collective-permute-start.29 = (bf16[3,512,256]{2,1,0:T(8,128)(2,1)S(1)}, bf16[3,512,256]{2,1,0:T(8,128)(2,1)S(1)}, u32[]{:S(2)}, u32[]{:S(2)}) collective-permute-start(bf16[3,512,256]{2,1,0:T(8,128)(2,1)S(1)} %get-tuple-element.142), channel_id=1, source_target_pairs={{0,4},{1,5},{2,6},{3,7},{4,0},{5,1},{6,2},{7,3},{8,12},{9,13},{10,... | collective-permute-start | bytes 2359304 | tf_op jit(solution)/shard_map/ppermute | solution.py:460
  133.1 17.1 %collective-permute-start.27 = (bf16[3,512,256]{2,1,0:T(8,128)(2,1)S(1)}, bf16[3,512,256]{2,1,0:T(8,128)(2,1)S(1)}, u32[]{:S(2)}, u32[]{:S(2)}) collective-permute-start(bf16[3,512,256]{2,1,0:T(8,128)(2,1)S(1)} %collective-permute-done.26.a_ref), channel_id=1, source_target_pairs={{4,8},{5,9},{6,10},{7,11},{8,4},{9,5},{10,6},{11,7},{20,24},{21,25... | collective-permute-start | bytes 2359304 | tf_op jit(solution)/shard_map/ppermute | solution.py:460
  134.5 17.4 %collective-permute-start.31 = (bf16[3,512,256]{2,1,0:T(8,128)(2,1)S(1)}, bf16[3,512,256]{2,1,0:T(8,128)(2,1)S(1)}, u32[]{:S(2)}, u32[]{:S(2)}) collective-permute-start(bf16[3,512,256]{2,1,0:T(8,128)(2,1)S(1)} %choose.7.refs_3_), channel_id=1, source_target_pairs={{0,2},{1,3},{2,0},{3,1},{4,6},{5,7},{6,4},{7,5},{8,10},{9,11},{10,... | collective-permute-start | bytes 2359304 | tf_op jit(solution)/shard_map/ppermute | solution.py:460
  136.7 30.0 %collective-permute-start.28 = (bf16[640,768]{1,0:T(8,128)(2,1)S(1)}, bf16[640,768]{1,0:T(8,128)(2,1)S(1)}, u32[]{:S(2)}, u32[]{:S(2)}) collective-permute-start(bf16[640,768]{1,0:T(8,128)(2,1)S(1)} %project.13), channel_id=1, source_target_pairs={{0,16},{1,17},{2,18},{3,19},{4,20},{5,21},{6,22},{7,23},{8,24},{9,... | collective-permute-start | bytes 2949128 | tf_op jit(solution)/shard_map/ppermute | solution.py:460
  150.2 20.6 %collective-permute-start.30 = (bf16[3,512,256]{2,1,0:T(8,128)(2,1)S(1)}, bf16[3,512,256]{2,1,0:T(8,128)(2,1)S(1)}, u32[]{:S(2)}, u32[]{:S(2)}) collective-permute-start(bf16[3,512,256]{2,1,0:T(8,128)(2,1)S(1)} %collective-permute-done.29.refs_1_), channel_id=1, source_target_pairs={{4,8},{5,9},{6,10},{7,11},{8,4},{9,5},{10,6},{11,7},{20,24},{21,25... | collective-permute-start | bytes 2359304 | tf_op jit(solution)/shard_map/ppermute | solution.py:460
  151.9 20.7 %collective-permute-start.35 = (bf16[3,512,256]{2,1,0:T(8,128)(2,1)S(1)}, bf16[3,512,256]{2,1,0:T(8,128)(2,1)S(1)}, u32[]{:S(2)}, u32[]{:S(2)}) collective-permute-start(bf16[3,512,256]{2,1,0:T(8,128)(2,1)S(1)} %collective-permute-done.27), channel_id=1, source_target_pairs={{4,0},{5,1},{6,2},{7,3},{8,12},{9,13},{10,14},{11,15},{20,16},{21,... | collective-permute-start | bytes 2359304 | tf_op jit(solution)/shard_map/ppermute | solution.py:460
  153.2 19.4 %collective-permute-start.34 = (bf16[3,512,256]{2,1,0:T(8,128)(2,1)S(1)}, bf16[3,512,256]{2,1,0:T(8,128)(2,1)S(1)}, u32[]{:S(2)}, u32[]{:S(2)}) collective-permute-start(bf16[3,512,256]{2,1,0:T(8,128)(2,1)S(1)} %collective-permute-done.29.refs_1_), channel_id=1, source_target_pairs={{0,2},{1,3},{2,0},{3,1},{4,6},{5,7},{6,4},{7,5},{8,10},{9,11},{10,... | collective-permute-start | bytes 2359304 | tf_op jit(solution)/shard_map/ppermute | solution.py:460
  153.5 17.3 %collective-permute-start.32 = (bf16[1,256,1024]{2,1,0:T(8,128)(2,1)S(1)}, bf16[1,256,1024]{2,1,0:T(8,128)(2,1)S(1)}, u32[]{:S(2)}, u32[]{:S(2)}) collective-permute-start(bf16[1,256,1024]{2,1,0:T(8,128)(2,1)S(1)} %get-tuple-element.156.refs_0_), channel_id=1, source_target_pairs={{0,4},{1,5},{2,6},{3,7},{12,8},{13,9},{14,10},{15,11},{16,20},{17,... | collective-permute-start | bytes 1572872 | tf_op jit(solution)/shard_map/ppermute | solution.py:460
  170.9 19.7 %collective-permute-start.33 = (bf16[2,1,256,1024]{3,2,1,0:T(8,128)(2,1)S(1)}, bf16[2,1,256,1024]{3,2,1,0:T(8,128)(2,1)S(1)}, u32[]{:S(2)}, u32[]{:S(2)}) collective-permute-start(bf16[2,1,256,1024]{3,2,1,0:T(8,128)(2,1)S(1)} %stack.21), channel_id=1, source_target_pairs={{4,8},{5,9},{6,10},{7,11},{8,4},{9,5},{10,6},{11,7},{20,24},{21,25... | collective-permute-start | bytes 3145736 | tf_op jit(solution)/shard_map/ppermute | solution.py:460
  172.6 18.0 %collective-permute-start.36 = (bf16[1664,256]{1,0:T(8,128)(2,1)S(1)}, bf16[1664,256]{1,0:T(8,128)(2,1)S(1)}, u32[]{:S(2)}, u32[]{:S(2)}) collective-permute-start(bf16[1664,256]{1,0:T(8,128)(2,1)S(1)} %pack.1), channel_id=1, source_target_pairs={{0,4},{1,5},{2,6},{3,7},{4,0},{5,1},{6,2},{7,3},{8,12},{9,13},{10,... | collective-permute-start | bytes 2555912 | tf_op jit(solution)/shard_map/ppermute | solution.py:460
  176.3 15.6 %collective-permute-start.40 = (bf16[3,512,256]{2,1,0:T(8,128)(2,1)S(1)}, bf16[3,512,256]{2,1,0:T(8,128)(2,1)S(1)}, u32[]{:S(2)}, u32[]{:S(2)}) collective-permute-start(bf16[3,512,256]{2,1,0:T(8,128)(2,1)S(1)} %choose.8.refs_1_), channel_id=1, source_target_pairs={{0,2},{1,3},{2,0},{3,1},{4,6},{5,7},{6,4},{7,5},{8,10},{9,11},{10,... | collective-permute-start | bytes 2359304 | tf_op jit(solution)/shard_map/ppermute | solution.py:460
  176.4 7.1 %collective-permute-start.37 = (bf16[640,256]{1,0:T(8,128)(2,1)S(1)}, bf16[640,256]{1,0:T(8,128)(2,1)S(1)}, u32[]{:S(2)}, u32[]{:S(2)}) collective-permute-start(bf16[640,256]{1,0:T(8,128)(2,1)S(1)} %attend.2.piece_ref.refs_0_), channel_id=1, source_target_pairs={{0,1},{1,0},{2,3},{3,2},{4,5},{5,4},{6,7},{7,6},{8,9},{9,8},{10,11... | collective-permute-start | bytes 983048 | tf_op jit(solution)/shard_map/ppermute | solution.py:460
  190.6 26.6 %collective-permute-start.38 = (bf16[2,1,256,1024]{3,2,1,0:T(8,128)(2,1)S(1)}, bf16[2,1,256,1024]{3,2,1,0:T(8,128)(2,1)S(1)}, u32[]{:S(2)}, u32[]{:S(2)}) collective-permute-start(bf16[2,1,256,1024]{3,2,1,0:T(8,128)(2,1)S(1)} %collective-permute-done.33), channel_id=1, source_target_pairs={{4,0},{5,1},{6,2},{7,3},{8,12},{9,13},{10,14},{11,15},{20,16},{21,... | collective-permute-start | bytes 3145736 | tf_op jit(solution)/shard_map/ppermute | solution.py:460
  193.7 23.5 %collective-permute-start.39 = (bf16[2,1,256,1024]{3,2,1,0:T(8,128)(2,1)S(1)}, bf16[2,1,256,1024]{3,2,1,0:T(8,128)(2,1)S(1)}, u32[]{:S(2)}, u32[]{:S(2)}) collective-permute-start(bf16[2,1,256,1024]{3,2,1,0:T(8,128)(2,1)S(1)} %stack.22), channel_id=1, source_target_pairs={{4,8},{5,9},{6,10},{7,11},{8,4},{9,5},{10,6},{11,7},{20,24},{21,25... | collective-permute-start | bytes 3145736 | tf_op jit(solution)/shard_map/ppermute | solution.py:460
  197.4 19.8 %collective-permute-start.44 = (bf16[1,256,1024]{2,1,0:T(8,128)(2,1)S(1)}, bf16[1,256,1024]{2,1,0:T(8,128)(2,1)S(1)}, u32[]{:S(2)}, u32[]{:S(2)}) collective-permute-start(bf16[1,256,1024]{2,1,0:T(8,128)(2,1)S(1)} %choose.9.refs_6_.refs_18_), channel_id=1, source_target_pairs={{0,2},{1,3},{2,0},{3,1},{4,6},{5,7},{6,4},{7,5},{8,10},{9,11},{10,... | collective-permute-start | bytes 1572872 | tf_op jit(solution)/shard_map/ppermute | solution.py:460
  197.8 19.5 %collective-permute-start.43 = (bf16[640,256]{1,0:T(8,128)(2,1)S(1)}, bf16[640,256]{1,0:T(8,128)(2,1)S(1)}, u32[]{:S(2)}, u32[]{:S(2)}) collective-permute-start(bf16[640,256]{1,0:T(8,128)(2,1)S(1)} %get-tuple-element.163.refs_2_), channel_id=1, source_target_pairs={{0,1},{1,0},{2,3},{3,2},{4,5},{5,4},{6,7},{7,6},{8,9},{9,8},{10,11... | collective-permute-start | bytes 983048 | tf_op jit(solution)/shard_map/ppermute | solution.py:460
  203.0 14.2 %collective-permute-start.42 = (bf16[640,256]{1,0:T(8,128)(2,1)S(1)}, bf16[640,256]{1,0:T(8,128)(2,1)S(1)}, u32[]{:S(2)}, u32[]{:S(2)}) collective-permute-start(bf16[640,256]{1,0:T(8,128)(2,1)S(1)} %attend.3.refs_0_), channel_id=1, source_target_pairs={{0,1},{1,0},{2,3},{3,2},{4,5},{5,4},{6,7},{7,6},{8,9},{9,8},{10,11... | collective-permute-start | bytes 983048 | tf_op jit(solution)/shard_map/ppermute | solution.py:460
  217.2 7.1 %collective-permute-start.45 = (bf16[640,256]{1,0:T(8,128)(2,1)S(1)}, bf16[640,256]{1,0:T(8,128)(2,1)S(1)}, u32[]{:S(2)}, u32[]{:S(2)}) collective-permute-start(bf16[640,256]{1,0:T(8,128)(2,1)S(1)} %attend.3.refs_0_), channel_id=1, source_target_pairs={{0,4},{1,5},{2,6},{3,7},{4,0},{5,1},{6,2},{7,3},{8,12},{9,13},{10,... | collective-permute-start | bytes 983048 | tf_op jit(solution)/shard_map/ppermute | solution.py:460
  226.4 13.9 %collective-permute-start.50 = (bf16[2,1,256,512]{3,2,1,0:T(8,128)(2,1)S(1)}, bf16[2,1,256,512]{3,2,1,0:T(8,128)(2,1)S(1)}, u32[]{:S(2)}, u32[]{:S(2)}) collective-permute-start(bf16[2,1,256,512]{3,2,1,0:T(8,128)(2,1)S(1)} %get-tuple-element.168.refs_12_.refs_14_.refs_20_.refs_22_), channel_id=1, source_target_pairs={{0,2},{1,3},{2,0},{3,1},{4,6},{5,7},{6,4},{7,5},{8,10},{9,11},{10,... | collective-permute-start | bytes 1572872 | tf_op jit(solution)/shard_map/ppermute | solution.py:460
  229.4 9.8 %collective-permute-start.51 = (bf16[640,256]{1,0:T(8,128)(2,1)S(1)}, bf16[640,256]{1,0:T(8,128)(2,1)S(1)}, u32[]{:S(2)}, u32[]{:S(2)}) collective-permute-start(bf16[640,256]{1,0:T(8,128)(2,1)S(1)} %collective-permute-done.45.refs_2_), channel_id=1, source_target_pairs={{0,1},{1,0},{2,3},{3,2},{4,5},{5,4},{6,7},{7,6},{8,9},{9,8},{10,11... | collective-permute-start | bytes 983048 | tf_op jit(solution)/shard_map/ppermute | solution.py:460
  244.5 14.2 %collective-permute-start.53 = (bf16[2,1,256,512]{3,2,1,0:T(8,128)(2,1)S(1)}, bf16[2,1,256,512]{3,2,1,0:T(8,128)(2,1)S(1)}, u32[]{:S(2)}, u32[]{:S(2)}) collective-permute-start(bf16[2,1,256,512]{3,2,1,0:T(8,128)(2,1)S(1)} %get-tuple-element.178.refs_12_.refs_14_.refs_20_.refs_22_), channel_id=1, source_target_pairs={{0,2},{1,3},{2,0},{3,1},{4,6},{5,7},{6,4},{7,5},{8,10},{9,11},{10,... | collective-permute-start | bytes 1572872 | tf_op jit(solution)/shard_map/ppermute | solution.py:460
  246.8 9.8 %collective-permute-start.55 = (bf16[320,512]{1,0:T(8,128)(2,1)S(1)}, bf16[320,512]{1,0:T(8,128)(2,1)S(1)}, u32[]{:S(2)}, u32[]{:S(2)}) collective-permute-start(bf16[320,512]{1,0:T(8,128)(2,1)S(1)} %join.2), channel_id=1, source_target_pairs={{0,4},{1,5},{2,6},{3,7},{4,0},{5,1},{6,2},{7,3},{8,12},{9,13},{10,... | collective-permute-start | bytes 983048 | tf_op jit(solution)/shard_map/ppermute | solution.py:460
  263.0 9.8 %collective-permute-start.60 = (bf16[320,512]{1,0:T(8,128)(2,1)S(1)}, bf16[320,512]{1,0:T(8,128)(2,1)S(1)}, u32[]{:S(2)}, u32[]{:S(2)}) collective-permute-start(bf16[320,512]{1,0:T(8,128)(2,1)S(1)} %join.3), channel_id=1, source_target_pairs={{0,4},{1,5},{2,6},{3,7},{4,0},{5,1},{6,2},{7,3},{8,12},{9,13},{10,... | collective-permute-start | bytes 983048 | tf_op jit(solution)/shard_map/ppermute | solution.py:460
  265.7 7.1 %collective-permute-start.59 = (bf16[640,512]{1,0:T(8,128)(2,1)S(1)}, bf16[640,512]{1,0:T(8,128)(2,1)S(1)}, u32[]{:S(2)}, u32[]{:S(2)}) collective-permute-start(bf16[640,512]{1,0:T(8,128)(2,1)S(1)} %combine.9.refs_4_), channel_id=1, source_target_pairs={{0,16},{1,17},{2,18},{3,19},{4,20},{5,21},{6,22},{7,23},{8,24},{9,... | collective-permute-start | bytes 1966088 | tf_op jit(solution)/shard_map/ppermute | solution.py:460
  (20 other events, 205.3 us)

commit v18 on v17

--- a/solution.py
+++ b/solution.py
@@ -64,6 +64,34 @@
             away_ref[kind] = jnp.where(outer, high, low)
 
     return call("halves", kernel, here, [weight], [shaped((kinds, depth, part))] * 4)
+
+
+def fetched_halves(here, weight, chunk, chunks):
+    kinds, depth, width = weight.shape
+    half = width // 2
+    part = half // chunks
+
+    def kernel(h_ref, in_ref, low_ref, high_ref, mine_ref, away_ref, sems):
+        copies = []
+        for i, ref in enumerate((low_ref, high_ref)):
+            columns = pl.ds(i * half + chunk * part, part)
+            copies.append(pltpu.make_async_copy(in_ref.at[:, :, columns], ref, sems.at[i]))
+            copies[-1].start()
+        for copy in copies:
+            copy.wait()
+        outer = Here(h_ref).outer
+        mine_ref[...] = jnp.where(outer, low_ref[...], high_ref[...])
+        away_ref[...] = jnp.where(outer, high_ref[...], low_ref[...])
+
+    return pl.pallas_call(
+        kernel,
+        in_specs=[pl.BlockSpec(memory_space=SMEM), pl.BlockSpec(memory_space=pl.ANY)],
+        out_specs=[pl.BlockSpec(memory_space=VMEM)] * 4,
+        out_shape=[VMEM((kinds, depth, part), weight.dtype)] * 4,
+        scratch_shapes=[pltpu.SemaphoreType.DMA((2,))],
+        compiler_params=pltpu.CompilerParams(vmem_limit_bytes=60 * 2**20),
+        name="fetched_halves",
+    )(here, weight)
 
 
 def own_rows_of(here, tokens, kind):
@@ -495,7 +523,7 @@
         own_kind = modality[None, :]
 
         weight = after(qkv_weight[0].transpose(1, 0, 2), here, gains, own_kind)
-        low_a, high_a, mine_a, away_a = halves(here, weight, 0, 2)
+        low_a, high_a, mine_a, away_a = fetched_halves(here, weight, 0, 2)
         m1a = move(low_a, across_or_stay)
         e1a = move(away_a, edge)
         p1a = move(mine_a, pair)

time: 277 us -> 278 us (level)
    pallas_call x40 -> x39, Pallas kernels: 61.9 us -> 61.1 us  [call(): pl.pallas_call(kernel, in_specs=[pl.BlockSpec(memory_space=SMEM)] + [pl.B...]
where the time goes in v18:
time: 278 us; the launch traced here: 277 us
  waiting for transfers between devices  137 us (49%)
  starting transfers between devices  68.4 us (25%)
  Pallas kernels  65.7 us (24%)
  local copies, waits for them, and re-layouts  4.92 us (2%)
    ppermute x62, waiting for transfers between devices, move(): lax.ppermute(after(array, *earlier) if earlier else array, AXES, pairs)  137 us
    ppermute x62, starting transfers between devices, move(): lax.ppermute(after(array, *earlier) if earlier else array, AXES, pairs)  68.4 us
    pallas_call x39, Pallas kernels, call(): pl.pallas_call(kernel, in_specs=[pl.BlockSpec(memory_space=SMEM)] + [pl.B...  61.1 us
  transfers between devices with their start and end apart: 62, of which 32 were waited for; matrix products, arithmetic and copies ran while one was open for 0% of the time, Pallas kernels for 20%

profile of v18, /device:TPU:0, one launch (start us, length us, event | category | flops | bytes accessed | tf_op | source)
XLA Modules:
  0.0 277.0 jit_solution(8068711339157358477)
XLA Ops:
  1.3 2.2 fetched_halves.1
  3.5 3.0 %collective-permute-start.2 = (bf16[3,512,256]{2,1,0:T(8,128)(2,1)S(1)}, bf16[3,512,256]{2,1,0:T(8,128)(2,1)S(1)}, u32[]{:S(2)}, u32[]{:S(2)}) collective-permute-start(bf16[3,512,256]{2,1,0:T(8,128)(2,1)S(1)} %get-tuple-element.101.refs_1_), channel_id=1, source_target_pairs={{0,2},{1,3},{2,0},{3,1},{4,6},{5,7},{6,4},{7,5},{8,10},{9,11},{10,... | collective-permute-start | bytes 2359304 | tf_op jit(solution)/shard_map/ppermute | solution.py:488
  8.8 15.3 %collective-permute-done.2.refs_2_ = bf16[3,512,256]{2,1,0:T(8,128)(2,1)S(1)} collective-permute-done((bf16[3,512,256]{2,1,0:T(8,128)(2,1)S(1)}, bf16[3,512,256]{2,1,0:T(8,128)(2,1)S(1)}, u32[]{:S(2)}, u32[]{:S(2)}) %collective-permute-start.2) | collective-permute-done | bytes 786464 | tf_op jit(solution)/shard_map/ppermute | solution.py:488
  26.7 7.7 %collective-permute-start.3 = (bf16[3,512,256]{2,1,0:T(8,128)(2,1)S(1)}, bf16[3,512,256]{2,1,0:T(8,128)(2,1)S(1)}, u32[]{:S(2)}, u32[]{:S(2)}) collective-permute-start(bf16[3,512,256]{2,1,0:T(8,128)(2,1)S(1)} %collective-permute-done), channel_id=1, source_target_pairs={{0,4},{1,5},{2,6},{3,7},{4,0},{5,1},{6,2},{7,3},{8,12},{9,13},{10,... | collective-permute-start | bytes 2359304 | tf_op jit(solution)/shard_map/ppermute | solution.py:488
  34.3 1.7 copy-done.1
  39.0 1.9 copy-done
  41.7 2.7 collective-permute-done.4.refs_4_
  44.4 5.4 %collective-permute-done.3.a_ref = bf16[3,512,256]{2,1,0:T(8,128)(2,1)S(1)} collective-permute-done((bf16[3,512,256]{2,1,0:T(8,128)(2,1)S(1)}, bf16[3,512,256]{2,1,0:T(8,128)(2,1)S(1)}, u32[]{:S(2)}, u32[]{:S(2)}) %collective-permute-start.3) | collective-permute-done | bytes 786464 | tf_op jit(solution)/shard_map/ppermute | solution.py:488
  52.7 3.5 %collective-permute-start.6 = (bf16[160,2048]{1,0:T(8,128)(2,1)S(1)}, bf16[160,2048]{1,0:T(8,128)(2,1)S(1)}, u32[]{:S(2)}, u32[]{:S(2)}) collective-permute-start(bf16[160,2048]{1,0:T(8,128)(2,1)S(1)} %get-tuple-element.108), channel_id=1, source_target_pairs={{0,4},{1,5},{2,6},{3,7},{4,0},{5,1},{6,2},{7,3},{8,12},{9,13},{10,... | collective-permute-start | bytes 1966088 | tf_op jit(solution)/shard_map/ppermute | solution.py:488
  56.3 9.4 %collective-permute-done.10.refs_2_ = bf16[320,2048]{1,0:T(8,128)(2,1)S(1)} collective-permute-done((bf16[320,2048]{1,0:T(8,128)(2,1)S(1)}, bf16[320,2048]{1,0:T(8,128)(2,1)S(1)}, u32[]{:S(2)}, u32[]{:S(2)}) %collective-permute-start.10) | collective-permute-done | bytes 1310752 | tf_op jit(solution)/shard_map/ppermute | solution.py:488
  65.7 2.1 collective-permute-done.6.refs_2_
  67.8 3.3 %collective-permute-start.9 = (bf16[176,2048]{1,0:T(8,128)(2,1)S(1)}, bf16[176,2048]{1,0:T(8,128)(2,1)S(1)}, u32[]{:S(2)}, u32[]{:S(2)}) collective-permute-start(bf16[176,2048]{1,0:T(8,128)(2,1)S(1)} %get-tuple-element.112), channel_id=1, source_target_pairs={{0,4},{1,5},{2,6},{3,7},{4,0},{5,1},{6,2},{7,3},{8,12},{9,13},{10,... | collective-permute-start | bytes 2162696 | tf_op jit(solution)/shard_map/ppermute | solution.py:488
  76.3 3.2 %normalize.3.refs_0_ = bf16[2,8,640,512]{3,2,1,0:T(8,128)(2,1)S(1)} custom-call(s32[3]{0:T(128)S(1)} %copy-done.4, f32[8,1,512]{2,1,0:T(1,128)S(1)} %bitcast.9, bf16[640,2048]{1,0:T(8,128)(2,1)S(1)} %copy-done.2, bf16[320,2048]{1,0:T(8,128)(2,1)S(1)} %collective-permute-done.10.refs_2_, bf16[320,2048]{1,0:T(8,128)(2,1)S(1)} %collective-permute-done.11.refs_3_), custom_call_target="tpu_custom_call" | custom-call | tf_op jit(solution)/shard_map/normalize/pallas_call | solution.py:32
  79.5 7.2 %collective-permute-done.12.refs_3_ = bf16[160,2048]{1,0:T(8,128)(2,1)S(1)} collective-permute-done((bf16[160,2048]{1,0:T(8,128)(2,1)S(1)}, bf16[160,2048]{1,0:T(8,128)(2,1)S(1)}, u32[]{:S(2)}, u32[]{:S(2)}) %collective-permute-start.12) | collective-permute-done | bytes 655392 | tf_op jit(solution)/shard_map/ppermute | solution.py:488
  87.9 2.8 %collective-permute-done.22.refs_2_ = bf16[3,512,256]{2,1,0:T(8,128)(2,1)S(1)} collective-permute-done((bf16[3,512,256]{2,1,0:T(8,128)(2,1)S(1)}, bf16[3,512,256]{2,1,0:T(8,128)(2,1)S(1)}, u32[]{:S(2)}, u32[]{:S(2)}) %collective-permute-start.22) | collective-permute-done | bytes 786464 | tf_op jit(solution)/shard_map/ppermute | solution.py:488
  94.1 4.6 %collective-permute-start.25 = (bf16[1,256,1024]{2,1,0:T(8,128)(2,1)S(1)}, bf16[1,256,1024]{2,1,0:T(8,128)(2,1)S(1)}, u32[]{:S(2)}, u32[]{:S(2)}) collective-permute-start(bf16[1,256,1024]{2,1,0:T(8,128)(2,1)S(1)} %get-tuple-element.153.refs_0_.block_ref), channel_id=1, source_target_pairs={{0,4},{1,5},{2,6},{3,7},{12,8},{13,9},{14,10},{15,11},{16,20},{17,... | collective-permute-start | bytes 1572872 | tf_op jit(solution)/shard_map/ppermute | solution.py:488
  99.3 3.7 %project.10.refs_7_ = f32[2,640,768]{2,1,0:T(8,128)S(1)} custom-call(s32[3]{0:T(128)S(1)} %copy-done.4, bf16[2,8,640,512]{3,2,1,0:T(8,128)(2,1)S(1)} %normalize.3.refs_0_, bf16[3,512,256]{2,1,0:T(8,128)(2,1)S(1)} %get-tuple-element.101.refs_1_, bf16[3,512,256]{2,1,0:T(8,128)(2,1)S(1)} %collective-permute-done.2.refs_2_, ...), custom_call_target="tpu_custom_call" | custom-call | tf_op jit(solution)/shard_map/project/pallas_call | solution.py:32
  103.0 1.8 normalize.4.refs_0_
  105.6 4.8 %collective-permute-done.21.a_ref = bf16[3,512,256]{2,1,0:T(8,128)(2,1)S(1)} collective-permute-done((bf16[3,512,256]{2,1,0:T(8,128)(2,1)S(1)}, bf16[3,512,256]{2,1,0:T(8,128)(2,1)S(1)}, u32[]{:S(2)}, u32[]{:S(2)}) %collective-permute-start.21) | collective-permute-done | bytes 786464 | tf_op jit(solution)/shard_map/ppermute | solution.py:488
  110.4 3.5 %collective-permute-start.26 = (bf16[3,512,256]{2,1,0:T(8,128)(2,1)S(1)}, bf16[3,512,256]{2,1,0:T(8,128)(2,1)S(1)}, u32[]{:S(2)}, u32[]{:S(2)}) collective-permute-start(bf16[3,512,256]{2,1,0:T(8,128)(2,1)S(1)} %collective-permute-done.17), channel_id=1, source_target_pairs={{0,4},{1,5},{2,6},{3,7},{4,0},{5,1},{6,2},{7,3},{8,12},{9,13},{10,... | collective-permute-start | bytes 2359304 | tf_op jit(solution)/shard_map/ppermute | solution.py:488
  118.5 1.8 normalize.5.refs_0_
  120.3 3.7 %project.11.refs_3_ = f32[2,640,768]{2,1,0:T(8,128)S(1)} custom-call(s32[3]{0:T(128)S(1)} %copy-done.4, bf16[2,8,640,512]{3,2,1,0:T(8,128)(2,1)S(1)} %normalize.5.refs_0_, bf16[3,512,256]{2,1,0:T(8,128)(2,1)S(1)} %get-tuple-element.101.refs_1_, bf16[3,512,256]{2,1,0:T(8,128)(2,1)S(1)} %collective-permute-done.2.refs_2_, ...), custom_call_target="tpu_custom_call", output_to_operand_aliasing={{}: (8, {})} | custom-call | tf_op jit(solution)/shard_map/project/pallas_call | solution.py:32
  124.1 6.7 %collective-permute-done.26.a_ref = bf16[3,512,256]{2,1,0:T(8,128)(2,1)S(1)} collective-permute-done((bf16[3,512,256]{2,1,0:T(8,128)(2,1)S(1)}, bf16[3,512,256]{2,1,0:T(8,128)(2,1)S(1)}, u32[]{:S(2)}, u32[]{:S(2)}) %collective-permute-start.26) | collective-permute-done | bytes 786464 | tf_op jit(solution)/shard_map/ppermute | solution.py:488
  130.7 2.1 collective-permute-done.24.refs_2_
  138.5 11.7 %collective-permute-done.29.refs_1_ = bf16[3,512,256]{2,1,0:T(8,128)(2,1)S(1)} collective-permute-done((bf16[3,512,256]{2,1,0:T(8,128)(2,1)S(1)}, bf16[3,512,256]{2,1,0:T(8,128)(2,1)S(1)}, u32[]{:S(2)}, u32[]{:S(2)}) %collective-permute-start.29) | collective-permute-done | bytes 786464 | tf_op jit(solution)/shard_map/ppermute | solution.py:488
  153.6 7.1 %collective-permute-start.32 = (bf16[1,256,1024]{2,1,0:T(8,128)(2,1)S(1)}, bf16[1,256,1024]{2,1,0:T(8,128)(2,1)S(1)}, u32[]{:S(2)}, u32[]{:S(2)}) collective-permute-start(bf16[1,256,1024]{2,1,0:T(8,128)(2,1)S(1)} %get-tuple-element.156.refs_0_), channel_id=1, source_target_pairs={{0,4},{1,5},{2,6},{3,7},{12,8},{13,9},{14,10},{15,11},{16,20},{17,... | collective-permute-start | bytes 1572872 | tf_op jit(solution)/shard_map/ppermute | solution.py:488
  161.3 2.7 project.14.refs_5_
  164.0 2.7 project.15.refs_3_
  166.7 4.2 %attend.2.piece_ref.refs_0_ = bf16[640,256]{1,0:T(8,128)(2,1)S(1)} custom-call(s32[3]{0:T(128)S(1)} %copy-done.4, s32[1,640]{1,0:T(1,128)S(1)} %broadcast_in_dim.3.kind_ref.own_kind_ref, s32[1,640]{1,0:T(1,128)S(1)} %kinds_behind.1.other_kind_ref.kind_ref, bf16[640,768]{1,0:T(8,128)(2,1)S(1)} %project.12.own_ref, ...), custom_call_target="tpu_custom_call" | custom-call | tf_op jit(solution)/shard_map/attend/pallas_call | solution.py:32
  172.6 3.1 %collective-permute-start.36 = (bf16[1664,256]{1,0:T(8,128)(2,1)S(1)}, bf16[1664,256]{1,0:T(8,128)(2,1)S(1)}, u32[]{:S(2)}, u32[]{:S(2)}) collective-permute-start(bf16[1664,256]{1,0:T(8,128)(2,1)S(1)} %pack.1), channel_id=1, source_target_pairs={{0,4},{1,5},{2,6},{3,7},{4,0},{5,1},{6,2},{7,3},{8,12},{9,13},{10,... | collective-permute-start | bytes 2555912 | tf_op jit(solution)/shard_map/ppermute | solution.py:488
  178.4 1.9 project.16.refs_3_
  180.3 1.9 project.17.refs_3_
  183.5 7.1 %collective-permute-done.36.in_ref = bf16[1664,256]{1,0:T(8,128)(2,1)S(1)} collective-permute-done((bf16[1664,256]{1,0:T(8,128)(2,1)S(1)}, bf16[1664,256]{1,0:T(8,128)(2,1)S(1)}, u32[]{:S(2)}, u32[]{:S(2)}) %collective-permute-start.36) | collective-permute-done | bytes 852000 | tf_op jit(solution)/shard_map/ppermute | solution.py:488
  191.9 1.7 project.19
  198.9 4.1 %attend.3.refs_0_ = bf16[640,256]{1,0:T(8,128)(2,1)S(1)} custom-call(s32[3]{0:T(128)S(1)} %copy-done.4, s32[1,640]{1,0:T(1,128)S(1)} %broadcast_in_dim.3.kind_ref.own_kind_ref, s32[1,640]{1,0:T(1,128)S(1)} %kinds_behind.1.other_kind_ref.kind_ref, bf16[640,768]{1,0:T(8,128)(2,1)S(1)} %project.18.own_ref, bf16[640,768]{1,0:T(8,128)(2,1)S(1)} %collective-permute-done.41.got_ref), custom_call_target="tpu_custom_call" | custom-call | tf_op jit(solution)/shard_map/attend/pallas_call | solution.py:32
  204.0 13.2 %collective-permute-done.38.a_ref = bf16[2,1,256,1024]{3,2,1,0:T(8,128)(2,1)S(1)} collective-permute-done((bf16[2,1,256,1024]{3,2,1,0:T(8,128)(2,1)S(1)}, bf16[2,1,256,1024]{3,2,1,0:T(8,128)(2,1)S(1)}, u32[]{:S(2)}, u32[]{:S(2)}) %collective-permute-start.38) | collective-permute-done | bytes 1048608 | tf_op jit(solution)/shard_map/ppermute | solution.py:488
  217.3 7.0 %collective-permute-done.45.refs_2_ = bf16[640,256]{1,0:T(8,128)(2,1)S(1)} collective-permute-done((bf16[640,256]{1,0:T(8,128)(2,1)S(1)}, bf16[640,256]{1,0:T(8,128)(2,1)S(1)}, u32[]{:S(2)}, u32[]{:S(2)}) %collective-permute-start.45) | collective-permute-done | bytes 327712 | tf_op jit(solution)/shard_map/ppermute | solution.py:488
  227.0 2.4 collective-permute-done.49.refs_2_
  230.3 2.1 combine.5.refs_24_
  232.4 6.7 %collective-permute-done.51.refs_3_ = bf16[640,256]{1,0:T(8,128)(2,1)S(1)} collective-permute-done((bf16[640,256]{1,0:T(8,128)(2,1)S(1)}, bf16[640,256]{1,0:T(8,128)(2,1)S(1)}, u32[]{:S(2)}, u32[]{:S(2)}) %collective-permute-start.51) | collective-permute-done | bytes 327712 | tf_op jit(solution)/shard_map/ppermute | solution.py:488
  242.6 1.8 combine.6
  247.9 8.8 %collective-permute-done.55.refs_2_ = bf16[320,512]{1,0:T(8,128)(2,1)S(1)} collective-permute-done((bf16[320,512]{1,0:T(8,128)(2,1)S(1)}, bf16[320,512]{1,0:T(8,128)(2,1)S(1)}, u32[]{:S(2)}, u32[]{:S(2)}) %collective-permute-start.55) | collective-permute-done | bytes 327712 | tf_op jit(solution)/shard_map/ppermute | solution.py:488
  256.7 2.1 collective-permute-done.53.refs_13_.refs_15_.refs_21_.refs_23_
  258.7 1.7 combine.7
  264.0 1.7 combine.9.refs_4_
  265.8 1.7 combine.8.refs_0_
  268.2 4.6 %collective-permute-done.60.refs_6_ = bf16[320,512]{1,0:T(8,128)(2,1)S(1)} collective-permute-done((bf16[320,512]{1,0:T(8,128)(2,1)S(1)}, bf16[320,512]{1,0:T(8,128)(2,1)S(1)}, u32[]{:S(2)}, u32[]{:S(2)}) %collective-permute-start.60) | collective-permute-done | bytes 327712 | tf_op jit(solution)/shard_map/ppermute | solution.py:488
  274.4 2.4 assemble.1
  (131 shorter events, 67.4 us)
Async XLA Ops:
  3.5 20.6 %collective-permute-start.2 = (bf16[3,512,256]{2,1,0:T(8,128)(2,1)S(1)}, bf16[3,512,256]{2,1,0:T(8,128)(2,1)S(1)}, u32[]{:S(2)}, u32[]{:S(2)}) collective-permute-start(bf16[3,512,256]{2,1,0:T(8,128)(2,1)S(1)} %get-tuple-element.101.refs_1_), channel_id=1, source_target_pairs={{0,2},{1,3},{2,0},{3,1},{4,6},{5,7},{6,4},{7,5},{8,10},{9,11},{10,... | collective-permute-start | bytes 2359304 | tf_op jit(solution)/shard_map/ppermute | solution.py:488
  6.5 19.0 %collective-permute-start.1 = (bf16[3,512,256]{2,1,0:T(8,128)(2,1)S(1)}, bf16[3,512,256]{2,1,0:T(8,128)(2,1)S(1)}, u32[]{:S(2)}, u32[]{:S(2)}) collective-permute-start(bf16[3,512,256]{2,1,0:T(8,128)(2,1)S(1)} %get-tuple-element.100), channel_id=1, source_target_pairs={{0,4},{1,5},{2,6},{3,7},{4,0},{5,1},{6,2},{7,3},{8,12},{9,13},{10,... | collective-permute-start | bytes 2359304 | tf_op jit(solution)/shard_map/ppermute | solution.py:488
  8.1 17.4 %collective-permute-start = (bf16[3,512,256]{2,1,0:T(8,128)(2,1)S(1)}, bf16[3,512,256]{2,1,0:T(8,128)(2,1)S(1)}, u32[]{:S(2)}, u32[]{:S(2)}) collective-permute-start(bf16[3,512,256]{2,1,0:T(8,128)(2,1)S(1)} %get-tuple-element.96), channel_id=1, source_target_pairs={{0,0},{1,1},{2,2},{3,3},{4,8},{5,9},{6,10},{7,11},{8,4},{9,5},{10,... | collective-permute-start | bytes 2359304 | tf_op jit(solution)/shard_map/ppermute | solution.py:488
  25.5 16.1 %collective-permute-start.5 = (bf16[3,512,256]{2,1,0:T(8,128)(2,1)S(1)}, bf16[3,512,256]{2,1,0:T(8,128)(2,1)S(1)}, u32[]{:S(2)}, u32[]{:S(2)}) collective-permute-start(bf16[3,512,256]{2,1,0:T(8,128)(2,1)S(1)} %get-tuple-element.105), channel_id=1, source_target_pairs={{4,8},{5,9},{6,10},{7,11},{8,4},{9,5},{10,6},{11,7},{20,24},{21,25... | collective-permute-start | bytes 2359304 | tf_op jit(solution)/shard_map/ppermute | solution.py:488
  26.2 18.2 %collective-permute-start.4 = (bf16[3,512,256]{2,1,0:T(8,128)(2,1)S(1)}, bf16[3,512,256]{2,1,0:T(8,128)(2,1)S(1)}, u32[]{:S(2)}, u32[]{:S(2)}) collective-permute-start(bf16[3,512,256]{2,1,0:T(8,128)(2,1)S(1)} %collective-permute-done.1.refs_3_), channel_id=1, source_target_pairs={{0,2},{1,3},{2,0},{3,1},{4,6},{5,7},{6,4},{7,5},{8,10},{9,11},{10,... | collective-permute-start | bytes 2359304 | tf_op jit(solution)/shard_map/ppermute | solution.py:488
  26.7 23.2 %collective-permute-start.3 = (bf16[3,512,256]{2,1,0:T(8,128)(2,1)S(1)}, bf16[3,512,256]{2,1,0:T(8,128)(2,1)S(1)}, u32[]{:S(2)}, u32[]{:S(2)}) collective-permute-start(bf16[3,512,256]{2,1,0:T(8,128)(2,1)S(1)} %collective-permute-done), channel_id=1, source_target_pairs={{0,4},{1,5},{2,6},{3,7},{4,0},{5,1},{6,2},{7,3},{8,12},{9,13},{10,... | collective-permute-start | bytes 2359304 | tf_op jit(solution)/shard_map/ppermute | solution.py:488
  37.4 28.3 %collective-permute-start.10 = (bf16[320,2048]{1,0:T(8,128)(2,1)S(1)}, bf16[320,2048]{1,0:T(8,128)(2,1)S(1)}, u32[]{:S(2)}, u32[]{:S(2)}) collective-permute-start(bf16[320,2048]{1,0:T(8,128)(2,1)S(1)} %get-tuple-element.114), channel_id=1, source_target_pairs={{0,1},{1,0},{2,3},{3,2},{4,5},{5,4},{6,7},{7,6},{8,9},{9,8},{10,11... | collective-permute-start | bytes 3932168 | tf_op jit(solution)/shard_map/ppermute | solution.py:488
  49.8 15.8 %collective-permute-start.8 = (bf16[3,512,256]{2,1,0:T(8,128)(2,1)S(1)}, bf16[3,512,256]{2,1,0:T(8,128)(2,1)S(1)}, u32[]{:S(2)}, u32[]{:S(2)}) collective-permute-start(bf16[3,512,256]{2,1,0:T(8,128)(2,1)S(1)} %collective-permute-done.3.a_ref), channel_id=1, source_target_pairs={{4,8},{5,9},{6,10},{7,11},{8,4},{9,5},{10,6},{11,7},{20,24},{21,25... | collective-permute-start | bytes 2359304 | tf_op jit(solution)/shard_map/ppermute | solution.py:488
  51.2 16.7 %collective-permute-start.7 = (bf16[3,512,256]{2,1,0:T(8,128)(2,1)S(1)}, bf16[3,512,256]{2,1,0:T(8,128)(2,1)S(1)}, u32[]{:S(2)}, u32[]{:S(2)}) collective-permute-start(bf16[3,512,256]{2,1,0:T(8,128)(2,1)S(1)} %choose.5.refs_5_), channel_id=1, source_target_pairs={{0,2},{1,3},{2,0},{3,1},{4,6},{5,7},{6,4},{7,5},{8,10},{9,11},{10,... | collective-permute-start | bytes 2359304 | tf_op jit(solution)/shard_map/ppermute | solution.py:488
  52.7 15.0 %collective-permute-start.6 = (bf16[160,2048]{1,0:T(8,128)(2,1)S(1)}, bf16[160,2048]{1,0:T(8,128)(2,1)S(1)}, u32[]{:S(2)}, u32[]{:S(2)}) collective-permute-start(bf16[160,2048]{1,0:T(8,128)(2,1)S(1)} %get-tuple-element.108), channel_id=1, source_target_pairs={{0,4},{1,5},{2,6},{3,7},{4,0},{5,1},{6,2},{7,3},{8,12},{9,13},{10,... | collective-permute-start | bytes 1966088 | tf_op jit(solution)/shard_map/ppermute | solution.py:488
  65.7 10.6 %collective-permute-start.11 = (bf16[320,2048]{1,0:T(8,128)(2,1)S(1)}, bf16[320,2048]{1,0:T(8,128)(2,1)S(1)}, u32[]{:S(2)}, u32[]{:S(2)}) collective-permute-start(bf16[320,2048]{1,0:T(8,128)(2,1)S(1)} %collective-permute-done.10.refs_2_), channel_id=1, source_target_pairs={{0,16},{1,17},{2,18},{3,19},{4,20},{5,21},{6,22},{7,23},{8,24},{9,... | collective-permute-start | bytes 3932168 | tf_op jit(solution)/shard_map/ppermute | solution.py:488
  67.8 18.9 %collective-permute-start.9 = (bf16[176,2048]{1,0:T(8,128)(2,1)S(1)}, bf16[176,2048]{1,0:T(8,128)(2,1)S(1)}, u32[]{:S(2)}, u32[]{:S(2)}) collective-permute-start(bf16[176,2048]{1,0:T(8,128)(2,1)S(1)} %get-tuple-element.112), channel_id=1, source_target_pairs={{0,4},{1,5},{2,6},{3,7},{4,0},{5,1},{6,2},{7,3},{8,12},{9,13},{10,... | collective-permute-start | bytes 2162696 | tf_op jit(solution)/shard_map/ppermute | solution.py:488
  71.1 15.6 %collective-permute-start.12 = (bf16[160,2048]{1,0:T(8,128)(2,1)S(1)}, bf16[160,2048]{1,0:T(8,128)(2,1)S(1)}, u32[]{:S(2)}, u32[]{:S(2)}) collective-permute-start(bf16[160,2048]{1,0:T(8,128)(2,1)S(1)} %collective-permute-done.6.refs_2_), channel_id=1, source_target_pairs={{0,1},{1,0},{2,3},{3,2},{4,5},{5,4},{6,7},{7,6},{8,9},{9,8},{10,11... | collective-permute-start | bytes 1966088 | tf_op jit(solution)/shard_map/ppermute | solution.py:488
  72.6 18.1 %collective-permute-start.22 = (bf16[3,512,256]{2,1,0:T(8,128)(2,1)S(1)}, bf16[3,512,256]{2,1,0:T(8,128)(2,1)S(1)}, u32[]{:S(2)}, u32[]{:S(2)}) collective-permute-start(bf16[3,512,256]{2,1,0:T(8,128)(2,1)S(1)} %get-tuple-element.133.refs_1_), channel_id=1, source_target_pairs={{0,2},{1,3},{2,0},{3,1},{4,6},{5,7},{6,4},{7,5},{8,10},{9,11},{10,... | collective-permute-start | bytes 2359304 | tf_op jit(solution)/shard_map/ppermute | solution.py:488
  74.1 17.9 %collective-permute-start.16 = (bf16[3,512,256]{2,1,0:T(8,128)(2,1)S(1)}, bf16[3,512,256]{2,1,0:T(8,128)(2,1)S(1)}, u32[]{:S(2)}, u32[]{:S(2)}) collective-permute-start(bf16[3,512,256]{2,1,0:T(8,128)(2,1)S(1)} %collective-permute-done.1.refs_3_), channel_id=1, source_target_pairs={{4,8},{5,9},{6,10},{7,11},{8,4},{9,5},{10,6},{11,7},{20,24},{21,25... | collective-permute-start | bytes 2359304 | tf_op jit(solution)/shard_map/ppermute | solution.py:488
  86.7 7.4 %collective-permute-start.13 = (bf16[160,2048]{1,0:T(8,128)(2,1)S(1)}, bf16[160,2048]{1,0:T(8,128)(2,1)S(1)}, u32[]{:S(2)}, u32[]{:S(2)}) collective-permute-start(bf16[160,2048]{1,0:T(8,128)(2,1)S(1)} %collective-permute-done.6.refs_2_), channel_id=1, source_target_pairs={{0,16},{1,17},{2,18},{3,19},{4,20},{5,21},{6,22},{7,23},{8,24},{9,... | collective-permute-start | bytes 1966088 | tf_op jit(solution)/shard_map/ppermute | solution.py:488
  87.2 17.6 %collective-permute-start.17 = (bf16[3,512,256]{2,1,0:T(8,128)(2,1)S(1)}, bf16[3,512,256]{2,1,0:T(8,128)(2,1)S(1)}, u32[]{:S(2)}, u32[]{:S(2)}) collective-permute-start(bf16[3,512,256]{2,1,0:T(8,128)(2,1)S(1)} %get-tuple-element.124), channel_id=1, source_target_pairs={{0,0},{1,1},{2,2},{3,3},{4,8},{5,9},{6,10},{7,11},{8,4},{9,5},{10,... | collective-permute-start | bytes 2359304 | tf_op jit(solution)/shard_map/ppermute | solution.py:488
  90.7 19.7 %collective-permute-start.21 = (bf16[3,512,256]{2,1,0:T(8,128)(2,1)S(1)}, bf16[3,512,256]{2,1,0:T(8,128)(2,1)S(1)}, u32[]{:S(2)}, u32[]{:S(2)}) collective-permute-start(bf16[3,512,256]{2,1,0:T(8,128)(2,1)S(1)} %collective-permute-done.8), channel_id=1, source_target_pairs={{4,0},{5,1},{6,2},{7,3},{8,12},{9,13},{10,14},{11,15},{20,16},{21,... | collective-permute-start | bytes 2359304 | tf_op jit(solution)/shard_map/ppermute | solution.py:488
  92.0 18.4 %collective-permute-start.15 = (bf16[176,2048]{1,0:T(8,128)(2,1)S(1)}, bf16[176,2048]{1,0:T(8,128)(2,1)S(1)}, u32[]{:S(2)}, u32[]{:S(2)}) collective-permute-start(bf16[176,2048]{1,0:T(8,128)(2,1)S(1)} %collective-permute-done.9.in_ref.refs_2_), channel_id=1, source_target_pairs={{0,1},{1,0},{2,3},{3,2},{4,5},{5,4},{6,7},{7,6},{8,9},{9,8},{10,11... | collective-permute-start | bytes 2162696 | tf_op jit(solution)/shard_map/ppermute | solution.py:488
  92.6 17.8 %collective-permute-start.23 = (bf16[1,256,1024]{2,1,0:T(8,128)(2,1)S(1)}, bf16[1,256,1024]{2,1,0:T(8,128)(2,1)S(1)}, u32[]{:S(2)}, u32[]{:S(2)}) collective-permute-start(bf16[1,256,1024]{2,1,0:T(8,128)(2,1)S(1)} %get-tuple-element.134.refs_4_.refs_16_), channel_id=1, source_target_pairs={{0,2},{1,3},{2,0},{3,1},{4,6},{5,7},{6,4},{7,5},{8,10},{9,11},{10,... | collective-permute-start | bytes 1572872 | tf_op jit(solution)/shard_map/ppermute | solution.py:488
  94.1 16.3 %collective-permute-start.25 = (bf16[1,256,1024]{2,1,0:T(8,128)(2,1)S(1)}, bf16[1,256,1024]{2,1,0:T(8,128)(2,1)S(1)}, u32[]{:S(2)}, u32[]{:S(2)}) collective-permute-start(bf16[1,256,1024]{2,1,0:T(8,128)(2,1)S(1)} %get-tuple-element.153.refs_0_.block_ref), channel_id=1, source_target_pairs={{0,4},{1,5},{2,6},{3,7},{12,8},{13,9},{14,10},{15,11},{16,20},{17,... | collective-permute-start | bytes 1572872 | tf_op jit(solution)/shard_map/ppermute | solution.py:488
  104.8 19.2 %collective-permute-start.20 = (bf16[3,512,256]{2,1,0:T(8,128)(2,1)S(1)}, bf16[3,512,256]{2,1,0:T(8,128)(2,1)S(1)}, u32[]{:S(2)}, u32[]{:S(2)}) collective-permute-start(bf16[3,512,256]{2,1,0:T(8,128)(2,1)S(1)} %get-tuple-element.129), channel_id=1, source_target_pairs={{4,8},{5,9},{6,10},{7,11},{8,4},{9,5},{10,6},{11,7},{20,24},{21,25... | collective-permute-start | bytes 2359304 | tf_op jit(solution)/shard_map/ppermute | solution.py:488
  110.4 20.3 %collective-permute-start.26 = (bf16[3,512,256]{2,1,0:T(8,128)(2,1)S(1)}, bf16[3,512,256]{2,1,0:T(8,128)(2,1)S(1)}, u32[]{:S(2)}, u32[]{:S(2)}) collective-permute-start(bf16[3,512,256]{2,1,0:T(8,128)(2,1)S(1)} %collective-permute-done.17), channel_id=1, source_target_pairs={{0,4},{1,5},{2,6},{3,7},{4,0},{5,1},{6,2},{7,3},{8,12},{9,13},{10,... | collective-permute-start | bytes 2359304 | tf_op jit(solution)/shard_map/ppermute | solution.py:488
  114.5 18.4 %collective-permute-start.24 = (bf16[3,512,256]{2,1,0:T(8,128)(2,1)S(1)}, bf16[3,512,256]{2,1,0:T(8,128)(2,1)S(1)}, u32[]{:S(2)}, u32[]{:S(2)}) collective-permute-start(bf16[3,512,256]{2,1,0:T(8,128)(2,1)S(1)} %choose.6.refs_1_), channel_id=1, source_target_pairs={{0,2},{1,3},{2,0},{3,1},{4,6},{5,7},{6,4},{7,5},{8,10},{9,11},{10,... | collective-permute-start | bytes 2359304 | tf_op jit(solution)/shard_map/ppermute | solution.py:488
  132.9 17.4 %collective-permute-start.29 = (bf16[3,512,256]{2,1,0:T(8,128)(2,1)S(1)}, bf16[3,512,256]{2,1,0:T(8,128)(2,1)S(1)}, u32[]{:S(2)}, u32[]{:S(2)}) collective-permute-start(bf16[3,512,256]{2,1,0:T(8,128)(2,1)S(1)} %get-tuple-element.142), channel_id=1, source_target_pairs={{0,4},{1,5},{2,6},{3,7},{4,0},{5,1},{6,2},{7,3},{8,12},{9,13},{10,... | collective-permute-start | bytes 2359304 | tf_op jit(solution)/shard_map/ppermute | solution.py:488
  133.2 17.1 %collective-permute-start.27 = (bf16[3,512,256]{2,1,0:T(8,128)(2,1)S(1)}, bf16[3,512,256]{2,1,0:T(8,128)(2,1)S(1)}, u32[]{:S(2)}, u32[]{:S(2)}) collective-permute-start(bf16[3,512,256]{2,1,0:T(8,128)(2,1)S(1)} %collective-permute-done.26.a_ref), channel_id=1, source_target_pairs={{4,8},{5,9},{6,10},{7,11},{8,4},{9,5},{10,6},{11,7},{20,24},{21,25... | collective-permute-start | bytes 2359304 | tf_op jit(solution)/shard_map/ppermute | solution.py:488
  134.5 17.4 %collective-permute-start.31 = (bf16[3,512,256]{2,1,0:T(8,128)(2,1)S(1)}, bf16[3,512,256]{2,1,0:T(8,128)(2,1)S(1)}, u32[]{:S(2)}, u32[]{:S(2)}) collective-permute-start(bf16[3,512,256]{2,1,0:T(8,128)(2,1)S(1)} %choose.7.refs_3_), channel_id=1, source_target_pairs={{0,2},{1,3},{2,0},{3,1},{4,6},{5,7},{6,4},{7,5},{8,10},{9,11},{10,... | collective-permute-start | bytes 2359304 | tf_op jit(solution)/shard_map/ppermute | solution.py:488
  136.7 30.0 %collective-permute-start.28 = (bf16[640,768]{1,0:T(8,128)(2,1)S(1)}, bf16[640,768]{1,0:T(8,128)(2,1)S(1)}, u32[]{:S(2)}, u32[]{:S(2)}) collective-permute-start(bf16[640,768]{1,0:T(8,128)(2,1)S(1)} %project.13), channel_id=1, source_target_pairs={{0,16},{1,17},{2,18},{3,19},{4,20},{5,21},{6,22},{7,23},{8,24},{9,... | collective-permute-start | bytes 2949128 | tf_op jit(solution)/shard_map/ppermute | solution.py:488
  150.3 20.7 %collective-permute-start.30 = (bf16[3,512,256]{2,1,0:T(8,128)(2,1)S(1)}, bf16[3,512,256]{2,1,0:T(8,128)(2,1)S(1)}, u32[]{:S(2)}, u32[]{:S(2)}) collective-permute-start(bf16[3,512,256]{2,1,0:T(8,128)(2,1)S(1)} %collective-permute-done.29.refs_1_), channel_id=1, source_target_pairs={{4,8},{5,9},{6,10},{7,11},{8,4},{9,5},{10,6},{11,7},{20,24},{21,25... | collective-permute-start | bytes 2359304 | tf_op jit(solution)/shard_map/ppermute | solution.py:488
  151.9 20.7 %collective-permute-start.35 = (bf16[3,512,256]{2,1,0:T(8,128)(2,1)S(1)}, bf16[3,512,256]{2,1,0:T(8,128)(2,1)S(1)}, u32[]{:S(2)}, u32[]{:S(2)}) collective-permute-start(bf16[3,512,256]{2,1,0:T(8,128)(2,1)S(1)} %collective-permute-done.27), channel_id=1, source_target_pairs={{4,0},{5,1},{6,2},{7,3},{8,12},{9,13},{10,14},{11,15},{20,16},{21,... | collective-permute-start | bytes 2359304 | tf_op jit(solution)/shard_map/ppermute | solution.py:488
  153.2 19.4 %collective-permute-start.34 = (bf16[3,512,256]{2,1,0:T(8,128)(2,1)S(1)}, bf16[3,512,256]{2,1,0:T(8,128)(2,1)S(1)}, u32[]{:S(2)}, u32[]{:S(2)}) collective-permute-start(bf16[3,512,256]{2,1,0:T(8,128)(2,1)S(1)} %collective-permute-done.29.refs_1_), channel_id=1, source_target_pairs={{0,2},{1,3},{2,0},{3,1},{4,6},{5,7},{6,4},{7,5},{8,10},{9,11},{10,... | collective-permute-start | bytes 2359304 | tf_op jit(solution)/shard_map/ppermute | solution.py:488
  153.6 17.3 %collective-permute-start.32 = (bf16[1,256,1024]{2,1,0:T(8,128)(2,1)S(1)}, bf16[1,256,1024]{2,1,0:T(8,128)(2,1)S(1)}, u32[]{:S(2)}, u32[]{:S(2)}) collective-permute-start(bf16[1,256,1024]{2,1,0:T(8,128)(2,1)S(1)} %get-tuple-element.156.refs_0_), channel_id=1, source_target_pairs={{0,4},{1,5},{2,6},{3,7},{12,8},{13,9},{14,10},{15,11},{16,20},{17,... | collective-permute-start | bytes 1572872 | tf_op jit(solution)/shard_map/ppermute | solution.py:488
  170.9 19.7 %collective-permute-start.33 = (bf16[2,1,256,1024]{3,2,1,0:T(8,128)(2,1)S(1)}, bf16[2,1,256,1024]{3,2,1,0:T(8,128)(2,1)S(1)}, u32[]{:S(2)}, u32[]{:S(2)}) collective-permute-start(bf16[2,1,256,1024]{3,2,1,0:T(8,128)(2,1)S(1)} %stack.21), channel_id=1, source_target_pairs={{4,8},{5,9},{6,10},{7,11},{8,4},{9,5},{10,6},{11,7},{20,24},{21,25... | collective-permute-start | bytes 3145736 | tf_op jit(solution)/shard_map/ppermute | solution.py:488
  172.6 18.0 %collective-permute-start.36 = (bf16[1664,256]{1,0:T(8,128)(2,1)S(1)}, bf16[1664,256]{1,0:T(8,128)(2,1)S(1)}, u32[]{:S(2)}, u32[]{:S(2)}) collective-permute-start(bf16[1664,256]{1,0:T(8,128)(2,1)S(1)} %pack.1), channel_id=1, source_target_pairs={{0,4},{1,5},{2,6},{3,7},{4,0},{5,1},{6,2},{7,3},{8,12},{9,13},{10,... | collective-permute-start | bytes 2555912 | tf_op jit(solution)/shard_map/ppermute | solution.py:488
  176.3 15.6 %collective-permute-start.40 = (bf16[3,512,256]{2,1,0:T(8,128)(2,1)S(1)}, bf16[3,512,256]{2,1,0:T(8,128)(2,1)S(1)}, u32[]{:S(2)}, u32[]{:S(2)}) collective-permute-start(bf16[3,512,256]{2,1,0:T(8,128)(2,1)S(1)} %choose.8.refs_1_), channel_id=1, source_target_pairs={{0,2},{1,3},{2,0},{3,1},{4,6},{5,7},{6,4},{7,5},{8,10},{9,11},{10,... | collective-permute-start | bytes 2359304 | tf_op jit(solution)/shard_map/ppermute | solution.py:488
  176.4 7.1 %collective-permute-start.37 = (bf16[640,256]{1,0:T(8,128)(2,1)S(1)}, bf16[640,256]{1,0:T(8,128)(2,1)S(1)}, u32[]{:S(2)}, u32[]{:S(2)}) collective-permute-start(bf16[640,256]{1,0:T(8,128)(2,1)S(1)} %attend.2.piece_ref.refs_0_), channel_id=1, source_target_pairs={{0,1},{1,0},{2,3},{3,2},{4,5},{5,4},{6,7},{7,6},{8,9},{9,8},{10,11... | collective-permute-start | bytes 983048 | tf_op jit(solution)/shard_map/ppermute | solution.py:488
  190.6 26.6 %collective-permute-start.38 = (bf16[2,1,256,1024]{3,2,1,0:T(8,128)(2,1)S(1)}, bf16[2,1,256,1024]{3,2,1,0:T(8,128)(2,1)S(1)}, u32[]{:S(2)}, u32[]{:S(2)}) collective-permute-start(bf16[2,1,256,1024]{3,2,1,0:T(8,128)(2,1)S(1)} %collective-permute-done.33), channel_id=1, source_target_pairs={{4,0},{5,1},{6,2},{7,3},{8,12},{9,13},{10,14},{11,15},{20,16},{21,... | collective-permute-start | bytes 3145736 | tf_op jit(solution)/shard_map/ppermute | solution.py:488
  193.7 23.5 %collective-permute-start.39 = (bf16[2,1,256,1024]{3,2,1,0:T(8,128)(2,1)S(1)}, bf16[2,1,256,1024]{3,2,1,0:T(8,128)(2,1)S(1)}, u32[]{:S(2)}, u32[]{:S(2)}) collective-permute-start(bf16[2,1,256,1024]{3,2,1,0:T(8,128)(2,1)S(1)} %stack.22), channel_id=1, source_target_pairs={{4,8},{5,9},{6,10},{7,11},{8,4},{9,5},{10,6},{11,7},{20,24},{21,25... | collective-permute-start | bytes 3145736 | tf_op jit(solution)/shard_map/ppermute | solution.py:488
  197.4 19.8 %collective-permute-start.44 = (bf16[1,256,1024]{2,1,0:T(8,128)(2,1)S(1)}, bf16[1,256,1024]{2,1,0:T(8,128)(2,1)S(1)}, u32[]{:S(2)}, u32[]{:S(2)}) collective-permute-start(bf16[1,256,1024]{2,1,0:T(8,128)(2,1)S(1)} %choose.9.refs_6_.refs_18_), channel_id=1, source_target_pairs={{0,2},{1,3},{2,0},{3,1},{4,6},{5,7},{6,4},{7,5},{8,10},{9,11},{10,... | collective-permute-start | bytes 1572872 | tf_op jit(solution)/shard_map/ppermute | solution.py:488
  197.8 19.5 %collective-permute-start.43 = (bf16[640,256]{1,0:T(8,128)(2,1)S(1)}, bf16[640,256]{1,0:T(8,128)(2,1)S(1)}, u32[]{:S(2)}, u32[]{:S(2)}) collective-permute-start(bf16[640,256]{1,0:T(8,128)(2,1)S(1)} %get-tuple-element.163.refs_2_), channel_id=1, source_target_pairs={{0,1},{1,0},{2,3},{3,2},{4,5},{5,4},{6,7},{7,6},{8,9},{9,8},{10,11... | collective-permute-start | bytes 983048 | tf_op jit(solution)/shard_map/ppermute | solution.py:488
  203.0 14.2 %collective-permute-start.42 = (bf16[640,256]{1,0:T(8,128)(2,1)S(1)}, bf16[640,256]{1,0:T(8,128)(2,1)S(1)}, u32[]{:S(2)}, u32[]{:S(2)}) collective-permute-start(bf16[640,256]{1,0:T(8,128)(2,1)S(1)} %attend.3.refs_0_), channel_id=1, source_target_pairs={{0,1},{1,0},{2,3},{3,2},{4,5},{5,4},{6,7},{7,6},{8,9},{9,8},{10,11... | collective-permute-start | bytes 983048 | tf_op jit(solution)/shard_map/ppermute | solution.py:488
  217.3 7.1 %collective-permute-start.45 = (bf16[640,256]{1,0:T(8,128)(2,1)S(1)}, bf16[640,256]{1,0:T(8,128)(2,1)S(1)}, u32[]{:S(2)}, u32[]{:S(2)}) collective-permute-start(bf16[640,256]{1,0:T(8,128)(2,1)S(1)} %attend.3.refs_0_), channel_id=1, source_target_pairs={{0,4},{1,5},{2,6},{3,7},{4,0},{5,1},{6,2},{7,3},{8,12},{9,13},{10,... | collective-permute-start | bytes 983048 | tf_op jit(solution)/shard_map/ppermute | solution.py:488
  226.4 13.9 %collective-permute-start.50 = (bf16[2,1,256,512]{3,2,1,0:T(8,128)(2,1)S(1)}, bf16[2,1,256,512]{3,2,1,0:T(8,128)(2,1)S(1)}, u32[]{:S(2)}, u32[]{:S(2)}) collective-permute-start(bf16[2,1,256,512]{3,2,1,0:T(8,128)(2,1)S(1)} %get-tuple-element.168.refs_12_.refs_14_.refs_20_.refs_22_), channel_id=1, source_target_pairs={{0,2},{1,3},{2,0},{3,1},{4,6},{5,7},{6,4},{7,5},{8,10},{9,11},{10,... | collective-permute-start | bytes 1572872 | tf_op jit(solution)/shard_map/ppermute | solution.py:488
  229.4 9.8 %collective-permute-start.51 = (bf16[640,256]{1,0:T(8,128)(2,1)S(1)}, bf16[640,256]{1,0:T(8,128)(2,1)S(1)}, u32[]{:S(2)}, u32[]{:S(2)}) collective-permute-start(bf16[640,256]{1,0:T(8,128)(2,1)S(1)} %collective-permute-done.45.refs_2_), channel_id=1, source_target_pairs={{0,1},{1,0},{2,3},{3,2},{4,5},{5,4},{6,7},{7,6},{8,9},{9,8},{10,11... | collective-permute-start | bytes 983048 | tf_op jit(solution)/shard_map/ppermute | solution.py:488
  244.5 14.2 %collective-permute-start.53 = (bf16[2,1,256,512]{3,2,1,0:T(8,128)(2,1)S(1)}, bf16[2,1,256,512]{3,2,1,0:T(8,128)(2,1)S(1)}, u32[]{:S(2)}, u32[]{:S(2)}) collective-permute-start(bf16[2,1,256,512]{3,2,1,0:T(8,128)(2,1)S(1)} %get-tuple-element.178.refs_12_.refs_14_.refs_20_.refs_22_), channel_id=1, source_target_pairs={{0,2},{1,3},{2,0},{3,1},{4,6},{5,7},{6,4},{7,5},{8,10},{9,11},{10,... | collective-permute-start | bytes 1572872 | tf_op jit(solution)/shard_map/ppermute | solution.py:488
  246.8 9.8 %collective-permute-start.55 = (bf16[320,512]{1,0:T(8,128)(2,1)S(1)}, bf16[320,512]{1,0:T(8,128)(2,1)S(1)}, u32[]{:S(2)}, u32[]{:S(2)}) collective-permute-start(bf16[320,512]{1,0:T(8,128)(2,1)S(1)} %join.2), channel_id=1, source_target_pairs={{0,4},{1,5},{2,6},{3,7},{4,0},{5,1},{6,2},{7,3},{8,12},{9,13},{10,... | collective-permute-start | bytes 983048 | tf_op jit(solution)/shard_map/ppermute | solution.py:488
  263.0 9.8 %collective-permute-start.60 = (bf16[320,512]{1,0:T(8,128)(2,1)S(1)}, bf16[320,512]{1,0:T(8,128)(2,1)S(1)}, u32[]{:S(2)}, u32[]{:S(2)}) collective-permute-start(bf16[320,512]{1,0:T(8,128)(2,1)S(1)} %join.3), channel_id=1, source_target_pairs={{0,4},{1,5},{2,6},{3,7},{4,0},{5,1},{6,2},{7,3},{8,12},{9,13},{10,... | collective-permute-start | bytes 983048 | tf_op jit(solution)/shard_map/ppermute | solution.py:488
  265.8 7.1 %collective-permute-start.59 = (bf16[640,512]{1,0:T(8,128)(2,1)S(1)}, bf16[640,512]{1,0:T(8,128)(2,1)S(1)}, u32[]{:S(2)}, u32[]{:S(2)}) collective-permute-start(bf16[640,512]{1,0:T(8,128)(2,1)S(1)} %combine.9.refs_4_), channel_id=1, source_target_pairs={{0,16},{1,17},{2,18},{3,19},{4,20},{5,21},{6,22},{7,23},{8,24},{9,... | collective-permute-start | bytes 1966088 | tf_op jit(solution)/shard_map/ppermute | solution.py:488
  (20 other events, 161.5 us)
